TPU v7x, 32 devices: a whole 2x2x4 slice. The times are simulated.
32 devices in a mesh: rep: 8 (over y, x, core), shard: 4 (over z).
Axes of the slice: x: 2, y: 2, z: 4, core: 2. Of those that a mesh axis runs over, the one named last changes fastest.
Arguments:
- tokens: bfloat16 [16, 1024, 2048], P('rep', 'shard'), may hold values from -6 to 6
- lengths: int32 [16], P('rep'), may hold values from 256 to 1024, as said below
- attn_gain: bfloat16 [2048], P('shard'), may hold values from 0.099609375 to 1.8984375
- w_query: bfloat16 [2048, 2048], P('shard'), may hold values from -0.125 to 0.125
- key_matrix: bfloat16 [2048, 1024], P('shard'), may hold values from -0.125 to 0.125
- value_matrix: bfloat16 [2048, 1024], P('shard'), may hold values from -0.125 to 0.125
- query_gain: bfloat16 [128], replicated, may hold values from 0.69921875 to 2
- key_gain: bfloat16 [128], replicated, may hold values from 0.69921875 to 2
- w_out: bfloat16 [2048, 2048], P('shard'), may hold values from -0.75 to 0.75
- mlp_gain: bfloat16 [2048], P('shard'), may hold values from 0.099609375 to 1.8984375
- w_gate: bfloat16 [2048, 6144], P('shard'), may hold values from -0.125 to 0.125
- w_up: bfloat16 [2048, 6144], P('shard'), may hold values from -0.125 to 0.125
- w_down: bfloat16 [2048, 6144], P('shard'), may hold values from -0.078125 to 0.078125
- cotangent: bfloat16 [16, 1024, 2048], P('rep', 'shard'), may hold values from -6 to 6
Outputs:
- output: bfloat16 [16, 1024, 2048], P('rep', 'shard')
- grad_tokens: bfloat16 [16, 1024, 2048], P('rep', 'shard')
- grad_attn_gain: float32 [2048], P('shard')
- grad_query: float32 [2048, 2048], P('shard')
- grad_key: float32 [2048, 1024], P('shard')
- grad_value: float32 [2048, 1024], P('shard')
- grad_query_gain: float32 [128], replicated
- grad_key_gain: float32 [128], replicated
- grad_out: float32 [2048, 2048], P('shard')
- grad_mlp_gain: float32 [2048], P('shard')
- grad_gate: float32 [2048, 6144], P('shard')
- grad_up: float32 [2048, 6144], P('shard')
- grad_down: float32 [2048, 6144], P('shard')
Inputs may be any that keep to these rules, and one draw needn't show every extreme that they name: `lengths`: among the 2 sequences of each index of rep, one, drawn from the seed, has length 1024.
All inputs are finite; a program needn't handle non-finite values.
Results may differ from a plain program's by a relative error of at most 0.02.
Values may be sent and summed in bfloat16 or wider, within the bound.
No kernel may reach another device: no remote copies, remote signals or barrier semaphores. Data moves between devices by JAX's collectives and lax.ppermute only.
A program may use at most 512 MiB of HBM per device.

v0:
```python
import jax
import jax.numpy as jnp
from jax import lax
from jax.sharding import PartitionSpec as P

WINDOW = 512


EPS = 1e-06
ROPE_BASE = 1000000.0
NEG = -1e30


def passed_along(x, axis, by):
    devices = lax.axis_size(axis)
    pairs = [(i, i + by) for i in range(devices) if 0 <= i + by < devices]
    return lax.ppermute(x, axis, pairs)


def tables(positions, head_dim):
    half = head_dim // 2
    freq = ROPE_BASE ** (-jnp.arange(half, dtype=jnp.float32) * 2.0 / head_dim)
    angle = positions.astype(jnp.float32)[:, None] * freq[None, :]
    angle = jnp.concatenate([angle, angle], -1)
    return (jnp.cos(angle)[None, :, None, :], jnp.sin(angle)[None, :, None, :])


def rotated_rows(value_rows):
    half = value_rows.shape[-1] // 2
    return jnp.concatenate([-value_rows[..., half:], value_rows[..., :half]], -1)


def head_norm(raw, gain):
    inverse = lax.rsqrt(jnp.mean(raw * raw, -1, keepdims=True) + EPS)
    unit = raw * inverse
    return (unit, inverse, unit * gain)


def norm_back(unit, inverse, grad_unit):
    return inverse * (grad_unit - unit * jnp.mean(grad_unit * unit, -1, keepdims=True))


def head_norm_back(unit, inverse, grad_normed, gain):
    grad_raw = norm_back(unit, inverse, grad_normed * gain)
    return (grad_raw, jnp.sum(unit * grad_normed, axis=(0, 1, 2)))


def scores(query_rows, keys, allowed, scale):
    raw = (
        jnp.einsum("sqhgd,skhd->shgqk", query_rows, keys, preferred_element_type=jnp.float32)
        * scale
    )
    return jnp.where(allowed[:, None, None], raw, NEG)


def outer(left, right):
    return jnp.einsum("rc,rf->cf", left, right, preferred_element_type=jnp.float32)


def on_device(
    tokens,
    lengths,
    attn_gain,
    w_query,
    key_matrix,
    value_matrix,
    query_gain,
    key_gain,
    w_out,
    mlp_gain,
    w_gate,
    w_up,
    w_down,
    cotangent,
):
    seq_count, piece, width = tokens.shape
    head_dim = query_gain.shape[0]
    heads_q = w_query.shape[1] // head_dim
    heads_kv = key_matrix.shape[1] // head_dim
    groups = heads_q // heads_kv
    rows = seq_count * piece
    scale = head_dim ** (-0.5)
    reach = (WINDOW + piece - 2) // piece
    owned = width // lax.axis_size("shard")
    shard_at = lax.axis_index("shard")
    query_pos = shard_at * piece + jnp.arange(piece, dtype=jnp.int32)
    key_pos = (shard_at - reach) * piece + jnp.arange((reach + 1) * piece, dtype=jnp.int32)
    near = (
        (key_pos[None, :] <= query_pos[:, None])
        & (query_pos[:, None] - key_pos[None, :] < WINDOW)
        & (key_pos[None, :] >= 0)
    )
    live = (key_pos[None, None, :] < lengths[:, None, None]) | (
        key_pos[None, :] == query_pos[:, None]
    )[None]
    allowed = near[None] & live
    valid = (query_pos[None, :] < lengths[:, None]).astype(jnp.float32).reshape(rows, 1)
    cosine_table, sine_table = tables(query_pos, head_dim)
    x_rows = tokens.astype(jnp.float32).reshape(rows, width)
    inverse_in = lax.rsqrt(jnp.mean(x_rows * x_rows, -1, keepdims=True) + EPS)
    x_unit = x_rows * inverse_in
    gain_piece = lax.all_gather(attn_gain, "shard", axis=0, tiled=True)
    query_piece = lax.all_gather(w_query, "shard", axis=0, tiled=True)
    key_piece = lax.all_gather(key_matrix, "shard", axis=0, tiled=True)
    value_piece = lax.all_gather(value_matrix, "shard", axis=0, tiled=True)
    normed_piece = (x_unit * gain_piece.astype(jnp.float32)).astype(jnp.bfloat16)
    acc_q = jnp.dot(normed_piece, query_piece, preferred_element_type=jnp.float32)
    acc_k = jnp.dot(normed_piece, key_piece, preferred_element_type=jnp.float32)
    acc_v = jnp.dot(normed_piece, value_piece, preferred_element_type=jnp.float32)
    normalized_rows = normed_piece
    gains = gain_piece.astype(jnp.float32)
    attn_in = normalized_rows
    attn_gains = gains
    query_unit, query_inverse, query_rows_normalized = head_norm(
        acc_q.reshape(seq_count, piece, heads_q, head_dim), query_gain.astype(jnp.float32)
    )
    key_unit, key_inverse, key_normed = head_norm(
        acc_k.reshape(seq_count, piece, heads_kv, head_dim), key_gain.astype(jnp.float32)
    )
    query_rows = (
        (query_rows_normalized * cosine_table + rotated_rows(query_rows_normalized) * sine_table)
        .astype(jnp.bfloat16)
        .reshape(seq_count, piece, heads_kv, groups, head_dim)
    )
    keys_own = (key_normed * cosine_table + rotated_rows(key_normed) * sine_table).astype(
        jnp.bfloat16
    )
    values_own = acc_v.reshape(seq_count, piece, heads_kv, head_dim).astype(jnp.bfloat16)
    own_pair = jnp.stack([keys_own, values_own])
    parts = []
    for fetch_back in range(reach, 0, -1):
        parts.append(passed_along(own_pair, "shard", fetch_back))
    parts.append(own_pair)
    near_pair = jnp.concatenate(parts, 2)
    score = scores(query_rows, near_pair[0], allowed, scale)
    top = jnp.max(score, -1, keepdims=True)
    expo = jnp.exp(score - top)
    total = jnp.sum(expo, -1, keepdims=True)
    prob = expo / total
    log_total = top + jnp.log(total)
    mixed = jnp.einsum(
        "shgqk,skhd->sqhgd",
        prob.astype(jnp.bfloat16),
        near_pair[1],
        preferred_element_type=jnp.float32,
    )
    mixed_rows = mixed.reshape(rows, heads_q * head_dim).astype(jnp.bfloat16)
    resid = x_rows + jnp.einsum(
        "rf,nf->rn",
        mixed_rows,
        lax.all_gather(w_out, "shard", axis=0, tiled=True),
        preferred_element_type=jnp.float32,
    )
    inverse_mid = lax.rsqrt(jnp.mean(resid * resid, -1, keepdims=True) + EPS)
    mid_unit = resid * inverse_mid
    gain_piece = lax.all_gather(mlp_gain, "shard", axis=0, tiled=True)
    gate_piece = lax.all_gather(w_gate, "shard", axis=0, tiled=True)
    up_piece = lax.all_gather(w_up, "shard", axis=0, tiled=True)
    normed_piece = (mid_unit * gain_piece.astype(jnp.float32)).astype(jnp.bfloat16)
    acc_gate = jnp.dot(normed_piece, gate_piece, preferred_element_type=jnp.float32)
    acc_up = jnp.dot(normed_piece, up_piece, preferred_element_type=jnp.float32)
    normalized_rows = normed_piece
    gains = gain_piece.astype(jnp.float32)
    mlp_in = normalized_rows
    sigma = jax.nn.sigmoid(acc_gate)
    swish = acc_gate * sigma
    act = (swish * acc_up).astype(jnp.bfloat16)
    mlp_out = jnp.einsum(
        "rf,nf->rn",
        act,
        lax.all_gather(w_down, "shard", axis=0, tiled=True),
        preferred_element_type=jnp.float32,
    )
    output = (valid * (resid + mlp_out)).astype(jnp.bfloat16).reshape(seq_count, piece, width)
    grad_y = cotangent.astype(jnp.float32).reshape(rows, width) * valid
    grad_y_low = grad_y.astype(jnp.bfloat16)
    grad_act = jnp.dot(
        grad_y_low,
        lax.all_gather(w_down, "shard", axis=0, tiled=True),
        preferred_element_type=jnp.float32,
    )
    grad_gate = (grad_act * acc_up * sigma * (1.0 + acc_gate * (1.0 - sigma))).astype(jnp.bfloat16)
    grad_up = (grad_act * swish).astype(jnp.bfloat16)
    gate_piece, up_piece = lax.all_gather((w_gate, w_up), "shard", axis=0, tiled=True)
    grad_mid = jnp.einsum(
        "rf,nf->rn", grad_gate, gate_piece, preferred_element_type=jnp.float32
    ) + jnp.einsum("rf,nf->rn", grad_up, up_piece, preferred_element_type=jnp.float32)
    grad_resid = grad_y + norm_back(mid_unit, inverse_mid, grad_mid * gains)
    mlp_gain_part = jnp.sum(mid_unit * grad_mid, 0)
    normalized_rows = mlp_in
    mlp_grads = jax.tree.map(
        lambda part: lax.psum_scatter(
            part.astype(jnp.bfloat16), "shard", scatter_dimension=0, tiled=True
        ).astype(jnp.float32),
        (
            outer(normalized_rows, grad_gate),
            outer(normalized_rows, grad_up),
            outer(grad_y_low, act),
        ),
    )
    resid_low = grad_resid.astype(jnp.bfloat16)
    grad_mixed = jnp.dot(
        resid_low,
        lax.all_gather(w_out, "shard", axis=0, tiled=True),
        preferred_element_type=jnp.float32,
    )
    grad_mixed = grad_mixed.astype(jnp.bfloat16).reshape(
        seq_count, piece, heads_kv, groups, head_dim
    )
    prob_again = jnp.exp(scores(query_rows, near_pair[0], allowed, scale) - log_total)
    grad_prob = jnp.einsum(
        "sqhgd,skhd->shgqk", grad_mixed, near_pair[1], preferred_element_type=jnp.float32
    )
    grad_values = jnp.einsum(
        "shgqk,sqhgd->skhd",
        prob_again.astype(jnp.bfloat16),
        grad_mixed,
        preferred_element_type=jnp.float32,
    )
    grad_score = (
        prob_again * (grad_prob - jnp.sum(prob_again * grad_prob, -1, keepdims=True))
    ).astype(jnp.bfloat16)
    grad_queries = (
        jnp.einsum(
            "shgqk,skhd->sqhgd", grad_score, near_pair[0], preferred_element_type=jnp.float32
        )
        * scale
    )
    grad_keys = (
        jnp.einsum("shgqk,sqhgd->skhd", grad_score, query_rows, preferred_element_type=jnp.float32)
        * scale
    )
    grad_pair = jnp.stack([grad_keys, grad_values])
    own_grad = grad_pair[:, :, reach * piece :]
    for back in range(1, reach + 1):
        lower = (reach - back) * piece
        own_grad = own_grad + passed_along(grad_pair[:, :, lower : lower + piece], "shard", -back)
    grad_query_post = grad_queries.reshape(seq_count, piece, heads_q, head_dim)
    grad_query_normed = grad_query_post * cosine_table - rotated_rows(grad_query_post * sine_table)
    grad_key_normed = own_grad[0] * cosine_table - rotated_rows(own_grad[0] * sine_table)
    grad_query_raw, query_gain_grad = head_norm_back(
        query_unit, query_inverse, grad_query_normed, query_gain.astype(jnp.float32)
    )
    grad_key_raw, key_gain_grad = head_norm_back(
        key_unit, key_inverse, grad_key_normed, key_gain.astype(jnp.float32)
    )
    grad_query_low = grad_query_raw.reshape(rows, heads_q * head_dim).astype(jnp.bfloat16)
    grad_key_low = grad_key_raw.reshape(rows, heads_kv * head_dim).astype(jnp.bfloat16)
    grad_value_low = own_grad[1].reshape(rows, heads_kv * head_dim).astype(jnp.bfloat16)
    query_piece, key_piece, value_piece = lax.all_gather(
        (w_query, key_matrix, value_matrix), "shard", axis=0, tiled=True
    )
    grad_in = (
        jnp.einsum("rf,nf->rn", grad_query_low, query_piece, preferred_element_type=jnp.float32)
        + jnp.einsum("rf,nf->rn", grad_key_low, key_piece, preferred_element_type=jnp.float32)
        + jnp.einsum("rf,nf->rn", grad_value_low, value_piece, preferred_element_type=jnp.float32)
    )
    grad_tokens = (
        (grad_resid + norm_back(x_unit, inverse_in, grad_in * attn_gains))
        .astype(jnp.bfloat16)
        .reshape(seq_count, piece, width)
    )
    attn_gain_part = jnp.sum(x_unit * grad_in, 0)
    normalized_rows = attn_in
    attn_grads = jax.tree.map(
        lambda part: lax.psum_scatter(
            part.astype(jnp.bfloat16), "shard", scatter_dimension=0, tiled=True
        ).astype(jnp.float32),
        (
            outer(normalized_rows, grad_query_low),
            outer(normalized_rows, grad_key_low),
            outer(normalized_rows, grad_value_low),
            outer(resid_low, mixed_rows),
        ),
    )
    head_grads = lax.psum(
        (query_gain_grad, key_gain_grad, attn_gain_part, mlp_gain_part), ("rep", "shard")
    )
    attn_gain_total = lax.dynamic_slice_in_dim(head_grads[2], shard_at * owned, owned, 0)
    mlp_gain_total = lax.dynamic_slice_in_dim(head_grads[3], shard_at * owned, owned, 0)
    summed = (
        lax.psum(attn_grads[0].astype(jnp.bfloat16), "rep").astype(jnp.float32),
        lax.psum(attn_grads[1].astype(jnp.bfloat16), "rep").astype(jnp.float32),
        lax.psum(attn_grads[2].astype(jnp.bfloat16), "rep").astype(jnp.float32),
        lax.psum(attn_grads[3].astype(jnp.bfloat16), "rep").astype(jnp.float32),
        lax.psum(mlp_grads[0].astype(jnp.bfloat16), "rep").astype(jnp.float32),
        lax.psum(mlp_grads[1].astype(jnp.bfloat16), "rep").astype(jnp.float32),
        lax.psum(mlp_grads[2].astype(jnp.bfloat16), "rep").astype(jnp.float32),
    )
    attn_grads = summed[:4]
    mlp_grads = summed[4:]
    return (
        output,
        grad_tokens,
        attn_gain_total,
        attn_grads[0],
        attn_grads[1],
        attn_grads[2],
        head_grads[0],
        head_grads[1],
        attn_grads[3],
        mlp_gain_total,
        mlp_grads[0],
        mlp_grads[1],
        mlp_grads[2],
    )


def solution(mesh):
    return jax.shard_map(
        on_device,
        mesh=mesh,
        in_specs=(
            P("rep", "shard", None),
            P("rep"),
            P("shard"),
            P("shard", None),
            P("shard", None),
            P("shard", None),
            P(),
            P(),
            P("shard", None),
            P("shard"),
            P("shard", None),
            P("shard", None),
            P("shard", None),
            P("rep", "shard", None),
        ),
        out_specs=(
            P("rep", "shard", None),
            P("rep", "shard", None),
            P("shard"),
            P("shard", None),
            P("shard", None),
            P("shard", None),
            P(),
            P(),
            P("shard", None),
            P("shard"),
            P("shard", None),
            P("shard", None),
            P("shard", None),
        ),
        check_vma=False,
    )
```

profile of v0, /device:TPU:0, one launch (start us, length us, event | category | flops | bytes accessed | tf_op | source)
XLA Modules:
  0.0 4381.5 jit_solution(15991989277253414572)
XLA Ops:
  12.0 13.7 all-gather
  29.2 63.9 %all-gather.12.cloned.1.call-done = bf16[2048,1024]{1,0:T(8,128)(2,1)} async-done(((bf16[512,1024]{1,0:T(8,128)(2,1)}), bf16[2048,1024]{1,0:T(8,128)(2,1)}) %all-gather.12.cloned.1.call-update) | async-done | bytes 4194320 | tf_op jit(solution)/shard_map/all_gather | solution.py:105
  99.5 74.5 %all-gather.10.cloned.1.call-done = bf16[2048,1024]{1,0:T(8,128)(2,1)} async-done(((bf16[512,1024]{1,0:T(8,128)(2,1)}), bf16[2048,1024]{1,0:T(8,128)(2,1)}) %all-gather.10.cloned.1.call-update) | async-done | bytes 4194320 | tf_op jit(solution)/shard_map/all_gather | solution.py:104
  201.3 311.5 %all-gather.1 = bf16[4,1,512]{2,1,0:T(2,128)(2,1)S(1)} all-gather(bf16[1,1,512]{2,1,0:T(2,128)(2,1)S(1)} %reshape.441), channel_id=1, replica_groups=mesh['rep'=8,'shard'=4] {'shard'}, dimensions={0}, use_global_device_ids=true | all-gather | bytes 5120 | tf_op jit(solution)/shard_map/all_gather | solution.py:156
  522.8 12.2 copy.60
  569.1 13.3 convert_bitcast_fusion
  604.5 413.9 %all-gather.20.cloned.1.call-done = bf16[2048,6144]{1,0:T(8,128)(2,1)} async-done(((bf16[512,6144]{1,0:T(8,128)(2,1)}), bf16[2048,6144]{1,0:T(8,128)(2,1)}) %all-gather.20.cloned.1.call-update) | async-done | bytes 25165840 | tf_op jit(solution)/shard_map/all_gather | solution.py:158
  1018.3 20.7 fusion.83
  1039.0 404.2 %all-gather.18.cloned.1.call-done = bf16[2048,6144]{1,0:T(8,128)(2,1)} async-done(((bf16[512,6144]{1,0:T(8,128)(2,1)}), bf16[2048,6144]{1,0:T(8,128)(2,1)}) %all-gather.18.cloned.1.call-update) | async-done | bytes 25165840 | tf_op jit(solution)/shard_map/all_gather | solution.py:157
  1443.2 20.7 fusion.82
  1463.8 404.3 %all-gather.22.cloned.1.call-done = bf16[2048,6144]{1,0:T(8,128)(2,1)} async-done(((bf16[512,6144]{1,0:T(8,128)(2,1)}), bf16[2048,6144]{1,0:T(8,128)(2,1)}) %all-gather.22.cloned.1.call-update) | async-done | bytes 25165840 | tf_op jit(solution)/shard_map/all_gather | solution.py:171
  1868.1 32.6 multiply_convert_fusion
  1900.7 21.1 fusion.84
  1921.8 21.1 multiply_reduce_fusion
  1962.6 13.9 fusion.35
  1976.5 21.0 fusion
  1997.5 21.3 fusion.2
  2033.6 93.0 %collective-permute-done.2 = f32[2,2,256,8,128]{2,4,3,1,0:T(8,128)S(1)} collective-permute-done((f32[2,2,256,8,128]{2,4,3,1,0:T(8,128)S(1)}, f32[2,2,256,8,128]{2,4,3,1,0:T(8,128)S(1)}, u32[]{:S(2)}, u32[]{:S(2)}) %collective-permute-start.2) | collective-permute-done | bytes 4194336 | tf_op jit(solution)/shard_map/ppermute | solution.py:17
  2126.6 177.1 %collective-permute-done.3 = f32[2,2,256,8,128]{2,4,3,1,0:T(8,128)S(1)} collective-permute-done((f32[2,2,256,8,128]{2,4,3,1,0:T(8,128)S(1)}, f32[2,2,256,8,128]{2,4,3,1,0:T(8,128)S(1)}, u32[]{:S(2)}, u32[]{:S(2)}) %collective-permute-start.3) | collective-permute-done | bytes 4194336 | tf_op jit(solution)/shard_map/ppermute | solution.py:17
  2368.9 19.5 convolution_convert_fusion.1
  2388.4 19.4 convolution_convert_fusion.2
  2409.4 19.4 convolution_convert_fusion
  2429.0 44.9 %reduce-scatter.12.cloned.1.call-done = bf16[512,1024]{1,0:T(8,128)(2,1)} async-done(((bf16[2048,1024]{1,0:T(8,128)(2,1)}), bf16[512,1024]{1,0:T(8,128)(2,1)}) %reduce-scatter.12.cloned.1.call-update) | async-done | bytes 1048592 | tf_op jit(solution)/shard_map/reduce_scatter | solution.py:266
  2473.9 147.8 %reduce-scatter.14.cloned.1.call-done = bf16[512,2048]{1,0:T(8,128)(2,1)} async-done(((bf16[2048,2048]{1,0:T(8,128)(2,1)}), bf16[512,2048]{1,0:T(8,128)(2,1)}) %reduce-scatter.14.cloned.1.call-update) | async-done | bytes 2097168 | tf_op jit(solution)/shard_map/reduce_scatter | solution.py:266
  2621.7 148.2 %reduce-scatter.8.cloned.1.call-done = bf16[512,2048]{1,0:T(8,128)(2,1)} async-done(((bf16[2048,2048]{1,0:T(8,128)(2,1)}), bf16[512,2048]{1,0:T(8,128)(2,1)}) %reduce-scatter.8.cloned.1.call-update) | async-done | bytes 2097168 | tf_op jit(solution)/shard_map/reduce_scatter | solution.py:266
  2769.8 417.4 %reduce-scatter.18.cloned.1.call-done = bf16[512,6144]{1,0:T(8,128)(2,1)} async-done(((bf16[2048,6144]{1,0:T(8,128)(2,1)}), bf16[512,6144]{1,0:T(8,128)(2,1)}) %reduce-scatter.18.cloned.1.call-update) | async-done | bytes 6291472 | tf_op jit(solution)/shard_map/reduce_scatter | solution.py:192
  3187.2 418.7 %reduce-scatter.16.cloned.1.call-done = bf16[512,6144]{1,0:T(8,128)(2,1)} async-done(((bf16[2048,6144]{1,0:T(8,128)(2,1)}), bf16[512,6144]{1,0:T(8,128)(2,1)}) %reduce-scatter.16.cloned.1.call-update) | async-done | bytes 6291472 | tf_op jit(solution)/shard_map/reduce_scatter | solution.py:192
  3605.9 418.5 %reduce-scatter.20.cloned.1.call-done = bf16[512,6144]{1,0:T(8,128)(2,1)} async-done(((bf16[2048,6144]{1,0:T(8,128)(2,1)}), bf16[512,6144]{1,0:T(8,128)(2,1)}) %reduce-scatter.20.cloned.1.call-update) | async-done | bytes 6291472 | tf_op jit(solution)/shard_map/reduce_scatter | solution.py:192
  4025.1 19.9 multiply_convert_fusion.4
  4052.0 11.5 fusion.28
  4063.5 44.4 %all-reduce = (f32[2048]{0:T(1024)S(1)}, f32[128]{0:T(128)}, f32[128]{0:T(128)}, f32[2048]{0:T(1024)S(1)}) all-reduce(f32[2048]{0:T(1024)S(1)} %get-tuple-element.17, f32[128]{0:T(128)S(1)} %copy-done.55, f32[128]{0:T(128)S(1)} %copy-done.54, f32[2048]{0:T(1024)S(1)} %copy-done.49), channel_id=1, replica_groups=mesh['rep'=8,'shard'=4] {'rep','shard'}, use_global_device_ids=true, to_apply=%region_12.13 | all-reduce | flops 4352 | bytes 34816 | tf_op jit(solution)/shard_map/psum | solution.py:276
  4115.1 229.6 %all-reduce.4.cloned.1.call-done = (bf16[512,2048]{1,0:T(8,128)(2,1)}, bf16[512,1024]{1,0:T(8,128)(2,1)}, bf16[512,1024]{1,0:T(8,128)(2,1)}, bf16[512,2048]{1,0:...) async-done(((bf16[512,2048]{1,0:T(8,128)(2,1)}, bf16[512,1024]{1,0:T(8,128)(2,1)}, bf16[512,1024]{1,0:T(8,128)(2,1)}, ...) | async-done | bytes 25165840 | tf_op jit(solution)/shard_map/psum | solution.py:282
  (266 shorter events, 253.8 us)
Async XLA Ops:
  7.2 85.9 %all-gather.12.cloned.1.call-start = ((), (), s32[]{:S(2)}) async-start(), calls=%async_computation.8 | async-start | bytes 5242880 | tf_op jit(solution)/shard_map/all_gather | solution.py:105
  7.9 166.1 %all-gather.10.cloned.1.call-start = ((), (), s32[]{:S(2)}) async-start(), calls=%async_computation.7 | async-start | bytes 5242880 | tf_op jit(solution)/shard_map/all_gather | solution.py:104
  8.7 514.1 %all-gather.14.cloned.1.call-start = ((), (), s32[]{:S(2)}) async-start(), calls=%async_computation.9 | async-start | bytes 10485760 | tf_op jit(solution)/shard_map/all_gather | solution.py:103
  9.4 583.6 %all-gather.16.cloned.1.call-start = ((), (), s32[]{:S(2)}) async-start(), calls=%async_computation.10 | async-start | bytes 10485760 | tf_op jit(solution)/shard_map/all_gather | solution.py:151
  10.0 1008.3 %all-gather.20.cloned.1.call-start = ((), (), s32[]{:S(2)}) async-start(), calls=%async_computation.12 | async-start | bytes 31457280 | tf_op jit(solution)/shard_map/all_gather | solution.py:158
  10.6 1432.6 %all-gather.18.cloned.1.call-start = ((), (), s32[]{:S(2)}) async-start(), calls=%async_computation.11 | async-start | bytes 31457280 | tf_op jit(solution)/shard_map/all_gather | solution.py:157
  11.2 1857.0 %all-gather.22.cloned.1.call-start = ((), (), s32[]{:S(2)}) async-start(), calls=%async_computation.13 | async-start | bytes 31457280 | tf_op jit(solution)/shard_map/all_gather | solution.py:171
  11.9 2417.1 %reduce-scatter.10.cloned.1.call-start = ((), (), s32[]{:S(2)}) async-start(), calls=%async_computation.15 | async-start | bytes 5242880 | tf_op jit(solution)/shard_map/reduce_scatter | solution.py:266
  12.0 175.2 %copy-start.50 = (f32[128]{0:T(128)}, f32[128]{0:T(128)S(1)}, u32[]{:S(2)}) copy-start(f32[128]{0:T(128)S(1)} %convert_element_type.184) | copy-start | bytes 1540
  25.7 73.8 %copy-start.43 = (f32[4,1,512]{2,1,0:T(1,128)}, f32[4,1,512]{2,1,0:T(1,128)S(1)}, u32[]{:S(2)}) copy-start(f32[4,1,512]{2,1,0:T(1,128)S(1)} %convert_element_type.228) | copy-start | bytes 24580
  26.3 160.9 %copy-start.20 = (f32[256,128]{0,1:T(8,128)}, f32[256,128]{0,1:T(8,128)S(1)}, u32[]{:S(2)}) copy-start(f32[256,128]{0,1:T(8,128)S(1)} %get-tuple-element.47) | copy-start | bytes 393220
  26.3 160.9 %copy-start.23 = (f32[256,128]{0,1:T(8,128)}, f32[256,128]{0,1:T(8,128)S(1)}, u32[]{:S(2)}) copy-start(f32[256,128]{0,1:T(8,128)S(1)} %get-tuple-element.48) | copy-start | bytes 393220
  195.1 322.1 %collective-permute-start.1 = (bf16[2,2,256,8,128]{2,4,3,1,0:T(8,128)(2,1)}, bf16[2,2,256,8,128]{2,4,3,1,0:T(8,128)(2,1)}, u32[]{:S(2)}, u32[]{:S(2)}) collective-permute-start(bf16[2,2,256,8,128]{2,4,3,1,0:T(8,128)(2,1)} %pad_maximum_fusion.1), channel_id=1, source_target_pairs={{0,1},{1,2},{2,3},{4,5},{5,6},{6,7},{8,9},{9,10},{10,11},{12,13},{... | collective-permute-start | bytes 6291464 | tf_op jit(solution)/shard_map/ppermute | solution.py:17
  197.7 319.5 %collective-permute-start = (bf16[2,2,256,8,128]{2,4,3,1,0:T(8,128)(2,1)}, bf16[2,2,256,8,128]{2,4,3,1,0:T(8,128)(2,1)}, u32[]{:S(2)}, u32[]{:S(2)}) collective-permute-start(bf16[2,2,256,8,128]{2,4,3,1,0:T(8,128)(2,1)} %pad_maximum_fusion.1), channel_id=1, source_target_pairs={{0,2},{1,3},{4,6},{5,7},{8,10},{9,11},{12,14},{13,15},{16,18},{17,... | collective-permute-start | bytes 6291464 | tf_op jit(solution)/shard_map/ppermute | solution.py:17
  201.2 316.0 %copy-start.19 = (bf16[1,2,256,8,128]{2,4,3,1,0:T(8,128)(2,1)S(1)}, bf16[1,2,256,8,128]{2,4,3,1,0:T(8,128)(2,1)}, u32[]{:S(2)}) copy-start(bf16[1,2,256,8,128]{2,4,3,1,0:T(8,128)(2,1)} %copy-done.18) | copy-start | bytes 3145732
  201.2 342.9 %copy-start.52 = (f32[128]{0:T(128)}, f32[128]{0:T(128)S(1)}, u32[]{:S(2)}) copy-start(f32[128]{0:T(128)S(1)} %convert_element_type.188) | copy-start | bytes 1540
  201.3 312.4 %copy-start.45 = (f32[1,2,2,128]{3,1,2,0:T(2,128)}, f32[1,2,2,128]{3,1,2,0:T(2,128)S(1)}, u32[]{:S(2)}) copy-start(f32[1,2,2,128]{3,1,2,0:T(2,128)S(1)} %copy.91) | copy-start | bytes 6148
  513.6 55.5 %copy-start.11 = (pred[2,256,768]{1,2,0:T(8,128)(4,1)}, pred[2,256,768]{1,2,0:T(8,128)(4,1)S(1)}, u32[]{:S(2)}) copy-start(pred[2,256,768]{1,2,0:T(8,128)(4,1)S(1)} %or_and_fusion) | copy-start | bytes 1179652
  604.4 838.7 %copy-start.26 = (bf16[512,2048]{1,0:T(8,128)(2,1)}, bf16[512,2048]{1,0:T(8,128)(2,1)S(1)}, u32[]{:S(2)}) copy-start(bf16[512,2048]{1,0:T(8,128)(2,1)S(1)} %multiply_convert_fusion.5) | copy-start | bytes 6291460
  1921.7 21.1 copy-start.10
  1921.7 21.1 copy-start.13
  1921.8 21.1 copy-start.46
  2030.9 95.7 %collective-permute-start.2 = (f32[2,2,256,8,128]{2,4,3,1,0:T(8,128)S(1)}, f32[2,2,256,8,128]{2,4,3,1,0:T(8,128)S(1)}, u32[]{:S(2)}, u32[]{:S(2)}) collective-permute-start(f32[2,2,256,8,128]{2,4,3,1,0:T(8,128)S(1)} %get-tuple-element.37), channel_id=1, source_target_pairs={{1,0},{2,1},{3,2},{5,4},{6,5},{7,6},{9,8},{10,9},{11,10},{13,12},{... | collective-permute-start | bytes 12582920 | tf_op jit(solution)/shard_map/ppermute | solution.py:17
  2032.2 274.2 %copy-start.25 = (f32[256,128]{0,1:T(8,128)S(1)}, f32[256,128]{0,1:T(8,128)}, u32[]{:S(2)}) copy-start(f32[256,128]{0,1:T(8,128)} %copy-done.23) | copy-start | bytes 393220
  2032.2 271.5 %collective-permute-start.3 = (f32[2,2,256,8,128]{2,4,3,1,0:T(8,128)S(1)}, f32[2,2,256,8,128]{2,4,3,1,0:T(8,128)S(1)}, u32[]{:S(2)}, u32[]{:S(2)}) collective-permute-start(f32[2,2,256,8,128]{2,4,3,1,0:T(8,128)S(1)} %get-tuple-element.38), channel_id=1, source_target_pairs={{2,0},{3,1},{6,4},{7,5},{10,8},{11,9},{14,12},{15,13},{18,16},{19,... | collective-permute-start | bytes 12582920 | tf_op jit(solution)/shard_map/ppermute | solution.py:17
  2319.1 154.7 %reduce-scatter.12.cloned.1.call-start = ((), (), s32[]{:S(2)}) async-start(), calls=%async_computation.16 | async-start | bytes 5242880 | tf_op jit(solution)/shard_map/reduce_scatter | solution.py:266
  2328.3 293.3 %reduce-scatter.14.cloned.1.call-start = ((), (), s32[]{:S(2)}) async-start(), calls=%async_computation.17 | async-start | bytes 10485760 | tf_op jit(solution)/shard_map/reduce_scatter | solution.py:266
  2339.2 430.6 %reduce-scatter.8.cloned.1.call-start = ((), (), s32[]{:S(2)}) async-start(), calls=%async_computation.14 | async-start | bytes 10485760 | tf_op jit(solution)/shard_map/reduce_scatter | solution.py:266
  2367.3 819.9 %reduce-scatter.18.cloned.1.call-start = ((), (), s32[]{:S(2)}) async-start(), calls=%async_computation.19 | async-start | bytes 31457280 | tf_op jit(solution)/shard_map/reduce_scatter | solution.py:192
  2388.3 1217.5 %reduce-scatter.16.cloned.1.call-start = ((), (), s32[]{:S(2)}) async-start(), calls=%async_computation.18 | async-start | bytes 31457280 | tf_op jit(solution)/shard_map/reduce_scatter | solution.py:192
  2407.8 1616.6 %reduce-scatter.20.cloned.1.call-start = ((), (), s32[]{:S(2)}) async-start(), calls=%async_computation.20 | async-start | bytes 31457280 | tf_op jit(solution)/shard_map/reduce_scatter | solution.py:192
  2428.8 1916.0 %all-reduce.4.cloned.1.call-start = ((), (), s32[]{:S(2)}) async-start(), calls=%async_computation.21 | async-start | bytes 50331648 | tf_op jit(solution)/shard_map/psum | solution.py:282
  (56 other events, 298.5 us)
Sparse Core Ops, SparseCore 0:
  9.6 83.4 all-gather.11
  94.7 79.2 all-gather.9
  175.6 233.6 all-gather.13
  410.7 168.3 all-gather.15
  580.5 437.8 all-gather.19
  1019.7 423.3 all-gather.17
  1444.7 423.3 all-gather.21
  2319.3 74.8 reduce-scatter.9
  2396.6 77.2 reduce-scatter.11
  2476.7 144.9 reduce-scatter.13
  2624.6 145.1 reduce-scatter.7
  2772.1 415.1 reduce-scatter.17
  3189.7 416.1 reduce-scatter.15
  3608.1 416.1 reduce-scatter.19
  4030.0 314.7 all-reduce.3
where the time goes:
time: 4390 us; the launch traced here: 4380 us
  waiting for transfers between devices  3460 us (79%)
  blocking collectives  370 us (8%)
  matrix products  356 us (8%)
  other arithmetic  102 us (2%)
  local copies, waits for them, and re-layouts  68.5 us (2%)
    reduce_scatter x7, waiting for transfers between devices, on_device(): lax.psum_scatter(part.astype(jnp.bfloat16), 'shard', scatter_dimension=0,...  1600 us
    all_gather x1, waiting for transfers between devices, on_device(): up_piece = lax.all_gather(w_up, 'shard', axis=0, tiled=True)  414 us
    all_gather x1, waiting for transfers between devices, on_device(): lax.all_gather(w_down, 'shard', axis=0, tiled=True)  404 us
    all_gather x1, waiting for transfers between devices, on_device(): gate_piece = lax.all_gather(w_gate, 'shard', axis=0, tiled=True)  404 us
    all_gather x1, blocking collectives, on_device(): gain_piece = lax.all_gather(mlp_gain, 'shard', axis=0, tiled=True)  312 us
    ppermute x4, waiting for transfers between devices, passed_along(): return lax.ppermute(x, axis, pairs)  270 us
    psum x1, waiting for transfers between devices, on_device(): lax.psum(attn_grads[0].astype(jnp.bfloat16), 'rep').astype(jnp.float32)  230 us
    dot_general x7, matrix products, outer(): jnp.einsum('rc,rf->cf', left, right, preferred_element_type=jnp.float32)  92.4 us
  transfers between devices with their start and end apart: 19, of which 14 were waited for; matrix products, arithmetic and copies ran while one was open for 7% of the time, Pallas kernels for 0%

commit v1 on v0

--- a/solution.py
+++ b/solution.py
@@ -306,9 +306,378 @@
     )
 
 
+CORE, ACROSS_X, ACROSS_Y = 1, 2, 4
+
+
+def across(x, mask):
+    count = lax.axis_size("rep")
+    return lax.ppermute(x, "rep", [(i, i ^ mask) for i in range(count)])
+
+
+def around(x):
+    count = lax.axis_size("shard")
+    return lax.ppermute(x, "shard", [(i, (i + 1) % count) for i in range(count)])
+
+
+def after(x, *done):
+    return lax.optimization_barrier((x, *done))[0]
+
+
+def plane_gather(piece):
+    half = piece.shape[0] // 2
+    from_x = across(piece, ACROSS_X)
+    from_y = across(piece, ACROSS_Y)
+    far = [across(from_x[:half], ACROSS_Y), across(from_y[half:], ACROSS_X)]
+    return [piece, from_x, from_y, jnp.concatenate(far, 0)]
+
+
+def plane_sum(blocks):
+    low = jnp.bfloat16
+    half = blocks[0].shape[0] // 2
+    head = [b[:half] for b in blocks]
+    tail = [b[half:] for b in blocks]
+    head_two = head[2] + across(head[3].astype(low), ACROSS_X)
+    head_own = head[0] + across(head[1].astype(low), ACROSS_X)
+    tail_one = tail[1] + across(tail[3].astype(low), ACROSS_Y)
+    tail_own = tail[0] + across(tail[2].astype(low), ACROSS_Y)
+    head_own = head_own + across(head_two.astype(low), ACROSS_Y)
+    tail_own = tail_own + across(tail_one.astype(low), ACROSS_X)
+    return jnp.concatenate([head_own, tail_own], 0)
+
+
+def sequence_pairs(turn):
+    groups, shards = lax.axis_size("rep"), lax.axis_size("shard")
+    pairs = []
+    for group in range(groups):
+        chip, core = divmod(group, 2)
+        for at in range(shards):
+            to_group, to_shard = 2 * chip + at // 2, 2 * core + (turn ^ (at & 1))
+            pairs.append((group * shards + at, to_group * shards + to_shard))
+    return pairs
+
+
+def to_sequences(x):
+    odd = lax.axis_index("shard") & 1
+    came = [
+        lax.ppermute(
+            lax.dynamic_index_in_dim(x, turn ^ odd, 0, keepdims=False),
+            ("rep", "shard"),
+            sequence_pairs(turn),
+        )
+        for turn in range(2)
+    ]
+    even = odd == 0
+    return jnp.concatenate(
+        [jnp.where(even, came[0], came[1]), jnp.where(even, came[1], came[0])], 0
+    )
+
+
+def from_sequences(x):
+    odd = lax.axis_index("shard") & 1
+    x = x.reshape(2, x.shape[0] // 2, *x.shape[1:])
+    came = [
+        lax.ppermute(
+            lax.dynamic_index_in_dim(x, turn ^ odd, 0, keepdims=False),
+            ("rep", "shard"),
+            [(to, at) for at, to in sequence_pairs(turn)],
+        )
+        for turn in range(2)
+    ]
+    even = odd == 0
+    return jnp.stack([jnp.where(even, came[0], came[1]), jnp.where(even, came[1], came[0])])
+
+
+def column_block(weights, at):
+    cuts = [w.shape[1] // 8 for w in weights]
+    return jnp.concatenate(
+        [lax.dynamic_slice_in_dim(w, at * cut, cut, 1) for w, cut in zip(weights, cuts)], 1
+    )
+
+
+def gather_blocks(weights, first=None):
+    me = lax.axis_index("rep")
+    own = [column_block(weights, me ^ i) for i in range(8)]
+    travelling = own[0] if first is None else after(own[0], first)
+    rows = [[block] for block in own]
+    for _ in range(1, lax.axis_size("shard")):
+        travelling = around(travelling)
+        for i, block in enumerate(plane_gather(travelling)):
+            rows[2 * i].append(block)
+            rows[2 * i + 1].append(across(block, CORE))
+    return jnp.concatenate([jnp.concatenate(r, 0) for r in rows], 1), travelling
+
+
+def rolled(x):
+    count, at = lax.axis_size("shard"), lax.axis_index("shard")
+    width = x.shape[1] // count
+    return jnp.concatenate(
+        [
+            lax.dynamic_slice_in_dim(x, ((at - i) % count) * width, width, 1)
+            for i in range(count)
+        ],
+        1,
+    )
+
+
+def sum_blocks(grad, columns):
+    low = jnp.bfloat16
+    blocks = [grad[:, i * columns : (i + 1) * columns] for i in range(8)]
+    chips = [
+        blocks[2 * i] + across(blocks[2 * i + 1].astype(low), CORE) for i in range(4)
+    ]
+    own = plane_sum(chips)
+    count = lax.axis_size("shard")
+    piece = own.shape[0] // count
+    total = own[piece : 2 * piece]
+    for i in range(2, count + 1):
+        at = i % count
+        total = own[at * piece : (at + 1) * piece] + around(total.astype(low))
+    return total.astype(low)
+
+
+def spread_blocks(block, columns):
+    me = lax.axis_index("rep")
+    pieces = []
+    for piece in plane_gather(block):
+        pieces += [piece, across(piece, CORE)]
+    outs = []
+    start = 0
+    for width in columns:
+        out = jnp.zeros((block.shape[0], 8 * width), jnp.float32)
+        for i, piece in enumerate(pieces):
+            out = lax.dynamic_update_slice_in_dim(
+                out, piece[:, start : start + width].astype(jnp.float32), (me ^ i) * width, 1
+            )
+        outs.append(out)
+        start += width
+    return outs
+
+
+def on_device_block(
+    tokens,
+    lengths,
+    attn_gain,
+    w_query,
+    key_matrix,
+    value_matrix,
+    query_gain,
+    key_gain,
+    w_out,
+    mlp_gain,
+    w_gate,
+    w_up,
+    w_down,
+    cotangent,
+):
+    low, full = jnp.bfloat16, jnp.float32
+    width = tokens.shape[2]
+    head_dim = query_gain.shape[0]
+    heads_q = w_query.shape[1] // head_dim
+    heads_kv = key_matrix.shape[1] // head_dim
+    groups = heads_q // heads_kv
+    scale = head_dim ** (-0.5)
+    owned = width // lax.axis_size("shard")
+    shard_at = lax.axis_index("shard")
+    me = lax.axis_index("rep")
+    core = me & 1
+
+    x_low = to_sequences(tokens)
+    rows = x_low.shape[0]
+    qkv_all, qkv_came = gather_blocks((w_query, key_matrix, value_matrix))
+    out_all, out_came = gather_blocks((w_out,), qkv_came)
+    gate_up_own = lax.all_gather(
+        after(column_block((w_gate, w_up), me), qkv_came), "shard", axis=0, tiled=True
+    )
+    down_own = lax.all_gather(
+        after(column_block((w_down,), me), out_came), "shard", axis=0, tiled=True
+    )
+    gate_up = [gate_up_own, across(gate_up_own, CORE)]
+    down = [down_own, across(down_own, CORE)]
+    grad_y_low = to_sequences(after(cotangent, out_came))
+
+    other_lengths = across(lengths, CORE)
+    both = jnp.where(
+        core == 0,
+        jnp.concatenate([lengths, other_lengths]),
+        jnp.concatenate([other_lengths, lengths]),
+    )
+    length = lax.dynamic_index_in_dim(both, shard_at, 0, keepdims=False)
+    query_pos = core * rows + jnp.arange(rows, dtype=jnp.int32)
+    key_pos = (core - 1) * rows + jnp.arange(2 * rows, dtype=jnp.int32)
+    allowed = (
+        (key_pos[None, :] <= query_pos[:, None])
+        & (query_pos[:, None] - key_pos[None, :] < WINDOW)
+        & (key_pos[None, :] >= 0)
+        & ((key_pos[None, :] < length) | (key_pos[None, :] == query_pos[:, None]))
+    )
+    valid = (query_pos < length)[:, None]
+    cosine_table, sine_table = tables(query_pos, head_dim)
+    cosine_table, sine_table = cosine_table[0], sine_table[0]
+    attn_gains = lax.all_gather(attn_gain, "shard", axis=0, tiled=True).astype(full)
+    mlp_gains = lax.all_gather(mlp_gain, "shard", axis=0, tiled=True).astype(full)
+    query_gains, key_gains = query_gain.astype(full), key_gain.astype(full)
+
+    x_rows = x_low.astype(full)
+    inverse_in = lax.rsqrt(jnp.mean(x_rows * x_rows, -1, keepdims=True) + EPS)
+    x_unit = x_rows * inverse_in
+    normed = rolled((x_unit * attn_gains).astype(low))
+    qkv = jnp.dot(normed, qkv_all, preferred_element_type=full)
+    qkv = qkv.reshape(rows, heads_kv, groups + 2, head_dim)
+    query_unit, query_inverse, query_normed = head_norm(
+        qkv[:, :, :groups].reshape(rows, heads_q, head_dim), query_gains
+    )
+    key_unit, key_inverse, key_normed = head_norm(qkv[:, :, groups], key_gains)
+    query_rows = (query_normed * cosine_table + rotated_rows(query_normed) * sine_table).astype(low)
+    query_rows = query_rows.reshape(rows, heads_kv, groups, head_dim)
+    keys_own = (key_normed * cosine_table + rotated_rows(key_normed) * sine_table).astype(low)
+    values_own = qkv[:, :, groups + 1].astype(low)
+    own_pair = jnp.stack([keys_own, values_own])
+    count = lax.axis_size("rep")
+
+    def other_order(x):
+        pairs = x.reshape(*x.shape[:2], heads_kv // 2, 2, head_dim)
+        return pairs[:, :, :, ::-1].reshape(x.shape)
+
+    earlier = lax.ppermute(
+        other_order(own_pair), "rep", [(i, i + 1) for i in range(0, count, 2)]
+    )
+    keys, values = jnp.concatenate([earlier, own_pair], 1)
+
+    def masked_scores():
+        raw = jnp.einsum("qhgd,khd->hgqk", query_rows, keys, preferred_element_type=full) * scale
+        return jnp.where(allowed[None, None], raw, NEG)
+
+    score = masked_scores()
+    top = jnp.max(score, -1, keepdims=True)
+    expo = jnp.exp(score - top)
+    total = jnp.sum(expo, -1, keepdims=True)
+    prob = expo / total
+    log_total = top + jnp.log(total)
+    mixed = jnp.einsum("hgqk,khd->qhgd", prob.astype(low), values, preferred_element_type=full)
+    mixed = mixed.reshape(rows, heads_q * head_dim).astype(low)
+    branch = jnp.einsum("rf,nf->rn", mixed, out_all, preferred_element_type=full)
+
+    resid = x_rows + rolled(branch)
+    inverse_mid = lax.rsqrt(jnp.mean(resid * resid, -1, keepdims=True) + EPS)
+    mid_unit = resid * inverse_mid
+    mid = (mid_unit * mlp_gains).astype(low)
+
+    grad_y_low = jnp.where(valid, grad_y_low, jnp.zeros_like(grad_y_low))
+    grad_y_all = jnp.concatenate(plane_gather(grad_y_low), 0)
+    mid_all = jnp.concatenate(plane_gather(after(mid, grad_y_all)), 0)
+
+    acts, grads_pre = [], []
+    for part in range(2):
+        pre = jnp.dot(mid_all, gate_up[part], preferred_element_type=full)
+        gate, up = jnp.split(pre, 2, 1)
+        sigma = jax.nn.sigmoid(gate)
+        swish = gate * sigma
+        acts.append((swish * up).astype(low))
+        grad_act = jnp.dot(grad_y_all, down[part], preferred_element_type=full)
+        grad_gate = (grad_act * up * sigma * (1.0 + gate * (1.0 - sigma))).astype(low)
+        grad_up = (grad_act * swish).astype(low)
+        grads_pre.append(jnp.concatenate([grad_gate, grad_up], 1))
+
+    def both_parts(left, right):
+        return sum(
+            jnp.einsum("rf,nf->rn", l, r, preferred_element_type=full) for l, r in zip(left, right)
+        )
+
+    grad_mid_parts = both_parts(grads_pre, gate_up)
+    grad_mid = plane_sum(jnp.split(grad_mid_parts, 4, 0))
+    mlp_out = plane_sum(jnp.split(after(both_parts(acts, down), grad_mid), 4, 0))
+    output = from_sequences(jnp.where(valid, resid + mlp_out, 0.0).astype(low))
+
+    def mlp_weight_grad(left, parts):
+        other = outer(left, parts[1]).astype(low)
+        own = outer(left, parts[0]) + across(other, CORE)
+        return lax.psum_scatter(own.astype(low), "shard", scatter_dimension=0, tiled=True)
+
+    gate_up_grad = mlp_weight_grad(mid_all, grads_pre)
+    down_grad = mlp_weight_grad(grad_y_all, acts)
+    grad_gate_total, grad_up_total = spread_blocks(
+        gate_up_grad, (gate_up_grad.shape[1] // 2,) * 2
+    )
+    (grad_down_total,) = spread_blocks(down_grad, (down_grad.shape[1],))
+
+    mlp_gain_part = jnp.sum(mid_unit * grad_mid, 0)
+    grad_resid = grad_y_low.astype(full) + norm_back(mid_unit, inverse_mid, grad_mid * mlp_gains)
+    resid_low = rolled(grad_resid.astype(low))
+    grad_mixed = jnp.dot(resid_low, out_all, preferred_element_type=full).astype(low)
+    grad_out_all = outer(resid_low, mixed)
+    grad_mixed = grad_mixed.reshape(rows, heads_kv, groups, head_dim)
+    prob_again = jnp.exp(masked_scores() - log_total)
+    grad_prob = jnp.einsum("qhgd,khd->hgqk", grad_mixed, values, preferred_element_type=full)
+    grad_values = jnp.einsum(
+        "hgqk,qhgd->khd", prob_again.astype(low), grad_mixed, preferred_element_type=full
+    )
+    grad_score = (
+        prob_again * (grad_prob - jnp.sum(prob_again * grad_prob, -1, keepdims=True))
+    ).astype(low)
+    grad_queries = (
+        jnp.einsum("hgqk,khd->qhgd", grad_score, keys, preferred_element_type=full) * scale
+    )
+    grad_keys = (
+        jnp.einsum("hgqk,qhgd->khd", grad_score, query_rows, preferred_element_type=full) * scale
+    )
+    grad_pair = jnp.stack([grad_keys, grad_values])
+    own_grad = grad_pair[:, rows:] + lax.ppermute(
+        other_order(grad_pair[:, :rows].astype(low)), "rep", [(i + 1, i) for i in range(0, count, 2)]
+    )
+    grad_query_post = grad_queries.reshape(rows, heads_q, head_dim)
+    grad_query_normed = grad_query_post * cosine_table - rotated_rows(grad_query_post * sine_table)
+    grad_key_normed = own_grad[0] * cosine_table - rotated_rows(own_grad[0] * sine_table)
+    grad_query_raw = norm_back(query_unit, query_inverse, grad_query_normed * query_gains)
+    grad_key_raw = norm_back(key_unit, key_inverse, grad_key_normed * key_gains)
+    query_gain_part = jnp.sum(query_unit * grad_query_normed, axis=(0, 1))
+    key_gain_part = jnp.sum(key_unit * grad_key_normed, axis=(0, 1))
+    grad_qkv = jnp.concatenate(
+        [
+            grad_query_raw.reshape(rows, heads_kv, groups, head_dim).astype(low),
+            grad_key_raw[:, :, None].astype(low),
+            own_grad[1][:, :, None].astype(low),
+        ],
+        2,
+    ).reshape(rows, -1)
+    grad_in = rolled(jnp.einsum("rf,nf->rn", grad_qkv, qkv_all, preferred_element_type=full))
+    grad_tokens = from_sequences(
+        (grad_resid + norm_back(x_unit, inverse_in, grad_in * attn_gains)).astype(low)
+    )
+    attn_gain_part = jnp.sum(x_unit * grad_in, 0)
+
+    out_block = w_out.shape[1] // 8
+    qkv_block = qkv_all.shape[1] // 8
+    (grad_out_total,) = spread_blocks(sum_blocks(grad_out_all, out_block), (out_block,))
+    grad_query_total, grad_key_total, grad_value_total = spread_blocks(
+        sum_blocks(outer(normed, grad_qkv), qkv_block),
+        (groups * head_dim, head_dim, head_dim),
+    )
+    gain_grads = lax.psum(
+        (query_gain_part, key_gain_part, attn_gain_part, mlp_gain_part), ("rep", "shard")
+    )
+    attn_gain_total = lax.dynamic_slice_in_dim(gain_grads[2], shard_at * owned, owned, 0)
+    mlp_gain_total = lax.dynamic_slice_in_dim(gain_grads[3], shard_at * owned, owned, 0)
+    return (
+        output,
+        grad_tokens,
+        attn_gain_total,
+        grad_query_total,
+        grad_key_total,
+        grad_value_total,
+        gain_grads[0],
+        gain_grads[1],
+        grad_out_total,
+        mlp_gain_total,
+        grad_gate_total,
+        grad_up_total,
+        grad_down_total,
+    )
+
+
 def solution(mesh):
+    sizes = (mesh.shape["rep"], mesh.shape["shard"])
     return jax.shard_map(
-        on_device,
+        on_device_block if sizes == (8, 4) else on_device,
         mesh=mesh,
         in_specs=(
             P("rep", "shard", None),

time: 4390 us -> 1570 us (0.36)
  waiting for transfers between devices: 3460 us -> 403 us
  blocking collectives: 370 us -> 183 us
  starting transfers between devices: 10.2 us -> 176 us
  other arithmetic: 102 us -> 251 us
  local copies, waits for them, and re-layouts: 68.5 us -> 166 us
    reduce_scatter x7 -> x2, waiting for transfers between devices: 1600 us -> 0.01 us  [mlp_weight_grad(): lax.psum_scatter(own.astype(low), 'shard', scatter_dimension=0, tiled=True)]
    all_gather x7 -> x2, waiting for transfers between devices: 1360 us -> 0.01 us  [the longest x1 0.01 us: on_device_block(): lax.all_gather(after(column_block((w_down,), me), out_came), 'shard', axi...]
    psum x1 -> x0, waiting for transfers between devices: 230 us -> none  [on_device(): lax.psum(attn_grads[0].astype(jnp.bfloat16), 'rep').astype(jnp.float32)]
    all_gather x2, blocking collectives: 325 us -> 113 us  [the longest x1 100 us: on_device_block(): lax.all_gather(attn_gain, 'shard', axis=0, tiled=True).astype(full)]
    ppermute x4 -> x147, starting transfers between devices: 8.83 us -> 175 us  [the longest x125 96.5 us: across(): return lax.ppermute(x, 'rep', [(i, i ^ mask) for i in range(count)])]
    ppermute x4 -> x147, waiting for transfers between devices: 270 us -> 403 us  [the longest x125 258 us: across(): return lax.ppermute(x, 'rep', [(i, i ^ mask) for i in range(count)])]
    unnamed x142 -> x392, local copies, waits for them, and re-layouts: 17.7 us -> 70.6 us
    dot_general x20 -> x18, matrix products: 263 us -> 270 us  [the longest x4 67.4 us: both_parts(): jnp.einsum('rf,nf->rn', l, r, preferred_element_type=full)]
  transfers between devices with their start and end apart: 19 -> 151, of which waited for: 14 -> 48; matrix products, arithmetic and copies ran while one was open for 7% -> 42% of each run, Pallas kernels for 0% -> 0%
where the time goes in v1:
time: 1570 us; the launch traced here: 1560 us
  waiting for transfers between devices  403 us (26%)
  matrix products  366 us (23%)
  other arithmetic  251 us (16%)
  blocking collectives  183 us (12%)
  starting transfers between devices  176 us (11%)
  local copies, waits for them, and re-layouts  166 us (11%)
  between operations  17.1 us (1%)
    ppermute x125, waiting for transfers between devices, across(): return lax.ppermute(x, 'rep', [(i, i ^ mask) for i in range(count)])  258 us
    ppermute x12, waiting for transfers between devices, around(): lax.ppermute(x, 'shard', [(i, (i + 1) % count) for i in range(count)])  113 us
    all_gather x1, blocking collectives, on_device_block(): lax.all_gather(attn_gain, 'shard', axis=0, tiled=True).astype(full)  100 us
    dot_general x6, matrix products, outer(): jnp.einsum('rc,rf->cf', left, right, preferred_element_type=jnp.float32)  96.6 us
    ppermute x125, starting transfers between devices, across(): return lax.ppermute(x, 'rep', [(i, i ^ mask) for i in range(count)])  96.5 us
    unnamed x392, local copies, waits for them, and re-layouts  70.6 us
    psum x1, blocking collectives, on_device_block(): lax.psum((query_gain_part, key_gain_part, attn_gain_part, mlp_gain_part),...  70.2 us
    dot_general x4, matrix products, both_parts(): jnp.einsum('rf,nf->rn', l, r, preferred_element_type=full)  67.4 us
  transfers between devices with their start and end apart: 151, of which 48 were waited for; matrix products, arithmetic and copies ran while one was open for 42% of the time, Pallas kernels for 0%

profile of v1, /device:TPU:0, one launch (start us, length us, event | category | flops | bytes accessed | tf_op | source)
XLA Modules:
  0.0 1561.5 jit_solution(7280068445917519862)
XLA Ops:
  15.7 14.1 collective-permute-done.3
  29.7 15.2 collective-permute-done.4
  46.2 13.1 collective-permute-done.5
  88.0 100.1 %all-gather = bf16[4,1,512]{2,1,0:T(2,128)(2,1)S(1)} all-gather(bf16[1,1,512]{2,1,0:T(2,128)(2,1)S(1)} %reshape.632), channel_id=1, replica_groups=mesh['rep'=8,'shard'=4] {'shard'}, dimensions={0}, use_global_device_ids=true | all-gather | bytes 5120 | tf_op jit(solution)/shard_map/all_gather | solution.py:516
  420.7 13.6 fusion.9
  434.3 14.3 fusion.3
  448.6 15.6 %fusion.75 = bf16[8,128,2,512]{3,1,2,0:T(8,128)(2,1)S(1)} fusion(f32[8,2,512]{2,1,0:T(2,128)S(1)} %fusion.3, f32[8,2,512]{2,1,0:T(2,128)S(1)} %get-tuple-element.195, f32[8,1024,512,2]{2,1,3,0:T(8,128)} %get-tuple-element.196, pred[512,1024]{0,1:T(8,128)(4,1)S(1)} %fusion.74, bf16[2,1024,8,128]{3,1,2,0:T(8,128)(2,1)} %copy-done.22), kind=kOutput, calls=%fused_computation.191 | convolution fusion | flops 2190475264 | bytes 38338560 | tf_op jit(solution)/shard_map/hgqk,khd->qhgd/dot_general | solution.py:556
  515.1 38.0 %collective-permute-done.64 = bf16[512,2048]{1,0:T(8,128)(2,1)} collective-permute-done((bf16[512,2048]{1,0:T(8,128)(2,1)}, bf16[512,2048]{1,0:T(8,128)(2,1)}, u32[]{:S(2)}, u32[]{:S(2)}) %collective-permute-start.64) | collective-permute-done | bytes 2097184 | tf_op jit(solution)/shard_map/ppermute | solution.py:314
  581.8 19.1 %fusion.126 = f32[2048,1536]{0,1:T(8,128)} fusion(bf16[2048,2048]{1,0:T(8,128)(2,1)} %constant_dynamic-update-slice_fusion.5, bf16[2048,1536]{1,0:T(8,128)(2,1)} %all-gather.5.cloned.1.call-done), kind=kOutput, calls=%fused_computation.443 | convolution fusion | flops 12884901888 | bytes 27262976 | tf_op jit(solution)/shard_map/dot_general | solution.py:571
  601.0 17.6 %multiply_convert_fusion.3 = (bf16[2048,768]{0,1:T(8,128)(2,1)}, bf16[2048,768]{0,1:T(8,128)(2,1)}, bf16[2048,768]{0,1:T(8,128)(2,1)}) fusion(f32[2048,1536]{0,1:T(8,128)} %fusion.126, bf16[2048,2048]{1,0:T(8,128)(2,1)} %constant_dynamic-update-slice_fusion, bf16[2048,768]{1,0:T(8,128)(2,1)S(1)} %copy-done.167), kind=kOutput, calls=%fused_computation.27 | convolution fusion | flops 6466043904 | bytes 33554432 | tf_op jit(solution)/shard_map/dot_general | solution.py:576
  618.6 19.0 %fusion.127 = f32[2048,1536]{0,1:T(8,128)} fusion(bf16[2048,2048]{1,0:T(8,128)(2,1)} %constant_dynamic-update-slice_fusion.5, bf16[2048,1536]{1,0:T(8,128)(2,1)} %collective-permute-done.68), kind=kOutput, calls=%fused_computation.444 | convolution fusion | flops 12884901888 | bytes 27262976 | tf_op jit(solution)/shard_map/dot_general | solution.py:571
  637.6 17.3 %multiply_convert_fusion.1 = (bf16[2048,768]{0,1:T(8,128)(2,1)S(1)}, bf16[2048,768]{0,1:T(8,128)(2,1)}, bf16[2048,768]{0,1:T(8,128)(2,1)}) fusion(f32[2048,1536]{0,1:T(8,128)} %fusion.127, bf16[2048,2048]{1,0:T(8,128)(2,1)} %constant_dynamic-update-slice_fusion, bf16[2048,768]{1,0:T(8,128)(2,1)} %collective-permute-done.69), kind=kOutput, calls=%fused_computation.25 | convolution fusion | flops 6466043904 | bytes 33554432 | tf_op jit(solution)/shard_map/dot_general | solution.py:576
  656.6 19.4 %convolution_convert_fusion = bf16[2048,1536]{1,0:T(8,128)(2,1)} fusion(bf16[2048,2048]{1,0:T(8,128)(2,1)} %constant_dynamic-update-slice_fusion.5, bf16[2048,768]{0,1:T(8,128)(2,1)} %get-tuple-element.51, bf16[2048,768]{0,1:T(8,128)(2,1)S(1)} %get-tuple-element.50), kind=kOutput, calls=%fused_computation.19 | convolution fusion | flops 12900630528 | bytes 20971520 | tf_op jit(solution)/shard_map/rc,rf->cf/dot_general | solution.py:57
  676.0 20.2 %fusion.24 = f32[2048,2048]{1,0:T(8,128)} fusion(bf16[2048,1536]{1,0:T(8,128)(2,1)} %collective-permute-done.68, bf16[2048,768]{0,1:T(8,128)(2,1)S(1)} %copy-done.176, bf16[2048,768]{0,1:T(8,128)(2,1)} %copy-done.175), kind=kOutput, calls=%fused_computation.80 | convolution fusion | flops 12897484800 | bytes 29360128 | tf_op jit(solution)/shard_map/rf,nf->rn/dot_general | solution.py:583
  696.2 20.6 %fusion.122 = (bf16[2048,2048]{1,0:T(8,128)(2,1)S(1)}, f32[2048,2048]{1,0:T(8,128)}) fusion(f32[2048,2048]{1,0:T(8,128)} %fusion.24, bf16[2048,1536]{1,0:T(8,128)(2,1)} %all-gather.5.cloned.1.call-done, bf16[2048,768]{0,1:T(8,128)(2,1)} %get-tuple-element.49, bf16[2048,768]{0,1:T(8,128)(2,1)S(1)} %copy-done.173), kind=kOutput, calls=%fused_computation.439 | convolution fusion | flops 12905873408 | bytes 54525952 | tf_op jit(solution)/shard_map/rf,nf->rn/dot_general | solution.py:583
  748.4 14.6 convolution_add_fusion.1
  764.9 23.9 %collective-permute-done.72 = bf16[256,2048]{1,0:T(8,128)(2,1)S(1)} collective-permute-done((bf16[256,2048]{1,0:T(8,128)(2,1)S(1)}, bf16[256,2048]{1,0:T(8,128)(2,1)S(1)}, u32[]{:S(2)}, u32[]{:S(2)}) %collective-permute-start.72) | collective-permute-done | bytes 1048608 | tf_op jit(solution)/shard_map/ppermute | solution.py:314
  838.0 24.1 %fusion = (f32[8,2,512]{2,1,0:T(2,128)}, f32[8,1024,512,2]{2,1,3,0:T(8,128)}) fusion(f32[8,2,512]{2,1,0:T(2,128)S(1)} %bitcast.260, f32[8,1024,512,2]{2,1,3,0:T(8,128)} %get-tuple-element.196, pred[512,1024]{0,1:T(8,128)(4,1)S(1)} %copy-done.18, bf16[512,8,2,128]{0,3,2,1:T(8,128)(2,1)S(1)} %bitcast.238, bf16[2,1024,8,128]{3,1,2,0:T(8,128)(2,1)} %copy-done.22), kind=kOutput, calls=%fused_computation.2 | convolution fusion | flops 2189418496 | bytes 71892992 | tf_op jit(solution)/shard_map/qhgd,khd->hgqk/dot_general | solution.py:610
  862.2 16.1 %fusion.25 = f32[1,1024,8,128]{3,1,2,0:T(8,128)} fusion(bf16[512,8,2,128]{0,3,2,1:T(8,128)(2,1)S(1)} %bitcast.239, f32[8,2,512]{2,1,0:T(2,128)S(1)} %bitcast.261, f32[8,1024,512,2]{2,1,3,0:T(8,128)} %get-tuple-element.196, pred[512,1024]{0,1:T(8,128)(4,1)S(1)} %copy-done.18), kind=kOutput, calls=%fused_computation.83 | convolution fusion | flops 2181038080 | bytes 40402944 | tf_op jit(solution)/shard_map/hgqk,qhgd->khd/dot_general | solution.py:611
  878.2 28.5 %fusion.2 = bf16[8,2,512,1024]{2,3,1,0:T(8,128)(2,1)} fusion(f32[8,1024,512,2]{2,1,3,0:T(8,128)} %get-tuple-element.200, f32[8,2,512]{2,1,0:T(2,128)} %get-tuple-element.199, f32[8,2,512]{2,1,0:T(2,128)} %bitcast.259, f32[8,1024,512,2]{2,1,3,0:T(8,128)} %get-tuple-element.196, pred[512,1024]{0,1:T(8,128)(4,1)S(1)} %copy-done.18), kind=kLoop, calls=%fused_computation.4 | loop fusion | flops 50331648 | bytes 84475904 | tf_op jit(solution)/shard_map/convert_element_type | solution.py:616
  979.3 14.1 collective-permute-done.77
  1024.8 13.3 fusion.129
  1042.2 21.6 %fusion.123 = (bf16[2048,4096]{1,0:T(8,128)(2,1)}, f32[2048,4096]{1,0:T(8,128)}) fusion(bf16[512,4096]{0,1:T(8,128)(2,1)} %bitcast.227, bf16[512,512]{1,0:T(8,128)(2,1)} %copy-done.63, bf16[512,512]{1,0:T(8,128)(2,1)} %copy-done.64, bf16[512,512]{1,0:T(8,128)(2,1)} %copy-done.65, bf16[512,512]{1,0:T(8,128)(2,1)} %copy-done.62), kind=kOutput, calls=%fused_computation.440 | convolution fusion | flops 8606711808 | bytes 56623104 | tf_op jit(solution)/shard_map/rc,rf->cf/dot_general | solution.py:57
  1082.0 70.2 %all-reduce = (f32[2048]{0:T(1024)S(1)}, f32[128]{0:T(128)}, f32[128]{0:T(128)}, f32[2048]{0:T(1024)S(1)}) all-reduce(f32[2048]{0:T(1024)S(1)} %get-tuple-element.29, f32[128]{0:T(128)S(1)} %copy-done.163, f32[128]{0:T(128)S(1)} %copy-done.164, f32[2048]{0:T(1024)S(1)} %copy-done.155), channel_id=1, replica_groups=mesh['rep'=8,'shard'=4] {'rep','shard'}, use_global_device_ids=true, to_apply=%region_12.13 | all-reduce | flops 4352 | bytes 34816 | tf_op jit(solution)/shard_map/psum | solution.py:655
  1171.6 31.4 %collective-permute-done.120 = bf16[512,256]{1,0:T(8,128)(2,1)S(1)} collective-permute-done((bf16[512,256]{1,0:T(8,128)(2,1)S(1)}, bf16[512,256]{1,0:T(8,128)(2,1)S(1)}, u32[]{:S(2)}, u32[]{:S(2)}) %collective-permute-start.120) | collective-permute-done | bytes 262176 | tf_op jit(solution)/shard_map/ppermute | solution.py:319
  1209.8 19.2 %add_convert_fusion = bf16[2048,1536]{1,0:T(8,128)(2,1)} fusion(bf16[2048,1536]{1,0:T(8,128)(2,1)} %collective-permute-done.129, bf16[2048,2048]{1,0:T(8,128)(2,1)} %constant_dynamic-update-slice_fusion.5, bf16[2048,768]{0,1:T(8,128)(2,1)} %get-tuple-element.49, bf16[2048,768]{0,1:T(8,128)(2,1)S(1)} %copy-done.174), kind=kOutput, calls=%fused_computation.14 | convolution fusion | flops 12906921984 | bytes 27262976 | tf_op jit(solution)/shard_map/rc,rf->cf/dot_general | solution.py:57
  1239.6 14.5 slice_add_fusion.2
  1262.5 19.7 %collective-permute-done.126 = bf16[256,256]{1,0:T(8,128)(2,1)S(1)} collective-permute-done((bf16[256,256]{1,0:T(8,128)(2,1)S(1)}, bf16[256,256]{1,0:T(8,128)(2,1)S(1)}, u32[]{:S(2)}, u32[]{:S(2)}) %collective-permute-start.126) | collective-permute-done | bytes 131104 | tf_op jit(solution)/shard_map/ppermute | solution.py:314
  1292.5 16.7 %collective-permute-done.94 = bf16[1024,512]{1,0:T(8,128)(2,1)S(1)} collective-permute-done((bf16[1024,512]{1,0:T(8,128)(2,1)S(1)}, bf16[1024,512]{1,0:T(8,128)(2,1)S(1)}, u32[]{:S(2)}, u32[]{:S(2)}) %collective-permute-start.94) | collective-permute-done | bytes 1048608 | tf_op jit(solution)/shard_map/ppermute | solution.py:314
  1345.9 32.1 %collective-permute-done.83 = bf16[256,2048]{1,0:T(8,128)(2,1)S(1)} collective-permute-done((bf16[256,2048]{1,0:T(8,128)(2,1)S(1)}, bf16[256,2048]{1,0:T(8,128)(2,1)S(1)}, u32[]{:S(2)}, u32[]{:S(2)}) %collective-permute-start.83) | collective-permute-done | bytes 1048608 | tf_op jit(solution)/shard_map/ppermute | solution.py:379
  1395.4 27.5 %collective-permute-start.98 = (bf16[512,512]{1,0:T(8,128)(2,1)S(1)}, bf16[512,512]{1,0:T(8,128)(2,1)S(1)}, u32[]{:S(2)}, u32[]{:S(2)}) collective-permute-start(bf16[512,512]{1,0:T(8,128)(2,1)S(1)} %fusion.85), channel_id=1, source_target_pairs={{0,1},{1,2},{2,3},{3,0},{4,5},{5,6},{6,7},{7,4},{8,9},{9,10},{10,1... | collective-permute-start | bytes 1572872 | tf_op jit(solution)/shard_map/ppermute | solution.py:319
  1489.8 25.5 %collective-permute-done.131 = bf16[512,1536]{1,0:T(8,128)(2,1)S(1)} collective-permute-done((bf16[512,1536]{1,0:T(8,128)(2,1)}, bf16[512,1536]{1,0:T(8,128)(2,1)S(1)}, u32[]{:S(2)}, u32[]{:S(2)}) %collective-permute-start.131) | collective-permute-done | bytes 1572896 | tf_op jit(solution)/shard_map/ppermute | solution.py:314
  (930 shorter events, 774.3 us)
Async XLA Ops:
  7.2 556.0 %all-gather.7.cloned.1.call-start = ((), (), s32[]{:S(2)}) async-start(), calls=%async_computation.3 | async-start | bytes 3932160 | tf_op jit(solution)/shard_map/all_gather | solution.py:491
  84.5 494.9 %all-gather.5.cloned.1.call-start = ((), (), s32[]{:S(2)}) async-start(), calls=%async_computation.2 | async-start | bytes 7864320 | tf_op jit(solution)/shard_map/all_gather | solution.py:488
  84.5 127.2 %collective-permute-start = (s32[2]{0:T(128)}, s32[2]{0:T(128)}, u32[]{:S(2)}, u32[]{:S(2)}) collective-permute-start(s32[2]{0:T(128)} %param.15), channel_id=1, source_target_pairs={{0,4},{4,0},{8,12},{12,8},{16,20},{20,16},{24,28},{28,24},{1,5},{5... | collective-permute-start | bytes 32 | tf_op jit(solution)/shard_map/ppermute | solution.py:314
  86.1 139.1 %collective-permute-start.1 = (bf16[256,2048]{1,0:T(8,128)(2,1)}, bf16[256,2048]{1,0:T(8,128)(2,1)S(1)}, u32[]{:S(2)}, u32[]{:S(2)}) collective-permute-start(bf16[256,2048]{1,0:T(8,128)(2,1)} %get-tuple-element.136), channel_id=1, source_target_pairs={{0,0},{1,1},{2,4},{3,5},{4,2},{5,3},{6,6},{7,7},{8,8},{9,9},{10,12... | collective-permute-start | bytes 3145736 | tf_op jit(solution)/shard_map/ppermute | solution.py:362
  88.0 139.0 %collective-permute-start.2 = (bf16[256,2048]{1,0:T(8,128)(2,1)}, bf16[256,2048]{1,0:T(8,128)(2,1)S(1)}, u32[]{:S(2)}, u32[]{:S(2)}) collective-permute-start(bf16[256,2048]{1,0:T(8,128)(2,1)} %get-tuple-element.137), channel_id=1, source_target_pairs={{0,1},{1,0},{2,5},{3,4},{4,3},{5,2},{6,7},{7,6},{8,9},{9,8},{10,13... | collective-permute-start | bytes 3145736 | tf_op jit(solution)/shard_map/ppermute | solution.py:362
  246.8 1132.3 %reduce-scatter.5.cloned.1.call-start = ((), (), s32[]{:S(2)}) async-start(), calls=%async_computation.5 | async-start | bytes 3932160 | tf_op jit(solution)/shard_map/reduce_scatter | solution.py:594
  315.9 94.6 %collective-permute-start.55 = (bf16[512,256]{1,0:T(8,128)(2,1)}, bf16[512,256]{1,0:T(8,128)(2,1)}, u32[]{:S(2)}, u32[]{:S(2)}) collective-permute-start(bf16[512,256]{1,0:T(8,128)(2,1)} %pad_maximum_fusion.40), channel_id=1, source_target_pairs={{0,4},{4,0},{8,12},{12,8},{16,20},{20,16},{24,28},{28,24},{1,5},{5... | collective-permute-start | bytes 786440 | tf_op jit(solution)/shard_map/ppermute | solution.py:314
  316.3 97.9 %collective-permute-start.58 = (bf16[256,2048]{1,0:T(8,128)(2,1)}, bf16[256,2048]{1,0:T(8,128)(2,1)}, u32[]{:S(2)}, u32[]{:S(2)}) collective-permute-start(bf16[256,2048]{1,0:T(8,128)(2,1)} %get-tuple-element.117), channel_id=1, source_target_pairs={{0,0},{1,1},{2,4},{3,5},{4,2},{5,3},{6,6},{7,7},{8,8},{9,9},{10,12... | collective-permute-start | bytes 3145736 | tf_op jit(solution)/shard_map/ppermute | solution.py:362
  327.0 87.2 %collective-permute-start.59 = (bf16[256,2048]{1,0:T(8,128)(2,1)}, bf16[256,2048]{1,0:T(8,128)(2,1)}, u32[]{:S(2)}, u32[]{:S(2)}) collective-permute-start(bf16[256,2048]{1,0:T(8,128)(2,1)} %get-tuple-element.118), channel_id=1, source_target_pairs={{0,1},{1,0},{2,5},{3,4},{4,3},{5,2},{6,7},{7,6},{8,9},{9,8},{10,13... | collective-permute-start | bytes 3145736 | tf_op jit(solution)/shard_map/ppermute | solution.py:362
  327.3 84.6 %collective-permute-start.56 = (bf16[512,256]{1,0:T(8,128)(2,1)}, bf16[512,256]{1,0:T(8,128)(2,1)}, u32[]{:S(2)}, u32[]{:S(2)}) collective-permute-start(bf16[512,256]{1,0:T(8,128)(2,1)} %pad_maximum_fusion.41), channel_id=1, source_target_pairs={{0,4},{4,0},{8,12},{12,8},{16,20},{20,16},{24,28},{28,24},{1,5},{5... | collective-permute-start | bytes 786440 | tf_op jit(solution)/shard_map/ppermute | solution.py:314
  419.0 57.4 %collective-permute-start.60 = (bf16[512,2048]{1,0:T(8,128)(2,1)}, bf16[512,2048]{1,0:T(8,128)(2,1)}, u32[]{:S(2)}, u32[]{:S(2)}) collective-permute-start(bf16[512,2048]{1,0:T(8,128)(2,1)} %get-tuple-element.41), channel_id=1, source_target_pairs={{0,8},{4,12},{8,0},{12,4},{16,24},{20,28},{24,16},{28,20},{1,9},{5... | collective-permute-start | bytes 6291464 | tf_op jit(solution)/shard_map/ppermute | solution.py:314
  419.4 60.2 %collective-permute-start.61 = (bf16[512,2048]{1,0:T(8,128)(2,1)}, bf16[512,2048]{1,0:T(8,128)(2,1)}, u32[]{:S(2)}, u32[]{:S(2)}) collective-permute-start(bf16[512,2048]{1,0:T(8,128)(2,1)} %get-tuple-element.41), channel_id=1, source_target_pairs={{0,16},{4,20},{8,24},{12,28},{16,0},{20,4},{24,8},{28,12},{1,17},{... | collective-permute-start | bytes 6291464 | tf_op jit(solution)/shard_map/ppermute | solution.py:314
  508.3 48.7 %collective-permute-start.65 = (bf16[512,2048]{1,0:T(8,128)(2,1)}, bf16[512,2048]{1,0:T(8,128)(2,1)}, u32[]{:S(2)}, u32[]{:S(2)}) collective-permute-start(bf16[512,2048]{1,0:T(8,128)(2,1)} %multiply_convert_fusion.7), channel_id=1, source_target_pairs={{0,16},{4,20},{8,24},{12,28},{16,0},{20,4},{24,8},{28,12},{1,17},{... | collective-permute-start | bytes 6291464 | tf_op jit(solution)/shard_map/ppermute | solution.py:314
  563.2 74.4 %collective-permute-start.69 = (bf16[2048,768]{1,0:T(8,128)(2,1)}, bf16[2048,768]{1,0:T(8,128)(2,1)}, u32[]{:S(2)}, u32[]{:S(2)}) collective-permute-start(bf16[2048,768]{1,0:T(8,128)(2,1)} %all-gather.7.cloned.1.call-done), channel_id=1, source_target_pairs={{0,4},{4,0},{8,12},{12,8},{16,20},{20,16},{24,28},{28,24},{1,5},{5... | collective-permute-start | bytes 9437192 | tf_op jit(solution)/shard_map/ppermute | solution.py:314
  721.3 85.0 %collective-permute-start.73 = (bf16[256,2048]{1,0:T(8,128)(2,1)}, bf16[256,2048]{1,0:T(8,128)(2,1)}, u32[]{:S(2)}, u32[]{:S(2)}) collective-permute-start(bf16[256,2048]{1,0:T(8,128)(2,1)} %get-tuple-element.76), channel_id=1, source_target_pairs={{0,16},{4,20},{8,24},{12,28},{16,0},{20,4},{24,8},{28,12},{1,17},{... | collective-permute-start | bytes 3145736 | tf_op jit(solution)/shard_map/ppermute | solution.py:314
  733.2 60.3 %collective-permute-start.138 = (bf16[2048,768]{1,0:T(8,128)(2,1)}, bf16[2048,768]{1,0:T(8,128)(2,1)}, u32[]{:S(2)}, u32[]{:S(2)}) collective-permute-start(bf16[2048,768]{1,0:T(8,128)(2,1)} %convolution_convert_fusion.1), channel_id=1, source_target_pairs={{0,4},{4,0},{8,12},{12,8},{16,20},{20,16},{24,28},{28,24},{1,5},{5... | collective-permute-start | bytes 9437192 | tf_op jit(solution)/shard_map/ppermute | solution.py:314
  764.9 442.1 %collective-permute-start.129 = (bf16[2048,1536]{1,0:T(8,128)(2,1)}, bf16[2048,1536]{1,0:T(8,128)(2,1)}, u32[]{:S(2)}, u32[]{:S(2)}) collective-permute-start(bf16[2048,1536]{1,0:T(8,128)(2,1)} %convolution_convert_fusion), channel_id=1, source_target_pairs={{0,4},{4,0},{8,12},{12,8},{16,20},{20,16},{24,28},{28,24},{1,5},{5... | collective-permute-start | bytes 18874376 | tf_op jit(solution)/shard_map/ppermute | solution.py:314
  806.3 672.0 %reduce-scatter.3.cloned.1.call-start = ((), (), s32[]{:S(2)}) async-start(), calls=%async_computation.4 | async-start | bytes 7864320 | tf_op jit(solution)/shard_map/reduce_scatter | solution.py:594
  978.1 93.9 %collective-permute-start.110 = (bf16[1024,256]{1,0:T(8,128)(2,1)}, bf16[1024,256]{1,0:T(8,128)(2,1)}, u32[]{:S(2)}, u32[]{:S(2)}) collective-permute-start(bf16[1024,256]{1,0:T(8,128)(2,1)} %slice.859), channel_id=1, source_target_pairs={{0,8},{4,12},{8,0},{12,4},{16,24},{20,28},{24,16},{28,20},{1,9},{5... | collective-permute-start | bytes 1572872 | tf_op jit(solution)/shard_map/ppermute | solution.py:314
  1004.7 67.7 %collective-permute-start.115 = (bf16[1024,256]{1,0:T(8,128)(2,1)}, bf16[1024,256]{1,0:T(8,128)(2,1)}, u32[]{:S(2)}, u32[]{:S(2)}) collective-permute-start(bf16[1024,256]{1,0:T(8,128)(2,1)} %slice.858), channel_id=1, source_target_pairs={{0,16},{4,20},{8,24},{12,28},{16,0},{20,4},{24,8},{28,12},{1,17},{... | collective-permute-start | bytes 1572872 | tf_op jit(solution)/shard_map/ppermute | solution.py:314
  1006.6 66.8 %collective-permute-start.114 = (bf16[1024,256]{1,0:T(8,128)(2,1)}, bf16[1024,256]{1,0:T(8,128)(2,1)}, u32[]{:S(2)}, u32[]{:S(2)}) collective-permute-start(bf16[1024,256]{1,0:T(8,128)(2,1)} %fusion.83), channel_id=1, source_target_pairs={{0,16},{4,20},{8,24},{12,28},{16,0},{20,4},{24,8},{28,12},{1,17},{... | collective-permute-start | bytes 1572872 | tf_op jit(solution)/shard_map/ppermute | solution.py:314
  1008.6 65.9 %collective-permute-start.117 = (bf16[1024,256]{1,0:T(8,128)(2,1)}, bf16[1024,256]{1,0:T(8,128)(2,1)}, u32[]{:S(2)}, u32[]{:S(2)}) collective-permute-start(bf16[1024,256]{1,0:T(8,128)(2,1)} %fusion.81), channel_id=1, source_target_pairs={{0,8},{4,12},{8,0},{12,4},{16,24},{20,28},{24,16},{28,20},{1,9},{5... | collective-permute-start | bytes 1572872 | tf_op jit(solution)/shard_map/ppermute | solution.py:314
  1072.0 82.7 %collective-permute-start.76 = (bf16[256,2048]{1,0:T(8,128)(2,1)}, bf16[256,2048]{1,0:T(8,128)(2,1)}, u32[]{:S(2)}, u32[]{:S(2)}) collective-permute-start(bf16[256,2048]{1,0:T(8,128)(2,1)} %get-tuple-element.70), channel_id=1, source_target_pairs={{0,8},{4,12},{8,0},{12,4},{16,24},{20,28},{24,16},{28,20},{1,9},{5... | collective-permute-start | bytes 3145736 | tf_op jit(solution)/shard_map/ppermute | solution.py:314
  1072.5 84.5 %collective-permute-start.80 = (bf16[256,2048]{1,0:T(8,128)(2,1)}, bf16[256,2048]{1,0:T(8,128)(2,1)}, u32[]{:S(2)}, u32[]{:S(2)}) collective-permute-start(bf16[256,2048]{1,0:T(8,128)(2,1)} %get-tuple-element.71), channel_id=1, source_target_pairs={{0,16},{4,20},{8,24},{12,28},{16,0},{20,4},{24,8},{28,12},{1,17},{... | collective-permute-start | bytes 3145736 | tf_op jit(solution)/shard_map/ppermute | solution.py:314
  1073.3 91.4 %collective-permute-start.78 = (bf16[256,2048]{1,0:T(8,128)(2,1)}, bf16[256,2048]{1,0:T(8,128)(2,1)}, u32[]{:S(2)}, u32[]{:S(2)}) collective-permute-start(bf16[256,2048]{1,0:T(8,128)(2,1)} %add_convert_fusion.4), channel_id=1, source_target_pairs={{0,16},{4,20},{8,24},{12,28},{16,0},{20,4},{24,8},{28,12},{1,17},{... | collective-permute-start | bytes 3145736 | tf_op jit(solution)/shard_map/ppermute | solution.py:314
  1077.0 76.5 %collective-permute-start.118 = (bf16[512,256]{1,0:T(8,128)(2,1)S(1)}, bf16[512,256]{1,0:T(8,128)(2,1)}, u32[]{:S(2)}, u32[]{:S(2)}) collective-permute-start(bf16[512,256]{1,0:T(8,128)(2,1)S(1)} %slice.861), channel_id=1, source_target_pairs={{0,1},{1,2},{2,3},{3,0},{4,5},{5,6},{6,7},{7,4},{8,9},{9,10},{10,1... | collective-permute-start | bytes 786440 | tf_op jit(solution)/shard_map/ppermute | solution.py:319
  1154.7 51.8 %collective-permute-start.79 = (bf16[256,2048]{1,0:T(8,128)(2,1)S(1)}, bf16[256,2048]{1,0:T(8,128)(2,1)S(1)}, u32[]{:S(2)}, u32[]{:S(2)}) collective-permute-start(bf16[256,2048]{1,0:T(8,128)(2,1)S(1)} %copy-done.109), channel_id=1, source_target_pairs={{0,16},{4,20},{8,24},{12,28},{16,0},{20,4},{24,8},{28,12},{1,17},{... | collective-permute-start | bytes 3145736 | tf_op jit(solution)/shard_map/ppermute | solution.py:314
  1157.0 50.1 %collective-permute-start.85 = (bf16[256,2048]{1,0:T(8,128)(2,1)S(1)}, bf16[256,2048]{1,0:T(8,128)(2,1)}, u32[]{:S(2)}, u32[]{:S(2)}) collective-permute-start(bf16[256,2048]{1,0:T(8,128)(2,1)S(1)} %get-tuple-element.100), channel_id=1, source_target_pairs={{0,0},{1,1},{4,2},{5,3},{2,4},{3,5},{6,6},{7,7},{8,8},{9,9},{12,10... | collective-permute-start | bytes 3145736 | tf_op jit(solution)/shard_map/ppermute | solution.py:379
  1291.8 54.1 %collective-permute-start.82 = (bf16[256,2048]{1,0:T(8,128)(2,1)S(1)}, bf16[256,2048]{1,0:T(8,128)(2,1)S(1)}, u32[]{:S(2)}, u32[]{:S(2)}) collective-permute-start(bf16[256,2048]{1,0:T(8,128)(2,1)S(1)} %get-tuple-element.113), channel_id=1, source_target_pairs={{0,0},{1,1},{4,2},{5,3},{2,4},{3,5},{6,6},{7,7},{8,8},{9,9},{12,10... | collective-permute-start | bytes 3145736 | tf_op jit(solution)/shard_map/ppermute | solution.py:379
  1309.2 68.8 %collective-permute-start.83 = (bf16[256,2048]{1,0:T(8,128)(2,1)S(1)}, bf16[256,2048]{1,0:T(8,128)(2,1)S(1)}, u32[]{:S(2)}, u32[]{:S(2)}) collective-permute-start(bf16[256,2048]{1,0:T(8,128)(2,1)S(1)} %get-tuple-element.114), channel_id=1, source_target_pairs={{1,0},{0,1},{5,2},{4,3},{3,4},{2,5},{7,6},{6,7},{9,8},{8,9},{13,10... | collective-permute-start | bytes 3145736 | tf_op jit(solution)/shard_map/ppermute | solution.py:379
  1335.7 58.5 %collective-permute-start.97 = (bf16[512,512]{1,0:T(8,128)(2,1)}, bf16[512,512]{1,0:T(8,128)(2,1)}, u32[]{:S(2)}, u32[]{:S(2)}) collective-permute-start(bf16[512,512]{1,0:T(8,128)(2,1)} %slice.860), channel_id=1, source_target_pairs={{0,1},{1,2},{2,3},{3,0},{4,5},{5,6},{6,7},{7,4},{8,9},{9,10},{10,1... | collective-permute-start | bytes 1572872 | tf_op jit(solution)/shard_map/ppermute | solution.py:319
  1379.1 52.6 %collective-permute-start.139 = (bf16[512,768]{1,0:T(8,128)(2,1)}, bf16[512,768]{1,0:T(8,128)(2,1)S(1)}, u32[]{:S(2)}, u32[]{:S(2)}) collective-permute-start(bf16[512,768]{1,0:T(8,128)(2,1)} %reduce-scatter.5.cloned.1.call-done), channel_id=1, source_target_pairs={{0,4},{4,0},{8,12},{12,8},{16,20},{20,16},{24,28},{28,24},{1,5},{5... | collective-permute-start | bytes 2359304 | tf_op jit(solution)/shard_map/ppermute | solution.py:314
  (300 other events, 6079.1 us)
Sparse Core Ops, SparseCore 0:
  84.6 94.2 all-gather.6
  246.9 141.6 all-gather.4
  806.4 59.1 reduce-scatter.4
  1229.2 150.4 reduce-scatter.2

commit v2 on v0

--- a/solution.py
+++ b/solution.py
@@ -1,6 +1,8 @@
 import jax
 import jax.numpy as jnp
 from jax import lax
+from jax.experimental import pallas as pl
+from jax.experimental.pallas import tpu as pltpu
 from jax.sharding import PartitionSpec as P
 
 WINDOW = 512
@@ -306,9 +308,621 @@
     )
 
 
+CORE, ACROSS_X, ACROSS_Y = 1, 2, 4
+VMEM_BYTES = 56 * 2**20
+
+
+def across(x, mask):
+    count = lax.axis_size("rep")
+    return lax.ppermute(x, "rep", [(i, i ^ mask) for i in range(count)])
+
+
+def around(x, by):
+    count = lax.axis_size("shard")
+    return lax.ppermute(x, "shard", [(i, (i + by) % count) for i in range(count)])
+
+
+def after(x, *done):
+    return lax.optimization_barrier((x, *done))[0]
+
+
+def ring_gather(x):
+    before, behind = around(x, 1), around(x, -1)
+    return [x, before, around(before, 1), behind]
+
+
+def ring_sum(chunks, kind):
+    last = chunks[3] + around(chunks[2].astype(kind), 1)
+    return chunks[0] + around(chunks[1].astype(kind), -1) + around(last.astype(kind), 1)
+
+
+def plane_gather(piece):
+    half = piece.shape[0] // 2
+    from_x = across(piece, ACROSS_X)
+    from_y = across(piece, ACROSS_Y)
+    far = [across(from_x[:half], ACROSS_Y), across(from_y[half:], ACROSS_X)]
+    return [piece, from_x, from_y, jnp.concatenate(far, 0)]
+
+
+def plane_sum(own, blocks):
+    low = jnp.bfloat16
+    half = own.shape[0] // 2
+    one, two, three = blocks
+    head_two = two[:half] + across(three[:half].astype(low), ACROSS_X)
+    head_own = own[:half] + across(one[:half].astype(low), ACROSS_X)
+    tail_one = one[half:] + across(three[half:].astype(low), ACROSS_Y)
+    tail_own = own[half:] + across(two[half:].astype(low), ACROSS_Y)
+    head_own = head_own + across(head_two.astype(low), ACROSS_Y)
+    tail_own = tail_own + across(tail_one.astype(low), ACROSS_X)
+    return jnp.concatenate([head_own, tail_own], 0)
+
+
+def sequence_pairs(turn):
+    groups, shards = lax.axis_size("rep"), lax.axis_size("shard")
+    pairs = []
+    for group in range(groups):
+        chip, core = divmod(group, 2)
+        for at in range(shards):
+            to_group, to_shard = 2 * chip + at // 2, 2 * core + (turn ^ (at & 1))
+            pairs.append((group * shards + at, to_group * shards + to_shard))
+    return pairs
+
+
+def rolled(x):
+    count, at = lax.axis_size("shard"), lax.axis_index("shard")
+    width = x.shape[1] // count
+    return jnp.concatenate(
+        [lax.dynamic_slice_in_dim(x, ((at - i) % count) * width, width, 1) for i in range(count)],
+        1,
+    )
+
+
+def to_sequences(x):
+    odd = lax.axis_index("shard") & 1
+    came = [
+        lax.ppermute(
+            lax.dynamic_index_in_dim(x, turn ^ odd, 0, keepdims=False),
+            ("rep", "shard"),
+            sequence_pairs(turn),
+        )
+        for turn in range(2)
+    ]
+    even = odd == 0
+    return rolled(
+        jnp.concatenate(
+            [jnp.where(even, came[0], came[1]), jnp.where(even, came[1], came[0])], 0
+        )
+    )
+
+
+def from_sequences(x):
+    odd = lax.axis_index("shard") & 1
+    x = rolled(x).reshape(2, x.shape[0] // 2, x.shape[1])
+    came = [
+        lax.ppermute(
+            lax.dynamic_index_in_dim(x, turn ^ odd, 0, keepdims=False),
+            ("rep", "shard"),
+            [(to, at) for at, to in sequence_pairs(turn)],
+        )
+        for turn in range(2)
+    ]
+    even = odd == 0
+    return jnp.stack([jnp.where(even, came[0], came[1]), jnp.where(even, came[1], came[0])])
+
+
+def column_block(weights, at):
+    cuts = [w.shape[1] // 8 for w in weights]
+    return jnp.concatenate(
+        [lax.dynamic_slice_in_dim(w, at * cut, cut, 1) for w, cut in zip(weights, cuts)], 1
+    )
+
+
+def gather_blocks(weights, first=()):
+    me = lax.axis_index("rep")
+    own = [column_block(weights, me ^ i) for i in range(8)]
+    came = ring_gather(after(own[0], *first))[1:]
+    rows = [[block] for block in own]
+    for shard in came:
+        for i, block in enumerate(plane_gather(shard)):
+            rows[2 * i].append(block)
+            rows[2 * i + 1].append(across(block, CORE))
+    return rows, came
+
+
+def spread_blocks(block, columns):
+    me = lax.axis_index("rep")
+    pieces = []
+    for piece in plane_gather(block):
+        pieces += [piece, across(piece, CORE)]
+    outs = []
+    start = 0
+    for width in columns:
+        out = jnp.zeros((block.shape[0], 8 * width), jnp.float32)
+        for i, piece in enumerate(pieces):
+            out = lax.dynamic_update_slice_in_dim(
+                out, piece[:, start : start + width].astype(jnp.float32), (me ^ i) * width, 1
+            )
+        outs.append(out)
+        start += width
+    return outs
+
+
+def everywhere_sum(x):
+    for mask in (CORE, ACROSS_X, ACROSS_Y):
+        x = x + across(x, mask)
+    return x
+
+
+def turned(x):
+    return pltpu.roll(x, x.shape[-1] // 2, x.ndim - 1)
+
+
+def nt(left, right):
+    return lax.dot_general(
+        left, right, (((1,), (1,)), ((), ())), preferred_element_type=jnp.float32
+    )
+
+
+def tn(left, right):
+    return lax.dot_general(
+        left, right, (((0,), (0,)), ((), ())), preferred_element_type=jnp.float32
+    )
+
+
+def unit_of(raw):
+    inverse = lax.rsqrt(jnp.mean(raw * raw, -1, keepdims=True) + EPS)
+    return raw * inverse, inverse
+
+
+def project_body(normed, w0, w1, w2, w3, cosine, sine, gains, raw, query, key, value):
+    weights = (w0, w1, w2, w3)
+    step = w0.shape[0]
+    dim = cosine.shape[1]
+    raw[...] = sum(
+        jnp.dot(
+            normed[:, i * step : (i + 1) * step], weights[i][...],
+            preferred_element_type=jnp.float32,
+        )
+        for i in range(4)
+    )
+    for i in range(3):
+        unit, _ = unit_of(raw[:, i * dim : (i + 1) * dim])
+        head = unit * gains[i // 2 : i // 2 + 1, :]
+        head = (head * cosine[...] + turned(head) * sine[...]).astype(jnp.bfloat16)
+        if i < 2:
+            query[:, i * dim : (i + 1) * dim] = head
+        else:
+            key[...] = head
+    value[...] = raw[:, 3 * dim :].astype(jnp.bfloat16)
+
+
+def window_scores(info, query, keys, part, scale):
+    rows, columns = query.shape[0], keys.shape[0]
+    half = columns - rows
+    row = lax.broadcasted_iota(jnp.int32, (rows, columns), 0)
+    column = lax.broadcasted_iota(jnp.int32, (rows, columns), 1)
+    gap = column - row - half
+    slot = column + ((info[0] - 1) * half + part * rows)
+    allowed = (gap <= 0) & (gap > -half) & (slot >= 0) & ((slot < info[1]) | (gap == 0))
+    return nt(query, keys) * scale, allowed
+
+
+def near(before, own, part):
+    rows = own.shape[0] // 2
+    if part == 0:
+        return jnp.concatenate([before[...], own[:rows]], 0)
+    return jnp.concatenate([before[rows:], own[...]], 0)
+
+
+def attend_body(info, query, key_before, key, value_before, value, mixed, log_total):
+    dim = key.shape[1]
+    rows = query.shape[0] // 2
+    for part in range(2):
+        keys, values = near(key_before, key, part), near(value_before, value, part)
+        at = slice(part * rows, (part + 1) * rows)
+        for head in range(2):
+            on = slice(head * dim, (head + 1) * dim)
+            score, allowed = window_scores(info, query[at, on], keys, part, dim**-0.5)
+            score = jnp.where(allowed, score, NEG)
+            top = jnp.max(score, -1, keepdims=True)
+            expo = jnp.exp(score - top)
+            total = jnp.sum(expo, -1, keepdims=True)
+            prob = (expo * (1.0 / total)).astype(jnp.bfloat16)
+            mixed[at, on] = jnp.dot(prob, values, preferred_element_type=jnp.float32).astype(
+                jnp.bfloat16
+            )
+            log_total[at, on] = jnp.broadcast_to(top + jnp.log(total), (rows, dim))
+
+
+def attend_back_body(
+    info, query, key_before, key, value_before, value, log_total, grad_mixed, raw, cosine, sine,
+    gain, grad_query, grad_own, grad_before, gain_part, grad_keys, grad_values,
+):
+    dim = key.shape[1]
+    rows = query.shape[0] // 2
+    scale = dim**-0.5
+    grad_keys[...] = jnp.zeros_like(grad_keys)
+    grad_values[...] = jnp.zeros_like(grad_values)
+    gain_total = jnp.zeros((1, dim), jnp.float32)
+    for part in range(2):
+        keys, values = near(key_before, key, part), near(value_before, value, part)
+        at = slice(part * rows, (part + 1) * rows)
+        seen = slice(part * rows, part * rows + keys.shape[0])
+        for head in range(2):
+            on = slice(head * dim, (head + 1) * dim)
+            score, allowed = window_scores(info, query[at, on], keys, part, scale)
+            prob = jnp.where(allowed, jnp.exp(score - log_total[at, on][:, :1]), 0.0)
+            grad_prob = nt(grad_mixed[at, on], values)
+            inner = jnp.sum(prob * grad_prob, -1, keepdims=True)
+            grad_score = (prob * (grad_prob - inner)).astype(jnp.bfloat16)
+            grad_values[seen, :] += tn(prob.astype(jnp.bfloat16), grad_mixed[at, on])
+            grad_keys[seen, :] += tn(grad_score, query[at, on]) * scale
+            back = jnp.dot(grad_score, keys, preferred_element_type=jnp.float32) * scale
+            back = back * cosine[at, :] - turned(back) * sine[at, :]
+            unit, inverse = unit_of(raw[at, on])
+            gain_total += jnp.sum(unit * back, 0, keepdims=True)
+            back = back * gain[...]
+            back = inverse * (back - unit * jnp.mean(back * unit, -1, keepdims=True))
+            grad_query[at, on] = back.astype(jnp.bfloat16)
+    gain_part[...] = gain_total
+    grad_before[:, :dim] = grad_keys[: 2 * rows, :].astype(jnp.bfloat16)
+    grad_before[:, dim:] = grad_values[: 2 * rows, :].astype(jnp.bfloat16)
+    grad_own[:, :dim] = grad_keys[2 * rows :, :]
+    grad_own[:, dim:] = grad_values[2 * rows :, :]
+
+
+def finish_body(grad_query, grad_own, came, raw, cosine, sine, gain, grad_block, gain_part):
+    dim = cosine.shape[1]
+    back = grad_own[:, :dim] + came[:, :dim].astype(jnp.float32)
+    back = back * cosine[...] - turned(back) * sine[...]
+    unit, inverse = unit_of(raw[...])
+    gain_part[...] = jnp.sum(unit * back, 0, keepdims=True)
+    back = back * gain[...]
+    back = inverse * (back - unit * jnp.mean(back * unit, -1, keepdims=True))
+    grad_block[:, : 2 * dim] = grad_query[...]
+    grad_block[:, 2 * dim : 3 * dim] = back.astype(jnp.bfloat16)
+    grad_value = grad_own[:, dim:] + came[:, dim:].astype(jnp.float32)
+    grad_block[:, 3 * dim :] = grad_value.astype(jnp.bfloat16)
+
+
+def vmem_call(body, outs, flops, scratch=(), scalars=0, specs=None, name=None):
+    def call(*args):
+        in_specs = [
+            pl.BlockSpec(memory_space=pltpu.SMEM if i < scalars else pltpu.VMEM)
+            for i in range(len(args))
+        ]
+        for at, spec in (specs or {}).items():
+            in_specs[at] = spec
+        return pl.pallas_call(
+            body,
+            grid=(1,),
+            out_shape=outs,
+            in_specs=in_specs,
+            out_specs=jax.tree.map(lambda _: pl.BlockSpec(memory_space=pltpu.VMEM), outs),
+            scratch_shapes=scratch,
+            compiler_params=pltpu.CompilerParams(vmem_limit_bytes=VMEM_BYTES),
+            cost_estimate=pl.CostEstimate(
+                flops=flops,
+                bytes_accessed=sum(a.size * a.dtype.itemsize for a in args),
+                transcendentals=0,
+            ),
+            name=name,
+        )(*args)
+
+    return call
+
+
+def column_spec(rows, columns, at):
+    return pl.BlockSpec((rows, columns), lambda i: (0, at))
+
+
+def hidden_body(mid, grad_y, gate_w, up_w, down_w, act, grad_gate, grad_up):
+    gate = jnp.dot(mid[...], gate_w[...], preferred_element_type=jnp.float32)
+    up = jnp.dot(mid[...], up_w[...], preferred_element_type=jnp.float32)
+    grad_act = jnp.dot(grad_y[...], down_w[...], preferred_element_type=jnp.float32)
+    sigma = jax.nn.sigmoid(gate)
+    swish = gate * sigma
+    act[...] = (swish * up).astype(jnp.bfloat16)
+    grad_gate[...] = (grad_act * up * sigma * (1.0 + gate * (1.0 - sigma))).astype(jnp.bfloat16)
+    grad_up[...] = (grad_act * swish).astype(jnp.bfloat16)
+
+
+def hidden_units(mid, grad_y, gate_w, up_w, down_w):
+    rows, width = mid.shape
+    units = gate_w.shape[1]
+    high, cut = rows // 2, units // 6
+    row_spec = pl.BlockSpec((high, width), lambda i, j: (i, 0))
+    weight_spec = pl.BlockSpec((width, cut), lambda i, j: (0, j))
+    out_spec = pl.BlockSpec((high, cut), lambda i, j: (i, j))
+    return pl.pallas_call(
+        hidden_body,
+        grid=(2, 6),
+        out_shape=[jax.ShapeDtypeStruct((rows, units), jnp.bfloat16)] * 3,
+        in_specs=[row_spec, row_spec, weight_spec, weight_spec, weight_spec],
+        out_specs=[out_spec] * 3,
+        compiler_params=pltpu.CompilerParams(vmem_limit_bytes=VMEM_BYTES),
+        cost_estimate=pl.CostEstimate(
+            flops=6 * rows * width * units, bytes_accessed=10 * rows * width, transcendentals=0
+        ),
+        name="hidden_units",
+    )(mid, grad_y, gate_w, up_w, down_w)
+
+
+def from_hidden(lefts, rights, first_block, blocks):
+    count = len(lefts)
+    rows, units = lefts[0].shape[0] // 4, lefts[0].shape[1]
+    width = rights[0].shape[0]
+    cut = width // 4
+
+    def body(*refs):
+        out = refs[-1]
+        out[...] = sum(nt(refs[i][...], refs[count + i][...]) for i in range(count)).astype(
+            jnp.bfloat16
+        )
+
+    return pl.pallas_call(
+        body,
+        grid=(blocks, 4),
+        out_shape=jax.ShapeDtypeStruct((blocks * rows, width), jnp.bfloat16),
+        in_specs=[pl.BlockSpec((rows, units), lambda i, j: (i + first_block, 0))] * count
+        + [pl.BlockSpec((cut, units), lambda i, j: (j, 0))] * count,
+        out_specs=pl.BlockSpec((rows, cut), lambda i, j: (i, j)),
+        compiler_params=pltpu.CompilerParams(vmem_limit_bytes=VMEM_BYTES),
+        cost_estimate=pl.CostEstimate(
+            flops=2 * count * blocks * rows * width * units,
+            bytes_accessed=2 * count * width * units,
+            transcendentals=0,
+        ),
+        name="from_hidden",
+    )(*lefts, *rights)
+
+
+def on_device_block(
+    tokens,
+    lengths,
+    attn_gain,
+    w_query,
+    key_matrix,
+    value_matrix,
+    query_gain,
+    key_gain,
+    w_out,
+    mlp_gain,
+    w_gate,
+    w_up,
+    w_down,
+    cotangent,
+):
+    low, full = jnp.bfloat16, jnp.float32
+    width = tokens.shape[2]
+    head_dim = query_gain.shape[0]
+    shards = lax.axis_size("shard")
+    shard_at = lax.axis_index("shard")
+    me = lax.axis_index("rep")
+    core = me & 1
+    count = lax.axis_size("rep")
+
+    qkv_rows, qkv_came = gather_blocks((w_query, key_matrix, value_matrix))
+    x_low = to_sequences(after(tokens, qkv_came[0], qkv_came[2]))
+    rows = x_low.shape[0]
+    out_rows, out_came = gather_blocks((w_out,), (x_low,))
+    gains = jnp.concatenate(
+        ring_gather(jnp.stack([attn_gain, mlp_gain])), 1
+    ).astype(full)
+    attn_gains, mlp_gains = gains[:1], gains[1:]
+    query_gains = query_gain.astype(full)[None]
+    key_gains = key_gain.astype(full)[None]
+
+    other_lengths = across(lengths, CORE)
+    both = jnp.where(
+        core == 0,
+        jnp.concatenate([lengths, other_lengths]),
+        jnp.concatenate([other_lengths, lengths]),
+    )
+    length = lax.dynamic_index_in_dim(both, shard_at, 0, keepdims=False)
+    info = jnp.stack([core, length]).astype(jnp.int32)
+    query_pos = core * rows + jnp.arange(rows, dtype=jnp.int32)
+    valid = (query_pos < length)[:, None]
+    cosine, sine = tables(query_pos, head_dim)
+    cosine, sine = cosine[0, :, 0], sine[0, :, 0]
+    sine = jnp.concatenate([-sine[:, : head_dim // 2], sine[:, head_dim // 2 :]], 1)
+
+    gate_up_own = [column_block((w_gate, w_up), me ^ i) for i in range(2)]
+    down_own = [column_block((w_down,), me ^ i) for i in range(2)]
+    gate_up_came = ring_gather(after(gate_up_own[0], *out_came))[1:]
+    grad_y_low = to_sequences(after(cotangent, gate_up_came[0], gate_up_came[2]))
+    down_came = ring_gather(after(down_own[0], grad_y_low))[1:]
+
+    def whole(own, came):
+        came = [own[0], *came], [own[1], *(across(c, CORE) for c in came)]
+        return [jnp.concatenate(part, 0) for part in came]
+
+    gate_up = whole(gate_up_own, gate_up_came)
+    units = gate_up[0].shape[1] // 2
+    gate_all = jnp.concatenate([part[:, :units] for part in gate_up], 1)
+    up_all = jnp.concatenate([part[:, units:] for part in gate_up], 1)
+    down_all = jnp.concatenate(whole(down_own, down_came), 1)
+
+    x_rows = x_low.astype(full)
+    inverse_in = lax.rsqrt(jnp.mean(x_rows * x_rows, -1, keepdims=True) + EPS)
+    x_unit = x_rows * inverse_in
+    normed = (x_unit * attn_gains).astype(low)
+    pair_columns = 2 * head_dim
+    head_rows = jax.ShapeDtypeStruct((rows, head_dim), low)
+    pair_rows = jax.ShapeDtypeStruct((rows, pair_columns), low)
+    project = vmem_call(
+        project_body,
+        [jax.ShapeDtypeStruct((rows, 2 * pair_columns), full), pair_rows, head_rows, head_rows],
+        4 * rows * width * pair_columns,
+        name="project",
+    )
+    attend = vmem_call(
+        attend_body,
+        [pair_rows, jax.ShapeDtypeStruct((rows, pair_columns), full)],
+        12 * rows * rows * pair_columns,
+        scalars=1,
+        name="attend",
+    )
+    head_gains = jnp.concatenate([query_gains, key_gains], 0)
+    upward = [(i, i + 1) for i in range(0, count, 2)]
+    downward = [(i + 1, i) for i in range(0, count, 2)]
+    raws, queries, kept, own_pairs = [], [], [], []
+    for i in range(8):
+        raw, query, key, value = project(normed, *qkv_rows[i], cosine, sine, head_gains)
+        raws.append(raw)
+        queries.append(query)
+        own_pairs.append((key, value))
+    mixed_blocks, log_totals = [], []
+    for i in range(8):
+        key, value = own_pairs[i]
+        key_before, value_before = (
+            lax.ppermute(part, "rep", upward) for part in own_pairs[i ^ 1]
+        )
+        pairs = (key_before, key, value_before, value)
+        mixed, log_total = attend(info, queries[i], *pairs)
+        kept.append(pairs)
+        mixed_blocks.append(mixed)
+        log_totals.append(log_total)
+    mixed = jnp.concatenate(mixed_blocks, 1)
+    out_all = jnp.concatenate([jnp.concatenate(r, 0) for r in out_rows], 1)
+    branch = jnp.einsum("rf,nf->rn", mixed, out_all, preferred_element_type=full)
+
+    resid = x_rows + branch
+    inverse_mid = lax.rsqrt(jnp.mean(resid * resid, -1, keepdims=True) + EPS)
+    mid_unit = resid * inverse_mid
+    mid = (mid_unit * mlp_gains).astype(low)
+    mid_all = jnp.concatenate(plane_gather(mid), 0)
+    grad_y_low = jnp.where(valid, grad_y_low, jnp.zeros_like(grad_y_low))
+    grad_y_all = jnp.concatenate(plane_gather(grad_y_low), 0)
+    act, grad_gate, grad_up = hidden_units(mid_all, grad_y_all, gate_all, up_all, down_all)
+
+    def plane_total(lefts, rights):
+        far = from_hidden(lefts, rights, 1, 3)
+        own = from_hidden([after(left, far) for left in lefts], rights, 0, 1)
+        return plane_sum(own.astype(full), jnp.split(far, 3, 0))
+
+    grad_mid = plane_total((grad_gate, grad_up), (gate_all, up_all))
+    mlp_out = plane_total((act,), (down_all,))
+    output = from_sequences(jnp.where(valid, resid + mlp_out, 0.0).astype(low))
+
+    others = [
+        outer(left, right[:, units:]).astype(low)
+        for left, right in ((grad_y_all, act), (mid_all, grad_gate), (mid_all, grad_up))
+    ]
+    owns = [
+        (outer(left, right[:, :units]) + across(other, CORE)).astype(low)
+        for (left, right), other in zip(
+            ((grad_y_all, act), (mid_all, grad_gate), (mid_all, grad_up)), others
+        )
+    ]
+    grad_mid = after(grad_mid, *owns)
+    totals = [ring_sum(jnp.split(own, shards, 0), low).astype(low) for own in owns]
+    (grad_down_total,), (grad_gate_total,), (grad_up_total,) = (
+        spread_blocks(total, (units,)) for total in totals
+    )
+
+    mlp_gain_part = jnp.sum(mid_unit * grad_mid, 0)
+    grad_resid = grad_y_low.astype(full) + norm_back(mid_unit, inverse_mid, grad_mid * mlp_gains)
+    resid_low = grad_resid.astype(low)
+    grad_mixed = jnp.dot(resid_low, out_all, preferred_element_type=full).astype(low)
+    grad_blocks = [None] * 8
+    query_gain_part, key_gain_part = 0.0, 0.0
+    finish = vmem_call(
+        finish_body,
+        [
+            jax.ShapeDtypeStruct((rows, 2 * pair_columns), low),
+            jax.ShapeDtypeStruct((1, head_dim), full),
+        ],
+        rows * head_dim,
+        specs={3: column_spec(rows, head_dim, 2)},
+        name="finish",
+    )
+    order = (7, 6, 3, 2, 5, 4, 1, 0)
+    backs = [None] * 8
+    for i in order:
+        attend_back = vmem_call(
+            attend_back_body,
+            [
+                pair_rows,
+                jax.ShapeDtypeStruct((rows, pair_columns), full),
+                pair_rows,
+                jax.ShapeDtypeStruct((1, head_dim), full),
+            ],
+            30 * rows * rows * pair_columns,
+            scratch=[pltpu.VMEM((2 * rows, head_dim), full)] * 2,
+            scalars=1,
+            specs={
+                7: column_spec(rows, pair_columns, i),
+                8: column_spec(rows, pair_columns, 0),
+            },
+            name="attend_back",
+        )
+        backs[i] = attend_back(
+            info, queries[i], *kept[i], log_totals[i], grad_mixed, raws[i], cosine, sine,
+            query_gains,
+        )
+        query_gain_part += backs[i][3]
+    for i in order:
+        came = lax.ppermute(backs[i ^ 1][2], "rep", downward)
+        grad_blocks[i], part = finish(
+            backs[i][0], backs[i][1], came, raws[i], cosine, sine, key_gains
+        )
+        key_gain_part += part
+
+    def block_totals(left, blocks):
+        chips = [None] * 4
+        for i in (3, 1, 2, 0):
+            other = outer(left, blocks[2 * i + 1]).astype(low)
+            chips[i] = outer(left, blocks[2 * i]) + across(other, CORE)
+        own = plane_sum(chips[0], chips[1:])
+        return ring_sum(jnp.split(own, shards, 0), low).astype(low)
+
+    out_total = block_totals(resid_low, mixed_blocks)
+    (grad_out_total,) = spread_blocks(out_total, (pair_columns,))
+    qkv_total = block_totals(normed, grad_blocks)
+    grad_query_total, grad_key_total, grad_value_total = spread_blocks(
+        qkv_total, (pair_columns, head_dim, head_dim)
+    )
+
+    grad_qkv = jnp.concatenate(grad_blocks, 1)
+    qkv_all = jnp.concatenate([jnp.concatenate(r, 0) for r in qkv_rows], 1)
+    grad_in = jnp.einsum("rf,nf->rn", grad_qkv, qkv_all, preferred_element_type=full)
+    grad_tokens = from_sequences(
+        (grad_resid + norm_back(x_unit, inverse_in, grad_in * attn_gains)).astype(low)
+    )
+    attn_gain_part = jnp.sum(x_unit * grad_in, 0)
+
+    parts = everywhere_sum(
+        jnp.concatenate(
+            [attn_gain_part, mlp_gain_part, query_gain_part[0], key_gain_part[0]]
+        )
+    )
+    wide = parts[: 2 * width].reshape(2, shards, width // shards)
+    wide = ring_sum([wide[:, i] for i in range(shards)], full)
+    narrow = parts[2 * width :]
+    for by in (1, 2):
+        narrow = narrow + lax.ppermute(narrow, "shard", [(i, i ^ by) for i in range(shards)])
+    return (
+        output,
+        grad_tokens,
+        wide[0],
+        grad_query_total,
+        grad_key_total,
+        grad_value_total,
+        narrow[:head_dim],
+        narrow[head_dim:],
+        grad_out_total,
+        wide[1],
+        grad_gate_total,
+        grad_up_total,
+        grad_down_total,
+    )
+
+
 def solution(mesh):
+    sizes = (mesh.shape["rep"], mesh.shape["shard"])
     return jax.shard_map(
-        on_device,
+        on_device_block if sizes == (8, 4) else on_device,
         mesh=mesh,
         in_specs=(
             P("rep", "shard", None),

time: 4390 us -> 1610 us (0.37)
  waiting for transfers between devices: 3460 us -> 548 us
  blocking collectives: 370 us -> 0 us
  starting transfers between devices: 10.2 us -> 368 us
  Pallas kernels: 0 us -> 264 us
  matrix products: 356 us -> 133 us
  local copies, waits for them, and re-layouts: 68.5 us -> 127 us
  other arithmetic: 102 us -> 149 us
    reduce_scatter x7 -> x0, waiting for transfers between devices: 1600 us -> none  [on_device(): lax.psum_scatter(part.astype(jnp.bfloat16), 'shard', scatter_dimension=0,...]
    all_gather x7 -> x0, waiting for transfers between devices: 1360 us -> none  [the longest x1 414 us: on_device(): up_piece = lax.all_gather(w_up, 'shard', axis=0, tiled=True)]
    ppermute x4 -> x208, starting transfers between devices: 8.83 us -> 368 us  [the longest x141 195 us: across(): return lax.ppermute(x, 'rep', [(i, i ^ mask) for i in range(count)])]
    all_gather x2 -> x0, blocking collectives: 325 us -> none  [the longest x1 312 us: on_device(): gain_piece = lax.all_gather(mlp_gain, 'shard', axis=0, tiled=True)]
    ppermute x4 -> x208, waiting for transfers between devices: 270 us -> 548 us  [the longest x141 322 us: across(): return lax.ppermute(x, 'rep', [(i, i ^ mask) for i in range(count)])]
    pallas_call x0 -> x37, Pallas kernels: none -> 264 us  [the longest x32 147 us: call(): pl.pallas_call(body, grid=(1,), out_shape=outs, in_specs=in_specs, out_sp...]
    dot_general x20 -> x3, matrix products: 263 us -> 33.5 us  [the longest x1 15.9 us: on_device_block(): jnp.einsum('rf,nf->rn', grad_qkv, qkv_all, preferred_element_type=full)]
    psum x1 -> x0, waiting for transfers between devices: 230 us -> none  [on_device(): lax.psum(attn_grads[0].astype(jnp.bfloat16), 'rep').astype(jnp.float32)]
  transfers between devices with their start and end apart: 19 -> 208, of which waited for: 14 -> 58; matrix products, arithmetic and copies ran while one was open for 7% -> 20% of each run, Pallas kernels for 0% -> 10%
where the time goes in v2:
time: 1610 us; the launch traced here: 1590 us
  waiting for transfers between devices  548 us (34%)
  starting transfers between devices  368 us (23%)
  Pallas kernels  264 us (16%)
  other arithmetic  149 us (9%)
  matrix products  133 us (8%)
  local copies, waits for them, and re-layouts  127 us (8%)
    ppermute x141, waiting for transfers between devices, across(): return lax.ppermute(x, 'rep', [(i, i ^ mask) for i in range(count)])  322 us
    ppermute x141, starting transfers between devices, across(): return lax.ppermute(x, 'rep', [(i, i ^ mask) for i in range(count)])  195 us
    ppermute x33, waiting for transfers between devices, around(): lax.ppermute(x, 'shard', [(i, (i + by) % count) for i in range(count)])  192 us
    pallas_call x32, Pallas kernels, call(): pl.pallas_call(body, grid=(1,), out_shape=outs, in_specs=in_specs, out_sp...  147 us
    ppermute x33, starting transfers between devices, around(): lax.ppermute(x, 'shard', [(i, (i + by) % count) for i in range(count)])  118 us
    dot_general x22, matrix products, outer(): jnp.einsum('rc,rf->cf', left, right, preferred_element_type=jnp.float32)  99.9 us
    pallas_call x4, Pallas kernels, from_hidden(): pl.pallas_call(body, grid=(blocks, 4), out_shape=jax.ShapeDtypeStruct((bl...  67 us
    unnamed x458, local copies, waits for them, and re-layouts  63.6 us
  transfers between devices with their start and end apart: 208, of which 58 were waited for; matrix products, arithmetic and copies ran while one was open for 20% of the time, Pallas kernels for 10%

profile of v2, /device:TPU:0, one launch (start us, length us, event | category | flops | bytes accessed | tf_op | source)
XLA Modules:
  0.0 1593.6 jit_solution(16670165447916876122)
XLA Ops:
  64.3 27.4 %collective-permute-done.8.w2 = bf16[512,512]{1,0:T(8,128)(2,1)} collective-permute-done((bf16[512,512]{1,0:T(8,128)(2,1)}, bf16[512,512]{1,0:T(8,128)(2,1)}, u32[]{:S(2)}, u32[]{:S(2)}) %collective-permute-start.8) | collective-permute-done | bytes 524320 | tf_op jit(solution)/shard_map/ppermute | solution.py:322
  340.3 17.7 %collective-permute-done.80 = bf16[512,1536]{1,0:T(8,128)(2,1)S(1)} collective-permute-done((bf16[512,1536]{1,0:T(8,128)(2,1)S(1)}, bf16[512,1536]{1,0:T(8,128)(2,1)S(1)}, u32[]{:S(2)}, u32[]{:S(2)}) %collective-permute-start.80) | collective-permute-done | bytes 1572896 | tf_op jit(solution)/shard_map/ppermute | solution.py:322
  358.7 31.0 %collective-permute-done.81 = bf16[512,1536]{1,0:T(8,128)(2,1)} collective-permute-done((bf16[512,1536]{1,0:T(8,128)(2,1)S(1)}, bf16[512,1536]{1,0:T(8,128)(2,1)}, u32[]{:S(2)}, u32[]{:S(2)}) %collective-permute-start.81) | collective-permute-done | bytes 1572896 | tf_op jit(solution)/shard_map/ppermute | solution.py:322
  392.6 11.6 maximum_maximum_fusion.down_w.refs_1_
  418.1 54.6 %collective-permute-start.89 = (bf16[512,1536]{1,0:T(8,128)(2,1)S(1)}, bf16[512,1536]{1,0:T(8,128)(2,1)}, u32[]{:S(2)}, u32[]{:S(2)}) collective-permute-start(bf16[512,1536]{1,0:T(8,128)(2,1)S(1)} %collective-permute-done.80), channel_id=1, source_target_pairs={{0,4},{4,0},{8,12},{12,8},{16,20},{20,16},{24,28},{28,24},{1,5},{5... | collective-permute-start | bytes 4718600 | tf_op jit(solution)/shard_map/ppermute | solution.py:317
  480.7 17.7 %collective-permute-done.78 = bf16[256,2048]{1,0:T(8,128)(2,1)S(1)} collective-permute-done((bf16[256,2048]{1,0:T(8,128)(2,1)S(1)}, bf16[256,2048]{1,0:T(8,128)(2,1)S(1)}, u32[]{:S(2)}, u32[]{:S(2)}) %collective-permute-start.78) | collective-permute-done | bytes 1048608 | tf_op jit(solution)/shard_map/ppermute | solution.py:317
  510.8 33.0 %collective-permute-done.84 = bf16[512,2048]{1,0:T(8,128)(2,1)S(1)} collective-permute-done((bf16[512,2048]{1,0:T(8,128)(2,1)S(1)}, bf16[512,2048]{1,0:T(8,128)(2,1)S(1)}, u32[]{:S(2)}, u32[]{:S(2)}) %collective-permute-start.84) | collective-permute-done | bytes 2097184 | tf_op jit(solution)/shard_map/ppermute | solution.py:317
  573.8 50.1 %hidden_units.1 = (bf16[2048,1536]{1,0:T(8,128)(2,1)}, bf16[2048,1536]{1,0:T(8,128)(2,1)}, bf16[2048,1536]{1,0:T(8,128)(2,1)}) custom-call(bf16[2048,2048]{1,0:T(8,128)(2,1)} %constant_dynamic-update-slice_fusion.14.mid, bf16[2048,2048]{1,0:T(8,128)(2,1)} %constant_dynamic-update-slice_fusion.19.grad_y, bf16[2048,1536]{1,0:T(8,128)(2,1)} %pad_maximum_fusion.2.gate_w.refs_2_, ...), custom_call_target="tpu_custom_call" | custom-call | flops 38654705664 | bytes 41943040 | tf_op jit(solution)/shard_map/hidden_units/pallas_call | solution.py:637
  623.9 11.5 convolution_convert_fusion.2
  635.4 19.0 %from_hidden.4 = bf16[1536,2048]{1,0:T(8,128)(2,1)} custom-call(bf16[2048,1536]{1,0:T(8,128)(2,1)} %get-tuple-element.159.refs_0_, bf16[2048,1536]{1,0:T(8,128)(2,1)} %maximum_maximum_fusion.down_w.refs_1_), custom_call_target="tpu_custom_call" | custom-call | flops 9663676416 | bytes 6291456 | tf_op jit(solution)/shard_map/from_hidden/pallas_call | solution.py:663
  654.4 11.5 convolution_convert_fusion.1
  665.9 29.4 %from_hidden.6 = bf16[1536,2048]{1,0:T(8,128)(2,1)} custom-call(bf16[2048,1536]{1,0:T(8,128)(2,1)} %get-tuple-element.162.refs_0_, bf16[2048,1536]{1,0:T(8,128)(2,1)} %get-tuple-element.163.refs_1_, bf16[2048,1536]{1,0:T(8,128)(2,1)} %pad_maximum_fusion.2.gate_w.refs_2_, bf16[2048,1536]{1,0:T(8,128)(2,1)} %pad_maximum_fusion.3.up_w.refs_3_), custom_call_target="tpu_custom_call" | custom-call | flops 19327352832 | bytes 12582912 | tf_op jit(solution)/shard_map/from_hidden/pallas_call | solution.py:663
  730.4 17.3 %collective-permute-done.106 = bf16[256,2048]{1,0:T(8,128)(2,1)S(1)} collective-permute-done((bf16[256,2048]{1,0:T(8,128)(2,1)S(1)}, bf16[256,2048]{1,0:T(8,128)(2,1)S(1)}, u32[]{:S(2)}, u32[]{:S(2)}) %collective-permute-start.106) | collective-permute-done | bytes 1048608 | tf_op jit(solution)/shard_map/ppermute | solution.py:317
  749.1 18.0 %collective-permute-done.99 = bf16[256,2048]{1,0:T(8,128)(2,1)} collective-permute-done((bf16[256,2048]{1,0:T(8,128)(2,1)S(1)}, bf16[256,2048]{1,0:T(8,128)(2,1)}, u32[]{:S(2)}, u32[]{:S(2)}) %collective-permute-start.99) | collective-permute-done | bytes 1048608 | tf_op jit(solution)/shard_map/ppermute | solution.py:317
  767.8 11.2 from_hidden.7
  817.1 17.6 %collective-permute-done.100 = bf16[256,2048]{1,0:T(8,128)(2,1)S(1)} collective-permute-done((bf16[256,2048]{1,0:T(8,128)(2,1)}, bf16[256,2048]{1,0:T(8,128)(2,1)S(1)}, u32[]{:S(2)}, u32[]{:S(2)}) %collective-permute-start.100) | collective-permute-done | bytes 1048608 | tf_op jit(solution)/shard_map/ppermute | solution.py:317
  849.7 13.6 add_convert_fusion.1
  1015.6 15.9 fusion.10
  1066.2 14.3 collective-permute-done.198
  1097.5 13.5 collective-permute-start.186
  1117.4 13.1 collective-permute-start.197
  1130.7 15.3 collective-permute-done.124
  1158.8 35.1 %collective-permute-done.186 = bf16[512,768]{1,0:T(8,128)(2,1)S(1)} collective-permute-done((bf16[512,768]{1,0:T(8,128)(2,1)S(1)}, bf16[512,768]{1,0:T(8,128)(2,1)S(1)}, u32[]{:S(2)}, u32[]{:S(2)}) %collective-permute-start.186) | collective-permute-done | bytes 786464 | tf_op jit(solution)/shard_map/ppermute | solution.py:322
  1193.9 32.2 %collective-permute-start.135 = (bf16[2048,512]{1,0:T(8,128)(2,1)}, bf16[2048,512]{1,0:T(8,128)(2,1)}, u32[]{:S(2)}, u32[]{:S(2)}) collective-permute-start(bf16[2048,512]{1,0:T(8,128)(2,1)} %convolution_convert_fusion.3), channel_id=1, source_target_pairs={{0,4},{4,0},{8,12},{12,8},{16,20},{20,16},{24,28},{28,24},{1,5},{5... | collective-permute-start | bytes 6291464 | tf_op jit(solution)/shard_map/ppermute | solution.py:317
  1226.1 40.8 %collective-permute-start.188 = (bf16[512,768]{1,0:T(8,128)(2,1)S(1)}, bf16[512,768]{1,0:T(8,128)(2,1)S(1)}, u32[]{:S(2)}, u32[]{:S(2)}) collective-permute-start(bf16[512,768]{1,0:T(8,128)(2,1)S(1)} %slice_add_fusion.20), channel_id=1, source_target_pairs={{0,1},{1,2},{2,3},{3,0},{4,5},{5,6},{6,7},{7,4},{8,9},{9,10},{10,1... | collective-permute-start | bytes 2359304 | tf_op jit(solution)/shard_map/ppermute | solution.py:322
  1306.4 12.6 collective-permute-done.179
  1360.7 11.6 collective-permute-done.203
  1409.5 42.3 %collective-permute-done.172 = bf16[256,256]{1,0:T(8,128)(2,1)S(1)} collective-permute-done((bf16[256,256]{1,0:T(8,128)(2,1)S(1)}, bf16[256,256]{1,0:T(8,128)(2,1)S(1)}, u32[]{:S(2)}, u32[]{:S(2)}) %collective-permute-start.172) | collective-permute-done | bytes 131104 | tf_op jit(solution)/shard_map/ppermute | solution.py:317
  1466.6 11.2 collective-permute-done.136
  1482.4 18.0 %collective-permute-done.133 = bf16[1024,512]{1,0:T(8,128)(2,1)S(1)} collective-permute-done((bf16[1024,512]{1,0:T(8,128)(2,1)S(1)}, bf16[1024,512]{1,0:T(8,128)(2,1)S(1)}, u32[]{:S(2)}, u32[]{:S(2)}) %collective-permute-start.133) | collective-permute-done | bytes 1048608 | tf_op jit(solution)/shard_map/ppermute | solution.py:317
  1500.4 22.1 %collective-permute-done.141 = bf16[1024,512]{1,0:T(8,128)(2,1)S(1)} collective-permute-done((bf16[1024,512]{1,0:T(8,128)(2,1)S(1)}, bf16[1024,512]{1,0:T(8,128)(2,1)S(1)}, u32[]{:S(2)}, u32[]{:S(2)}) %collective-permute-start.141) | collective-permute-done | bytes 1048608 | tf_op jit(solution)/shard_map/ppermute | solution.py:317
  1531.7 11.3 collective-permute-done.142
  (1134 shorter events, 887.8 us)
Async XLA Ops:
  41.2 54.6 %collective-permute-start.4 = (bf16[256,2048]{1,0:T(8,128)(2,1)S(1)}, bf16[256,2048]{1,0:T(8,128)(2,1)S(1)}, u32[]{:S(2)}, u32[]{:S(2)}) collective-permute-start(bf16[256,2048]{1,0:T(8,128)(2,1)S(1)} %get-tuple-element.332), channel_id=1, source_target_pairs={{0,1},{1,0},{2,5},{3,4},{4,3},{5,2},{6,7},{7,6},{8,9},{9,8},{10,13... | collective-permute-start | bytes 3145736 | tf_op jit(solution)/shard_map/ppermute | solution.py:383
  42.6 53.8 %collective-permute-start.3 = (bf16[256,2048]{1,0:T(8,128)(2,1)S(1)}, bf16[256,2048]{1,0:T(8,128)(2,1)S(1)}, u32[]{:S(2)}, u32[]{:S(2)}) collective-permute-start(bf16[256,2048]{1,0:T(8,128)(2,1)S(1)} %get-tuple-element.333), channel_id=1, source_target_pairs={{0,0},{1,1},{2,4},{3,5},{4,2},{5,3},{6,6},{7,7},{8,8},{9,9},{10,12... | collective-permute-start | bytes 3145736 | tf_op jit(solution)/shard_map/ppermute | solution.py:383
  177.7 96.9 %collective-permute-start.92 = (bf16[512,768]{1,0:T(8,128)(2,1)}, bf16[512,768]{1,0:T(8,128)(2,1)}, u32[]{:S(2)}, u32[]{:S(2)}) collective-permute-start(bf16[512,768]{1,0:T(8,128)(2,1)} %get-tuple-element.157), channel_id=1, source_target_pairs={{0,1},{1,2},{2,3},{3,0},{4,5},{5,6},{6,7},{7,4},{8,9},{9,10},{10,1... | collective-permute-start | bytes 2359304 | tf_op jit(solution)/shard_map/ppermute | solution.py:322
  313.6 78.2 %collective-permute-start.95 = (bf16[512,768]{1,0:T(8,128)(2,1)}, bf16[512,768]{1,0:T(8,128)(2,1)}, u32[]{:S(2)}, u32[]{:S(2)}) collective-permute-start(bf16[512,768]{1,0:T(8,128)(2,1)} %collective-permute-done.92), channel_id=1, source_target_pairs={{0,4},{4,0},{8,12},{12,8},{16,20},{20,16},{24,28},{28,24},{1,5},{5... | collective-permute-start | bytes 2359304 | tf_op jit(solution)/shard_map/ppermute | solution.py:317
  313.6 77.7 %collective-permute-start.97 = (bf16[512,768]{1,0:T(8,128)(2,1)}, bf16[512,768]{1,0:T(8,128)(2,1)}, u32[]{:S(2)}, u32[]{:S(2)}) collective-permute-start(bf16[512,768]{1,0:T(8,128)(2,1)} %collective-permute-done.94), channel_id=1, source_target_pairs={{0,4},{4,0},{8,12},{12,8},{16,20},{20,16},{24,28},{28,24},{1,5},{5... | collective-permute-start | bytes 2359304 | tf_op jit(solution)/shard_map/ppermute | solution.py:317
  314.1 78.4 %collective-permute-start.96 = (bf16[512,768]{1,0:T(8,128)(2,1)}, bf16[512,768]{1,0:T(8,128)(2,1)}, u32[]{:S(2)}, u32[]{:S(2)}) collective-permute-start(bf16[512,768]{1,0:T(8,128)(2,1)} %collective-permute-done.93), channel_id=1, source_target_pairs={{0,4},{4,0},{8,12},{12,8},{16,20},{20,16},{24,28},{28,24},{1,5},{5... | collective-permute-start | bytes 2359304 | tf_op jit(solution)/shard_map/ppermute | solution.py:317
  319.3 70.4 %collective-permute-start.81 = (bf16[512,1536]{1,0:T(8,128)(2,1)S(1)}, bf16[512,1536]{1,0:T(8,128)(2,1)}, u32[]{:S(2)}, u32[]{:S(2)}) collective-permute-start(bf16[512,1536]{1,0:T(8,128)(2,1)S(1)} %copy-done.67), channel_id=1, source_target_pairs={{0,3},{1,0},{2,1},{3,2},{4,7},{5,4},{6,5},{7,6},{8,11},{9,8},{10,9... | collective-permute-start | bytes 4718600 | tf_op jit(solution)/shard_map/ppermute | solution.py:322
  358.1 115.1 %collective-permute-start.76 = (bf16[512,2048]{1,0:T(8,128)(2,1)S(1)}, bf16[512,2048]{1,0:T(8,128)(2,1)S(1)}, u32[]{:S(2)}, u32[]{:S(2)}) collective-permute-start(bf16[512,2048]{1,0:T(8,128)(2,1)S(1)} %get-tuple-element.244), channel_id=1, source_target_pairs={{0,8},{4,12},{8,0},{12,4},{16,24},{20,28},{24,16},{28,20},{1,9},{5... | collective-permute-start | bytes 6291464 | tf_op jit(solution)/shard_map/ppermute | solution.py:317
  389.7 84.2 %collective-permute-start.77 = (bf16[512,2048]{1,0:T(8,128)(2,1)S(1)}, bf16[512,2048]{1,0:T(8,128)(2,1)S(1)}, u32[]{:S(2)}, u32[]{:S(2)}) collective-permute-start(bf16[512,2048]{1,0:T(8,128)(2,1)S(1)} %get-tuple-element.244), channel_id=1, source_target_pairs={{0,16},{4,20},{8,24},{12,28},{16,0},{20,4},{24,8},{28,12},{1,17},{... | collective-permute-start | bytes 6291464 | tf_op jit(solution)/shard_map/ppermute | solution.py:317
  405.7 142.5 %collective-permute-start.91 = (bf16[512,1536]{1,0:T(8,128)(2,1)}, bf16[512,1536]{1,0:T(8,128)(2,1)}, u32[]{:S(2)}, u32[]{:S(2)}) collective-permute-start(bf16[512,1536]{1,0:T(8,128)(2,1)} %collective-permute-done.81), channel_id=1, source_target_pairs={{0,4},{4,0},{8,12},{12,8},{16,20},{20,16},{24,28},{28,24},{1,5},{5... | collective-permute-start | bytes 4718600 | tf_op jit(solution)/shard_map/ppermute | solution.py:317
  417.4 61.9 %collective-permute-start.88 = (bf16[512,1536]{1,0:T(8,128)(2,1)S(1)}, bf16[512,1536]{1,0:T(8,128)(2,1)}, u32[]{:S(2)}, u32[]{:S(2)}) collective-permute-start(bf16[512,1536]{1,0:T(8,128)(2,1)S(1)} %collective-permute-done.80), channel_id=1, source_target_pairs={{0,1},{1,2},{2,3},{3,0},{4,5},{5,6},{6,7},{7,4},{8,9},{9,10},{10,1... | collective-permute-start | bytes 4718600 | tf_op jit(solution)/shard_map/ppermute | solution.py:322
  418.1 130.0 %collective-permute-start.89 = (bf16[512,1536]{1,0:T(8,128)(2,1)S(1)}, bf16[512,1536]{1,0:T(8,128)(2,1)}, u32[]{:S(2)}, u32[]{:S(2)}) collective-permute-start(bf16[512,1536]{1,0:T(8,128)(2,1)S(1)} %collective-permute-done.80), channel_id=1, source_target_pairs={{0,4},{4,0},{8,12},{12,8},{16,20},{20,16},{24,28},{28,24},{1,5},{5... | collective-permute-start | bytes 4718600 | tf_op jit(solution)/shard_map/ppermute | solution.py:317
  479.3 64.5 %collective-permute-start.84 = (bf16[512,2048]{1,0:T(8,128)(2,1)S(1)}, bf16[512,2048]{1,0:T(8,128)(2,1)S(1)}, u32[]{:S(2)}, u32[]{:S(2)}) collective-permute-start(bf16[512,2048]{1,0:T(8,128)(2,1)S(1)} %get-tuple-element.242), channel_id=1, source_target_pairs={{0,8},{4,12},{8,0},{12,4},{16,24},{20,28},{24,16},{28,20},{1,9},{5... | collective-permute-start | bytes 6291464 | tf_op jit(solution)/shard_map/ppermute | solution.py:317
  704.4 62.7 %collective-permute-start.99 = (bf16[256,2048]{1,0:T(8,128)(2,1)S(1)}, bf16[256,2048]{1,0:T(8,128)(2,1)}, u32[]{:S(2)}, u32[]{:S(2)}) collective-permute-start(bf16[256,2048]{1,0:T(8,128)(2,1)S(1)} %get-tuple-element.256), channel_id=1, source_target_pairs={{0,8},{4,12},{8,0},{12,4},{16,24},{20,28},{24,16},{28,20},{1,9},{5... | collective-permute-start | bytes 3145736 | tf_op jit(solution)/shard_map/ppermute | solution.py:317
  715.9 67.6 %collective-permute-start.109 = (bf16[256,2048]{1,0:T(8,128)(2,1)}, bf16[256,2048]{1,0:T(8,128)(2,1)}, u32[]{:S(2)}, u32[]{:S(2)}) collective-permute-start(bf16[256,2048]{1,0:T(8,128)(2,1)} %get-tuple-element.249), channel_id=1, source_target_pairs={{0,16},{4,20},{8,24},{12,28},{16,0},{20,4},{24,8},{28,12},{1,17},{... | collective-permute-start | bytes 3145736 | tf_op jit(solution)/shard_map/ppermute | solution.py:317
  725.2 114.1 %collective-permute-start.112 = (bf16[2048,768]{1,0:T(8,128)(2,1)}, bf16[2048,768]{1,0:T(8,128)(2,1)}, u32[]{:S(2)}, u32[]{:S(2)}) collective-permute-start(bf16[2048,768]{1,0:T(8,128)(2,1)} %convolution_convert_fusion.2), channel_id=1, source_target_pairs={{0,4},{4,0},{8,12},{12,8},{16,20},{20,16},{24,28},{28,24},{1,5},{5... | collective-permute-start | bytes 9437192 | tf_op jit(solution)/shard_map/ppermute | solution.py:317
  725.8 53.2 %collective-permute-start.102 = (bf16[256,2048]{1,0:T(8,128)(2,1)}, bf16[256,2048]{1,0:T(8,128)(2,1)}, u32[]{:S(2)}, u32[]{:S(2)}) collective-permute-start(bf16[256,2048]{1,0:T(8,128)(2,1)} %get-tuple-element.254), channel_id=1, source_target_pairs={{0,16},{4,20},{8,24},{12,28},{16,0},{20,4},{24,8},{28,12},{1,17},{... | collective-permute-start | bytes 3145736 | tf_op jit(solution)/shard_map/ppermute | solution.py:317
  973.8 114.7 %collective-permute-start.154 = (bf16[2048,256]{1,0:T(8,128)(2,1)}, bf16[2048,256]{1,0:T(8,128)(2,1)S(1)}, u32[]{:S(2)}, u32[]{:S(2)}) collective-permute-start(bf16[2048,256]{1,0:T(8,128)(2,1)} %convolution_convert_fusion.11), channel_id=1, source_target_pairs={{0,4},{4,0},{8,12},{12,8},{16,20},{20,16},{24,28},{28,24},{1,5},{5... | collective-permute-start | bytes 3145736 | tf_op jit(solution)/shard_map/ppermute | solution.py:317
  984.8 78.1 %collective-permute-start.176 = (bf16[512,768]{1,0:T(8,128)(2,1)}, bf16[512,768]{1,0:T(8,128)(2,1)}, u32[]{:S(2)}, u32[]{:S(2)}) collective-permute-start(bf16[512,768]{1,0:T(8,128)(2,1)} %get-tuple-element.282), channel_id=1, source_target_pairs={{0,1},{1,2},{2,3},{3,0},{4,5},{5,6},{6,7},{7,4},{8,9},{9,10},{10,1... | collective-permute-start | bytes 2359304 | tf_op jit(solution)/shard_map/ppermute | solution.py:322
  993.6 70.8 %collective-permute-start.187 = (bf16[512,768]{1,0:T(8,128)(2,1)}, bf16[512,768]{1,0:T(8,128)(2,1)}, u32[]{:S(2)}, u32[]{:S(2)}) collective-permute-start(bf16[512,768]{1,0:T(8,128)(2,1)} %get-tuple-element.280), channel_id=1, source_target_pairs={{0,1},{1,2},{2,3},{3,0},{4,5},{5,6},{6,7},{7,4},{8,9},{9,10},{10,1... | collective-permute-start | bytes 2359304 | tf_op jit(solution)/shard_map/ppermute | solution.py:322
  1085.4 60.6 %collective-permute-start.124 = (bf16[256,2048]{1,0:T(8,128)(2,1)S(1)}, bf16[256,2048]{1,0:T(8,128)(2,1)S(1)}, u32[]{:S(2)}, u32[]{:S(2)}) collective-permute-start(bf16[256,2048]{1,0:T(8,128)(2,1)S(1)} %get-tuple-element.290), channel_id=1, source_target_pairs={{1,0},{0,1},{5,2},{4,3},{3,4},{2,5},{7,6},{6,7},{9,8},{8,9},{13,10... | collective-permute-start | bytes 3145736 | tf_op jit(solution)/shard_map/ppermute | solution.py:402
  1089.4 66.5 %collective-permute-start.175 = (bf16[512,768]{1,0:T(8,128)(2,1)S(1)}, bf16[512,768]{1,0:T(8,128)(2,1)S(1)}, u32[]{:S(2)}, u32[]{:S(2)}) collective-permute-start(bf16[512,768]{1,0:T(8,128)(2,1)S(1)} %copy-done.104), channel_id=1, source_target_pairs={{0,3},{1,0},{2,1},{3,2},{4,7},{5,4},{6,5},{7,6},{8,11},{9,8},{10,9... | collective-permute-start | bytes 2359304 | tf_op jit(solution)/shard_map/ppermute | solution.py:322
  1097.5 96.4 %collective-permute-start.186 = (bf16[512,768]{1,0:T(8,128)(2,1)S(1)}, bf16[512,768]{1,0:T(8,128)(2,1)S(1)}, u32[]{:S(2)}, u32[]{:S(2)}) collective-permute-start(bf16[512,768]{1,0:T(8,128)(2,1)S(1)} %copy-done.103), channel_id=1, source_target_pairs={{0,3},{1,0},{2,1},{3,2},{4,7},{5,4},{6,5},{7,6},{8,11},{9,8},{10,9... | collective-permute-start | bytes 2359304 | tf_op jit(solution)/shard_map/ppermute | solution.py:322
  1117.4 108.7 %collective-permute-start.197 = (bf16[512,768]{1,0:T(8,128)(2,1)S(1)}, bf16[512,768]{1,0:T(8,128)(2,1)S(1)}, u32[]{:S(2)}, u32[]{:S(2)}) collective-permute-start(bf16[512,768]{1,0:T(8,128)(2,1)S(1)} %copy-done.102), channel_id=1, source_target_pairs={{0,3},{1,0},{2,1},{3,2},{4,7},{5,4},{6,5},{7,6},{8,11},{9,8},{10,9... | collective-permute-start | bytes 2359304 | tf_op jit(solution)/shard_map/ppermute | solution.py:322
  1130.6 138.7 %collective-permute-start.177 = (bf16[512,768]{1,0:T(8,128)(2,1)S(1)}, bf16[512,768]{1,0:T(8,128)(2,1)S(1)}, u32[]{:S(2)}, u32[]{:S(2)}) collective-permute-start(bf16[512,768]{1,0:T(8,128)(2,1)S(1)} %slice_add_fusion.22), channel_id=1, source_target_pairs={{0,1},{1,2},{2,3},{3,0},{4,5},{5,6},{6,7},{7,4},{8,9},{9,10},{10,1... | collective-permute-start | bytes 2359304 | tf_op jit(solution)/shard_map/ppermute | solution.py:322
  1146.0 120.9 %collective-permute-start.159 = (bf16[1024,256]{1,0:T(8,128)(2,1)S(1)}, bf16[1024,256]{1,0:T(8,128)(2,1)S(1)}, u32[]{:S(2)}, u32[]{:S(2)}) collective-permute-start(bf16[1024,256]{1,0:T(8,128)(2,1)S(1)} %get-tuple-element.334), channel_id=1, source_target_pairs={{0,8},{4,12},{8,0},{12,4},{16,24},{20,28},{24,16},{28,20},{1,9},{5... | collective-permute-start | bytes 1572872 | tf_op jit(solution)/shard_map/ppermute | solution.py:317
  1155.9 112.0 %collective-permute-start.163 = (bf16[1024,256]{1,0:T(8,128)(2,1)S(1)}, bf16[1024,256]{1,0:T(8,128)(2,1)S(1)}, u32[]{:S(2)}, u32[]{:S(2)}) collective-permute-start(bf16[1024,256]{1,0:T(8,128)(2,1)S(1)} %get-tuple-element.335), channel_id=1, source_target_pairs={{0,16},{4,20},{8,24},{12,28},{16,0},{20,4},{24,8},{28,12},{1,17},{... | collective-permute-start | bytes 1572872 | tf_op jit(solution)/shard_map/ppermute | solution.py:317
  1193.9 107.5 %collective-permute-start.135 = (bf16[2048,512]{1,0:T(8,128)(2,1)}, bf16[2048,512]{1,0:T(8,128)(2,1)}, u32[]{:S(2)}, u32[]{:S(2)}) collective-permute-start(bf16[2048,512]{1,0:T(8,128)(2,1)} %convolution_convert_fusion.3), channel_id=1, source_target_pairs={{0,4},{4,0},{8,12},{12,8},{16,20},{20,16},{24,28},{28,24},{1,5},{5... | collective-permute-start | bytes 6291464 | tf_op jit(solution)/shard_map/ppermute | solution.py:317
  1226.1 53.9 %collective-permute-start.188 = (bf16[512,768]{1,0:T(8,128)(2,1)S(1)}, bf16[512,768]{1,0:T(8,128)(2,1)S(1)}, u32[]{:S(2)}, u32[]{:S(2)}) collective-permute-start(bf16[512,768]{1,0:T(8,128)(2,1)S(1)} %slice_add_fusion.20), channel_id=1, source_target_pairs={{0,1},{1,2},{2,3},{3,0},{4,5},{5,6},{6,7},{7,4},{8,9},{9,10},{10,1... | collective-permute-start | bytes 2359304 | tf_op jit(solution)/shard_map/ppermute | solution.py:322
  1399.5 66.2 %collective-permute-start.140 = (bf16[1024,512]{1,0:T(8,128)(2,1)S(1)}, bf16[1024,512]{1,0:T(8,128)(2,1)S(1)}, u32[]{:S(2)}, u32[]{:S(2)}) collective-permute-start(bf16[1024,512]{1,0:T(8,128)(2,1)S(1)} %copy-done.92), channel_id=1, source_target_pairs={{0,16},{4,20},{8,24},{12,28},{16,0},{20,4},{24,8},{28,12},{1,17},{... | collective-permute-start | bytes 3145736 | tf_op jit(solution)/shard_map/ppermute | solution.py:317
  1403.7 78.2 %collective-permute-start.139 = (bf16[1024,512]{1,0:T(8,128)(2,1)S(1)}, bf16[1024,512]{1,0:T(8,128)(2,1)S(1)}, u32[]{:S(2)}, u32[]{:S(2)}) collective-permute-start(bf16[1024,512]{1,0:T(8,128)(2,1)S(1)} %slice.624), channel_id=1, source_target_pairs={{0,16},{4,20},{8,24},{12,28},{16,0},{20,4},{24,8},{28,12},{1,17},{... | collective-permute-start | bytes 3145736 | tf_op jit(solution)/shard_map/ppermute | solution.py:317
  1481.8 61.9 %collective-permute-start.196 = (bf16[512,768]{1,0:T(8,128)(2,1)S(1)}, bf16[512,768]{1,0:T(8,128)(2,1)S(1)}, u32[]{:S(2)}, u32[]{:S(2)}) collective-permute-start(bf16[512,768]{1,0:T(8,128)(2,1)S(1)} %constant_dynamic-update-slice_fusion.39), channel_id=1, source_target_pairs={{0,4},{4,0},{8,12},{12,8},{16,20},{20,16},{24,28},{28,24},{1,5},{5... | collective-permute-start | bytes 2359304 | tf_op jit(solution)/shard_map/ppermute | solution.py:317
  (385 other events, 7846.0 us)

commit v3 on v2

--- a/solution.py
+++ b/solution.py
@@ -344,17 +344,15 @@
     return [piece, from_x, from_y, jnp.concatenate(far, 0)]
 
 
-def plane_sum(own, blocks):
+def plane_sum(own_head, own_tail, to_x, to_y, two_head, one_tail):
     low = jnp.bfloat16
-    half = own.shape[0] // 2
-    one, two, three = blocks
-    head_two = two[:half] + across(three[:half].astype(low), ACROSS_X)
-    head_own = own[:half] + across(one[:half].astype(low), ACROSS_X)
-    tail_one = one[half:] + across(three[half:].astype(low), ACROSS_Y)
-    tail_own = own[half:] + across(two[half:].astype(low), ACROSS_Y)
-    head_own = head_own + across(head_two.astype(low), ACROSS_Y)
-    tail_own = tail_own + across(tail_one.astype(low), ACROSS_X)
-    return jnp.concatenate([head_own, tail_own], 0)
+    from_x, from_y = across(to_x, ACROSS_X), across(to_y, ACROSS_Y)
+    half = own_head.shape[0]
+    two_head = two_head + from_x[half:]
+    one_tail = one_tail + from_y[half:]
+    own_head = own_head + from_x[:half] + across(two_head.astype(low), ACROSS_Y)
+    own_tail = own_tail + from_y[:half] + across(one_tail.astype(low), ACROSS_X)
+    return own_head, own_tail
 
 
 def sequence_pairs(turn):
@@ -388,16 +386,14 @@
         for turn in range(2)
     ]
     even = odd == 0
-    return rolled(
-        jnp.concatenate(
-            [jnp.where(even, came[0], came[1]), jnp.where(even, came[1], came[0])], 0
-        )
+    return jnp.concatenate(
+        [jnp.where(even, came[0], came[1]), jnp.where(even, came[1], came[0])], 0
     )
 
 
 def from_sequences(x):
     odd = lax.axis_index("shard") & 1
-    x = rolled(x).reshape(2, x.shape[0] // 2, x.shape[1])
+    x = x.reshape(2, x.shape[0] // 2, x.shape[1])
     came = [
         lax.ppermute(
             lax.dynamic_index_in_dim(x, turn ^ odd, 0, keepdims=False),
@@ -417,34 +413,41 @@
     )
 
 
-def gather_blocks(weights, first=()):
-    me = lax.axis_index("rep")
-    own = [column_block(weights, me ^ i) for i in range(8)]
-    came = ring_gather(after(own[0], *first))[1:]
-    rows = [[block] for block in own]
-    for shard in came:
-        for i, block in enumerate(plane_gather(shard)):
-            rows[2 * i].append(block)
-            rows[2 * i + 1].append(across(block, CORE))
-    return rows, came
-
-
-def spread_blocks(block, columns):
-    me = lax.axis_index("rep")
-    pieces = []
-    for piece in plane_gather(block):
-        pieces += [piece, across(piece, CORE)]
-    outs = []
-    start = 0
-    for width in columns:
-        out = jnp.zeros((block.shape[0], 8 * width), jnp.float32)
-        for i, piece in enumerate(pieces):
-            out = lax.dynamic_update_slice_in_dim(
-                out, piece[:, start : start + width].astype(jnp.float32), (me ^ i) * width, 1
-            )
-        outs.append(out)
-        start += width
-    return outs
+def spread_blocks(block):
+    own = jnp.concatenate(plane_gather(block), 0)
+    return own, across(own, CORE)
+
+
+def whole_body(me, own, other, out):
+    mine = (me[0] ^ pl.program_id(0)) & 1 == 0
+
+    @pl.when(mine)
+    def _():
+        out[...] = own[...].astype(jnp.float32)
+
+    @pl.when(jnp.logical_not(mine))
+    def _():
+        out[...] = other[...].astype(jnp.float32)
+
+
+def whole_columns(me, own, other, first, width):
+    rows = own.shape[0] // 4
+    spec = pl.BlockSpec((rows, width), lambda i, at: ((at[0] ^ i) >> 1, first // width))
+    return pl.pallas_call(
+        whole_body,
+        grid_spec=pltpu.PrefetchScalarGridSpec(
+            num_scalar_prefetch=1,
+            grid=(8,),
+            in_specs=[spec, spec],
+            out_specs=pl.BlockSpec((rows, width), lambda i, at: (0, i)),
+        ),
+        out_shape=jax.ShapeDtypeStruct((rows, 8 * width), jnp.float32),
+        compiler_params=pltpu.CompilerParams(vmem_limit_bytes=VMEM_BYTES),
+        cost_estimate=pl.CostEstimate(
+            flops=rows * 8 * width, bytes_accessed=48 * rows * width, transcendentals=0
+        ),
+        name="whole_columns",
+    )(me, own, other)
 
 
 def everywhere_sum(x):
@@ -474,26 +477,34 @@
     return raw * inverse, inverse
 
 
-def project_body(normed, w0, w1, w2, w3, cosine, sine, gains, raw, query, key, value):
-    weights = (w0, w1, w2, w3)
-    step = w0.shape[0]
+def project_body(
+    normed, own0, side0, far0, own1, side1, far1, cosine, sine, gains, raw, query, key_value
+):
+    step = own0.shape[0]
     dim = cosine.shape[1]
-    raw[...] = sum(
-        jnp.dot(
-            normed[:, i * step : (i + 1) * step], weights[i][...],
-            preferred_element_type=jnp.float32,
+    for block, (own, side, far) in enumerate(((own0, side0, far0), (own1, side1, far1))):
+        at = block * 4 * dim
+        raw[:, at : at + 4 * dim] = (
+            jnp.dot(normed[:, :step], own[...], preferred_element_type=jnp.float32)
+            + jnp.dot(
+                normed[:, step : 2 * step], side[:step], preferred_element_type=jnp.float32
+            )
+            + jnp.dot(
+                normed[:, 2 * step : 3 * step], far[...], preferred_element_type=jnp.float32
+            )
+            + jnp.dot(normed[:, 3 * step :], side[step:], preferred_element_type=jnp.float32)
         )
-        for i in range(4)
-    )
-    for i in range(3):
-        unit, _ = unit_of(raw[:, i * dim : (i + 1) * dim])
-        head = unit * gains[i // 2 : i // 2 + 1, :]
-        head = (head * cosine[...] + turned(head) * sine[...]).astype(jnp.bfloat16)
-        if i < 2:
-            query[:, i * dim : (i + 1) * dim] = head
-        else:
-            key[...] = head
-    value[...] = raw[:, 3 * dim :].astype(jnp.bfloat16)
+        for i in range(3):
+            unit, _ = unit_of(raw[:, at + i * dim : at + (i + 1) * dim])
+            head = unit * gains[i // 2 : i // 2 + 1, :]
+            head = (head * cosine[...] + turned(head) * sine[...]).astype(jnp.bfloat16)
+            if i < 2:
+                query[:, (2 * block + i) * dim : (2 * block + i + 1) * dim] = head
+            else:
+                key_value[:, 2 * block * dim : (2 * block + 1) * dim] = head
+        key_value[:, (2 * block + 1) * dim : (2 * block + 2) * dim] = raw[
+            :, at + 3 * dim : at + 4 * dim
+        ].astype(jnp.bfloat16)
 
 
 def window_scores(info, query, keys, part, scale):
@@ -507,82 +518,99 @@
     return nt(query, keys) * scale, allowed
 
 
-def near(before, own, part):
+def key_columns(block, dim):
+    key = slice(2 * block * dim, (2 * block + 1) * dim)
+    value = slice((2 * block + 1) * dim, (2 * block + 2) * dim)
+    return key, value
+
+
+def seen_pair(before, own, part, block, dim):
+    here, there = key_columns(block, dim), key_columns(1 - block, dim)
     rows = own.shape[0] // 2
     if part == 0:
-        return jnp.concatenate([before[...], own[:rows]], 0)
-    return jnp.concatenate([before[rows:], own[...]], 0)
-
-
-def attend_body(info, query, key_before, key, value_before, value, mixed, log_total):
-    dim = key.shape[1]
+        return [
+            jnp.concatenate([before[:, t], own[:rows, h]], 0) for h, t in zip(here, there)
+        ]
+    return [jnp.concatenate([before[rows:, t], own[:, h]], 0) for h, t in zip(here, there)]
+
+
+def attend_body(info, query, before, own, mixed, log_total):
+    dim = own.shape[1] // 4
     rows = query.shape[0] // 2
     for part in range(2):
-        keys, values = near(key_before, key, part), near(value_before, value, part)
         at = slice(part * rows, (part + 1) * rows)
-        for head in range(2):
-            on = slice(head * dim, (head + 1) * dim)
-            score, allowed = window_scores(info, query[at, on], keys, part, dim**-0.5)
-            score = jnp.where(allowed, score, NEG)
-            top = jnp.max(score, -1, keepdims=True)
-            expo = jnp.exp(score - top)
-            total = jnp.sum(expo, -1, keepdims=True)
-            prob = (expo * (1.0 / total)).astype(jnp.bfloat16)
-            mixed[at, on] = jnp.dot(prob, values, preferred_element_type=jnp.float32).astype(
-                jnp.bfloat16
-            )
-            log_total[at, on] = jnp.broadcast_to(top + jnp.log(total), (rows, dim))
+        for block in range(2):
+            keys, values = seen_pair(before, own, part, block, dim)
+            for head in (2 * block, 2 * block + 1):
+                on = slice(head * dim, (head + 1) * dim)
+                score, allowed = window_scores(info, query[at, on], keys, part, dim**-0.5)
+                score = jnp.where(allowed, score, NEG)
+                top = jnp.max(score, -1, keepdims=True)
+                expo = jnp.exp(score - top)
+                total = jnp.sum(expo, -1, keepdims=True)
+                prob = (expo * (1.0 / total)).astype(jnp.bfloat16)
+                mixed[at, on] = jnp.dot(
+                    prob, values, preferred_element_type=jnp.float32
+                ).astype(jnp.bfloat16)
+                log_total[at, on] = jnp.broadcast_to(top + jnp.log(total), (rows, dim))
 
 
 def attend_back_body(
-    info, query, key_before, key, value_before, value, log_total, grad_mixed, raw, cosine, sine,
-    gain, grad_query, grad_own, grad_before, gain_part, grad_keys, grad_values,
+    info, query, before, own, log_total, grad_mixed, raw, cosine, sine, gain,
+    grad_query, grad_own, grad_before, gain_part, grad_keys, grad_values,
 ):
-    dim = key.shape[1]
+    dim = own.shape[1] // 4
     rows = query.shape[0] // 2
     scale = dim**-0.5
-    grad_keys[...] = jnp.zeros_like(grad_keys)
-    grad_values[...] = jnp.zeros_like(grad_values)
     gain_total = jnp.zeros((1, dim), jnp.float32)
-    for part in range(2):
-        keys, values = near(key_before, key, part), near(value_before, value, part)
-        at = slice(part * rows, (part + 1) * rows)
-        seen = slice(part * rows, part * rows + keys.shape[0])
-        for head in range(2):
-            on = slice(head * dim, (head + 1) * dim)
-            score, allowed = window_scores(info, query[at, on], keys, part, scale)
-            prob = jnp.where(allowed, jnp.exp(score - log_total[at, on][:, :1]), 0.0)
-            grad_prob = nt(grad_mixed[at, on], values)
-            inner = jnp.sum(prob * grad_prob, -1, keepdims=True)
-            grad_score = (prob * (grad_prob - inner)).astype(jnp.bfloat16)
-            grad_values[seen, :] += tn(prob.astype(jnp.bfloat16), grad_mixed[at, on])
-            grad_keys[seen, :] += tn(grad_score, query[at, on]) * scale
-            back = jnp.dot(grad_score, keys, preferred_element_type=jnp.float32) * scale
-            back = back * cosine[at, :] - turned(back) * sine[at, :]
-            unit, inverse = unit_of(raw[at, on])
-            gain_total += jnp.sum(unit * back, 0, keepdims=True)
-            back = back * gain[...]
-            back = inverse * (back - unit * jnp.mean(back * unit, -1, keepdims=True))
-            grad_query[at, on] = back.astype(jnp.bfloat16)
+    for block in range(2):
+        grad_keys[...] = jnp.zeros_like(grad_keys)
+        grad_values[...] = jnp.zeros_like(grad_values)
+        for part in range(2):
+            keys, values = seen_pair(before, own, part, block, dim)
+            at = slice(part * rows, (part + 1) * rows)
+            seen = slice(part * rows, part * rows + keys.shape[0])
+            for head in (2 * block, 2 * block + 1):
+                on = slice(head * dim, (head + 1) * dim)
+                score, allowed = window_scores(info, query[at, on], keys, part, scale)
+                prob = jnp.where(allowed, jnp.exp(score - log_total[at, on][:, :1]), 0.0)
+                grad_prob = nt(grad_mixed[at, on], values)
+                inner = jnp.sum(prob * grad_prob, -1, keepdims=True)
+                grad_score = (prob * (grad_prob - inner)).astype(jnp.bfloat16)
+                grad_values[seen, :] += tn(prob.astype(jnp.bfloat16), grad_mixed[at, on])
+                grad_keys[seen, :] += tn(grad_score, query[at, on]) * scale
+                back = jnp.dot(grad_score, keys, preferred_element_type=jnp.float32) * scale
+                back = back * cosine[at, :] - turned(back) * sine[at, :]
+                there = (2 * head - head % 2) * dim
+                unit, inverse = unit_of(raw[at, there : there + dim])
+                gain_total += jnp.sum(unit * back, 0, keepdims=True)
+                back = back * gain[...]
+                back = inverse * (back - unit * jnp.mean(back * unit, -1, keepdims=True))
+                grad_query[at, on] = back.astype(jnp.bfloat16)
+        for grad, here, there in zip(
+            (grad_keys, grad_values), key_columns(block, dim), key_columns(1 - block, dim)
+        ):
+            grad_before[:, there] = grad[: 2 * rows, :].astype(jnp.bfloat16)
+            grad_own[:, here] = grad[2 * rows :, :]
     gain_part[...] = gain_total
-    grad_before[:, :dim] = grad_keys[: 2 * rows, :].astype(jnp.bfloat16)
-    grad_before[:, dim:] = grad_values[: 2 * rows, :].astype(jnp.bfloat16)
-    grad_own[:, :dim] = grad_keys[2 * rows :, :]
-    grad_own[:, dim:] = grad_values[2 * rows :, :]
-
-
-def finish_body(grad_query, grad_own, came, raw, cosine, sine, gain, grad_block, gain_part):
+
+
+def finish_body(grad_query, grad_own, came, raw, cosine, sine, gain, even, odd, gain_part):
     dim = cosine.shape[1]
-    back = grad_own[:, :dim] + came[:, :dim].astype(jnp.float32)
-    back = back * cosine[...] - turned(back) * sine[...]
-    unit, inverse = unit_of(raw[...])
-    gain_part[...] = jnp.sum(unit * back, 0, keepdims=True)
-    back = back * gain[...]
-    back = inverse * (back - unit * jnp.mean(back * unit, -1, keepdims=True))
-    grad_block[:, : 2 * dim] = grad_query[...]
-    grad_block[:, 2 * dim : 3 * dim] = back.astype(jnp.bfloat16)
-    grad_value = grad_own[:, dim:] + came[:, dim:].astype(jnp.float32)
-    grad_block[:, 3 * dim :] = grad_value.astype(jnp.bfloat16)
+    total = jnp.zeros((1, dim), jnp.float32)
+    for block, out in enumerate((even, odd)):
+        key, value = key_columns(block, dim)
+        back = grad_own[:, key] + came[:, key].astype(jnp.float32)
+        back = back * cosine[...] - turned(back) * sine[...]
+        unit, inverse = unit_of(raw[:, (4 * block + 2) * dim : (4 * block + 3) * dim])
+        total += jnp.sum(unit * back, 0, keepdims=True)
+        back = back * gain[...]
+        back = inverse * (back - unit * jnp.mean(back * unit, -1, keepdims=True))
+        out[:, : 2 * dim] = grad_query[:, 2 * block * dim : (2 * block + 2) * dim]
+        out[:, 2 * dim : 3 * dim] = back.astype(jnp.bfloat16)
+        grad_value = grad_own[:, value] + came[:, value].astype(jnp.float32)
+        out[:, 3 * dim :] = grad_value.astype(jnp.bfloat16)
+    gain_part[...] = total
 
 
 def vmem_call(body, outs, flops, scratch=(), scalars=0, specs=None, name=None):
@@ -627,54 +655,70 @@
     grad_up[...] = (grad_act * swish).astype(jnp.bfloat16)
 
 
-def hidden_units(mid, grad_y, gate_w, up_w, down_w):
+def hidden_units(mid, grad_y, gate_up_w, down_w):
     rows, width = mid.shape
-    units = gate_w.shape[1]
-    high, cut = rows // 2, units // 6
+    units = down_w.shape[1]
+    high, cut = rows // 2, units // 3
     row_spec = pl.BlockSpec((high, width), lambda i, j: (i, 0))
-    weight_spec = pl.BlockSpec((width, cut), lambda i, j: (0, j))
     out_spec = pl.BlockSpec((high, cut), lambda i, j: (i, j))
     return pl.pallas_call(
         hidden_body,
-        grid=(2, 6),
+        grid=(2, 3),
         out_shape=[jax.ShapeDtypeStruct((rows, units), jnp.bfloat16)] * 3,
-        in_specs=[row_spec, row_spec, weight_spec, weight_spec, weight_spec],
+        in_specs=[
+            row_spec,
+            row_spec,
+            pl.BlockSpec((width, cut), lambda i, j: (0, j)),
+            pl.BlockSpec((width, cut), lambda i, j: (0, j + 3)),
+            pl.BlockSpec((width, cut), lambda i, j: (0, j)),
+        ],
         out_specs=[out_spec] * 3,
         compiler_params=pltpu.CompilerParams(vmem_limit_bytes=VMEM_BYTES),
         cost_estimate=pl.CostEstimate(
             flops=6 * rows * width * units, bytes_accessed=10 * rows * width, transcendentals=0
         ),
         name="hidden_units",
-    )(mid, grad_y, gate_w, up_w, down_w)
-
-
-def from_hidden(lefts, rights, first_block, blocks):
-    count = len(lefts)
-    rows, units = lefts[0].shape[0] // 4, lefts[0].shape[1]
-    width = rights[0].shape[0]
+    )(mid, grad_y, gate_up_w, gate_up_w, down_w)
+
+
+def from_hidden(pairs, first, step):
+    count = len(pairs)
+    rows, units = pairs[0][0].shape[0] // 8, pairs[0][0].shape[1]
+    width = pairs[0][1].shape[0]
     cut = width // 4
 
     def body(*refs):
-        out = refs[-1]
-        out[...] = sum(nt(refs[i][...], refs[count + i][...]) for i in range(count)).astype(
-            jnp.bfloat16
-        )
-
+        refs, out = refs[:-1], refs[-1]
+        out[...] = sum(
+            nt(
+                jnp.concatenate([refs[3 * i][...], refs[3 * i + 1][...]], 0),
+                refs[3 * i + 2][...],
+            )
+            for i in range(count)
+        ).astype(jnp.bfloat16)
+
+    specs, args = [], []
+    for left, right, at in pairs:
+        specs += [
+            pl.BlockSpec((rows, units), lambda j: (first, 0)),
+            pl.BlockSpec((rows, units), lambda j: (first + step, 0)),
+            pl.BlockSpec((cut, units), lambda j, at=at: (j, at)),
+        ]
+        args += [left, left, right]
     return pl.pallas_call(
         body,
-        grid=(blocks, 4),
-        out_shape=jax.ShapeDtypeStruct((blocks * rows, width), jnp.bfloat16),
-        in_specs=[pl.BlockSpec((rows, units), lambda i, j: (i + first_block, 0))] * count
-        + [pl.BlockSpec((cut, units), lambda i, j: (j, 0))] * count,
-        out_specs=pl.BlockSpec((rows, cut), lambda i, j: (i, j)),
+        grid=(4,),
+        out_shape=jax.ShapeDtypeStruct((2 * rows, width), jnp.bfloat16),
+        in_specs=specs,
+        out_specs=pl.BlockSpec((2 * rows, cut), lambda j: (0, j)),
         compiler_params=pltpu.CompilerParams(vmem_limit_bytes=VMEM_BYTES),
         cost_estimate=pl.CostEstimate(
-            flops=2 * count * blocks * rows * width * units,
+            flops=4 * count * rows * width * units,
             bytes_accessed=2 * count * width * units,
             transcendentals=0,
         ),
         name="from_hidden",
-    )(*lefts, *rights)
+    )(*args)
 
 
 def on_device_block(
@@ -702,13 +746,32 @@
     core = me & 1
     count = lax.axis_size("rep")
 
-    qkv_rows, qkv_came = gather_blocks((w_query, key_matrix, value_matrix))
-    x_low = to_sequences(after(tokens, qkv_came[0], qkv_came[2]))
+    own_blocks = [
+        column_block((w_query, key_matrix, value_matrix), me ^ i) for i in range(8)
+    ]
+    before, behind = around(own_blocks[0], 1), around(own_blocks[0], -1)
+    x_low = to_sequences(after(tokens, before, behind))
     rows = x_low.shape[0]
-    out_rows, out_came = gather_blocks((w_out,), (x_low,))
+    far = around(before, 1)
+    side_blocks = plane_gather(jnp.concatenate([before, behind], 0))
+    far_blocks = plane_gather(far)
+    other_side = [across(block, CORE) for block in side_blocks]
+    other_far = [across(block, CORE) for block in far_blocks]
+    qkv_refs = [
+        (
+            own_blocks[2 * i], side_blocks[i], far_blocks[i],
+            own_blocks[2 * i + 1], other_side[i], other_far[i],
+        )
+        for i in range(4)
+    ]
+    out_own = lax.all_gather(
+        after(column_block((w_out,), me), far), "shard", axis=0, tiled=True
+    )
+    gain_parts = jnp.stack([attn_gain, mlp_gain])
     gains = jnp.concatenate(
-        ring_gather(jnp.stack([attn_gain, mlp_gain])), 1
+        [gain_parts, *(around(gain_parts, by) for by in (1, 2, 3))], 1
     ).astype(full)
+    gains = rolled(gains)
     attn_gains, mlp_gains = gains[:1], gains[1:]
     query_gains = query_gain.astype(full)[None]
     key_gains = key_gain.astype(full)[None]
@@ -727,64 +790,49 @@
     cosine, sine = cosine[0, :, 0], sine[0, :, 0]
     sine = jnp.concatenate([-sine[:, : head_dim // 2], sine[:, head_dim // 2 :]], 1)
 
-    gate_up_own = [column_block((w_gate, w_up), me ^ i) for i in range(2)]
-    down_own = [column_block((w_down,), me ^ i) for i in range(2)]
-    gate_up_came = ring_gather(after(gate_up_own[0], *out_came))[1:]
-    grad_y_low = to_sequences(after(cotangent, gate_up_came[0], gate_up_came[2]))
-    down_came = ring_gather(after(down_own[0], grad_y_low))[1:]
-
-    def whole(own, came):
-        came = [own[0], *came], [own[1], *(across(c, CORE) for c in came)]
-        return [jnp.concatenate(part, 0) for part in came]
-
-    gate_up = whole(gate_up_own, gate_up_came)
-    units = gate_up[0].shape[1] // 2
-    gate_all = jnp.concatenate([part[:, :units] for part in gate_up], 1)
-    up_all = jnp.concatenate([part[:, units:] for part in gate_up], 1)
-    down_all = jnp.concatenate(whole(down_own, down_came), 1)
+    gate_up_own = lax.all_gather(
+        after(column_block((w_gate, w_up), me), out_own), "shard", axis=0, tiled=True
+    )
+    down_own = lax.all_gather(
+        after(column_block((w_down,), me), gate_up_own), "shard", axis=0, tiled=True
+    )
+    out_chips = plane_gather(after(out_own, *far_blocks))
+    out_blocks = [block for chip in out_chips for block in (chip, across(chip, CORE))]
+    grad_y_low = to_sequences(after(cotangent, out_own))
+    gate_up = [gate_up_own, across(gate_up_own, CORE)]
+    down = [down_own, across(down_own, CORE)]
+    units = down_own.shape[1]
 
     x_rows = x_low.astype(full)
     inverse_in = lax.rsqrt(jnp.mean(x_rows * x_rows, -1, keepdims=True) + EPS)
     x_unit = x_rows * inverse_in
-    normed = (x_unit * attn_gains).astype(low)
-    pair_columns = 2 * head_dim
-    head_rows = jax.ShapeDtypeStruct((rows, head_dim), low)
-    pair_rows = jax.ShapeDtypeStruct((rows, pair_columns), low)
+    normed = rolled((x_unit * attn_gains).astype(low))
+    head_columns = 2 * head_dim
+    block_columns = 4 * head_dim
+    quad_rows = jax.ShapeDtypeStruct((rows, block_columns), low)
     project = vmem_call(
         project_body,
-        [jax.ShapeDtypeStruct((rows, 2 * pair_columns), full), pair_rows, head_rows, head_rows],
-        4 * rows * width * pair_columns,
+        [jax.ShapeDtypeStruct((rows, 2 * block_columns), full), quad_rows, quad_rows],
+        4 * rows * width * block_columns,
         name="project",
     )
     attend = vmem_call(
         attend_body,
-        [pair_rows, jax.ShapeDtypeStruct((rows, pair_columns), full)],
-        12 * rows * rows * pair_columns,
+        [quad_rows, jax.ShapeDtypeStruct((rows, block_columns), full)],
+        12 * rows * rows * block_columns,
         scalars=1,
         name="attend",
     )
     head_gains = jnp.concatenate([query_gains, key_gains], 0)
     upward = [(i, i + 1) for i in range(0, count, 2)]
     downward = [(i + 1, i) for i in range(0, count, 2)]
-    raws, queries, kept, own_pairs = [], [], [], []
-    for i in range(8):
-        raw, query, key, value = project(normed, *qkv_rows[i], cosine, sine, head_gains)
-        raws.append(raw)
-        queries.append(query)
-        own_pairs.append((key, value))
-    mixed_blocks, log_totals = [], []
-    for i in range(8):
-        key, value = own_pairs[i]
-        key_before, value_before = (
-            lax.ppermute(part, "rep", upward) for part in own_pairs[i ^ 1]
-        )
-        pairs = (key_before, key, value_before, value)
-        mixed, log_total = attend(info, queries[i], *pairs)
-        kept.append(pairs)
-        mixed_blocks.append(mixed)
-        log_totals.append(log_total)
-    mixed = jnp.concatenate(mixed_blocks, 1)
-    out_all = jnp.concatenate([jnp.concatenate(r, 0) for r in out_rows], 1)
+    projected = [project(normed, *qkv_refs[i], cosine, sine, head_gains) for i in range(4)]
+    earlier = [lax.ppermute(p[2], "rep", upward) for p in projected]
+    attended = [
+        attend(info, projected[i][1], earlier[i], projected[i][2]) for i in range(4)
+    ]
+    mixed = jnp.concatenate([a[0] for a in attended], 1)
+    out_all = jnp.concatenate(out_blocks, 1)
     branch = jnp.einsum("rf,nf->rn", mixed, out_all, preferred_element_type=full)
 
     resid = x_rows + branch
@@ -794,99 +842,133 @@
     mid_all = jnp.concatenate(plane_gather(mid), 0)
     grad_y_low = jnp.where(valid, grad_y_low, jnp.zeros_like(grad_y_low))
     grad_y_all = jnp.concatenate(plane_gather(grad_y_low), 0)
-    act, grad_gate, grad_up = hidden_units(mid_all, grad_y_all, gate_all, up_all, down_all)
-
-    def plane_total(lefts, rights):
-        far = from_hidden(lefts, rights, 1, 3)
-        own = from_hidden([after(left, far) for left in lefts], rights, 0, 1)
-        return plane_sum(own.astype(full), jnp.split(far, 3, 0))
-
-    grad_mid = plane_total((grad_gate, grad_up), (gate_all, up_all))
-    mlp_out = plane_total((act,), (down_all,))
-    output = from_sequences(jnp.where(valid, resid + mlp_out, 0.0).astype(low))
-
-    others = [
-        outer(left, right[:, units:]).astype(low)
-        for left, right in ((grad_y_all, act), (mid_all, grad_gate), (mid_all, grad_up))
-    ]
-    owns = [
-        (outer(left, right[:, :units]) + across(other, CORE)).astype(low)
-        for (left, right), other in zip(
-            ((grad_y_all, act), (mid_all, grad_gate), (mid_all, grad_up)), others
+    hidden = [hidden_units(mid_all, grad_y_all, gate_up[i], down[i]) for i in range(2)]
+
+    def plane_total(pairs, first=()):
+        def some(at, step, *done):
+            left = after(pairs[0][0], *done) if done else pairs[0][0]
+            return from_hidden([(left, *pairs[0][1:]), *pairs[1:]], at, step)
+
+        to_x = some(2, 4, *first)
+        to_y = some(5, 2, to_x)
+        rest = some(3, 1, to_y)
+        own = some(0, 1, rest)
+        half = own.shape[0] // 2
+        parts = plane_sum(
+            own[:half].astype(full), own[half:].astype(full), to_x, to_y,
+            rest[half:].astype(full), rest[:half].astype(full),
         )
+        return jnp.concatenate(parts, 0)
+
+    grad_mid = plane_total(
+        [(hidden[i][1 + j], gate_up[i], j) for i in range(2) for j in range(2)]
+    )
+    others, owns = [], []
+    for i, left in ((0, grad_y_all), (1, mid_all), (2, mid_all)):
+        others.append(outer(left, hidden[1][i]).astype(low))
+    for i, left in ((0, grad_y_all), (1, mid_all), (2, mid_all)):
+        owns.append((outer(left, hidden[0][i]) + across(others[i], CORE)).astype(low))
+    totals = [
+        lax.psum_scatter(own, "shard", scatter_dimension=0, tiled=True) for own in owns
     ]
     grad_mid = after(grad_mid, *owns)
-    totals = [ring_sum(jnp.split(own, shards, 0), low).astype(low) for own in owns]
-    (grad_down_total,), (grad_gate_total,), (grad_up_total,) = (
-        spread_blocks(total, (units,)) for total in totals
+    mlp_out = plane_total([(hidden[i][0], down[i], 0) for i in range(2)], (grad_mid,))
+    output = from_sequences(jnp.where(valid, resid + mlp_out, 0.0).astype(low))
+    my_group = me.astype(jnp.int32)[None]
+    grad_down_total, grad_gate_total, grad_up_total = (
+        whole_columns(my_group, *spread_blocks(total), 0, units) for total in totals
     )
 
     mlp_gain_part = jnp.sum(mid_unit * grad_mid, 0)
     grad_resid = grad_y_low.astype(full) + norm_back(mid_unit, inverse_mid, grad_mid * mlp_gains)
     resid_low = grad_resid.astype(low)
     grad_mixed = jnp.dot(resid_low, out_all, preferred_element_type=full).astype(low)
-    grad_blocks = [None] * 8
-    query_gain_part, key_gain_part = 0.0, 0.0
+    attend_back = [
+        vmem_call(
+            attend_back_body,
+            [
+                quad_rows,
+                jax.ShapeDtypeStruct((rows, block_columns), full),
+                quad_rows,
+                jax.ShapeDtypeStruct((1, head_dim), full),
+            ],
+            30 * rows * rows * block_columns,
+            scratch=[pltpu.VMEM((2 * rows, head_dim), full)] * 2,
+            scalars=1,
+            specs={5: column_spec(rows, block_columns, i)},
+            name="attend_back",
+        )
+        for i in range(4)
+    ]
     finish = vmem_call(
         finish_body,
-        [
-            jax.ShapeDtypeStruct((rows, 2 * pair_columns), low),
-            jax.ShapeDtypeStruct((1, head_dim), full),
-        ],
+        [quad_rows, quad_rows, jax.ShapeDtypeStruct((1, head_dim), full)],
         rows * head_dim,
-        specs={3: column_spec(rows, head_dim, 2)},
         name="finish",
     )
-    order = (7, 6, 3, 2, 5, 4, 1, 0)
-    backs = [None] * 8
+    order = (3, 1, 2, 0)
+    order_of_chips = (1, 3, 2, 0)
+    backs, finished = {}, {}
     for i in order:
-        attend_back = vmem_call(
-            attend_back_body,
-            [
-                pair_rows,
-                jax.ShapeDtypeStruct((rows, pair_columns), full),
-                pair_rows,
-                jax.ShapeDtypeStruct((1, head_dim), full),
-            ],
-            30 * rows * rows * pair_columns,
-            scratch=[pltpu.VMEM((2 * rows, head_dim), full)] * 2,
-            scalars=1,
-            specs={
-                7: column_spec(rows, pair_columns, i),
-                8: column_spec(rows, pair_columns, 0),
-            },
-            name="attend_back",
-        )
-        backs[i] = attend_back(
-            info, queries[i], *kept[i], log_totals[i], grad_mixed, raws[i], cosine, sine,
+        raw, query, own_pair = projected[i]
+        backs[i] = attend_back[i](
+            info, query, earlier[i], own_pair, attended[i][1], grad_mixed, raw, cosine, sine,
             query_gains,
         )
-        query_gain_part += backs[i][3]
     for i in order:
-        came = lax.ppermute(backs[i ^ 1][2], "rep", downward)
-        grad_blocks[i], part = finish(
-            backs[i][0], backs[i][1], came, raws[i], cosine, sine, key_gains
+        came = lax.ppermute(backs[i][2], "rep", downward)
+        finished[i] = finish(
+            backs[i][0], backs[i][1], came, projected[i][0], cosine, sine, key_gains
         )
-        key_gain_part += part
-
-    def block_totals(left, blocks):
-        chips = [None] * 4
-        for i in (3, 1, 2, 0):
-            other = outer(left, blocks[2 * i + 1]).astype(low)
-            chips[i] = outer(left, blocks[2 * i]) + across(other, CORE)
-        own = plane_sum(chips[0], chips[1:])
+    query_gain_part = sum(backs[i][3] for i in order)
+    key_gain_part = sum(finished[i][2] for i in order)
+
+    def block_total(left, even, odd):
+        columns = even[0].shape[1]
+        half = width // 2
+        even, odd = jnp.concatenate(even, 1), jnp.concatenate(odd, 1)
+        other = outer(left, odd).astype(low)
+        total = outer(left, even) + across(other, CORE)
+        to_x = total[:half, : 2 * columns].astype(low)
+        to_y = total[half:, columns : 3 * columns].astype(low)
+        head, tail = plane_sum(
+            total[:half, 3 * columns :], total[half:, 3 * columns :],
+            jnp.concatenate([to_x[:, :columns], to_x[:, columns:]], 0),
+            jnp.concatenate([to_y[:, columns:], to_y[:, :columns]], 0),
+            total[:half, 2 * columns : 3 * columns], total[half:, :columns],
+        )
+        own = jnp.concatenate([head, tail], 0)
         return ring_sum(jnp.split(own, shards, 0), low).astype(low)
 
-    out_total = block_totals(resid_low, mixed_blocks)
-    (grad_out_total,) = spread_blocks(out_total, (pair_columns,))
-    qkv_total = block_totals(normed, grad_blocks)
-    grad_query_total, grad_key_total, grad_value_total = spread_blocks(
-        qkv_total, (pair_columns, head_dim, head_dim)
-    )
-
-    grad_qkv = jnp.concatenate(grad_blocks, 1)
-    qkv_all = jnp.concatenate([jnp.concatenate(r, 0) for r in qkv_rows], 1)
-    grad_in = jnp.einsum("rf,nf->rn", grad_qkv, qkv_all, preferred_element_type=full)
+    out_total = block_total(
+        rolled(resid_low),
+        [attended[i][0][:, :head_columns] for i in order_of_chips],
+        [attended[i][0][:, head_columns:] for i in order_of_chips],
+    )
+    qkv_total = block_total(
+        normed,
+        [finished[i][0] for i in order_of_chips],
+        [finished[i][1] for i in order_of_chips],
+    )
+    grad_out_total = whole_columns(my_group, *spread_blocks(out_total), 0, head_columns)
+    qkv_spread = spread_blocks(qkv_total)
+    grad_query_total = whole_columns(my_group, *qkv_spread, 0, head_columns)
+    grad_key_total = whole_columns(my_group, *qkv_spread, head_columns, head_dim)
+    grad_value_total = whole_columns(my_group, *qkv_spread, 3 * head_dim, head_dim)
+
+    grad_qkv = jnp.concatenate([part for i in range(4) for part in finished[i][:2]], 1)
+    step = width // shards
+    qkv_all = jnp.concatenate(
+        [
+            jnp.concatenate([own, side[:step], ahead, side[step:]], 0)
+            for refs in qkv_refs
+            for own, side, ahead in (refs[:3], refs[3:])
+        ],
+        1,
+    )
+    grad_in = rolled(
+        jnp.einsum("rf,nf->rn", grad_qkv, qkv_all, preferred_element_type=full)
+    )
     grad_tokens = from_sequences(
         (grad_resid + norm_back(x_unit, inverse_in, grad_in * attn_gains)).astype(low)
     )
@@ -897,11 +979,12 @@
             [attn_gain_part, mlp_gain_part, query_gain_part[0], key_gain_part[0]]
         )
     )
-    wide = parts[: 2 * width].reshape(2, shards, width // shards)
-    wide = ring_sum([wide[:, i] for i in range(shards)], full)
+    for by in (1, 2):
+        parts = parts + lax.ppermute(parts, "shard", [(i, i ^ by) for i in range(shards)])
+    wide = lax.dynamic_slice_in_dim(
+        parts[: 2 * width].reshape(2, width), shard_at * step, step, 1
+    )
     narrow = parts[2 * width :]
-    for by in (1, 2):
-        narrow = narrow + lax.ppermute(narrow, "shard", [(i, i ^ by) for i in range(shards)])
     return (
         output,
         grad_tokens,

time: 1610 us -> 1210 us (0.75)
  waiting for transfers between devices: 548 us -> 304 us
  starting transfers between devices: 368 us -> 194 us
  Pallas kernels: 264 us -> 319 us
  other arithmetic: 149 us -> 120 us
    ppermute x33 -> x12, waiting for transfers between devices: 192 us -> 36.4 us  [around(): lax.ppermute(x, 'shard', [(i, (i + by) % count) for i in range(count)])]
    ppermute x141 -> x84, starting transfers between devices: 195 us -> 84 us  [across(): return lax.ppermute(x, 'rep', [(i, i ^ mask) for i in range(count)])]
    ppermute x141 -> x84, waiting for transfers between devices: 322 us -> 220 us  [across(): return lax.ppermute(x, 'rep', [(i, i ^ mask) for i in range(count)])]
    ppermute x33 -> x12, starting transfers between devices: 118 us -> 30.2 us  [around(): lax.ppermute(x, 'shard', [(i, (i + by) % count) for i in range(count)])]
    pallas_call x5 -> x17, Pallas kernels: 117 us -> 191 us  [the longest x8 76.6 us: from_hidden(): pl.pallas_call(body, grid=(4,), out_shape=jax.ShapeDtypeStruct((2 * rows,...]
    concatenate x10 -> x6, other arithmetic: 35.5 us -> 8.96 us  [the longest x1 2.52 us: on_device_block(): jnp.concatenate([jnp.concatenate([own, side[:step], ahead, side[step:]],...]
    dynamic_update_slice x49 -> x0, other arithmetic: 24.4 us -> none  [spread_blocks(): lax.dynamic_update_slice_in_dim(out, piece[:, start:start + width].astype...]
    ppermute x4, starting transfers between devices: 4.12 us -> 26.7 us  [from_sequences(): lax.ppermute(lax.dynamic_index_in_dim(x, turn ^ odd, 0, keepdims=False),...]
  transfers between devices with their start and end apart: 208 -> 120, of which waited for: 58 -> 35; matrix products, arithmetic and copies ran while one was open for 20% -> 29% of each run, Pallas kernels for 10% -> 22%
where the time goes in v3:
time: 1210 us; the launch traced here: 1200 us
  Pallas kernels  319 us (26%)
  waiting for transfers between devices  304 us (25%)
  starting transfers between devices  194 us (16%)
  matrix products  132 us (11%)
  other arithmetic  120 us (10%)
  local copies, waits for them, and re-layouts  116 us (10%)
  between operations  16.5 us (1%)
    ppermute x84, waiting for transfers between devices, across(): return lax.ppermute(x, 'rep', [(i, i ^ mask) for i in range(count)])  220 us
    pallas_call x16, Pallas kernels, call(): pl.pallas_call(body, grid=(1,), out_shape=outs, in_specs=in_specs, out_sp...  128 us
    dot_general x10, matrix products, outer(): jnp.einsum('rc,rf->cf', left, right, preferred_element_type=jnp.float32)  102 us
    ppermute x84, starting transfers between devices, across(): return lax.ppermute(x, 'rep', [(i, i ^ mask) for i in range(count)])  84 us
    pallas_call x8, Pallas kernels, from_hidden(): pl.pallas_call(body, grid=(4,), out_shape=jax.ShapeDtypeStruct((2 * rows,...  76.6 us
    pallas_call x2, Pallas kernels, hidden_units(): pl.pallas_call(hidden_body, grid=(2, 3), out_shape=[jax.ShapeDtypeStruct(...  57.9 us
    unnamed x326, local copies, waits for them, and re-layouts  57.7 us
    pallas_call x7, Pallas kernels, whole_columns(): pl.pallas_call(whole_body, grid_spec=pltpu.PrefetchScalarGridSpec(num_sca...  56.9 us
  transfers between devices with their start and end apart: 120, of which 35 were waited for; matrix products, arithmetic and copies ran while one was open for 29% of the time, Pallas kernels for 22%

profile of v3, /device:TPU:0, one launch (start us, length us, event | category | flops | bytes accessed | tf_op | source)
XLA Modules:
  0.0 1202.3 jit_solution(15875887980305346499)
XLA Ops:
  71.8 30.0 %collective-permute-done.4 = bf16[256,2048]{1,0:T(8,128)(2,1)S(1)} collective-permute-done((bf16[256,2048]{1,0:T(8,128)(2,1)}, bf16[256,2048]{1,0:T(8,128)(2,1)S(1)}, u32[]{:S(2)}, u32[]{:S(2)}) %collective-permute-start.4) | collective-permute-done | bytes 1048608 | tf_op jit(solution)/shard_map/ppermute | solution.py:381
  195.5 11.6 collective-permute-start.42
  227.7 17.5 %attend.5 = (bf16[512,512]{1,0:T(8,128)(2,1)}, f32[512,512]{1,0:T(8,128)}) custom-call(s32[2]{0:T(128)} %pad_add_fusion.info, bf16[512,512]{1,0:T(8,128)(2,1)} %get-tuple-element.85.query, bf16[512,512]{1,0:T(8,128)(2,1)} %copy-done.140, bf16[512,512]{1,0:T(8,128)(2,1)} %get-tuple-element.86.own), custom_call_target="tpu_custom_call" | custom-call | flops 1610612736 | bytes 1572872 | tf_op jit(solution)/shard_map/attend/pallas_call | solution.py:624
  255.3 12.2 %collective-permute-start.28 = (bf16[512,512]{1,0:T(8,128)(2,1)}, bf16[512,512]{1,0:T(8,128)(2,1)}, u32[]{:S(2)}, u32[]{:S(2)}) collective-permute-start(bf16[512,512]{1,0:T(8,128)(2,1)} %get-tuple-element.92.own), channel_id=1, source_target_pairs={{0,4},{8,12},{16,20},{24,28},{1,5},{9,13},{17,21},{25,29},{2,6},{1... | collective-permute-start | bytes 1572872 | tf_op jit(solution)/shard_map/ppermute | solution.py:830
  314.7 14.3 %collective-permute-done.43 = bf16[512,2048]{1,0:T(8,128)(2,1)} collective-permute-done((bf16[512,2048]{1,0:T(8,128)(2,1)}, bf16[512,2048]{1,0:T(8,128)(2,1)}, u32[]{:S(2)}, u32[]{:S(2)}) %collective-permute-start.43) | collective-permute-done | bytes 2097184 | tf_op jit(solution)/shard_map/ppermute | solution.py:317
  345.5 28.4 %collective-permute-done.37 = bf16[512,2048]{1,0:T(8,128)(2,1)S(1)} collective-permute-done((bf16[512,2048]{1,0:T(8,128)(2,1)}, bf16[512,2048]{1,0:T(8,128)(2,1)S(1)}, u32[]{:S(2)}, u32[]{:S(2)}) %collective-permute-start.37) | collective-permute-done | bytes 2097184 | tf_op jit(solution)/shard_map/ppermute | solution.py:317
  376.4 21.5 %collective-permute-done.45 = bf16[256,2048]{1,0:T(8,128)(2,1)S(1)} collective-permute-done((bf16[256,2048]{1,0:T(8,128)(2,1)S(1)}, bf16[256,2048]{1,0:T(8,128)(2,1)S(1)}, u32[]{:S(2)}, u32[]{:S(2)}) %collective-permute-start.45) | collective-permute-done | bytes 1048608 | tf_op jit(solution)/shard_map/ppermute | solution.py:317
  407.8 12.0 collective-permute-done.39
  426.9 29.1 %hidden_units.2 = (bf16[2048,768]{1,0:T(8,128)(2,1)}, bf16[2048,768]{1,0:T(8,128)(2,1)}, bf16[2048,768]{1,0:T(8,128)(2,1)}) custom-call(bf16[2048,2048]{1,0:T(8,128)(2,1)} %constant_dynamic-update-slice_fusion.14.mid, bf16[2048,2048]{1,0:T(8,128)(2,1)} %constant_dynamic-update-slice_fusion.19.grad_y, ...), custom_call_target="tpu_custom_call" | custom-call | flops 19327352832 | bytes 41943040 | tf_op jit(solution)/shard_map/hidden_units/pallas_call | solution.py:664
  457.8 28.8 %hidden_units.3 = (bf16[2048,768]{1,0:T(8,128)(2,1)}, bf16[2048,768]{1,0:T(8,128)(2,1)}, bf16[2048,768]{1,0:T(8,128)(2,1)}) custom-call(bf16[2048,2048]{1,0:T(8,128)(2,1)} %constant_dynamic-update-slice_fusion.14.mid, bf16[2048,2048]{1,0:T(8,128)(2,1)} %constant_dynamic-update-slice_fusion.19.grad_y, ...), custom_call_target="tpu_custom_call" | custom-call | flops 19327352832 | bytes 41943040 | tf_op jit(solution)/shard_map/hidden_units/pallas_call | solution.py:664
  486.5 11.4 from_hidden.8
  498.6 11.8 from_hidden.9
  522.2 11.7 from_hidden.10
  555.5 11.6 from_hidden.11
  572.8 12.9 %add_convert_fusion.1 = bf16[2048,768]{1,0:T(8,128)(2,1)} fusion(bf16[2048,768]{1,0:T(8,128)(2,1)} %collective-permute-done.54, bf16[2048,2048]{1,0:T(8,128)(2,1)} %constant_dynamic-update-slice_fusion.14.mid, bf16[2048,768]{1,0:T(8,128)(2,1)S(1)} %copy-done.5), kind=kOutput, calls=%fused_computation.4 | convolution fusion | flops 6447169536 | bytes 17825792 | tf_op jit(solution)/shard_map/rc,rf->cf/dot_general | solution.py:59
  603.7 12.6 %add_convert_fusion = bf16[2048,768]{1,0:T(8,128)(2,1)} fusion(bf16[2048,768]{1,0:T(8,128)(2,1)} %collective-permute-done.55, bf16[2048,2048]{1,0:T(8,128)(2,1)} %constant_dynamic-update-slice_fusion.14.mid, bf16[2048,768]{1,0:T(8,128)(2,1)S(1)} %copy-done.4), kind=kOutput, calls=%fused_computation.3 | convolution fusion | flops 6447169536 | bytes 17825792 | tf_op jit(solution)/shard_map/rc,rf->cf/dot_general | solution.py:59
  616.3 12.5 %add_convert_fusion.2 = bf16[2048,768]{1,0:T(8,128)(2,1)} fusion(bf16[2048,768]{1,0:T(8,128)(2,1)} %collective-permute-done.53, bf16[2048,2048]{1,0:T(8,128)(2,1)} %constant_dynamic-update-slice_fusion.19.grad_y, bf16[2048,768]{1,0:T(8,128)(2,1)S(1)} %copy-done.2), kind=kOutput, calls=%fused_computation.5 | convolution fusion | flops 6447169536 | bytes 17825792 | tf_op jit(solution)/shard_map/rc,rf->cf/dot_general | solution.py:59
  659.8 11.2 attend_back.5
  672.5 11.2 attend_back.6
  750.8 11.7 fusion.96
  793.7 13.3 %fusion.94 = (bf16[2048,2048]{1,0:T(8,128)(2,1)}, f32[2048,2048]{1,0:T(8,128)}) fusion(bf16[2048,2048]{1,0:T(8,128)(2,1)} %collective-permute-done.73, bf16[512,512]{1,0:T(8,128)(2,1)S(1)} %copy-done.48, bf16[512,512]{1,0:T(8,128)(2,1)S(1)} %copy-done.52, bf16[512,512]{1,0:T(8,128)(2,1)S(1)} %copy-done.54, bf16[512,512]{1,0:T(8,128)(2,1)S(1)} %copy-done.50, ...), kind=kOutput, calls=%fused_computation.308 | convolution fusion | flops 4324327424 | bytes 37748736 | tf_op jit(solution)/shard_map/rc,rf->cf/dot_general | solution.py:59
  819.6 11.6 collective-permute-start.71
  846.4 15.4 %collective-permute-done.90 = bf16[2048,256]{1,0:T(8,128)(2,1)S(1)} collective-permute-done((bf16[2048,256]{1,0:T(8,128)(2,1)S(1)}, bf16[2048,256]{1,0:T(8,128)(2,1)S(1)}, u32[]{:S(2)}, u32[]{:S(2)}) %collective-permute-start.90) | collective-permute-done | bytes 1048608 | tf_op jit(solution)/shard_map/ppermute | solution.py:317
  861.8 11.2 collective-permute-done.88
  890.2 11.6 collective-permute-start.92
  901.9 16.2 %collective-permute-done.77 = bf16[2048,512]{1,0:T(8,128)(2,1)} collective-permute-done((bf16[2048,512]{1,0:T(8,128)(2,1)}, bf16[2048,512]{1,0:T(8,128)(2,1)}, u32[]{:S(2)}, u32[]{:S(2)}) %collective-permute-start.77) | collective-permute-done | bytes 2097184 | tf_op jit(solution)/shard_map/ppermute | solution.py:317
  918.1 17.9 %collective-permute-done.75 = bf16[1024,512]{1,0:T(8,128)(2,1)} collective-permute-done((bf16[1024,512]{1,0:T(8,128)(2,1)}, bf16[1024,512]{1,0:T(8,128)(2,1)}, u32[]{:S(2)}, u32[]{:S(2)}) %collective-permute-start.75) | collective-permute-done | bytes 1048608 | tf_op jit(solution)/shard_map/ppermute | solution.py:317
  972.6 12.2 %collective-permute-done.99 = bf16[512,768]{1,0:T(8,128)(2,1)} collective-permute-done((bf16[512,768]{1,0:T(8,128)(2,1)}, bf16[512,768]{1,0:T(8,128)(2,1)}, u32[]{:S(2)}, u32[]{:S(2)}) %collective-permute-start.99) | collective-permute-done | bytes 786464 | tf_op jit(solution)/shard_map/ppermute | solution.py:317
  1039.5 13.7 %collective-permute-done.76 = bf16[512,512]{1,0:T(8,128)(2,1)S(1)} collective-permute-done((bf16[512,512]{1,0:T(8,128)(2,1)S(1)}, bf16[512,512]{1,0:T(8,128)(2,1)S(1)}, u32[]{:S(2)}, u32[]{:S(2)}) %collective-permute-start.76) | collective-permute-done | bytes 524320 | tf_op jit(solution)/shard_map/ppermute | solution.py:322
  1053.8 11.2 collective-permute-done.80
  1101.6 15.6 %collective-permute-start.67 = (bf16[256,2048]{1,0:T(8,128)(2,1)}, bf16[256,2048]{1,0:T(8,128)(2,1)S(1)}, u32[]{:S(2)}, u32[]{:S(2)}) collective-permute-start(bf16[256,2048]{1,0:T(8,128)(2,1)} %get-tuple-element.186), channel_id=1, source_target_pairs={{1,0},{0,1},{5,2},{4,3},{3,4},{2,5},{7,6},{6,7},{9,8},{8,9},{13,10... | collective-permute-start | bytes 3145736 | tf_op jit(solution)/shard_map/ppermute | solution.py:398
  1119.6 12.0 %collective-permute-done.67 = bf16[256,2048]{1,0:T(8,128)(2,1)S(1)} collective-permute-done((bf16[256,2048]{1,0:T(8,128)(2,1)}, bf16[256,2048]{1,0:T(8,128)(2,1)S(1)}, u32[]{:S(2)}, u32[]{:S(2)}) %collective-permute-start.67) | collective-permute-done | bytes 1048608 | tf_op jit(solution)/shard_map/ppermute | solution.py:398
  (729 shorter events, 699.7 us)
Async XLA Ops:
  7.2 107.7 %all-gather.4.cloned.1.call-start = ((), (), s32[]{:S(2)}) async-start(), calls=%async_computation.3 | async-start | bytes 1310720 | tf_op jit(solution)/shard_map/all_gather | solution.py:767
  43.3 142.7 %collective-permute-start = (s32[2]{0:T(128)}, s32[2]{0:T(128)}, u32[]{:S(2)}, u32[]{:S(2)}) collective-permute-start(s32[2]{0:T(128)} %param.15), channel_id=1, source_target_pairs={{0,4},{4,0},{8,12},{12,8},{16,20},{20,16},{24,28},{28,24},{1,5},{5... | collective-permute-start | bytes 32 | tf_op jit(solution)/shard_map/ppermute | solution.py:317
  61.1 234.8 %all-gather.6.cloned.1.call-start = ((), (), s32[]{:S(2)}) async-start(), calls=%async_computation.4 | async-start | bytes 7864320 | tf_op jit(solution)/shard_map/all_gather | solution.py:793
  70.3 61.9 %collective-permute-start.17 = (bf16[1024,512]{1,0:T(8,128)(2,1)}, bf16[1024,512]{1,0:T(8,128)(2,1)}, u32[]{:S(2)}, u32[]{:S(2)}) collective-permute-start(bf16[1024,512]{1,0:T(8,128)(2,1)} %constant_dynamic-update-slice_fusion.side0), channel_id=1, source_target_pairs={{0,16},{4,20},{8,24},{12,28},{16,0},{20,4},{24,8},{28,12},{1,17},{... | collective-permute-start | bytes 3145736 | tf_op jit(solution)/shard_map/ppermute | solution.py:317
  114.9 282.9 %all-gather.8.cloned.1.call-start = ((), (), s32[]{:S(2)}) async-start(), calls=%async_computation.5 | async-start | bytes 3932160 | tf_op jit(solution)/shard_map/all_gather | solution.py:796
  188.8 56.5 %collective-permute-start.32 = (bf16[2048,256]{1,0:T(8,128)(2,1)}, bf16[2048,256]{1,0:T(8,128)(2,1)S(1)}, u32[]{:S(2)}, u32[]{:S(2)}) collective-permute-start(bf16[2048,256]{1,0:T(8,128)(2,1)} %all-gather.4.cloned.1.call-done), channel_id=1, source_target_pairs={{0,16},{4,20},{8,24},{12,28},{16,0},{20,4},{24,8},{28,12},{1,17},{... | collective-permute-start | bytes 3145736 | tf_op jit(solution)/shard_map/ppermute | solution.py:317
  193.6 61.7 %collective-permute-start.41 = (bf16[256,2048]{1,0:T(8,128)(2,1)}, bf16[256,2048]{1,0:T(8,128)(2,1)S(1)}, u32[]{:S(2)}, u32[]{:S(2)}) collective-permute-start(bf16[256,2048]{1,0:T(8,128)(2,1)} %get-tuple-element.201), channel_id=1, source_target_pairs={{0,0},{1,1},{2,4},{3,5},{4,2},{5,3},{6,6},{7,7},{8,8},{9,9},{10,12... | collective-permute-start | bytes 3145736 | tf_op jit(solution)/shard_map/ppermute | solution.py:381
  195.5 72.1 %collective-permute-start.42 = (bf16[256,2048]{1,0:T(8,128)(2,1)S(1)}, bf16[256,2048]{1,0:T(8,128)(2,1)}, u32[]{:S(2)}, u32[]{:S(2)}) collective-permute-start(bf16[256,2048]{1,0:T(8,128)(2,1)S(1)} %get-tuple-element.202), channel_id=1, source_target_pairs={{0,1},{1,0},{2,5},{3,4},{4,3},{5,2},{6,7},{7,6},{8,9},{9,8},{10,13... | collective-permute-start | bytes 3145736 | tf_op jit(solution)/shard_map/ppermute | solution.py:381
  296.0 651.8 %reduce-scatter.4.cloned.1.call-start = ((), (), s32[]{:S(2)}) async-start(), calls=%async_computation.6 | async-start | bytes 3932160 | tf_op jit(solution)/shard_map/reduce_scatter | solution.py:872
  306.7 149.3 %collective-permute-start.47 = (bf16[2048,1536]{1,0:T(8,128)(2,1)}, bf16[2048,1536]{1,0:T(8,128)(2,1)}, u32[]{:S(2)}, u32[]{:S(2)}) collective-permute-start(bf16[2048,1536]{1,0:T(8,128)(2,1)} %all-gather.6.cloned.1.call-done.gate_w.up_w.refs_2_.refs_5_), channel_id=1, source_target_pairs={{0,4},{4,0},{8,12},{12,8},{16,20},{20,16},{24,28},{28,24},{1,5},{5... | collective-permute-start | bytes 18874376 | tf_op jit(solution)/shard_map/ppermute | solution.py:317
  309.8 64.1 %collective-permute-start.37 = (bf16[512,2048]{1,0:T(8,128)(2,1)}, bf16[512,2048]{1,0:T(8,128)(2,1)S(1)}, u32[]{:S(2)}, u32[]{:S(2)}) collective-permute-start(bf16[512,2048]{1,0:T(8,128)(2,1)} %get-tuple-element.160), channel_id=1, source_target_pairs={{0,8},{4,12},{8,0},{12,4},{16,24},{20,28},{24,16},{28,20},{1,9},{5... | collective-permute-start | bytes 6291464 | tf_op jit(solution)/shard_map/ppermute | solution.py:317
  310.3 88.6 %collective-permute-start.38 = (bf16[512,2048]{1,0:T(8,128)(2,1)}, bf16[512,2048]{1,0:T(8,128)(2,1)}, u32[]{:S(2)}, u32[]{:S(2)}) collective-permute-start(bf16[512,2048]{1,0:T(8,128)(2,1)} %get-tuple-element.160), channel_id=1, source_target_pairs={{0,16},{4,20},{8,24},{12,28},{16,0},{20,4},{24,8},{28,12},{1,17},{... | collective-permute-start | bytes 6291464 | tf_op jit(solution)/shard_map/ppermute | solution.py:317
  330.4 67.5 %collective-permute-start.45 = (bf16[256,2048]{1,0:T(8,128)(2,1)S(1)}, bf16[256,2048]{1,0:T(8,128)(2,1)S(1)}, u32[]{:S(2)}, u32[]{:S(2)}) collective-permute-start(bf16[256,2048]{1,0:T(8,128)(2,1)S(1)} %slice.381), channel_id=1, source_target_pairs={{0,16},{4,20},{8,24},{12,28},{16,0},{20,4},{24,8},{28,12},{1,17},{... | collective-permute-start | bytes 3145736 | tf_op jit(solution)/shard_map/ppermute | solution.py:317
  336.8 64.0 %collective-permute-start.46 = (bf16[256,2048]{1,0:T(8,128)(2,1)}, bf16[256,2048]{1,0:T(8,128)(2,1)}, u32[]{:S(2)}, u32[]{:S(2)}) collective-permute-start(bf16[256,2048]{1,0:T(8,128)(2,1)} %slice.382), channel_id=1, source_target_pairs={{0,8},{4,12},{8,0},{12,4},{16,24},{20,28},{24,16},{28,20},{1,9},{5... | collective-permute-start | bytes 3145736 | tf_op jit(solution)/shard_map/ppermute | solution.py:317
  397.9 58.2 %collective-permute-start.48 = (bf16[2048,768]{1,0:T(8,128)(2,1)}, bf16[2048,768]{1,0:T(8,128)(2,1)S(1)}, u32[]{:S(2)}, u32[]{:S(2)}) collective-permute-start(bf16[2048,768]{1,0:T(8,128)(2,1)} %all-gather.8.cloned.1.call-done.down_w.refs_2_), channel_id=1, source_target_pairs={{0,4},{4,0},{8,12},{12,8},{16,20},{20,16},{24,28},{28,24},{1,5},{5... | collective-permute-start | bytes 9437192 | tf_op jit(solution)/shard_map/ppermute | solution.py:317
  497.9 69.1 %collective-permute-start.49 = (bf16[512,2048]{1,0:T(8,128)(2,1)}, bf16[512,2048]{1,0:T(8,128)(2,1)}, u32[]{:S(2)}, u32[]{:S(2)}) collective-permute-start(bf16[512,2048]{1,0:T(8,128)(2,1)} %from_hidden.8), channel_id=1, source_target_pairs={{0,8},{4,12},{8,0},{12,4},{16,24},{20,28},{24,16},{28,20},{1,9},{5... | collective-permute-start | bytes 6291464 | tf_op jit(solution)/shard_map/ppermute | solution.py:317
  510.3 56.8 %collective-permute-start.51 = (bf16[512,2048]{1,0:T(8,128)(2,1)}, bf16[512,2048]{1,0:T(8,128)(2,1)}, u32[]{:S(2)}, u32[]{:S(2)}) collective-permute-start(bf16[512,2048]{1,0:T(8,128)(2,1)} %from_hidden.9), channel_id=1, source_target_pairs={{0,16},{4,20},{8,24},{12,28},{16,0},{20,4},{24,8},{28,12},{1,17},{... | collective-permute-start | bytes 6291464 | tf_op jit(solution)/shard_map/ppermute | solution.py:317
  544.5 71.8 %collective-permute-start.53 = (bf16[2048,768]{1,0:T(8,128)(2,1)}, bf16[2048,768]{1,0:T(8,128)(2,1)}, u32[]{:S(2)}, u32[]{:S(2)}) collective-permute-start(bf16[2048,768]{1,0:T(8,128)(2,1)} %convolution_convert_fusion.4), channel_id=1, source_target_pairs={{0,4},{4,0},{8,12},{12,8},{16,20},{20,16},{24,28},{28,24},{1,5},{5... | collective-permute-start | bytes 9437192 | tf_op jit(solution)/shard_map/ppermute | solution.py:317
  585.6 378.7 %reduce-scatter.6.cloned.1.call-start = ((), (), s32[]{:S(2)}) async-start(), calls=%async_computation.7 | async-start | bytes 3932160 | tf_op jit(solution)/shard_map/reduce_scatter | solution.py:872
  658.3 57.6 %collective-permute-start.62 = (bf16[512,512]{1,0:T(8,128)(2,1)}, bf16[512,512]{1,0:T(8,128)(2,1)S(1)}, u32[]{:S(2)}, u32[]{:S(2)}) collective-permute-start(bf16[512,512]{1,0:T(8,128)(2,1)} %get-tuple-element.117), channel_id=1, source_target_pairs={{4,0},{12,8},{20,16},{28,24},{5,1},{13,9},{21,17},{29,25},{6,2},{1... | collective-permute-start | bytes 1572872 | tf_op jit(solution)/shard_map/ppermute | solution.py:919
  705.1 72.5 %collective-permute-start.56 = (bf16[512,2048]{1,0:T(8,128)(2,1)}, bf16[512,2048]{1,0:T(8,128)(2,1)}, u32[]{:S(2)}, u32[]{:S(2)}) collective-permute-start(bf16[512,2048]{1,0:T(8,128)(2,1)} %from_hidden.12), channel_id=1, source_target_pairs={{0,8},{4,12},{8,0},{12,4},{16,24},{20,28},{24,16},{28,20},{1,9},{5... | collective-permute-start | bytes 6291464 | tf_op jit(solution)/shard_map/ppermute | solution.py:317
  706.4 259.5 %reduce-scatter.8.cloned.1.call-start = ((), (), s32[]{:S(2)}) async-start(), calls=%async_computation.8 | async-start | bytes 3932160 | tf_op jit(solution)/shard_map/reduce_scatter | solution.py:872
  715.9 61.7 %collective-permute-start.58 = (bf16[512,2048]{1,0:T(8,128)(2,1)}, bf16[512,2048]{1,0:T(8,128)(2,1)}, u32[]{:S(2)}, u32[]{:S(2)}) collective-permute-start(bf16[512,2048]{1,0:T(8,128)(2,1)} %from_hidden.13), channel_id=1, source_target_pairs={{0,16},{4,20},{8,24},{12,28},{16,0},{20,4},{24,8},{28,12},{1,17},{... | collective-permute-start | bytes 6291464 | tf_op jit(solution)/shard_map/ppermute | solution.py:317
  782.0 58.8 %collective-permute-start.57 = (bf16[256,2048]{1,0:T(8,128)(2,1)}, bf16[256,2048]{1,0:T(8,128)(2,1)}, u32[]{:S(2)}, u32[]{:S(2)}) collective-permute-start(bf16[256,2048]{1,0:T(8,128)(2,1)} %get-tuple-element.193), channel_id=1, source_target_pairs={{0,16},{4,20},{8,24},{12,28},{16,0},{20,4},{24,8},{28,12},{1,17},{... | collective-permute-start | bytes 3145736 | tf_op jit(solution)/shard_map/ppermute | solution.py:317
  782.9 58.0 %collective-permute-start.59 = (bf16[256,2048]{1,0:T(8,128)(2,1)}, bf16[256,2048]{1,0:T(8,128)(2,1)}, u32[]{:S(2)}, u32[]{:S(2)}) collective-permute-start(bf16[256,2048]{1,0:T(8,128)(2,1)} %get-tuple-element.194), channel_id=1, source_target_pairs={{0,8},{4,12},{8,0},{12,4},{16,24},{20,28},{24,16},{28,20},{1,9},{5... | collective-permute-start | bytes 3145736 | tf_op jit(solution)/shard_map/ppermute | solution.py:317
  811.0 65.7 %collective-permute-start.74 = (bf16[2048,512]{1,0:T(8,128)(2,1)}, bf16[2048,512]{1,0:T(8,128)(2,1)}, u32[]{:S(2)}, u32[]{:S(2)}) collective-permute-start(bf16[2048,512]{1,0:T(8,128)(2,1)} %pad_maximum_fusion.6), channel_id=1, source_target_pairs={{0,8},{4,12},{8,0},{12,4},{16,24},{20,28},{24,16},{28,20},{1,9},{5... | collective-permute-start | bytes 6291464 | tf_op jit(solution)/shard_map/ppermute | solution.py:317
  840.8 77.3 %collective-permute-start.77 = (bf16[2048,512]{1,0:T(8,128)(2,1)}, bf16[2048,512]{1,0:T(8,128)(2,1)}, u32[]{:S(2)}, u32[]{:S(2)}) collective-permute-start(bf16[2048,512]{1,0:T(8,128)(2,1)} %pad_maximum_fusion.7), channel_id=1, source_target_pairs={{0,16},{4,20},{8,24},{12,28},{16,0},{20,4},{24,8},{28,12},{1,17},{... | collective-permute-start | bytes 6291464 | tf_op jit(solution)/shard_map/ppermute | solution.py:317
  890.2 59.6 %collective-permute-start.92 = (bf16[512,256]{1,0:T(8,128)(2,1)S(1)}, bf16[512,256]{1,0:T(8,128)(2,1)}, u32[]{:S(2)}, u32[]{:S(2)}) collective-permute-start(bf16[512,256]{1,0:T(8,128)(2,1)S(1)} %split.66), channel_id=1, source_target_pairs={{0,1},{1,2},{2,3},{3,0},{4,5},{5,6},{6,7},{7,4},{8,9},{9,10},{10,1... | collective-permute-start | bytes 786440 | tf_op jit(solution)/shard_map/ppermute | solution.py:322
  1070.7 72.7 %collective-permute-start.103 = (bf16[2048,768]{1,0:T(8,128)(2,1)}, bf16[2048,768]{1,0:T(8,128)(2,1)}, u32[]{:S(2)}, u32[]{:S(2)}) collective-permute-start(bf16[2048,768]{1,0:T(8,128)(2,1)} %constant_dynamic-update-slice_fusion.43.own), channel_id=1, source_target_pairs={{0,4},{4,0},{8,12},{12,8},{16,20},{20,16},{24,28},{28,24},{1,5},{5... | collective-permute-start | bytes 9437192 | tf_op jit(solution)/shard_map/ppermute | solution.py:317
  1070.7 83.7 %collective-permute-start.108 = (bf16[2048,768]{1,0:T(8,128)(2,1)}, bf16[2048,768]{1,0:T(8,128)(2,1)}, u32[]{:S(2)}, u32[]{:S(2)}) collective-permute-start(bf16[2048,768]{1,0:T(8,128)(2,1)} %constant_dynamic-update-slice_fusion.48.own), channel_id=1, source_target_pairs={{0,4},{4,0},{8,12},{12,8},{16,20},{20,16},{24,28},{28,24},{1,5},{5... | collective-permute-start | bytes 9437192 | tf_op jit(solution)/shard_map/ppermute | solution.py:317
  1078.9 86.6 %collective-permute-start.113 = (bf16[2048,768]{1,0:T(8,128)(2,1)}, bf16[2048,768]{1,0:T(8,128)(2,1)}, u32[]{:S(2)}, u32[]{:S(2)}) collective-permute-start(bf16[2048,768]{1,0:T(8,128)(2,1)} %constant_dynamic-update-slice_fusion.53.own), channel_id=1, source_target_pairs={{0,4},{4,0},{8,12},{12,8},{16,20},{20,16},{24,28},{28,24},{1,5},{5... | collective-permute-start | bytes 9437192 | tf_op jit(solution)/shard_map/ppermute | solution.py:317
  1117.3 59.2 %collective-permute-start.85 = (bf16[2048,512]{1,0:T(8,128)(2,1)S(1)}, bf16[2048,512]{1,0:T(8,128)(2,1)S(1)}, u32[]{:S(2)}, u32[]{:S(2)}) collective-permute-start(bf16[2048,512]{1,0:T(8,128)(2,1)S(1)} %constant_dynamic-update-slice_fusion.33.own), channel_id=1, source_target_pairs={{0,4},{4,0},{8,12},{12,8},{16,20},{20,16},{24,28},{28,24},{1,5},{5... | collective-permute-start | bytes 6291464 | tf_op jit(solution)/shard_map/ppermute | solution.py:317
  (229 other events, 4937.9 us)
Sparse Core Ops, SparseCore 0:
  61.3 39.9 all-gather.3
  115.1 145.9 all-gather.5
  296.1 71.1 all-gather.7
  585.8 68.9 reduce-scatter.3
  706.5 71.1 reduce-scatter.5
  779.8 65.6 reduce-scatter.7

commit v4 on v3

--- a/solution.py
+++ b/solution.py
@@ -336,23 +336,35 @@
     return chunks[0] + around(chunks[1].astype(kind), -1) + around(last.astype(kind), 1)
 
 
-def plane_gather(piece):
-    half = piece.shape[0] // 2
-    from_x = across(piece, ACROSS_X)
-    from_y = across(piece, ACROSS_Y)
-    far = [across(from_x[:half], ACROSS_Y), across(from_y[half:], ACROSS_X)]
-    return [piece, from_x, from_y, jnp.concatenate(far, 0)]
-
-
-def plane_sum(own_head, own_tail, to_x, to_y, two_head, one_tail):
-    low = jnp.bfloat16
-    from_x, from_y = across(to_x, ACROSS_X), across(to_y, ACROSS_Y)
-    half = own_head.shape[0]
-    two_head = two_head + from_x[half:]
-    one_tail = one_tail + from_y[half:]
-    own_head = own_head + from_x[:half] + across(two_head.astype(low), ACROSS_Y)
-    own_tail = own_tail + from_y[:half] + across(one_tail.astype(low), ACROSS_X)
-    return own_head, own_tail
+class Links:
+    def __init__(self):
+        self.sent = {ACROSS_X: [], ACROSS_Y: []}
+
+    def send(self, x, mask):
+        sent = self.sent[mask]
+        if len(sent) > 1:
+            x = after(x, sent[-2])
+        sent.append(across(x, mask))
+        return sent[-1]
+
+    def gather(self, *pieces):
+        near = [(self.send(p, ACROSS_X), self.send(p, ACROSS_Y)) for p in pieces]
+        out = []
+        for piece, (from_x, from_y) in zip(pieces, near):
+            half = piece.shape[0] // 2
+            far = self.send(from_x[:half], ACROSS_Y), self.send(from_y[half:], ACROSS_X)
+            out.append([piece, from_x, from_y, *far])
+        return out
+
+    def total(self, to_x, to_y, split, own_head, own_tail, two_head, one_tail):
+        low, full = jnp.bfloat16, jnp.float32
+        x_own, x_two = split(self.send(to_x, ACROSS_X))
+        y_own, y_one = split(self.send(to_y, ACROSS_Y))
+        two_head = (two_head.astype(full) + x_two).astype(low)
+        one_tail = (one_tail.astype(full) + y_one).astype(low)
+        own_head = own_head.astype(full) + x_own + self.send(two_head, ACROSS_Y)
+        own_tail = own_tail.astype(full) + y_own + self.send(one_tail, ACROSS_X)
+        return jnp.concatenate([own_head, own_tail], 0)
 
 
 def sequence_pairs(turn):
@@ -413,8 +425,8 @@
     )
 
 
-def spread_blocks(block):
-    own = jnp.concatenate(plane_gather(block), 0)
+def spread_blocks(links, block):
+    own = jnp.concatenate(links.gather(block)[0], 0)
     return own, across(own, CORE)
 
 
@@ -556,14 +568,18 @@
 
 
 def attend_back_body(
-    info, query, before, own, log_total, grad_mixed, raw, cosine, sine, gain,
-    grad_query, grad_own, grad_before, gain_part, grad_keys, grad_values,
+    info, query, before, own, log_total, grad_resid, weight0, weight1, raw, cosine, sine, gain,
+    grad_query, grad_own, grad_before, gain_part, grad_keys, grad_values, grad_mixed,
 ):
     dim = own.shape[1] // 4
     rows = query.shape[0] // 2
     scale = dim**-0.5
     gain_total = jnp.zeros((1, dim), jnp.float32)
-    for block in range(2):
+    for block, weight in enumerate((weight0, weight1)):
+        on = slice(2 * block * dim, 2 * (block + 1) * dim)
+        grad_mixed[:, on] = jnp.dot(
+            grad_resid[...], weight[...], preferred_element_type=jnp.float32
+        ).astype(jnp.bfloat16)
         grad_keys[...] = jnp.zeros_like(grad_keys)
         grad_values[...] = jnp.zeros_like(grad_values)
         for part in range(2):
@@ -613,14 +629,12 @@
     gain_part[...] = total
 
 
-def vmem_call(body, outs, flops, scratch=(), scalars=0, specs=None, name=None):
+def vmem_call(body, outs, flops, scratch=(), scalars=0, name=None):
     def call(*args):
         in_specs = [
             pl.BlockSpec(memory_space=pltpu.SMEM if i < scalars else pltpu.VMEM)
             for i in range(len(args))
         ]
-        for at, spec in (specs or {}).items():
-            in_specs[at] = spec
         return pl.pallas_call(
             body,
             grid=(1,),
@@ -640,85 +654,245 @@
     return call
 
 
-def column_spec(rows, columns, at):
-    return pl.BlockSpec((rows, columns), lambda i: (0, at))
-
-
-def hidden_body(mid, grad_y, gate_w, up_w, down_w, act, grad_gate, grad_up):
-    gate = jnp.dot(mid[...], gate_w[...], preferred_element_type=jnp.float32)
-    up = jnp.dot(mid[...], up_w[...], preferred_element_type=jnp.float32)
-    grad_act = jnp.dot(grad_y[...], down_w[...], preferred_element_type=jnp.float32)
-    sigma = jax.nn.sigmoid(gate)
-    swish = gate * sigma
-    act[...] = (swish * up).astype(jnp.bfloat16)
-    grad_gate[...] = (grad_act * up * sigma * (1.0 + gate * (1.0 - sigma))).astype(jnp.bfloat16)
-    grad_up[...] = (grad_act * swish).astype(jnp.bfloat16)
-
-
-def hidden_units(mid, grad_y, gate_up_w, down_w):
-    rows, width = mid.shape
-    units = down_w.shape[1]
-    high, cut = rows // 2, units // 3
-    row_spec = pl.BlockSpec((high, width), lambda i, j: (i, 0))
-    out_spec = pl.BlockSpec((high, cut), lambda i, j: (i, j))
+def hidden_units(mids, grads_y, weights):
+    width, units = weights.shape[0], weights.shape[1] // 3
+    count = len(mids)
+    heights = [m.shape[0] for m in mids]
+    rows, cut = sum(heights), units // 3
+
+    def body(*refs):
+        gate_w, up_w, w_down, act, grad_gate, grad_up = refs[2 * count :]
+        start = 0
+        for mid, grad_y in zip(refs[:count], refs[count : 2 * count]):
+            at = slice(start, start + mid.shape[0])
+            start += mid.shape[0]
+            gate = jnp.dot(mid[...], gate_w[...], preferred_element_type=jnp.float32)
+            up = jnp.dot(mid[...], up_w[...], preferred_element_type=jnp.float32)
+            grad_act = jnp.dot(grad_y[...], w_down[...], preferred_element_type=jnp.float32)
+            sigma = jax.nn.sigmoid(gate)
+            swish = gate * sigma
+            act[at, :] = (swish * up).astype(jnp.bfloat16)
+            slope = grad_act * up * sigma * (1.0 + gate * (1.0 - sigma))
+            grad_gate[at, :] = slope.astype(jnp.bfloat16)
+            grad_up[at, :] = (grad_act * swish).astype(jnp.bfloat16)
+
+    row_specs = [
+        pl.BlockSpec((h, width), lambda j: (0, 0), pipeline_mode=pl.Buffered(1)) for h in heights
+    ]
     return pl.pallas_call(
-        hidden_body,
-        grid=(2, 3),
+        body,
+        grid=(3,),
         out_shape=[jax.ShapeDtypeStruct((rows, units), jnp.bfloat16)] * 3,
         in_specs=[
-            row_spec,
-            row_spec,
-            pl.BlockSpec((width, cut), lambda i, j: (0, j)),
-            pl.BlockSpec((width, cut), lambda i, j: (0, j + 3)),
-            pl.BlockSpec((width, cut), lambda i, j: (0, j)),
+            *row_specs,
+            *row_specs,
+            pl.BlockSpec((width, cut), lambda j: (0, j)),
+            pl.BlockSpec((width, cut), lambda j: (0, j + 3)),
+            pl.BlockSpec((width, cut), lambda j: (0, j + 6)),
         ],
-        out_specs=[out_spec] * 3,
+        out_specs=[pl.BlockSpec((rows, cut), lambda j: (0, j))] * 3,
         compiler_params=pltpu.CompilerParams(vmem_limit_bytes=VMEM_BYTES),
         cost_estimate=pl.CostEstimate(
             flops=6 * rows * width * units, bytes_accessed=10 * rows * width, transcendentals=0
         ),
         name="hidden_units",
-    )(mid, grad_y, gate_up_w, gate_up_w, down_w)
-
-
-def from_hidden(pairs, first, step):
-    count = len(pairs)
+    )(*mids, *grads_y, weights, weights, weights)
+
+
+def from_hidden(pairs, eighths):
+    count, parts = len(pairs), len(eighths)
     rows, units = pairs[0][0].shape[0] // 8, pairs[0][0].shape[1]
     width = pairs[0][1].shape[0]
     cut = width // 4
 
     def body(*refs):
-        refs, out = refs[:-1], refs[-1]
-        out[...] = sum(
-            nt(
-                jnp.concatenate([refs[3 * i][...], refs[3 * i + 1][...]], 0),
-                refs[3 * i + 2][...],
-            )
-            for i in range(count)
-        ).astype(jnp.bfloat16)
+        ins, outs = refs[: -(parts // 2)], refs[-(parts // 2) :]
+        total = 0.0
+        for i in range(count):
+            part = ins[i * (parts + 1) : (i + 1) * (parts + 1)]
+            left = jnp.concatenate([p[...] for p in part[:-1]], 0)
+            total = total + nt(left, part[-1][...])
+        for i, out in enumerate(outs):
+            out[...] = total[2 * i * rows : 2 * (i + 1) * rows].astype(jnp.bfloat16)
 
     specs, args = [], []
     for left, right, at in pairs:
-        specs += [
-            pl.BlockSpec((rows, units), lambda j: (first, 0)),
-            pl.BlockSpec((rows, units), lambda j: (first + step, 0)),
-            pl.BlockSpec((cut, units), lambda j, at=at: (j, at)),
-        ]
-        args += [left, left, right]
+        specs += [pl.BlockSpec((rows, units), lambda j, e=e: (e, 0)) for e in eighths]
+        specs.append(pl.BlockSpec((cut, units), lambda j, at=at: (j, at)))
+        args += [left] * parts + [right]
     return pl.pallas_call(
         body,
         grid=(4,),
-        out_shape=jax.ShapeDtypeStruct((2 * rows, width), jnp.bfloat16),
+        out_shape=[jax.ShapeDtypeStruct((2 * rows, width), jnp.bfloat16)] * (parts // 2),
         in_specs=specs,
-        out_specs=pl.BlockSpec((2 * rows, cut), lambda j: (0, j)),
+        out_specs=[pl.BlockSpec((2 * rows, cut), lambda j: (0, j))] * (parts // 2),
         compiler_params=pltpu.CompilerParams(vmem_limit_bytes=VMEM_BYTES),
         cost_estimate=pl.CostEstimate(
-            flops=4 * count * rows * width * units,
+            flops=2 * parts * count * rows * width * units,
             bytes_accessed=2 * count * width * units,
             transcendentals=0,
         ),
         name="from_hidden",
     )(*args)
+
+
+def row_outer(lefts, groups, first, tiles, added=None, places=None):
+    rights = [right for group in groups for right in group]
+    places = range(len(rights)) if places is None else places
+    added = [] if added is None else [added] * len(rights)
+    width = lefts[0].shape[1]
+    tile = width // 8
+    count = len(lefts)
+    rows = sum(left.shape[0] for left in lefts)
+    columns = [sum(right.shape[1] for right in group) for group in groups]
+
+    def body(*refs):
+        left_refs = refs[:count]
+        right_refs = refs[count : count + len(rights)]
+        add_refs = refs[count + len(rights) : count + len(rights) + len(added)]
+        outs = refs[count + len(rights) + len(added) :]
+        place = 0
+        for i, group in enumerate(groups):
+            column = 0
+            for right in group:
+                on = slice(column, column + right.shape[1])
+                total, start = 0.0, 0
+                for left in left_refs:
+                    stop = start + left.shape[0]
+                    total = total + tn(left[...], right_refs[place][start:stop, :])
+                    start = stop
+                if added:
+                    total = total + add_refs[place][...].astype(jnp.float32)
+                outs[i][:, on] = total.astype(jnp.bfloat16)
+                place += 1
+                column += right.shape[1]
+
+    return pl.pallas_call(
+        body,
+        grid=(tiles,),
+        out_shape=[jax.ShapeDtypeStruct((tiles * tile, c), jnp.bfloat16) for c in columns],
+        in_specs=[
+            *(pl.BlockSpec((left.shape[0], tile), lambda j: (0, j + first)) for left in lefts),
+            *(
+                pl.BlockSpec(right.shape, lambda j: (0, 0), pipeline_mode=pl.Buffered(1))
+                for right in rights
+            ),
+            *(
+                pl.BlockSpec((tile, rights[0].shape[1]), lambda j, at=at: (j + first, at))
+                for at in places[: len(added)]
+            ),
+        ],
+        out_specs=[pl.BlockSpec((tile, c), lambda j: (j, 0)) for c in columns],
+        compiler_params=pltpu.CompilerParams(vmem_limit_bytes=VMEM_BYTES),
+        cost_estimate=pl.CostEstimate(
+            flops=2 * rows * tiles * tile * sum(columns),
+            bytes_accessed=2 * rows * (width + sum(columns)),
+            transcendentals=0,
+        ),
+        name="row_outer",
+    )(*lefts, *rights, *added)
+
+
+def close_body(x, *refs):
+    mixed, weights = refs[:4], refs[4:12]
+    gains, resid, mid = refs[12:]
+    at = pl.program_id(0)
+    step = x.shape[1]
+    columns = weights[0].shape[1]
+    total = x[...].astype(jnp.float32)
+    for i in range(8):
+        part = mixed[i // 2][:, (i % 2) * columns : (i % 2 + 1) * columns]
+        total = total + nt(part, weights[i][...])
+    resid[:, pl.ds(pl.multiple_of(at * step, step), step)] = total
+
+    @pl.when(at == 3)
+    def _():
+        unit, _ = unit_of(resid[...])
+        mid[...] = (unit * gains[...]).astype(jnp.bfloat16)
+
+
+def close_attention(x, mixed, weights, gains):
+    rows, width = x.shape
+    step = width // 4
+    whole = lambda a: pl.BlockSpec(a.shape, lambda j: (0, 0))
+    return pl.pallas_call(
+        close_body,
+        grid=(4,),
+        out_shape=[
+            jax.ShapeDtypeStruct((rows, width), jnp.float32),
+            jax.ShapeDtypeStruct((rows, width), jnp.bfloat16),
+        ],
+        in_specs=[
+            pl.BlockSpec((rows, step), lambda j: (0, j)),
+            *(whole(m) for m in mixed),
+            *(pl.BlockSpec((step, w.shape[1]), lambda j: (j, 0)) for w in weights),
+            whole(gains),
+        ],
+        out_specs=[pl.BlockSpec((rows, width), lambda j: (0, 0))] * 2,
+        compiler_params=pltpu.CompilerParams(vmem_limit_bytes=VMEM_BYTES),
+        cost_estimate=pl.CostEstimate(
+            flops=2 * rows * width * width, bytes_accessed=2 * width * width, transcendentals=0
+        ),
+        name="close_attention",
+    )(x, *mixed, *weights, gains)
+
+
+def back_to_rows(blocks, weights):
+    rows = blocks[0].shape[0]
+    step, columns = weights[0][0].shape
+    count = len(blocks)
+
+    def body(*refs):
+        lefts = refs[:count]
+        hbm = refs[count : 4 * count]
+        out = refs[4 * count]
+        held, sems = refs[4 * count + 1 :]
+        copies = []
+        for i in range(count):
+            own, side, far = hbm[3 * i : 3 * i + 3]
+            copies.append(
+                [
+                    pltpu.make_async_copy(own, held.at[i, :step], sems.at[i, 0]),
+                    pltpu.make_async_copy(
+                        side.at[:step], held.at[i, step : 2 * step], sems.at[i, 1]
+                    ),
+                    pltpu.make_async_copy(far, held.at[i, 2 * step : 3 * step], sems.at[i, 2]),
+                    pltpu.make_async_copy(side.at[step:], held.at[i, 3 * step :], sems.at[i, 3]),
+                ]
+            )
+        for some in copies:
+            for copy in some:
+                copy.start()
+        for i in range(count):
+            for copy in copies[i]:
+                copy.wait()
+            for k in range(4):
+                on = slice(k * step, (k + 1) * step)
+                part = nt(lefts[i][...], held[i, on])
+                if i == 0:
+                    out[:, on] = part
+                else:
+                    out[:, on] += part
+
+    return pl.pallas_call(
+        body,
+        grid=(1,),
+        out_shape=jax.ShapeDtypeStruct((rows, 4 * step), jnp.float32),
+        in_specs=[pl.BlockSpec(memory_space=pltpu.VMEM)] * count
+        + [pl.BlockSpec(memory_space=pl.ANY)] * (3 * count),
+        out_specs=pl.BlockSpec(memory_space=pltpu.VMEM),
+        scratch_shapes=[
+            pltpu.VMEM((count, 4 * step, columns), jnp.bfloat16),
+            pltpu.SemaphoreType.DMA((count, 4)),
+        ],
+        compiler_params=pltpu.CompilerParams(vmem_limit_bytes=VMEM_BYTES),
+        cost_estimate=pl.CostEstimate(
+            flops=8 * rows * step * columns * count,
+            bytes_accessed=8 * step * columns * count,
+            transcendentals=0,
+        ),
+        name="back_to_rows",
+    )(*blocks, *(part for w in weights for part in w))
 
 
 def on_device_block(
@@ -746,6 +920,7 @@
     core = me & 1
     count = lax.axis_size("rep")
 
+    links = Links()
     own_blocks = [
         column_block((w_query, key_matrix, value_matrix), me ^ i) for i in range(8)
     ]
@@ -753,20 +928,26 @@
     x_low = to_sequences(after(tokens, before, behind))
     rows = x_low.shape[0]
     far = around(before, 1)
-    side_blocks = plane_gather(jnp.concatenate([before, behind], 0))
-    far_blocks = plane_gather(far)
+    out_own = lax.all_gather(
+        after(column_block((w_out,), me), before, behind), "shard", axis=0, tiled=True
+    )
+    ffn_own = lax.all_gather(
+        after(column_block((w_gate, w_up, w_down), me), x_low), "shard", axis=0, tiled=True
+    )
+    side_blocks, far_blocks = (
+        [*blocks[:3], jnp.concatenate(blocks[3:], 0)]
+        for blocks in links.gather(jnp.concatenate([before, behind], 0), far)
+    )
     other_side = [across(block, CORE) for block in side_blocks]
     other_far = [across(block, CORE) for block in far_blocks]
-    qkv_refs = [
-        (
-            own_blocks[2 * i], side_blocks[i], far_blocks[i],
-            own_blocks[2 * i + 1], other_side[i], other_far[i],
+    qkv_weights = [
+        part
+        for i in range(4)
+        for part in (
+            (own_blocks[2 * i], side_blocks[i], far_blocks[i]),
+            (own_blocks[2 * i + 1], other_side[i], other_far[i]),
         )
-        for i in range(4)
     ]
-    out_own = lax.all_gather(
-        after(column_block((w_out,), me), far), "shard", axis=0, tiled=True
-    )
     gain_parts = jnp.stack([attn_gain, mlp_gain])
     gains = jnp.concatenate(
         [gain_parts, *(around(gain_parts, by) for by in (1, 2, 3))], 1
@@ -790,18 +971,14 @@
     cosine, sine = cosine[0, :, 0], sine[0, :, 0]
     sine = jnp.concatenate([-sine[:, : head_dim // 2], sine[:, head_dim // 2 :]], 1)
 
-    gate_up_own = lax.all_gather(
-        after(column_block((w_gate, w_up), me), out_own), "shard", axis=0, tiled=True
-    )
-    down_own = lax.all_gather(
-        after(column_block((w_down,), me), gate_up_own), "shard", axis=0, tiled=True
-    )
-    out_chips = plane_gather(after(out_own, *far_blocks))
+    out_chips = links.gather(out_own)[0]
+    out_chips = [*out_chips[:3], jnp.concatenate(out_chips[3:], 0)]
     out_blocks = [block for chip in out_chips for block in (chip, across(chip, CORE))]
-    grad_y_low = to_sequences(after(cotangent, out_own))
-    gate_up = [gate_up_own, across(gate_up_own, CORE)]
-    down = [down_own, across(down_own, CORE)]
-    units = down_own.shape[1]
+    grad_y_low = to_sequences(after(cotangent, x_low, out_own))
+    grad_y_low = jnp.where(valid, grad_y_low, jnp.zeros_like(grad_y_low))
+    grads_y = links.gather(grad_y_low)[0]
+    ffn = [ffn_own, across(ffn_own, CORE)]
+    units = ffn_own.shape[1] // 3
 
     x_rows = x_low.astype(full)
     inverse_in = lax.rsqrt(jnp.mean(x_rows * x_rows, -1, keepdims=True) + EPS)
@@ -826,80 +1003,65 @@
     head_gains = jnp.concatenate([query_gains, key_gains], 0)
     upward = [(i, i + 1) for i in range(0, count, 2)]
     downward = [(i + 1, i) for i in range(0, count, 2)]
-    projected = [project(normed, *qkv_refs[i], cosine, sine, head_gains) for i in range(4)]
+    projected = [
+        project(normed, *qkv_weights[2 * i], *qkv_weights[2 * i + 1], cosine, sine, head_gains)
+        for i in range(4)
+    ]
     earlier = [lax.ppermute(p[2], "rep", upward) for p in projected]
     attended = [
         attend(info, projected[i][1], earlier[i], projected[i][2]) for i in range(4)
     ]
-    mixed = jnp.concatenate([a[0] for a in attended], 1)
-    out_all = jnp.concatenate(out_blocks, 1)
-    branch = jnp.einsum("rf,nf->rn", mixed, out_all, preferred_element_type=full)
-
-    resid = x_rows + branch
+    mixed = [a[0] for a in attended]
+    resid, mid = close_attention(x_low, mixed, out_blocks, mlp_gains)
     inverse_mid = lax.rsqrt(jnp.mean(resid * resid, -1, keepdims=True) + EPS)
     mid_unit = resid * inverse_mid
-    mid = (mid_unit * mlp_gains).astype(low)
-    mid_all = jnp.concatenate(plane_gather(mid), 0)
-    grad_y_low = jnp.where(valid, grad_y_low, jnp.zeros_like(grad_y_low))
-    grad_y_all = jnp.concatenate(plane_gather(grad_y_low), 0)
-    hidden = [hidden_units(mid_all, grad_y_all, gate_up[i], down[i]) for i in range(2)]
-
-    def plane_total(pairs, first=()):
-        def some(at, step, *done):
-            left = after(pairs[0][0], *done) if done else pairs[0][0]
-            return from_hidden([(left, *pairs[0][1:]), *pairs[1:]], at, step)
-
-        to_x = some(2, 4, *first)
-        to_y = some(5, 2, to_x)
-        rest = some(3, 1, to_y)
-        own = some(0, 1, rest)
-        half = own.shape[0] // 2
-        parts = plane_sum(
-            own[:half].astype(full), own[half:].astype(full), to_x, to_y,
-            rest[half:].astype(full), rest[:half].astype(full),
+
+    mids = links.gather(mid)[0]
+    hidden = [hidden_units(mids, grads_y, ffn[i]) for i in range(2)]
+
+    def plane_total(pairs):
+        to_x, to_y = from_hidden(pairs, (2, 6, 5, 7))
+        rest, own = from_hidden([(after(pairs[0][0], to_x), *pairs[0][1:]), *pairs[1:]], (3, 4, 0, 1))
+        half = rows // 2
+        total = links.total(
+            to_x, to_y, lambda a: (a[:half], a[half:]),
+            own[:half], own[half:], rest[half:], rest[:half],
         )
-        return jnp.concatenate(parts, 0)
-
-    grad_mid = plane_total(
-        [(hidden[i][1 + j], gate_up[i], j) for i in range(2) for j in range(2)]
-    )
-    others, owns = [], []
-    for i, left in ((0, grad_y_all), (1, mid_all), (2, mid_all)):
-        others.append(outer(left, hidden[1][i]).astype(low))
-    for i, left in ((0, grad_y_all), (1, mid_all), (2, mid_all)):
-        owns.append((outer(left, hidden[0][i]) + across(others[i], CORE)).astype(low))
-    totals = [
-        lax.psum_scatter(own, "shard", scatter_dimension=0, tiled=True) for own in owns
-    ]
-    grad_mid = after(grad_mid, *owns)
-    mlp_out = plane_total([(hidden[i][0], down[i], 0) for i in range(2)], (grad_mid,))
+        return total, own
+
+    grad_mid, last = plane_total(
+        [(hidden[i][1 + j], ffn[i], j) for i in range(2) for j in range(2)]
+    )
+    acts = [after(hidden[0][0], last), hidden[1][0]]
+    mlp_out, last = plane_total([(acts[i], ffn[i], 2) for i in range(2)])
     output = from_sequences(jnp.where(valid, resid + mlp_out, 0.0).astype(low))
-    my_group = me.astype(jnp.int32)[None]
-    grad_down_total, grad_gate_total, grad_up_total = (
-        whole_columns(my_group, *spread_blocks(total), 0, units) for total in totals
-    )
+
+    def owned_part(lefts, rights, *done):
+        (other,) = row_outer(lefts, [[after(rights[1][0], *done), *rights[1][1:]]], 0, 8)
+        (own,) = row_outer(lefts, [rights[0]], 0, 8, across(other, CORE))
+        return own, other, lax.psum_scatter(own, "shard", scatter_dimension=0, tiled=True)
+
+    down_own, last, down_total = owned_part(grads_y, [[h[0]] for h in hidden], last)
+    gate_up_own, _, gate_up_total = owned_part(mids, [h[1:] for h in hidden], last)
+    grad_mid = after(grad_mid, down_own, gate_up_own)
 
     mlp_gain_part = jnp.sum(mid_unit * grad_mid, 0)
     grad_resid = grad_y_low.astype(full) + norm_back(mid_unit, inverse_mid, grad_mid * mlp_gains)
     resid_low = grad_resid.astype(low)
-    grad_mixed = jnp.dot(resid_low, out_all, preferred_element_type=full).astype(low)
-    attend_back = [
-        vmem_call(
-            attend_back_body,
-            [
-                quad_rows,
-                jax.ShapeDtypeStruct((rows, block_columns), full),
-                quad_rows,
-                jax.ShapeDtypeStruct((1, head_dim), full),
-            ],
-            30 * rows * rows * block_columns,
-            scratch=[pltpu.VMEM((2 * rows, head_dim), full)] * 2,
-            scalars=1,
-            specs={5: column_spec(rows, block_columns, i)},
-            name="attend_back",
-        )
-        for i in range(4)
-    ]
+    attend_back = vmem_call(
+        attend_back_body,
+        [
+            quad_rows,
+            jax.ShapeDtypeStruct((rows, block_columns), full),
+            quad_rows,
+            jax.ShapeDtypeStruct((1, head_dim), full),
+        ],
+        32 * rows * rows * block_columns,
+        scratch=[pltpu.VMEM((2 * rows, head_dim), full)] * 2
+        + [pltpu.VMEM((rows, block_columns), low)],
+        scalars=1,
+        name="attend_back",
+    )
     finish = vmem_call(
         finish_body,
         [quad_rows, quad_rows, jax.ShapeDtypeStruct((1, head_dim), full)],
@@ -907,13 +1069,12 @@
         name="finish",
     )
     order = (3, 1, 2, 0)
-    order_of_chips = (1, 3, 2, 0)
     backs, finished = {}, {}
     for i in order:
         raw, query, own_pair = projected[i]
-        backs[i] = attend_back[i](
-            info, query, earlier[i], own_pair, attended[i][1], grad_mixed, raw, cosine, sine,
-            query_gains,
+        backs[i] = attend_back(
+            info, query, earlier[i], own_pair, attended[i][1], resid_low, *out_blocks[2 * i : 2 * i + 2],
+            raw, cosine, sine, query_gains,
         )
     for i in order:
         came = lax.ppermute(backs[i][2], "rep", downward)
@@ -925,49 +1086,43 @@
 
     def block_total(left, even, odd):
         columns = even[0].shape[1]
-        half = width // 2
-        even, odd = jnp.concatenate(even, 1), jnp.concatenate(odd, 1)
-        other = outer(left, odd).astype(low)
-        total = outer(left, even) + across(other, CORE)
-        to_x = total[:half, : 2 * columns].astype(low)
-        to_y = total[half:, columns : 3 * columns].astype(low)
-        head, tail = plane_sum(
-            total[:half, 3 * columns :], total[half:, 3 * columns :],
-            jnp.concatenate([to_x[:, :columns], to_x[:, columns:]], 0),
-            jnp.concatenate([to_y[:, columns:], to_y[:, :columns]], 0),
-            total[:half, 2 * columns : 3 * columns], total[half:, :columns],
+        (other,) = row_outer([left], [odd], 0, 8)
+        came = across(other, CORE)
+        to_x, two_head, own_head = row_outer(
+            [left], [[even[1], even[3]], [even[2]], [even[0]]], 0, 4, came, (1, 3, 2, 0)
         )
-        own = jnp.concatenate([head, tail], 0)
+        to_y, one_tail, own_tail = row_outer(
+            [left], [[even[2], even[3]], [even[1]], [even[0]]], 4, 4, came, (2, 3, 1, 0)
+        )
+        own = links.total(
+            to_x, to_y, lambda a: (a[:, :columns], a[:, columns:]),
+            own_head, own_tail, two_head, one_tail,
+        )
         return ring_sum(jnp.split(own, shards, 0), low).astype(low)
 
     out_total = block_total(
         rolled(resid_low),
-        [attended[i][0][:, :head_columns] for i in order_of_chips],
-        [attended[i][0][:, head_columns:] for i in order_of_chips],
-    )
+        [m[:, :head_columns] for m in mixed],
+        [m[:, head_columns:] for m in mixed],
+    )
+    my_group = me.astype(jnp.int32)[None]
+    grad_down_total = whole_columns(my_group, *spread_blocks(links, down_total), 0, units)
     qkv_total = block_total(
-        normed,
-        [finished[i][0] for i in order_of_chips],
-        [finished[i][1] for i in order_of_chips],
-    )
-    grad_out_total = whole_columns(my_group, *spread_blocks(out_total), 0, head_columns)
-    qkv_spread = spread_blocks(qkv_total)
+        normed, [finished[i][0] for i in range(4)], [finished[i][1] for i in range(4)]
+    )
+    gate_up_spread = spread_blocks(links, gate_up_total)
+    grad_gate_total = whole_columns(my_group, *gate_up_spread, 0, units)
+    grad_up_total = whole_columns(my_group, *gate_up_spread, units, units)
+    out_spread = spread_blocks(links, out_total)
+    grad_out_total = whole_columns(my_group, *out_spread, 0, head_columns)
+    qkv_spread = spread_blocks(links, qkv_total)
     grad_query_total = whole_columns(my_group, *qkv_spread, 0, head_columns)
     grad_key_total = whole_columns(my_group, *qkv_spread, head_columns, head_dim)
     grad_value_total = whole_columns(my_group, *qkv_spread, 3 * head_dim, head_dim)
 
-    grad_qkv = jnp.concatenate([part for i in range(4) for part in finished[i][:2]], 1)
     step = width // shards
-    qkv_all = jnp.concatenate(
-        [
-            jnp.concatenate([own, side[:step], ahead, side[step:]], 0)
-            for refs in qkv_refs
-            for own, side, ahead in (refs[:3], refs[3:])
-        ],
-        1,
-    )
     grad_in = rolled(
-        jnp.einsum("rf,nf->rn", grad_qkv, qkv_all, preferred_element_type=full)
+        back_to_rows([part for i in range(4) for part in finished[i][:2]], qkv_weights)
     )
     grad_tokens = from_sequences(
         (grad_resid + norm_back(x_unit, inverse_in, grad_in * attn_gains)).astype(low)

time: 1210 us -> 1390 us (1.15)
  waiting for transfers between devices: 304 us -> 586 us
  matrix products: 132 us -> 0 us
  Pallas kernels: 319 us -> 443 us
  local copies, waits for them, and re-layouts: 116 us -> 72.6 us
  other arithmetic: 120 us -> 78.6 us
  starting transfers between devices: 194 us -> 178 us
    ppermute x84 -> x77, waiting for transfers between devices: 220 us -> 359 us  [across(): return lax.ppermute(x, 'rep', [(i, i ^ mask) for i in range(count)])]
    dot_general x13 -> x0, matrix products: 132 us -> none  [the longest x10 102 us: outer(): jnp.einsum('rc,rf->cf', left, right, preferred_element_type=jnp.float32)]
    pallas_call x10 -> x18, Pallas kernels: 134 us -> 255 us  [the longest x10 107 us: row_outer(): pl.pallas_call(body, grid=(tiles,), out_shape=[jax.ShapeDtypeStruct((tile...]
    all_gather x3 -> x2, waiting for transfers between devices: 0.01 us -> 90.4 us  [the longest x1 90.4 us: on_device_block(): lax.all_gather(after(column_block((w_gate, w_up, w_down), me), x_low), 's...]
    ppermute x12, waiting for transfers between devices: 36.4 us -> 91.9 us  [around(): lax.ppermute(x, 'shard', [(i, (i + by) % count) for i in range(count)])]
    unnamed x326 -> x254, local copies, waits for them, and re-layouts: 57.7 us -> 28.9 us
    unnamed x11 -> x2, other arithmetic: 20.5 us -> 0.37 us
    ppermute x4, starting transfers between devices: 26.7 us -> 12.2 us  [from_sequences(): lax.ppermute(lax.dynamic_index_in_dim(x, turn ^ odd, 0, keepdims=False),...]
  transfers between devices with their start and end apart: 120 -> 111, of which waited for: 35 -> 36; matrix products, arithmetic and copies ran while one was open for 29% -> 9% of each run, Pallas kernels for 22% -> 23%
where the time goes in v4:
time: 1390 us; the launch traced here: 1370 us
  waiting for transfers between devices  586 us (42%)
  Pallas kernels  443 us (32%)
  starting transfers between devices  178 us (13%)
  other arithmetic  78.6 us (6%)
  local copies, waits for them, and re-layouts  72.6 us (5%)
  between operations  15.8 us (1%)
    ppermute x77, waiting for transfers between devices, across(): return lax.ppermute(x, 'rep', [(i, i ^ mask) for i in range(count)])  359 us
    pallas_call x16, Pallas kernels, call(): pl.pallas_call(body, grid=(1,), out_shape=outs, in_specs=in_specs, out_sp...  132 us
    pallas_call x10, Pallas kernels, row_outer(): pl.pallas_call(body, grid=(tiles,), out_shape=[jax.ShapeDtypeStruct((tile...  107 us
    ppermute x12, waiting for transfers between devices, around(): lax.ppermute(x, 'shard', [(i, (i + by) % count) for i in range(count)])  91.9 us
    all_gather x1, waiting for transfers between devices, on_device_block(): lax.all_gather(after(column_block((w_gate, w_up, w_down), me), x_low), 's...  90.4 us
    ppermute x77, starting transfers between devices, across(): return lax.ppermute(x, 'rep', [(i, i ^ mask) for i in range(count)])  88.4 us
    pallas_call x2, Pallas kernels, hidden_units(): pl.pallas_call(body, grid=(3,), out_shape=[jax.ShapeDtypeStruct((rows, un...  60.6 us
    pallas_call x4, Pallas kernels, from_hidden(): pl.pallas_call(body, grid=(4,), out_shape=[jax.ShapeDtypeStruct((2 * rows...  59 us
  transfers between devices with their start and end apart: 111, of which 36 were waited for; matrix products, arithmetic and copies ran while one was open for 9% of the time, Pallas kernels for 23%

profile of v4, /device:TPU:0, one launch (start us, length us, event | category | flops | bytes accessed | tf_op | source)
XLA Modules:
  0.0 1374.1 jit_solution(4913989977935409994)
XLA Ops:
  16.9 12.3 collective-permute-done.2
  52.1 35.8 %collective-permute-done.4 = bf16[256,2048]{1,0:T(8,128)(2,1)} collective-permute-done((bf16[256,2048]{1,0:T(8,128)(2,1)}, bf16[256,2048]{1,0:T(8,128)(2,1)}, u32[]{:S(2)}, u32[]{:S(2)}) %collective-permute-start.4) | collective-permute-done | bytes 1048608 | tf_op jit(solution)/shard_map/ppermute | solution.py:393
  91.3 14.0 %collective-permute-start.7 = (bf16[2,512]{1,0:T(2,128)(2,1)S(1)}, bf16[2,512]{1,0:T(2,128)(2,1)S(1)}, u32[]{:S(2)}, u32[]{:S(2)}) collective-permute-start(bf16[2,512]{1,0:T(2,128)(2,1)S(1)} %pad_maximum_fusion.20), channel_id=1, source_target_pairs={{0,3},{1,0},{2,1},{3,2},{4,7},{5,4},{6,5},{7,6},{8,11},{9,8},{10,9... | collective-permute-start | bytes 6152 | tf_op jit(solution)/shard_map/ppermute | solution.py:322
  129.3 27.0 %collective-permute-done.8.far0.refs_10_ = bf16[512,512]{1,0:T(8,128)(2,1)S(1)} collective-permute-done((bf16[512,512]{1,0:T(8,128)(2,1)}, bf16[512,512]{1,0:T(8,128)(2,1)S(1)}, u32[]{:S(2)}, u32[]{:S(2)}) %collective-permute-start.8) | collective-permute-done | bytes 524320 | tf_op jit(solution)/shard_map/ppermute | solution.py:322
  200.8 90.4 %all-gather.5.cloned.1.call-done.refs_10_.refs_11_.refs_12_.refs_4_.refs_9_ = bf16[2048,2304]{1,0:T(8,128)(2,1)} async-done(((bf16[512,2304]{1,0:T(8,128)(2,1)}), bf16[2048,2304]{1,0:T(8,128)(2,1)}) %all-gather.5.cloned.1.call-update) | async-done | bytes 9437200 | tf_op jit(solution)/shard_map/all_gather | solution.py:934
  388.8 11.7 close_attention.1
  406.2 43.1 %collective-permute-done.40.refs_1_ = bf16[512,2048]{1,0:T(8,128)(2,1)S(1)} collective-permute-done((bf16[512,2048]{1,0:T(8,128)(2,1)}, bf16[512,2048]{1,0:T(8,128)(2,1)S(1)}, u32[]{:S(2)}, u32[]{:S(2)}) %collective-permute-start.40) | collective-permute-done | bytes 2097184 | tf_op jit(solution)/shard_map/ppermute | solution.py:317
  449.3 23.2 %collective-permute-done.43.refs_8_.refs_3_ = bf16[256,2048]{1,0:T(8,128)(2,1)S(1)} collective-permute-done((bf16[256,2048]{1,0:T(8,128)(2,1)S(1)}, bf16[256,2048]{1,0:T(8,128)(2,1)S(1)}, u32[]{:S(2)}, u32[]{:S(2)}) %collective-permute-start.43) | collective-permute-done | bytes 1048608 | tf_op jit(solution)/shard_map/ppermute | solution.py:317
  474.8 22.0 %collective-permute-done.44.refs_3_ = bf16[256,2048]{1,0:T(8,128)(2,1)S(1)} collective-permute-done((bf16[256,2048]{1,0:T(8,128)(2,1)S(1)}, bf16[256,2048]{1,0:T(8,128)(2,1)S(1)}, u32[]{:S(2)}, u32[]{:S(2)}) %collective-permute-start.44) | collective-permute-done | bytes 1048608 | tf_op jit(solution)/shard_map/ppermute | solution.py:317
  499.2 30.0 %hidden_units.2 = (bf16[2048,768]{1,0:T(8,128)(2,1)}, bf16[2048,768]{1,0:T(8,128)(2,1)}, bf16[2048,768]{1,0:T(8,128)(2,1)}) custom-call(bf16[512,2048]{1,0:T(8,128)(2,1)} %get-tuple-element.175.refs_0_, bf16[512,2048]{1,0:T(8,128)(2,1)} %copy-done.58, bf16[512,2048]{1,0:T(8,128)(2,1)} %copy-done.60, bf16[256,2048]{1,0:T(8,128)(2,1)} %copy-done.106, ...), custom_call_target="tpu_custom_call" | custom-call | flops 19327352832 | bytes 41943040 | tf_op jit(solution)/shard_map/hidden_units/pallas_call | solution.py:682
  529.3 30.6 %hidden_units.3 = (bf16[2048,768]{1,0:T(8,128)(2,1)}, bf16[2048,768]{1,0:T(8,128)(2,1)}, bf16[2048,768]{1,0:T(8,128)(2,1)}) custom-call(bf16[512,2048]{1,0:T(8,128)(2,1)} %get-tuple-element.175.refs_0_, bf16[512,2048]{1,0:T(8,128)(2,1)} %copy-done.58, bf16[512,2048]{1,0:T(8,128)(2,1)} %copy-done.60, bf16[256,2048]{1,0:T(8,128)(2,1)} %copy-done.106, ...), custom_call_target="tpu_custom_call" | custom-call | flops 19327352832 | bytes 41943040 | tf_op jit(solution)/shard_map/hidden_units/pallas_call | solution.py:682
  559.9 18.8 %from_hidden.4 = (bf16[512,2048]{1,0:T(8,128)(2,1)}, bf16[512,2048]{1,0:T(8,128)(2,1)}) custom-call(bf16[2048,768]{1,0:T(8,128)(2,1)} %get-tuple-element.187.refs_0_.refs_1_.refs_2_.refs_3_.refs_5_, bf16[2048,768]{1,0:T(8,128)(2,1)} %get-tuple-element.187.refs_0_.refs_1_.refs_2_.refs_3_.refs_5_, ...), custom_call_target="tpu_custom_call" | custom-call | flops 12884901888 | bytes 12582912 | tf_op jit(solution)/shard_map/from_hidden/pallas_call | solution.py:723
  578.7 18.8 %from_hidden.5 = (bf16[512,2048]{1,0:T(8,128)(2,1)}, bf16[512,2048]{1,0:T(8,128)(2,1)}) custom-call(bf16[2048,768]{1,0:T(8,128)(2,1)} %get-tuple-element.187.refs_0_.refs_1_.refs_2_.refs_3_.refs_5_, bf16[2048,768]{1,0:T(8,128)(2,1)} %get-tuple-element.187.refs_0_.refs_1_.refs_2_.refs_3_.refs_5_, ...), custom_call_target="tpu_custom_call" | custom-call | flops 12884901888 | bytes 12582912 | tf_op jit(solution)/shard_map/from_hidden/pallas_call | solution.py:723
  618.9 12.8 row_outer.10
  631.7 19.3 %row_outer.12 = bf16[2048,1536]{1,0:T(8,128)(2,1)} custom-call(bf16[512,2048]{1,0:T(8,128)(2,1)} %get-tuple-element.175.refs_0_, bf16[512,2048]{1,0:T(8,128)(2,1)} %copy-done.58, bf16[512,2048]{1,0:T(8,128)(2,1)} %copy-done.60, bf16[256,2048]{1,0:T(8,128)(2,1)} %copy-done.106, bf16[256,2048]{1,0:T(8,128)(2,1)} %copy-done.107, ...), custom_call_target="tpu_custom_call" | custom-call | flops 12884901888 | bytes 14680064 | tf_op jit(solution)/shard_map/row_outer/pallas_call | solution.py:770
  653.1 13.2 row_outer.11
  668.1 46.1 %collective-permute-done.48 = bf16[512,2048]{1,0:T(8,128)(2,1)S(1)} collective-permute-done((bf16[512,2048]{1,0:T(8,128)(2,1)}, bf16[512,2048]{1,0:T(8,128)(2,1)S(1)}, u32[]{:S(2)}, u32[]{:S(2)}) %collective-permute-start.48) | collective-permute-done | bytes 2097184 | tf_op jit(solution)/shard_map/ppermute | solution.py:317
  718.3 21.2 %collective-permute-done.54 = bf16[256,2048]{1,0:T(8,128)(2,1)S(1)} collective-permute-done((bf16[256,2048]{1,0:T(8,128)(2,1)S(1)}, bf16[256,2048]{1,0:T(8,128)(2,1)S(1)}, u32[]{:S(2)}, u32[]{:S(2)}) %collective-permute-start.54) | collective-permute-done | bytes 1048608 | tf_op jit(solution)/shard_map/ppermute | solution.py:317
  744.3 19.9 %row_outer.13 = bf16[2048,1536]{1,0:T(8,128)(2,1)} custom-call(bf16[512,2048]{1,0:T(8,128)(2,1)} %get-tuple-element.175.refs_0_, bf16[512,2048]{1,0:T(8,128)(2,1)} %copy-done.58, bf16[512,2048]{1,0:T(8,128)(2,1)} %copy-done.60, bf16[256,2048]{1,0:T(8,128)(2,1)} %copy-done.106, bf16[256,2048]{1,0:T(8,128)(2,1)} %copy-done.107, ...), custom_call_target="tpu_custom_call" | custom-call | flops 12884901888 | bytes 14680064 | tf_op jit(solution)/shard_map/row_outer/pallas_call | solution.py:770
  773.4 15.8 %attend_back.7 = (bf16[512,512]{1,0:T(8,128)(2,1)}, f32[512,512]{1,0:T(8,128)}, bf16[512,512]{1,0:T(8,128)(2,1)}, f32[1,128]{1,0:T(1,128)}) custom-call(s32[2]{0:T(128)} %pad_add_fusion.info, bf16[512,512]{1,0:T(8,128)(2,1)} %get-tuple-element.161.query, bf16[512,512]{1,0:T(8,128)(2,1)} %copy-done.115, bf16[512,512]{1,0:T(8,128)(2,1)} %get-tuple-element.162.own, ...), custom_call_target="tpu_custom_call" | custom-call | flops 4294967296 | bytes 9437704 | tf_op jit(solution)/shard_map/attend_back/pallas_call | solution.py:638
  790.9 14.6 %attend_back.6 = (bf16[512,512]{1,0:T(8,128)(2,1)}, f32[512,512]{1,0:T(8,128)}, bf16[512,512]{1,0:T(8,128)(2,1)}, f32[1,128]{1,0:T(1,128)}) custom-call(s32[2]{0:T(128)} %pad_add_fusion.info, bf16[512,512]{1,0:T(8,128)(2,1)} %get-tuple-element.154.query, bf16[512,512]{1,0:T(8,128)(2,1)} %copy-done.114, bf16[512,512]{1,0:T(8,128)(2,1)} %get-tuple-element.155.own, ...), custom_call_target="tpu_custom_call" | custom-call | flops 4294967296 | bytes 9437704 | tf_op jit(solution)/shard_map/attend_back/pallas_call | solution.py:638
  807.0 14.6 %attend_back.5 = (bf16[512,512]{1,0:T(8,128)(2,1)}, f32[512,512]{1,0:T(8,128)}, bf16[512,512]{1,0:T(8,128)(2,1)}, f32[1,128]{1,0:T(1,128)}) custom-call(s32[2]{0:T(128)} %pad_add_fusion.info, bf16[512,512]{1,0:T(8,128)(2,1)} %get-tuple-element.151.query, bf16[512,512]{1,0:T(8,128)(2,1)} %collective-permute-done.16.before, ...), custom_call_target="tpu_custom_call" | custom-call | flops 4294967296 | bytes 9437704 | tf_op jit(solution)/shard_map/attend_back/pallas_call | solution.py:638
  823.1 14.7 %attend_back.4 = (bf16[512,512]{1,0:T(8,128)(2,1)}, f32[512,512]{1,0:T(8,128)}, bf16[512,512]{1,0:T(8,128)(2,1)}, f32[1,128]{1,0:T(1,128)}) custom-call(s32[2]{0:T(128)} %pad_add_fusion.info, bf16[512,512]{1,0:T(8,128)(2,1)} %get-tuple-element.148.query, bf16[512,512]{1,0:T(8,128)(2,1)} %collective-permute-done.11.before, ...), custom_call_target="tpu_custom_call" | custom-call | flops 4294967296 | bytes 9437704 | tf_op jit(solution)/shard_map/attend_back/pallas_call | solution.py:638
  884.9 47.0 %collective-permute-done.49 = bf16[512,2048]{1,0:T(8,128)(2,1)} collective-permute-done((bf16[512,2048]{1,0:T(8,128)(2,1)}, bf16[512,2048]{1,0:T(8,128)(2,1)}, u32[]{:S(2)}, u32[]{:S(2)}) %collective-permute-start.49) | collective-permute-done | bytes 2097184 | tf_op jit(solution)/shard_map/ppermute | solution.py:317
  950.3 16.0 %back_to_rows.1 = f32[512,2048]{1,0:T(8,128)} custom-call(bf16[512,512]{1,0:T(8,128)(2,1)} %get-tuple-element.214.refs_0_.refs_4_, bf16[512,512]{1,0:T(8,128)(2,1)} %get-tuple-element.215.refs_1_, bf16[512,512]{1,0:T(8,128)(2,1)} %get-tuple-element.221.refs_2_.refs_1_.refs_3_, bf16[512,512]{1,0:T(8,128)(2,1)} %get-tuple-element.222.refs_3_.refs_2_, ...), custom_call_target="tpu_custom_call" | custom-call | flops 8589934592 | bytes 16777216 | tf_op jit(solution)/shard_map/back_to_rows/pallas_call | solution.py:877
  966.3 16.9 %collective-permute-done.73 = bf16[1024,512]{1,0:T(8,128)(2,1)S(1)} collective-permute-done((bf16[1024,512]{1,0:T(8,128)(2,1)}, bf16[1024,512]{1,0:T(8,128)(2,1)S(1)}, u32[]{:S(2)}, u32[]{:S(2)}) %collective-permute-start.73) | collective-permute-done | bytes 1048608 | tf_op jit(solution)/shard_map/ppermute | solution.py:317
  1022.4 45.2 %collective-permute-done.76 = bf16[1024,256]{1,0:T(8,128)(2,1)S(1)} collective-permute-done((bf16[1024,256]{1,0:T(8,128)(2,1)S(1)}, bf16[1024,256]{1,0:T(8,128)(2,1)S(1)}, u32[]{:S(2)}, u32[]{:S(2)}) %collective-permute-start.76) | collective-permute-done | bytes 524320 | tf_op jit(solution)/shard_map/ppermute | solution.py:317
  1098.1 20.3 %collective-permute-done.91 = bf16[512,1536]{1,0:T(8,128)(2,1)S(1)} collective-permute-done((bf16[512,1536]{1,0:T(8,128)(2,1)}, bf16[512,1536]{1,0:T(8,128)(2,1)S(1)}, u32[]{:S(2)}, u32[]{:S(2)}) %collective-permute-start.91) | collective-permute-done | bytes 1572896 | tf_op jit(solution)/shard_map/ppermute | solution.py:317
  1120.8 16.9 %collective-permute-done.94 = bf16[512,1536]{1,0:T(8,128)(2,1)} collective-permute-done((bf16[512,1536]{1,0:T(8,128)(2,1)}, bf16[512,1536]{1,0:T(8,128)(2,1)}, u32[]{:S(2)}, u32[]{:S(2)}) %collective-permute-start.94) | collective-permute-done | bytes 1572896 | tf_op jit(solution)/shard_map/ppermute | solution.py:317
  1193.5 20.9 %collective-permute-done.79 = bf16[512,512]{1,0:T(8,128)(2,1)S(1)} collective-permute-done((bf16[512,512]{1,0:T(8,128)(2,1)S(1)}, bf16[512,512]{1,0:T(8,128)(2,1)S(1)}, u32[]{:S(2)}, u32[]{:S(2)}) %collective-permute-start.79) | collective-permute-done | bytes 524320 | tf_op jit(solution)/shard_map/ppermute | solution.py:322
  1275.2 30.7 %collective-permute-start.104 = (bf16[2048,256]{1,0:T(8,128)(2,1)S(1)}, bf16[2048,256]{1,0:T(8,128)(2,1)}, u32[]{:S(2)}, u32[]{:S(2)}) collective-permute-start(bf16[2048,256]{1,0:T(8,128)(2,1)S(1)} %constant_dynamic-update-slice_fusion.13.own), channel_id=1, source_target_pairs={{0,4},{4,0},{8,12},{12,8},{16,20},{20,16},{24,28},{28,24},{1,5},{5... | collective-permute-start | bytes 3145736 | tf_op jit(solution)/shard_map/ppermute | solution.py:317
  1356.1 11.2 whole_columns.11
  (614 shorter events, 563.2 us)
Async XLA Ops:
  7.2 189.4 %all-gather.3.cloned.1.call-start = ((), (), s32[]{:S(2)}) async-start(), calls=%async_computation.2 | async-start | bytes 1310720 | tf_op jit(solution)/shard_map/all_gather | solution.py:931
  47.8 243.4 %all-gather.5.cloned.1.call-start = ((), (), s32[]{:S(2)}) async-start(), calls=%async_computation.3 | async-start | bytes 11796480 | tf_op jit(solution)/shard_map/all_gather | solution.py:934
  91.2 875.1 %reduce-scatter.3.cloned.1.call-start = ((), (), s32[]{:S(2)}) async-start(), calls=%async_computation.4 | async-start | bytes 3932160 | tf_op jit(solution)/shard_map/reduce_scatter | solution.py:1042
  193.8 98.7 %collective-permute-start.19 = (bf16[1024,512]{1,0:T(8,128)(2,1)}, bf16[1024,512]{1,0:T(8,128)(2,1)}, u32[]{:S(2)}, u32[]{:S(2)}) collective-permute-start(bf16[1024,512]{1,0:T(8,128)(2,1)} %collective-permute-done.17.side0.refs_21_), channel_id=1, source_target_pairs={{0,4},{4,0},{8,12},{12,8},{16,20},{20,16},{24,28},{28,24},{1,5},{5... | collective-permute-start | bytes 3145736 | tf_op jit(solution)/shard_map/ppermute | solution.py:317
  193.8 100.2 %collective-permute-start.14 = (bf16[1024,512]{1,0:T(8,128)(2,1)}, bf16[1024,512]{1,0:T(8,128)(2,1)}, u32[]{:S(2)}, u32[]{:S(2)}) collective-permute-start(bf16[1024,512]{1,0:T(8,128)(2,1)} %collective-permute-done.12.side0.refs_15_), channel_id=1, source_target_pairs={{0,4},{4,0},{8,12},{12,8},{16,20},{20,16},{24,28},{28,24},{1,5},{5... | collective-permute-start | bytes 3145736 | tf_op jit(solution)/shard_map/ppermute | solution.py:317
  195.1 101.2 %collective-permute-start.26 = (bf16[1024,512]{1,0:T(8,128)(2,1)}, bf16[1024,512]{1,0:T(8,128)(2,1)}, u32[]{:S(2)}, u32[]{:S(2)}) collective-permute-start(bf16[1024,512]{1,0:T(8,128)(2,1)} %constant_dynamic-update-slice_fusion.2.side0.refs_27_), channel_id=1, source_target_pairs={{0,4},{4,0},{8,12},{12,8},{16,20},{20,16},{24,28},{28,24},{1,5},{5... | collective-permute-start | bytes 3145736 | tf_op jit(solution)/shard_map/ppermute | solution.py:317
  196.6 108.8 %collective-permute-start.30 = (bf16[2048,256]{1,0:T(8,128)(2,1)}, bf16[2048,256]{1,0:T(8,128)(2,1)}, u32[]{:S(2)}, u32[]{:S(2)}) collective-permute-start(bf16[2048,256]{1,0:T(8,128)(2,1)} %all-gather.3.cloned.1.call-done.refs_4_.weight0), channel_id=1, source_target_pairs={{0,8},{4,12},{8,0},{12,4},{16,24},{20,28},{24,16},{28,20},{1,9},{5... | collective-permute-start | bytes 3145736 | tf_op jit(solution)/shard_map/ppermute | solution.py:317
  291.2 238.1 %collective-permute-start.47 = (bf16[2048,2304]{1,0:T(8,128)(2,1)}, bf16[2048,2304]{1,0:T(8,128)(2,1)}, u32[]{:S(2)}, u32[]{:S(2)}) collective-permute-start(bf16[2048,2304]{1,0:T(8,128)(2,1)} %all-gather.5.cloned.1.call-done.refs_10_.refs_11_.refs_12_.refs_4_.refs_9_), channel_id=1, source_target_pairs={{0,4},{4,0},{8,12},{12,8},{16,20},{20,16},{24,28},{28,24},{1,5},{5... | collective-permute-start | bytes 28311560 | tf_op jit(solution)/shard_map/ppermute | solution.py:317
  339.5 61.0 %collective-permute-start.39 = (bf16[512,2048]{1,0:T(8,128)(2,1)S(1)}, bf16[512,2048]{1,0:T(8,128)(2,1)S(1)}, u32[]{:S(2)}, u32[]{:S(2)}) collective-permute-start(bf16[512,2048]{1,0:T(8,128)(2,1)S(1)} %maximum_select_fusion.refs_5_.refs_0_), channel_id=1, source_target_pairs={{0,8},{4,12},{8,0},{12,4},{16,24},{20,28},{24,16},{28,20},{1,9},{5... | collective-permute-start | bytes 6291464 | tf_op jit(solution)/shard_map/ppermute | solution.py:317
  347.8 54.5 %collective-permute-start.41 = (bf16[512,2048]{1,0:T(8,128)(2,1)S(1)}, bf16[512,2048]{1,0:T(8,128)(2,1)}, u32[]{:S(2)}, u32[]{:S(2)}) collective-permute-start(bf16[512,2048]{1,0:T(8,128)(2,1)S(1)} %maximum_select_fusion.refs_5_.refs_0_), channel_id=1, source_target_pairs={{0,16},{4,20},{8,24},{12,28},{16,0},{20,4},{24,8},{28,12},{1,17},{... | collective-permute-start | bytes 6291464 | tf_op jit(solution)/shard_map/ppermute | solution.py:317
  400.5 48.7 %collective-permute-start.40 = (bf16[512,2048]{1,0:T(8,128)(2,1)}, bf16[512,2048]{1,0:T(8,128)(2,1)S(1)}, u32[]{:S(2)}, u32[]{:S(2)}) collective-permute-start(bf16[512,2048]{1,0:T(8,128)(2,1)} %get-tuple-element.175.refs_0_), channel_id=1, source_target_pairs={{0,8},{4,12},{8,0},{12,4},{16,24},{20,28},{24,16},{28,20},{1,9},{5... | collective-permute-start | bytes 6291464 | tf_op jit(solution)/shard_map/ppermute | solution.py:317
  402.3 71.8 %collective-permute-start.42 = (bf16[512,2048]{1,0:T(8,128)(2,1)}, bf16[512,2048]{1,0:T(8,128)(2,1)S(1)}, u32[]{:S(2)}, u32[]{:S(2)}) collective-permute-start(bf16[512,2048]{1,0:T(8,128)(2,1)} %get-tuple-element.175.refs_0_), channel_id=1, source_target_pairs={{0,16},{4,20},{8,24},{12,28},{16,0},{20,4},{24,8},{28,12},{1,17},{... | collective-permute-start | bytes 6291464 | tf_op jit(solution)/shard_map/ppermute | solution.py:317
  403.8 68.7 %collective-permute-start.43 = (bf16[256,2048]{1,0:T(8,128)(2,1)S(1)}, bf16[256,2048]{1,0:T(8,128)(2,1)S(1)}, u32[]{:S(2)}, u32[]{:S(2)}) collective-permute-start(bf16[256,2048]{1,0:T(8,128)(2,1)S(1)} %slice.250), channel_id=1, source_target_pairs={{0,16},{4,20},{8,24},{12,28},{16,0},{20,4},{24,8},{28,12},{1,17},{... | collective-permute-start | bytes 3145736 | tf_op jit(solution)/shard_map/ppermute | solution.py:317
  405.8 68.4 %collective-permute-start.45 = (bf16[256,2048]{1,0:T(8,128)(2,1)S(1)}, bf16[256,2048]{1,0:T(8,128)(2,1)S(1)}, u32[]{:S(2)}, u32[]{:S(2)}) collective-permute-start(bf16[256,2048]{1,0:T(8,128)(2,1)S(1)} %slice.252), channel_id=1, source_target_pairs={{0,8},{4,12},{8,0},{12,4},{16,24},{20,28},{24,16},{28,20},{1,9},{5... | collective-permute-start | bytes 3145736 | tf_op jit(solution)/shard_map/ppermute | solution.py:317
  651.0 93.3 %collective-permute-start.59 = (bf16[2048,1536]{1,0:T(8,128)(2,1)}, bf16[2048,1536]{1,0:T(8,128)(2,1)}, u32[]{:S(2)}, u32[]{:S(2)}) collective-permute-start(bf16[2048,1536]{1,0:T(8,128)(2,1)} %row_outer.12), channel_id=1, source_target_pairs={{0,4},{4,0},{8,12},{12,8},{16,20},{20,16},{24,28},{28,24},{1,5},{5... | collective-permute-start | bytes 18874376 | tf_op jit(solution)/shard_map/ppermute | solution.py:317
  666.3 406.9 %reduce-scatter.5.cloned.1.call-start = ((), (), s32[]{:S(2)}) async-start(), calls=%async_computation.5 | async-start | bytes 7864320 | tf_op jit(solution)/shard_map/reduce_scatter | solution.py:1042
  789.2 49.9 %collective-permute-start.63 = (bf16[512,512]{1,0:T(8,128)(2,1)}, bf16[512,512]{1,0:T(8,128)(2,1)S(1)}, u32[]{:S(2)}, u32[]{:S(2)}) collective-permute-start(bf16[512,512]{1,0:T(8,128)(2,1)} %get-tuple-element.234), channel_id=1, source_target_pairs={{4,0},{12,8},{20,16},{28,24},{5,1},{13,9},{21,17},{29,25},{6,2},{1... | collective-permute-start | bytes 1572872 | tf_op jit(solution)/shard_map/ppermute | solution.py:1080
  868.6 122.9 %collective-permute-start.71 = (bf16[2048,2048]{1,0:T(8,128)(2,1)}, bf16[2048,2048]{1,0:T(8,128)(2,1)}, u32[]{:S(2)}, u32[]{:S(2)}) collective-permute-start(bf16[2048,2048]{1,0:T(8,128)(2,1)} %row_outer.14), channel_id=1, source_target_pairs={{0,4},{4,0},{8,12},{12,8},{16,20},{20,16},{24,28},{28,24},{1,5},{5... | collective-permute-start | bytes 25165832 | tf_op jit(solution)/shard_map/ppermute | solution.py:317
  883.5 54.9 %collective-permute-start.72 = (bf16[2048,1024]{1,0:T(8,128)(2,1)}, bf16[2048,1024]{1,0:T(8,128)(2,1)}, u32[]{:S(2)}, u32[]{:S(2)}) collective-permute-start(bf16[2048,1024]{1,0:T(8,128)(2,1)} %row_outer.16), channel_id=1, source_target_pairs={{0,4},{4,0},{8,12},{12,8},{16,20},{20,16},{24,28},{28,24},{1,5},{5... | collective-permute-start | bytes 12582920 | tf_op jit(solution)/shard_map/ppermute | solution.py:317
  935.9 78.3 %collective-permute-start.55 = (bf16[256,2048]{1,0:T(8,128)(2,1)}, bf16[256,2048]{1,0:T(8,128)(2,1)}, u32[]{:S(2)}, u32[]{:S(2)}) collective-permute-start(bf16[256,2048]{1,0:T(8,128)(2,1)} %get-tuple-element.205), channel_id=1, source_target_pairs={{0,8},{4,12},{8,0},{12,4},{16,24},{20,28},{24,16},{28,20},{1,9},{5... | collective-permute-start | bytes 3145736 | tf_op jit(solution)/shard_map/ppermute | solution.py:317
  937.5 74.3 %collective-permute-start.51 = (bf16[256,2048]{1,0:T(8,128)(2,1)}, bf16[256,2048]{1,0:T(8,128)(2,1)}, u32[]{:S(2)}, u32[]{:S(2)}) collective-permute-start(bf16[256,2048]{1,0:T(8,128)(2,1)} %get-tuple-element.199), channel_id=1, source_target_pairs={{0,16},{4,20},{8,24},{12,28},{16,0},{20,4},{24,8},{28,12},{1,17},{... | collective-permute-start | bytes 3145736 | tf_op jit(solution)/shard_map/ppermute | solution.py:317
  1002.6 70.7 %collective-permute-start.75 = (bf16[1024,1024]{1,0:T(8,128)(2,1)}, bf16[1024,1024]{1,0:T(8,128)(2,1)}, u32[]{:S(2)}, u32[]{:S(2)}) collective-permute-start(bf16[1024,1024]{1,0:T(8,128)(2,1)} %get-tuple-element.250), channel_id=1, source_target_pairs={{0,8},{4,12},{8,0},{12,4},{16,24},{20,28},{24,16},{28,20},{1,9},{5... | collective-permute-start | bytes 6291464 | tf_op jit(solution)/shard_map/ppermute | solution.py:317
  1010.5 68.0 %collective-permute-start.82 = (bf16[1024,1024]{1,0:T(8,128)(2,1)}, bf16[1024,1024]{1,0:T(8,128)(2,1)}, u32[]{:S(2)}, u32[]{:S(2)}) collective-permute-start(bf16[1024,1024]{1,0:T(8,128)(2,1)} %get-tuple-element.261), channel_id=1, source_target_pairs={{0,16},{4,20},{8,24},{12,28},{16,0},{20,4},{24,8},{28,12},{1,17},{... | collective-permute-start | bytes 6291464 | tf_op jit(solution)/shard_map/ppermute | solution.py:317
  1011.8 55.8 %collective-permute-start.76 = (bf16[1024,256]{1,0:T(8,128)(2,1)S(1)}, bf16[1024,256]{1,0:T(8,128)(2,1)S(1)}, u32[]{:S(2)}, u32[]{:S(2)}) collective-permute-start(bf16[1024,256]{1,0:T(8,128)(2,1)S(1)} %add_convert_fusion.7), channel_id=1, source_target_pairs={{0,16},{4,20},{8,24},{12,28},{16,0},{20,4},{24,8},{28,12},{1,17},{... | collective-permute-start | bytes 1572872 | tf_op jit(solution)/shard_map/ppermute | solution.py:317
  1014.1 57.5 %collective-permute-start.83 = (bf16[1024,256]{1,0:T(8,128)(2,1)S(1)}, bf16[1024,256]{1,0:T(8,128)(2,1)S(1)}, u32[]{:S(2)}, u32[]{:S(2)}) collective-permute-start(bf16[1024,256]{1,0:T(8,128)(2,1)S(1)} %add_convert_fusion.6), channel_id=1, source_target_pairs={{0,8},{4,12},{8,0},{12,4},{16,24},{20,28},{24,16},{28,20},{1,9},{5... | collective-permute-start | bytes 1572872 | tf_op jit(solution)/shard_map/ppermute | solution.py:317
  1020.3 48.8 %collective-permute-start.67 = (f32[4352]{0:T(1024)S(1)}, f32[4352]{0:T(1024)S(1)}, u32[]{:S(2)}, u32[]{:S(2)}) collective-permute-start(f32[4352]{0:T(1024)S(1)} %fusion.24), channel_id=1, source_target_pairs={{0,8},{4,12},{8,0},{12,4},{16,24},{20,28},{24,16},{28,20},{1,9},{5... | collective-permute-start | bytes 52232 | tf_op jit(solution)/shard_map/ppermute | solution.py:317
  1078.5 59.2 %collective-permute-start.94 = (bf16[512,1536]{1,0:T(8,128)(2,1)}, bf16[512,1536]{1,0:T(8,128)(2,1)}, u32[]{:S(2)}, u32[]{:S(2)}) collective-permute-start(bf16[512,1536]{1,0:T(8,128)(2,1)} %reduce-scatter.5.cloned.1.call-done), channel_id=1, source_target_pairs={{0,16},{4,20},{8,24},{12,28},{16,0},{20,4},{24,8},{28,12},{1,17},{... | collective-permute-start | bytes 4718600 | tf_op jit(solution)/shard_map/ppermute | solution.py:317
  1084.8 54.0 %collective-permute-start.85 = (bf16[1024,512]{1,0:T(8,128)(2,1)}, bf16[1024,512]{1,0:T(8,128)(2,1)}, u32[]{:S(2)}, u32[]{:S(2)}) collective-permute-start(bf16[1024,512]{1,0:T(8,128)(2,1)} %add_convert_fusion), channel_id=1, source_target_pairs={{0,8},{4,12},{8,0},{12,4},{16,24},{20,28},{24,16},{28,20},{1,9},{5... | collective-permute-start | bytes 3145736 | tf_op jit(solution)/shard_map/ppermute | solution.py:317
  1093.5 93.6 %collective-permute-start.69 = (f32[4352]{0:T(1024)S(1)}, f32[4352]{0:T(1024)S(1)}, u32[]{:S(2)}, u32[]{:S(2)}) collective-permute-start(f32[4352]{0:T(1024)S(1)} %add.354), channel_id=1, source_target_pairs={{0,1},{1,0},{2,3},{3,2},{4,5},{5,4},{6,7},{7,6},{8,9},{9,8},{10,11... | collective-permute-start | bytes 52232 | tf_op jit(solution)/shard_map/ppermute | solution.py:1138
  1152.9 192.1 %collective-permute-start.105 = (bf16[2048,1536]{1,0:T(8,128)(2,1)}, bf16[2048,1536]{1,0:T(8,128)(2,1)}, u32[]{:S(2)}, u32[]{:S(2)}) collective-permute-start(bf16[2048,1536]{1,0:T(8,128)(2,1)} %constant_dynamic-update-slice_fusion.18.own), channel_id=1, source_target_pairs={{0,4},{4,0},{8,12},{12,8},{16,20},{20,16},{24,28},{28,24},{1,5},{5... | collective-permute-start | bytes 18874376 | tf_op jit(solution)/shard_map/ppermute | solution.py:317
  1241.2 67.9 %collective-permute-start.106 = (bf16[2048,768]{1,0:T(8,128)(2,1)}, bf16[2048,768]{1,0:T(8,128)(2,1)}, u32[]{:S(2)}, u32[]{:S(2)}) collective-permute-start(bf16[2048,768]{1,0:T(8,128)(2,1)} %constant_dynamic-update-slice_fusion.23.own), channel_id=1, source_target_pairs={{0,4},{4,0},{8,12},{12,8},{16,20},{20,16},{24,28},{28,24},{1,5},{5... | collective-permute-start | bytes 9437192 | tf_op jit(solution)/shard_map/ppermute | solution.py:317
  1272.5 54.1 %collective-permute-start.103 = (bf16[2048,512]{1,0:T(8,128)(2,1)S(1)}, bf16[2048,512]{1,0:T(8,128)(2,1)S(1)}, u32[]{:S(2)}, u32[]{:S(2)}) collective-permute-start(bf16[2048,512]{1,0:T(8,128)(2,1)S(1)} %constant_dynamic-update-slice_fusion.8.own), channel_id=1, source_target_pairs={{0,4},{4,0},{8,12},{12,8},{16,20},{20,16},{24,28},{28,24},{1,5},{5... | collective-permute-start | bytes 6291464 | tf_op jit(solution)/shard_map/ppermute | solution.py:317
  (197 other events, 3808.0 us)
Sparse Core Ops, SparseCore 0:
  47.9 50.7 all-gather.2
  100.9 190.2 all-gather.4
  666.5 64.4 reduce-scatter.2
  764.3 114.9 reduce-scatter.4

commit v5 on v4

--- a/solution.py
+++ b/solution.py
@@ -310,6 +310,7 @@
 
 CORE, ACROSS_X, ACROSS_Y = 1, 2, 4
 VMEM_BYTES = 56 * 2**20
+FREE = pl.CostEstimate(flops=1, bytes_accessed=1, transcendentals=0)
 
 
 def across(x, mask):
@@ -322,49 +323,41 @@
     return lax.ppermute(x, "shard", [(i, (i + by) % count) for i in range(count)])
 
 
-def after(x, *done):
-    return lax.optimization_barrier((x, *done))[0]
-
-
-def ring_gather(x):
-    before, behind = around(x, 1), around(x, -1)
-    return [x, before, around(before, 1), behind]
-
-
-def ring_sum(chunks, kind):
-    last = chunks[3] + around(chunks[2].astype(kind), 1)
-    return chunks[0] + around(chunks[1].astype(kind), -1) + around(last.astype(kind), 1)
-
-
-class Links:
-    def __init__(self):
-        self.sent = {ACROSS_X: [], ACROSS_Y: []}
-
-    def send(self, x, mask):
-        sent = self.sent[mask]
-        if len(sent) > 1:
-            x = after(x, sent[-2])
-        sent.append(across(x, mask))
-        return sent[-1]
-
-    def gather(self, *pieces):
-        near = [(self.send(p, ACROSS_X), self.send(p, ACROSS_Y)) for p in pieces]
-        out = []
-        for piece, (from_x, from_y) in zip(pieces, near):
-            half = piece.shape[0] // 2
-            far = self.send(from_x[:half], ACROSS_Y), self.send(from_y[half:], ACROSS_X)
-            out.append([piece, from_x, from_y, *far])
-        return out
-
-    def total(self, to_x, to_y, split, own_head, own_tail, two_head, one_tail):
-        low, full = jnp.bfloat16, jnp.float32
-        x_own, x_two = split(self.send(to_x, ACROSS_X))
-        y_own, y_one = split(self.send(to_y, ACROSS_Y))
-        two_head = (two_head.astype(full) + x_two).astype(low)
-        one_tail = (one_tail.astype(full) + y_one).astype(low)
-        own_head = own_head.astype(full) + x_own + self.send(two_head, ACROSS_Y)
-        own_tail = own_tail.astype(full) + y_own + self.send(one_tail, ACROSS_X)
-        return jnp.concatenate([own_head, own_tail], 0)
+class Stage(dict):
+    __getattr__ = dict.__getitem__
+    __setattr__ = dict.__setitem__
+
+    def end(self, *gone):
+        for name in gone:
+            del self[name]
+        self.update(lax.optimization_barrier(dict(self)))
+
+
+def in_order(calls):
+    outs = []
+    for call, first, *rest in calls:
+        if outs:
+            last = outs[-1][0] if isinstance(outs[-1], (list, tuple)) else outs[-1]
+            first = lax.optimization_barrier((first, last))[0]
+        outs.append(call(first, *rest))
+    return outs
+
+
+def ring_sum_first(chunks):
+    return around(chunks[2], 1), around(chunks[1], -1)
+
+
+def near(piece):
+    return across(piece, ACROSS_X), across(piece, ACROSS_Y)
+
+
+def far(from_x, from_y):
+    half = from_x.shape[0] // 2
+    return across(from_x[:half], ACROSS_Y), across(from_y[half:], ACROSS_X)
+
+
+def rounded_sum(*parts):
+    return sum(part.astype(jnp.float32) for part in parts).astype(jnp.bfloat16)
 
 
 def sequence_pairs(turn):
@@ -387,9 +380,9 @@
     )
 
 
-def to_sequences(x):
+def to_sequences_send(x):
     odd = lax.axis_index("shard") & 1
-    came = [
+    return [
         lax.ppermute(
             lax.dynamic_index_in_dim(x, turn ^ odd, 0, keepdims=False),
             ("rep", "shard"),
@@ -397,16 +390,12 @@
         )
         for turn in range(2)
     ]
-    even = odd == 0
-    return jnp.concatenate(
-        [jnp.where(even, came[0], came[1]), jnp.where(even, came[1], came[0])], 0
-    )
-
-
-def from_sequences(x):
+
+
+def from_sequences_send(x):
     odd = lax.axis_index("shard") & 1
     x = x.reshape(2, x.shape[0] // 2, x.shape[1])
-    came = [
+    return [
         lax.ppermute(
             lax.dynamic_index_in_dim(x, turn ^ odd, 0, keepdims=False),
             ("rep", "shard"),
@@ -414,8 +403,11 @@
         )
         for turn in range(2)
     ]
-    even = odd == 0
-    return jnp.stack([jnp.where(even, came[0], came[1]), jnp.where(even, came[1], came[0])])
+
+
+def in_turn(came):
+    even = lax.axis_index("shard") & 1 == 0
+    return [jnp.where(even, came[0], came[1]), jnp.where(even, came[1], came[0])]
 
 
 def column_block(weights, at):
@@ -425,47 +417,34 @@
     )
 
 
-def spread_blocks(links, block):
-    own = jnp.concatenate(links.gather(block)[0], 0)
-    return own, across(own, CORE)
-
-
-def whole_body(me, own, other, out):
-    mine = (me[0] ^ pl.program_id(0)) & 1 == 0
-
-    @pl.when(mine)
-    def _():
-        out[...] = own[...].astype(jnp.float32)
-
-    @pl.when(jnp.logical_not(mine))
-    def _():
-        out[...] = other[...].astype(jnp.float32)
-
-
-def whole_columns(me, own, other, first, width):
-    rows = own.shape[0] // 4
-    spec = pl.BlockSpec((rows, width), lambda i, at: ((at[0] ^ i) >> 1, first // width))
+def whole_columns(me, own, other, widths):
+    rows, columns = own.shape[0] // 4, own.shape[1]
+
+    def body(me_ref, own_ref, other_ref, *outs):
+        def put(block):
+            start = 0
+            for out, width in zip(outs, widths):
+                out[...] = block[:, start : start + width].astype(jnp.float32)
+                start += width
+
+        mine = (me_ref[0] ^ pl.program_id(0)) & 1 == 0
+        pl.when(mine)(lambda: put(own_ref))
+        pl.when(jnp.logical_not(mine))(lambda: put(other_ref))
+
+    spec = pl.BlockSpec((rows, columns), lambda i, at: ((at[0] ^ i) >> 1, 0))
     return pl.pallas_call(
-        whole_body,
+        body,
         grid_spec=pltpu.PrefetchScalarGridSpec(
             num_scalar_prefetch=1,
             grid=(8,),
             in_specs=[spec, spec],
-            out_specs=pl.BlockSpec((rows, width), lambda i, at: (0, i)),
+            out_specs=[pl.BlockSpec((rows, w), lambda i, at: (0, i)) for w in widths],
         ),
-        out_shape=jax.ShapeDtypeStruct((rows, 8 * width), jnp.float32),
+        out_shape=[jax.ShapeDtypeStruct((rows, 8 * w), jnp.float32) for w in widths],
         compiler_params=pltpu.CompilerParams(vmem_limit_bytes=VMEM_BYTES),
-        cost_estimate=pl.CostEstimate(
-            flops=rows * 8 * width, bytes_accessed=48 * rows * width, transcendentals=0
-        ),
+        cost_estimate=FREE,
         name="whole_columns",
     )(me, own, other)
-
-
-def everywhere_sum(x):
-    for mask in (CORE, ACROSS_X, ACROSS_Y):
-        x = x + across(x, mask)
-    return x
 
 
 def turned(x):
@@ -490,22 +469,15 @@
 
 
 def project_body(
-    normed, own0, side0, far0, own1, side1, far1, cosine, sine, gains, raw, query, key_value
+    normed, own0, came0, own1, came1, cosine, sine, gains, raw, query, key_value
 ):
     step = own0.shape[0]
     dim = cosine.shape[1]
-    for block, (own, side, far) in enumerate(((own0, side0, far0), (own1, side1, far1))):
+    for block, (own, came) in enumerate(((own0, came0), (own1, came1))):
         at = block * 4 * dim
-        raw[:, at : at + 4 * dim] = (
-            jnp.dot(normed[:, :step], own[...], preferred_element_type=jnp.float32)
-            + jnp.dot(
-                normed[:, step : 2 * step], side[:step], preferred_element_type=jnp.float32
-            )
-            + jnp.dot(
-                normed[:, 2 * step : 3 * step], far[...], preferred_element_type=jnp.float32
-            )
-            + jnp.dot(normed[:, 3 * step :], side[step:], preferred_element_type=jnp.float32)
-        )
+        raw[:, at : at + 4 * dim] = jnp.dot(
+            normed[:, :step], own[...], preferred_element_type=jnp.float32
+        ) + jnp.dot(normed[:, step:], came[...], preferred_element_type=jnp.float32)
         for i in range(3):
             unit, _ = unit_of(raw[:, at + i * dim : at + (i + 1) * dim])
             head = unit * gains[i // 2 : i // 2 + 1, :]
@@ -629,7 +601,7 @@
     gain_part[...] = total
 
 
-def vmem_call(body, outs, flops, scratch=(), scalars=0, name=None):
+def vmem_call(body, outs, scratch=(), scalars=0, name=None):
     def call(*args):
         in_specs = [
             pl.BlockSpec(memory_space=pltpu.SMEM if i < scalars else pltpu.VMEM)
@@ -643,11 +615,7 @@
             out_specs=jax.tree.map(lambda _: pl.BlockSpec(memory_space=pltpu.VMEM), outs),
             scratch_shapes=scratch,
             compiler_params=pltpu.CompilerParams(vmem_limit_bytes=VMEM_BYTES),
-            cost_estimate=pl.CostEstimate(
-                flops=flops,
-                bytes_accessed=sum(a.size * a.dtype.itemsize for a in args),
-                transcendentals=0,
-            ),
+        cost_estimate=FREE,
             name=name,
         )(*args)
 
@@ -692,9 +660,7 @@
         ],
         out_specs=[pl.BlockSpec((rows, cut), lambda j: (0, j))] * 3,
         compiler_params=pltpu.CompilerParams(vmem_limit_bytes=VMEM_BYTES),
-        cost_estimate=pl.CostEstimate(
-            flops=6 * rows * width * units, bytes_accessed=10 * rows * width, transcendentals=0
-        ),
+        cost_estimate=FREE,
         name="hidden_units",
     )(*mids, *grads_y, weights, weights, weights)
 
@@ -727,11 +693,7 @@
         in_specs=specs,
         out_specs=[pl.BlockSpec((2 * rows, cut), lambda j: (0, j))] * (parts // 2),
         compiler_params=pltpu.CompilerParams(vmem_limit_bytes=VMEM_BYTES),
-        cost_estimate=pl.CostEstimate(
-            flops=2 * parts * count * rows * width * units,
-            bytes_accessed=2 * count * width * units,
-            transcendentals=0,
-        ),
+        cost_estimate=FREE,
         name="from_hidden",
     )(*args)
 
@@ -830,9 +792,7 @@
         ],
         out_specs=[pl.BlockSpec((rows, width), lambda j: (0, 0))] * 2,
         compiler_params=pltpu.CompilerParams(vmem_limit_bytes=VMEM_BYTES),
-        cost_estimate=pl.CostEstimate(
-            flops=2 * rows * width * width, bytes_accessed=2 * width * width, transcendentals=0
-        ),
+        cost_estimate=FREE,
         name="close_attention",
     )(x, *mixed, *weights, gains)
 
@@ -844,20 +804,16 @@
 
     def body(*refs):
         lefts = refs[:count]
-        hbm = refs[count : 4 * count]
-        out = refs[4 * count]
-        held, sems = refs[4 * count + 1 :]
+        hbm = refs[count : 3 * count]
+        out = refs[3 * count]
+        held, sems = refs[3 * count + 1 :]
         copies = []
         for i in range(count):
-            own, side, far = hbm[3 * i : 3 * i + 3]
+            own, came = hbm[2 * i : 2 * i + 2]
             copies.append(
                 [
                     pltpu.make_async_copy(own, held.at[i, :step], sems.at[i, 0]),
-                    pltpu.make_async_copy(
-                        side.at[:step], held.at[i, step : 2 * step], sems.at[i, 1]
-                    ),
-                    pltpu.make_async_copy(far, held.at[i, 2 * step : 3 * step], sems.at[i, 2]),
-                    pltpu.make_async_copy(side.at[step:], held.at[i, 3 * step :], sems.at[i, 3]),
+                    pltpu.make_async_copy(came, held.at[i, step:], sems.at[i, 1]),
                 ]
             )
         for some in copies:
@@ -879,18 +835,14 @@
         grid=(1,),
         out_shape=jax.ShapeDtypeStruct((rows, 4 * step), jnp.float32),
         in_specs=[pl.BlockSpec(memory_space=pltpu.VMEM)] * count
-        + [pl.BlockSpec(memory_space=pl.ANY)] * (3 * count),
+        + [pl.BlockSpec(memory_space=pl.ANY)] * (2 * count),
         out_specs=pl.BlockSpec(memory_space=pltpu.VMEM),
         scratch_shapes=[
             pltpu.VMEM((count, 4 * step, columns), jnp.bfloat16),
-            pltpu.SemaphoreType.DMA((count, 4)),
+            pltpu.SemaphoreType.DMA((count, 2)),
         ],
         compiler_params=pltpu.CompilerParams(vmem_limit_bytes=VMEM_BYTES),
-        cost_estimate=pl.CostEstimate(
-            flops=8 * rows * step * columns * count,
-            bytes_accessed=8 * step * columns * count,
-            transcendentals=0,
-        ),
+        cost_estimate=FREE,
         name="back_to_rows",
     )(*blocks, *(part for w in weights for part in w))
 
@@ -920,240 +872,427 @@
     core = me & 1
     count = lax.axis_size("rep")
 
-    links = Links()
-    own_blocks = [
+    s = Stage(tokens=tokens, cotangent=cotangent)
+    piece = width // shards
+
+    s.own_blocks = [
         column_block((w_query, key_matrix, value_matrix), me ^ i) for i in range(8)
     ]
-    before, behind = around(own_blocks[0], 1), around(own_blocks[0], -1)
-    x_low = to_sequences(after(tokens, before, behind))
-    rows = x_low.shape[0]
-    far = around(before, 1)
-    out_own = lax.all_gather(
-        after(column_block((w_out,), me), before, behind), "shard", axis=0, tiled=True
-    )
-    ffn_own = lax.all_gather(
-        after(column_block((w_gate, w_up, w_down), me), x_low), "shard", axis=0, tiled=True
-    )
-    side_blocks, far_blocks = (
-        [*blocks[:3], jnp.concatenate(blocks[3:], 0)]
-        for blocks in links.gather(jnp.concatenate([before, behind], 0), far)
-    )
-    other_side = [across(block, CORE) for block in side_blocks]
-    other_far = [across(block, CORE) for block in far_blocks]
-    qkv_weights = [
-        part
-        for i in range(4)
-        for part in (
-            (own_blocks[2 * i], side_blocks[i], far_blocks[i]),
-            (own_blocks[2 * i + 1], other_side[i], other_far[i]),
-        )
-    ]
-    gain_parts = jnp.stack([attn_gain, mlp_gain])
-    gains = jnp.concatenate(
-        [gain_parts, *(around(gain_parts, by) for by in (1, 2, 3))], 1
-    ).astype(full)
-    gains = rolled(gains)
-    attn_gains, mlp_gains = gains[:1], gains[1:]
+    gain_rows = jnp.concatenate(
+        [jnp.stack([attn_gain, mlp_gain]), jnp.zeros((14, piece), low)], 0
+    )
+    travelling = jnp.concatenate([s.own_blocks[0], gain_rows], 0)
+    s.out_block = column_block((w_out,), me)
+    s.ffn_block = column_block((w_gate, w_up, w_down), me)
+    s.before, s.behind = around(travelling, 1), around(travelling, -1)
+    s.other_lengths = across(lengths, CORE)
+    s.end()
+
+    s.ahead = around(s.before, 1)
+    tokens_sent = to_sequences_send(s.tokens)
+    out_own = lax.all_gather(s.out_block, "shard", axis=0, tiled=True)
+    s.end("out_block", "tokens")
+
+    parts = (s.before, s.ahead, s.behind)
+    s.came = jnp.concatenate([part[:piece] for part in parts], 0)
+    s.gains = jnp.concatenate([gain_rows[:2], *(part[piece : piece + 2] for part in parts)], 1)
+    s.came_near = near(s.came)
+    s.x_came = tokens_sent
+    s.end("before", "behind", "ahead")
+
+    s.came_far = far(*s.came_near)
+    s.came_other = [across(block, CORE) for block in (s.came, *s.came_near)]
+    gains = rolled(s.gains.astype(full))
+    s.mlp_gains = gains[1:]
+    s.attn_gains = gains[:1]
+    s.x_low = jnp.concatenate(in_turn(s.x_came), 0)
+    rows = s.x_low.shape[0]
+    x_rows = s.x_low.astype(full)
+    s.inverse_in = lax.rsqrt(jnp.mean(x_rows * x_rows, -1, keepdims=True) + EPS)
+    s.normed = rolled((x_rows * s.inverse_in * s.attn_gains).astype(low))
     query_gains = query_gain.astype(full)[None]
     key_gains = key_gain.astype(full)[None]
-
-    other_lengths = across(lengths, CORE)
+    s.head_gains = jnp.concatenate([query_gains, key_gains], 0)
     both = jnp.where(
         core == 0,
-        jnp.concatenate([lengths, other_lengths]),
-        jnp.concatenate([other_lengths, lengths]),
+        jnp.concatenate([lengths, s.other_lengths]),
+        jnp.concatenate([s.other_lengths, lengths]),
     )
     length = lax.dynamic_index_in_dim(both, shard_at, 0, keepdims=False)
-    info = jnp.stack([core, length]).astype(jnp.int32)
+    s.info = jnp.stack([core, length]).astype(jnp.int32)
     query_pos = core * rows + jnp.arange(rows, dtype=jnp.int32)
-    valid = (query_pos < length)[:, None]
+    s.valid = (query_pos < length)[:, None].astype(full)
     cosine, sine = tables(query_pos, head_dim)
-    cosine, sine = cosine[0, :, 0], sine[0, :, 0]
-    sine = jnp.concatenate([-sine[:, : head_dim // 2], sine[:, head_dim // 2 :]], 1)
-
-    out_chips = links.gather(out_own)[0]
-    out_chips = [*out_chips[:3], jnp.concatenate(out_chips[3:], 0)]
-    out_blocks = [block for chip in out_chips for block in (chip, across(chip, CORE))]
-    grad_y_low = to_sequences(after(cotangent, x_low, out_own))
-    grad_y_low = jnp.where(valid, grad_y_low, jnp.zeros_like(grad_y_low))
-    grads_y = links.gather(grad_y_low)[0]
-    ffn = [ffn_own, across(ffn_own, CORE)]
-    units = ffn_own.shape[1] // 3
-
-    x_rows = x_low.astype(full)
-    inverse_in = lax.rsqrt(jnp.mean(x_rows * x_rows, -1, keepdims=True) + EPS)
-    x_unit = x_rows * inverse_in
-    normed = rolled((x_unit * attn_gains).astype(low))
+    s.cosine, sine = cosine[0, :, 0], sine[0, :, 0]
+    s.sine = jnp.concatenate([-sine[:, : head_dim // 2], sine[:, head_dim // 2 :]], 1)
+    s.out_own = out_own
+    s.end("gains", "x_came", "other_lengths")
+
     head_columns = 2 * head_dim
     block_columns = 4 * head_dim
     quad_rows = jax.ShapeDtypeStruct((rows, block_columns), low)
+    quad_sums = jax.ShapeDtypeStruct((rows, block_columns), full)
+    gain_sum = jax.ShapeDtypeStruct((1, head_dim), full)
     project = vmem_call(
         project_body,
         [jax.ShapeDtypeStruct((rows, 2 * block_columns), full), quad_rows, quad_rows],
-        4 * rows * width * block_columns,
         name="project",
     )
-    attend = vmem_call(
-        attend_body,
-        [quad_rows, jax.ShapeDtypeStruct((rows, block_columns), full)],
-        12 * rows * rows * block_columns,
-        scalars=1,
-        name="attend",
-    )
-    head_gains = jnp.concatenate([query_gains, key_gains], 0)
-    upward = [(i, i + 1) for i in range(0, count, 2)]
-    downward = [(i + 1, i) for i in range(0, count, 2)]
-    projected = [
-        project(normed, *qkv_weights[2 * i], *qkv_weights[2 * i + 1], cosine, sine, head_gains)
-        for i in range(4)
-    ]
-    earlier = [lax.ppermute(p[2], "rep", upward) for p in projected]
-    attended = [
-        attend(info, projected[i][1], earlier[i], projected[i][2]) for i in range(4)
-    ]
-    mixed = [a[0] for a in attended]
-    resid, mid = close_attention(x_low, mixed, out_blocks, mlp_gains)
-    inverse_mid = lax.rsqrt(jnp.mean(resid * resid, -1, keepdims=True) + EPS)
-    mid_unit = resid * inverse_mid
-
-    mids = links.gather(mid)[0]
-    hidden = [hidden_units(mids, grads_y, ffn[i]) for i in range(2)]
-
-    def plane_total(pairs):
-        to_x, to_y = from_hidden(pairs, (2, 6, 5, 7))
-        rest, own = from_hidden([(after(pairs[0][0], to_x), *pairs[0][1:]), *pairs[1:]], (3, 4, 0, 1))
-        half = rows // 2
-        total = links.total(
-            to_x, to_y, lambda a: (a[:half], a[half:]),
-            own[:half], own[half:], rest[half:], rest[:half],
-        )
-        return total, own
-
-    grad_mid, last = plane_total(
-        [(hidden[i][1 + j], ffn[i], j) for i in range(2) for j in range(2)]
-    )
-    acts = [after(hidden[0][0], last), hidden[1][0]]
-    mlp_out, last = plane_total([(acts[i], ffn[i], 2) for i in range(2)])
-    output = from_sequences(jnp.where(valid, resid + mlp_out, 0.0).astype(low))
-
-    def owned_part(lefts, rights, *done):
-        (other,) = row_outer(lefts, [[after(rights[1][0], *done), *rights[1][1:]]], 0, 8)
-        (own,) = row_outer(lefts, [rights[0]], 0, 8, across(other, CORE))
-        return own, other, lax.psum_scatter(own, "shard", scatter_dimension=0, tiled=True)
-
-    down_own, last, down_total = owned_part(grads_y, [[h[0]] for h in hidden], last)
-    gate_up_own, _, gate_up_total = owned_part(mids, [h[1:] for h in hidden], last)
-    grad_mid = after(grad_mid, down_own, gate_up_own)
-
-    mlp_gain_part = jnp.sum(mid_unit * grad_mid, 0)
-    grad_resid = grad_y_low.astype(full) + norm_back(mid_unit, inverse_mid, grad_mid * mlp_gains)
-    resid_low = grad_resid.astype(low)
+    attend = vmem_call(attend_body, [quad_rows, quad_sums], scalars=1, name="attend")
     attend_back = vmem_call(
         attend_back_body,
-        [
-            quad_rows,
-            jax.ShapeDtypeStruct((rows, block_columns), full),
-            quad_rows,
-            jax.ShapeDtypeStruct((1, head_dim), full),
-        ],
-        32 * rows * rows * block_columns,
+        [quad_rows, quad_sums, quad_rows, gain_sum],
         scratch=[pltpu.VMEM((2 * rows, head_dim), full)] * 2
         + [pltpu.VMEM((rows, block_columns), low)],
         scalars=1,
         name="attend_back",
     )
-    finish = vmem_call(
-        finish_body,
-        [quad_rows, quad_rows, jax.ShapeDtypeStruct((1, head_dim), full)],
-        rows * head_dim,
-        name="finish",
-    )
-    order = (3, 1, 2, 0)
-    backs, finished = {}, {}
-    for i in order:
-        raw, query, own_pair = projected[i]
-        backs[i] = attend_back(
-            info, query, earlier[i], own_pair, attended[i][1], resid_low, *out_blocks[2 * i : 2 * i + 2],
-            raw, cosine, sine, query_gains,
+    finish = vmem_call(finish_body, [quad_rows, quad_rows, gain_sum], name="finish")
+    upward = [(i, i + 1) for i in range(0, count, 2)]
+    downward = [(i + 1, i) for i in range(0, count, 2)]
+
+    def project_call(i, came, other):
+        return (
+            project, s.normed, s.own_blocks[2 * i], came, s.own_blocks[2 * i + 1], other,
+            s.cosine, s.sine, s.head_gains,
         )
-    for i in order:
-        came = lax.ppermute(backs[i][2], "rep", downward)
-        finished[i] = finish(
-            backs[i][0], backs[i][1], came, projected[i][0], cosine, sine, key_gains
+
+    ffn_own = lax.all_gather(s.ffn_block, "shard", axis=0, tiled=True)
+    came_last = jnp.concatenate(s.came_far, 0)
+    s.came_last = (came_last, across(came_last, CORE))
+    s.out_near = near(s.out_own)
+    s.projected = in_order(
+        [
+            project_call(i, block, other)
+            for i, (block, other) in enumerate(zip((s.came, *s.came_near), s.came_other))
+        ]
+    )
+    s.end("came_far", "ffn_block")
+
+    s.out_far = far(*s.out_near)
+    s.earlier = [lax.ppermute(p[2], "rep", upward) for p in s.projected]
+    s.projected_last = project_call(3, *s.came_last)[0](*project_call(3, *s.came_last)[1:])
+    s.end()
+
+    out_chips = (s.out_own, *s.out_near, jnp.concatenate(s.out_far, 0))
+    s.out_chips = [(block, across(block, CORE)) for block in out_chips]
+    s.earlier_last = lax.ppermute(s.projected_last[2], "rep", upward)
+
+    def attend_call(projected, earlier):
+        return (
+            lambda query, own, before: attend(s.info, query, before, own),
+            *projected[1:], earlier,
         )
-    query_gain_part = sum(backs[i][3] for i in order)
-    key_gain_part = sum(finished[i][2] for i in order)
-
-    def block_total(left, even, odd):
-        columns = even[0].shape[1]
-        (other,) = row_outer([left], [odd], 0, 8)
-        came = across(other, CORE)
-        to_x, two_head, own_head = row_outer(
-            [left], [[even[1], even[3]], [even[2]], [even[0]]], 0, 4, came, (1, 3, 2, 0)
+
+    s.attended = in_order([attend_call(*pair) for pair in zip(s.projected, s.earlier)])
+    s.end("out_own", "out_near", "out_far")
+
+    grad_y_sent = to_sequences_send(s.cotangent)
+    s.projected = [*s.projected, s.projected_last]
+    s.earlier = [*s.earlier, s.earlier_last]
+    s.out_blocks = [block for chip in s.out_chips for block in chip]
+    (last,) = in_order([attend_call(s.projected_last, s.earlier_last)])
+    s.attended = [*s.attended, last]
+    s.mixed = [a[0] for a in s.attended]
+    s.resid, s.mid = close_attention(s.x_low, s.mixed, s.out_blocks, s.mlp_gains)
+    s.end("out_chips", "projected_last", "earlier_last", "cotangent")
+
+    s.mid_near = near(s.mid)
+    s.grad_y_came = grad_y_sent
+    s.end()
+
+    s.mid_far = far(*s.mid_near)
+    grad_y = jnp.concatenate(in_turn(s.grad_y_came), 0)
+    s.grad_y = jnp.where(s.valid > 0, grad_y, jnp.zeros_like(grad_y))
+    s.grad_y_near = near(s.grad_y)
+    s.ffn_own = ffn_own
+    s.end("grad_y_came")
+
+    s.grad_y_far = far(*s.grad_y_near)
+    s.end()
+
+    s.mids = [s.mid, *s.mid_near, *s.mid_far]
+    s.grads_y = [s.grad_y, *s.grad_y_near, *s.grad_y_far]
+    s.ffn_other = across(s.ffn_own, CORE)
+    units = s.ffn_own.shape[1] // 3
+    s.hidden_own = hidden_units(s.mids, s.grads_y, s.ffn_own)
+    s.end("mid", "mid_near", "mid_far", "grad_y_near", "grad_y_far")
+
+    def hidden_pairs(own, other, first, last):
+        return [
+            (hidden[i], weights, at)
+            for hidden, weights in ((own, s.ffn_own), (other, s.ffn_other))
+            for at, i in enumerate(range(first, last))
+        ]
+
+    def gate_up_pairs(other):
+        return hidden_pairs(s.hidden_own, other, 1, 3)
+
+    def down_pairs():
+        return [(s.hidden_own[0], s.ffn_own, 2), (s.hidden_other[0], s.ffn_other, 2)]
+
+    def from_hidden_call(pairs, eighths):
+        return (
+            lambda first: from_hidden([(first, *pairs[0][1:]), *pairs[1:]], eighths),
+            pairs[0][0],
         )
-        to_y, one_tail, own_tail = row_outer(
-            [left], [[even[2], even[3]], [even[1]], [even[0]]], 4, 4, came, (2, 3, 1, 0)
+
+    def outer_call(lefts, rights, *added):
+        return lambda first: row_outer(lefts, [[first, *rights[1:]]], 0, 8, *added)[0], rights[0]
+
+    to_plane, rest_of_plane = (2, 6, 5, 7), (3, 4, 0, 1)
+    s.hidden_other = hidden_units(s.mids, s.grads_y, s.ffn_other)
+    s.mid_sent = from_hidden(gate_up_pairs(s.hidden_other), to_plane)
+    s.end()
+
+    def send_near(sent):
+        return across(sent[0], ACROSS_X), across(sent[1], ACROSS_Y)
+
+    def send_far(came, rest, split):
+        one_tail, two_head = rest
+        return (
+            across(rounded_sum(one_tail, split(came[1])[1]), ACROSS_X),
+            across(rounded_sum(two_head, split(came[0])[1]), ACROSS_Y),
         )
-        own = links.total(
-            to_x, to_y, lambda a: (a[:, :columns], a[:, columns:]),
-            own_head, own_tail, two_head, one_tail,
+
+    def total(came, came_far, own, split):
+        head, tail = own
+        full_sum = lambda *parts: sum(part.astype(full) for part in parts)
+        return jnp.concatenate(
+            [
+                full_sum(head, split(came[0])[0], came_far[1]),
+                full_sum(tail, split(came[1])[0], came_far[0]),
+            ],
+            0,
         )
-        return ring_sum(jnp.split(own, shards, 0), low).astype(low)
-
-    out_total = block_total(
-        rolled(resid_low),
-        [m[:, :head_columns] for m in mixed],
-        [m[:, head_columns:] for m in mixed],
-    )
+
+    by_rows = lambda a: jnp.split(a, 2, 0)
+    by_columns = lambda a: jnp.split(a, 2, 1)
+
+    s.mid_came = send_near(s.mid_sent)
+    s.mid_rest, s.down_outer, s.gate_up_outer = in_order(
+        [
+            from_hidden_call(gate_up_pairs(s.hidden_other), rest_of_plane),
+            outer_call(s.grads_y, s.hidden_other[:1]),
+            outer_call(s.mids, s.hidden_other[1:]),
+        ]
+    )
+    s.end("mid_sent")
+
+    s.mid_came_far = send_far(s.mid_came, by_rows(s.mid_rest[0]), by_rows)
+    s.down_came = across(s.down_outer, CORE)
+    s.gate_up_came = across(s.gate_up_outer, CORE)
+    s.mlp_sent, s.mlp_rest = in_order(
+        [
+            from_hidden_call(down_pairs(), to_plane),
+            from_hidden_call(down_pairs(), rest_of_plane),
+        ]
+    )
+    s.end("down_outer", "gate_up_outer")
+
+    mlp_came = send_near(s.mlp_sent)
+    grad_mid = total(s.mid_came, s.mid_came_far, by_rows(s.mid_rest[1]), by_rows)
+    inverse_mid = lax.rsqrt(jnp.mean(s.resid * s.resid, -1, keepdims=True) + EPS)
+    mid_unit = s.resid * inverse_mid
+    s.mlp_gain_part = jnp.sum(mid_unit * grad_mid, 0)
+    s.grad_resid = s.grad_y.astype(full) + norm_back(
+        mid_unit, inverse_mid, grad_mid * s.mlp_gains
+    )
+    s.resid_low = s.grad_resid.astype(low)
+    s.resid_rolled = rolled(s.resid_low)
+    (s.down_mine,) = in_order([outer_call(s.grads_y, s.hidden_own[:1], s.down_came)])
+    s.end("mid_came", "mid_came_far", "mid_rest", "down_came")
+
+    def back_call(i):
+        raw, query, own_pair = s.projected[i]
+        return (
+            lambda query, *rest: attend_back(s.info, query, *rest),
+            query, s.earlier[i], own_pair, s.attended[i][1], s.resid_low,
+            *s.out_blocks[2 * i : 2 * i + 2], raw, s.cosine, s.sine, s.head_gains[:1],
+        )
+
+    def finish_call(i):
+        return (
+            finish, s[f"back{i}"][0], s[f"back{i}"][1], s[f"returned{i}"], s.projected[i][0],
+            s.cosine, s.sine, s.head_gains[1:],
+        )
+
+    def give_back(*chips):
+        for i in chips:
+            s[f"returned{i}"] = lax.ppermute(s[f"back{i}"][2], "rep", downward)
+
+    def odd_call(left, blocks):
+        return lambda first: row_outer([first], [blocks], 0, 8)[0], left
+
+    def head_call(left, blocks, came):
+        groups = [[blocks[1], blocks[3]], [blocks[2]], [blocks[0]]]
+        return lambda first: row_outer([first], groups, 0, 4, came, (1, 3, 2, 0)), left
+
+    def tail_call(left, blocks, came):
+        groups = [[blocks[2], blocks[3]], [blocks[1]], [blocks[0]]]
+        return lambda first: row_outer([first], groups, 4, 4, came, (2, 3, 1, 0)), left
+
+    down_total = lax.psum_scatter(s.down_mine, "shard", scatter_dimension=0, tiled=True)
+    mixed_even = [m[:, :head_columns] for m in s.mixed]
+    mixed_odd = [m[:, head_columns:] for m in s.mixed]
+    s.out_odd, s.back3 = in_order([odd_call(s.resid_rolled, mixed_odd), back_call(3)])
+    s.mlp_came = mlp_came
+    s.end("down_mine")
+
+    s.mlp_came_far = send_far(s.mlp_came, by_rows(s.mlp_rest[0]), by_rows)
+    s.out_came = across(s.out_odd, CORE)
+    give_back(3)
+    s.back1, s.back2 = in_order([back_call(1), back_call(2)])
+    s.end("out_odd", "mlp_sent")
+
+    give_back(1, 2)
+    mlp_out = total(s.mlp_came, s.mlp_came_far, by_rows(s.mlp_rest[1]), by_rows)
+    s.output = (s.valid * (s.resid + mlp_out)).astype(low)
+    s.out_head, s.out_tail, s.back0, s.finished3 = in_order(
+        [
+            head_call(s.resid_rolled, mixed_even, s.out_came),
+            tail_call(s.resid_rolled, mixed_even, s.out_came),
+            back_call(0),
+            finish_call(3),
+        ]
+    )
+    s.end("mlp_came", "mlp_came_far", "mlp_rest", "out_came", "resid")
+
+    output_sent = from_sequences_send(s.output)
+    s.out_near = send_near((s.out_head[0], s.out_tail[0]))
+    give_back(0)
+    s.gate_up_mine, s.finished1, s.finished2 = in_order(
+        [
+            outer_call(s.mids, s.hidden_own[1:], s.gate_up_came),
+            finish_call(1),
+            finish_call(2),
+        ]
+    )
+    s.end("gate_up_came", "hidden_own", "hidden_other", "output")
+
+    gate_up_total = lax.psum_scatter(s.gate_up_mine, "shard", scatter_dimension=0, tiled=True)
+    s.out_far = send_far(s.out_near, (s.out_tail[1], s.out_head[1]), by_columns)
+    ((s.finished0),) = in_order([finish_call(0)])
+    s.finished = [s.finished0, s.finished1, s.finished2, s.finished3]
+    (s.qkv_odd,) = in_order([odd_call(s.normed, [f[1] for f in s.finished])])
+    s.down_total = down_total
+    s.output_came = output_sent
+    s.end("gate_up_mine", "finished0", "finished1", "finished2", "finished3")
+
+    s.qkv_came = across(s.qkv_odd, CORE)
+    s.down_near = near(s.down_total)
+    out_sum = total(s.out_near, s.out_far, (s.out_head[2], s.out_tail[2]), by_columns)
+    s.out_chunks = jnp.split(out_sum.astype(low), shards, 0)
+    s.out_ring = ring_sum_first(s.out_chunks)
+    grad_in = rolled(
+        back_to_rows(
+            [part for f in s.finished for part in f[:2]],
+            [
+                pair
+                for i, block in enumerate(zip((s.came, *s.came_near), s.came_other))
+                for pair in ((s.own_blocks[2 * i], block[0]), (s.own_blocks[2 * i + 1], block[1]))
+            ]
+            + [(s.own_blocks[6 + i], s.came_last[i]) for i in range(2)],
+        )
+    )
+    x_unit = s.x_low.astype(full) * s.inverse_in
+    s.attn_gain_part = jnp.sum(x_unit * grad_in, 0)
+    s.grad_tokens = (
+        s.grad_resid + norm_back(x_unit, s.inverse_in, grad_in * s.attn_gains)
+    ).astype(low)
+    s.end("qkv_odd", "out_near", "out_far", "out_head", "out_tail")
+
+    s.down_far = far(*s.down_near)
+    s.out_ring_last = around(rounded_sum(s.out_chunks[3], s.out_ring[0]), 1)
+    grad_tokens_sent = from_sequences_send(s.grad_tokens)
+    s.qkv_head, s.qkv_tail = in_order(
+        [
+            head_call(s.normed, [f[0] for f in s.finished], s.qkv_came),
+            tail_call(s.normed, [f[0] for f in s.finished], s.qkv_came),
+        ]
+    )
+    s.gain_parts = jnp.concatenate(
+        [
+            s.attn_gain_part,
+            s.mlp_gain_part,
+            sum(s[f"back{i}"][3] for i in range(4))[0],
+            sum(f[2] for f in s.finished)[0],
+        ]
+    )
+    s.end("qkv_came", "grad_tokens", "finished")
+
     my_group = me.astype(jnp.int32)[None]
-    grad_down_total = whole_columns(my_group, *spread_blocks(links, down_total), 0, units)
-    qkv_total = block_total(
-        normed, [finished[i][0] for i in range(4)], [finished[i][1] for i in range(4)]
-    )
-    gate_up_spread = spread_blocks(links, gate_up_total)
-    grad_gate_total = whole_columns(my_group, *gate_up_spread, 0, units)
-    grad_up_total = whole_columns(my_group, *gate_up_spread, units, units)
-    out_spread = spread_blocks(links, out_total)
-    grad_out_total = whole_columns(my_group, *out_spread, 0, head_columns)
-    qkv_spread = spread_blocks(links, qkv_total)
-    grad_query_total = whole_columns(my_group, *qkv_spread, 0, head_columns)
-    grad_key_total = whole_columns(my_group, *qkv_spread, head_columns, head_dim)
-    grad_value_total = whole_columns(my_group, *qkv_spread, 3 * head_dim, head_dim)
-
-    step = width // shards
-    grad_in = rolled(
-        back_to_rows([part for i in range(4) for part in finished[i][:2]], qkv_weights)
-    )
-    grad_tokens = from_sequences(
-        (grad_resid + norm_back(x_unit, inverse_in, grad_in * attn_gains)).astype(low)
-    )
-    attn_gain_part = jnp.sum(x_unit * grad_in, 0)
-
-    parts = everywhere_sum(
-        jnp.concatenate(
-            [attn_gain_part, mlp_gain_part, query_gain_part[0], key_gain_part[0]]
-        )
-    )
-    for by in (1, 2):
-        parts = parts + lax.ppermute(parts, "shard", [(i, i ^ by) for i in range(shards)])
+
+    def whole(spread, widths):
+        return whole_columns(my_group, *spread, widths)
+
+    s.qkv_near = send_near((s.qkv_head[0], s.qkv_tail[0]))
+    s.down_own = jnp.concatenate([s.down_total, *s.down_near, *s.down_far], 0)
+    s.down_other = across(s.down_own, CORE)
+    s.out_total = rounded_sum(s.out_chunks[0], s.out_ring[1], s.out_ring_last)
+    s.gain_came = across(s.gain_parts, CORE)
+    s.tokens_came = grad_tokens_sent
+    s.end("out_chunks", "out_ring", "out_ring_last")
+
+    s.qkv_far = send_far(s.qkv_near, (s.qkv_tail[1], s.qkv_head[1]), by_columns)
+    s.gain_parts = s.gain_parts + s.gain_came
+    s.gain_came = across(s.gain_parts, ACROSS_X)
+    s.whole_down = whole((s.down_own, s.down_other), (units,))
+    s.gate_up_total = gate_up_total
+    s.end("down_own", "down_other")
+
+    qkv_sum = total(s.qkv_near, s.qkv_far, (s.qkv_head[2], s.qkv_tail[2]), by_columns)
+    s.qkv_chunks = jnp.split(qkv_sum.astype(low), shards, 0)
+    s.qkv_ring = ring_sum_first(s.qkv_chunks)
+    s.gate_up_near = near(s.gate_up_total)
+    s.gain_parts = s.gain_parts + s.gain_came
+    s.gain_came = across(s.gain_parts, ACROSS_Y)
+    s.end("qkv_near", "qkv_far", "qkv_head", "qkv_tail")
+
+    s.qkv_ring_last = around(rounded_sum(s.qkv_chunks[3], s.qkv_ring[0]), 1)
+    s.gate_up_far = far(*s.gate_up_near)
+    s.gain_parts = s.gain_parts + s.gain_came
+    s.gain_came = lax.ppermute(s.gain_parts, "shard", [(i, i ^ 1) for i in range(shards)])
+    s.end()
+
+    qkv_total = rounded_sum(s.qkv_chunks[0], s.qkv_ring[1], s.qkv_ring_last)
+    s.attn_total = jnp.concatenate([qkv_total, s.out_total], 1)
+    s.attn_near = near(s.attn_total)
+    s.gate_up_own = jnp.concatenate([s.gate_up_total, *s.gate_up_near, *s.gate_up_far], 0)
+    s.gate_up_other = across(s.gate_up_own, CORE)
+    s.gain_parts = s.gain_parts + s.gain_came
+    s.gain_came = lax.ppermute(s.gain_parts, "shard", [(i, i ^ 2) for i in range(shards)])
+    s.end("qkv_chunks", "qkv_ring", "qkv_ring_last", "gate_up_near", "gate_up_far")
+
+    s.attn_far = far(*s.attn_near)
+    s.whole_gate_up = whole((s.gate_up_own, s.gate_up_other), (units, units))
+    s.end("gate_up_own", "gate_up_other")
+
+    s.attn_own = jnp.concatenate([s.attn_total, *s.attn_near, *s.attn_far], 0)
+    s.attn_other = across(s.attn_own, CORE)
+    s.end()
+
+    whole_query, whole_key, whole_value, whole_out = whole(
+        (s.attn_own, s.attn_other), (head_columns, head_dim, head_dim, head_columns)
+    )
+    gain_sums = s.gain_parts + s.gain_came
     wide = lax.dynamic_slice_in_dim(
-        parts[: 2 * width].reshape(2, width), shard_at * step, step, 1
-    )
-    narrow = parts[2 * width :]
+        gain_sums[: 2 * width].reshape(2, width), shard_at * piece, piece, 1
+    )
+    narrow = gain_sums[2 * width :]
     return (
-        output,
-        grad_tokens,
+        jnp.stack(in_turn(s.output_came)),
+        jnp.stack(in_turn(s.tokens_came)),
         wide[0],
-        grad_query_total,
-        grad_key_total,
-        grad_value_total,
+        whole_query,
+        whole_key,
+        whole_value,
         narrow[:head_dim],
         narrow[head_dim:],
-        grad_out_total,
+        whole_out,
         wide[1],
-        grad_gate_total,
-        grad_up_total,
-        grad_down_total,
+        *s.whole_gate_up,
+        *s.whole_down,
     )
 
 

time: 1390 us -> 1140 us (0.82)
  waiting for transfers between devices: 586 us -> 382 us
  other arithmetic: 78.6 us -> 61.2 us
  Pallas kernels: 443 us -> 427 us
    ppermute x77 -> x64, waiting for transfers between devices: 359 us -> 125 us  [across(): return lax.ppermute(x, 'rep', [(i, i ^ mask) for i in range(count)])]
    ppermute x18, waiting for transfers between devices: 44.5 us -> 202 us  [the longest x4 123 us: to_sequences_send(): lax.ppermute(lax.dynamic_index_in_dim(x, turn ^ odd, 0, keepdims=False),...]
    all_gather x2, waiting for transfers between devices: 90.4 us -> 0.01 us  [the longest x1 0.01 us: on_device_block(): out_own = lax.all_gather(s.out_block, 'shard', axis=0, tiled=True)]
    ppermute x12 -> x9, waiting for transfers between devices: 91.9 us -> 54.9 us  [around(): lax.ppermute(x, 'shard', [(i, (i + by) % count) for i in range(count)])]
    pallas_call x7 -> x3, Pallas kernels: 56.9 us -> 39.8 us  [whole_columns(): pl.pallas_call(body, grid_spec=pltpu.PrefetchScalarGridSpec(num_scalar_pr...]
    ppermute x77 -> x64, starting transfers between devices: 88.4 us -> 80.4 us  [across(): return lax.ppermute(x, 'rep', [(i, i ^ mask) for i in range(count)])]
    unnamed x254 -> x238, local copies, waits for them, and re-layouts: 28.9 us -> 25.1 us
    ppermute x12 -> x9, starting transfers between devices: 42.7 us -> 41.4 us  [around(): lax.ppermute(x, 'shard', [(i, (i + by) % count) for i in range(count)])]
  transfers between devices with their start and end apart: 111 -> 95, of which waited for: 36 -> 31; matrix products, arithmetic and copies ran while one was open for 9% -> 8% of each run, Pallas kernels for 23% -> 33%
where the time goes in v5:
time: 1140 us; the launch traced here: 1130 us
  Pallas kernels  427 us (37%)
  waiting for transfers between devices  382 us (34%)
  starting transfers between devices  172 us (15%)
  local copies, waits for them, and re-layouts  67.1 us (6%)
  other arithmetic  61.2 us (5%)
  between operations  15.8 us (1%)
    pallas_call x16, Pallas kernels, call(): pl.pallas_call(body, grid=(1,), out_shape=outs, in_specs=in_specs, out_sp...  133 us
    ppermute x64, waiting for transfers between devices, across(): return lax.ppermute(x, 'rep', [(i, i ^ mask) for i in range(count)])  125 us
    ppermute x4, waiting for transfers between devices, to_sequences_send(): lax.ppermute(lax.dynamic_index_in_dim(x, turn ^ odd, 0, keepdims=False),...  123 us
    pallas_call x10, Pallas kernels, row_outer(): pl.pallas_call(body, grid=(tiles,), out_shape=[jax.ShapeDtypeStruct((tile...  107 us
    ppermute x64, starting transfers between devices, across(): return lax.ppermute(x, 'rep', [(i, i ^ mask) for i in range(count)])  80.4 us
    ppermute x4, waiting for transfers between devices, from_sequences_send(): lax.ppermute(lax.dynamic_index_in_dim(x, turn ^ odd, 0, keepdims=False),...  66.8 us
    pallas_call x2, Pallas kernels, hidden_units(): pl.pallas_call(body, grid=(3,), out_shape=[jax.ShapeDtypeStruct((rows, un...  59.9 us
    pallas_call x4, Pallas kernels, from_hidden(): pl.pallas_call(body, grid=(4,), out_shape=[jax.ShapeDtypeStruct((2 * rows...  59.6 us
  transfers between devices with their start and end apart: 95, of which 31 were waited for; matrix products, arithmetic and copies ran while one was open for 8% of the time, Pallas kernels for 33%

profile of v5, /device:TPU:0, one launch (start us, length us, event | category | flops | bytes accessed | tf_op | source)
XLA Modules:
  0.0 1125.1 jit_solution(874359751493541689)
XLA Ops:
  32.5 10.1 collective-permute-done.1
  43.7 14.5 %collective-permute-done.3 = bf16[528,512]{1,0:T(8,128)(2,1)S(1)} collective-permute-done((bf16[528,512]{1,0:T(8,128)(2,1)}, bf16[528,512]{1,0:T(8,128)(2,1)S(1)}, u32[]{:S(2)}, u32[]{:S(2)}) %collective-permute-start.3) | collective-permute-done | bytes 540704 | tf_op jit(solution)/shard_map/ppermute | solution.py:323
  73.6 49.1 %collective-permute-done.7 = bf16[256,2048]{1,0:T(8,128)(2,1)S(1)} collective-permute-done((bf16[256,2048]{1,0:T(8,128)(2,1)}, bf16[256,2048]{1,0:T(8,128)(2,1)S(1)}, u32[]{:S(2)}, u32[]{:S(2)}) %collective-permute-start.7) | collective-permute-done | bytes 1048608 | tf_op jit(solution)/shard_map/ppermute | solution.py:386
  137.9 10.3 collective-permute-done.8
  232.5 11.7 %close_attention.1 = (f32[512,2048]{1,0:T(8,128)}, bf16[512,2048]{1,0:T(8,128)(2,1)}) custom-call(bf16[512,2048]{1,0:T(8,128)(2,1)} %pad_maximum_fusion.3.x, bf16[512,512]{1,0:T(8,128)(2,1)} %get-tuple-element.2336.refs_0_, bf16[512,512]{1,0:T(8,128)(2,1)} %get-tuple-element.2337.refs_1_, bf16[512,512]{1,0:T(8,128)(2,1)} %get-tuple-element.2338.refs_2_, ...), custom_call_target="tpu_custom_call" | custom-call | flops 1 | bytes 1 | tf_op jit(solution)/shard_map/close_attention/pallas_call | solution.py:780
  248.7 10.9 collective-permute-start.27
  259.6 74.2 %collective-permute-done.27 = bf16[256,2048]{1,0:T(8,128)(2,1)S(1)} collective-permute-done((bf16[256,2048]{1,0:T(8,128)(2,1)S(1)}, bf16[256,2048]{1,0:T(8,128)(2,1)S(1)}, u32[]{:S(2)}, u32[]{:S(2)}) %collective-permute-start.27) | collective-permute-done | bytes 1048608 | tf_op jit(solution)/shard_map/ppermute | solution.py:386
  338.8 59.3 %collective-permute-done.32.refs_3_ = bf16[256,2048]{1,0:T(8,128)(2,1)S(1)} collective-permute-done((bf16[256,2048]{1,0:T(8,128)(2,1)S(1)}, bf16[256,2048]{1,0:T(8,128)(2,1)S(1)}, u32[]{:S(2)}, u32[]{:S(2)}) %collective-permute-start.32) | collective-permute-done | bytes 1048608 | tf_op jit(solution)/shard_map/ppermute | solution.py:318
  406.3 15.2 %collective-permute-done.34.refs_8_.refs_3_ = bf16[256,2048]{1,0:T(8,128)(2,1)S(1)} collective-permute-done((bf16[256,2048]{1,0:T(8,128)(2,1)S(1)}, bf16[256,2048]{1,0:T(8,128)(2,1)S(1)}, u32[]{:S(2)}, u32[]{:S(2)}) %collective-permute-start.34) | collective-permute-done | bytes 1048608 | tf_op jit(solution)/shard_map/ppermute | solution.py:318
  430.2 30.0 %hidden_units.2 = (bf16[2048,768]{1,0:T(8,128)(2,1)}, bf16[2048,768]{1,0:T(8,128)(2,1)}, bf16[2048,768]{1,0:T(8,128)(2,1)}) custom-call(bf16[512,2048]{1,0:T(8,128)(2,1)} %get-tuple-element.2586.refs_0_, bf16[512,2048]{1,0:T(8,128)(2,1)} %copy-done.9, bf16[512,2048]{1,0:T(8,128)(2,1)} %copy-done.10, bf16[256,2048]{1,0:T(8,128)(2,1)} %copy-done.20, ...), custom_call_target="tpu_custom_call" | custom-call | flops 1 | bytes 1 | tf_op jit(solution)/shard_map/hidden_units/pallas_call | solution.py:650
  460.2 29.9 %hidden_units.3 = (bf16[2048,768]{1,0:T(8,128)(2,1)}, bf16[2048,768]{1,0:T(8,128)(2,1)}, bf16[2048,768]{1,0:T(8,128)(2,1)}) custom-call(bf16[512,2048]{1,0:T(8,128)(2,1)} %get-tuple-element.2586.refs_0_, bf16[512,2048]{1,0:T(8,128)(2,1)} %copy-done.9, bf16[512,2048]{1,0:T(8,128)(2,1)} %copy-done.10, bf16[256,2048]{1,0:T(8,128)(2,1)} %copy-done.20, ...), custom_call_target="tpu_custom_call" | custom-call | flops 1 | bytes 1 | tf_op jit(solution)/shard_map/hidden_units/pallas_call | solution.py:650
  490.1 19.2 %from_hidden.4 = (bf16[512,2048]{1,0:T(8,128)(2,1)}, bf16[512,2048]{1,0:T(8,128)(2,1)}) custom-call(bf16[2048,768]{1,0:T(8,128)(2,1)} %get-tuple-element.2591.refs_0_.refs_1_.refs_2_.refs_3_.refs_5_, bf16[2048,768]{1,0:T(8,128)(2,1)} %get-tuple-element.2591.refs_0_.refs_1_.refs_2_.refs_3_.refs_5_, ...), custom_call_target="tpu_custom_call" | custom-call | flops 1 | bytes 1 | tf_op jit(solution)/shard_map/from_hidden/pallas_call | solution.py:689
  511.7 18.9 %from_hidden.5 = (bf16[512,2048]{1,0:T(8,128)(2,1)}, bf16[512,2048]{1,0:T(8,128)(2,1)}) custom-call(bf16[2048,768]{1,0:T(8,128)(2,1)} %get-tuple-element.2591.refs_0_.refs_1_.refs_2_.refs_3_.refs_5_, bf16[2048,768]{1,0:T(8,128)(2,1)} %get-tuple-element.2591.refs_0_.refs_1_.refs_2_.refs_3_.refs_5_, ...), custom_call_target="tpu_custom_call" | custom-call | flops 1 | bytes 1 | tf_op jit(solution)/shard_map/from_hidden/pallas_call | solution.py:689
  530.6 12.6 %row_outer.10 = bf16[2048,768]{1,0:T(8,128)(2,1)} custom-call(bf16[512,2048]{1,0:T(8,128)(2,1)} %copy-done.5, bf16[512,2048]{1,0:T(8,128)(2,1)} %copy-done.11, bf16[512,2048]{1,0:T(8,128)(2,1)} %collective-permute-done.31.refs_7_.refs_2_, bf16[256,2048]{1,0:T(8,128)(2,1)} %copy-done.22, bf16[256,2048]{1,0:T(8,128)(2,1)} %copy-done.23, ...), custom_call_target="tpu_custom_call" | custom-call | flops 6442450944 | bytes 11534336 | tf_op jit(solution)/shard_map/row_outer/pallas_call | solution.py:732
  543.3 19.4 %row_outer.11 = bf16[2048,1536]{1,0:T(8,128)(2,1)} custom-call(bf16[512,2048]{1,0:T(8,128)(2,1)} %get-tuple-element.2586.refs_0_, bf16[512,2048]{1,0:T(8,128)(2,1)} %copy-done.9, bf16[512,2048]{1,0:T(8,128)(2,1)} %copy-done.10, bf16[256,2048]{1,0:T(8,128)(2,1)} %copy-done.20, bf16[256,2048]{1,0:T(8,128)(2,1)} %copy-done.21, ...), custom_call_target="tpu_custom_call" | custom-call | flops 12884901888 | bytes 14680064 | tf_op jit(solution)/shard_map/row_outer/pallas_call | solution.py:732
  567.5 10.6 from_hidden.6
  578.1 10.8 from_hidden.7
  608.0 13.3 %row_outer.12 = bf16[2048,768]{1,0:T(8,128)(2,1)} custom-call(bf16[512,2048]{1,0:T(8,128)(2,1)} %copy-done.5, bf16[512,2048]{1,0:T(8,128)(2,1)} %copy-done.11, bf16[512,2048]{1,0:T(8,128)(2,1)} %collective-permute-done.31.refs_7_.refs_2_, bf16[256,2048]{1,0:T(8,128)(2,1)} %copy-done.22, bf16[256,2048]{1,0:T(8,128)(2,1)} %copy-done.23, ...), custom_call_target="tpu_custom_call" | custom-call | flops 6442450944 | bytes 11534336 | tf_op jit(solution)/shard_map/row_outer/pallas_call | solution.py:732
  633.4 14.6 %attend_back.4 = (bf16[512,512]{1,0:T(8,128)(2,1)}, f32[512,512]{1,0:T(8,128)}, bf16[512,512]{1,0:T(8,128)(2,1)}, f32[1,128]{1,0:T(1,128)}) custom-call(s32[2]{0:T(128)} %pad_add_fusion.info, bf16[512,512]{1,0:T(8,128)(2,1)} %get-tuple-element.2340.query, bf16[512,512]{1,0:T(8,128)(2,1)} %copy-done.39, bf16[512,512]{1,0:T(8,128)(2,1)} %get-tuple-element.2342.own, ...), custom_call_target="tpu_custom_call" | custom-call | flops 1 | bytes 1 | tf_op jit(solution)/shard_map/attend_back/pallas_call | solution.py:610
  655.0 14.9 %attend_back.5 = (bf16[512,512]{1,0:T(8,128)(2,1)}, f32[512,512]{1,0:T(8,128)}, bf16[512,512]{1,0:T(8,128)(2,1)}, f32[1,128]{1,0:T(1,128)}) custom-call(s32[2]{0:T(128)} %pad_add_fusion.info, bf16[512,512]{1,0:T(8,128)(2,1)} %get-tuple-element.2410.query, bf16[512,512]{1,0:T(8,128)(2,1)} %copy-done.38, bf16[512,512]{1,0:T(8,128)(2,1)} %get-tuple-element.2412.own, ...), custom_call_target="tpu_custom_call" | custom-call | flops 1 | bytes 1 | tf_op jit(solution)/shard_map/attend_back/pallas_call | solution.py:610
  669.9 14.9 %attend_back.6 = (bf16[512,512]{1,0:T(8,128)(2,1)}, f32[512,512]{1,0:T(8,128)}, bf16[512,512]{1,0:T(8,128)(2,1)}, f32[1,128]{1,0:T(1,128)}) custom-call(s32[2]{0:T(128)} %pad_add_fusion.info, bf16[512,512]{1,0:T(8,128)(2,1)} %get-tuple-element.2425.query, bf16[512,512]{1,0:T(8,128)(2,1)} %copy-done.37, bf16[512,512]{1,0:T(8,128)(2,1)} %get-tuple-element.2427.own, ...), custom_call_target="tpu_custom_call" | custom-call | flops 1 | bytes 1 | tf_op jit(solution)/shard_map/attend_back/pallas_call | solution.py:610
  695.8 14.7 %attend_back.7 = (bf16[512,512]{1,0:T(8,128)(2,1)}, f32[512,512]{1,0:T(8,128)}, bf16[512,512]{1,0:T(8,128)(2,1)}, f32[1,128]{1,0:T(1,128)}) custom-call(s32[2]{0:T(128)} %pad_add_fusion.info, bf16[512,512]{1,0:T(8,128)(2,1)} %get-tuple-element.2492.query, bf16[512,512]{1,0:T(8,128)(2,1)} %copy-done.35, bf16[512,512]{1,0:T(8,128)(2,1)} %get-tuple-element.2494.own, ...), custom_call_target="tpu_custom_call" | custom-call | flops 1 | bytes 1 | tf_op jit(solution)/shard_map/attend_back/pallas_call | solution.py:610
  725.7 19.7 %row_outer.16 = bf16[2048,1536]{1,0:T(8,128)(2,1)} custom-call(bf16[512,2048]{1,0:T(8,128)(2,1)} %get-tuple-element.2586.refs_0_, bf16[512,2048]{1,0:T(8,128)(2,1)} %copy-done.9, bf16[512,2048]{1,0:T(8,128)(2,1)} %copy-done.10, bf16[256,2048]{1,0:T(8,128)(2,1)} %copy-done.20, bf16[256,2048]{1,0:T(8,128)(2,1)} %copy-done.21, ...), custom_call_target="tpu_custom_call" | custom-call | flops 12884901888 | bytes 14680064 | tf_op jit(solution)/shard_map/row_outer/pallas_call | solution.py:732
  782.0 15.9 %collective-permute-start.62 = (bf16[2048,2048]{1,0:T(8,128)(2,1)}, bf16[2048,2048]{1,0:T(8,128)(2,1)}, u32[]{:S(2)}, u32[]{:S(2)}) collective-permute-start(bf16[2048,2048]{1,0:T(8,128)(2,1)} %row_outer.17), channel_id=1, source_target_pairs={{0,4},{4,0},{8,12},{12,8},{16,20},{20,16},{24,28},{28,24},{1,5},{5... | collective-permute-start | bytes 25165832 | tf_op jit(solution)/shard_map/ppermute | solution.py:318
  800.1 15.8 %back_to_rows.1 = f32[512,2048]{1,0:T(8,128)} custom-call(bf16[512,512]{1,0:T(8,128)(2,1)} %get-tuple-element.2755.refs_0_.refs_4_, bf16[512,512]{1,0:T(8,128)(2,1)} %get-tuple-element.2687.refs_1_, bf16[512,512]{1,0:T(8,128)(2,1)} %get-tuple-element.2752.refs_2_.refs_1_.refs_3_, bf16[512,512]{1,0:T(8,128)(2,1)} %get-tuple-element.2689.refs_2_.refs_3_, ...), custom_call_target="tpu_custom_call" | custom-call | flops 1 | bytes 1 | tf_op jit(solution)/shard_map/back_to_rows/pallas_call | solution.py:833
  835.2 10.6 collective-permute-done.60
  845.8 11.5 %collective-permute-done.61 = bf16[512,256]{1,0:T(8,128)(2,1)S(1)} collective-permute-done((bf16[512,256]{1,0:T(8,128)(2,1)S(1)}, bf16[512,256]{1,0:T(8,128)(2,1)S(1)}, u32[]{:S(2)}, u32[]{:S(2)}) %collective-permute-start.61) | collective-permute-done | bytes 262176 | tf_op jit(solution)/shard_map/ppermute | solution.py:323
  890.7 66.8 %collective-permute-done.71 = bf16[256,2048]{1,0:T(8,128)(2,1)S(1)} collective-permute-done((bf16[256,2048]{1,0:T(8,128)(2,1)S(1)}, bf16[256,2048]{1,0:T(8,128)(2,1)S(1)}, u32[]{:S(2)}, u32[]{:S(2)}) %collective-permute-start.71) | collective-permute-done | bytes 1048608 | tf_op jit(solution)/shard_map/ppermute | solution.py:399
  965.1 11.0 whole_columns.3
  989.5 17.2 %collective-permute-start.79 = (bf16[512,512]{1,0:T(8,128)(2,1)S(1)}, bf16[512,512]{1,0:T(8,128)(2,1)S(1)}, u32[]{:S(2)}, u32[]{:S(2)}) collective-permute-start(bf16[512,512]{1,0:T(8,128)(2,1)S(1)} %get-tuple-element.2939), channel_id=1, source_target_pairs={{0,3},{1,0},{2,1},{3,2},{4,7},{5,4},{6,5},{7,6},{8,11},{9,8},{10,9... | collective-permute-start | bytes 1572872 | tf_op jit(solution)/shard_map/ppermute | solution.py:323
  1072.5 17.8 %whole_columns.4 = (f32[512,6144]{1,0:T(8,128)}, f32[512,6144]{1,0:T(8,128)}) custom-call(s32[1]{0:T(128)} %bitcast.22.me_ref, bf16[2048,1536]{1,0:T(8,128)(2,1)} %copy-done.12, bf16[2048,1536]{1,0:T(8,128)(2,1)} %copy-done.17), custom_call_target="tpu_custom_call" | custom-call | flops 1 | bytes 1 | tf_op jit(solution)/shard_map/whole_columns/pallas_call | solution.py:435
  1106.7 11.0 whole_columns.5
  (571 shorter events, 432.9 us)
Async XLA Ops:
  7.2 130.7 %all-gather.3.cloned.1.call-start = ((), (), s32[]{:S(2)}) async-start(), calls=%async_computation.2 | async-start | bytes 1310720 | tf_op jit(solution)/shard_map/all_gather | solution.py:893
  62.1 60.7 %collective-permute-start.4 = (bf16[1536,512]{1,0:T(8,128)(2,1)}, bf16[1536,512]{1,0:T(8,128)(2,1)}, u32[]{:S(2)}, u32[]{:S(2)}) collective-permute-start(bf16[1536,512]{1,0:T(8,128)(2,1)} %pad_maximum_fusion.8.came0.refs_9_), channel_id=1, source_target_pairs={{0,8},{4,12},{8,0},{12,4},{16,24},{20,28},{24,16},{28,20},{1,9},{5... | collective-permute-start | bytes 4718600 | tf_op jit(solution)/shard_map/ppermute | solution.py:318
  63.5 59.2 %collective-permute-start.5 = (bf16[1536,512]{1,0:T(8,128)(2,1)}, bf16[1536,512]{1,0:T(8,128)(2,1)}, u32[]{:S(2)}, u32[]{:S(2)}) collective-permute-start(bf16[1536,512]{1,0:T(8,128)(2,1)} %pad_maximum_fusion.8.came0.refs_9_), channel_id=1, source_target_pairs={{0,16},{4,20},{8,24},{12,28},{16,0},{20,4},{24,8},{28,12},{1,17},{... | collective-permute-start | bytes 4718600 | tf_op jit(solution)/shard_map/ppermute | solution.py:318
  69.2 53.5 %collective-permute-start.7 = (bf16[256,2048]{1,0:T(8,128)(2,1)}, bf16[256,2048]{1,0:T(8,128)(2,1)S(1)}, u32[]{:S(2)}, u32[]{:S(2)}) collective-permute-start(bf16[256,2048]{1,0:T(8,128)(2,1)} %get-tuple-element.2927), channel_id=1, source_target_pairs={{0,1},{1,0},{2,5},{3,4},{4,3},{5,2},{6,7},{7,6},{8,9},{9,8},{10,13... | collective-permute-start | bytes 3145736 | tf_op jit(solution)/shard_map/ppermute | solution.py:386
  72.1 327.5 %all-gather.5.cloned.1.call-start = ((), (), s32[]{:S(2)}) async-start(), calls=%async_computation.3 | async-start | bytes 11796480 | tf_op jit(solution)/shard_map/all_gather | solution.py:960
  148.4 633.5 %reduce-scatter.3.cloned.1.call-start = ((), (), s32[]{:S(2)}) async-start(), calls=%async_computation.4 | async-start | bytes 3932160 | tf_op jit(solution)/shard_map/reduce_scatter | solution.py:1135
  244.3 89.5 %collective-permute-start.28 = (bf16[512,2048]{1,0:T(8,128)(2,1)}, bf16[512,2048]{1,0:T(8,128)(2,1)S(1)}, u32[]{:S(2)}, u32[]{:S(2)}) collective-permute-start(bf16[512,2048]{1,0:T(8,128)(2,1)} %get-tuple-element.2586.refs_0_), channel_id=1, source_target_pairs={{0,8},{4,12},{8,0},{12,4},{16,24},{20,28},{24,16},{28,20},{1,9},{5... | collective-permute-start | bytes 6291464 | tf_op jit(solution)/shard_map/ppermute | solution.py:318
  245.7 88.1 %collective-permute-start.29 = (bf16[512,2048]{1,0:T(8,128)(2,1)}, bf16[512,2048]{1,0:T(8,128)(2,1)S(1)}, u32[]{:S(2)}, u32[]{:S(2)}) collective-permute-start(bf16[512,2048]{1,0:T(8,128)(2,1)} %get-tuple-element.2586.refs_0_), channel_id=1, source_target_pairs={{0,16},{4,20},{8,24},{12,28},{16,0},{20,4},{24,8},{28,12},{1,17},{... | collective-permute-start | bytes 6291464 | tf_op jit(solution)/shard_map/ppermute | solution.py:318
  248.7 85.1 %collective-permute-start.27 = (bf16[256,2048]{1,0:T(8,128)(2,1)S(1)}, bf16[256,2048]{1,0:T(8,128)(2,1)S(1)}, u32[]{:S(2)}, u32[]{:S(2)}) collective-permute-start(bf16[256,2048]{1,0:T(8,128)(2,1)S(1)} %get-tuple-element.2919), channel_id=1, source_target_pairs={{0,1},{1,0},{2,5},{3,4},{4,3},{5,2},{6,7},{7,6},{8,9},{9,8},{10,13... | collective-permute-start | bytes 3145736 | tf_op jit(solution)/shard_map/ppermute | solution.py:386
  334.4 63.8 %collective-permute-start.30 = (bf16[512,2048]{1,0:T(8,128)(2,1)S(1)}, bf16[512,2048]{1,0:T(8,128)(2,1)S(1)}, u32[]{:S(2)}, u32[]{:S(2)}) collective-permute-start(bf16[512,2048]{1,0:T(8,128)(2,1)S(1)} %maximum_select_fusion.refs_5_.refs_0_), channel_id=1, source_target_pairs={{0,8},{4,12},{8,0},{12,4},{16,24},{20,28},{24,16},{28,20},{1,9},{5... | collective-permute-start | bytes 6291464 | tf_op jit(solution)/shard_map/ppermute | solution.py:318
  335.1 64.5 %collective-permute-start.31 = (bf16[512,2048]{1,0:T(8,128)(2,1)S(1)}, bf16[512,2048]{1,0:T(8,128)(2,1)}, u32[]{:S(2)}, u32[]{:S(2)}) collective-permute-start(bf16[512,2048]{1,0:T(8,128)(2,1)S(1)} %maximum_select_fusion.refs_5_.refs_0_), channel_id=1, source_target_pairs={{0,16},{4,20},{8,24},{12,28},{16,0},{20,4},{24,8},{28,12},{1,17},{... | collective-permute-start | bytes 6291464 | tf_op jit(solution)/shard_map/ppermute | solution.py:318
  336.8 61.4 %collective-permute-start.32 = (bf16[256,2048]{1,0:T(8,128)(2,1)S(1)}, bf16[256,2048]{1,0:T(8,128)(2,1)S(1)}, u32[]{:S(2)}, u32[]{:S(2)}) collective-permute-start(bf16[256,2048]{1,0:T(8,128)(2,1)S(1)} %slice.156), channel_id=1, source_target_pairs={{0,16},{4,20},{8,24},{12,28},{16,0},{20,4},{24,8},{28,12},{1,17},{... | collective-permute-start | bytes 3145736 | tf_op jit(solution)/shard_map/ppermute | solution.py:318
  337.4 60.8 %collective-permute-start.33 = (bf16[256,2048]{1,0:T(8,128)(2,1)S(1)}, bf16[256,2048]{1,0:T(8,128)(2,1)S(1)}, u32[]{:S(2)}, u32[]{:S(2)}) collective-permute-start(bf16[256,2048]{1,0:T(8,128)(2,1)S(1)} %slice.157), channel_id=1, source_target_pairs={{0,8},{4,12},{8,0},{12,4},{16,24},{20,28},{24,16},{28,20},{1,9},{5... | collective-permute-start | bytes 3145736 | tf_op jit(solution)/shard_map/ppermute | solution.py:318
  423.5 36.7 %collective-permute-start.36 = (bf16[2048,2304]{1,0:T(8,128)(2,1)}, bf16[2048,2304]{1,0:T(8,128)(2,1)}, u32[]{:S(2)}, u32[]{:S(2)}) collective-permute-start(bf16[2048,2304]{1,0:T(8,128)(2,1)} %all-gather.5.cloned.1.call-done.refs_10_.refs_11_.refs_12_.refs_4_.refs_9_), channel_id=1, source_target_pairs={{0,4},{4,0},{8,12},{12,8},{16,20},{20,16},{24,28},{28,24},{1,5},{5... | collective-permute-start | bytes 28311560 | tf_op jit(solution)/shard_map/ppermute | solution.py:318
  509.3 53.4 %collective-permute-start.37 = (bf16[512,2048]{1,0:T(8,128)(2,1)}, bf16[512,2048]{1,0:T(8,128)(2,1)S(1)}, u32[]{:S(2)}, u32[]{:S(2)}) collective-permute-start(bf16[512,2048]{1,0:T(8,128)(2,1)} %get-tuple-element.2106), channel_id=1, source_target_pairs={{0,8},{4,12},{8,0},{12,4},{16,24},{20,28},{24,16},{28,20},{1,9},{5... | collective-permute-start | bytes 6291464 | tf_op jit(solution)/shard_map/ppermute | solution.py:318
  511.4 51.3 %collective-permute-start.38 = (bf16[512,2048]{1,0:T(8,128)(2,1)}, bf16[512,2048]{1,0:T(8,128)(2,1)S(1)}, u32[]{:S(2)}, u32[]{:S(2)}) collective-permute-start(bf16[512,2048]{1,0:T(8,128)(2,1)} %get-tuple-element.2107), channel_id=1, source_target_pairs={{0,16},{4,20},{8,24},{12,28},{16,0},{20,4},{24,8},{28,12},{1,17},{... | collective-permute-start | bytes 6291464 | tf_op jit(solution)/shard_map/ppermute | solution.py:318
  597.6 50.4 %collective-permute-start.43 = (bf16[512,2048]{1,0:T(8,128)(2,1)}, bf16[512,2048]{1,0:T(8,128)(2,1)}, u32[]{:S(2)}, u32[]{:S(2)}) collective-permute-start(bf16[512,2048]{1,0:T(8,128)(2,1)} %get-tuple-element.2294), channel_id=1, source_target_pairs={{0,8},{4,12},{8,0},{12,4},{16,24},{20,28},{24,16},{28,20},{1,9},{5... | collective-permute-start | bytes 6291464 | tf_op jit(solution)/shard_map/ppermute | solution.py:318
  599.3 48.7 %collective-permute-start.44 = (bf16[512,2048]{1,0:T(8,128)(2,1)}, bf16[512,2048]{1,0:T(8,128)(2,1)}, u32[]{:S(2)}, u32[]{:S(2)}) collective-permute-start(bf16[512,2048]{1,0:T(8,128)(2,1)} %get-tuple-element.2295), channel_id=1, source_target_pairs={{0,16},{4,20},{8,24},{12,28},{16,0},{20,4},{24,8},{28,12},{1,17},{... | collective-permute-start | bytes 6291464 | tf_op jit(solution)/shard_map/ppermute | solution.py:318
  648.0 36.9 %collective-permute-start.47 = (bf16[2048,1024]{1,0:T(8,128)(2,1)}, bf16[2048,1024]{1,0:T(8,128)(2,1)}, u32[]{:S(2)}, u32[]{:S(2)}) collective-permute-start(bf16[2048,1024]{1,0:T(8,128)(2,1)} %row_outer.13), channel_id=1, source_target_pairs={{0,4},{4,0},{8,12},{12,8},{16,20},{20,16},{24,28},{28,24},{1,5},{5... | collective-permute-start | bytes 12582920 | tf_op jit(solution)/shard_map/ppermute | solution.py:318
  648.1 329.3 %reduce-scatter.5.cloned.1.call-start = ((), (), s32[]{:S(2)}) async-start(), calls=%async_computation.5 | async-start | bytes 7864320 | tf_op jit(solution)/shard_map/reduce_scatter | solution.py:1173
  721.1 41.2 %collective-permute-start.51 = (bf16[1024,512]{1,0:T(8,128)(2,1)}, bf16[1024,512]{1,0:T(8,128)(2,1)}, u32[]{:S(2)}, u32[]{:S(2)}) collective-permute-start(bf16[1024,512]{1,0:T(8,128)(2,1)} %get-tuple-element.2615), channel_id=1, source_target_pairs={{0,8},{4,12},{8,0},{12,4},{16,24},{20,28},{24,16},{28,20},{1,9},{5... | collective-permute-start | bytes 3145736 | tf_op jit(solution)/shard_map/ppermute | solution.py:318
  722.6 39.7 %collective-permute-start.52 = (bf16[1024,512]{1,0:T(8,128)(2,1)}, bf16[1024,512]{1,0:T(8,128)(2,1)}, u32[]{:S(2)}, u32[]{:S(2)}) collective-permute-start(bf16[1024,512]{1,0:T(8,128)(2,1)} %get-tuple-element.2618), channel_id=1, source_target_pairs={{0,16},{4,20},{8,24},{12,28},{16,0},{20,4},{24,8},{28,12},{1,17},{... | collective-permute-start | bytes 3145736 | tf_op jit(solution)/shard_map/ppermute | solution.py:318
  724.5 37.8 %collective-permute-start.53 = (bf16[512,512]{1,0:T(8,128)(2,1)}, bf16[512,512]{1,0:T(8,128)(2,1)}, u32[]{:S(2)}, u32[]{:S(2)}) collective-permute-start(bf16[512,512]{1,0:T(8,128)(2,1)} %get-tuple-element.2568), channel_id=1, source_target_pairs={{4,0},{12,8},{20,16},{28,24},{5,1},{13,9},{21,17},{29,25},{6,2},{1... | collective-permute-start | bytes 1572872 | tf_op jit(solution)/shard_map/ppermute | solution.py:1122
  782.0 75.3 %collective-permute-start.62 = (bf16[2048,2048]{1,0:T(8,128)(2,1)}, bf16[2048,2048]{1,0:T(8,128)(2,1)}, u32[]{:S(2)}, u32[]{:S(2)}) collective-permute-start(bf16[2048,2048]{1,0:T(8,128)(2,1)} %row_outer.17), channel_id=1, source_target_pairs={{0,4},{4,0},{8,12},{12,8},{16,20},{20,16},{24,28},{28,24},{1,5},{5... | collective-permute-start | bytes 25165832 | tf_op jit(solution)/shard_map/ppermute | solution.py:318
  798.0 59.3 %collective-permute-start.58 = (bf16[512,768]{1,0:T(8,128)(2,1)}, bf16[512,768]{1,0:T(8,128)(2,1)S(1)}, u32[]{:S(2)}, u32[]{:S(2)}) collective-permute-start(bf16[512,768]{1,0:T(8,128)(2,1)} %reduce-scatter.3.cloned.1.call-done), channel_id=1, source_target_pairs={{0,8},{4,12},{8,0},{12,4},{16,24},{20,28},{24,16},{28,20},{1,9},{5... | collective-permute-start | bytes 2359304 | tf_op jit(solution)/shard_map/ppermute | solution.py:318
  799.6 57.7 %collective-permute-start.59 = (bf16[512,768]{1,0:T(8,128)(2,1)}, bf16[512,768]{1,0:T(8,128)(2,1)S(1)}, u32[]{:S(2)}, u32[]{:S(2)}) collective-permute-start(bf16[512,768]{1,0:T(8,128)(2,1)} %reduce-scatter.3.cloned.1.call-done), channel_id=1, source_target_pairs={{0,16},{4,20},{8,24},{12,28},{16,0},{20,4},{24,8},{28,12},{1,17},{... | collective-permute-start | bytes 2359304 | tf_op jit(solution)/shard_map/ppermute | solution.py:318
  878.4 79.1 %collective-permute-start.66 = (bf16[2048,768]{1,0:T(8,128)(2,1)S(1)}, bf16[2048,768]{1,0:T(8,128)(2,1)S(1)}, u32[]{:S(2)}, u32[]{:S(2)}) collective-permute-start(bf16[2048,768]{1,0:T(8,128)(2,1)S(1)} %constant_dynamic-update-slice_fusion.4.own_ref), channel_id=1, source_target_pairs={{0,4},{4,0},{8,12},{12,8},{16,20},{20,16},{24,28},{28,24},{1,5},{5... | collective-permute-start | bytes 9437192 | tf_op jit(solution)/shard_map/ppermute | solution.py:318
  880.8 76.7 %collective-permute-start.68 = (bf16[1024,1024]{1,0:T(8,128)(2,1)S(1)}, bf16[1024,1024]{1,0:T(8,128)(2,1)S(1)}, u32[]{:S(2)}, u32[]{:S(2)}) collective-permute-start(bf16[1024,1024]{1,0:T(8,128)(2,1)S(1)} %copy-done.107), channel_id=1, source_target_pairs={{0,8},{4,12},{8,0},{12,4},{16,24},{20,28},{24,16},{28,20},{1,9},{5... | collective-permute-start | bytes 6291464 | tf_op jit(solution)/shard_map/ppermute | solution.py:318
  881.8 75.6 %collective-permute-start.69 = (bf16[1024,1024]{1,0:T(8,128)(2,1)S(1)}, bf16[1024,1024]{1,0:T(8,128)(2,1)S(1)}, u32[]{:S(2)}, u32[]{:S(2)}) collective-permute-start(bf16[1024,1024]{1,0:T(8,128)(2,1)S(1)} %copy-done.108), channel_id=1, source_target_pairs={{0,16},{4,20},{8,24},{12,28},{16,0},{20,4},{24,8},{28,12},{1,17},{... | collective-permute-start | bytes 6291464 | tf_op jit(solution)/shard_map/ppermute | solution.py:318
  884.1 73.3 %collective-permute-start.71 = (bf16[256,2048]{1,0:T(8,128)(2,1)S(1)}, bf16[256,2048]{1,0:T(8,128)(2,1)S(1)}, u32[]{:S(2)}, u32[]{:S(2)}) collective-permute-start(bf16[256,2048]{1,0:T(8,128)(2,1)S(1)} %get-tuple-element.2901), channel_id=1, source_target_pairs={{1,0},{0,1},{5,2},{4,3},{3,4},{2,5},{7,6},{6,7},{9,8},{8,9},{13,10... | collective-permute-start | bytes 3145736 | tf_op jit(solution)/shard_map/ppermute | solution.py:399
  981.0 41.6 %collective-permute-start.76 = (bf16[512,1536]{1,0:T(8,128)(2,1)}, bf16[512,1536]{1,0:T(8,128)(2,1)S(1)}, u32[]{:S(2)}, u32[]{:S(2)}) collective-permute-start(bf16[512,1536]{1,0:T(8,128)(2,1)} %reduce-scatter.5.cloned.1.call-done), channel_id=1, source_target_pairs={{0,8},{4,12},{8,0},{12,4},{16,24},{20,28},{24,16},{28,20},{1,9},{5... | collective-permute-start | bytes 4718600 | tf_op jit(solution)/shard_map/ppermute | solution.py:318
  981.5 41.1 %collective-permute-start.77 = (bf16[512,1536]{1,0:T(8,128)(2,1)}, bf16[512,1536]{1,0:T(8,128)(2,1)S(1)}, u32[]{:S(2)}, u32[]{:S(2)}) collective-permute-start(bf16[512,1536]{1,0:T(8,128)(2,1)} %reduce-scatter.5.cloned.1.call-done), channel_id=1, source_target_pairs={{0,16},{4,20},{8,24},{12,28},{16,0},{20,4},{24,8},{28,12},{1,17},{... | collective-permute-start | bytes 4718600 | tf_op jit(solution)/shard_map/ppermute | solution.py:318
  (176 other events, 2570.0 us)
Sparse Core Ops, SparseCore 0:
  72.3 48.8 all-gather.2
  148.5 212.7 all-gather.4
  648.2 64.4 reduce-scatter.2
  798.1 161.9 reduce-scatter.4

commit v6 on v5

--- a/solution.py
+++ b/solution.py
@@ -326,10 +326,9 @@
 class Stage(dict):
     __getattr__ = dict.__getitem__
     __setattr__ = dict.__setitem__
-
-    def end(self, *gone):
-        for name in gone:
-            del self[name]
+    __delattr__ = dict.__delitem__
+
+    def end(self):
         self.update(lax.optimization_barrier(dict(self)))
 
 
@@ -341,6 +340,14 @@
             first = lax.optimization_barrier((first, last))[0]
         outs.append(call(first, *rest))
     return outs
+
+
+def ring_chunks(x):
+    count, at = lax.axis_size("shard"), lax.axis_index("shard")
+    rows = x.shape[0] // count
+    return [
+        lax.dynamic_slice_in_dim(x, ((at - i) % count) * rows, rows, 0) for i in range(count)
+    ]
 
 
 def ring_sum_first(chunks):
@@ -872,7 +879,8 @@
     core = me & 1
     count = lax.axis_size("rep")
 
-    s = Stage(tokens=tokens, cotangent=cotangent)
+    s = Stage()
+    s.cotangent = cotangent
     piece = width // shards
 
     s.own_blocks = [
@@ -882,6 +890,7 @@
         [jnp.stack([attn_gain, mlp_gain]), jnp.zeros((14, piece), low)], 0
     )
     travelling = jnp.concatenate([s.own_blocks[0], gain_rows], 0)
+    s.tokens = tokens
     s.out_block = column_block((w_out,), me)
     s.ffn_block = column_block((w_gate, w_up, w_down), me)
     s.before, s.behind = around(travelling, 1), around(travelling, -1)
@@ -891,15 +900,19 @@
     s.ahead = around(s.before, 1)
     tokens_sent = to_sequences_send(s.tokens)
     out_own = lax.all_gather(s.out_block, "shard", axis=0, tiled=True)
-    s.end("out_block", "tokens")
+    del s.out_block, s.tokens
+    s.end()
 
     parts = (s.before, s.ahead, s.behind)
     s.came = jnp.concatenate([part[:piece] for part in parts], 0)
     s.gains = jnp.concatenate([gain_rows[:2], *(part[piece : piece + 2] for part in parts)], 1)
     s.came_near = near(s.came)
     s.x_came = tokens_sent
-    s.end("before", "behind", "ahead")
-
+    del s.before, s.behind, s.ahead
+    s.end()
+
+    ffn_own = lax.all_gather(s.ffn_block, "shard", axis=0, tiled=True)
+    grad_y_sent = to_sequences_send(s.cotangent)
     s.came_far = far(*s.came_near)
     s.came_other = [across(block, CORE) for block in (s.came, *s.came_near)]
     gains = rolled(s.gains.astype(full))
@@ -926,7 +939,8 @@
     s.cosine, sine = cosine[0, :, 0], sine[0, :, 0]
     s.sine = jnp.concatenate([-sine[:, : head_dim // 2], sine[:, head_dim // 2 :]], 1)
     s.out_own = out_own
-    s.end("gains", "x_came", "other_lengths")
+    del s.gains, s.x_came, s.other_lengths, s.ffn_block, s.cotangent
+    s.end()
 
     head_columns = 2 * head_dim
     block_columns = 4 * head_dim
@@ -957,58 +971,63 @@
             s.cosine, s.sine, s.head_gains,
         )
 
-    ffn_own = lax.all_gather(s.ffn_block, "shard", axis=0, tiled=True)
+    def attend_call(projected, earlier):
+        return (
+            lambda query, own, before: attend(s.info, query, before, own),
+            *projected[1:], earlier,
+        )
+
     came_last = jnp.concatenate(s.came_far, 0)
     s.came_last = (came_last, across(came_last, CORE))
     s.out_near = near(s.out_own)
+    s.out_own_other = across(s.out_own, CORE)
     s.projected = in_order(
         [
             project_call(i, block, other)
             for i, (block, other) in enumerate(zip((s.came, *s.came_near), s.came_other))
         ]
     )
-    s.end("came_far", "ffn_block")
+    del s.came_far
+    s.end()
 
     s.out_far = far(*s.out_near)
+    s.out_near_other = [across(block, CORE) for block in s.out_near]
     s.earlier = [lax.ppermute(p[2], "rep", upward) for p in s.projected]
-    s.projected_last = project_call(3, *s.came_last)[0](*project_call(3, *s.came_last)[1:])
-    s.end()
-
-    out_chips = (s.out_own, *s.out_near, jnp.concatenate(s.out_far, 0))
-    s.out_chips = [(block, across(block, CORE)) for block in out_chips]
+    (s.projected_last,) = in_order([project_call(3, *s.came_last)])
+    s.grad_y_came = grad_y_sent
+    s.end()
+
+    grad_y = jnp.concatenate(in_turn(s.grad_y_came), 0)
+    s.grad_y = jnp.where(s.valid > 0, grad_y, jnp.zeros_like(grad_y))
+    grad_y_near = near(s.grad_y)
+    out_last = jnp.concatenate(s.out_far, 0)
+    s.out_last = (out_last, across(out_last, CORE))
     s.earlier_last = lax.ppermute(s.projected_last[2], "rep", upward)
-
-    def attend_call(projected, earlier):
-        return (
-            lambda query, own, before: attend(s.info, query, before, own),
-            *projected[1:], earlier,
-        )
-
     s.attended = in_order([attend_call(*pair) for pair in zip(s.projected, s.earlier)])
-    s.end("out_own", "out_near", "out_far")
-
-    grad_y_sent = to_sequences_send(s.cotangent)
+    del s.out_far, s.grad_y_came
+    s.end()
+
     s.projected = [*s.projected, s.projected_last]
     s.earlier = [*s.earlier, s.earlier_last]
-    s.out_blocks = [block for chip in s.out_chips for block in chip]
+    s.out_blocks = [
+        s.out_own, s.out_own_other, s.out_near[0], s.out_near_other[0], s.out_near[1],
+        s.out_near_other[1], *s.out_last,
+    ]
     (last,) = in_order([attend_call(s.projected_last, s.earlier_last)])
     s.attended = [*s.attended, last]
     s.mixed = [a[0] for a in s.attended]
     s.resid, s.mid = close_attention(s.x_low, s.mixed, s.out_blocks, s.mlp_gains)
-    s.end("out_chips", "projected_last", "earlier_last", "cotangent")
+    s.grad_y_near = grad_y_near
+    del s.out_own, s.out_own_other, s.out_near, s.out_near_other, s.out_last
+    del s.projected_last, s.earlier_last
+    s.end()
 
     s.mid_near = near(s.mid)
-    s.grad_y_came = grad_y_sent
+    s.grad_y_far = far(*s.grad_y_near)
     s.end()
 
     s.mid_far = far(*s.mid_near)
-    grad_y = jnp.concatenate(in_turn(s.grad_y_came), 0)
-    s.grad_y = jnp.where(s.valid > 0, grad_y, jnp.zeros_like(grad_y))
-    s.grad_y_near = near(s.grad_y)
     s.ffn_own = ffn_own
-    s.end("grad_y_came")
-
-    s.grad_y_far = far(*s.grad_y_near)
     s.end()
 
     s.mids = [s.mid, *s.mid_near, *s.mid_far]
@@ -1016,17 +1035,15 @@
     s.ffn_other = across(s.ffn_own, CORE)
     units = s.ffn_own.shape[1] // 3
     s.hidden_own = hidden_units(s.mids, s.grads_y, s.ffn_own)
-    s.end("mid", "mid_near", "mid_far", "grad_y_near", "grad_y_far")
-
-    def hidden_pairs(own, other, first, last):
+    del s.mid, s.mid_near, s.mid_far, s.grad_y_near, s.grad_y_far
+    s.end()
+
+    def gate_up_pairs():
         return [
-            (hidden[i], weights, at)
-            for hidden, weights in ((own, s.ffn_own), (other, s.ffn_other))
-            for at, i in enumerate(range(first, last))
+            (hidden[i], weights, i - 1)
+            for hidden, weights in ((s.hidden_own, s.ffn_own), (s.hidden_other, s.ffn_other))
+            for i in (1, 2)
         ]
-
-    def gate_up_pairs(other):
-        return hidden_pairs(s.hidden_own, other, 1, 3)
 
     def down_pairs():
         return [(s.hidden_own[0], s.ffn_own, 2), (s.hidden_other[0], s.ffn_other, 2)]
@@ -1039,11 +1056,6 @@
 
     def outer_call(lefts, rights, *added):
         return lambda first: row_outer(lefts, [[first, *rights[1:]]], 0, 8, *added)[0], rights[0]
-
-    to_plane, rest_of_plane = (2, 6, 5, 7), (3, 4, 0, 1)
-    s.hidden_other = hidden_units(s.mids, s.grads_y, s.ffn_other)
-    s.mid_sent = from_hidden(gate_up_pairs(s.hidden_other), to_plane)
-    s.end()
 
     def send_near(sent):
         return across(sent[0], ACROSS_X), across(sent[1], ACROSS_Y)
@@ -1068,19 +1080,31 @@
 
     by_rows = lambda a: jnp.split(a, 2, 0)
     by_columns = lambda a: jnp.split(a, 2, 1)
+    to_plane, rest_of_plane = (2, 6, 5, 7), (3, 4, 0, 1)
+
+    s.hidden_other = hidden_units(s.mids, s.grads_y, s.ffn_other)
+    (s.down_outer,) = in_order([outer_call(s.grads_y, s.hidden_other[:1])])
+    s.end()
+
+    s.down_came = across(s.down_outer, CORE)
+    s.mid_sent = from_hidden(gate_up_pairs(), to_plane)
+    del s.down_outer
+    s.end()
 
     s.mid_came = send_near(s.mid_sent)
-    s.mid_rest, s.down_outer, s.gate_up_outer = in_order(
+    s.down_mine, s.mid_rest, s.gate_up_outer = in_order(
         [
-            from_hidden_call(gate_up_pairs(s.hidden_other), rest_of_plane),
-            outer_call(s.grads_y, s.hidden_other[:1]),
+            outer_call(s.grads_y, s.hidden_own[:1], s.down_came),
+            from_hidden_call(gate_up_pairs(), rest_of_plane),
             outer_call(s.mids, s.hidden_other[1:]),
         ]
     )
-    s.end("mid_sent")
-
+    del s.mid_sent, s.down_came
+    s.end()
+
+    s.down_chunks = ring_chunks(s.down_mine)
+    s.down_ring = ring_sum_first(s.down_chunks)
     s.mid_came_far = send_far(s.mid_came, by_rows(s.mid_rest[0]), by_rows)
-    s.down_came = across(s.down_outer, CORE)
     s.gate_up_came = across(s.gate_up_outer, CORE)
     s.mlp_sent, s.mlp_rest = in_order(
         [
@@ -1088,9 +1112,11 @@
             from_hidden_call(down_pairs(), rest_of_plane),
         ]
     )
-    s.end("down_outer", "gate_up_outer")
+    del s.gate_up_outer, s.down_mine
+    s.end()
 
     mlp_came = send_near(s.mlp_sent)
+    s.down_last = around(rounded_sum(s.down_chunks[3], s.down_ring[0]), 1)
     grad_mid = total(s.mid_came, s.mid_came_far, by_rows(s.mid_rest[1]), by_rows)
     inverse_mid = lax.rsqrt(jnp.mean(s.resid * s.resid, -1, keepdims=True) + EPS)
     mid_unit = s.resid * inverse_mid
@@ -1100,8 +1126,10 @@
     )
     s.resid_low = s.grad_resid.astype(low)
     s.resid_rolled = rolled(s.resid_low)
-    (s.down_mine,) = in_order([outer_call(s.grads_y, s.hidden_own[:1], s.down_came)])
-    s.end("mid_came", "mid_came_far", "mid_rest", "down_came")
+    (s.gate_up_mine,) = in_order([outer_call(s.mids, s.hidden_own[1:], s.gate_up_came)])
+    del s.mid_came, s.mid_came_far, s.mid_rest, s.gate_up_came, s.hidden_own, s.hidden_other
+    del s.mids, s.grads_y, s.ffn_own, s.ffn_other
+    s.end()
 
     def back_call(i):
         raw, query, own_pair = s.projected[i]
@@ -1113,13 +1141,14 @@
 
     def finish_call(i):
         return (
-            finish, s[f"back{i}"][0], s[f"back{i}"][1], s[f"returned{i}"], s.projected[i][0],
+            finish, s.backs[i][0], s.backs[i][1], s.returned[i], s.projected[i][0],
             s.cosine, s.sine, s.head_gains[1:],
         )
 
     def give_back(*chips):
-        for i in chips:
-            s[f"returned{i}"] = lax.ppermute(s[f"back{i}"][2], "rep", downward)
+        s.returned = s.returned | {
+            i: lax.ppermute(s.backs[i][2], "rep", downward) for i in chips
+        }
 
     def odd_call(left, blocks):
         return lambda first: row_outer([first], [blocks], 0, 8)[0], left
@@ -1132,23 +1161,31 @@
         groups = [[blocks[2], blocks[3]], [blocks[1]], [blocks[0]]]
         return lambda first: row_outer([first], groups, 4, 4, came, (2, 3, 1, 0)), left
 
-    down_total = lax.psum_scatter(s.down_mine, "shard", scatter_dimension=0, tiled=True)
+    s.down_total = rounded_sum(s.down_chunks[0], s.down_ring[1], s.down_last)
+    s.gate_up_chunks = ring_chunks(s.gate_up_mine)
+    gate_up_ring = ring_sum_first(s.gate_up_chunks)
     mixed_even = [m[:, :head_columns] for m in s.mixed]
     mixed_odd = [m[:, head_columns:] for m in s.mixed]
-    s.out_odd, s.back3 = in_order([odd_call(s.resid_rolled, mixed_odd), back_call(3)])
+    s.returned = {}
+    s.out_odd, back = in_order([odd_call(s.resid_rolled, mixed_odd), back_call(3)])
+    s.backs = {3: back}
     s.mlp_came = mlp_came
-    s.end("down_mine")
+    del s.gate_up_mine, s.mlp_sent, s.down_chunks, s.down_ring, s.down_last
+    s.end()
 
     s.mlp_came_far = send_far(s.mlp_came, by_rows(s.mlp_rest[0]), by_rows)
     s.out_came = across(s.out_odd, CORE)
     give_back(3)
-    s.back1, s.back2 = in_order([back_call(1), back_call(2)])
-    s.end("out_odd", "mlp_sent")
-
+    back1, back2 = in_order([back_call(1), back_call(2)])
+    s.backs = s.backs | {1: back1, 2: back2}
+    del s.out_odd
+    s.end()
+
+    s.down_near = near(s.down_total)
     give_back(1, 2)
     mlp_out = total(s.mlp_came, s.mlp_came_far, by_rows(s.mlp_rest[1]), by_rows)
     s.output = (s.valid * (s.resid + mlp_out)).astype(low)
-    s.out_head, s.out_tail, s.back0, s.finished3 = in_order(
+    s.out_head, s.out_tail, back, finished = in_order(
         [
             head_call(s.resid_rolled, mixed_even, s.out_came),
             tail_call(s.resid_rolled, mixed_even, s.out_came),
@@ -1156,124 +1193,178 @@
             finish_call(3),
         ]
     )
-    s.end("mlp_came", "mlp_came_far", "mlp_rest", "out_came", "resid")
-
+    s.backs = s.backs | {0: back}
+    s.finished = {3: finished}
+    s.gate_up_ring = gate_up_ring
+    del s.mlp_came, s.mlp_came_far, s.mlp_rest, s.out_came, s.resid
+    s.end()
+
+    gate_up_last = around(rounded_sum(s.gate_up_chunks[3], s.gate_up_ring[0]), 1)
+    s.out_near = send_near((s.out_head[0], s.out_tail[0]))
+    s.down_far = far(*s.down_near)
+    give_back(0)
+    finished1, finished2 = in_order([finish_call(1), finish_call(2)])
+    s.finished = s.finished | {1: finished1, 2: finished2}
+    s.end()
+
+    s.out_far = send_far(s.out_near, (s.out_tail[1], s.out_head[1]), by_columns)
+    s.down_own = jnp.concatenate([s.down_total, *s.down_near, *s.down_far], 0)
+    s.down_other = across(s.down_own, CORE)
+    (finished,) = in_order([finish_call(0)])
+    s.finished = s.finished | {0: finished}
+    (s.qkv_odd,) = in_order([odd_call(s.normed, [s.finished[i][1] for i in range(4)])])
+    s.gate_up_last = gate_up_last
+    del s.down_total, s.down_near, s.down_far
+    s.end()
+
+    my_group = me.astype(jnp.int32)[None]
+
+    def whole_call(widths, own, other):
+        return lambda first: whole_columns(my_group, first, other, widths), own
+
+    s.qkv_came = across(s.qkv_odd, CORE)
+    s.gate_up_total = rounded_sum(s.gate_up_chunks[0], s.gate_up_ring[1], s.gate_up_last)
+    s.gate_up_near = near(s.gate_up_total)
     output_sent = from_sequences_send(s.output)
-    s.out_near = send_near((s.out_head[0], s.out_tail[0]))
-    give_back(0)
-    s.gate_up_mine, s.finished1, s.finished2 = in_order(
-        [
-            outer_call(s.mids, s.hidden_own[1:], s.gate_up_came),
-            finish_call(1),
-            finish_call(2),
-        ]
-    )
-    s.end("gate_up_came", "hidden_own", "hidden_other", "output")
-
-    gate_up_total = lax.psum_scatter(s.gate_up_mine, "shard", scatter_dimension=0, tiled=True)
-    s.out_far = send_far(s.out_near, (s.out_tail[1], s.out_head[1]), by_columns)
-    ((s.finished0),) = in_order([finish_call(0)])
-    s.finished = [s.finished0, s.finished1, s.finished2, s.finished3]
-    (s.qkv_odd,) = in_order([odd_call(s.normed, [f[1] for f in s.finished])])
-    s.down_total = down_total
-    s.output_came = output_sent
-    s.end("gate_up_mine", "finished0", "finished1", "finished2", "finished3")
-
-    s.qkv_came = across(s.qkv_odd, CORE)
-    s.down_near = near(s.down_total)
     out_sum = total(s.out_near, s.out_far, (s.out_head[2], s.out_tail[2]), by_columns)
     s.out_chunks = jnp.split(out_sum.astype(low), shards, 0)
     s.out_ring = ring_sum_first(s.out_chunks)
-    grad_in = rolled(
-        back_to_rows(
-            [part for f in s.finished for part in f[:2]],
-            [
-                pair
-                for i, block in enumerate(zip((s.came, *s.came_near), s.came_other))
-                for pair in ((s.own_blocks[2 * i], block[0]), (s.own_blocks[2 * i + 1], block[1]))
-            ]
-            + [(s.own_blocks[6 + i], s.came_last[i]) for i in range(2)],
-        )
-    )
+    weights = [
+        pair
+        for i, block in enumerate(zip((s.came, *s.came_near), s.came_other))
+        for pair in ((s.own_blocks[2 * i], block[0]), (s.own_blocks[2 * i + 1], block[1]))
+    ] + [(s.own_blocks[6 + i], s.came_last[i]) for i in range(2)]
+    blocks = [part for i in range(4) for part in s.finished[i][:2]]
+    grad_in, s.whole_down = in_order(
+        [
+            (lambda first: back_to_rows([first, *blocks[1:]], weights), blocks[0]),
+            whole_call((units,), s.down_own, s.down_other),
+        ]
+    )
+    grad_in = rolled(grad_in)
     x_unit = s.x_low.astype(full) * s.inverse_in
     s.attn_gain_part = jnp.sum(x_unit * grad_in, 0)
     s.grad_tokens = (
         s.grad_resid + norm_back(x_unit, s.inverse_in, grad_in * s.attn_gains)
     ).astype(low)
-    s.end("qkv_odd", "out_near", "out_far", "out_head", "out_tail")
-
-    s.down_far = far(*s.down_near)
+    del s.gate_up_chunks, s.gate_up_ring, s.gate_up_last, s.output
+    del s.qkv_odd, s.out_near, s.out_far, s.out_head, s.out_tail, s.down_own, s.down_other
+    del s.own_blocks, s.came, s.came_near, s.came_other, s.came_last, s.grad_resid, s.x_low
+    s.end()
+
+    s.gate_up_far = far(*s.gate_up_near)
     s.out_ring_last = around(rounded_sum(s.out_chunks[3], s.out_ring[0]), 1)
-    grad_tokens_sent = from_sequences_send(s.grad_tokens)
-    s.qkv_head, s.qkv_tail = in_order(
+    even = [s.finished[i][0] for i in range(4)]
+    halves = [
+        [block[:, half * head_columns : (half + 1) * head_columns] for block in even]
+        for half in range(2)
+    ]
+    came_halves = [
+        jnp.concatenate(
+            [
+                s.qkv_came[:, i * block_columns + half * head_columns :][:, :head_columns]
+                for i in range(4)
+            ],
+            1,
+        )
+        for half in range(2)
+    ]
+    first_head, first_tail, second_head, second_tail = in_order(
         [
-            head_call(s.normed, [f[0] for f in s.finished], s.qkv_came),
-            tail_call(s.normed, [f[0] for f in s.finished], s.qkv_came),
+            call(s.normed, halves[half], came_halves[half])
+            for half in range(2)
+            for call in (head_call, tail_call)
         ]
     )
+    s.heads = [first_head, second_head]
+    s.tails = [first_tail, second_tail]
     s.gain_parts = jnp.concatenate(
         [
             s.attn_gain_part,
             s.mlp_gain_part,
-            sum(s[f"back{i}"][3] for i in range(4))[0],
-            sum(f[2] for f in s.finished)[0],
+            sum(s.backs[i][3] for i in range(4))[0],
+            sum(s.finished[i][2] for i in range(4))[0],
         ]
     )
-    s.end("qkv_came", "grad_tokens", "finished")
-
-    my_group = me.astype(jnp.int32)[None]
-
-    def whole(spread, widths):
-        return whole_columns(my_group, *spread, widths)
-
-    s.qkv_near = send_near((s.qkv_head[0], s.qkv_tail[0]))
-    s.down_own = jnp.concatenate([s.down_total, *s.down_near, *s.down_far], 0)
-    s.down_other = across(s.down_own, CORE)
+    del s.qkv_came, s.finished, s.backs
+    s.end()
+
+    grad_tokens_sent = from_sequences_send(s.grad_tokens)
+
+    def qkv_near(half):
+        return send_near((s.heads[half][0], s.tails[half][0]))
+
+    def qkv_far(came, half):
+        return send_far(came, (s.tails[half][1], s.heads[half][1]), by_columns)
+
+    def qkv_chunks(came, came_far, half):
+        own = total(came, came_far, (s.heads[half][2], s.tails[half][2]), by_columns)
+        return jnp.split(own.astype(low), shards, 0)
+
+    s.near0 = qkv_near(0)
+    s.gate_up_own = jnp.concatenate([s.gate_up_total, *s.gate_up_near, *s.gate_up_far], 0)
+    s.gate_up_other = across(s.gate_up_own, CORE)
     s.out_total = rounded_sum(s.out_chunks[0], s.out_ring[1], s.out_ring_last)
     s.gain_came = across(s.gain_parts, CORE)
-    s.tokens_came = grad_tokens_sent
-    s.end("out_chunks", "out_ring", "out_ring_last")
-
-    s.qkv_far = send_far(s.qkv_near, (s.qkv_tail[1], s.qkv_head[1]), by_columns)
+    del s.out_chunks, s.out_ring, s.out_ring_last, s.gate_up_near, s.gate_up_far
+    s.output_came = output_sent
+    del s.gate_up_total, s.grad_tokens
+    s.end()
+
+    s.far0 = qkv_far(s.near0, 0)
+    s.near1 = qkv_near(1)
     s.gain_parts = s.gain_parts + s.gain_came
     s.gain_came = across(s.gain_parts, ACROSS_X)
-    s.whole_down = whole((s.down_own, s.down_other), (units,))
-    s.gate_up_total = gate_up_total
-    s.end("down_own", "down_other")
-
-    qkv_sum = total(s.qkv_near, s.qkv_far, (s.qkv_head[2], s.qkv_tail[2]), by_columns)
-    s.qkv_chunks = jnp.split(qkv_sum.astype(low), shards, 0)
-    s.qkv_ring = ring_sum_first(s.qkv_chunks)
-    s.gate_up_near = near(s.gate_up_total)
+    (s.whole_gate_up,) = in_order([whole_call((units, units), s.gate_up_own, s.gate_up_other)])
+    s.tokens_came = grad_tokens_sent
+    del s.gate_up_own, s.gate_up_other
+    s.end()
+
+    s.chunks0 = qkv_chunks(s.near0, s.far0, 0)
+    s.ring0 = ring_sum_first(s.chunks0)
+    s.far1 = qkv_far(s.near1, 1)
     s.gain_parts = s.gain_parts + s.gain_came
     s.gain_came = across(s.gain_parts, ACROSS_Y)
-    s.end("qkv_near", "qkv_far", "qkv_head", "qkv_tail")
-
-    s.qkv_ring_last = around(rounded_sum(s.qkv_chunks[3], s.qkv_ring[0]), 1)
-    s.gate_up_far = far(*s.gate_up_near)
+    del s.near0, s.far0
+    s.end()
+
+    s.last0 = around(rounded_sum(s.chunks0[3], s.ring0[0]), 1)
+    s.chunks1 = qkv_chunks(s.near1, s.far1, 1)
+    s.ring1 = ring_sum_first(s.chunks1)
     s.gain_parts = s.gain_parts + s.gain_came
     s.gain_came = lax.ppermute(s.gain_parts, "shard", [(i, i ^ 1) for i in range(shards)])
-    s.end()
-
-    qkv_total = rounded_sum(s.qkv_chunks[0], s.qkv_ring[1], s.qkv_ring_last)
-    s.attn_total = jnp.concatenate([qkv_total, s.out_total], 1)
-    s.attn_near = near(s.attn_total)
-    s.gate_up_own = jnp.concatenate([s.gate_up_total, *s.gate_up_near, *s.gate_up_far], 0)
-    s.gate_up_other = across(s.gate_up_own, CORE)
+    del s.near1, s.far1, s.heads, s.tails
+    s.end()
+
+    query_total = rounded_sum(s.chunks0[0], s.ring0[1], s.last0)
+    s.total0 = jnp.concatenate([query_total, s.out_total], 1)
+    s.spread0 = near(s.total0)
+    s.last1 = around(rounded_sum(s.chunks1[3], s.ring1[0]), 1)
     s.gain_parts = s.gain_parts + s.gain_came
     s.gain_came = lax.ppermute(s.gain_parts, "shard", [(i, i ^ 2) for i in range(shards)])
-    s.end("qkv_chunks", "qkv_ring", "qkv_ring_last", "gate_up_near", "gate_up_far")
-
-    s.attn_far = far(*s.attn_near)
-    s.whole_gate_up = whole((s.gate_up_own, s.gate_up_other), (units, units))
-    s.end("gate_up_own", "gate_up_other")
-
-    s.attn_own = jnp.concatenate([s.attn_total, *s.attn_near, *s.attn_far], 0)
-    s.attn_other = across(s.attn_own, CORE)
-    s.end()
-
-    whole_query, whole_key, whole_value, whole_out = whole(
-        (s.attn_own, s.attn_other), (head_columns, head_dim, head_dim, head_columns)
+    del s.chunks0, s.ring0, s.last0, s.out_total
+    s.end()
+
+    s.spread_far0 = far(*s.spread0)
+    s.total1 = rounded_sum(s.chunks1[0], s.ring1[1], s.last1)
+    s.spread1 = near(s.total1)
+    del s.chunks1, s.ring1, s.last1
+    s.end()
+
+    s.own0 = jnp.concatenate([s.total0, *s.spread0, *s.spread_far0], 0)
+    s.other0 = across(s.own0, CORE)
+    s.spread_far1 = far(*s.spread1)
+    del s.total0, s.spread0, s.spread_far0
+    s.end()
+
+    s.own1 = jnp.concatenate([s.total1, *s.spread1, *s.spread_far1], 0)
+    s.other1 = across(s.own1, CORE)
+    (s.whole0,) = in_order([whole_call((head_columns, head_columns), s.own0, s.other0)])
+    del s.own0, s.other0, s.total1, s.spread1, s.spread_far1
+    s.end()
+
+    ((whole_key, whole_value),) = in_order(
+        [whole_call((head_dim, head_dim), s.own1, s.other1)]
     )
     gain_sums = s.gain_parts + s.gain_came
     wide = lax.dynamic_slice_in_dim(
@@ -1284,12 +1375,12 @@
         jnp.stack(in_turn(s.output_came)),
         jnp.stack(in_turn(s.tokens_came)),
         wide[0],
-        whole_query,
+        s.whole0[0],
         whole_key,
         whole_value,
         narrow[:head_dim],
         narrow[head_dim:],
-        whole_out,
+        s.whole0[1],
         wide[1],
         *s.whole_gate_up,
         *s.whole_down,

time: 1140 us -> 1220 us (1.070)
  starting transfers between devices: 172 us -> 251 us
  waiting for transfers between devices: 382 us -> 345 us
  other arithmetic: 61.2 us -> 82.2 us
  local copies, waits for them, and re-layouts: 67.1 us -> 79.8 us
    ppermute x4, waiting for transfers between devices: 123 us -> 70.6 us  [to_sequences_send(): lax.ppermute(lax.dynamic_index_in_dim(x, turn ^ odd, 0, keepdims=False),...]
    ppermute x4, waiting for transfers between devices: 66.8 us -> 33.8 us  [from_sequences_send(): lax.ppermute(lax.dynamic_index_in_dim(x, turn ^ odd, 0, keepdims=False),...]
    ppermute x64 -> x73, waiting for transfers between devices: 125 us -> 155 us  [across(): return lax.ppermute(x, 'rep', [(i, i ^ mask) for i in range(count)])]
    ppermute x9 -> x18, starting transfers between devices: 41.4 us -> 70.6 us  [around(): lax.ppermute(x, 'shard', [(i, (i + by) % count) for i in range(count)])]
    ppermute x64 -> x73, starting transfers between devices: 80.4 us -> 109 us  [across(): return lax.ppermute(x, 'rep', [(i, i ^ mask) for i in range(count)])]
    ppermute x4, starting transfers between devices: 14.2 us -> 34.9 us  [from_sequences_send(): lax.ppermute(lax.dynamic_index_in_dim(x, turn ^ odd, 0, keepdims=False),...]
    ppermute x9 -> x18, waiting for transfers between devices: 54.9 us -> 62.2 us  [around(): lax.ppermute(x, 'shard', [(i, (i + by) % count) for i in range(count)])]
    pallas_call x10 -> x12, Pallas kernels: 107 us -> 114 us  [row_outer(): pl.pallas_call(body, grid=(tiles,), out_shape=[jax.ShapeDtypeStruct((tile...]
  transfers between devices with their start and end apart: 95 -> 111, of which waited for: 31 -> 32; matrix products, arithmetic and copies ran while one was open for 8% -> 9% of each run, Pallas kernels for 33% -> 32%
where the time goes in v6:
time: 1220 us; the launch traced here: 1210 us
  Pallas kernels  436 us (36%)
  waiting for transfers between devices  345 us (28%)
  starting transfers between devices  251 us (21%)
  other arithmetic  82.2 us (7%)
  local copies, waits for them, and re-layouts  79.8 us (7%)
  between operations  16.7 us (1%)
    ppermute x73, waiting for transfers between devices, across(): return lax.ppermute(x, 'rep', [(i, i ^ mask) for i in range(count)])  155 us
    pallas_call x16, Pallas kernels, call(): pl.pallas_call(body, grid=(1,), out_shape=outs, in_specs=in_specs, out_sp...  131 us
    pallas_call x12, Pallas kernels, row_outer(): pl.pallas_call(body, grid=(tiles,), out_shape=[jax.ShapeDtypeStruct((tile...  114 us
    ppermute x73, starting transfers between devices, across(): return lax.ppermute(x, 'rep', [(i, i ^ mask) for i in range(count)])  109 us
    ppermute x4, waiting for transfers between devices, to_sequences_send(): lax.ppermute(lax.dynamic_index_in_dim(x, turn ^ odd, 0, keepdims=False),...  70.6 us
    ppermute x18, starting transfers between devices, around(): lax.ppermute(x, 'shard', [(i, (i + by) % count) for i in range(count)])  70.6 us
    ppermute x18, waiting for transfers between devices, around(): lax.ppermute(x, 'shard', [(i, (i + by) % count) for i in range(count)])  62.2 us
    pallas_call x2, Pallas kernels, hidden_units(): pl.pallas_call(body, grid=(3,), out_shape=[jax.ShapeDtypeStruct((rows, un...  59.9 us
  transfers between devices with their start and end apart: 111, of which 32 were waited for; matrix products, arithmetic and copies ran while one was open for 9% of the time, Pallas kernels for 32%

profile of v6, /device:TPU:0, one launch (start us, length us, event | category | flops | bytes accessed | tf_op | source)
XLA Modules:
  0.0 1211.6 jit_solution(11814624897223843036)
XLA Ops:
  43.0 14.4 %collective-permute-done.3 = bf16[528,512]{1,0:T(8,128)(2,1)S(1)} collective-permute-done((bf16[528,512]{1,0:T(8,128)(2,1)}, bf16[528,512]{1,0:T(8,128)(2,1)S(1)}, u32[]{:S(2)}, u32[]{:S(2)}) %collective-permute-start.3) | collective-permute-done | bytes 540704 | tf_op jit(solution)/shard_map/ppermute | solution.py:323
  66.9 52.3 %collective-permute-done.7 = bf16[256,2048]{1,0:T(8,128)(2,1)S(1)} collective-permute-done((bf16[256,2048]{1,0:T(8,128)(2,1)S(1)}, bf16[256,2048]{1,0:T(8,128)(2,1)S(1)}, u32[]{:S(2)}, u32[]{:S(2)}) %collective-permute-start.7) | collective-permute-done | bytes 1048608 | tf_op jit(solution)/shard_map/ppermute | solution.py:393
  163.8 12.0 collective-permute-done.14.refs_6_.weight0
  175.9 11.5 collective-permute-start.21
  211.7 36.0 %collective-permute-start.25 = (bf16[2048,256]{1,0:T(8,128)(2,1)S(1)}, bf16[2048,256]{1,0:T(8,128)(2,1)S(1)}, u32[]{:S(2)}, u32[]{:S(2)}) collective-permute-start(bf16[2048,256]{1,0:T(8,128)(2,1)S(1)} %collective-permute-done.15.refs_8_.weight0), channel_id=1, source_target_pairs={{0,4},{4,0},{8,12},{12,8},{16,20},{20,16},{24,28},{28,24},{1,5},{5... | collective-permute-start | bytes 3145736 | tf_op jit(solution)/shard_map/ppermute | solution.py:318
  249.4 18.3 %collective-permute-done.21 = bf16[256,2048]{1,0:T(8,128)(2,1)} collective-permute-done((bf16[256,2048]{1,0:T(8,128)(2,1)}, bf16[256,2048]{1,0:T(8,128)(2,1)}, u32[]{:S(2)}, u32[]{:S(2)}) %collective-permute-start.21) | collective-permute-done | bytes 1048608 | tf_op jit(solution)/shard_map/ppermute | solution.py:393
  319.6 11.7 close_attention.1
  335.7 65.9 %collective-permute-done.30.refs_8_.refs_3_ = bf16[256,2048]{1,0:T(8,128)(2,1)S(1)} collective-permute-done((bf16[256,2048]{1,0:T(8,128)(2,1)S(1)}, bf16[256,2048]{1,0:T(8,128)(2,1)S(1)}, u32[]{:S(2)}, u32[]{:S(2)}) %collective-permute-start.30) | collective-permute-done | bytes 1048608 | tf_op jit(solution)/shard_map/ppermute | solution.py:318
  405.1 20.5 %collective-permute-done.34.refs_3_ = bf16[256,2048]{1,0:T(8,128)(2,1)S(1)} collective-permute-done((bf16[256,2048]{1,0:T(8,128)(2,1)S(1)}, bf16[256,2048]{1,0:T(8,128)(2,1)S(1)}, u32[]{:S(2)}, u32[]{:S(2)}) %collective-permute-start.34) | collective-permute-done | bytes 1048608 | tf_op jit(solution)/shard_map/ppermute | solution.py:318
  427.1 29.6 %hidden_units.2 = (bf16[2048,768]{1,0:T(8,128)(2,1)}, bf16[2048,768]{1,0:T(8,128)(2,1)}, bf16[2048,768]{1,0:T(8,128)(2,1)}) custom-call(bf16[512,2048]{1,0:T(8,128)(2,1)} %get-tuple-element.2344.refs_0_, bf16[512,2048]{1,0:T(8,128)(2,1)} %copy-done.11, bf16[512,2048]{1,0:T(8,128)(2,1)} %copy-done.12, bf16[256,2048]{1,0:T(8,128)(2,1)} %copy-done.25, ...), custom_call_target="tpu_custom_call" | custom-call | flops 1 | bytes 1 | tf_op jit(solution)/shard_map/hidden_units/pallas_call | solution.py:657
  456.7 30.2 %hidden_units.3 = (bf16[2048,768]{1,0:T(8,128)(2,1)}, bf16[2048,768]{1,0:T(8,128)(2,1)}, bf16[2048,768]{1,0:T(8,128)(2,1)}) custom-call(bf16[512,2048]{1,0:T(8,128)(2,1)} %get-tuple-element.2344.refs_0_, bf16[512,2048]{1,0:T(8,128)(2,1)} %copy-done.11, bf16[512,2048]{1,0:T(8,128)(2,1)} %copy-done.12, bf16[256,2048]{1,0:T(8,128)(2,1)} %copy-done.25, ...), custom_call_target="tpu_custom_call" | custom-call | flops 1 | bytes 1 | tf_op jit(solution)/shard_map/hidden_units/pallas_call | solution.py:657
  487.0 12.6 %row_outer.12 = bf16[2048,768]{1,0:T(8,128)(2,1)} custom-call(bf16[512,2048]{1,0:T(8,128)(2,1)} %copy-done.6, bf16[512,2048]{1,0:T(8,128)(2,1)} %copy-done.13, bf16[512,2048]{1,0:T(8,128)(2,1)} %copy-done.14, bf16[256,2048]{1,0:T(8,128)(2,1)} %copy-done.26, bf16[256,2048]{1,0:T(8,128)(2,1)} %copy-done.27, ...), custom_call_target="tpu_custom_call" | custom-call | flops 6442450944 | bytes 11534336 | tf_op jit(solution)/shard_map/row_outer/pallas_call | solution.py:739
  500.0 19.1 %from_hidden.4 = (bf16[512,2048]{1,0:T(8,128)(2,1)}, bf16[512,2048]{1,0:T(8,128)(2,1)}) custom-call(bf16[2048,768]{1,0:T(8,128)(2,1)} %get-tuple-element.2349.refs_0_.refs_1_.refs_2_.refs_3_.refs_5_, bf16[2048,768]{1,0:T(8,128)(2,1)} %get-tuple-element.2349.refs_0_.refs_1_.refs_2_.refs_3_.refs_5_, ...), custom_call_target="tpu_custom_call" | custom-call | flops 1 | bytes 1 | tf_op jit(solution)/shard_map/from_hidden/pallas_call | solution.py:696
  522.8 13.2 %row_outer.13 = bf16[2048,768]{1,0:T(8,128)(2,1)} custom-call(bf16[512,2048]{1,0:T(8,128)(2,1)} %copy-done.6, bf16[512,2048]{1,0:T(8,128)(2,1)} %copy-done.13, bf16[512,2048]{1,0:T(8,128)(2,1)} %copy-done.14, bf16[256,2048]{1,0:T(8,128)(2,1)} %copy-done.26, bf16[256,2048]{1,0:T(8,128)(2,1)} %copy-done.27, ...), custom_call_target="tpu_custom_call" | custom-call | flops 6442450944 | bytes 11534336 | tf_op jit(solution)/shard_map/row_outer/pallas_call | solution.py:739
  536.0 18.8 %from_hidden.5 = (bf16[512,2048]{1,0:T(8,128)(2,1)}, bf16[512,2048]{1,0:T(8,128)(2,1)}) custom-call(bf16[2048,768]{1,0:T(8,128)(2,1)} %get-tuple-element.2349.refs_0_.refs_1_.refs_2_.refs_3_.refs_5_, bf16[2048,768]{1,0:T(8,128)(2,1)} %get-tuple-element.2349.refs_0_.refs_1_.refs_2_.refs_3_.refs_5_, ...), custom_call_target="tpu_custom_call" | custom-call | flops 1 | bytes 1 | tf_op jit(solution)/shard_map/from_hidden/pallas_call | solution.py:696
  554.8 19.5 %row_outer.14 = bf16[2048,1536]{1,0:T(8,128)(2,1)} custom-call(bf16[512,2048]{1,0:T(8,128)(2,1)} %get-tuple-element.2344.refs_0_, bf16[512,2048]{1,0:T(8,128)(2,1)} %copy-done.11, bf16[512,2048]{1,0:T(8,128)(2,1)} %copy-done.12, bf16[256,2048]{1,0:T(8,128)(2,1)} %copy-done.25, bf16[256,2048]{1,0:T(8,128)(2,1)} %collective-permute-done.35.refs_4_, ...), custom_call_target="tpu_custom_call" | custom-call | flops 12884901888 | bytes 14680064 | tf_op jit(solution)/shard_map/row_outer/pallas_call | solution.py:739
  580.9 46.0 %collective-permute-start.40 = (bf16[512,768]{1,0:T(8,128)(2,1)}, bf16[512,768]{1,0:T(8,128)(2,1)}, u32[]{:S(2)}, u32[]{:S(2)}) collective-permute-start(bf16[512,768]{1,0:T(8,128)(2,1)} %get-tuple-element.3040), channel_id=1, source_target_pairs={{0,1},{1,2},{2,3},{3,0},{4,5},{5,6},{6,7},{7,4},{8,9},{9,10},{10,1... | collective-permute-start | bytes 2359304 | tf_op jit(solution)/shard_map/ppermute | solution.py:323
  648.4 12.0 collective-permute-done.41
  672.3 19.7 %row_outer.15 = bf16[2048,1536]{1,0:T(8,128)(2,1)} custom-call(bf16[512,2048]{1,0:T(8,128)(2,1)} %get-tuple-element.2344.refs_0_, bf16[512,2048]{1,0:T(8,128)(2,1)} %copy-done.11, bf16[512,2048]{1,0:T(8,128)(2,1)} %copy-done.12, bf16[256,2048]{1,0:T(8,128)(2,1)} %copy-done.25, bf16[256,2048]{1,0:T(8,128)(2,1)} %collective-permute-done.35.refs_4_, ...), custom_call_target="tpu_custom_call" | custom-call | flops 12884901888 | bytes 14680064 | tf_op jit(solution)/shard_map/row_outer/pallas_call | solution.py:739
  712.3 14.7 %attend_back.4 = (bf16[512,512]{1,0:T(8,128)(2,1)}, f32[512,512]{1,0:T(8,128)}, bf16[512,512]{1,0:T(8,128)(2,1)}, f32[1,128]{1,0:T(1,128)}) custom-call(s32[2]{0:T(128)} %pad_add_fusion.info, bf16[512,512]{1,0:T(8,128)(2,1)} %get-tuple-element.2419.query, bf16[512,512]{1,0:T(8,128)(2,1)} %collective-permute-done.26.before, ...), custom_call_target="tpu_custom_call" | custom-call | flops 1 | bytes 1 | tf_op jit(solution)/shard_map/attend_back/pallas_call | solution.py:617
  742.3 14.6 %attend_back.5 = (bf16[512,512]{1,0:T(8,128)(2,1)}, f32[512,512]{1,0:T(8,128)}, bf16[512,512]{1,0:T(8,128)(2,1)}, f32[1,128]{1,0:T(1,128)}) custom-call(s32[2]{0:T(128)} %pad_add_fusion.info, bf16[512,512]{1,0:T(8,128)(2,1)} %get-tuple-element.2487.query, bf16[512,512]{1,0:T(8,128)(2,1)} %copy-done.44, bf16[512,512]{1,0:T(8,128)(2,1)} %get-tuple-element.2489.own, ...), custom_call_target="tpu_custom_call" | custom-call | flops 1 | bytes 1 | tf_op jit(solution)/shard_map/attend_back/pallas_call | solution.py:617
  756.9 14.8 %attend_back.6 = (bf16[512,512]{1,0:T(8,128)(2,1)}, f32[512,512]{1,0:T(8,128)}, bf16[512,512]{1,0:T(8,128)(2,1)}, f32[1,128]{1,0:T(1,128)}) custom-call(s32[2]{0:T(128)} %pad_add_fusion.info, bf16[512,512]{1,0:T(8,128)(2,1)} %get-tuple-element.2502.query, bf16[512,512]{1,0:T(8,128)(2,1)} %collective-permute-done.19.before, ...), custom_call_target="tpu_custom_call" | custom-call | flops 1 | bytes 1 | tf_op jit(solution)/shard_map/attend_back/pallas_call | solution.py:617
  795.4 14.6 %attend_back.7 = (bf16[512,512]{1,0:T(8,128)(2,1)}, f32[512,512]{1,0:T(8,128)}, bf16[512,512]{1,0:T(8,128)(2,1)}, f32[1,128]{1,0:T(1,128)}) custom-call(s32[2]{0:T(128)} %pad_add_fusion.info, bf16[512,512]{1,0:T(8,128)(2,1)} %get-tuple-element.2564.query, bf16[512,512]{1,0:T(8,128)(2,1)} %copy-done.42, bf16[512,512]{1,0:T(8,128)(2,1)} %get-tuple-element.2566.own, ...), custom_call_target="tpu_custom_call" | custom-call | flops 1 | bytes 1 | tf_op jit(solution)/shard_map/attend_back/pallas_call | solution.py:617
  835.3 18.8 %collective-permute-done.58 = bf16[256,768]{1,0:T(8,128)(2,1)S(1)} collective-permute-done((bf16[256,768]{1,0:T(8,128)(2,1)S(1)}, bf16[256,768]{1,0:T(8,128)(2,1)S(1)}, u32[]{:S(2)}, u32[]{:S(2)}) %collective-permute-start.58) | collective-permute-done | bytes 393248 | tf_op jit(solution)/shard_map/ppermute | solution.py:318
  882.1 20.1 %collective-permute-done.64 = bf16[512,1536]{1,0:T(8,128)(2,1)S(1)} collective-permute-done((bf16[512,1536]{1,0:T(8,128)(2,1)}, bf16[512,1536]{1,0:T(8,128)(2,1)S(1)}, u32[]{:S(2)}, u32[]{:S(2)}) %collective-permute-start.64) | collective-permute-done | bytes 1572896 | tf_op jit(solution)/shard_map/ppermute | solution.py:323
  913.8 15.8 %back_to_rows.1 = f32[512,2048]{1,0:T(8,128)} custom-call(bf16[512,512]{1,0:T(8,128)(2,1)} %get-tuple-element.2825.refs_0_, bf16[512,512]{1,0:T(8,128)(2,1)} %get-tuple-element.2759.refs_1_, bf16[512,512]{1,0:T(8,128)(2,1)} %get-tuple-element.2822.refs_2_, bf16[512,512]{1,0:T(8,128)(2,1)} %get-tuple-element.2761.refs_2_.refs_3_, ...), custom_call_target="tpu_custom_call" | custom-call | flops 1 | bytes 1 | tf_op jit(solution)/shard_map/back_to_rows/pallas_call | solution.py:840
  998.8 19.7 %collective-permute-done.80 = bf16[256,2048]{1,0:T(8,128)(2,1)S(1)} collective-permute-done((bf16[256,2048]{1,0:T(8,128)(2,1)S(1)}, bf16[256,2048]{1,0:T(8,128)(2,1)S(1)}, u32[]{:S(2)}, u32[]{:S(2)}) %collective-permute-start.80) | collective-permute-done | bytes 1048608 | tf_op jit(solution)/shard_map/ppermute | solution.py:406
  1018.5 16.2 %collective-permute-start.75 = (f32[4352]{0:T(1024)S(1)}, f32[4352]{0:T(1024)S(1)}, u32[]{:S(2)}, u32[]{:S(2)}) collective-permute-start(f32[4352]{0:T(1024)S(1)} %pad_maximum_fusion.22), channel_id=1, source_target_pairs={{0,4},{4,0},{8,12},{12,8},{16,20},{20,16},{24,28},{28,24},{1,5},{5... | collective-permute-start | bytes 52232 | tf_op jit(solution)/shard_map/ppermute | solution.py:318
  1035.6 32.3 %collective-permute-start.87 = (bf16[256,2048]{1,0:T(8,128)(2,1)S(1)}, bf16[256,2048]{1,0:T(8,128)(2,1)}, u32[]{:S(2)}, u32[]{:S(2)}) collective-permute-start(bf16[256,2048]{1,0:T(8,128)(2,1)S(1)} %get-tuple-element.3047), channel_id=1, source_target_pairs={{1,0},{0,1},{5,2},{4,3},{3,4},{2,5},{7,6},{6,7},{9,8},{8,9},{13,10... | collective-permute-start | bytes 3145736 | tf_op jit(solution)/shard_map/ppermute | solution.py:406
  1075.1 14.1 %collective-permute-done.87 = bf16[256,2048]{1,0:T(8,128)(2,1)} collective-permute-done((bf16[256,2048]{1,0:T(8,128)(2,1)S(1)}, bf16[256,2048]{1,0:T(8,128)(2,1)}, u32[]{:S(2)}, u32[]{:S(2)}) %collective-permute-start.87) | collective-permute-done | bytes 1048608 | tf_op jit(solution)/shard_map/ppermute | solution.py:406
  1090.3 17.8 %whole_columns.5 = (f32[512,6144]{1,0:T(8,128)}, f32[512,6144]{1,0:T(8,128)}) custom-call(s32[1]{0:T(128)} %bitcast.14.me_ref, bf16[2048,1536]{1,0:T(8,128)(2,1)} %copy-done.15, bf16[2048,1536]{1,0:T(8,128)(2,1)} %copy-done.21), custom_call_target="tpu_custom_call" | custom-call | flops 1 | bytes 1 | tf_op jit(solution)/shard_map/whole_columns/pallas_call | solution.py:442
  1130.8 15.8 %collective-permute-done.93 = f32[4352]{0:T(1024)S(1)} collective-permute-done((f32[4352]{0:T(1024)S(1)}, f32[4352]{0:T(1024)S(1)}, u32[]{:S(2)}, u32[]{:S(2)}) %collective-permute-start.93) | collective-permute-done | bytes 17440 | tf_op jit(solution)/shard_map/ppermute | solution.py:1335
  (690 shorter events, 502.0 us)
Async XLA Ops:
  7.2 129.5 %all-gather.3.cloned.1.call-start = ((), (), s32[]{:S(2)}) async-start(), calls=%async_computation | async-start | bytes 1310720 | tf_op jit(solution)/shard_map/all_gather | solution.py:902
  61.4 57.9 %collective-permute-start.4 = (bf16[1536,512]{1,0:T(8,128)(2,1)}, bf16[1536,512]{1,0:T(8,128)(2,1)}, u32[]{:S(2)}, u32[]{:S(2)}) collective-permute-start(bf16[1536,512]{1,0:T(8,128)(2,1)} %pad_maximum_fusion.10.came0.refs_9_), channel_id=1, source_target_pairs={{0,8},{4,12},{8,0},{12,4},{16,24},{20,28},{24,16},{28,20},{1,9},{5... | collective-permute-start | bytes 4718600 | tf_op jit(solution)/shard_map/ppermute | solution.py:318
  62.8 56.4 %collective-permute-start.5 = (bf16[1536,512]{1,0:T(8,128)(2,1)}, bf16[1536,512]{1,0:T(8,128)(2,1)}, u32[]{:S(2)}, u32[]{:S(2)}) collective-permute-start(bf16[1536,512]{1,0:T(8,128)(2,1)} %pad_maximum_fusion.10.came0.refs_9_), channel_id=1, source_target_pairs={{0,16},{4,20},{8,24},{12,28},{16,0},{20,4},{24,8},{28,12},{1,17},{... | collective-permute-start | bytes 4718600 | tf_op jit(solution)/shard_map/ppermute | solution.py:318
  64.4 362.7 %all-gather.5.cloned.1.call-start = ((), (), s32[]{:S(2)}) async-start(), calls=%async_computation.1 | async-start | bytes 11796480 | tf_op jit(solution)/shard_map/all_gather | solution.py:914
  65.4 53.9 %collective-permute-start.7 = (bf16[256,2048]{1,0:T(8,128)(2,1)S(1)}, bf16[256,2048]{1,0:T(8,128)(2,1)S(1)}, u32[]{:S(2)}, u32[]{:S(2)}) collective-permute-start(bf16[256,2048]{1,0:T(8,128)(2,1)S(1)} %get-tuple-element.3073), channel_id=1, source_target_pairs={{0,1},{1,0},{2,5},{3,4},{4,3},{5,2},{6,7},{7,6},{8,9},{9,8},{10,13... | collective-permute-start | bytes 3145736 | tf_op jit(solution)/shard_map/ppermute | solution.py:393
  150.2 58.7 %collective-permute-start.13 = (bf16[1536,512]{1,0:T(8,128)(2,1)S(1)}, bf16[1536,512]{1,0:T(8,128)(2,1)S(1)}, u32[]{:S(2)}, u32[]{:S(2)}) collective-permute-start(bf16[1536,512]{1,0:T(8,128)(2,1)S(1)} %constant_dynamic-update-slice_fusion.came0.refs_21_), channel_id=1, source_target_pairs={{0,4},{4,0},{8,12},{12,8},{16,20},{20,16},{24,28},{28,24},{1,5},{5... | collective-permute-start | bytes 4718600 | tf_op jit(solution)/shard_map/ppermute | solution.py:318
  150.9 58.0 %collective-permute-start.15 = (bf16[2048,256]{1,0:T(8,128)(2,1)S(1)}, bf16[2048,256]{1,0:T(8,128)(2,1)S(1)}, u32[]{:S(2)}, u32[]{:S(2)}) collective-permute-start(bf16[2048,256]{1,0:T(8,128)(2,1)S(1)} %copy-done.28), channel_id=1, source_target_pairs={{0,16},{4,20},{8,24},{12,28},{16,0},{20,4},{24,8},{28,12},{1,17},{... | collective-permute-start | bytes 3145736 | tf_op jit(solution)/shard_map/ppermute | solution.py:318
  152.4 56.5 %collective-permute-start.16 = (bf16[2048,256]{1,0:T(8,128)(2,1)S(1)}, bf16[2048,256]{1,0:T(8,128)(2,1)}, u32[]{:S(2)}, u32[]{:S(2)}) collective-permute-start(bf16[2048,256]{1,0:T(8,128)(2,1)S(1)} %copy-done.28), channel_id=1, source_target_pairs={{0,4},{4,0},{8,12},{12,8},{16,20},{20,16},{24,28},{28,24},{1,5},{5... | collective-permute-start | bytes 3145736 | tf_op jit(solution)/shard_map/ppermute | solution.py:318
  153.9 57.8 %collective-permute-start.20 = (bf16[256,2048]{1,0:T(8,128)(2,1)}, bf16[256,2048]{1,0:T(8,128)(2,1)}, u32[]{:S(2)}, u32[]{:S(2)}) collective-permute-start(bf16[256,2048]{1,0:T(8,128)(2,1)} %get-tuple-element.3066), channel_id=1, source_target_pairs={{0,0},{1,1},{2,4},{3,5},{4,2},{5,3},{6,6},{7,7},{8,8},{9,9},{10,12... | collective-permute-start | bytes 3145736 | tf_op jit(solution)/shard_map/ppermute | solution.py:393
  175.9 91.8 %collective-permute-start.21 = (bf16[256,2048]{1,0:T(8,128)(2,1)}, bf16[256,2048]{1,0:T(8,128)(2,1)}, u32[]{:S(2)}, u32[]{:S(2)}) collective-permute-start(bf16[256,2048]{1,0:T(8,128)(2,1)} %get-tuple-element.3065), channel_id=1, source_target_pairs={{0,1},{1,0},{2,5},{3,4},{4,3},{5,2},{6,7},{7,6},{8,9},{9,8},{10,13... | collective-permute-start | bytes 3145736 | tf_op jit(solution)/shard_map/ppermute | solution.py:393
  209.0 60.8 %collective-permute-start.17 = (bf16[512,512]{1,0:T(8,128)(2,1)S(1)}, bf16[512,512]{1,0:T(8,128)(2,1)S(1)}, u32[]{:S(2)}, u32[]{:S(2)}) collective-permute-start(bf16[512,512]{1,0:T(8,128)(2,1)S(1)} %copy-done.41), channel_id=1, source_target_pairs={{0,4},{8,12},{16,20},{24,28},{1,5},{9,13},{17,21},{25,29},{2,6},{1... | collective-permute-start | bytes 1572872 | tf_op jit(solution)/shard_map/ppermute | solution.py:995
  210.3 61.2 %collective-permute-start.18 = (bf16[512,512]{1,0:T(8,128)(2,1)S(1)}, bf16[512,512]{1,0:T(8,128)(2,1)S(1)}, u32[]{:S(2)}, u32[]{:S(2)}) collective-permute-start(bf16[512,512]{1,0:T(8,128)(2,1)S(1)} %copy-done.43), channel_id=1, source_target_pairs={{0,4},{8,12},{16,20},{24,28},{1,5},{9,13},{17,21},{25,29},{2,6},{1... | collective-permute-start | bytes 1572872 | tf_op jit(solution)/shard_map/ppermute | solution.py:995
  211.6 72.8 %collective-permute-start.24 = (bf16[2048,256]{1,0:T(8,128)(2,1)S(1)}, bf16[2048,256]{1,0:T(8,128)(2,1)S(1)}, u32[]{:S(2)}, u32[]{:S(2)}) collective-permute-start(bf16[2048,256]{1,0:T(8,128)(2,1)S(1)} %collective-permute-done.14.refs_6_.weight0), channel_id=1, source_target_pairs={{0,4},{4,0},{8,12},{12,8},{16,20},{20,16},{24,28},{28,24},{1,5},{5... | collective-permute-start | bytes 3145736 | tf_op jit(solution)/shard_map/ppermute | solution.py:318
  211.7 72.7 %collective-permute-start.25 = (bf16[2048,256]{1,0:T(8,128)(2,1)S(1)}, bf16[2048,256]{1,0:T(8,128)(2,1)S(1)}, u32[]{:S(2)}, u32[]{:S(2)}) collective-permute-start(bf16[2048,256]{1,0:T(8,128)(2,1)S(1)} %collective-permute-done.15.refs_8_.weight0), channel_id=1, source_target_pairs={{0,4},{4,0},{8,12},{12,8},{16,20},{20,16},{24,28},{28,24},{1,5},{5... | collective-permute-start | bytes 3145736 | tf_op jit(solution)/shard_map/ppermute | solution.py:318
  331.3 70.3 %collective-permute-start.32 = (bf16[512,2048]{1,0:T(8,128)(2,1)}, bf16[512,2048]{1,0:T(8,128)(2,1)S(1)}, u32[]{:S(2)}, u32[]{:S(2)}) collective-permute-start(bf16[512,2048]{1,0:T(8,128)(2,1)} %get-tuple-element.2344.refs_0_), channel_id=1, source_target_pairs={{0,8},{4,12},{8,0},{12,4},{16,24},{20,28},{24,16},{28,20},{1,9},{5... | collective-permute-start | bytes 6291464 | tf_op jit(solution)/shard_map/ppermute | solution.py:318
  332.8 69.9 %collective-permute-start.33 = (bf16[512,2048]{1,0:T(8,128)(2,1)}, bf16[512,2048]{1,0:T(8,128)(2,1)S(1)}, u32[]{:S(2)}, u32[]{:S(2)}) collective-permute-start(bf16[512,2048]{1,0:T(8,128)(2,1)} %get-tuple-element.2344.refs_0_), channel_id=1, source_target_pairs={{0,16},{4,20},{8,24},{12,28},{16,0},{20,4},{24,8},{28,12},{1,17},{... | collective-permute-start | bytes 6291464 | tf_op jit(solution)/shard_map/ppermute | solution.py:318
  334.9 66.7 %collective-permute-start.30 = (bf16[256,2048]{1,0:T(8,128)(2,1)S(1)}, bf16[256,2048]{1,0:T(8,128)(2,1)S(1)}, u32[]{:S(2)}, u32[]{:S(2)}) collective-permute-start(bf16[256,2048]{1,0:T(8,128)(2,1)S(1)} %slice.226), channel_id=1, source_target_pairs={{0,16},{4,20},{8,24},{12,28},{16,0},{20,4},{24,8},{28,12},{1,17},{... | collective-permute-start | bytes 3145736 | tf_op jit(solution)/shard_map/ppermute | solution.py:318
  335.1 66.6 %collective-permute-start.31 = (bf16[256,2048]{1,0:T(8,128)(2,1)S(1)}, bf16[256,2048]{1,0:T(8,128)(2,1)S(1)}, u32[]{:S(2)}, u32[]{:S(2)}) collective-permute-start(bf16[256,2048]{1,0:T(8,128)(2,1)S(1)} %slice.227), channel_id=1, source_target_pairs={{0,8},{4,12},{8,0},{12,4},{16,24},{20,28},{24,16},{28,20},{1,9},{5... | collective-permute-start | bytes 3145736 | tf_op jit(solution)/shard_map/ppermute | solution.py:318
  520.8 53.6 %collective-permute-start.38 = (bf16[512,2048]{1,0:T(8,128)(2,1)}, bf16[512,2048]{1,0:T(8,128)(2,1)S(1)}, u32[]{:S(2)}, u32[]{:S(2)}) collective-permute-start(bf16[512,2048]{1,0:T(8,128)(2,1)} %get-tuple-element.2191), channel_id=1, source_target_pairs={{0,8},{4,12},{8,0},{12,4},{16,24},{20,28},{24,16},{28,20},{1,9},{5... | collective-permute-start | bytes 6291464 | tf_op jit(solution)/shard_map/ppermute | solution.py:318
  521.3 53.0 %collective-permute-start.39 = (bf16[512,2048]{1,0:T(8,128)(2,1)}, bf16[512,2048]{1,0:T(8,128)(2,1)S(1)}, u32[]{:S(2)}, u32[]{:S(2)}) collective-permute-start(bf16[512,2048]{1,0:T(8,128)(2,1)} %get-tuple-element.2192), channel_id=1, source_target_pairs={{0,16},{4,20},{8,24},{12,28},{16,0},{20,4},{24,8},{28,12},{1,17},{... | collective-permute-start | bytes 6291464 | tf_op jit(solution)/shard_map/ppermute | solution.py:318
  574.4 86.0 %collective-permute-start.42 = (bf16[2048,1536]{1,0:T(8,128)(2,1)}, bf16[2048,1536]{1,0:T(8,128)(2,1)}, u32[]{:S(2)}, u32[]{:S(2)}) collective-permute-start(bf16[2048,1536]{1,0:T(8,128)(2,1)} %row_outer.14), channel_id=1, source_target_pairs={{0,4},{4,0},{8,12},{12,8},{16,20},{20,16},{24,28},{28,24},{1,5},{5... | collective-permute-start | bytes 18874376 | tf_op jit(solution)/shard_map/ppermute | solution.py:318
  577.5 82.9 %collective-permute-start.43 = (bf16[256,2048]{1,0:T(8,128)(2,1)}, bf16[256,2048]{1,0:T(8,128)(2,1)S(1)}, u32[]{:S(2)}, u32[]{:S(2)}) collective-permute-start(bf16[256,2048]{1,0:T(8,128)(2,1)} %get-tuple-element.3062), channel_id=1, source_target_pairs={{0,8},{4,12},{8,0},{12,4},{16,24},{20,28},{24,16},{28,20},{1,9},{5... | collective-permute-start | bytes 3145736 | tf_op jit(solution)/shard_map/ppermute | solution.py:318
  578.9 81.5 %collective-permute-start.44 = (bf16[256,2048]{1,0:T(8,128)(2,1)}, bf16[256,2048]{1,0:T(8,128)(2,1)S(1)}, u32[]{:S(2)}, u32[]{:S(2)}) collective-permute-start(bf16[256,2048]{1,0:T(8,128)(2,1)} %get-tuple-element.3061), channel_id=1, source_target_pairs={{0,16},{4,20},{8,24},{12,28},{16,0},{20,4},{24,8},{28,12},{1,17},{... | collective-permute-start | bytes 3145736 | tf_op jit(solution)/shard_map/ppermute | solution.py:318
  580.9 67.5 %collective-permute-start.40 = (bf16[512,768]{1,0:T(8,128)(2,1)}, bf16[512,768]{1,0:T(8,128)(2,1)}, u32[]{:S(2)}, u32[]{:S(2)}) collective-permute-start(bf16[512,768]{1,0:T(8,128)(2,1)} %get-tuple-element.3040), channel_id=1, source_target_pairs={{0,1},{1,2},{2,3},{3,0},{4,5},{5,6},{6,7},{7,4},{8,9},{9,10},{10,1... | collective-permute-start | bytes 2359304 | tf_op jit(solution)/shard_map/ppermute | solution.py:323
  669.6 65.2 %collective-permute-start.46 = (bf16[512,2048]{1,0:T(8,128)(2,1)}, bf16[512,2048]{1,0:T(8,128)(2,1)}, u32[]{:S(2)}, u32[]{:S(2)}) collective-permute-start(bf16[512,2048]{1,0:T(8,128)(2,1)} %get-tuple-element.2369), channel_id=1, source_target_pairs={{0,8},{4,12},{8,0},{12,4},{16,24},{20,28},{24,16},{28,20},{1,9},{5... | collective-permute-start | bytes 6291464 | tf_op jit(solution)/shard_map/ppermute | solution.py:318
  670.9 63.9 %collective-permute-start.47 = (bf16[512,2048]{1,0:T(8,128)(2,1)}, bf16[512,2048]{1,0:T(8,128)(2,1)}, u32[]{:S(2)}, u32[]{:S(2)}) collective-permute-start(bf16[512,2048]{1,0:T(8,128)(2,1)} %get-tuple-element.2370), channel_id=1, source_target_pairs={{0,16},{4,20},{8,24},{12,28},{16,0},{20,4},{24,8},{28,12},{1,17},{... | collective-permute-start | bytes 6291464 | tf_op jit(solution)/shard_map/ppermute | solution.py:318
  741.3 72.9 %collective-permute-start.54 = (bf16[512,1536]{1,0:T(8,128)(2,1)}, bf16[512,1536]{1,0:T(8,128)(2,1)}, u32[]{:S(2)}, u32[]{:S(2)}) collective-permute-start(bf16[512,1536]{1,0:T(8,128)(2,1)} %get-tuple-element.3032), channel_id=1, source_target_pairs={{0,1},{1,2},{2,3},{3,0},{4,5},{5,6},{6,7},{7,4},{8,9},{9,10},{10,1... | collective-permute-start | bytes 4718600 | tf_op jit(solution)/shard_map/ppermute | solution.py:323
  992.3 75.7 %collective-permute-start.76 = (bf16[2048,1536]{1,0:T(8,128)(2,1)S(1)}, bf16[2048,1536]{1,0:T(8,128)(2,1)S(1)}, u32[]{:S(2)}, u32[]{:S(2)}) collective-permute-start(bf16[2048,1536]{1,0:T(8,128)(2,1)S(1)} %constant_dynamic-update-slice_fusion.9.own_ref), channel_id=1, source_target_pairs={{0,4},{4,0},{8,12},{12,8},{16,20},{20,16},{24,28},{28,24},{1,5},{5... | collective-permute-start | bytes 18874376 | tf_op jit(solution)/shard_map/ppermute | solution.py:318
  994.3 73.7 %collective-permute-start.77 = (bf16[1024,512]{1,0:T(8,128)(2,1)S(1)}, bf16[1024,512]{1,0:T(8,128)(2,1)S(1)}, u32[]{:S(2)}, u32[]{:S(2)}) collective-permute-start(bf16[1024,512]{1,0:T(8,128)(2,1)S(1)} %copy-done.139), channel_id=1, source_target_pairs={{0,8},{4,12},{8,0},{12,4},{16,24},{20,28},{24,16},{28,20},{1,9},{5... | collective-permute-start | bytes 3145736 | tf_op jit(solution)/shard_map/ppermute | solution.py:318
  995.4 72.6 %collective-permute-start.78 = (bf16[1024,512]{1,0:T(8,128)(2,1)S(1)}, bf16[1024,512]{1,0:T(8,128)(2,1)S(1)}, u32[]{:S(2)}, u32[]{:S(2)}) collective-permute-start(bf16[1024,512]{1,0:T(8,128)(2,1)S(1)} %copy-done.140), channel_id=1, source_target_pairs={{0,16},{4,20},{8,24},{12,28},{16,0},{20,4},{24,8},{28,12},{1,17},{... | collective-permute-start | bytes 3145736 | tf_op jit(solution)/shard_map/ppermute | solution.py:318
  997.0 77.4 %collective-permute-start.86 = (bf16[256,2048]{1,0:T(8,128)(2,1)S(1)}, bf16[256,2048]{1,0:T(8,128)(2,1)}, u32[]{:S(2)}, u32[]{:S(2)}) collective-permute-start(bf16[256,2048]{1,0:T(8,128)(2,1)S(1)} %get-tuple-element.3048), channel_id=1, source_target_pairs={{0,0},{1,1},{4,2},{5,3},{2,4},{3,5},{6,6},{7,7},{8,8},{9,9},{12,10... | collective-permute-start | bytes 3145736 | tf_op jit(solution)/shard_map/ppermute | solution.py:406
  1035.6 53.6 %collective-permute-start.87 = (bf16[256,2048]{1,0:T(8,128)(2,1)S(1)}, bf16[256,2048]{1,0:T(8,128)(2,1)}, u32[]{:S(2)}, u32[]{:S(2)}) collective-permute-start(bf16[256,2048]{1,0:T(8,128)(2,1)S(1)} %get-tuple-element.3047), channel_id=1, source_target_pairs={{1,0},{0,1},{5,2},{4,3},{3,4},{2,5},{7,6},{6,7},{9,8},{8,9},{13,10... | collective-permute-start | bytes 3145736 | tf_op jit(solution)/shard_map/ppermute | solution.py:406
  (221 other events, 3785.1 us)
Sparse Core Ops, SparseCore 0:
  64.5 38.2 all-gather.2
  119.4 219.1 all-gather.4

commit v7 on v6

--- a/solution.py
+++ b/solution.py
@@ -340,14 +340,6 @@
             first = lax.optimization_barrier((first, last))[0]
         outs.append(call(first, *rest))
     return outs
-
-
-def ring_chunks(x):
-    count, at = lax.axis_size("shard"), lax.axis_index("shard")
-    rows = x.shape[0] // count
-    return [
-        lax.dynamic_slice_in_dim(x, ((at - i) % count) * rows, rows, 0) for i in range(count)
-    ]
 
 
 def ring_sum_first(chunks):
@@ -705,7 +697,7 @@
     )(*args)
 
 
-def row_outer(lefts, groups, first, tiles, added=None, places=None):
+def row_outer(lefts, groups, first, tiles, added=None, places=None, part=None):
     rights = [right for group in groups for right in group]
     places = range(len(rights)) if places is None else places
     added = [] if added is None else [added] * len(rights)
@@ -713,7 +705,8 @@
     tile = width // 8
     count = len(lefts)
     rows = sum(left.shape[0] for left in lefts)
-    columns = [sum(right.shape[1] for right in group) for group in groups]
+    wide = rights[0].shape[1] // (1 if part is None else 2)
+    columns = [wide * len(group) for group in groups]
 
     def body(*refs):
         left_refs = refs[:count]
@@ -723,8 +716,8 @@
         place = 0
         for i, group in enumerate(groups):
             column = 0
-            for right in group:
-                on = slice(column, column + right.shape[1])
+            for _ in group:
+                on = slice(column, column + wide)
                 total, start = 0.0, 0
                 for left in left_refs:
                     stop = start + left.shape[0]
@@ -734,7 +727,7 @@
                     total = total + add_refs[place][...].astype(jnp.float32)
                 outs[i][:, on] = total.astype(jnp.bfloat16)
                 place += 1
-                column += right.shape[1]
+                column += wide
 
     return pl.pallas_call(
         body,
@@ -743,11 +736,13 @@
         in_specs=[
             *(pl.BlockSpec((left.shape[0], tile), lambda j: (0, j + first)) for left in lefts),
             *(
-                pl.BlockSpec(right.shape, lambda j: (0, 0), pipeline_mode=pl.Buffered(1))
+                pl.BlockSpec(
+                    (right.shape[0], wide), lambda j: (0, part or 0), pipeline_mode=pl.Buffered(1)
+                )
                 for right in rights
             ),
             *(
-                pl.BlockSpec((tile, rights[0].shape[1]), lambda j, at=at: (j + first, at))
+                pl.BlockSpec((tile, wide), lambda j, at=at: (j + first, at))
                 for at in places[: len(added)]
             ),
         ],
@@ -911,7 +906,6 @@
     del s.before, s.behind, s.ahead
     s.end()
 
-    ffn_own = lax.all_gather(s.ffn_block, "shard", axis=0, tiled=True)
     grad_y_sent = to_sequences_send(s.cotangent)
     s.came_far = far(*s.came_near)
     s.came_other = [across(block, CORE) for block in (s.came, *s.came_near)]
@@ -939,7 +933,7 @@
     s.cosine, sine = cosine[0, :, 0], sine[0, :, 0]
     s.sine = jnp.concatenate([-sine[:, : head_dim // 2], sine[:, head_dim // 2 :]], 1)
     s.out_own = out_own
-    del s.gains, s.x_came, s.other_lengths, s.ffn_block, s.cotangent
+    del s.gains, s.x_came, s.other_lengths, s.cotangent
     s.end()
 
     head_columns = 2 * head_dim
@@ -987,14 +981,16 @@
             for i, (block, other) in enumerate(zip((s.came, *s.came_near), s.came_other))
         ]
     )
+    s.grad_y_came = grad_y_sent
     del s.came_far
     s.end()
 
+    ffn_own = lax.all_gather(s.ffn_block, "shard", axis=0, tiled=True)
     s.out_far = far(*s.out_near)
     s.out_near_other = [across(block, CORE) for block in s.out_near]
     s.earlier = [lax.ppermute(p[2], "rep", upward) for p in s.projected]
     (s.projected_last,) = in_order([project_call(3, *s.came_last)])
-    s.grad_y_came = grad_y_sent
+    del s.ffn_block
     s.end()
 
     grad_y = jnp.concatenate(in_turn(s.grad_y_came), 0)
@@ -1102,8 +1098,7 @@
     del s.mid_sent, s.down_came
     s.end()
 
-    s.down_chunks = ring_chunks(s.down_mine)
-    s.down_ring = ring_sum_first(s.down_chunks)
+    down_total = lax.psum_scatter(s.down_mine, "shard", scatter_dimension=0, tiled=True)
     s.mid_came_far = send_far(s.mid_came, by_rows(s.mid_rest[0]), by_rows)
     s.gate_up_came = across(s.gate_up_outer, CORE)
     s.mlp_sent, s.mlp_rest = in_order(
@@ -1116,7 +1111,6 @@
     s.end()
 
     mlp_came = send_near(s.mlp_sent)
-    s.down_last = around(rounded_sum(s.down_chunks[3], s.down_ring[0]), 1)
     grad_mid = total(s.mid_came, s.mid_came_far, by_rows(s.mid_rest[1]), by_rows)
     inverse_mid = lax.rsqrt(jnp.mean(s.resid * s.resid, -1, keepdims=True) + EPS)
     mid_unit = s.resid * inverse_mid
@@ -1150,27 +1144,26 @@
             i: lax.ppermute(s.backs[i][2], "rep", downward) for i in chips
         }
 
-    def odd_call(left, blocks):
-        return lambda first: row_outer([first], [blocks], 0, 8)[0], left
-
-    def head_call(left, blocks, came):
+    def odd_call(left, blocks, part=None):
+        return lambda first: row_outer([first], [blocks], 0, 8, part=part)[0], left
+
+    def head_call(left, blocks, came, part=None, places=(0, 1, 2, 3)):
         groups = [[blocks[1], blocks[3]], [blocks[2]], [blocks[0]]]
-        return lambda first: row_outer([first], groups, 0, 4, came, (1, 3, 2, 0)), left
-
-    def tail_call(left, blocks, came):
+        at = [places[i] for i in (1, 3, 2, 0)]
+        return lambda first: row_outer([first], groups, 0, 4, came, at, part), left
+
+    def tail_call(left, blocks, came, part=None, places=(0, 1, 2, 3)):
         groups = [[blocks[2], blocks[3]], [blocks[1]], [blocks[0]]]
-        return lambda first: row_outer([first], groups, 4, 4, came, (2, 3, 1, 0)), left
-
-    s.down_total = rounded_sum(s.down_chunks[0], s.down_ring[1], s.down_last)
-    s.gate_up_chunks = ring_chunks(s.gate_up_mine)
-    gate_up_ring = ring_sum_first(s.gate_up_chunks)
-    mixed_even = [m[:, :head_columns] for m in s.mixed]
-    mixed_odd = [m[:, head_columns:] for m in s.mixed]
+        at = [places[i] for i in (2, 3, 1, 0)]
+        return lambda first: row_outer([first], groups, 4, 4, came, at, part), left
+
+    gate_up_total = lax.psum_scatter(s.gate_up_mine, "shard", scatter_dimension=0, tiled=True)
     s.returned = {}
-    s.out_odd, back = in_order([odd_call(s.resid_rolled, mixed_odd), back_call(3)])
+    s.out_odd, back = in_order([odd_call(s.resid_rolled, s.mixed, 1), back_call(3)])
     s.backs = {3: back}
     s.mlp_came = mlp_came
-    del s.gate_up_mine, s.mlp_sent, s.down_chunks, s.down_ring, s.down_last
+    s.down_total = down_total
+    del s.gate_up_mine, s.mlp_sent
     s.end()
 
     s.mlp_came_far = send_far(s.mlp_came, by_rows(s.mlp_rest[0]), by_rows)
@@ -1187,24 +1180,24 @@
     s.output = (s.valid * (s.resid + mlp_out)).astype(low)
     s.out_head, s.out_tail, back, finished = in_order(
         [
-            head_call(s.resid_rolled, mixed_even, s.out_came),
-            tail_call(s.resid_rolled, mixed_even, s.out_came),
+            head_call(s.resid_rolled, s.mixed, s.out_came, 0),
+            tail_call(s.resid_rolled, s.mixed, s.out_came, 0),
             back_call(0),
             finish_call(3),
         ]
     )
     s.backs = s.backs | {0: back}
     s.finished = {3: finished}
-    s.gate_up_ring = gate_up_ring
     del s.mlp_came, s.mlp_came_far, s.mlp_rest, s.out_came, s.resid
     s.end()
 
-    gate_up_last = around(rounded_sum(s.gate_up_chunks[3], s.gate_up_ring[0]), 1)
+    output_sent = from_sequences_send(s.output)
     s.out_near = send_near((s.out_head[0], s.out_tail[0]))
     s.down_far = far(*s.down_near)
     give_back(0)
     finished1, finished2 = in_order([finish_call(1), finish_call(2)])
     s.finished = s.finished | {1: finished1, 2: finished2}
+    del s.output
     s.end()
 
     s.out_far = send_far(s.out_near, (s.out_tail[1], s.out_head[1]), by_columns)
@@ -1213,7 +1206,7 @@
     (finished,) = in_order([finish_call(0)])
     s.finished = s.finished | {0: finished}
     (s.qkv_odd,) = in_order([odd_call(s.normed, [s.finished[i][1] for i in range(4)])])
-    s.gate_up_last = gate_up_last
+    s.gate_up_total = gate_up_total
     del s.down_total, s.down_near, s.down_far
     s.end()
 
@@ -1223,9 +1216,7 @@
         return lambda first: whole_columns(my_group, first, other, widths), own
 
     s.qkv_came = across(s.qkv_odd, CORE)
-    s.gate_up_total = rounded_sum(s.gate_up_chunks[0], s.gate_up_ring[1], s.gate_up_last)
     s.gate_up_near = near(s.gate_up_total)
-    output_sent = from_sequences_send(s.output)
     out_sum = total(s.out_near, s.out_far, (s.out_head[2], s.out_tail[2]), by_columns)
     s.out_chunks = jnp.split(out_sum.astype(low), shards, 0)
     s.out_ring = ring_sum_first(s.out_chunks)
@@ -1247,7 +1238,7 @@
     s.grad_tokens = (
         s.grad_resid + norm_back(x_unit, s.inverse_in, grad_in * s.attn_gains)
     ).astype(low)
-    del s.gate_up_chunks, s.gate_up_ring, s.gate_up_last, s.output
+    s.output_came = output_sent
     del s.qkv_odd, s.out_near, s.out_far, s.out_head, s.out_tail, s.down_own, s.down_other
     del s.own_blocks, s.came, s.came_near, s.came_other, s.came_last, s.grad_resid, s.x_low
     s.end()
@@ -1255,23 +1246,9 @@
     s.gate_up_far = far(*s.gate_up_near)
     s.out_ring_last = around(rounded_sum(s.out_chunks[3], s.out_ring[0]), 1)
     even = [s.finished[i][0] for i in range(4)]
-    halves = [
-        [block[:, half * head_columns : (half + 1) * head_columns] for block in even]
-        for half in range(2)
-    ]
-    came_halves = [
-        jnp.concatenate(
-            [
-                s.qkv_came[:, i * block_columns + half * head_columns :][:, :head_columns]
-                for i in range(4)
-            ],
-            1,
-        )
-        for half in range(2)
-    ]
     first_head, first_tail, second_head, second_tail = in_order(
         [
-            call(s.normed, halves[half], came_halves[half])
+            call(s.normed, even, s.qkv_came, half, range(half, 8, 2))
             for half in range(2)
             for call in (head_call, tail_call)
         ]
@@ -1307,7 +1284,6 @@
     s.out_total = rounded_sum(s.out_chunks[0], s.out_ring[1], s.out_ring_last)
     s.gain_came = across(s.gain_parts, CORE)
     del s.out_chunks, s.out_ring, s.out_ring_last, s.gate_up_near, s.gate_up_far
-    s.output_came = output_sent
     del s.gate_up_total, s.grad_tokens
     s.end()
 
@@ -1316,7 +1292,6 @@
     s.gain_parts = s.gain_parts + s.gain_came
     s.gain_came = across(s.gain_parts, ACROSS_X)
     (s.whole_gate_up,) = in_order([whole_call((units, units), s.gate_up_own, s.gate_up_other)])
-    s.tokens_came = grad_tokens_sent
     del s.gate_up_own, s.gate_up_other
     s.end()
 
@@ -1326,6 +1301,7 @@
     s.gain_parts = s.gain_parts + s.gain_came
     s.gain_came = across(s.gain_parts, ACROSS_Y)
     del s.near0, s.far0
+    s.tokens_came = grad_tokens_sent
     s.end()
 
     s.last0 = around(rounded_sum(s.chunks0[3], s.ring0[0]), 1)

time: 1220 us -> 1070 us (0.88)
  starting transfers between devices: 251 us -> 153 us
  waiting for transfers between devices: 345 us -> 322 us
  other arithmetic: 82.2 us -> 67.6 us
  local copies, waits for them, and re-layouts: 79.8 us -> 65.8 us
    ppermute x18 -> x12, starting transfers between devices: 70.6 us -> 34.1 us  [around(): lax.ppermute(x, 'shard', [(i, (i + by) % count) for i in range(count)])]
    ppermute x4, starting transfers between devices: 34.9 us -> 8.3 us  [from_sequences_send(): lax.ppermute(lax.dynamic_index_in_dim(x, turn ^ odd, 0, keepdims=False),...]
    ppermute x4, waiting for transfers between devices: 70.6 us -> 44 us  [to_sequences_send(): lax.ppermute(lax.dynamic_index_in_dim(x, turn ^ odd, 0, keepdims=False),...]
    ppermute x73, waiting for transfers between devices: 155 us -> 182 us  [across(): return lax.ppermute(x, 'rep', [(i, i ^ mask) for i in range(count)])]
    ppermute x73, starting transfers between devices: 109 us -> 83.2 us  [across(): return lax.ppermute(x, 'rep', [(i, i ^ mask) for i in range(count)])]
    ppermute x4, waiting for transfers between devices: 33.8 us -> 15.6 us  [from_sequences_send(): lax.ppermute(lax.dynamic_index_in_dim(x, turn ^ odd, 0, keepdims=False),...]
    unnamed x300 -> x272, local copies, waits for them, and re-layouts: 24 us -> 29.4 us
    ppermute x18 -> x12, waiting for transfers between devices: 62.2 us -> 58 us  [around(): lax.ppermute(x, 'shard', [(i, (i + by) % count) for i in range(count)])]
  transfers between devices with their start and end apart: 111 -> 107, of which waited for: 32 -> 34; matrix products, arithmetic and copies ran while one was open for 9% -> 8% of each run, Pallas kernels for 32% -> 37%
where the time goes in v7:
time: 1070 us; the launch traced here: 1060 us
  Pallas kernels  438 us (41%)
  waiting for transfers between devices  322 us (30%)
  starting transfers between devices  153 us (14%)
  other arithmetic  67.6 us (6%)
  local copies, waits for them, and re-layouts  65.8 us (6%)
  between operations  16.5 us (2%)
    ppermute x73, waiting for transfers between devices, across(): return lax.ppermute(x, 'rep', [(i, i ^ mask) for i in range(count)])  182 us
    pallas_call x16, Pallas kernels, call(): pl.pallas_call(body, grid=(1,), out_shape=outs, in_specs=in_specs, out_sp...  132 us
    pallas_call x12, Pallas kernels, row_outer(): pl.pallas_call(body, grid=(tiles,), out_shape=[jax.ShapeDtypeStruct((tile...  115 us
    ppermute x73, starting transfers between devices, across(): return lax.ppermute(x, 'rep', [(i, i ^ mask) for i in range(count)])  83.2 us
    pallas_call x4, Pallas kernels, from_hidden(): pl.pallas_call(body, grid=(4,), out_shape=[jax.ShapeDtypeStruct((2 * rows...  59.9 us
    pallas_call x2, Pallas kernels, hidden_units(): pl.pallas_call(body, grid=(3,), out_shape=[jax.ShapeDtypeStruct((rows, un...  59.5 us
    ppermute x12, waiting for transfers between devices, around(): lax.ppermute(x, 'shard', [(i, (i + by) % count) for i in range(count)])  58 us
    pallas_call x4, Pallas kernels, whole_columns(): pl.pallas_call(body, grid_spec=pltpu.PrefetchScalarGridSpec(num_scalar_pr...  44.3 us
  transfers between devices with their start and end apart: 107, of which 34 were waited for; matrix products, arithmetic and copies ran while one was open for 8% of the time, Pallas kernels for 37%

profile of v7, /device:TPU:0, one launch (start us, length us, event | category | flops | bytes accessed | tf_op | source)
XLA Modules:
  0.0 1062.9 jit_solution(1059774441359489313)
XLA Ops:
  32.0 11.3 %collective-permute-done = bf16[528,512]{1,0:T(8,128)(2,1)} collective-permute-done((bf16[528,512]{1,0:T(8,128)(2,1)}, bf16[528,512]{1,0:T(8,128)(2,1)}, u32[]{:S(2)}, u32[]{:S(2)}) %collective-permute-start) | collective-permute-done | bytes 540704 | tf_op jit(solution)/shard_map/ppermute | solution.py:323
  45.0 13.5 %collective-permute-done.3 = bf16[528,512]{1,0:T(8,128)(2,1)S(1)} collective-permute-done((bf16[528,512]{1,0:T(8,128)(2,1)}, bf16[528,512]{1,0:T(8,128)(2,1)S(1)}, u32[]{:S(2)}, u32[]{:S(2)}) %collective-permute-start.3) | collective-permute-done | bytes 540704 | tf_op jit(solution)/shard_map/ppermute | solution.py:323
  74.0 34.4 %collective-permute-done.7 = bf16[256,2048]{1,0:T(8,128)(2,1)S(1)} collective-permute-done((bf16[256,2048]{1,0:T(8,128)(2,1)}, bf16[256,2048]{1,0:T(8,128)(2,1)S(1)}, u32[]{:S(2)}, u32[]{:S(2)}) %collective-permute-start.7) | collective-permute-done | bytes 1048608 | tf_op jit(solution)/shard_map/ppermute | solution.py:385
  110.9 22.1 %collective-permute-start.11 = (bf16[1536,512]{1,0:T(8,128)(2,1)}, bf16[1536,512]{1,0:T(8,128)(2,1)}, u32[]{:S(2)}, u32[]{:S(2)}) collective-permute-start(bf16[1536,512]{1,0:T(8,128)(2,1)} %collective-permute-done.4.came0.refs_13_), channel_id=1, source_target_pairs={{0,4},{4,0},{8,12},{12,8},{16,20},{20,16},{24,28},{28,24},{1,5},{5... | collective-permute-start | bytes 4718600 | tf_op jit(solution)/shard_map/ppermute | solution.py:318
  145.2 11.1 %collective-permute-done.9 = bf16[768,512]{1,0:T(8,128)(2,1)} collective-permute-done((bf16[768,512]{1,0:T(8,128)(2,1)S(1)}, bf16[768,512]{1,0:T(8,128)(2,1)}, u32[]{:S(2)}, u32[]{:S(2)}) %collective-permute-start.9) | collective-permute-done | bytes 786464 | tf_op jit(solution)/shard_map/ppermute | solution.py:318
  267.1 11.7 %close_attention.1 = (f32[512,2048]{1,0:T(8,128)}, bf16[512,2048]{1,0:T(8,128)(2,1)}) custom-call(bf16[512,2048]{1,0:T(8,128)(2,1)} %pad_maximum_fusion.3.x, bf16[512,512]{1,0:T(8,128)(2,1)} %get-tuple-element.2554.refs_0_.refs_1_.refs_4_, bf16[512,512]{1,0:T(8,128)(2,1)} %get-tuple-element.2551.refs_1_.refs_2_.refs_3_, ...), custom_call_target="tpu_custom_call" | custom-call | flops 1 | bytes 1 | tf_op jit(solution)/shard_map/close_attention/pallas_call | solution.py:782
  283.5 65.2 %collective-permute-done.31.refs_9_.refs_4_ = bf16[256,2048]{1,0:T(8,128)(2,1)S(1)} collective-permute-done((bf16[256,2048]{1,0:T(8,128)(2,1)S(1)}, bf16[256,2048]{1,0:T(8,128)(2,1)S(1)}, u32[]{:S(2)}, u32[]{:S(2)}) %collective-permute-start.31) | collective-permute-done | bytes 1048608 | tf_op jit(solution)/shard_map/ppermute | solution.py:318
  354.0 20.2 %collective-permute-done.35.refs_4_ = bf16[256,2048]{1,0:T(8,128)(2,1)S(1)} collective-permute-done((bf16[256,2048]{1,0:T(8,128)(2,1)S(1)}, bf16[256,2048]{1,0:T(8,128)(2,1)S(1)}, u32[]{:S(2)}, u32[]{:S(2)}) %collective-permute-start.35) | collective-permute-done | bytes 1048608 | tf_op jit(solution)/shard_map/ppermute | solution.py:318
  376.7 29.6 %hidden_units.2 = (bf16[2048,768]{1,0:T(8,128)(2,1)}, bf16[2048,768]{1,0:T(8,128)(2,1)}, bf16[2048,768]{1,0:T(8,128)(2,1)}) custom-call(bf16[512,2048]{1,0:T(8,128)(2,1)} %get-tuple-element.2336.refs_0_, bf16[512,2048]{1,0:T(8,128)(2,1)} %copy-done.11, bf16[512,2048]{1,0:T(8,128)(2,1)} %copy-done.10, bf16[256,2048]{1,0:T(8,128)(2,1)} %copy-done.24, ...), custom_call_target="tpu_custom_call" | custom-call | flops 1 | bytes 1 | tf_op jit(solution)/shard_map/hidden_units/pallas_call | solution.py:649
  406.3 29.9 %hidden_units.3 = (bf16[2048,768]{1,0:T(8,128)(2,1)}, bf16[2048,768]{1,0:T(8,128)(2,1)}, bf16[2048,768]{1,0:T(8,128)(2,1)}) custom-call(bf16[512,2048]{1,0:T(8,128)(2,1)} %get-tuple-element.2336.refs_0_, bf16[512,2048]{1,0:T(8,128)(2,1)} %copy-done.11, bf16[512,2048]{1,0:T(8,128)(2,1)} %copy-done.10, bf16[256,2048]{1,0:T(8,128)(2,1)} %copy-done.24, ...), custom_call_target="tpu_custom_call" | custom-call | flops 1 | bytes 1 | tf_op jit(solution)/shard_map/hidden_units/pallas_call | solution.py:649
  436.2 12.6 %row_outer.12 = bf16[2048,768]{1,0:T(8,128)(2,1)} custom-call(bf16[512,2048]{1,0:T(8,128)(2,1)} %copy-done.6, bf16[512,2048]{1,0:T(8,128)(2,1)} %copy-done.13, bf16[512,2048]{1,0:T(8,128)(2,1)} %copy-done.12, bf16[256,2048]{1,0:T(8,128)(2,1)} %copy-done.26, bf16[256,2048]{1,0:T(8,128)(2,1)} %copy-done.25, ...), custom_call_target="tpu_custom_call" | custom-call | flops 6442450944 | bytes 11534336 | tf_op jit(solution)/shard_map/row_outer/pallas_call | solution.py:732
  448.8 19.0 %from_hidden.4 = (bf16[512,2048]{1,0:T(8,128)(2,1)}, bf16[512,2048]{1,0:T(8,128)(2,1)}) custom-call(bf16[2048,768]{1,0:T(8,128)(2,1)} %get-tuple-element.2341.refs_0_.refs_1_.refs_2_.refs_3_.refs_5_, bf16[2048,768]{1,0:T(8,128)(2,1)} %get-tuple-element.2341.refs_0_.refs_1_.refs_2_.refs_3_.refs_5_, ...), custom_call_target="tpu_custom_call" | custom-call | flops 1 | bytes 1 | tf_op jit(solution)/shard_map/from_hidden/pallas_call | solution.py:688
  469.7 13.2 %row_outer.13 = bf16[2048,768]{1,0:T(8,128)(2,1)} custom-call(bf16[512,2048]{1,0:T(8,128)(2,1)} %copy-done.6, bf16[512,2048]{1,0:T(8,128)(2,1)} %copy-done.13, bf16[512,2048]{1,0:T(8,128)(2,1)} %copy-done.12, bf16[256,2048]{1,0:T(8,128)(2,1)} %copy-done.26, bf16[256,2048]{1,0:T(8,128)(2,1)} %copy-done.25, ...), custom_call_target="tpu_custom_call" | custom-call | flops 6442450944 | bytes 11534336 | tf_op jit(solution)/shard_map/row_outer/pallas_call | solution.py:732
  482.9 18.8 %from_hidden.5 = (bf16[512,2048]{1,0:T(8,128)(2,1)}, bf16[512,2048]{1,0:T(8,128)(2,1)}) custom-call(bf16[2048,768]{1,0:T(8,128)(2,1)} %get-tuple-element.2341.refs_0_.refs_1_.refs_2_.refs_3_.refs_5_, bf16[2048,768]{1,0:T(8,128)(2,1)} %get-tuple-element.2341.refs_0_.refs_1_.refs_2_.refs_3_.refs_5_, ...), custom_call_target="tpu_custom_call" | custom-call | flops 1 | bytes 1 | tf_op jit(solution)/shard_map/from_hidden/pallas_call | solution.py:688
  501.7 19.7 %row_outer.14 = bf16[2048,1536]{1,0:T(8,128)(2,1)} custom-call(bf16[512,2048]{1,0:T(8,128)(2,1)} %get-tuple-element.2336.refs_0_, bf16[512,2048]{1,0:T(8,128)(2,1)} %copy-done.11, bf16[512,2048]{1,0:T(8,128)(2,1)} %copy-done.10, bf16[256,2048]{1,0:T(8,128)(2,1)} %copy-done.24, bf16[256,2048]{1,0:T(8,128)(2,1)} %copy-done.23, ...), custom_call_target="tpu_custom_call" | custom-call | flops 12884901888 | bytes 14680064 | tf_op jit(solution)/shard_map/row_outer/pallas_call | solution.py:732
  529.0 11.2 %from_hidden.6 = (bf16[512,2048]{1,0:T(8,128)(2,1)}, bf16[512,2048]{1,0:T(8,128)(2,1)}) custom-call(bf16[2048,768]{1,0:T(8,128)(2,1)} %get-tuple-element.2277.refs_5_.refs_0_.refs_1_.refs_2_.refs_3_, bf16[2048,768]{1,0:T(8,128)(2,1)} %get-tuple-element.2277.refs_5_.refs_0_.refs_1_.refs_2_.refs_3_, ...), custom_call_target="tpu_custom_call" | custom-call | flops 1 | bytes 1 | tf_op jit(solution)/shard_map/from_hidden/pallas_call | solution.py:688
  566.1 19.7 %row_outer.15 = bf16[2048,1536]{1,0:T(8,128)(2,1)} custom-call(bf16[512,2048]{1,0:T(8,128)(2,1)} %get-tuple-element.2336.refs_0_, bf16[512,2048]{1,0:T(8,128)(2,1)} %copy-done.11, bf16[512,2048]{1,0:T(8,128)(2,1)} %copy-done.10, bf16[256,2048]{1,0:T(8,128)(2,1)} %copy-done.24, bf16[256,2048]{1,0:T(8,128)(2,1)} %copy-done.23, ...), custom_call_target="tpu_custom_call" | custom-call | flops 12884901888 | bytes 14680064 | tf_op jit(solution)/shard_map/row_outer/pallas_call | solution.py:732
  598.1 15.0 %attend_back.4 = (bf16[512,512]{1,0:T(8,128)(2,1)}, f32[512,512]{1,0:T(8,128)}, bf16[512,512]{1,0:T(8,128)(2,1)}, f32[1,128]{1,0:T(1,128)}) custom-call(s32[2]{0:T(128)} %pad_add_fusion.info, bf16[512,512]{1,0:T(8,128)(2,1)} %get-tuple-element.2411.query, bf16[512,512]{1,0:T(8,128)(2,1)} %collective-permute-done.26.before, ...), custom_call_target="tpu_custom_call" | custom-call | flops 1 | bytes 1 | tf_op jit(solution)/shard_map/attend_back/pallas_call | solution.py:609
  621.4 14.6 %attend_back.5 = (bf16[512,512]{1,0:T(8,128)(2,1)}, f32[512,512]{1,0:T(8,128)}, bf16[512,512]{1,0:T(8,128)(2,1)}, f32[1,128]{1,0:T(1,128)}) custom-call(s32[2]{0:T(128)} %pad_add_fusion.info, bf16[512,512]{1,0:T(8,128)(2,1)} %get-tuple-element.2476.query, bf16[512,512]{1,0:T(8,128)(2,1)} %copy-done.40, bf16[512,512]{1,0:T(8,128)(2,1)} %get-tuple-element.2478.own, ...), custom_call_target="tpu_custom_call" | custom-call | flops 1 | bytes 1 | tf_op jit(solution)/shard_map/attend_back/pallas_call | solution.py:609
  636.0 15.2 %attend_back.6 = (bf16[512,512]{1,0:T(8,128)(2,1)}, f32[512,512]{1,0:T(8,128)}, bf16[512,512]{1,0:T(8,128)(2,1)}, f32[1,128]{1,0:T(1,128)}) custom-call(s32[2]{0:T(128)} %pad_add_fusion.info, bf16[512,512]{1,0:T(8,128)(2,1)} %get-tuple-element.2491.query, bf16[512,512]{1,0:T(8,128)(2,1)} %copy-done.39, bf16[512,512]{1,0:T(8,128)(2,1)} %get-tuple-element.2493.own, ...), custom_call_target="tpu_custom_call" | custom-call | flops 1 | bytes 1 | tf_op jit(solution)/shard_map/attend_back/pallas_call | solution.py:609
  673.5 14.6 %attend_back.7 = (bf16[512,512]{1,0:T(8,128)(2,1)}, f32[512,512]{1,0:T(8,128)}, bf16[512,512]{1,0:T(8,128)(2,1)}, f32[1,128]{1,0:T(1,128)}) custom-call(s32[2]{0:T(128)} %pad_add_fusion.info, bf16[512,512]{1,0:T(8,128)(2,1)} %get-tuple-element.2559.query, bf16[512,512]{1,0:T(8,128)(2,1)} %copy-done.38, bf16[512,512]{1,0:T(8,128)(2,1)} %get-tuple-element.2561.own, ...), custom_call_target="tpu_custom_call" | custom-call | flops 1 | bytes 1 | tf_op jit(solution)/shard_map/attend_back/pallas_call | solution.py:609
  709.1 18.7 %collective-permute-done.54 = bf16[256,768]{1,0:T(8,128)(2,1)S(1)} collective-permute-done((bf16[256,768]{1,0:T(8,128)(2,1)S(1)}, bf16[256,768]{1,0:T(8,128)(2,1)S(1)}, u32[]{:S(2)}, u32[]{:S(2)}) %collective-permute-start.54) | collective-permute-done | bytes 393248 | tf_op jit(solution)/shard_map/ppermute | solution.py:318
  758.2 15.8 %back_to_rows.1 = f32[512,2048]{1,0:T(8,128)} custom-call(bf16[512,512]{1,0:T(8,128)(2,1)} %get-tuple-element.2810.refs_0_.refs_4_, bf16[512,512]{1,0:T(8,128)(2,1)} %get-tuple-element.2745.refs_1_, bf16[512,512]{1,0:T(8,128)(2,1)} %get-tuple-element.2807.refs_2_.refs_1_.refs_3_, bf16[512,512]{1,0:T(8,128)(2,1)} %get-tuple-element.2747.refs_2_.refs_3_, ...), custom_call_target="tpu_custom_call" | custom-call | flops 1 | bytes 1 | tf_op jit(solution)/shard_map/back_to_rows/pallas_call | solution.py:835
  788.8 11.0 %whole_columns.4 = f32[512,6144]{1,0:T(8,128)} custom-call(s32[1]{0:T(128)} %bitcast.17.me_ref, bf16[2048,768]{1,0:T(8,128)(2,1)} %copy-done.22, bf16[2048,768]{1,0:T(8,128)(2,1)} %collective-permute-done.58.other_ref), custom_call_target="tpu_custom_call" | custom-call | flops 1 | bytes 1 | tf_op jit(solution)/shard_map/whole_columns/pallas_call | solution.py:434
  799.9 17.2 %collective-permute-done.63 = bf16[512,256]{1,0:T(8,128)(2,1)S(1)} collective-permute-done((bf16[512,256]{1,0:T(8,128)(2,1)}, bf16[512,256]{1,0:T(8,128)(2,1)S(1)}, u32[]{:S(2)}, u32[]{:S(2)}) %collective-permute-start.63) | collective-permute-done | bytes 262176 | tf_op jit(solution)/shard_map/ppermute | solution.py:323
  861.0 15.3 %collective-permute-done.73 = bf16[1024,512]{1,0:T(8,128)(2,1)S(1)} collective-permute-done((bf16[1024,512]{1,0:T(8,128)(2,1)S(1)}, bf16[1024,512]{1,0:T(8,128)(2,1)S(1)}, u32[]{:S(2)}, u32[]{:S(2)}) %collective-permute-start.73) | collective-permute-done | bytes 1048608 | tf_op jit(solution)/shard_map/ppermute | solution.py:318
  886.1 17.9 %whole_columns.5 = (f32[512,6144]{1,0:T(8,128)}, f32[512,6144]{1,0:T(8,128)}) custom-call(s32[1]{0:T(128)} %bitcast.17.me_ref, bf16[2048,1536]{1,0:T(8,128)(2,1)} %copy-done.14, bf16[2048,1536]{1,0:T(8,128)(2,1)} %copy-done.20), custom_call_target="tpu_custom_call" | custom-call | flops 1 | bytes 1 | tf_op jit(solution)/shard_map/whole_columns/pallas_call | solution.py:434
  904.0 11.6 %collective-permute-done.77 = f32[4352]{0:T(1024)S(1)} collective-permute-done((f32[4352]{0:T(1024)S(1)}, f32[4352]{0:T(1024)S(1)}, u32[]{:S(2)}, u32[]{:S(2)}) %collective-permute-start.77) | collective-permute-done | bytes 17440 | tf_op jit(solution)/shard_map/ppermute | solution.py:318
  931.9 15.6 %collective-permute-done.86 = bf16[256,2048]{1,0:T(8,128)(2,1)S(1)} collective-permute-done((bf16[256,2048]{1,0:T(8,128)(2,1)S(1)}, bf16[256,2048]{1,0:T(8,128)(2,1)S(1)}, u32[]{:S(2)}, u32[]{:S(2)}) %collective-permute-start.86) | collective-permute-done | bytes 1048608 | tf_op jit(solution)/shard_map/ppermute | solution.py:398
  951.3 15.1 %collective-permute-done.83 = bf16[512,256]{1,0:T(8,128)(2,1)S(1)} collective-permute-done((bf16[512,256]{1,0:T(8,128)(2,1)S(1)}, bf16[512,256]{1,0:T(8,128)(2,1)S(1)}, u32[]{:S(2)}, u32[]{:S(2)}) %collective-permute-start.83) | collective-permute-done | bytes 262176 | tf_op jit(solution)/shard_map/ppermute | solution.py:323
  966.5 12.4 %collective-permute-start.88 = (bf16[512,256]{1,0:T(8,128)(2,1)S(1)}, bf16[512,256]{1,0:T(8,128)(2,1)S(1)}, u32[]{:S(2)}, u32[]{:S(2)}) collective-permute-start(bf16[512,256]{1,0:T(8,128)(2,1)S(1)} %add_convert_fusion.20), channel_id=1, source_target_pairs={{0,1},{1,2},{2,3},{3,0},{4,5},{5,6},{6,7},{7,4},{8,9},{9,10},{10,1... | collective-permute-start | bytes 786440 | tf_op jit(solution)/shard_map/ppermute | solution.py:323
  984.7 14.9 %collective-permute-done.87 = f32[4352]{0:T(1024)S(1)} collective-permute-done((f32[4352]{0:T(1024)S(1)}, f32[4352]{0:T(1024)S(1)}, u32[]{:S(2)}, u32[]{:S(2)}) %collective-permute-start.87) | collective-permute-done | bytes 17440 | tf_op jit(solution)/shard_map/ppermute | solution.py:1311
  (639 shorter events, 458.1 us)
Async XLA Ops:
  7.2 150.7 %all-gather.3.cloned.1.call-start = ((), (), s32[]{:S(2)}) async-start(), calls=%async_computation.2 | async-start | bytes 1310720 | tf_op jit(solution)/shard_map/all_gather | solution.py:897
  62.4 46.0 %collective-permute-start.5 = (bf16[1536,512]{1,0:T(8,128)(2,1)}, bf16[1536,512]{1,0:T(8,128)(2,1)}, u32[]{:S(2)}, u32[]{:S(2)}) collective-permute-start(bf16[1536,512]{1,0:T(8,128)(2,1)} %pad_maximum_fusion.8.came0.refs_9_), channel_id=1, source_target_pairs={{0,16},{4,20},{8,24},{12,28},{16,0},{20,4},{24,8},{28,12},{1,17},{... | collective-permute-start | bytes 4718600 | tf_op jit(solution)/shard_map/ppermute | solution.py:318
  63.9 44.5 %collective-permute-start.4 = (bf16[1536,512]{1,0:T(8,128)(2,1)}, bf16[1536,512]{1,0:T(8,128)(2,1)}, u32[]{:S(2)}, u32[]{:S(2)}) collective-permute-start(bf16[1536,512]{1,0:T(8,128)(2,1)} %pad_maximum_fusion.8.came0.refs_9_), channel_id=1, source_target_pairs={{0,8},{4,12},{8,0},{12,4},{16,24},{20,28},{24,16},{28,20},{1,9},{5... | collective-permute-start | bytes 4718600 | tf_op jit(solution)/shard_map/ppermute | solution.py:318
  67.6 40.8 %collective-permute-start.7 = (bf16[256,2048]{1,0:T(8,128)(2,1)}, bf16[256,2048]{1,0:T(8,128)(2,1)S(1)}, u32[]{:S(2)}, u32[]{:S(2)}) collective-permute-start(bf16[256,2048]{1,0:T(8,128)(2,1)} %get-tuple-element.3043), channel_id=1, source_target_pairs={{0,1},{1,0},{2,5},{3,4},{4,3},{5,2},{6,7},{7,6},{8,9},{9,8},{10,13... | collective-permute-start | bytes 3145736 | tf_op jit(solution)/shard_map/ppermute | solution.py:385
  67.6 40.8 %collective-permute-start.6 = (bf16[256,2048]{1,0:T(8,128)(2,1)}, bf16[256,2048]{1,0:T(8,128)(2,1)S(1)}, u32[]{:S(2)}, u32[]{:S(2)}) collective-permute-start(bf16[256,2048]{1,0:T(8,128)(2,1)} %get-tuple-element.3044), channel_id=1, source_target_pairs={{0,0},{1,1},{2,4},{3,5},{4,2},{5,3},{6,6},{7,7},{8,8},{9,9},{10,12... | collective-permute-start | bytes 3145736 | tf_op jit(solution)/shard_map/ppermute | solution.py:385
  72.5 303.2 %all-gather.5.cloned.1.call-start = ((), (), s32[]{:S(2)}) async-start(), calls=%async_computation.3 | async-start | bytes 11796480 | tf_op jit(solution)/shard_map/all_gather | solution.py:988
  110.9 47.1 %collective-permute-start.11 = (bf16[1536,512]{1,0:T(8,128)(2,1)}, bf16[1536,512]{1,0:T(8,128)(2,1)}, u32[]{:S(2)}, u32[]{:S(2)}) collective-permute-start(bf16[1536,512]{1,0:T(8,128)(2,1)} %collective-permute-done.4.came0.refs_13_), channel_id=1, source_target_pairs={{0,4},{4,0},{8,12},{12,8},{16,20},{20,16},{24,28},{28,24},{1,5},{5... | collective-permute-start | bytes 4718600 | tf_op jit(solution)/shard_map/ppermute | solution.py:318
  160.4 46.3 %collective-permute-start.13 = (bf16[1536,512]{1,0:T(8,128)(2,1)S(1)}, bf16[1536,512]{1,0:T(8,128)(2,1)S(1)}, u32[]{:S(2)}, u32[]{:S(2)}) collective-permute-start(bf16[1536,512]{1,0:T(8,128)(2,1)S(1)} %constant_dynamic-update-slice_fusion.came0.refs_21_), channel_id=1, source_target_pairs={{0,4},{4,0},{8,12},{12,8},{16,20},{20,16},{24,28},{28,24},{1,5},{5... | collective-permute-start | bytes 4718600 | tf_op jit(solution)/shard_map/ppermute | solution.py:318
  163.2 41.9 %collective-permute-start.14 = (bf16[256,2048]{1,0:T(8,128)(2,1)}, bf16[256,2048]{1,0:T(8,128)(2,1)}, u32[]{:S(2)}, u32[]{:S(2)}) collective-permute-start(bf16[256,2048]{1,0:T(8,128)(2,1)} %get-tuple-element.3036), channel_id=1, source_target_pairs={{0,0},{1,1},{2,4},{3,5},{4,2},{5,3},{6,6},{7,7},{8,8},{9,9},{10,12... | collective-permute-start | bytes 3145736 | tf_op jit(solution)/shard_map/ppermute | solution.py:385
  209.0 404.2 %reduce-scatter.3.cloned.1.call-start = ((), (), s32[]{:S(2)}) async-start(), calls=%async_computation.4 | async-start | bytes 3932160 | tf_op jit(solution)/shard_map/reduce_scatter | solution.py:1101
  234.0 44.9 %collective-permute-start.29 = (bf16[512,2048]{1,0:T(8,128)(2,1)S(1)}, bf16[512,2048]{1,0:T(8,128)(2,1)S(1)}, u32[]{:S(2)}, u32[]{:S(2)}) collective-permute-start(bf16[512,2048]{1,0:T(8,128)(2,1)S(1)} %maximum_select_fusion.refs_5_.refs_0_), channel_id=1, source_target_pairs={{0,16},{4,20},{8,24},{12,28},{16,0},{20,4},{24,8},{28,12},{1,17},{... | collective-permute-start | bytes 6291464 | tf_op jit(solution)/shard_map/ppermute | solution.py:318
  234.7 44.4 %collective-permute-start.28 = (bf16[512,2048]{1,0:T(8,128)(2,1)S(1)}, bf16[512,2048]{1,0:T(8,128)(2,1)S(1)}, u32[]{:S(2)}, u32[]{:S(2)}) collective-permute-start(bf16[512,2048]{1,0:T(8,128)(2,1)S(1)} %maximum_select_fusion.refs_5_.refs_0_), channel_id=1, source_target_pairs={{0,8},{4,12},{8,0},{12,4},{16,24},{20,28},{24,16},{28,20},{1,9},{5... | collective-permute-start | bytes 6291464 | tf_op jit(solution)/shard_map/ppermute | solution.py:318
  279.1 69.7 %collective-permute-start.33 = (bf16[512,2048]{1,0:T(8,128)(2,1)}, bf16[512,2048]{1,0:T(8,128)(2,1)S(1)}, u32[]{:S(2)}, u32[]{:S(2)}) collective-permute-start(bf16[512,2048]{1,0:T(8,128)(2,1)} %get-tuple-element.2336.refs_0_), channel_id=1, source_target_pairs={{0,16},{4,20},{8,24},{12,28},{16,0},{20,4},{24,8},{28,12},{1,17},{... | collective-permute-start | bytes 6291464 | tf_op jit(solution)/shard_map/ppermute | solution.py:318
  280.7 69.4 %collective-permute-start.32 = (bf16[512,2048]{1,0:T(8,128)(2,1)}, bf16[512,2048]{1,0:T(8,128)(2,1)S(1)}, u32[]{:S(2)}, u32[]{:S(2)}) collective-permute-start(bf16[512,2048]{1,0:T(8,128)(2,1)} %get-tuple-element.2336.refs_0_), channel_id=1, source_target_pairs={{0,8},{4,12},{8,0},{12,4},{16,24},{20,28},{24,16},{28,20},{1,9},{5... | collective-permute-start | bytes 6291464 | tf_op jit(solution)/shard_map/ppermute | solution.py:318
  281.8 67.0 %collective-permute-start.31 = (bf16[256,2048]{1,0:T(8,128)(2,1)S(1)}, bf16[256,2048]{1,0:T(8,128)(2,1)S(1)}, u32[]{:S(2)}, u32[]{:S(2)}) collective-permute-start(bf16[256,2048]{1,0:T(8,128)(2,1)S(1)} %slice.143), channel_id=1, source_target_pairs={{0,8},{4,12},{8,0},{12,4},{16,24},{20,28},{24,16},{28,20},{1,9},{5... | collective-permute-start | bytes 3145736 | tf_op jit(solution)/shard_map/ppermute | solution.py:318
  283.0 65.8 %collective-permute-start.30 = (bf16[256,2048]{1,0:T(8,128)(2,1)S(1)}, bf16[256,2048]{1,0:T(8,128)(2,1)S(1)}, u32[]{:S(2)}, u32[]{:S(2)}) collective-permute-start(bf16[256,2048]{1,0:T(8,128)(2,1)S(1)} %slice.142), channel_id=1, source_target_pairs={{0,16},{4,20},{8,24},{12,28},{16,0},{20,4},{24,8},{28,12},{1,17},{... | collective-permute-start | bytes 3145736 | tf_op jit(solution)/shard_map/ppermute | solution.py:318
  467.8 53.6 %collective-permute-start.38 = (bf16[512,2048]{1,0:T(8,128)(2,1)}, bf16[512,2048]{1,0:T(8,128)(2,1)}, u32[]{:S(2)}, u32[]{:S(2)}) collective-permute-start(bf16[512,2048]{1,0:T(8,128)(2,1)} %get-tuple-element.2188), channel_id=1, source_target_pairs={{0,8},{4,12},{8,0},{12,4},{16,24},{20,28},{24,16},{28,20},{1,9},{5... | collective-permute-start | bytes 6291464 | tf_op jit(solution)/shard_map/ppermute | solution.py:318
  468.5 52.9 %collective-permute-start.39 = (bf16[512,2048]{1,0:T(8,128)(2,1)}, bf16[512,2048]{1,0:T(8,128)(2,1)}, u32[]{:S(2)}, u32[]{:S(2)}) collective-permute-start(bf16[512,2048]{1,0:T(8,128)(2,1)} %get-tuple-element.2189), channel_id=1, source_target_pairs={{0,16},{4,20},{8,24},{12,28},{16,0},{20,4},{24,8},{28,12},{1,17},{... | collective-permute-start | bytes 6291464 | tf_op jit(solution)/shard_map/ppermute | solution.py:318
  521.8 230.2 %reduce-scatter.5.cloned.1.call-start = ((), (), s32[]{:S(2)}) async-start(), calls=%async_computation.5 | async-start | bytes 7864320 | tf_op jit(solution)/shard_map/reduce_scatter | solution.py:1160
  553.6 59.6 %collective-permute-start.43 = (bf16[512,2048]{1,0:T(8,128)(2,1)}, bf16[512,2048]{1,0:T(8,128)(2,1)}, u32[]{:S(2)}, u32[]{:S(2)}) collective-permute-start(bf16[512,2048]{1,0:T(8,128)(2,1)} %get-tuple-element.2361), channel_id=1, source_target_pairs={{0,8},{4,12},{8,0},{12,4},{16,24},{20,28},{24,16},{28,20},{1,9},{5... | collective-permute-start | bytes 6291464 | tf_op jit(solution)/shard_map/ppermute | solution.py:318
  554.9 58.2 %collective-permute-start.44 = (bf16[512,2048]{1,0:T(8,128)(2,1)}, bf16[512,2048]{1,0:T(8,128)(2,1)}, u32[]{:S(2)}, u32[]{:S(2)}) collective-permute-start(bf16[512,2048]{1,0:T(8,128)(2,1)} %get-tuple-element.2362), channel_id=1, source_target_pairs={{0,16},{4,20},{8,24},{12,28},{16,0},{20,4},{24,8},{28,12},{1,17},{... | collective-permute-start | bytes 6291464 | tf_op jit(solution)/shard_map/ppermute | solution.py:318
  653.4 41.5 %collective-permute-start.50 = (bf16[512,768]{1,0:T(8,128)(2,1)}, bf16[512,768]{1,0:T(8,128)(2,1)S(1)}, u32[]{:S(2)}, u32[]{:S(2)}) collective-permute-start(bf16[512,768]{1,0:T(8,128)(2,1)} %reduce-scatter.3.cloned.1.call-done), channel_id=1, source_target_pairs={{0,16},{4,20},{8,24},{12,28},{16,0},{20,4},{24,8},{28,12},{1,17},{... | collective-permute-start | bytes 2359304 | tf_op jit(solution)/shard_map/ppermute | solution.py:318
  654.4 40.5 %collective-permute-start.49 = (bf16[512,768]{1,0:T(8,128)(2,1)}, bf16[512,768]{1,0:T(8,128)(2,1)S(1)}, u32[]{:S(2)}, u32[]{:S(2)}) collective-permute-start(bf16[512,768]{1,0:T(8,128)(2,1)} %reduce-scatter.3.cloned.1.call-done), channel_id=1, source_target_pairs={{0,8},{4,12},{8,0},{12,4},{16,24},{20,28},{24,16},{28,20},{1,9},{5... | collective-permute-start | bytes 2359304 | tf_op jit(solution)/shard_map/ppermute | solution.py:318
  654.8 40.0 %collective-permute-start.51 = (bf16[512,512]{1,0:T(8,128)(2,1)}, bf16[512,512]{1,0:T(8,128)(2,1)}, u32[]{:S(2)}, u32[]{:S(2)}) collective-permute-start(bf16[512,512]{1,0:T(8,128)(2,1)} %get-tuple-element.2575), channel_id=1, source_target_pairs={{4,0},{12,8},{20,16},{28,24},{5,1},{13,9},{21,17},{29,25},{6,2},{1... | collective-permute-start | bytes 1572872 | tf_op jit(solution)/shard_map/ppermute | solution.py:1144
  656.1 38.8 %collective-permute-start.52 = (bf16[512,512]{1,0:T(8,128)(2,1)}, bf16[512,512]{1,0:T(8,128)(2,1)}, u32[]{:S(2)}, u32[]{:S(2)}) collective-permute-start(bf16[512,512]{1,0:T(8,128)(2,1)} %get-tuple-element.2579), channel_id=1, source_target_pairs={{4,0},{12,8},{20,16},{28,24},{5,1},{13,9},{21,17},{29,25},{6,2},{1... | collective-permute-start | bytes 1572872 | tf_op jit(solution)/shard_map/ppermute | solution.py:1144
  752.0 65.2 %collective-permute-start.67 = (bf16[2048,2048]{1,0:T(8,128)(2,1)}, bf16[2048,2048]{1,0:T(8,128)(2,1)}, u32[]{:S(2)}, u32[]{:S(2)}) collective-permute-start(bf16[2048,2048]{1,0:T(8,128)(2,1)} %row_outer.19), channel_id=1, source_target_pairs={{0,4},{4,0},{8,12},{12,8},{16,20},{20,16},{24,28},{28,24},{1,5},{5... | collective-permute-start | bytes 25165832 | tf_op jit(solution)/shard_map/ppermute | solution.py:318
  756.1 61.0 %collective-permute-start.62 = (bf16[512,1536]{1,0:T(8,128)(2,1)}, bf16[512,1536]{1,0:T(8,128)(2,1)S(1)}, u32[]{:S(2)}, u32[]{:S(2)}) collective-permute-start(bf16[512,1536]{1,0:T(8,128)(2,1)} %reduce-scatter.5.cloned.1.call-done), channel_id=1, source_target_pairs={{0,16},{4,20},{8,24},{12,28},{16,0},{20,4},{24,8},{28,12},{1,17},{... | collective-permute-start | bytes 4718600 | tf_op jit(solution)/shard_map/ppermute | solution.py:318
  756.8 60.4 %collective-permute-start.61 = (bf16[512,1536]{1,0:T(8,128)(2,1)}, bf16[512,1536]{1,0:T(8,128)(2,1)S(1)}, u32[]{:S(2)}, u32[]{:S(2)}) collective-permute-start(bf16[512,1536]{1,0:T(8,128)(2,1)} %reduce-scatter.5.cloned.1.call-done), channel_id=1, source_target_pairs={{0,8},{4,12},{8,0},{12,4},{16,24},{20,28},{24,16},{28,20},{1,9},{5... | collective-permute-start | bytes 4718600 | tf_op jit(solution)/shard_map/ppermute | solution.py:318
  879.7 42.2 %collective-permute-start.78 = (bf16[1024,512]{1,0:T(8,128)(2,1)}, bf16[1024,512]{1,0:T(8,128)(2,1)}, u32[]{:S(2)}, u32[]{:S(2)}) collective-permute-start(bf16[1024,512]{1,0:T(8,128)(2,1)} %get-tuple-element.2865), channel_id=1, source_target_pairs={{0,8},{4,12},{8,0},{12,4},{16,24},{20,28},{24,16},{28,20},{1,9},{5... | collective-permute-start | bytes 3145736 | tf_op jit(solution)/shard_map/ppermute | solution.py:318
  880.7 41.3 %collective-permute-start.79 = (bf16[1024,512]{1,0:T(8,128)(2,1)}, bf16[1024,512]{1,0:T(8,128)(2,1)S(1)}, u32[]{:S(2)}, u32[]{:S(2)}) collective-permute-start(bf16[1024,512]{1,0:T(8,128)(2,1)} %get-tuple-element.2868), channel_id=1, source_target_pairs={{0,16},{4,20},{8,24},{12,28},{16,0},{20,4},{24,8},{28,12},{1,17},{... | collective-permute-start | bytes 3145736 | tf_op jit(solution)/shard_map/ppermute | solution.py:318
  883.0 38.3 %collective-permute-start.76 = (bf16[1024,256]{1,0:T(8,128)(2,1)}, bf16[1024,256]{1,0:T(8,128)(2,1)}, u32[]{:S(2)}, u32[]{:S(2)}) collective-permute-start(bf16[1024,256]{1,0:T(8,128)(2,1)} %add_convert_fusion.11), channel_id=1, source_target_pairs={{0,16},{4,20},{8,24},{12,28},{16,0},{20,4},{24,8},{28,12},{1,17},{... | collective-permute-start | bytes 1572872 | tf_op jit(solution)/shard_map/ppermute | solution.py:318
  928.0 38.4 %collective-permute-start.81 = (bf16[1024,256]{1,0:T(8,128)(2,1)S(1)}, bf16[1024,256]{1,0:T(8,128)(2,1)S(1)}, u32[]{:S(2)}, u32[]{:S(2)}) collective-permute-start(bf16[1024,256]{1,0:T(8,128)(2,1)S(1)} %add_convert_fusion.7), channel_id=1, source_target_pairs={{0,16},{4,20},{8,24},{12,28},{16,0},{20,4},{24,8},{28,12},{1,17},{... | collective-permute-start | bytes 1572872 | tf_op jit(solution)/shard_map/ppermute | solution.py:318
  (203 other events, 2612.9 us)
Sparse Core Ops, SparseCore 0:
  72.6 47.3 all-gather.2
  209.1 165.9 all-gather.4
  521.9 62.5 reduce-scatter.2
  588.8 113.6 reduce-scatter.4

commit v8 on v7

--- a/solution.py
+++ b/solution.py
@@ -490,15 +490,21 @@
         ].astype(jnp.bfloat16)
 
 
-def window_scores(info, query, keys, part, scale):
-    rows, columns = query.shape[0], keys.shape[0]
+def window_mask(info, part, rows, columns):
     half = columns - rows
     row = lax.broadcasted_iota(jnp.int32, (rows, columns), 0)
     column = lax.broadcasted_iota(jnp.int32, (rows, columns), 1)
     gap = column - row - half
     slot = column + ((info[0] - 1) * half + part * rows)
     allowed = (gap <= 0) & (gap > -half) & (slot >= 0) & ((slot < info[1]) | (gap == 0))
-    return nt(query, keys) * scale, allowed
+    mask = jnp.where(allowed, 0.0, NEG)
+    return jnp.concatenate([mask, mask], 0)
+
+
+def two_heads(ref, at, block, dim):
+    return jnp.concatenate(
+        [ref[at, h * dim : (h + 1) * dim] for h in (2 * block, 2 * block + 1)], 0
+    )
 
 
 def key_columns(block, dim):
@@ -522,20 +528,20 @@
     rows = query.shape[0] // 2
     for part in range(2):
         at = slice(part * rows, (part + 1) * rows)
+        mask = window_mask(info, part, rows, 3 * rows)
         for block in range(2):
             keys, values = seen_pair(before, own, part, block, dim)
-            for head in (2 * block, 2 * block + 1):
-                on = slice(head * dim, (head + 1) * dim)
-                score, allowed = window_scores(info, query[at, on], keys, part, dim**-0.5)
-                score = jnp.where(allowed, score, NEG)
-                top = jnp.max(score, -1, keepdims=True)
-                expo = jnp.exp(score - top)
-                total = jnp.sum(expo, -1, keepdims=True)
-                prob = (expo * (1.0 / total)).astype(jnp.bfloat16)
-                mixed[at, on] = jnp.dot(
-                    prob, values, preferred_element_type=jnp.float32
-                ).astype(jnp.bfloat16)
-                log_total[at, on] = jnp.broadcast_to(top + jnp.log(total), (rows, dim))
+            score = nt(two_heads(query, at, block, dim), keys) * dim**-0.5 + mask
+            top = jnp.max(score, -1, keepdims=True)
+            expo = jnp.exp(score - top)
+            total = jnp.sum(expo, -1, keepdims=True)
+            prob = (expo * (1.0 / total)).astype(jnp.bfloat16)
+            out = jnp.dot(prob, values, preferred_element_type=jnp.float32).astype(jnp.bfloat16)
+            log = jnp.broadcast_to(top + jnp.log(total), (2 * rows, dim))
+            for i in range(2):
+                on = slice((2 * block + i) * dim, (2 * block + i + 1) * dim)
+                mixed[at, on] = out[i * rows : (i + 1) * rows]
+                log_total[at, on] = log[i * rows : (i + 1) * rows]
 
 
 def attend_back_body(
@@ -546,6 +552,7 @@
     rows = query.shape[0] // 2
     scale = dim**-0.5
     gain_total = jnp.zeros((1, dim), jnp.float32)
+    masks = [window_mask(info, part, rows, 3 * rows) for part in range(2)]
     for block, weight in enumerate((weight0, weight1)):
         on = slice(2 * block * dim, 2 * (block + 1) * dim)
         grad_mixed[:, on] = jnp.dot(
@@ -556,24 +563,27 @@
         for part in range(2):
             keys, values = seen_pair(before, own, part, block, dim)
             at = slice(part * rows, (part + 1) * rows)
-            seen = slice(part * rows, part * rows + keys.shape[0])
-            for head in (2 * block, 2 * block + 1):
-                on = slice(head * dim, (head + 1) * dim)
-                score, allowed = window_scores(info, query[at, on], keys, part, scale)
-                prob = jnp.where(allowed, jnp.exp(score - log_total[at, on][:, :1]), 0.0)
-                grad_prob = nt(grad_mixed[at, on], values)
-                inner = jnp.sum(prob * grad_prob, -1, keepdims=True)
-                grad_score = (prob * (grad_prob - inner)).astype(jnp.bfloat16)
-                grad_values[seen, :] += tn(prob.astype(jnp.bfloat16), grad_mixed[at, on])
-                grad_keys[seen, :] += tn(grad_score, query[at, on]) * scale
-                back = jnp.dot(grad_score, keys, preferred_element_type=jnp.float32) * scale
+            seen = slice(part * rows, part * rows + 3 * rows)
+            queries = two_heads(query, at, block, dim)
+            grads = two_heads(grad_mixed, at, block, dim)
+            log = two_heads(log_total, at, block, dim)[:, :1]
+            prob = jnp.exp(nt(queries, keys) * scale + masks[part] - log)
+            grad_prob = nt(grads, values)
+            inner = jnp.sum(prob * grad_prob, -1, keepdims=True)
+            grad_score = (prob * (grad_prob - inner)).astype(jnp.bfloat16)
+            grad_values[seen, :] += tn(prob.astype(jnp.bfloat16), grads)
+            grad_keys[seen, :] += tn(grad_score, queries) * scale
+            both = jnp.dot(grad_score, keys, preferred_element_type=jnp.float32) * scale
+            for i in range(2):
+                head = 2 * block + i
+                back = both[i * rows : (i + 1) * rows]
                 back = back * cosine[at, :] - turned(back) * sine[at, :]
                 there = (2 * head - head % 2) * dim
                 unit, inverse = unit_of(raw[at, there : there + dim])
                 gain_total += jnp.sum(unit * back, 0, keepdims=True)
                 back = back * gain[...]
                 back = inverse * (back - unit * jnp.mean(back * unit, -1, keepdims=True))
-                grad_query[at, on] = back.astype(jnp.bfloat16)
+                grad_query[at, head * dim : (head + 1) * dim] = back.astype(jnp.bfloat16)
         for grad, here, there in zip(
             (grad_keys, grad_values), key_columns(block, dim), key_columns(1 - block, dim)
         ):
@@ -902,13 +912,15 @@
     s.came = jnp.concatenate([part[:piece] for part in parts], 0)
     s.gains = jnp.concatenate([gain_rows[:2], *(part[piece : piece + 2] for part in parts)], 1)
     s.came_near = near(s.came)
+    s.came_own = across(s.came, CORE)
     s.x_came = tokens_sent
     del s.before, s.behind, s.ahead
     s.end()
 
     grad_y_sent = to_sequences_send(s.cotangent)
     s.came_far = far(*s.came_near)
-    s.came_other = [across(block, CORE) for block in (s.came, *s.came_near)]
+    s.came_other = [s.came_own, *(across(block, CORE) for block in s.came_near)]
+    s.grad_y_came = grad_y_sent
     gains = rolled(s.gains.astype(full))
     s.mlp_gains = gains[1:]
     s.attn_gains = gains[:1]
@@ -933,7 +945,7 @@
     s.cosine, sine = cosine[0, :, 0], sine[0, :, 0]
     s.sine = jnp.concatenate([-sine[:, : head_dim // 2], sine[:, head_dim // 2 :]], 1)
     s.out_own = out_own
-    del s.gains, s.x_came, s.other_lengths, s.cotangent
+    del s.gains, s.x_came, s.other_lengths, s.cotangent, s.came_own
     s.end()
 
     head_columns = 2 * head_dim
@@ -971,6 +983,7 @@
             *projected[1:], earlier,
         )
 
+    ffn_own = lax.all_gather(s.ffn_block, "shard", axis=0, tiled=True)
     came_last = jnp.concatenate(s.came_far, 0)
     s.came_last = (came_last, across(came_last, CORE))
     s.out_near = near(s.out_own)
@@ -981,16 +994,13 @@
             for i, (block, other) in enumerate(zip((s.came, *s.came_near), s.came_other))
         ]
     )
-    s.grad_y_came = grad_y_sent
-    del s.came_far
-    s.end()
-
-    ffn_own = lax.all_gather(s.ffn_block, "shard", axis=0, tiled=True)
+    del s.came_far, s.ffn_block
+    s.end()
+
     s.out_far = far(*s.out_near)
     s.out_near_other = [across(block, CORE) for block in s.out_near]
     s.earlier = [lax.ppermute(p[2], "rep", upward) for p in s.projected]
     (s.projected_last,) = in_order([project_call(3, *s.came_last)])
-    del s.ffn_block
     s.end()
 
     grad_y = jnp.concatenate(in_turn(s.grad_y_came), 0)
@@ -1192,12 +1202,14 @@
     s.end()
 
     output_sent = from_sequences_send(s.output)
+    s.output_first = output_sent[0]
     s.out_near = send_near((s.out_head[0], s.out_tail[0]))
     s.down_far = far(*s.down_near)
     give_back(0)
     finished1, finished2 = in_order([finish_call(1), finish_call(2)])
     s.finished = s.finished | {1: finished1, 2: finished2}
     del s.output
+    s.gate_up_total = gate_up_total
     s.end()
 
     s.out_far = send_far(s.out_near, (s.out_tail[1], s.out_head[1]), by_columns)
@@ -1206,7 +1218,7 @@
     (finished,) = in_order([finish_call(0)])
     s.finished = s.finished | {0: finished}
     (s.qkv_odd,) = in_order([odd_call(s.normed, [s.finished[i][1] for i in range(4)])])
-    s.gate_up_total = gate_up_total
+    s.output_second = output_sent[1]
     del s.down_total, s.down_near, s.down_far
     s.end()
 
@@ -1238,7 +1250,6 @@
     s.grad_tokens = (
         s.grad_resid + norm_back(x_unit, s.inverse_in, grad_in * s.attn_gains)
     ).astype(low)
-    s.output_came = output_sent
     del s.qkv_odd, s.out_near, s.out_far, s.out_head, s.out_tail, s.down_own, s.down_other
     del s.own_blocks, s.came, s.came_near, s.came_other, s.came_last, s.grad_resid, s.x_low
     s.end()
@@ -1263,6 +1274,7 @@
             sum(s.finished[i][2] for i in range(4))[0],
         ]
     )
+    s.gain_came = across(s.gain_parts, CORE)
     del s.qkv_came, s.finished, s.backs
     s.end()
 
@@ -1282,7 +1294,9 @@
     s.gate_up_own = jnp.concatenate([s.gate_up_total, *s.gate_up_near, *s.gate_up_far], 0)
     s.gate_up_other = across(s.gate_up_own, CORE)
     s.out_total = rounded_sum(s.out_chunks[0], s.out_ring[1], s.out_ring_last)
-    s.gain_came = across(s.gain_parts, CORE)
+    s.gain_parts = s.gain_parts + s.gain_came
+    s.gain_came = across(s.gain_parts, ACROSS_X)
+    s.tokens_first = grad_tokens_sent[0]
     del s.out_chunks, s.out_ring, s.out_ring_last, s.gate_up_near, s.gate_up_far
     del s.gate_up_total, s.grad_tokens
     s.end()
@@ -1290,7 +1304,8 @@
     s.far0 = qkv_far(s.near0, 0)
     s.near1 = qkv_near(1)
     s.gain_parts = s.gain_parts + s.gain_came
-    s.gain_came = across(s.gain_parts, ACROSS_X)
+    s.gain_came = across(s.gain_parts, ACROSS_Y)
+    s.tokens_second = grad_tokens_sent[1]
     (s.whole_gate_up,) = in_order([whole_call((units, units), s.gate_up_own, s.gate_up_other)])
     del s.gate_up_own, s.gate_up_other
     s.end()
@@ -1299,16 +1314,15 @@
     s.ring0 = ring_sum_first(s.chunks0)
     s.far1 = qkv_far(s.near1, 1)
     s.gain_parts = s.gain_parts + s.gain_came
-    s.gain_came = across(s.gain_parts, ACROSS_Y)
+    s.gain_came = lax.ppermute(s.gain_parts, "shard", [(i, i ^ 1) for i in range(shards)])
     del s.near0, s.far0
-    s.tokens_came = grad_tokens_sent
     s.end()
 
     s.last0 = around(rounded_sum(s.chunks0[3], s.ring0[0]), 1)
     s.chunks1 = qkv_chunks(s.near1, s.far1, 1)
     s.ring1 = ring_sum_first(s.chunks1)
     s.gain_parts = s.gain_parts + s.gain_came
-    s.gain_came = lax.ppermute(s.gain_parts, "shard", [(i, i ^ 1) for i in range(shards)])
+    s.gain_came = lax.ppermute(s.gain_parts, "shard", [(i, i ^ 2) for i in range(shards)])
     del s.near1, s.far1, s.heads, s.tails
     s.end()
 
@@ -1316,8 +1330,7 @@
     s.total0 = jnp.concatenate([query_total, s.out_total], 1)
     s.spread0 = near(s.total0)
     s.last1 = around(rounded_sum(s.chunks1[3], s.ring1[0]), 1)
-    s.gain_parts = s.gain_parts + s.gain_came
-    s.gain_came = lax.ppermute(s.gain_parts, "shard", [(i, i ^ 2) for i in range(shards)])
+    s.gain_sums = s.gain_parts + s.gain_came
     del s.chunks0, s.ring0, s.last0, s.out_total
     s.end()
 
@@ -1342,14 +1355,14 @@
     ((whole_key, whole_value),) = in_order(
         [whole_call((head_dim, head_dim), s.own1, s.other1)]
     )
-    gain_sums = s.gain_parts + s.gain_came
+    gain_sums = s.gain_sums
     wide = lax.dynamic_slice_in_dim(
         gain_sums[: 2 * width].reshape(2, width), shard_at * piece, piece, 1
     )
     narrow = gain_sums[2 * width :]
     return (
-        jnp.stack(in_turn(s.output_came)),
-        jnp.stack(in_turn(s.tokens_came)),
+        jnp.stack(in_turn([s.output_first, s.output_second])),
+        jnp.stack(in_turn([s.tokens_first, s.tokens_second])),
         wide[0],
         s.whole0[0],
         whole_key,

time: 1070 us -> 1050 us (0.981)
  Pallas kernels: 438 us -> 426 us
  waiting for transfers between devices: 322 us -> 311 us
    ppermute x4, waiting for transfers between devices: 44 us -> 19.1 us  [to_sequences_send(): lax.ppermute(lax.dynamic_index_in_dim(x, turn ^ odd, 0, keepdims=False),...]
    ppermute x73, waiting for transfers between devices: 182 us -> 206 us  [across(): return lax.ppermute(x, 'rep', [(i, i ^ mask) for i in range(count)])]
    ppermute x12, waiting for transfers between devices: 58 us -> 37.1 us  [around(): lax.ppermute(x, 'shard', [(i, (i + by) % count) for i in range(count)])]
    ppermute x73, starting transfers between devices: 83.2 us -> 102 us  [across(): return lax.ppermute(x, 'rep', [(i, i ^ mask) for i in range(count)])]
    ppermute x12, starting transfers between devices: 34.1 us -> 15.6 us  [around(): lax.ppermute(x, 'shard', [(i, (i + by) % count) for i in range(count)])]
    pallas_call x16, Pallas kernels: 132 us -> 120 us  [call(): pl.pallas_call(body, grid=(1,), out_shape=outs, in_specs=in_specs, out_sp...]
    ppermute x4, waiting for transfers between devices: 15.6 us -> 26.7 us  [from_sequences_send(): lax.ppermute(lax.dynamic_index_in_dim(x, turn ^ odd, 0, keepdims=False),...]
    unnamed x272 -> x266, local copies, waits for them, and re-layouts: 29.4 us -> 29 us
  transfers between devices with their start and end apart: 107 -> 107, of which waited for: 34 -> 35; matrix products, arithmetic and copies ran while one was open for 8% -> 8% of each run, Pallas kernels for 37% -> 36%
where the time goes in v8:
time: 1050 us; the launch traced here: 1040 us
  Pallas kernels  426 us (41%)
  waiting for transfers between devices  311 us (30%)
  starting transfers between devices  155 us (15%)
  other arithmetic  66 us (6%)
  local copies, waits for them, and re-layouts  65.6 us (6%)
  between operations  16.2 us (2%)
    ppermute x73, waiting for transfers between devices, across(): return lax.ppermute(x, 'rep', [(i, i ^ mask) for i in range(count)])  206 us
    pallas_call x16, Pallas kernels, call(): pl.pallas_call(body, grid=(1,), out_shape=outs, in_specs=in_specs, out_sp...  120 us
    pallas_call x12, Pallas kernels, row_outer(): pl.pallas_call(body, grid=(tiles,), out_shape=[jax.ShapeDtypeStruct((tile...  115 us
    ppermute x73, starting transfers between devices, across(): return lax.ppermute(x, 'rep', [(i, i ^ mask) for i in range(count)])  102 us
    pallas_call x2, Pallas kernels, hidden_units(): pl.pallas_call(body, grid=(3,), out_shape=[jax.ShapeDtypeStruct((rows, un...  59.4 us
    pallas_call x4, Pallas kernels, from_hidden(): pl.pallas_call(body, grid=(4,), out_shape=[jax.ShapeDtypeStruct((2 * rows...  59.2 us
    pallas_call x4, Pallas kernels, whole_columns(): pl.pallas_call(body, grid_spec=pltpu.PrefetchScalarGridSpec(num_scalar_pr...  44.3 us
    ppermute x12, waiting for transfers between devices, around(): lax.ppermute(x, 'shard', [(i, (i + by) % count) for i in range(count)])  37.1 us
  transfers between devices with their start and end apart: 107, of which 35 were waited for; matrix products, arithmetic and copies ran while one was open for 8% of the time, Pallas kernels for 36%

profile of v8, /device:TPU:0, one launch (start us, length us, event | category | flops | bytes accessed | tf_op | source)
XLA Modules:
  0.0 1040.2 jit_solution(16428458593608798418)
XLA Ops:
  32.0 11.3 %collective-permute-done = bf16[528,512]{1,0:T(8,128)(2,1)} collective-permute-done((bf16[528,512]{1,0:T(8,128)(2,1)}, bf16[528,512]{1,0:T(8,128)(2,1)}, u32[]{:S(2)}, u32[]{:S(2)}) %collective-permute-start) | collective-permute-done | bytes 540704 | tf_op jit(solution)/shard_map/ppermute | solution.py:323
  45.0 13.5 %collective-permute-done.3 = bf16[528,512]{1,0:T(8,128)(2,1)S(1)} collective-permute-done((bf16[528,512]{1,0:T(8,128)(2,1)}, bf16[528,512]{1,0:T(8,128)(2,1)S(1)}, u32[]{:S(2)}, u32[]{:S(2)}) %collective-permute-start.3) | collective-permute-done | bytes 540704 | tf_op jit(solution)/shard_map/ppermute | solution.py:323
  81.9 19.1 %collective-permute-done.8 = bf16[256,2048]{1,0:T(8,128)(2,1)S(1)} collective-permute-done((bf16[256,2048]{1,0:T(8,128)(2,1)}, bf16[256,2048]{1,0:T(8,128)(2,1)S(1)}, u32[]{:S(2)}, u32[]{:S(2)}) %collective-permute-start.8) | collective-permute-done | bytes 1048608 | tf_op jit(solution)/shard_map/ppermute | solution.py:385
  103.5 30.8 %collective-permute-start.11 = (bf16[1536,512]{1,0:T(8,128)(2,1)}, bf16[1536,512]{1,0:T(8,128)(2,1)}, u32[]{:S(2)}, u32[]{:S(2)}) collective-permute-start(bf16[1536,512]{1,0:T(8,128)(2,1)} %collective-permute-done.4.came0.refs_13_), channel_id=1, source_target_pairs={{0,4},{4,0},{8,12},{12,8},{16,20},{20,16},{24,28},{28,24},{1,5},{5... | collective-permute-start | bytes 4718600 | tf_op jit(solution)/shard_map/ppermute | solution.py:318
  138.2 9.5 collective-permute-start.13
  161.4 14.2 %collective-permute-done.9 = bf16[768,512]{1,0:T(8,128)(2,1)} collective-permute-done((bf16[768,512]{1,0:T(8,128)(2,1)}, bf16[768,512]{1,0:T(8,128)(2,1)}, u32[]{:S(2)}, u32[]{:S(2)}) %collective-permute-start.9) | collective-permute-done | bytes 786464 | tf_op jit(solution)/shard_map/ppermute | solution.py:318
  272.1 12.1 %close_attention.1 = (f32[512,2048]{1,0:T(8,128)}, bf16[512,2048]{1,0:T(8,128)(2,1)}) custom-call(bf16[512,2048]{1,0:T(8,128)(2,1)} %pad_maximum_fusion.3.x, bf16[512,512]{1,0:T(8,128)(2,1)} %get-tuple-element.2562.refs_0_.refs_1_.refs_4_, bf16[512,512]{1,0:T(8,128)(2,1)} %get-tuple-element.2559.refs_1_.refs_2_.refs_3_, ...), custom_call_target="tpu_custom_call" | custom-call | flops 1 | bytes 1 | tf_op jit(solution)/shard_map/close_attention/pallas_call | solution.py:792
  293.1 62.5 %collective-permute-done.31.refs_9_.refs_4_ = bf16[256,2048]{1,0:T(8,128)(2,1)S(1)} collective-permute-done((bf16[256,2048]{1,0:T(8,128)(2,1)S(1)}, bf16[256,2048]{1,0:T(8,128)(2,1)S(1)}, u32[]{:S(2)}, u32[]{:S(2)}) %collective-permute-start.31) | collective-permute-done | bytes 1048608 | tf_op jit(solution)/shard_map/ppermute | solution.py:318
  360.7 18.1 %collective-permute-done.35.refs_4_ = bf16[256,2048]{1,0:T(8,128)(2,1)S(1)} collective-permute-done((bf16[256,2048]{1,0:T(8,128)(2,1)S(1)}, bf16[256,2048]{1,0:T(8,128)(2,1)S(1)}, u32[]{:S(2)}, u32[]{:S(2)}) %collective-permute-start.35) | collective-permute-done | bytes 1048608 | tf_op jit(solution)/shard_map/ppermute | solution.py:318
  381.1 29.6 %hidden_units.2 = (bf16[2048,768]{1,0:T(8,128)(2,1)}, bf16[2048,768]{1,0:T(8,128)(2,1)}, bf16[2048,768]{1,0:T(8,128)(2,1)}) custom-call(bf16[512,2048]{1,0:T(8,128)(2,1)} %get-tuple-element.2344.refs_0_, bf16[512,2048]{1,0:T(8,128)(2,1)} %copy-done.12, bf16[512,2048]{1,0:T(8,128)(2,1)} %copy-done.11, bf16[256,2048]{1,0:T(8,128)(2,1)} %copy-done.24, ...), custom_call_target="tpu_custom_call" | custom-call | flops 1 | bytes 1 | tf_op jit(solution)/shard_map/hidden_units/pallas_call | solution.py:659
  410.6 29.9 %hidden_units.3 = (bf16[2048,768]{1,0:T(8,128)(2,1)}, bf16[2048,768]{1,0:T(8,128)(2,1)}, bf16[2048,768]{1,0:T(8,128)(2,1)}) custom-call(bf16[512,2048]{1,0:T(8,128)(2,1)} %get-tuple-element.2344.refs_0_, bf16[512,2048]{1,0:T(8,128)(2,1)} %copy-done.12, bf16[512,2048]{1,0:T(8,128)(2,1)} %copy-done.11, bf16[256,2048]{1,0:T(8,128)(2,1)} %copy-done.24, ...), custom_call_target="tpu_custom_call" | custom-call | flops 1 | bytes 1 | tf_op jit(solution)/shard_map/hidden_units/pallas_call | solution.py:659
  440.5 12.6 %row_outer.12 = bf16[2048,768]{1,0:T(8,128)(2,1)} custom-call(bf16[512,2048]{1,0:T(8,128)(2,1)} %copy-done.6, bf16[512,2048]{1,0:T(8,128)(2,1)} %copy-done.14, bf16[512,2048]{1,0:T(8,128)(2,1)} %copy-done.13, bf16[256,2048]{1,0:T(8,128)(2,1)} %copy-done.26, bf16[256,2048]{1,0:T(8,128)(2,1)} %copy-done.25, ...), custom_call_target="tpu_custom_call" | custom-call | flops 6442450944 | bytes 11534336 | tf_op jit(solution)/shard_map/row_outer/pallas_call | solution.py:742
  453.1 19.0 %from_hidden.4 = (bf16[512,2048]{1,0:T(8,128)(2,1)}, bf16[512,2048]{1,0:T(8,128)(2,1)}) custom-call(bf16[2048,768]{1,0:T(8,128)(2,1)} %get-tuple-element.2349.refs_0_.refs_1_.refs_2_.refs_3_.refs_5_, bf16[2048,768]{1,0:T(8,128)(2,1)} %get-tuple-element.2349.refs_0_.refs_1_.refs_2_.refs_3_.refs_5_, ...), custom_call_target="tpu_custom_call" | custom-call | flops 1 | bytes 1 | tf_op jit(solution)/shard_map/from_hidden/pallas_call | solution.py:698
  473.7 13.2 %row_outer.13 = bf16[2048,768]{1,0:T(8,128)(2,1)} custom-call(bf16[512,2048]{1,0:T(8,128)(2,1)} %copy-done.6, bf16[512,2048]{1,0:T(8,128)(2,1)} %copy-done.14, bf16[512,2048]{1,0:T(8,128)(2,1)} %copy-done.13, bf16[256,2048]{1,0:T(8,128)(2,1)} %copy-done.26, bf16[256,2048]{1,0:T(8,128)(2,1)} %copy-done.25, ...), custom_call_target="tpu_custom_call" | custom-call | flops 6442450944 | bytes 11534336 | tf_op jit(solution)/shard_map/row_outer/pallas_call | solution.py:742
  487.0 18.8 %from_hidden.5 = (bf16[512,2048]{1,0:T(8,128)(2,1)}, bf16[512,2048]{1,0:T(8,128)(2,1)}) custom-call(bf16[2048,768]{1,0:T(8,128)(2,1)} %get-tuple-element.2349.refs_0_.refs_1_.refs_2_.refs_3_.refs_5_, bf16[2048,768]{1,0:T(8,128)(2,1)} %get-tuple-element.2349.refs_0_.refs_1_.refs_2_.refs_3_.refs_5_, ...), custom_call_target="tpu_custom_call" | custom-call | flops 1 | bytes 1 | tf_op jit(solution)/shard_map/from_hidden/pallas_call | solution.py:698
  505.8 19.5 %row_outer.14 = bf16[2048,1536]{1,0:T(8,128)(2,1)} custom-call(bf16[512,2048]{1,0:T(8,128)(2,1)} %get-tuple-element.2344.refs_0_, bf16[512,2048]{1,0:T(8,128)(2,1)} %copy-done.12, bf16[512,2048]{1,0:T(8,128)(2,1)} %copy-done.11, bf16[256,2048]{1,0:T(8,128)(2,1)} %copy-done.24, bf16[256,2048]{1,0:T(8,128)(2,1)} %copy-done.23, ...), custom_call_target="tpu_custom_call" | custom-call | flops 12884901888 | bytes 14680064 | tf_op jit(solution)/shard_map/row_outer/pallas_call | solution.py:742
  533.1 10.6 %from_hidden.6 = (bf16[512,2048]{1,0:T(8,128)(2,1)}, bf16[512,2048]{1,0:T(8,128)(2,1)}) custom-call(bf16[2048,768]{1,0:T(8,128)(2,1)} %get-tuple-element.2285.refs_5_.refs_0_.refs_1_.refs_2_.refs_3_, bf16[2048,768]{1,0:T(8,128)(2,1)} %get-tuple-element.2285.refs_5_.refs_0_.refs_1_.refs_2_.refs_3_, ...), custom_call_target="tpu_custom_call" | custom-call | flops 1 | bytes 1 | tf_op jit(solution)/shard_map/from_hidden/pallas_call | solution.py:698
  543.7 10.8 %from_hidden.7 = (bf16[512,2048]{1,0:T(8,128)(2,1)}, bf16[512,2048]{1,0:T(8,128)(2,1)}) custom-call(bf16[2048,768]{1,0:T(8,128)(2,1)} %get-tuple-element.2285.refs_5_.refs_0_.refs_1_.refs_2_.refs_3_, bf16[2048,768]{1,0:T(8,128)(2,1)} %get-tuple-element.2285.refs_5_.refs_0_.refs_1_.refs_2_.refs_3_, ...), custom_call_target="tpu_custom_call" | custom-call | flops 1 | bytes 1 | tf_op jit(solution)/shard_map/from_hidden/pallas_call | solution.py:698
  570.2 19.8 %row_outer.15 = bf16[2048,1536]{1,0:T(8,128)(2,1)} custom-call(bf16[512,2048]{1,0:T(8,128)(2,1)} %get-tuple-element.2344.refs_0_, bf16[512,2048]{1,0:T(8,128)(2,1)} %copy-done.12, bf16[512,2048]{1,0:T(8,128)(2,1)} %copy-done.11, bf16[256,2048]{1,0:T(8,128)(2,1)} %copy-done.24, bf16[256,2048]{1,0:T(8,128)(2,1)} %copy-done.23, ...), custom_call_target="tpu_custom_call" | custom-call | flops 12884901888 | bytes 14680064 | tf_op jit(solution)/shard_map/row_outer/pallas_call | solution.py:742
  601.5 13.3 %attend_back.4 = (bf16[512,512]{1,0:T(8,128)(2,1)}, f32[512,512]{1,0:T(8,128)}, bf16[512,512]{1,0:T(8,128)(2,1)}, f32[1,128]{1,0:T(1,128)}) custom-call(s32[2]{0:T(128)} %pad_add_fusion.info, bf16[512,512]{1,0:T(8,128)(2,1)} %get-tuple-element.2419.query, bf16[512,512]{1,0:T(8,128)(2,1)} %collective-permute-done.26.before, ...), custom_call_target="tpu_custom_call" | custom-call | flops 1 | bytes 1 | tf_op jit(solution)/shard_map/attend_back/pallas_call | solution.py:619
  614.8 22.7 %collective-permute-done.43 = bf16[512,2048]{1,0:T(8,128)(2,1)} collective-permute-done((bf16[512,2048]{1,0:T(8,128)(2,1)}, bf16[512,2048]{1,0:T(8,128)(2,1)}, u32[]{:S(2)}, u32[]{:S(2)}) %collective-permute-start.43) | collective-permute-done | bytes 2097184 | tf_op jit(solution)/shard_map/ppermute | solution.py:318
  646.1 13.1 %attend_back.5 = (bf16[512,512]{1,0:T(8,128)(2,1)}, f32[512,512]{1,0:T(8,128)}, bf16[512,512]{1,0:T(8,128)(2,1)}, f32[1,128]{1,0:T(1,128)}) custom-call(s32[2]{0:T(128)} %pad_add_fusion.info, bf16[512,512]{1,0:T(8,128)(2,1)} %get-tuple-element.2484.query, bf16[512,512]{1,0:T(8,128)(2,1)} %collective-permute-done.20.before, ...), custom_call_target="tpu_custom_call" | custom-call | flops 1 | bytes 1 | tf_op jit(solution)/shard_map/attend_back/pallas_call | solution.py:619
  659.3 13.7 %attend_back.6 = (bf16[512,512]{1,0:T(8,128)(2,1)}, f32[512,512]{1,0:T(8,128)}, bf16[512,512]{1,0:T(8,128)(2,1)}, f32[1,128]{1,0:T(1,128)}) custom-call(s32[2]{0:T(128)} %pad_add_fusion.info, bf16[512,512]{1,0:T(8,128)(2,1)} %get-tuple-element.2499.query, bf16[512,512]{1,0:T(8,128)(2,1)} %collective-permute-done.21.before, ...), custom_call_target="tpu_custom_call" | custom-call | flops 1 | bytes 1 | tf_op jit(solution)/shard_map/attend_back/pallas_call | solution.py:619
  694.5 13.2 %attend_back.7 = (bf16[512,512]{1,0:T(8,128)(2,1)}, f32[512,512]{1,0:T(8,128)}, bf16[512,512]{1,0:T(8,128)(2,1)}, f32[1,128]{1,0:T(1,128)}) custom-call(s32[2]{0:T(128)} %pad_add_fusion.info, bf16[512,512]{1,0:T(8,128)(2,1)} %get-tuple-element.2567.query, bf16[512,512]{1,0:T(8,128)(2,1)} %copy-done.37, bf16[512,512]{1,0:T(8,128)(2,1)} %get-tuple-element.2569.own, ...), custom_call_target="tpu_custom_call" | custom-call | flops 1 | bytes 1 | tf_op jit(solution)/shard_map/attend_back/pallas_call | solution.py:619
  720.8 27.6 %collective-permute-done.54 = bf16[256,768]{1,0:T(8,128)(2,1)S(1)} collective-permute-done((bf16[256,768]{1,0:T(8,128)(2,1)S(1)}, bf16[256,768]{1,0:T(8,128)(2,1)S(1)}, u32[]{:S(2)}, u32[]{:S(2)}) %collective-permute-start.54) | collective-permute-done | bytes 393248 | tf_op jit(solution)/shard_map/ppermute | solution.py:318
  774.4 10.2 row_outer.19
  798.5 15.8 %back_to_rows.1 = f32[512,2048]{1,0:T(8,128)} custom-call(bf16[512,512]{1,0:T(8,128)(2,1)} %get-tuple-element.2822.refs_0_.refs_4_, bf16[512,512]{1,0:T(8,128)(2,1)} %get-tuple-element.2756.refs_1_, bf16[512,512]{1,0:T(8,128)(2,1)} %get-tuple-element.2819.refs_2_.refs_1_.refs_3_, bf16[512,512]{1,0:T(8,128)(2,1)} %get-tuple-element.2758.refs_2_.refs_3_, ...), custom_call_target="tpu_custom_call" | custom-call | flops 1 | bytes 1 | tf_op jit(solution)/shard_map/back_to_rows/pallas_call | solution.py:845
  820.8 11.0 %whole_columns.4 = f32[512,6144]{1,0:T(8,128)} custom-call(s32[1]{0:T(128)} %bitcast.17.me_ref, bf16[2048,768]{1,0:T(8,128)(2,1)} %copy-done.22, bf16[2048,768]{1,0:T(8,128)(2,1)} %collective-permute-done.59.other_ref), custom_call_target="tpu_custom_call" | custom-call | flops 1 | bytes 1 | tf_op jit(solution)/shard_map/whole_columns/pallas_call | solution.py:434
  867.7 21.2 %collective-permute-done.72 = f32[4352]{0:T(1024)S(1)} collective-permute-done((f32[4352]{0:T(1024)S(1)}, f32[4352]{0:T(1024)S(1)}, u32[]{:S(2)}, u32[]{:S(2)}) %collective-permute-start.72) | collective-permute-done | bytes 17440 | tf_op jit(solution)/shard_map/ppermute | solution.py:318
  896.8 21.3 %collective-permute-done.82 = bf16[256,2048]{1,0:T(8,128)(2,1)S(1)} collective-permute-done((bf16[256,2048]{1,0:T(8,128)(2,1)S(1)}, bf16[256,2048]{1,0:T(8,128)(2,1)S(1)}, u32[]{:S(2)}, u32[]{:S(2)}) %collective-permute-start.82) | collective-permute-done | bytes 1048608 | tf_op jit(solution)/shard_map/ppermute | solution.py:398
  919.0 17.8 %whole_columns.5 = (f32[512,6144]{1,0:T(8,128)}, f32[512,6144]{1,0:T(8,128)}) custom-call(s32[1]{0:T(128)} %bitcast.17.me_ref, bf16[2048,1536]{1,0:T(8,128)(2,1)} %copy-done.15, bf16[2048,1536]{1,0:T(8,128)(2,1)} %copy-done.20), custom_call_target="tpu_custom_call" | custom-call | flops 1 | bytes 1 | tf_op jit(solution)/shard_map/whole_columns/pallas_call | solution.py:434
  959.3 13.1 %collective-permute-done.88 = f32[4352]{0:T(1024)S(1)} collective-permute-done((f32[4352]{0:T(1024)S(1)}, f32[4352]{0:T(1024)S(1)}, u32[]{:S(2)}, u32[]{:S(2)}) %collective-permute-start.88) | collective-permute-done | bytes 17440 | tf_op jit(solution)/shard_map/ppermute | solution.py:1325
  (633 shorter events, 435.1 us)
Async XLA Ops:
  7.2 154.2 %all-gather.3.cloned.1.call-start = ((), (), s32[]{:S(2)}) async-start(), calls=%async_computation.2 | async-start | bytes 1310720 | tf_op jit(solution)/shard_map/all_gather | solution.py:907
  61.1 40.0 %collective-permute-start.6 = (bf16[1536,512]{1,0:T(8,128)(2,1)S(1)}, bf16[1536,512]{1,0:T(8,128)(2,1)}, u32[]{:S(2)}, u32[]{:S(2)}) collective-permute-start(bf16[1536,512]{1,0:T(8,128)(2,1)S(1)} %pad_maximum_fusion.8.came0.refs_9_), channel_id=1, source_target_pairs={{0,4},{4,0},{8,12},{12,8},{16,20},{20,16},{24,28},{28,24},{1,5},{5... | collective-permute-start | bytes 4718600 | tf_op jit(solution)/shard_map/ppermute | solution.py:318
  61.2 39.9 %collective-permute-start.5 = (bf16[1536,512]{1,0:T(8,128)(2,1)S(1)}, bf16[1536,512]{1,0:T(8,128)(2,1)}, u32[]{:S(2)}, u32[]{:S(2)}) collective-permute-start(bf16[1536,512]{1,0:T(8,128)(2,1)S(1)} %pad_maximum_fusion.8.came0.refs_9_), channel_id=1, source_target_pairs={{0,16},{4,20},{8,24},{12,28},{16,0},{20,4},{24,8},{28,12},{1,17},{... | collective-permute-start | bytes 4718600 | tf_op jit(solution)/shard_map/ppermute | solution.py:318
  62.8 38.3 %collective-permute-start.4 = (bf16[1536,512]{1,0:T(8,128)(2,1)S(1)}, bf16[1536,512]{1,0:T(8,128)(2,1)}, u32[]{:S(2)}, u32[]{:S(2)}) collective-permute-start(bf16[1536,512]{1,0:T(8,128)(2,1)S(1)} %pad_maximum_fusion.8.came0.refs_9_), channel_id=1, source_target_pairs={{0,8},{4,12},{8,0},{12,4},{16,24},{20,28},{24,16},{28,20},{1,9},{5... | collective-permute-start | bytes 4718600 | tf_op jit(solution)/shard_map/ppermute | solution.py:318
  80.3 299.7 %all-gather.5.cloned.1.call-start = ((), (), s32[]{:S(2)}) async-start(), calls=%async_computation.3 | async-start | bytes 11796480 | tf_op jit(solution)/shard_map/all_gather | solution.py:986
  103.5 72.1 %collective-permute-start.11 = (bf16[1536,512]{1,0:T(8,128)(2,1)}, bf16[1536,512]{1,0:T(8,128)(2,1)}, u32[]{:S(2)}, u32[]{:S(2)}) collective-permute-start(bf16[1536,512]{1,0:T(8,128)(2,1)} %collective-permute-done.4.came0.refs_13_), channel_id=1, source_target_pairs={{0,4},{4,0},{8,12},{12,8},{16,20},{20,16},{24,28},{28,24},{1,5},{5... | collective-permute-start | bytes 4718600 | tf_op jit(solution)/shard_map/ppermute | solution.py:318
  135.4 40.1 %collective-permute-start.12 = (bf16[1536,512]{1,0:T(8,128)(2,1)}, bf16[1536,512]{1,0:T(8,128)(2,1)}, u32[]{:S(2)}, u32[]{:S(2)}) collective-permute-start(bf16[1536,512]{1,0:T(8,128)(2,1)} %collective-permute-done.5.came0.refs_17_), channel_id=1, source_target_pairs={{0,4},{4,0},{8,12},{12,8},{16,20},{20,16},{24,28},{28,24},{1,5},{5... | collective-permute-start | bytes 4718600 | tf_op jit(solution)/shard_map/ppermute | solution.py:318
  175.6 439.2 %reduce-scatter.3.cloned.1.call-start = ((), (), s32[]{:S(2)}) async-start(), calls=%async_computation.4 | async-start | bytes 3932160 | tf_op jit(solution)/shard_map/reduce_scatter | solution.py:1111
  242.4 45.0 %collective-permute-start.29 = (bf16[512,2048]{1,0:T(8,128)(2,1)S(1)}, bf16[512,2048]{1,0:T(8,128)(2,1)S(1)}, u32[]{:S(2)}, u32[]{:S(2)}) collective-permute-start(bf16[512,2048]{1,0:T(8,128)(2,1)S(1)} %maximum_select_fusion.refs_5_.refs_0_), channel_id=1, source_target_pairs={{0,16},{4,20},{8,24},{12,28},{16,0},{20,4},{24,8},{28,12},{1,17},{... | collective-permute-start | bytes 6291464 | tf_op jit(solution)/shard_map/ppermute | solution.py:318
  243.9 44.9 %collective-permute-start.28 = (bf16[512,2048]{1,0:T(8,128)(2,1)S(1)}, bf16[512,2048]{1,0:T(8,128)(2,1)S(1)}, u32[]{:S(2)}, u32[]{:S(2)}) collective-permute-start(bf16[512,2048]{1,0:T(8,128)(2,1)S(1)} %maximum_select_fusion.refs_5_.refs_0_), channel_id=1, source_target_pairs={{0,8},{4,12},{8,0},{12,4},{16,24},{20,28},{24,16},{28,20},{1,9},{5... | collective-permute-start | bytes 6291464 | tf_op jit(solution)/shard_map/ppermute | solution.py:318
  288.8 66.8 %collective-permute-start.33 = (bf16[512,2048]{1,0:T(8,128)(2,1)}, bf16[512,2048]{1,0:T(8,128)(2,1)S(1)}, u32[]{:S(2)}, u32[]{:S(2)}) collective-permute-start(bf16[512,2048]{1,0:T(8,128)(2,1)} %get-tuple-element.2344.refs_0_), channel_id=1, source_target_pairs={{0,16},{4,20},{8,24},{12,28},{16,0},{20,4},{24,8},{28,12},{1,17},{... | collective-permute-start | bytes 6291464 | tf_op jit(solution)/shard_map/ppermute | solution.py:318
  289.2 67.3 %collective-permute-start.32 = (bf16[512,2048]{1,0:T(8,128)(2,1)}, bf16[512,2048]{1,0:T(8,128)(2,1)S(1)}, u32[]{:S(2)}, u32[]{:S(2)}) collective-permute-start(bf16[512,2048]{1,0:T(8,128)(2,1)} %get-tuple-element.2344.refs_0_), channel_id=1, source_target_pairs={{0,8},{4,12},{8,0},{12,4},{16,24},{20,28},{24,16},{28,20},{1,9},{5... | collective-permute-start | bytes 6291464 | tf_op jit(solution)/shard_map/ppermute | solution.py:318
  290.8 64.7 %collective-permute-start.31 = (bf16[256,2048]{1,0:T(8,128)(2,1)S(1)}, bf16[256,2048]{1,0:T(8,128)(2,1)S(1)}, u32[]{:S(2)}, u32[]{:S(2)}) collective-permute-start(bf16[256,2048]{1,0:T(8,128)(2,1)S(1)} %slice.143), channel_id=1, source_target_pairs={{0,8},{4,12},{8,0},{12,4},{16,24},{20,28},{24,16},{28,20},{1,9},{5... | collective-permute-start | bytes 3145736 | tf_op jit(solution)/shard_map/ppermute | solution.py:318
  291.6 63.9 %collective-permute-start.30 = (bf16[256,2048]{1,0:T(8,128)(2,1)S(1)}, bf16[256,2048]{1,0:T(8,128)(2,1)S(1)}, u32[]{:S(2)}, u32[]{:S(2)}) collective-permute-start(bf16[256,2048]{1,0:T(8,128)(2,1)S(1)} %slice.142), channel_id=1, source_target_pairs={{0,16},{4,20},{8,24},{12,28},{16,0},{20,4},{24,8},{28,12},{1,17},{... | collective-permute-start | bytes 3145736 | tf_op jit(solution)/shard_map/ppermute | solution.py:318
  472.1 53.2 %collective-permute-start.38 = (bf16[512,2048]{1,0:T(8,128)(2,1)}, bf16[512,2048]{1,0:T(8,128)(2,1)}, u32[]{:S(2)}, u32[]{:S(2)}) collective-permute-start(bf16[512,2048]{1,0:T(8,128)(2,1)} %get-tuple-element.2196), channel_id=1, source_target_pairs={{0,8},{4,12},{8,0},{12,4},{16,24},{20,28},{24,16},{28,20},{1,9},{5... | collective-permute-start | bytes 6291464 | tf_op jit(solution)/shard_map/ppermute | solution.py:318
  472.8 52.5 %collective-permute-start.39 = (bf16[512,2048]{1,0:T(8,128)(2,1)}, bf16[512,2048]{1,0:T(8,128)(2,1)}, u32[]{:S(2)}, u32[]{:S(2)}) collective-permute-start(bf16[512,2048]{1,0:T(8,128)(2,1)} %get-tuple-element.2197), channel_id=1, source_target_pairs={{0,16},{4,20},{8,24},{12,28},{16,0},{20,4},{24,8},{28,12},{1,17},{... | collective-permute-start | bytes 6291464 | tf_op jit(solution)/shard_map/ppermute | solution.py:318
  525.9 234.8 %reduce-scatter.5.cloned.1.call-start = ((), (), s32[]{:S(2)}) async-start(), calls=%async_computation.5 | async-start | bytes 7864320 | tf_op jit(solution)/shard_map/reduce_scatter | solution.py:1170
  590.0 47.6 %collective-permute-start.43 = (bf16[512,2048]{1,0:T(8,128)(2,1)}, bf16[512,2048]{1,0:T(8,128)(2,1)}, u32[]{:S(2)}, u32[]{:S(2)}) collective-permute-start(bf16[512,2048]{1,0:T(8,128)(2,1)} %get-tuple-element.2369), channel_id=1, source_target_pairs={{0,8},{4,12},{8,0},{12,4},{16,24},{20,28},{24,16},{28,20},{1,9},{5... | collective-permute-start | bytes 6291464 | tf_op jit(solution)/shard_map/ppermute | solution.py:318
  591.5 46.5 %collective-permute-start.44 = (bf16[512,2048]{1,0:T(8,128)(2,1)}, bf16[512,2048]{1,0:T(8,128)(2,1)}, u32[]{:S(2)}, u32[]{:S(2)}) collective-permute-start(bf16[512,2048]{1,0:T(8,128)(2,1)} %get-tuple-element.2370), channel_id=1, source_target_pairs={{0,16},{4,20},{8,24},{12,28},{16,0},{20,4},{24,8},{28,12},{1,17},{... | collective-permute-start | bytes 6291464 | tf_op jit(solution)/shard_map/ppermute | solution.py:318
  675.2 38.6 %collective-permute-start.50 = (bf16[512,768]{1,0:T(8,128)(2,1)}, bf16[512,768]{1,0:T(8,128)(2,1)S(1)}, u32[]{:S(2)}, u32[]{:S(2)}) collective-permute-start(bf16[512,768]{1,0:T(8,128)(2,1)} %reduce-scatter.3.cloned.1.call-done), channel_id=1, source_target_pairs={{0,16},{4,20},{8,24},{12,28},{16,0},{20,4},{24,8},{28,12},{1,17},{... | collective-permute-start | bytes 2359304 | tf_op jit(solution)/shard_map/ppermute | solution.py:318
  675.9 37.9 %collective-permute-start.49 = (bf16[512,768]{1,0:T(8,128)(2,1)}, bf16[512,768]{1,0:T(8,128)(2,1)}, u32[]{:S(2)}, u32[]{:S(2)}) collective-permute-start(bf16[512,768]{1,0:T(8,128)(2,1)} %reduce-scatter.3.cloned.1.call-done), channel_id=1, source_target_pairs={{0,8},{4,12},{8,0},{12,4},{16,24},{20,28},{24,16},{28,20},{1,9},{5... | collective-permute-start | bytes 2359304 | tf_op jit(solution)/shard_map/ppermute | solution.py:318
  713.8 45.8 %collective-permute-start.55 = (bf16[1024,512]{1,0:T(8,128)(2,1)}, bf16[1024,512]{1,0:T(8,128)(2,1)S(1)}, u32[]{:S(2)}, u32[]{:S(2)}) collective-permute-start(bf16[1024,512]{1,0:T(8,128)(2,1)} %get-tuple-element.2678), channel_id=1, source_target_pairs={{0,8},{4,12},{8,0},{12,4},{16,24},{20,28},{24,16},{28,20},{1,9},{5... | collective-permute-start | bytes 3145736 | tf_op jit(solution)/shard_map/ppermute | solution.py:318
  715.2 45.4 %collective-permute-start.56 = (bf16[1024,512]{1,0:T(8,128)(2,1)}, bf16[1024,512]{1,0:T(8,128)(2,1)}, u32[]{:S(2)}, u32[]{:S(2)}) collective-permute-start(bf16[1024,512]{1,0:T(8,128)(2,1)} %get-tuple-element.2681), channel_id=1, source_target_pairs={{0,16},{4,20},{8,24},{12,28},{16,0},{20,4},{24,8},{28,12},{1,17},{... | collective-permute-start | bytes 3145736 | tf_op jit(solution)/shard_map/ppermute | solution.py:318
  716.8 43.9 %collective-permute-start.57 = (bf16[256,2048]{1,0:T(8,128)(2,1)S(1)}, bf16[256,2048]{1,0:T(8,128)(2,1)S(1)}, u32[]{:S(2)}, u32[]{:S(2)}) collective-permute-start(bf16[256,2048]{1,0:T(8,128)(2,1)S(1)} %get-tuple-element.3032), channel_id=1, source_target_pairs={{0,0},{1,1},{4,2},{5,3},{2,4},{3,5},{6,6},{7,7},{8,8},{9,9},{12,10... | collective-permute-start | bytes 3145736 | tf_op jit(solution)/shard_map/ppermute | solution.py:398
  718.3 41.2 %collective-permute-start.58 = (bf16[512,512]{1,0:T(8,128)(2,1)S(1)}, bf16[512,512]{1,0:T(8,128)(2,1)S(1)}, u32[]{:S(2)}, u32[]{:S(2)}) collective-permute-start(bf16[512,512]{1,0:T(8,128)(2,1)S(1)} %copy-done.123), channel_id=1, source_target_pairs={{4,0},{12,8},{20,16},{28,24},{5,1},{13,9},{21,17},{29,25},{6,2},{1... | collective-permute-start | bytes 1572872 | tf_op jit(solution)/shard_map/ppermute | solution.py:1154
  790.0 42.0 %collective-permute-start.67 = (bf16[2048,2048]{1,0:T(8,128)(2,1)}, bf16[2048,2048]{1,0:T(8,128)(2,1)}, u32[]{:S(2)}, u32[]{:S(2)}) collective-permute-start(bf16[2048,2048]{1,0:T(8,128)(2,1)} %row_outer.19), channel_id=1, source_target_pairs={{0,4},{4,0},{8,12},{12,8},{16,20},{20,16},{24,28},{28,24},{1,5},{5... | collective-permute-start | bytes 25165832 | tf_op jit(solution)/shard_map/ppermute | solution.py:318
  790.1 41.9 %collective-permute-start.64 = (bf16[512,1536]{1,0:T(8,128)(2,1)S(1)}, bf16[512,1536]{1,0:T(8,128)(2,1)S(1)}, u32[]{:S(2)}, u32[]{:S(2)}) collective-permute-start(bf16[512,1536]{1,0:T(8,128)(2,1)S(1)} %copy-done.41), channel_id=1, source_target_pairs={{0,16},{4,20},{8,24},{12,28},{16,0},{20,4},{24,8},{28,12},{1,17},{... | collective-permute-start | bytes 4718600 | tf_op jit(solution)/shard_map/ppermute | solution.py:318
  791.6 40.4 %collective-permute-start.63 = (bf16[512,1536]{1,0:T(8,128)(2,1)S(1)}, bf16[512,1536]{1,0:T(8,128)(2,1)S(1)}, u32[]{:S(2)}, u32[]{:S(2)}) collective-permute-start(bf16[512,1536]{1,0:T(8,128)(2,1)S(1)} %copy-done.41), channel_id=1, source_target_pairs={{0,8},{4,12},{8,0},{12,4},{16,24},{20,28},{24,16},{28,20},{1,9},{5... | collective-permute-start | bytes 4718600 | tf_op jit(solution)/shard_map/ppermute | solution.py:318
  892.4 44.5 %collective-permute-start.80 = (bf16[1024,512]{1,0:T(8,128)(2,1)}, bf16[1024,512]{1,0:T(8,128)(2,1)S(1)}, u32[]{:S(2)}, u32[]{:S(2)}) collective-permute-start(bf16[1024,512]{1,0:T(8,128)(2,1)} %get-tuple-element.2879), channel_id=1, source_target_pairs={{0,8},{4,12},{8,0},{12,4},{16,24},{20,28},{24,16},{28,20},{1,9},{5... | collective-permute-start | bytes 3145736 | tf_op jit(solution)/shard_map/ppermute | solution.py:318
  893.9 43.0 %collective-permute-start.81 = (bf16[1024,512]{1,0:T(8,128)(2,1)}, bf16[1024,512]{1,0:T(8,128)(2,1)S(1)}, u32[]{:S(2)}, u32[]{:S(2)}) collective-permute-start(bf16[1024,512]{1,0:T(8,128)(2,1)} %get-tuple-element.2882), channel_id=1, source_target_pairs={{0,16},{4,20},{8,24},{12,28},{16,0},{20,4},{24,8},{28,12},{1,17},{... | collective-permute-start | bytes 3145736 | tf_op jit(solution)/shard_map/ppermute | solution.py:318
  895.2 41.6 %collective-permute-start.78 = (bf16[1024,256]{1,0:T(8,128)(2,1)S(1)}, bf16[1024,256]{1,0:T(8,128)(2,1)}, u32[]{:S(2)}, u32[]{:S(2)}) collective-permute-start(bf16[1024,256]{1,0:T(8,128)(2,1)S(1)} %add_convert_fusion.11), channel_id=1, source_target_pairs={{0,16},{4,20},{8,24},{12,28},{16,0},{20,4},{24,8},{28,12},{1,17},{... | collective-permute-start | bytes 1572872 | tf_op jit(solution)/shard_map/ppermute | solution.py:318
  896.3 40.6 %collective-permute-start.77 = (bf16[1024,256]{1,0:T(8,128)(2,1)S(1)}, bf16[1024,256]{1,0:T(8,128)(2,1)}, u32[]{:S(2)}, u32[]{:S(2)}) collective-permute-start(bf16[1024,256]{1,0:T(8,128)(2,1)S(1)} %add_convert_fusion.12), channel_id=1, source_target_pairs={{0,8},{4,12},{8,0},{12,4},{16,24},{20,28},{24,16},{28,20},{1,9},{5... | collective-permute-start | bytes 1572872 | tf_op jit(solution)/shard_map/ppermute | solution.py:318
  (200 other events, 2656.5 us)
Sparse Core Ops, SparseCore 0:
  80.4 44.4 all-gather.2
  175.7 175.4 all-gather.4
  526.0 58.1 reduce-scatter.2
  590.1 108.7 reduce-scatter.4

commit v9 on v8

--- a/solution.py
+++ b/solution.py
@@ -920,7 +920,6 @@
     grad_y_sent = to_sequences_send(s.cotangent)
     s.came_far = far(*s.came_near)
     s.came_other = [s.came_own, *(across(block, CORE) for block in s.came_near)]
-    s.grad_y_came = grad_y_sent
     gains = rolled(s.gains.astype(full))
     s.mlp_gains = gains[1:]
     s.attn_gains = gains[:1]
@@ -983,7 +982,6 @@
             *projected[1:], earlier,
         )
 
-    ffn_own = lax.all_gather(s.ffn_block, "shard", axis=0, tiled=True)
     came_last = jnp.concatenate(s.came_far, 0)
     s.came_last = (came_last, across(came_last, CORE))
     s.out_near = near(s.out_own)
@@ -994,23 +992,27 @@
             for i, (block, other) in enumerate(zip((s.came, *s.came_near), s.came_other))
         ]
     )
-    del s.came_far, s.ffn_block
-    s.end()
-
+    s.grad_y_came = grad_y_sent
+    del s.came_far
+    s.end()
+
+    ffn_own = lax.all_gather(s.ffn_block, "shard", axis=0, tiled=True)
+    grad_y = jnp.concatenate(in_turn(s.grad_y_came), 0)
+    s.grad_y = jnp.where(s.valid > 0, grad_y, jnp.zeros_like(grad_y))
+    grad_y_near = near(s.grad_y)
     s.out_far = far(*s.out_near)
     s.out_near_other = [across(block, CORE) for block in s.out_near]
     s.earlier = [lax.ppermute(p[2], "rep", upward) for p in s.projected]
     (s.projected_last,) = in_order([project_call(3, *s.came_last)])
-    s.end()
-
-    grad_y = jnp.concatenate(in_turn(s.grad_y_came), 0)
-    s.grad_y = jnp.where(s.valid > 0, grad_y, jnp.zeros_like(grad_y))
-    grad_y_near = near(s.grad_y)
+    del s.ffn_block, s.grad_y_came
+    s.end()
+
     out_last = jnp.concatenate(s.out_far, 0)
     s.out_last = (out_last, across(out_last, CORE))
     s.earlier_last = lax.ppermute(s.projected_last[2], "rep", upward)
     s.attended = in_order([attend_call(*pair) for pair in zip(s.projected, s.earlier)])
-    del s.out_far, s.grad_y_came
+    s.grad_y_near = grad_y_near
+    del s.out_far
     s.end()
 
     s.projected = [*s.projected, s.projected_last]
@@ -1023,13 +1025,12 @@
     s.attended = [*s.attended, last]
     s.mixed = [a[0] for a in s.attended]
     s.resid, s.mid = close_attention(s.x_low, s.mixed, s.out_blocks, s.mlp_gains)
-    s.grad_y_near = grad_y_near
+    s.grad_y_far = far(*s.grad_y_near)
     del s.out_own, s.out_own_other, s.out_near, s.out_near_other, s.out_last
     del s.projected_last, s.earlier_last
     s.end()
 
     s.mid_near = near(s.mid)
-    s.grad_y_far = far(*s.grad_y_near)
     s.end()
 
     s.mid_far = far(*s.mid_near)
@@ -1120,21 +1121,6 @@
     del s.gate_up_outer, s.down_mine
     s.end()
 
-    mlp_came = send_near(s.mlp_sent)
-    grad_mid = total(s.mid_came, s.mid_came_far, by_rows(s.mid_rest[1]), by_rows)
-    inverse_mid = lax.rsqrt(jnp.mean(s.resid * s.resid, -1, keepdims=True) + EPS)
-    mid_unit = s.resid * inverse_mid
-    s.mlp_gain_part = jnp.sum(mid_unit * grad_mid, 0)
-    s.grad_resid = s.grad_y.astype(full) + norm_back(
-        mid_unit, inverse_mid, grad_mid * s.mlp_gains
-    )
-    s.resid_low = s.grad_resid.astype(low)
-    s.resid_rolled = rolled(s.resid_low)
-    (s.gate_up_mine,) = in_order([outer_call(s.mids, s.hidden_own[1:], s.gate_up_came)])
-    del s.mid_came, s.mid_came_far, s.mid_rest, s.gate_up_came, s.hidden_own, s.hidden_other
-    del s.mids, s.grads_y, s.ffn_own, s.ffn_other
-    s.end()
-
     def back_call(i):
         raw, query, own_pair = s.projected[i]
         return (
@@ -1167,21 +1153,37 @@
         at = [places[i] for i in (2, 3, 1, 0)]
         return lambda first: row_outer([first], groups, 4, 4, came, at, part), left
 
+    s.mlp_came = send_near(s.mlp_sent)
+    grad_mid = total(s.mid_came, s.mid_came_far, by_rows(s.mid_rest[1]), by_rows)
+    inverse_mid = lax.rsqrt(jnp.mean(s.resid * s.resid, -1, keepdims=True) + EPS)
+    mid_unit = s.resid * inverse_mid
+    s.mlp_gain_part = jnp.sum(mid_unit * grad_mid, 0)
+    s.grad_resid = s.grad_y.astype(full) + norm_back(
+        mid_unit, inverse_mid, grad_mid * s.mlp_gains
+    )
+    s.resid_low = s.grad_resid.astype(low)
+    s.resid_rolled = rolled(s.resid_low)
+    s.returned = {}
+    back, s.out_odd, s.gate_up_mine = in_order(
+        [
+            back_call(3),
+            odd_call(s.resid_rolled, s.mixed, 1),
+            outer_call(s.mids, s.hidden_own[1:], s.gate_up_came),
+        ]
+    )
+    s.backs = {3: back}
+    s.down_total = down_total
+    del s.mid_came, s.mid_came_far, s.mid_rest, s.gate_up_came, s.hidden_own, s.hidden_other
+    del s.mids, s.grads_y, s.ffn_own, s.ffn_other, s.mlp_sent
+    s.end()
+
     gate_up_total = lax.psum_scatter(s.gate_up_mine, "shard", scatter_dimension=0, tiled=True)
-    s.returned = {}
-    s.out_odd, back = in_order([odd_call(s.resid_rolled, s.mixed, 1), back_call(3)])
-    s.backs = {3: back}
-    s.mlp_came = mlp_came
-    s.down_total = down_total
-    del s.gate_up_mine, s.mlp_sent
-    s.end()
-
     s.mlp_came_far = send_far(s.mlp_came, by_rows(s.mlp_rest[0]), by_rows)
     s.out_came = across(s.out_odd, CORE)
     give_back(3)
     back1, back2 = in_order([back_call(1), back_call(2)])
     s.backs = s.backs | {1: back1, 2: back2}
-    del s.out_odd
+    del s.out_odd, s.gate_up_mine
     s.end()
 
     s.down_near = near(s.down_total)
@@ -1201,24 +1203,23 @@
     del s.mlp_came, s.mlp_came_far, s.mlp_rest, s.out_came, s.resid
     s.end()
 
-    output_sent = from_sequences_send(s.output)
-    s.output_first = output_sent[0]
     s.out_near = send_near((s.out_head[0], s.out_tail[0]))
     s.down_far = far(*s.down_near)
     give_back(0)
     finished1, finished2 = in_order([finish_call(1), finish_call(2)])
     s.finished = s.finished | {1: finished1, 2: finished2}
-    del s.output
     s.gate_up_total = gate_up_total
     s.end()
 
+    def odd_half(half):
+        return odd_call(s.normed, [s.finished[i][1] for i in range(4)], half)
+
     s.out_far = send_far(s.out_near, (s.out_tail[1], s.out_head[1]), by_columns)
-    s.down_own = jnp.concatenate([s.down_total, *s.down_near, *s.down_far], 0)
-    s.down_other = across(s.down_own, CORE)
+    s.down_spread = jnp.concatenate([s.down_total, *s.down_near, *s.down_far], 0)
+    s.down_spread_other = across(s.down_spread, CORE)
     (finished,) = in_order([finish_call(0)])
     s.finished = s.finished | {0: finished}
-    (s.qkv_odd,) = in_order([odd_call(s.normed, [s.finished[i][1] for i in range(4)])])
-    s.output_second = output_sent[1]
+    (s.odd0,) = in_order([odd_half(0)])
     del s.down_total, s.down_near, s.down_far
     s.end()
 
@@ -1227,8 +1228,8 @@
     def whole_call(widths, own, other):
         return lambda first: whole_columns(my_group, first, other, widths), own
 
-    s.qkv_came = across(s.qkv_odd, CORE)
     s.gate_up_near = near(s.gate_up_total)
+    s.came0 = across(s.odd0, CORE)
     out_sum = total(s.out_near, s.out_far, (s.out_head[2], s.out_tail[2]), by_columns)
     s.out_chunks = jnp.split(out_sum.astype(low), shards, 0)
     s.out_ring = ring_sum_first(s.out_chunks)
@@ -1238,139 +1239,129 @@
         for pair in ((s.own_blocks[2 * i], block[0]), (s.own_blocks[2 * i + 1], block[1]))
     ] + [(s.own_blocks[6 + i], s.came_last[i]) for i in range(2)]
     blocks = [part for i in range(4) for part in s.finished[i][:2]]
-    grad_in, s.whole_down = in_order(
+    s.odd1, grad_in = in_order(
         [
+            odd_half(1),
             (lambda first: back_to_rows([first, *blocks[1:]], weights), blocks[0]),
-            whole_call((units,), s.down_own, s.down_other),
         ]
     )
     grad_in = rolled(grad_in)
     x_unit = s.x_low.astype(full) * s.inverse_in
-    s.attn_gain_part = jnp.sum(x_unit * grad_in, 0)
-    s.grad_tokens = (
-        s.grad_resid + norm_back(x_unit, s.inverse_in, grad_in * s.attn_gains)
-    ).astype(low)
-    del s.qkv_odd, s.out_near, s.out_far, s.out_head, s.out_tail, s.down_own, s.down_other
-    del s.own_blocks, s.came, s.came_near, s.came_other, s.came_last, s.grad_resid, s.x_low
-    s.end()
-
-    s.gate_up_far = far(*s.gate_up_near)
-    s.out_ring_last = around(rounded_sum(s.out_chunks[3], s.out_ring[0]), 1)
-    even = [s.finished[i][0] for i in range(4)]
-    first_head, first_tail, second_head, second_tail = in_order(
-        [
-            call(s.normed, even, s.qkv_came, half, range(half, 8, 2))
-            for half in range(2)
-            for call in (head_call, tail_call)
-        ]
-    )
-    s.heads = [first_head, second_head]
-    s.tails = [first_tail, second_tail]
     s.gain_parts = jnp.concatenate(
         [
-            s.attn_gain_part,
+            jnp.sum(x_unit * grad_in, 0),
             s.mlp_gain_part,
             sum(s.backs[i][3] for i in range(4))[0],
             sum(s.finished[i][2] for i in range(4))[0],
         ]
     )
+    s.grad_tokens = (
+        s.grad_resid + norm_back(x_unit, s.inverse_in, grad_in * s.attn_gains)
+    ).astype(low)
+    del s.odd0, s.out_near, s.out_far, s.out_head, s.out_tail, s.backs
+    del s.own_blocks, s.came, s.came_near, s.came_other, s.came_last, s.grad_resid, s.x_low
+    s.end()
+
+    def halves_call(half, came):
+        even = [s.finished[i][0] for i in range(4)]
+        return [call(s.normed, even, came, half) for call in (head_call, tail_call)]
+
+    output_sent = from_sequences_send(s.output)
+    s.came1 = across(s.odd1, CORE)
+    s.out_ring_last = around(rounded_sum(s.out_chunks[3], s.out_ring[0]), 1)
+    s.head0, s.tail0 = in_order(halves_call(0, s.came0))
+    del s.odd1, s.came0
+    s.end()
+
+    def qkv_chunks(came, came_far, head, tail):
+        own = total(came, came_far, (head[2], tail[2]), by_columns)
+        return jnp.split(own.astype(low), shards, 0)
+
+    s.near0 = send_near((s.head0[0], s.tail0[0]))
     s.gain_came = across(s.gain_parts, CORE)
-    del s.qkv_came, s.finished, s.backs
-    s.end()
-
-    grad_tokens_sent = from_sequences_send(s.grad_tokens)
-
-    def qkv_near(half):
-        return send_near((s.heads[half][0], s.tails[half][0]))
-
-    def qkv_far(came, half):
-        return send_far(came, (s.tails[half][1], s.heads[half][1]), by_columns)
-
-    def qkv_chunks(came, came_far, half):
-        own = total(came, came_far, (s.heads[half][2], s.tails[half][2]), by_columns)
-        return jnp.split(own.astype(low), shards, 0)
-
-    s.near0 = qkv_near(0)
-    s.gate_up_own = jnp.concatenate([s.gate_up_total, *s.gate_up_near, *s.gate_up_far], 0)
-    s.gate_up_other = across(s.gate_up_own, CORE)
+    s.head1, s.tail1, s.whole_down = in_order(
+        [*halves_call(1, s.came1), whole_call((units,), s.down_spread, s.down_spread_other)]
+    )
     s.out_total = rounded_sum(s.out_chunks[0], s.out_ring[1], s.out_ring_last)
+    s.output_came = output_sent
+    del s.came1, s.down_spread, s.down_spread_other, s.output, s.finished
+    del s.out_chunks, s.out_ring, s.out_ring_last
+    s.end()
+
+    tokens_sent = from_sequences_send(s.grad_tokens)
+    s.far0 = send_far(s.near0, (s.tail0[1], s.head0[1]), by_columns)
+    s.near1 = send_near((s.head1[0], s.tail1[0]))
     s.gain_parts = s.gain_parts + s.gain_came
+    s.tokens_first = tokens_sent[0]
+    s.end()
+
+    s.chunks0 = qkv_chunks(s.near0, s.far0, s.head0, s.tail0)
+    s.ring0 = ring_sum_first(s.chunks0)
+    s.far1 = send_far(s.near1, (s.tail1[1], s.head1[1]), by_columns)
     s.gain_came = across(s.gain_parts, ACROSS_X)
-    s.tokens_first = grad_tokens_sent[0]
-    del s.out_chunks, s.out_ring, s.out_ring_last, s.gate_up_near, s.gate_up_far
-    del s.gate_up_total, s.grad_tokens
-    s.end()
-
-    s.far0 = qkv_far(s.near0, 0)
-    s.near1 = qkv_near(1)
+    del s.near0, s.far0, s.head0, s.tail0
+    s.end()
+
+    s.last0 = around(rounded_sum(s.chunks0[3], s.ring0[0]), 1)
+    s.chunks1 = qkv_chunks(s.near1, s.far1, s.head1, s.tail1)
+    s.ring1 = ring_sum_first(s.chunks1)
+    s.gate_up_far = far(*s.gate_up_near)
     s.gain_parts = s.gain_parts + s.gain_came
-    s.gain_came = across(s.gain_parts, ACROSS_Y)
-    s.tokens_second = grad_tokens_sent[1]
-    (s.whole_gate_up,) = in_order([whole_call((units, units), s.gate_up_own, s.gate_up_other)])
-    del s.gate_up_own, s.gate_up_other
-    s.end()
-
-    s.chunks0 = qkv_chunks(s.near0, s.far0, 0)
-    s.ring0 = ring_sum_first(s.chunks0)
-    s.far1 = qkv_far(s.near1, 1)
-    s.gain_parts = s.gain_parts + s.gain_came
-    s.gain_came = lax.ppermute(s.gain_parts, "shard", [(i, i ^ 1) for i in range(shards)])
-    del s.near0, s.far0
-    s.end()
-
-    s.last0 = around(rounded_sum(s.chunks0[3], s.ring0[0]), 1)
-    s.chunks1 = qkv_chunks(s.near1, s.far1, 1)
-    s.ring1 = ring_sum_first(s.chunks1)
-    s.gain_parts = s.gain_parts + s.gain_came
-    s.gain_came = lax.ppermute(s.gain_parts, "shard", [(i, i ^ 2) for i in range(shards)])
-    del s.near1, s.far1, s.heads, s.tails
+    del s.near1, s.far1, s.head1, s.tail1
     s.end()
 
     query_total = rounded_sum(s.chunks0[0], s.ring0[1], s.last0)
     s.total0 = jnp.concatenate([query_total, s.out_total], 1)
     s.spread0 = near(s.total0)
     s.last1 = around(rounded_sum(s.chunks1[3], s.ring1[0]), 1)
-    s.gain_sums = s.gain_parts + s.gain_came
-    del s.chunks0, s.ring0, s.last0, s.out_total
+    s.gate_up_own = jnp.concatenate([s.gate_up_total, *s.gate_up_near, *s.gate_up_far], 0)
+    s.gate_up_other = across(s.gate_up_own, CORE)
+    s.gain_came = across(s.gain_parts, ACROSS_Y)
+    del s.chunks0, s.ring0, s.last0, s.out_total, s.gate_up_near, s.gate_up_far, s.gate_up_total
     s.end()
 
     s.spread_far0 = far(*s.spread0)
     s.total1 = rounded_sum(s.chunks1[0], s.ring1[1], s.last1)
     s.spread1 = near(s.total1)
-    del s.chunks1, s.ring1, s.last1
+    s.gain_parts = s.gain_parts + s.gain_came
+    s.gain_came = lax.ppermute(s.gain_parts, "shard", [(i, i ^ 1) for i in range(shards)])
+    (s.whole_gate_up,) = in_order([whole_call((units, units), s.gate_up_own, s.gate_up_other)])
+    del s.chunks1, s.ring1, s.last1, s.gate_up_own, s.gate_up_other
     s.end()
 
     s.own0 = jnp.concatenate([s.total0, *s.spread0, *s.spread_far0], 0)
     s.other0 = across(s.own0, CORE)
     s.spread_far1 = far(*s.spread1)
+    s.gain_parts = s.gain_parts + s.gain_came
+    s.gain_came = lax.ppermute(s.gain_parts, "shard", [(i, i ^ 2) for i in range(shards)])
     del s.total0, s.spread0, s.spread_far0
     s.end()
 
     s.own1 = jnp.concatenate([s.total1, *s.spread1, *s.spread_far1], 0)
     s.other1 = across(s.own1, CORE)
     (s.whole0,) = in_order([whole_call((head_columns, head_columns), s.own0, s.other0)])
+    gain_sums = s.gain_parts + s.gain_came
+    s.wide = lax.dynamic_slice_in_dim(
+        gain_sums[: 2 * width].reshape(2, width), shard_at * piece, piece, 1
+    )
+    s.narrow = gain_sums[2 * width :]
     del s.own0, s.other0, s.total1, s.spread1, s.spread_far1
     s.end()
 
     ((whole_key, whole_value),) = in_order(
         [whole_call((head_dim, head_dim), s.own1, s.other1)]
     )
-    gain_sums = s.gain_sums
-    wide = lax.dynamic_slice_in_dim(
-        gain_sums[: 2 * width].reshape(2, width), shard_at * piece, piece, 1
-    )
-    narrow = gain_sums[2 * width :]
     return (
-        jnp.stack(in_turn([s.output_first, s.output_second])),
-        jnp.stack(in_turn([s.tokens_first, s.tokens_second])),
-        wide[0],
+        jnp.stack(in_turn(s.output_came)),
+        jnp.stack(in_turn([s.tokens_first, tokens_sent[1]])),
+        s.wide[0],
         s.whole0[0],
         whole_key,
         whole_value,
-        narrow[:head_dim],
-        narrow[head_dim:],
+        s.narrow[:head_dim],
+        s.narrow[head_dim:],
         s.whole0[1],
-        wide[1],
+        s.wide[1],
         *s.whole_gate_up,
         *s.whole_down,
     )

time: 1050 us -> 1000 us (0.952)
  waiting for transfers between devices: 311 us -> 243 us
    ppermute x73 -> x74, waiting for transfers between devices: 206 us -> 159 us  [across(): return lax.ppermute(x, 'rep', [(i, i ^ mask) for i in range(count)])]
    ppermute x12, starting transfers between devices: 15.6 us -> 37.2 us  [around(): lax.ppermute(x, 'shard', [(i, (i + by) % count) for i in range(count)])]
    ppermute x4, waiting for transfers between devices: 26.7 us -> 16.1 us  [from_sequences_send(): lax.ppermute(lax.dynamic_index_in_dim(x, turn ^ odd, 0, keepdims=False),...]
    ppermute x73 -> x74, starting transfers between devices: 102 us -> 95.3 us  [across(): return lax.ppermute(x, 'rep', [(i, i ^ mask) for i in range(count)])]
    pallas_call x12 -> x13, Pallas kernels: 115 us -> 120 us  [row_outer(): pl.pallas_call(body, grid=(tiles,), out_shape=[jax.ShapeDtypeStruct((tile...]
    unnamed x266 -> x252, local copies, waits for them, and re-layouts: 29 us -> 28.7 us
  transfers between devices with their start and end apart: 107 -> 108, of which waited for: 35 -> 31; matrix products, arithmetic and copies ran while one was open for 8% -> 10% of each run, Pallas kernels for 36% -> 38%
where the time goes in v9:
time: 1000 us; the launch traced here: 992 us
  Pallas kernels  430 us (43%)
  waiting for transfers between devices  243 us (24%)
  starting transfers between devices  165 us (16%)
  other arithmetic  70 us (7%)
  local copies, waits for them, and re-layouts  68 us (7%)
  between operations  16.1 us (2%)
    ppermute x74, waiting for transfers between devices, across(): return lax.ppermute(x, 'rep', [(i, i ^ mask) for i in range(count)])  159 us
    pallas_call x13, Pallas kernels, row_outer(): pl.pallas_call(body, grid=(tiles,), out_shape=[jax.ShapeDtypeStruct((tile...  120 us
    pallas_call x16, Pallas kernels, call(): pl.pallas_call(body, grid=(1,), out_shape=outs, in_specs=in_specs, out_sp...  119 us
    ppermute x74, starting transfers between devices, across(): return lax.ppermute(x, 'rep', [(i, i ^ mask) for i in range(count)])  95.3 us
    pallas_call x2, Pallas kernels, hidden_units(): pl.pallas_call(body, grid=(3,), out_shape=[jax.ShapeDtypeStruct((rows, un...  59.8 us
    pallas_call x4, Pallas kernels, from_hidden(): pl.pallas_call(body, grid=(4,), out_shape=[jax.ShapeDtypeStruct((2 * rows...  59.1 us
    pallas_call x4, Pallas kernels, whole_columns(): pl.pallas_call(body, grid_spec=pltpu.PrefetchScalarGridSpec(num_scalar_pr...  44.3 us
    ppermute x12, waiting for transfers between devices, around(): lax.ppermute(x, 'shard', [(i, (i + by) % count) for i in range(count)])  37.2 us
  transfers between devices with their start and end apart: 108, of which 31 were waited for; matrix products, arithmetic and copies ran while one was open for 10% of the time, Pallas kernels for 38%

profile of v9, /device:TPU:0, one launch (start us, length us, event | category | flops | bytes accessed | tf_op | source)
XLA Modules:
  0.0 992.2 jit_solution(18206317136060591478)
XLA Ops:
  32.0 11.3 %collective-permute-done = bf16[528,512]{1,0:T(8,128)(2,1)} collective-permute-done((bf16[528,512]{1,0:T(8,128)(2,1)}, bf16[528,512]{1,0:T(8,128)(2,1)}, u32[]{:S(2)}, u32[]{:S(2)}) %collective-permute-start) | collective-permute-done | bytes 540704 | tf_op jit(solution)/shard_map/ppermute | solution.py:323
  45.0 13.5 %collective-permute-done.3 = bf16[528,512]{1,0:T(8,128)(2,1)S(1)} collective-permute-done((bf16[528,512]{1,0:T(8,128)(2,1)}, bf16[528,512]{1,0:T(8,128)(2,1)S(1)}, u32[]{:S(2)}, u32[]{:S(2)}) %collective-permute-start.3) | collective-permute-done | bytes 540704 | tf_op jit(solution)/shard_map/ppermute | solution.py:323
  67.9 9.5 collective-permute-start.7
  82.0 19.0 %collective-permute-done.8 = bf16[256,2048]{1,0:T(8,128)(2,1)S(1)} collective-permute-done((bf16[256,2048]{1,0:T(8,128)(2,1)}, bf16[256,2048]{1,0:T(8,128)(2,1)S(1)}, u32[]{:S(2)}, u32[]{:S(2)}) %collective-permute-start.8) | collective-permute-done | bytes 1048608 | tf_op jit(solution)/shard_map/ppermute | solution.py:385
  103.1 31.2 %collective-permute-start.11 = (bf16[1536,512]{1,0:T(8,128)(2,1)}, bf16[1536,512]{1,0:T(8,128)(2,1)}, u32[]{:S(2)}, u32[]{:S(2)}) collective-permute-start(bf16[1536,512]{1,0:T(8,128)(2,1)} %collective-permute-done.4.came0.refs_13_), channel_id=1, source_target_pairs={{0,4},{4,0},{8,12},{12,8},{16,20},{20,16},{24,28},{28,24},{1,5},{5... | collective-permute-start | bytes 4718600 | tf_op jit(solution)/shard_map/ppermute | solution.py:318
  148.1 10.6 %collective-permute-done.10 = bf16[768,512]{1,0:T(8,128)(2,1)} collective-permute-done((bf16[768,512]{1,0:T(8,128)(2,1)}, bf16[768,512]{1,0:T(8,128)(2,1)}, u32[]{:S(2)}, u32[]{:S(2)}) %collective-permute-start.10) | collective-permute-done | bytes 786464 | tf_op jit(solution)/shard_map/ppermute | solution.py:318
  243.4 13.4 %collective-permute-done.28.refs_7_.refs_2_ = bf16[512,2048]{1,0:T(8,128)(2,1)S(1)} collective-permute-done((bf16[512,2048]{1,0:T(8,128)(2,1)S(1)}, bf16[512,2048]{1,0:T(8,128)(2,1)S(1)}, u32[]{:S(2)}, u32[]{:S(2)}) %collective-permute-start.28) | collective-permute-done | bytes 2097184 | tf_op jit(solution)/shard_map/ppermute | solution.py:318
  266.9 11.7 %close_attention.1 = (f32[512,2048]{1,0:T(8,128)}, bf16[512,2048]{1,0:T(8,128)(2,1)}) custom-call(bf16[512,2048]{1,0:T(8,128)(2,1)} %pad_maximum_fusion.3.x, bf16[512,512]{1,0:T(8,128)(2,1)} %get-tuple-element.2416.refs_0_.refs_1_.refs_4_, bf16[512,512]{1,0:T(8,128)(2,1)} %get-tuple-element.2413.refs_1_.refs_2_.refs_3_, ...), custom_call_target="tpu_custom_call" | custom-call | flops 1 | bytes 1 | tf_op jit(solution)/shard_map/close_attention/pallas_call | solution.py:792
  286.6 42.8 %collective-permute-done.33.refs_2_ = bf16[512,2048]{1,0:T(8,128)(2,1)S(1)} collective-permute-done((bf16[512,2048]{1,0:T(8,128)(2,1)}, bf16[512,2048]{1,0:T(8,128)(2,1)S(1)}, u32[]{:S(2)}, u32[]{:S(2)}) %collective-permute-start.33) | collective-permute-done | bytes 2097184 | tf_op jit(solution)/shard_map/ppermute | solution.py:318
  333.7 19.5 %collective-permute-done.35.refs_4_ = bf16[256,2048]{1,0:T(8,128)(2,1)S(1)} collective-permute-done((bf16[256,2048]{1,0:T(8,128)(2,1)S(1)}, bf16[256,2048]{1,0:T(8,128)(2,1)S(1)}, u32[]{:S(2)}, u32[]{:S(2)}) %collective-permute-start.35) | collective-permute-done | bytes 1048608 | tf_op jit(solution)/shard_map/ppermute | solution.py:318
  358.6 29.7 %hidden_units.2 = (bf16[2048,768]{1,0:T(8,128)(2,1)}, bf16[2048,768]{1,0:T(8,128)(2,1)}, bf16[2048,768]{1,0:T(8,128)(2,1)}) custom-call(bf16[512,2048]{1,0:T(8,128)(2,1)} %get-tuple-element.2288.refs_0_, bf16[512,2048]{1,0:T(8,128)(2,1)} %copy-done.13, bf16[512,2048]{1,0:T(8,128)(2,1)} %copy-done.12, bf16[256,2048]{1,0:T(8,128)(2,1)} %copy-done.26, ...), custom_call_target="tpu_custom_call" | custom-call | flops 1 | bytes 1 | tf_op jit(solution)/shard_map/hidden_units/pallas_call | solution.py:659
  388.3 30.1 %hidden_units.3 = (bf16[2048,768]{1,0:T(8,128)(2,1)}, bf16[2048,768]{1,0:T(8,128)(2,1)}, bf16[2048,768]{1,0:T(8,128)(2,1)}) custom-call(bf16[512,2048]{1,0:T(8,128)(2,1)} %get-tuple-element.2288.refs_0_, bf16[512,2048]{1,0:T(8,128)(2,1)} %copy-done.13, bf16[512,2048]{1,0:T(8,128)(2,1)} %copy-done.12, bf16[256,2048]{1,0:T(8,128)(2,1)} %copy-done.26, ...), custom_call_target="tpu_custom_call" | custom-call | flops 1 | bytes 1 | tf_op jit(solution)/shard_map/hidden_units/pallas_call | solution.py:659
  418.4 12.6 %row_outer.13 = bf16[2048,768]{1,0:T(8,128)(2,1)} custom-call(bf16[512,2048]{1,0:T(8,128)(2,1)} %copy-done.7, bf16[512,2048]{1,0:T(8,128)(2,1)} %copy-done.15, bf16[512,2048]{1,0:T(8,128)(2,1)} %copy-done.14, bf16[256,2048]{1,0:T(8,128)(2,1)} %copy-done.28, bf16[256,2048]{1,0:T(8,128)(2,1)} %copy-done.27, ...), custom_call_target="tpu_custom_call" | custom-call | flops 6442450944 | bytes 11534336 | tf_op jit(solution)/shard_map/row_outer/pallas_call | solution.py:742
  431.5 18.8 %from_hidden.4 = (bf16[512,2048]{1,0:T(8,128)(2,1)}, bf16[512,2048]{1,0:T(8,128)(2,1)}) custom-call(bf16[2048,768]{1,0:T(8,128)(2,1)} %get-tuple-element.2299.refs_0_.refs_1_.refs_2_.refs_3_.refs_5_, bf16[2048,768]{1,0:T(8,128)(2,1)} %get-tuple-element.2299.refs_0_.refs_1_.refs_2_.refs_3_.refs_5_, ...), custom_call_target="tpu_custom_call" | custom-call | flops 1 | bytes 1 | tf_op jit(solution)/shard_map/from_hidden/pallas_call | solution.py:698
  453.3 13.2 %row_outer.14 = bf16[2048,768]{1,0:T(8,128)(2,1)} custom-call(bf16[512,2048]{1,0:T(8,128)(2,1)} %copy-done.7, bf16[512,2048]{1,0:T(8,128)(2,1)} %copy-done.15, bf16[512,2048]{1,0:T(8,128)(2,1)} %copy-done.14, bf16[256,2048]{1,0:T(8,128)(2,1)} %copy-done.28, bf16[256,2048]{1,0:T(8,128)(2,1)} %copy-done.27, ...), custom_call_target="tpu_custom_call" | custom-call | flops 6442450944 | bytes 11534336 | tf_op jit(solution)/shard_map/row_outer/pallas_call | solution.py:742
  466.5 18.8 %from_hidden.5 = (bf16[512,2048]{1,0:T(8,128)(2,1)}, bf16[512,2048]{1,0:T(8,128)(2,1)}) custom-call(bf16[2048,768]{1,0:T(8,128)(2,1)} %get-tuple-element.2299.refs_0_.refs_1_.refs_2_.refs_3_.refs_5_, bf16[2048,768]{1,0:T(8,128)(2,1)} %get-tuple-element.2299.refs_0_.refs_1_.refs_2_.refs_3_.refs_5_, ...), custom_call_target="tpu_custom_call" | custom-call | flops 1 | bytes 1 | tf_op jit(solution)/shard_map/from_hidden/pallas_call | solution.py:698
  485.3 19.4 %row_outer.15 = bf16[2048,1536]{1,0:T(8,128)(2,1)} custom-call(bf16[512,2048]{1,0:T(8,128)(2,1)} %get-tuple-element.2288.refs_0_, bf16[512,2048]{1,0:T(8,128)(2,1)} %copy-done.13, bf16[512,2048]{1,0:T(8,128)(2,1)} %copy-done.12, bf16[256,2048]{1,0:T(8,128)(2,1)} %copy-done.26, bf16[256,2048]{1,0:T(8,128)(2,1)} %copy-done.25, ...), custom_call_target="tpu_custom_call" | custom-call | flops 12884901888 | bytes 14680064 | tf_op jit(solution)/shard_map/row_outer/pallas_call | solution.py:742
  511.8 10.6 %from_hidden.6 = (bf16[512,2048]{1,0:T(8,128)(2,1)}, bf16[512,2048]{1,0:T(8,128)(2,1)}) custom-call(bf16[2048,768]{1,0:T(8,128)(2,1)} %get-tuple-element.2208.refs_5_.refs_0_.refs_1_.refs_2_.refs_3_, bf16[2048,768]{1,0:T(8,128)(2,1)} %get-tuple-element.2208.refs_5_.refs_0_.refs_1_.refs_2_.refs_3_, ...), custom_call_target="tpu_custom_call" | custom-call | flops 1 | bytes 1 | tf_op jit(solution)/shard_map/from_hidden/pallas_call | solution.py:698
  522.4 10.9 %from_hidden.7 = (bf16[512,2048]{1,0:T(8,128)(2,1)}, bf16[512,2048]{1,0:T(8,128)(2,1)}) custom-call(bf16[2048,768]{1,0:T(8,128)(2,1)} %get-tuple-element.2208.refs_5_.refs_0_.refs_1_.refs_2_.refs_3_, bf16[2048,768]{1,0:T(8,128)(2,1)} %get-tuple-element.2208.refs_5_.refs_0_.refs_1_.refs_2_.refs_3_, ...), custom_call_target="tpu_custom_call" | custom-call | flops 1 | bytes 1 | tf_op jit(solution)/shard_map/from_hidden/pallas_call | solution.py:698
  547.6 13.4 %attend_back.4 = (bf16[512,512]{1,0:T(8,128)(2,1)}, f32[512,512]{1,0:T(8,128)}, bf16[512,512]{1,0:T(8,128)(2,1)}, f32[1,128]{1,0:T(1,128)}) custom-call(s32[2]{0:T(128)} %pad_add_fusion.info, bf16[512,512]{1,0:T(8,128)(2,1)} %get-tuple-element.2255.query, bf16[512,512]{1,0:T(8,128)(2,1)} %copy-done.40, bf16[512,512]{1,0:T(8,128)(2,1)} %get-tuple-element.2257.own, ...), custom_call_target="tpu_custom_call" | custom-call | flops 1 | bytes 1 | tf_op jit(solution)/shard_map/attend_back/pallas_call | solution.py:619
  571.1 19.7 %row_outer.17 = bf16[2048,1536]{1,0:T(8,128)(2,1)} custom-call(bf16[512,2048]{1,0:T(8,128)(2,1)} %get-tuple-element.2288.refs_0_, bf16[512,2048]{1,0:T(8,128)(2,1)} %copy-done.13, bf16[512,2048]{1,0:T(8,128)(2,1)} %copy-done.12, bf16[256,2048]{1,0:T(8,128)(2,1)} %copy-done.26, bf16[256,2048]{1,0:T(8,128)(2,1)} %copy-done.25, ...), custom_call_target="tpu_custom_call" | custom-call | flops 12884901888 | bytes 14680064 | tf_op jit(solution)/shard_map/row_outer/pallas_call | solution.py:742
  600.1 13.2 %attend_back.5 = (bf16[512,512]{1,0:T(8,128)(2,1)}, f32[512,512]{1,0:T(8,128)}, bf16[512,512]{1,0:T(8,128)(2,1)}, f32[1,128]{1,0:T(1,128)}) custom-call(s32[2]{0:T(128)} %pad_add_fusion.info, bf16[512,512]{1,0:T(8,128)(2,1)} %get-tuple-element.2338.query, bf16[512,512]{1,0:T(8,128)(2,1)} %copy-done.39, bf16[512,512]{1,0:T(8,128)(2,1)} %get-tuple-element.2340.own, ...), custom_call_target="tpu_custom_call" | custom-call | flops 1 | bytes 1 | tf_op jit(solution)/shard_map/attend_back/pallas_call | solution.py:619
  613.3 13.5 %attend_back.6 = (bf16[512,512]{1,0:T(8,128)(2,1)}, f32[512,512]{1,0:T(8,128)}, bf16[512,512]{1,0:T(8,128)(2,1)}, f32[1,128]{1,0:T(1,128)}) custom-call(s32[2]{0:T(128)} %pad_add_fusion.info, bf16[512,512]{1,0:T(8,128)(2,1)} %get-tuple-element.2353.query, bf16[512,512]{1,0:T(8,128)(2,1)} %collective-permute-done.21.before, ...), custom_call_target="tpu_custom_call" | custom-call | flops 1 | bytes 1 | tf_op jit(solution)/shard_map/attend_back/pallas_call | solution.py:619
  648.8 13.2 %attend_back.7 = (bf16[512,512]{1,0:T(8,128)(2,1)}, f32[512,512]{1,0:T(8,128)}, bf16[512,512]{1,0:T(8,128)(2,1)}, f32[1,128]{1,0:T(1,128)}) custom-call(s32[2]{0:T(128)} %pad_add_fusion.info, bf16[512,512]{1,0:T(8,128)(2,1)} %get-tuple-element.2421.query, bf16[512,512]{1,0:T(8,128)(2,1)} %copy-done.37, bf16[512,512]{1,0:T(8,128)(2,1)} %get-tuple-element.2423.own, ...), custom_call_target="tpu_custom_call" | custom-call | flops 1 | bytes 1 | tf_op jit(solution)/shard_map/attend_back/pallas_call | solution.py:619
  685.0 19.1 %collective-permute-done.54 = bf16[256,768]{1,0:T(8,128)(2,1)S(1)} collective-permute-done((bf16[256,768]{1,0:T(8,128)(2,1)S(1)}, bf16[256,768]{1,0:T(8,128)(2,1)S(1)}, u32[]{:S(2)}, u32[]{:S(2)}) %collective-permute-start.54) | collective-permute-done | bytes 393248 | tf_op jit(solution)/shard_map/ppermute | solution.py:318
  742.3 15.8 %back_to_rows.1 = f32[512,2048]{1,0:T(8,128)} custom-call(bf16[512,512]{1,0:T(8,128)(2,1)} %get-tuple-element.2695.refs_0_.refs_4_, bf16[512,512]{1,0:T(8,128)(2,1)} %get-tuple-element.2612.refs_1_, bf16[512,512]{1,0:T(8,128)(2,1)} %get-tuple-element.2692.refs_2_.refs_1_.refs_3_, bf16[512,512]{1,0:T(8,128)(2,1)} %get-tuple-element.2615.refs_2_.refs_3_, ...), custom_call_target="tpu_custom_call" | custom-call | flops 1 | bytes 1 | tf_op jit(solution)/shard_map/back_to_rows/pallas_call | solution.py:845
  797.5 11.2 %whole_columns.4 = f32[512,6144]{1,0:T(8,128)} custom-call(s32[1]{0:T(128)} %bitcast.19.me_ref, bf16[2048,768]{1,0:T(8,128)(2,1)} %copy-done.24, bf16[2048,768]{1,0:T(8,128)(2,1)} %collective-permute-done.58.other_ref), custom_call_target="tpu_custom_call" | custom-call | flops 1 | bytes 1 | tf_op jit(solution)/shard_map/whole_columns/pallas_call | solution.py:434
  818.5 15.4 %collective-permute-done.74 = bf16[1024,256]{1,0:T(8,128)(2,1)S(1)} collective-permute-done((bf16[1024,256]{1,0:T(8,128)(2,1)S(1)}, bf16[1024,256]{1,0:T(8,128)(2,1)S(1)}, u32[]{:S(2)}, u32[]{:S(2)}) %collective-permute-start.74) | collective-permute-done | bytes 524320 | tf_op jit(solution)/shard_map/ppermute | solution.py:318
  835.2 22.0 %collective-permute-start.82 = (bf16[512,256]{1,0:T(8,128)(2,1)S(1)}, bf16[512,256]{1,0:T(8,128)(2,1)S(1)}, u32[]{:S(2)}, u32[]{:S(2)}) collective-permute-start(bf16[512,256]{1,0:T(8,128)(2,1)S(1)} %get-tuple-element.2929), channel_id=1, source_target_pairs={{0,3},{1,0},{2,1},{3,2},{4,7},{5,4},{6,5},{7,6},{8,11},{9,8},{10,9... | collective-permute-start | bytes 786440 | tf_op jit(solution)/shard_map/ppermute | solution.py:323
  861.7 9.0 collective-permute-done.80
  921.6 17.8 %whole_columns.5 = (f32[512,6144]{1,0:T(8,128)}, f32[512,6144]{1,0:T(8,128)}) custom-call(s32[1]{0:T(128)} %bitcast.19.me_ref, bf16[2048,1536]{1,0:T(8,128)(2,1)} %copy-done.16, bf16[2048,1536]{1,0:T(8,128)(2,1)} %copy-done.22), custom_call_target="tpu_custom_call" | custom-call | flops 1 | bytes 1 | tf_op jit(solution)/shard_map/whole_columns/pallas_call | solution.py:434
  958.3 16.1 %collective-permute-done.103 = bf16[256,2048]{1,0:T(8,128)(2,1)} collective-permute-done((bf16[256,2048]{1,0:T(8,128)(2,1)}, bf16[256,2048]{1,0:T(8,128)(2,1)}, u32[]{:S(2)}, u32[]{:S(2)}) %collective-permute-start.103) | collective-permute-done | bytes 1048608 | tf_op jit(solution)/shard_map/ppermute | solution.py:398
  (624 shorter events, 430.2 us)
Async XLA Ops:
  7.2 140.9 %all-gather.3.cloned.1.call-start = ((), (), s32[]{:S(2)}) async-start(), calls=%async_computation.2 | async-start | bytes 1310720 | tf_op jit(solution)/shard_map/all_gather | solution.py:907
  61.1 40.0 %collective-permute-start.6 = (bf16[1536,512]{1,0:T(8,128)(2,1)S(1)}, bf16[1536,512]{1,0:T(8,128)(2,1)}, u32[]{:S(2)}, u32[]{:S(2)}) collective-permute-start(bf16[1536,512]{1,0:T(8,128)(2,1)S(1)} %pad_maximum_fusion.8.came0.refs_9_), channel_id=1, source_target_pairs={{0,4},{4,0},{8,12},{12,8},{16,20},{20,16},{24,28},{28,24},{1,5},{5... | collective-permute-start | bytes 4718600 | tf_op jit(solution)/shard_map/ppermute | solution.py:318
  61.2 39.9 %collective-permute-start.5 = (bf16[1536,512]{1,0:T(8,128)(2,1)S(1)}, bf16[1536,512]{1,0:T(8,128)(2,1)}, u32[]{:S(2)}, u32[]{:S(2)}) collective-permute-start(bf16[1536,512]{1,0:T(8,128)(2,1)S(1)} %pad_maximum_fusion.8.came0.refs_9_), channel_id=1, source_target_pairs={{0,16},{4,20},{8,24},{12,28},{16,0},{20,4},{24,8},{28,12},{1,17},{... | collective-permute-start | bytes 4718600 | tf_op jit(solution)/shard_map/ppermute | solution.py:318
  62.7 38.3 %collective-permute-start.4 = (bf16[1536,512]{1,0:T(8,128)(2,1)S(1)}, bf16[1536,512]{1,0:T(8,128)(2,1)}, u32[]{:S(2)}, u32[]{:S(2)}) collective-permute-start(bf16[1536,512]{1,0:T(8,128)(2,1)S(1)} %pad_maximum_fusion.8.came0.refs_9_), channel_id=1, source_target_pairs={{0,8},{4,12},{8,0},{12,4},{16,24},{20,28},{24,16},{28,20},{1,9},{5... | collective-permute-start | bytes 4718600 | tf_op jit(solution)/shard_map/ppermute | solution.py:318
  80.4 278.2 %all-gather.5.cloned.1.call-start = ((), (), s32[]{:S(2)}) async-start(), calls=%async_computation.3 | async-start | bytes 11796480 | tf_op jit(solution)/shard_map/all_gather | solution.py:999
  103.1 55.8 %collective-permute-start.11 = (bf16[1536,512]{1,0:T(8,128)(2,1)}, bf16[1536,512]{1,0:T(8,128)(2,1)}, u32[]{:S(2)}, u32[]{:S(2)}) collective-permute-start(bf16[1536,512]{1,0:T(8,128)(2,1)} %collective-permute-done.4.came0.refs_13_), channel_id=1, source_target_pairs={{0,4},{4,0},{8,12},{12,8},{16,20},{20,16},{24,28},{28,24},{1,5},{5... | collective-permute-start | bytes 4718600 | tf_op jit(solution)/shard_map/ppermute | solution.py:318
  192.4 398.5 %reduce-scatter.3.cloned.1.call-start = ((), (), s32[]{:S(2)}) async-start(), calls=%async_computation.4 | async-start | bytes 3932160 | tf_op jit(solution)/shard_map/reduce_scatter | solution.py:1112
  209.9 46.9 %collective-permute-start.28 = (bf16[512,2048]{1,0:T(8,128)(2,1)S(1)}, bf16[512,2048]{1,0:T(8,128)(2,1)S(1)}, u32[]{:S(2)}, u32[]{:S(2)}) collective-permute-start(bf16[512,2048]{1,0:T(8,128)(2,1)S(1)} %maximum_select_fusion.refs_5_.refs_0_), channel_id=1, source_target_pairs={{0,16},{4,20},{8,24},{12,28},{16,0},{20,4},{24,8},{28,12},{1,17},{... | collective-permute-start | bytes 6291464 | tf_op jit(solution)/shard_map/ppermute | solution.py:318
  211.5 46.6 %collective-permute-start.27 = (bf16[512,2048]{1,0:T(8,128)(2,1)S(1)}, bf16[512,2048]{1,0:T(8,128)(2,1)S(1)}, u32[]{:S(2)}, u32[]{:S(2)}) collective-permute-start(bf16[512,2048]{1,0:T(8,128)(2,1)S(1)} %maximum_select_fusion.refs_5_.refs_0_), channel_id=1, source_target_pairs={{0,8},{4,12},{8,0},{12,4},{16,24},{20,28},{24,16},{28,20},{1,9},{5... | collective-permute-start | bytes 6291464 | tf_op jit(solution)/shard_map/ppermute | solution.py:318
  284.5 44.9 %collective-permute-start.33 = (bf16[512,2048]{1,0:T(8,128)(2,1)}, bf16[512,2048]{1,0:T(8,128)(2,1)S(1)}, u32[]{:S(2)}, u32[]{:S(2)}) collective-permute-start(bf16[512,2048]{1,0:T(8,128)(2,1)} %get-tuple-element.2288.refs_0_), channel_id=1, source_target_pairs={{0,16},{4,20},{8,24},{12,28},{16,0},{20,4},{24,8},{28,12},{1,17},{... | collective-permute-start | bytes 6291464 | tf_op jit(solution)/shard_map/ppermute | solution.py:318
  285.7 44.8 %collective-permute-start.32 = (bf16[512,2048]{1,0:T(8,128)(2,1)}, bf16[512,2048]{1,0:T(8,128)(2,1)S(1)}, u32[]{:S(2)}, u32[]{:S(2)}) collective-permute-start(bf16[512,2048]{1,0:T(8,128)(2,1)} %get-tuple-element.2288.refs_0_), channel_id=1, source_target_pairs={{0,8},{4,12},{8,0},{12,4},{16,24},{20,28},{24,16},{28,20},{1,9},{5... | collective-permute-start | bytes 6291464 | tf_op jit(solution)/shard_map/ppermute | solution.py:318
  450.3 54.5 %collective-permute-start.38 = (bf16[512,2048]{1,0:T(8,128)(2,1)}, bf16[512,2048]{1,0:T(8,128)(2,1)}, u32[]{:S(2)}, u32[]{:S(2)}) collective-permute-start(bf16[512,2048]{1,0:T(8,128)(2,1)} %get-tuple-element.2119), channel_id=1, source_target_pairs={{0,8},{4,12},{8,0},{12,4},{16,24},{20,28},{24,16},{28,20},{1,9},{5... | collective-permute-start | bytes 6291464 | tf_op jit(solution)/shard_map/ppermute | solution.py:318
  451.9 52.9 %collective-permute-start.39 = (bf16[512,2048]{1,0:T(8,128)(2,1)}, bf16[512,2048]{1,0:T(8,128)(2,1)}, u32[]{:S(2)}, u32[]{:S(2)}) collective-permute-start(bf16[512,2048]{1,0:T(8,128)(2,1)} %get-tuple-element.2120), channel_id=1, source_target_pairs={{0,16},{4,20},{8,24},{12,28},{16,0},{20,4},{24,8},{28,12},{1,17},{... | collective-permute-start | bytes 6291464 | tf_op jit(solution)/shard_map/ppermute | solution.py:318
  504.9 201.6 %reduce-scatter.5.cloned.1.call-start = ((), (), s32[]{:S(2)}) async-start(), calls=%async_computation.5 | async-start | bytes 7864320 | tf_op jit(solution)/shard_map/reduce_scatter | solution.py:1180
  535.4 55.5 %collective-permute-start.43 = (bf16[512,2048]{1,0:T(8,128)(2,1)}, bf16[512,2048]{1,0:T(8,128)(2,1)}, u32[]{:S(2)}, u32[]{:S(2)}) collective-permute-start(bf16[512,2048]{1,0:T(8,128)(2,1)} %get-tuple-element.2303), channel_id=1, source_target_pairs={{0,8},{4,12},{8,0},{12,4},{16,24},{20,28},{24,16},{28,20},{1,9},{5... | collective-permute-start | bytes 6291464 | tf_op jit(solution)/shard_map/ppermute | solution.py:318
  536.9 54.0 %collective-permute-start.44 = (bf16[512,2048]{1,0:T(8,128)(2,1)}, bf16[512,2048]{1,0:T(8,128)(2,1)}, u32[]{:S(2)}, u32[]{:S(2)}) collective-permute-start(bf16[512,2048]{1,0:T(8,128)(2,1)} %get-tuple-element.2304), channel_id=1, source_target_pairs={{0,16},{4,20},{8,24},{12,28},{16,0},{20,4},{24,8},{28,12},{1,17},{... | collective-permute-start | bytes 6291464 | tf_op jit(solution)/shard_map/ppermute | solution.py:318
  590.9 36.0 %collective-permute-start.47 = (bf16[2048,1024]{1,0:T(8,128)(2,1)}, bf16[2048,1024]{1,0:T(8,128)(2,1)S(1)}, u32[]{:S(2)}, u32[]{:S(2)}) collective-permute-start(bf16[2048,1024]{1,0:T(8,128)(2,1)} %row_outer.16), channel_id=1, source_target_pairs={{0,4},{4,0},{8,12},{12,8},{16,20},{20,16},{24,28},{28,24},{1,5},{5... | collective-permute-start | bytes 12582920 | tf_op jit(solution)/shard_map/ppermute | solution.py:318
  629.0 40.7 %collective-permute-start.50 = (bf16[512,768]{1,0:T(8,128)(2,1)}, bf16[512,768]{1,0:T(8,128)(2,1)S(1)}, u32[]{:S(2)}, u32[]{:S(2)}) collective-permute-start(bf16[512,768]{1,0:T(8,128)(2,1)} %reduce-scatter.3.cloned.1.call-done), channel_id=1, source_target_pairs={{0,16},{4,20},{8,24},{12,28},{16,0},{20,4},{24,8},{28,12},{1,17},{... | collective-permute-start | bytes 2359304 | tf_op jit(solution)/shard_map/ppermute | solution.py:318
  630.4 39.3 %collective-permute-start.49 = (bf16[512,768]{1,0:T(8,128)(2,1)}, bf16[512,768]{1,0:T(8,128)(2,1)}, u32[]{:S(2)}, u32[]{:S(2)}) collective-permute-start(bf16[512,768]{1,0:T(8,128)(2,1)} %reduce-scatter.3.cloned.1.call-done), channel_id=1, source_target_pairs={{0,8},{4,12},{8,0},{12,4},{16,24},{20,28},{24,16},{28,20},{1,9},{5... | collective-permute-start | bytes 2359304 | tf_op jit(solution)/shard_map/ppermute | solution.py:318
  631.0 38.6 %collective-permute-start.51 = (bf16[512,512]{1,0:T(8,128)(2,1)}, bf16[512,512]{1,0:T(8,128)(2,1)S(1)}, u32[]{:S(2)}, u32[]{:S(2)}) collective-permute-start(bf16[512,512]{1,0:T(8,128)(2,1)} %get-tuple-element.2437), channel_id=1, source_target_pairs={{4,0},{12,8},{20,16},{28,24},{5,1},{13,9},{21,17},{29,25},{6,2},{1... | collective-permute-start | bytes 1572872 | tf_op jit(solution)/shard_map/ppermute | solution.py:1140
  632.3 37.3 %collective-permute-start.52 = (bf16[512,512]{1,0:T(8,128)(2,1)}, bf16[512,512]{1,0:T(8,128)(2,1)S(1)}, u32[]{:S(2)}, u32[]{:S(2)}) collective-permute-start(bf16[512,512]{1,0:T(8,128)(2,1)} %get-tuple-element.2441), channel_id=1, source_target_pairs={{4,0},{12,8},{20,16},{28,24},{5,1},{13,9},{21,17},{29,25},{6,2},{1... | collective-permute-start | bytes 1572872 | tf_op jit(solution)/shard_map/ppermute | solution.py:1140
  669.7 36.8 %collective-permute-start.55 = (bf16[1024,512]{1,0:T(8,128)(2,1)}, bf16[1024,512]{1,0:T(8,128)(2,1)}, u32[]{:S(2)}, u32[]{:S(2)}) collective-permute-start(bf16[1024,512]{1,0:T(8,128)(2,1)} %get-tuple-element.2532), channel_id=1, source_target_pairs={{0,8},{4,12},{8,0},{12,4},{16,24},{20,28},{24,16},{28,20},{1,9},{5... | collective-permute-start | bytes 3145736 | tf_op jit(solution)/shard_map/ppermute | solution.py:318
  671.1 35.4 %collective-permute-start.56 = (bf16[1024,512]{1,0:T(8,128)(2,1)}, bf16[1024,512]{1,0:T(8,128)(2,1)S(1)}, u32[]{:S(2)}, u32[]{:S(2)}) collective-permute-start(bf16[1024,512]{1,0:T(8,128)(2,1)} %get-tuple-element.2535), channel_id=1, source_target_pairs={{0,16},{4,20},{8,24},{12,28},{16,0},{20,4},{24,8},{28,12},{1,17},{... | collective-permute-start | bytes 3145736 | tf_op jit(solution)/shard_map/ppermute | solution.py:318
  671.6 34.1 %collective-permute-start.57 = (bf16[512,512]{1,0:T(8,128)(2,1)}, bf16[512,512]{1,0:T(8,128)(2,1)S(1)}, u32[]{:S(2)}, u32[]{:S(2)}) collective-permute-start(bf16[512,512]{1,0:T(8,128)(2,1)} %get-tuple-element.2490), channel_id=1, source_target_pairs={{4,0},{12,8},{20,16},{28,24},{5,1},{13,9},{21,17},{29,25},{6,2},{1... | collective-permute-start | bytes 1572872 | tf_op jit(solution)/shard_map/ppermute | solution.py:1140
  726.9 38.9 %collective-permute-start.61 = (bf16[2048,1024]{1,0:T(8,128)(2,1)}, bf16[2048,1024]{1,0:T(8,128)(2,1)S(1)}, u32[]{:S(2)}, u32[]{:S(2)}) collective-permute-start(bf16[2048,1024]{1,0:T(8,128)(2,1)} %row_outer.20), channel_id=1, source_target_pairs={{0,4},{4,0},{8,12},{12,8},{16,20},{20,16},{24,28},{28,24},{1,5},{5... | collective-permute-start | bytes 12582920 | tf_op jit(solution)/shard_map/ppermute | solution.py:318
  726.9 38.9 %collective-permute-start.63 = (bf16[512,1536]{1,0:T(8,128)(2,1)}, bf16[512,1536]{1,0:T(8,128)(2,1)S(1)}, u32[]{:S(2)}, u32[]{:S(2)}) collective-permute-start(bf16[512,1536]{1,0:T(8,128)(2,1)} %reduce-scatter.5.cloned.1.call-done), channel_id=1, source_target_pairs={{0,16},{4,20},{8,24},{12,28},{16,0},{20,4},{24,8},{28,12},{1,17},{... | collective-permute-start | bytes 4718600 | tf_op jit(solution)/shard_map/ppermute | solution.py:318
  727.5 38.2 %collective-permute-start.62 = (bf16[512,1536]{1,0:T(8,128)(2,1)}, bf16[512,1536]{1,0:T(8,128)(2,1)}, u32[]{:S(2)}, u32[]{:S(2)}) collective-permute-start(bf16[512,1536]{1,0:T(8,128)(2,1)} %reduce-scatter.5.cloned.1.call-done), channel_id=1, source_target_pairs={{0,8},{4,12},{8,0},{12,4},{16,24},{20,28},{24,16},{28,20},{1,9},{5... | collective-permute-start | bytes 4718600 | tf_op jit(solution)/shard_map/ppermute | solution.py:318
  731.2 34.5 %collective-permute-start.65 = (bf16[512,256]{1,0:T(8,128)(2,1)}, bf16[512,256]{1,0:T(8,128)(2,1)}, u32[]{:S(2)}, u32[]{:S(2)}) collective-permute-start(bf16[512,256]{1,0:T(8,128)(2,1)} %get-tuple-element.2933), channel_id=1, source_target_pairs={{0,3},{1,0},{2,1},{3,2},{4,7},{5,4},{6,5},{7,6},{8,11},{9,8},{10,9... | collective-permute-start | bytes 786440 | tf_op jit(solution)/shard_map/ppermute | solution.py:323
  732.4 33.4 %collective-permute-start.64 = (bf16[512,256]{1,0:T(8,128)(2,1)}, bf16[512,256]{1,0:T(8,128)(2,1)}, u32[]{:S(2)}, u32[]{:S(2)}) collective-permute-start(bf16[512,256]{1,0:T(8,128)(2,1)} %get-tuple-element.2932), channel_id=1, source_target_pairs={{0,1},{1,2},{2,3},{3,0},{4,5},{5,6},{6,7},{7,4},{8,9},{9,10},{10,1... | collective-permute-start | bytes 786440 | tf_op jit(solution)/shard_map/ppermute | solution.py:323
  773.4 35.3 %collective-permute-start.72 = (bf16[256,2048]{1,0:T(8,128)(2,1)S(1)}, bf16[256,2048]{1,0:T(8,128)(2,1)S(1)}, u32[]{:S(2)}, u32[]{:S(2)}) collective-permute-start(bf16[256,2048]{1,0:T(8,128)(2,1)S(1)} %get-tuple-element.2873), channel_id=1, source_target_pairs={{1,0},{0,1},{5,2},{4,3},{3,4},{2,5},{7,6},{6,7},{9,8},{8,9},{13,10... | collective-permute-start | bytes 3145736 | tf_op jit(solution)/shard_map/ppermute | solution.py:398
  774.2 34.6 %collective-permute-start.71 = (bf16[256,2048]{1,0:T(8,128)(2,1)S(1)}, bf16[256,2048]{1,0:T(8,128)(2,1)S(1)}, u32[]{:S(2)}, u32[]{:S(2)}) collective-permute-start(bf16[256,2048]{1,0:T(8,128)(2,1)S(1)} %get-tuple-element.2874), channel_id=1, source_target_pairs={{0,0},{1,1},{4,2},{5,3},{2,4},{3,5},{6,6},{7,7},{8,8},{9,9},{12,10... | collective-permute-start | bytes 3145736 | tf_op jit(solution)/shard_map/ppermute | solution.py:398
  835.2 35.5 %collective-permute-start.82 = (bf16[512,256]{1,0:T(8,128)(2,1)S(1)}, bf16[512,256]{1,0:T(8,128)(2,1)S(1)}, u32[]{:S(2)}, u32[]{:S(2)}) collective-permute-start(bf16[512,256]{1,0:T(8,128)(2,1)S(1)} %get-tuple-element.2929), channel_id=1, source_target_pairs={{0,3},{1,0},{2,1},{3,2},{4,7},{5,4},{6,5},{7,6},{8,11},{9,8},{10,9... | collective-permute-start | bytes 786440 | tf_op jit(solution)/shard_map/ppermute | solution.py:323
  (194 other events, 2371.7 us)
Sparse Core Ops, SparseCore 0:
  80.5 44.4 all-gather.2
  192.5 166.0 all-gather.4
  505.0 57.2 reduce-scatter.2
  591.0 107.9 reduce-scatter.4

commit v10 on v9

--- a/solution.py
+++ b/solution.py
@@ -379,16 +379,13 @@
     )
 
 
-def to_sequences_send(x):
+def sequence_cuts(x):
     odd = lax.axis_index("shard") & 1
-    return [
-        lax.ppermute(
-            lax.dynamic_index_in_dim(x, turn ^ odd, 0, keepdims=False),
-            ("rep", "shard"),
-            sequence_pairs(turn),
-        )
-        for turn in range(2)
-    ]
+    return [lax.dynamic_index_in_dim(x, turn ^ odd, 0, keepdims=False) for turn in range(2)]
+
+
+def to_sequence(cut, turn):
+    return lax.ppermute(cut, ("rep", "shard"), sequence_pairs(turn))
 
 
 def from_sequences_send(x):
@@ -416,8 +413,8 @@
     )
 
 
-def whole_columns(me, own, other, widths):
-    rows, columns = own.shape[0] // 4, own.shape[1]
+def whole_columns(me, own, other, widths, part=0):
+    rows, columns = own.shape[0] // 4, sum(widths)
 
     def body(me_ref, own_ref, other_ref, *outs):
         def put(block):
@@ -430,7 +427,7 @@
         pl.when(mine)(lambda: put(own_ref))
         pl.when(jnp.logical_not(mine))(lambda: put(other_ref))
 
-    spec = pl.BlockSpec((rows, columns), lambda i, at: ((at[0] ^ i) >> 1, 0))
+    spec = pl.BlockSpec((rows, columns), lambda i, at: ((at[0] ^ i) >> 1, part))
     return pl.pallas_call(
         body,
         grid_spec=pltpu.PrefetchScalarGridSpec(
@@ -885,7 +882,6 @@
     count = lax.axis_size("rep")
 
     s = Stage()
-    s.cotangent = cotangent
     piece = width // shards
 
     s.own_blocks = [
@@ -895,7 +891,8 @@
         [jnp.stack([attn_gain, mlp_gain]), jnp.zeros((14, piece), low)], 0
     )
     travelling = jnp.concatenate([s.own_blocks[0], gain_rows], 0)
-    s.tokens = tokens
+    s.tokens_cuts = sequence_cuts(tokens)
+    s.cotangent_cuts = sequence_cuts(cotangent)
     s.out_block = column_block((w_out,), me)
     s.ffn_block = column_block((w_gate, w_up, w_down), me)
     s.before, s.behind = around(travelling, 1), around(travelling, -1)
@@ -903,27 +900,35 @@
     s.end()
 
     s.ahead = around(s.before, 1)
-    tokens_sent = to_sequences_send(s.tokens)
+    s.side = jnp.concatenate([s.before[:piece], s.behind[:piece]], 0)
+    s.side_near = near(s.side)
+    s.x_first = to_sequence(s.tokens_cuts[0], 0)
+    s.end()
+
     out_own = lax.all_gather(s.out_block, "shard", axis=0, tiled=True)
-    del s.out_block, s.tokens
-    s.end()
-
-    parts = (s.before, s.ahead, s.behind)
-    s.came = jnp.concatenate([part[:piece] for part in parts], 0)
-    s.gains = jnp.concatenate([gain_rows[:2], *(part[piece : piece + 2] for part in parts)], 1)
-    s.came_near = near(s.came)
-    s.came_own = across(s.came, CORE)
-    s.x_came = tokens_sent
-    del s.before, s.behind, s.ahead
-    s.end()
-
-    grad_y_sent = to_sequences_send(s.cotangent)
-    s.came_far = far(*s.came_near)
-    s.came_other = [s.came_own, *(across(block, CORE) for block in s.came_near)]
+    s.far_piece = s.ahead[:piece]
+    s.far_near = near(s.far_piece)
+    s.side_last = far(*s.side_near)
+    s.x_second = to_sequence(s.tokens_cuts[1], 1)
+    s.gains = jnp.concatenate(
+        [gain_rows[:2], *(part[piece : piece + 2] for part in (s.before, s.ahead, s.behind))], 1
+    )
+    del s.out_block, s.tokens_cuts, s.before, s.behind, s.ahead
+    s.end()
+
+    def three(side, far_shard):
+        return jnp.concatenate([side[:piece], far_shard, side[piece:]], 0)
+
+    s.far_last = far(*s.far_near)
+    s.grad_y_first = to_sequence(s.cotangent_cuts[0], 0)
+    s.came = [
+        three(*pair) for pair in zip((s.side, *s.side_near), (s.far_piece, *s.far_near))
+    ]
+    s.came_other = [across(block, CORE) for block in s.came]
     gains = rolled(s.gains.astype(full))
     s.mlp_gains = gains[1:]
     s.attn_gains = gains[:1]
-    s.x_low = jnp.concatenate(in_turn(s.x_came), 0)
+    s.x_low = jnp.concatenate(in_turn([s.x_first, s.x_second]), 0)
     rows = s.x_low.shape[0]
     x_rows = s.x_low.astype(full)
     s.inverse_in = lax.rsqrt(jnp.mean(x_rows * x_rows, -1, keepdims=True) + EPS)
@@ -944,7 +949,8 @@
     s.cosine, sine = cosine[0, :, 0], sine[0, :, 0]
     s.sine = jnp.concatenate([-sine[:, : head_dim // 2], sine[:, head_dim // 2 :]], 1)
     s.out_own = out_own
-    del s.gains, s.x_came, s.other_lengths, s.cotangent, s.came_own
+    del s.gains, s.x_first, s.x_second, s.other_lengths
+    del s.side, s.side_near, s.far_piece, s.far_near
     s.end()
 
     head_columns = 2 * head_dim
@@ -970,69 +976,80 @@
     upward = [(i, i + 1) for i in range(0, count, 2)]
     downward = [(i + 1, i) for i in range(0, count, 2)]
 
-    def project_call(i, came, other):
+    def project_call(i):
         return (
-            project, s.normed, s.own_blocks[2 * i], came, s.own_blocks[2 * i + 1], other,
-            s.cosine, s.sine, s.head_gains,
+            project, s.normed, s.own_blocks[2 * i], s.came[i], s.own_blocks[2 * i + 1],
+            s.came_other[i], s.cosine, s.sine, s.head_gains,
         )
 
-    def attend_call(projected, earlier):
+    def attend_call(i):
         return (
             lambda query, own, before: attend(s.info, query, before, own),
-            *projected[1:], earlier,
+            *s.projected[i][1:], s.earlier[i],
         )
 
-    came_last = jnp.concatenate(s.came_far, 0)
-    s.came_last = (came_last, across(came_last, CORE))
-    s.out_near = near(s.out_own)
-    s.out_own_other = across(s.out_own, CORE)
-    s.projected = in_order(
-        [
-            project_call(i, block, other)
-            for i, (block, other) in enumerate(zip((s.came, *s.came_near), s.came_other))
-        ]
-    )
-    s.grad_y_came = grad_y_sent
-    del s.came_far
+    def give_up(i):
+        s.earlier = s.earlier | {i: lax.ppermute(s.projected[i][2], "rep", upward)}
+
+    def compute(projected, attended):
+        calls = [project_call(i) for i in projected] + [attend_call(i) for i in attended]
+        outs = in_order(calls)
+        s.projected = s.projected | dict(zip(projected, outs))
+        s.attended = s.attended | dict(zip(attended, outs[len(projected) :]))
+
+    s.projected, s.earlier, s.attended = {}, {}, {}
+    grad_y_second = to_sequence(s.cotangent_cuts[1], 1)
+    came_last = three(jnp.concatenate(s.side_last, 0), jnp.concatenate(s.far_last, 0))
+    out_near = near(s.out_own)
+    other_last = across(came_last, CORE)
+    compute([0], [])
+    s.came = [*s.came, came_last]
+    s.came_other = [*s.came_other, other_last]
+    del s.side_last, s.far_last, s.cotangent_cuts
+    s.end()
+
+    give_up(0)
+    s.out_other = [across(s.out_own, CORE)]
+    compute([1], [])
+    s.end()
+
+    give_up(1)
+    compute([2], [0])
+    s.out_near = out_near
+    s.grad_y_second = grad_y_second
     s.end()
 
     ffn_own = lax.all_gather(s.ffn_block, "shard", axis=0, tiled=True)
-    grad_y = jnp.concatenate(in_turn(s.grad_y_came), 0)
+    s.out_far = far(*s.out_near)
+    s.out_other = [*s.out_other, *(across(block, CORE) for block in s.out_near)]
+    give_up(2)
+    grad_y = jnp.concatenate(in_turn([s.grad_y_first, s.grad_y_second]), 0)
     s.grad_y = jnp.where(s.valid > 0, grad_y, jnp.zeros_like(grad_y))
+    compute([3], [1])
+    del s.ffn_block, s.grad_y_first, s.grad_y_second
+    s.end()
+
     grad_y_near = near(s.grad_y)
-    s.out_far = far(*s.out_near)
-    s.out_near_other = [across(block, CORE) for block in s.out_near]
-    s.earlier = [lax.ppermute(p[2], "rep", upward) for p in s.projected]
-    (s.projected_last,) = in_order([project_call(3, *s.came_last)])
-    del s.ffn_block, s.grad_y_came
-    s.end()
-
     out_last = jnp.concatenate(s.out_far, 0)
-    s.out_last = (out_last, across(out_last, CORE))
-    s.earlier_last = lax.ppermute(s.projected_last[2], "rep", upward)
-    s.attended = in_order([attend_call(*pair) for pair in zip(s.projected, s.earlier)])
+    s.out_other = [*s.out_other, across(out_last, CORE)]
+    s.out_mine = [s.out_own, *s.out_near, out_last]
+    give_up(3)
+    compute([], [2])
+    del s.out_own, s.out_near, s.out_far
+    s.end()
+
+    compute([], [3])
+    s.out_blocks = [part for pair in zip(s.out_mine, s.out_other) for part in pair]
+    s.mixed = [s.attended[i][0] for i in range(4)]
+    s.resid, s.mid = close_attention(s.x_low, s.mixed, s.out_blocks, s.mlp_gains)
+    del s.out_mine, s.out_other
+    s.end()
+
+    s.mid_near = near(s.mid)
     s.grad_y_near = grad_y_near
-    del s.out_far
-    s.end()
-
-    s.projected = [*s.projected, s.projected_last]
-    s.earlier = [*s.earlier, s.earlier_last]
-    s.out_blocks = [
-        s.out_own, s.out_own_other, s.out_near[0], s.out_near_other[0], s.out_near[1],
-        s.out_near_other[1], *s.out_last,
-    ]
-    (last,) = in_order([attend_call(s.projected_last, s.earlier_last)])
-    s.attended = [*s.attended, last]
-    s.mixed = [a[0] for a in s.attended]
-    s.resid, s.mid = close_attention(s.x_low, s.mixed, s.out_blocks, s.mlp_gains)
+    s.end()
+
     s.grad_y_far = far(*s.grad_y_near)
-    del s.out_own, s.out_own_other, s.out_near, s.out_near_other, s.out_last
-    del s.projected_last, s.earlier_last
-    s.end()
-
-    s.mid_near = near(s.mid)
-    s.end()
-
     s.mid_far = far(*s.mid_near)
     s.ffn_own = ffn_own
     s.end()
@@ -1225,8 +1242,8 @@
 
     my_group = me.astype(jnp.int32)[None]
 
-    def whole_call(widths, own, other):
-        return lambda first: whole_columns(my_group, first, other, widths), own
+    def whole_call(widths, own, other, part=0):
+        return lambda first: whole_columns(my_group, first, other, widths, part), own
 
     s.gate_up_near = near(s.gate_up_total)
     s.came0 = across(s.odd0, CORE)
@@ -1235,9 +1252,11 @@
     s.out_ring = ring_sum_first(s.out_chunks)
     weights = [
         pair
-        for i, block in enumerate(zip((s.came, *s.came_near), s.came_other))
-        for pair in ((s.own_blocks[2 * i], block[0]), (s.own_blocks[2 * i + 1], block[1]))
-    ] + [(s.own_blocks[6 + i], s.came_last[i]) for i in range(2)]
+        for i in range(4)
+        for pair in (
+            (s.own_blocks[2 * i], s.came[i]), (s.own_blocks[2 * i + 1], s.came_other[i])
+        )
+    ]
     blocks = [part for i in range(4) for part in s.finished[i][:2]]
     s.odd1, grad_in = in_order(
         [
@@ -1259,7 +1278,7 @@
         s.grad_resid + norm_back(x_unit, s.inverse_in, grad_in * s.attn_gains)
     ).astype(low)
     del s.odd0, s.out_near, s.out_far, s.out_head, s.out_tail, s.backs
-    del s.own_blocks, s.came, s.came_near, s.came_other, s.came_last, s.grad_resid, s.x_low
+    del s.own_blocks, s.came, s.came_other, s.grad_resid, s.x_low
     s.end()
 
     def halves_call(half, came):
@@ -1283,16 +1302,15 @@
         [*halves_call(1, s.came1), whole_call((units,), s.down_spread, s.down_spread_other)]
     )
     s.out_total = rounded_sum(s.out_chunks[0], s.out_ring[1], s.out_ring_last)
-    s.output_came = output_sent
+    s.output_first = output_sent[0]
     del s.came1, s.down_spread, s.down_spread_other, s.output, s.finished
     del s.out_chunks, s.out_ring, s.out_ring_last
     s.end()
 
-    tokens_sent = from_sequences_send(s.grad_tokens)
     s.far0 = send_far(s.near0, (s.tail0[1], s.head0[1]), by_columns)
     s.near1 = send_near((s.head1[0], s.tail1[0]))
     s.gain_parts = s.gain_parts + s.gain_came
-    s.tokens_first = tokens_sent[0]
+    s.output_second = output_sent[1]
     s.end()
 
     s.chunks0 = qkv_chunks(s.near0, s.far0, s.head0, s.tail0)
@@ -1310,6 +1328,7 @@
     del s.near1, s.far1, s.head1, s.tail1
     s.end()
 
+    tokens_sent = from_sequences_send(s.grad_tokens)
     query_total = rounded_sum(s.chunks0[0], s.ring0[1], s.last0)
     s.total0 = jnp.concatenate([query_total, s.out_total], 1)
     s.spread0 = near(s.total0)
@@ -1325,8 +1344,8 @@
     s.spread1 = near(s.total1)
     s.gain_parts = s.gain_parts + s.gain_came
     s.gain_came = lax.ppermute(s.gain_parts, "shard", [(i, i ^ 1) for i in range(shards)])
-    (s.whole_gate_up,) = in_order([whole_call((units, units), s.gate_up_own, s.gate_up_other)])
-    del s.chunks1, s.ring1, s.last1, s.gate_up_own, s.gate_up_other
+    ((s.whole_gate,),) = in_order([whole_call((units,), s.gate_up_own, s.gate_up_other)])
+    del s.chunks1, s.ring1, s.last1
     s.end()
 
     s.own0 = jnp.concatenate([s.total0, *s.spread0, *s.spread_far0], 0)
@@ -1334,7 +1353,9 @@
     s.spread_far1 = far(*s.spread1)
     s.gain_parts = s.gain_parts + s.gain_came
     s.gain_came = lax.ppermute(s.gain_parts, "shard", [(i, i ^ 2) for i in range(shards)])
-    del s.total0, s.spread0, s.spread_far0
+    ((s.whole_up,),) = in_order([whole_call((units,), s.gate_up_own, s.gate_up_other, 1)])
+    s.tokens_first = tokens_sent[0]
+    del s.total0, s.spread0, s.spread_far0, s.gate_up_own, s.gate_up_other
     s.end()
 
     s.own1 = jnp.concatenate([s.total1, *s.spread1, *s.spread_far1], 0)
@@ -1352,7 +1373,7 @@
         [whole_call((head_dim, head_dim), s.own1, s.other1)]
     )
     return (
-        jnp.stack(in_turn(s.output_came)),
+        jnp.stack(in_turn([s.output_first, s.output_second])),
         jnp.stack(in_turn([s.tokens_first, tokens_sent[1]])),
         s.wide[0],
         s.whole0[0],
@@ -1362,7 +1383,8 @@
         s.narrow[head_dim:],
         s.whole0[1],
         s.wide[1],
-        *s.whole_gate_up,
+        s.whole_gate,
+        s.whole_up,
         *s.whole_down,
     )
 

time: 1000 us -> 1020 us (1.020)
  waiting for transfers between devices: 243 us -> 270 us
  starting transfers between devices: 165 us -> 145 us
    ppermute x74 -> x78, waiting for transfers between devices: 159 us -> 198 us  [across(): return lax.ppermute(x, 'rep', [(i, i ^ mask) for i in range(count)])]
    ppermute x12, starting transfers between devices: 37.2 us -> 17.2 us  [around(): lax.ppermute(x, 'shard', [(i, (i + by) % count) for i in range(count)])]
    ppermute x8, waiting for transfers between devices: 21.4 us -> 5.37 us  [the longest x4 5.36 us: to_sequence(): return lax.ppermute(cut, ('rep', 'shard'), sequence_pairs(turn))]
    ppermute x74 -> x78, starting transfers between devices: 95.3 us -> 91.1 us  [across(): return lax.ppermute(x, 'rep', [(i, i ^ mask) for i in range(count)])]
    pallas_call x4 -> x5, Pallas kernels: 44.3 us -> 48.4 us  [whole_columns(): pl.pallas_call(body, grid_spec=pltpu.PrefetchScalarGridSpec(num_scalar_pr...]
    unnamed x252 -> x276, local copies, waits for them, and re-layouts: 28.7 us -> 29.9 us
  transfers between devices with their start and end apart: 108 -> 112, of which waited for: 31 -> 30; matrix products, arithmetic and copies ran while one was open for 10% -> 10% of each run, Pallas kernels for 38% -> 38%
where the time goes in v10:
time: 1020 us; the launch traced here: 1010 us
  Pallas kernels  435 us (43%)
  waiting for transfers between devices  270 us (26%)
  starting transfers between devices  145 us (14%)
  other arithmetic  72.7 us (7%)
  local copies, waits for them, and re-layouts  70.7 us (7%)
  between operations  16.3 us (2%)
    ppermute x78, waiting for transfers between devices, across(): return lax.ppermute(x, 'rep', [(i, i ^ mask) for i in range(count)])  198 us
    pallas_call x13, Pallas kernels, row_outer(): pl.pallas_call(body, grid=(tiles,), out_shape=[jax.ShapeDtypeStruct((tile...  121 us
    pallas_call x16, Pallas kernels, call(): pl.pallas_call(body, grid=(1,), out_shape=outs, in_specs=in_specs, out_sp...  119 us
    ppermute x78, starting transfers between devices, across(): return lax.ppermute(x, 'rep', [(i, i ^ mask) for i in range(count)])  91.1 us
    pallas_call x2, Pallas kernels, hidden_units(): pl.pallas_call(body, grid=(3,), out_shape=[jax.ShapeDtypeStruct((rows, un...  60.1 us
    pallas_call x4, Pallas kernels, from_hidden(): pl.pallas_call(body, grid=(4,), out_shape=[jax.ShapeDtypeStruct((2 * rows...  59.1 us
    pallas_call x5, Pallas kernels, whole_columns(): pl.pallas_call(body, grid_spec=pltpu.PrefetchScalarGridSpec(num_scalar_pr...  48.4 us
    ppermute x12, waiting for transfers between devices, around(): lax.ppermute(x, 'shard', [(i, (i + by) % count) for i in range(count)])  38.6 us
  transfers between devices with their start and end apart: 112, of which 30 were waited for; matrix products, arithmetic and copies ran while one was open for 10% of the time, Pallas kernels for 38%

profile of v10, /device:TPU:0, one launch (start us, length us, event | category | flops | bytes accessed | tf_op | source)
XLA Modules:
  0.0 1009.3 jit_solution(16184632049927141581)
XLA Ops:
  60.4 17.1 %collective-permute-done.3 = bf16[528,512]{1,0:T(8,128)(2,1)} collective-permute-done((bf16[528,512]{1,0:T(8,128)(2,1)}, bf16[528,512]{1,0:T(8,128)(2,1)}, u32[]{:S(2)}, u32[]{:S(2)}) %collective-permute-start.3) | collective-permute-done | bytes 540704 | tf_op jit(solution)/shard_map/ppermute | solution.py:323
  91.1 10.1 %collective-permute-done.10 = bf16[512,512]{1,0:T(8,128)(2,1)} collective-permute-done((bf16[512,512]{1,0:T(8,128)(2,1)}, bf16[512,512]{1,0:T(8,128)(2,1)}, u32[]{:S(2)}, u32[]{:S(2)}) %collective-permute-start.10) | collective-permute-done | bytes 524320 | tf_op jit(solution)/shard_map/ppermute | solution.py:318
  114.3 23.0 %collective-permute-start.14 = (bf16[1536,512]{1,0:T(8,128)(2,1)}, bf16[1536,512]{1,0:T(8,128)(2,1)}, u32[]{:S(2)}, u32[]{:S(2)}) collective-permute-start(bf16[1536,512]{1,0:T(8,128)(2,1)} %pad_maximum_fusion.10.came0.refs_17_), channel_id=1, source_target_pairs={{0,4},{4,0},{8,12},{12,8},{16,20},{20,16},{24,28},{28,24},{1,5},{5... | collective-permute-start | bytes 4718600 | tf_op jit(solution)/shard_map/ppermute | solution.py:318
  238.5 12.0 %close_attention.1 = (f32[512,2048]{1,0:T(8,128)}, bf16[512,2048]{1,0:T(8,128)(2,1)}) custom-call(bf16[512,2048]{1,0:T(8,128)(2,1)} %pad_maximum_fusion.3.x, bf16[512,512]{1,0:T(8,128)(2,1)} %get-tuple-element.2582.refs_0_.refs_1_.refs_4_, bf16[512,512]{1,0:T(8,128)(2,1)} %get-tuple-element.2579.refs_1_.refs_2_.refs_3_, ...), custom_call_target="tpu_custom_call" | custom-call | flops 1 | bytes 1 | tf_op jit(solution)/shard_map/close_attention/pallas_call | solution.py:789
  253.0 21.9 %collective-permute-done.33.refs_7_.refs_2_ = bf16[512,2048]{1,0:T(8,128)(2,1)S(1)} collective-permute-done((bf16[512,2048]{1,0:T(8,128)(2,1)S(1)}, bf16[512,2048]{1,0:T(8,128)(2,1)S(1)}, u32[]{:S(2)}, u32[]{:S(2)}) %collective-permute-start.33) | collective-permute-done | bytes 2097184 | tf_op jit(solution)/shard_map/ppermute | solution.py:318
  275.9 41.6 %collective-permute-done.35.refs_2_ = bf16[512,2048]{1,0:T(8,128)(2,1)S(1)} collective-permute-done((bf16[512,2048]{1,0:T(8,128)(2,1)}, bf16[512,2048]{1,0:T(8,128)(2,1)S(1)}, u32[]{:S(2)}, u32[]{:S(2)}) %collective-permute-start.35) | collective-permute-done | bytes 2097184 | tf_op jit(solution)/shard_map/ppermute | solution.py:318
  323.8 22.0 %collective-permute-done.39.refs_4_ = bf16[256,2048]{1,0:T(8,128)(2,1)S(1)} collective-permute-done((bf16[256,2048]{1,0:T(8,128)(2,1)S(1)}, bf16[256,2048]{1,0:T(8,128)(2,1)S(1)}, u32[]{:S(2)}, u32[]{:S(2)}) %collective-permute-start.39) | collective-permute-done | bytes 1048608 | tf_op jit(solution)/shard_map/ppermute | solution.py:318
  346.4 18.5 %collective-permute-done.37.refs_9_.refs_4_ = bf16[256,2048]{1,0:T(8,128)(2,1)S(1)} collective-permute-done((bf16[256,2048]{1,0:T(8,128)(2,1)S(1)}, bf16[256,2048]{1,0:T(8,128)(2,1)S(1)}, u32[]{:S(2)}, u32[]{:S(2)}) %collective-permute-start.37) | collective-permute-done | bytes 1048608 | tf_op jit(solution)/shard_map/ppermute | solution.py:318
  366.0 29.9 %hidden_units.2 = (bf16[2048,768]{1,0:T(8,128)(2,1)}, bf16[2048,768]{1,0:T(8,128)(2,1)}, bf16[2048,768]{1,0:T(8,128)(2,1)}) custom-call(bf16[512,2048]{1,0:T(8,128)(2,1)} %get-tuple-element.2454.refs_0_, bf16[512,2048]{1,0:T(8,128)(2,1)} %copy-done.14, bf16[512,2048]{1,0:T(8,128)(2,1)} %copy-done.13, bf16[256,2048]{1,0:T(8,128)(2,1)} %copy-done.25, ...), custom_call_target="tpu_custom_call" | custom-call | flops 1 | bytes 1 | tf_op jit(solution)/shard_map/hidden_units/pallas_call | solution.py:656
  395.9 30.2 %hidden_units.3 = (bf16[2048,768]{1,0:T(8,128)(2,1)}, bf16[2048,768]{1,0:T(8,128)(2,1)}, bf16[2048,768]{1,0:T(8,128)(2,1)}) custom-call(bf16[512,2048]{1,0:T(8,128)(2,1)} %get-tuple-element.2454.refs_0_, bf16[512,2048]{1,0:T(8,128)(2,1)} %copy-done.14, bf16[512,2048]{1,0:T(8,128)(2,1)} %copy-done.13, bf16[256,2048]{1,0:T(8,128)(2,1)} %copy-done.25, ...), custom_call_target="tpu_custom_call" | custom-call | flops 1 | bytes 1 | tf_op jit(solution)/shard_map/hidden_units/pallas_call | solution.py:656
  426.1 12.6 %row_outer.13 = bf16[2048,768]{1,0:T(8,128)(2,1)} custom-call(bf16[512,2048]{1,0:T(8,128)(2,1)} %copy-done.7, bf16[512,2048]{1,0:T(8,128)(2,1)} %copy-done.16, bf16[512,2048]{1,0:T(8,128)(2,1)} %copy-done.15, bf16[256,2048]{1,0:T(8,128)(2,1)} %collective-permute-done.36.refs_8_.refs_3_, bf16[256,2048]{1,0:T(8,128)(2,1)} %copy-done.26, ...), custom_call_target="tpu_custom_call" | custom-call | flops 6442450944 | bytes 11534336 | tf_op jit(solution)/shard_map/row_outer/pallas_call | solution.py:739
  438.7 18.8 %from_hidden.4 = (bf16[512,2048]{1,0:T(8,128)(2,1)}, bf16[512,2048]{1,0:T(8,128)(2,1)}) custom-call(bf16[2048,768]{1,0:T(8,128)(2,1)} %get-tuple-element.2465.refs_0_.refs_1_.refs_2_.refs_3_.refs_5_, bf16[2048,768]{1,0:T(8,128)(2,1)} %get-tuple-element.2465.refs_0_.refs_1_.refs_2_.refs_3_.refs_5_, ...), custom_call_target="tpu_custom_call" | custom-call | flops 1 | bytes 1 | tf_op jit(solution)/shard_map/from_hidden/pallas_call | solution.py:695
  460.0 13.2 %row_outer.14 = bf16[2048,768]{1,0:T(8,128)(2,1)} custom-call(bf16[512,2048]{1,0:T(8,128)(2,1)} %copy-done.7, bf16[512,2048]{1,0:T(8,128)(2,1)} %copy-done.16, bf16[512,2048]{1,0:T(8,128)(2,1)} %copy-done.15, bf16[256,2048]{1,0:T(8,128)(2,1)} %collective-permute-done.36.refs_8_.refs_3_, bf16[256,2048]{1,0:T(8,128)(2,1)} %copy-done.26, ...), custom_call_target="tpu_custom_call" | custom-call | flops 6442450944 | bytes 11534336 | tf_op jit(solution)/shard_map/row_outer/pallas_call | solution.py:739
  473.2 18.8 %from_hidden.5 = (bf16[512,2048]{1,0:T(8,128)(2,1)}, bf16[512,2048]{1,0:T(8,128)(2,1)}) custom-call(bf16[2048,768]{1,0:T(8,128)(2,1)} %get-tuple-element.2465.refs_0_.refs_1_.refs_2_.refs_3_.refs_5_, bf16[2048,768]{1,0:T(8,128)(2,1)} %get-tuple-element.2465.refs_0_.refs_1_.refs_2_.refs_3_.refs_5_, ...), custom_call_target="tpu_custom_call" | custom-call | flops 1 | bytes 1 | tf_op jit(solution)/shard_map/from_hidden/pallas_call | solution.py:695
  492.0 19.7 %row_outer.15 = bf16[2048,1536]{1,0:T(8,128)(2,1)} custom-call(bf16[512,2048]{1,0:T(8,128)(2,1)} %get-tuple-element.2454.refs_0_, bf16[512,2048]{1,0:T(8,128)(2,1)} %copy-done.14, bf16[512,2048]{1,0:T(8,128)(2,1)} %copy-done.13, bf16[256,2048]{1,0:T(8,128)(2,1)} %copy-done.25, bf16[256,2048]{1,0:T(8,128)(2,1)} %copy-done.24, ...), custom_call_target="tpu_custom_call" | custom-call | flops 12884901888 | bytes 14680064 | tf_op jit(solution)/shard_map/row_outer/pallas_call | solution.py:739
  518.8 10.6 %from_hidden.6 = (bf16[512,2048]{1,0:T(8,128)(2,1)}, bf16[512,2048]{1,0:T(8,128)(2,1)}) custom-call(bf16[2048,768]{1,0:T(8,128)(2,1)} %get-tuple-element.2374.refs_5_.refs_0_.refs_1_.refs_2_.refs_3_, bf16[2048,768]{1,0:T(8,128)(2,1)} %get-tuple-element.2374.refs_5_.refs_0_.refs_1_.refs_2_.refs_3_, ...), custom_call_target="tpu_custom_call" | custom-call | flops 1 | bytes 1 | tf_op jit(solution)/shard_map/from_hidden/pallas_call | solution.py:695
  529.4 10.9 %from_hidden.7 = (bf16[512,2048]{1,0:T(8,128)(2,1)}, bf16[512,2048]{1,0:T(8,128)(2,1)}) custom-call(bf16[2048,768]{1,0:T(8,128)(2,1)} %get-tuple-element.2374.refs_5_.refs_0_.refs_1_.refs_2_.refs_3_, bf16[2048,768]{1,0:T(8,128)(2,1)} %get-tuple-element.2374.refs_5_.refs_0_.refs_1_.refs_2_.refs_3_, ...), custom_call_target="tpu_custom_call" | custom-call | flops 1 | bytes 1 | tf_op jit(solution)/shard_map/from_hidden/pallas_call | solution.py:695
  554.9 13.4 %attend_back.4 = (bf16[512,512]{1,0:T(8,128)(2,1)}, f32[512,512]{1,0:T(8,128)}, bf16[512,512]{1,0:T(8,128)(2,1)}, f32[1,128]{1,0:T(1,128)}) custom-call(s32[2]{0:T(128)} %pad_add_fusion.info, bf16[512,512]{1,0:T(8,128)(2,1)} %get-tuple-element.2421.query, bf16[512,512]{1,0:T(8,128)(2,1)} %collective-permute-done.30.before, ...), custom_call_target="tpu_custom_call" | custom-call | flops 1 | bytes 1 | tf_op jit(solution)/shard_map/attend_back/pallas_call | solution.py:616
  578.3 19.7 %row_outer.17 = bf16[2048,1536]{1,0:T(8,128)(2,1)} custom-call(bf16[512,2048]{1,0:T(8,128)(2,1)} %get-tuple-element.2454.refs_0_, bf16[512,2048]{1,0:T(8,128)(2,1)} %copy-done.14, bf16[512,2048]{1,0:T(8,128)(2,1)} %copy-done.13, bf16[256,2048]{1,0:T(8,128)(2,1)} %copy-done.25, bf16[256,2048]{1,0:T(8,128)(2,1)} %copy-done.24, ...), custom_call_target="tpu_custom_call" | custom-call | flops 12884901888 | bytes 14680064 | tf_op jit(solution)/shard_map/row_outer/pallas_call | solution.py:739
  607.2 13.2 %attend_back.5 = (bf16[512,512]{1,0:T(8,128)(2,1)}, f32[512,512]{1,0:T(8,128)}, bf16[512,512]{1,0:T(8,128)(2,1)}, f32[1,128]{1,0:T(1,128)}) custom-call(s32[2]{0:T(128)} %pad_add_fusion.info, bf16[512,512]{1,0:T(8,128)(2,1)} %get-tuple-element.2504.query, bf16[512,512]{1,0:T(8,128)(2,1)} %copy-done.42, bf16[512,512]{1,0:T(8,128)(2,1)} %get-tuple-element.2506.own, ...), custom_call_target="tpu_custom_call" | custom-call | flops 1 | bytes 1 | tf_op jit(solution)/shard_map/attend_back/pallas_call | solution.py:616
  620.4 13.5 %attend_back.6 = (bf16[512,512]{1,0:T(8,128)(2,1)}, f32[512,512]{1,0:T(8,128)}, bf16[512,512]{1,0:T(8,128)(2,1)}, f32[1,128]{1,0:T(1,128)}) custom-call(s32[2]{0:T(128)} %pad_add_fusion.info, bf16[512,512]{1,0:T(8,128)(2,1)} %get-tuple-element.2519.query, bf16[512,512]{1,0:T(8,128)(2,1)} %copy-done.43, bf16[512,512]{1,0:T(8,128)(2,1)} %get-tuple-element.2521.own, ...), custom_call_target="tpu_custom_call" | custom-call | flops 1 | bytes 1 | tf_op jit(solution)/shard_map/attend_back/pallas_call | solution.py:616
  655.9 13.2 %attend_back.7 = (bf16[512,512]{1,0:T(8,128)(2,1)}, f32[512,512]{1,0:T(8,128)}, bf16[512,512]{1,0:T(8,128)(2,1)}, f32[1,128]{1,0:T(1,128)}) custom-call(s32[2]{0:T(128)} %pad_add_fusion.info, bf16[512,512]{1,0:T(8,128)(2,1)} %get-tuple-element.2587.query, bf16[512,512]{1,0:T(8,128)(2,1)} %copy-done.41, bf16[512,512]{1,0:T(8,128)(2,1)} %get-tuple-element.2589.own, ...), custom_call_target="tpu_custom_call" | custom-call | flops 1 | bytes 1 | tf_op jit(solution)/shard_map/attend_back/pallas_call | solution.py:616
  692.0 19.1 %collective-permute-done.58 = bf16[256,768]{1,0:T(8,128)(2,1)S(1)} collective-permute-done((bf16[256,768]{1,0:T(8,128)(2,1)S(1)}, bf16[256,768]{1,0:T(8,128)(2,1)S(1)}, u32[]{:S(2)}, u32[]{:S(2)}) %collective-permute-start.58) | collective-permute-done | bytes 393248 | tf_op jit(solution)/shard_map/ppermute | solution.py:318
  749.0 15.8 %back_to_rows.1 = f32[512,2048]{1,0:T(8,128)} custom-call(bf16[512,512]{1,0:T(8,128)(2,1)} %get-tuple-element.2861.refs_0_.refs_4_, bf16[512,512]{1,0:T(8,128)(2,1)} %get-tuple-element.2778.refs_1_, bf16[512,512]{1,0:T(8,128)(2,1)} %get-tuple-element.2858.refs_2_.refs_1_.refs_3_, bf16[512,512]{1,0:T(8,128)(2,1)} %get-tuple-element.2781.refs_2_.refs_3_, ...), custom_call_target="tpu_custom_call" | custom-call | flops 1 | bytes 1 | tf_op jit(solution)/shard_map/back_to_rows/pallas_call | solution.py:842
  804.5 11.0 %whole_columns.5 = f32[512,6144]{1,0:T(8,128)} custom-call(s32[1]{0:T(128)} %bitcast.18.me_ref, bf16[2048,768]{1,0:T(8,128)(2,1)} %copy-done.23, bf16[2048,768]{1,0:T(8,128)(2,1)} %collective-permute-done.62.other_ref), custom_call_target="tpu_custom_call" | custom-call | flops 1 | bytes 1 | tf_op jit(solution)/shard_map/whole_columns/pallas_call | solution.py:431
  825.2 29.2 %collective-permute-done.77 = bf16[1024,256]{1,0:T(8,128)(2,1)S(1)} collective-permute-done((bf16[1024,256]{1,0:T(8,128)(2,1)S(1)}, bf16[1024,256]{1,0:T(8,128)(2,1)S(1)}, u32[]{:S(2)}, u32[]{:S(2)}) %collective-permute-start.77) | collective-permute-done | bytes 524320 | tf_op jit(solution)/shard_map/ppermute | solution.py:318
  861.6 10.7 %collective-permute-done.83 = f32[4352]{0:T(1024)S(1)} collective-permute-done((f32[4352]{0:T(1024)S(1)}, f32[4352]{0:T(1024)S(1)}, u32[]{:S(2)}, u32[]{:S(2)}) %collective-permute-start.83) | collective-permute-done | bytes 17440 | tf_op jit(solution)/shard_map/ppermute | solution.py:318
  902.3 10.5 %collective-permute-done.91 = f32[4352]{0:T(1024)S(1)} collective-permute-done((f32[4352]{0:T(1024)S(1)}, f32[4352]{0:T(1024)S(1)}, u32[]{:S(2)}, u32[]{:S(2)}) %collective-permute-start.91) | collective-permute-done | bytes 17440 | tf_op jit(solution)/shard_map/ppermute | solution.py:318
  921.8 11.0 %whole_columns.6 = f32[512,6144]{1,0:T(8,128)} custom-call(s32[1]{0:T(128)} %bitcast.18.me_ref, bf16[2048,1536]{1,0:T(8,128)(2,1)} %copy-done.10, bf16[2048,1536]{1,0:T(8,128)(2,1)} %copy-done.11), custom_call_target="tpu_custom_call" | custom-call | flops 1 | bytes 1 | tf_op jit(solution)/shard_map/whole_columns/pallas_call | solution.py:431
  943.1 11.0 %whole_columns.7 = f32[512,6144]{1,0:T(8,128)} custom-call(s32[1]{0:T(128)} %bitcast.18.me_ref, bf16[2048,1536]{1,0:T(8,128)(2,1)} %copy-done.10, bf16[2048,1536]{1,0:T(8,128)(2,1)} %copy-done.11), custom_call_target="tpu_custom_call" | custom-call | flops 1 | bytes 1 | tf_op jit(solution)/shard_map/whole_columns/pallas_call | solution.py:431
  954.1 11.6 %collective-permute-done.101 = f32[4352]{0:T(1024)S(1)} collective-permute-done((f32[4352]{0:T(1024)S(1)}, f32[4352]{0:T(1024)S(1)}, u32[]{:S(2)}, u32[]{:S(2)}) %collective-permute-start.101) | collective-permute-done | bytes 17440 | tf_op jit(solution)/shard_map/ppermute | solution.py:1355
  977.7 14.2 %collective-permute-done.107 = bf16[256,2048]{1,0:T(8,128)(2,1)} collective-permute-done((bf16[256,2048]{1,0:T(8,128)(2,1)}, bf16[256,2048]{1,0:T(8,128)(2,1)}, u32[]{:S(2)}, u32[]{:S(2)}) %collective-permute-start.107) | collective-permute-done | bytes 1048608 | tf_op jit(solution)/shard_map/ppermute | solution.py:395
  (663 shorter events, 444.9 us)
Async XLA Ops:
  7.2 148.8 %all-gather.3.cloned.1.call-start = ((), (), s32[]{:S(2)}) async-start(), calls=%async_computation.2 | async-start | bytes 1310720 | tf_op jit(solution)/shard_map/all_gather | solution.py:908
  89.7 275.8 %all-gather.5.cloned.1.call-start = ((), (), s32[]{:S(2)}) async-start(), calls=%async_computation.3 | async-start | bytes 11796480 | tf_op jit(solution)/shard_map/all_gather | solution.py:1022
  109.3 38.5 %collective-permute-start.16 = (bf16[256,512]{1,0:T(8,128)(2,1)S(1)}, bf16[256,512]{1,0:T(8,128)(2,1)S(1)}, u32[]{:S(2)}, u32[]{:S(2)}) collective-permute-start(bf16[256,512]{1,0:T(8,128)(2,1)S(1)} %slice.168), channel_id=1, source_target_pairs={{0,8},{4,12},{8,0},{12,4},{16,24},{20,28},{24,16},{28,20},{1,9},{5... | collective-permute-start | bytes 786440 | tf_op jit(solution)/shard_map/ppermute | solution.py:318
  110.1 45.9 %collective-permute-start.17 = (bf16[256,2048]{1,0:T(8,128)(2,1)}, bf16[256,2048]{1,0:T(8,128)(2,1)S(1)}, u32[]{:S(2)}, u32[]{:S(2)}) collective-permute-start(bf16[256,2048]{1,0:T(8,128)(2,1)} %get-tuple-element.1560), channel_id=1, source_target_pairs={{0,0},{1,1},{2,4},{3,5},{4,2},{5,3},{6,6},{7,7},{8,8},{9,9},{10,12... | collective-permute-start | bytes 3145736 | tf_op jit(solution)/shard_map/ppermute | solution.py:388
  114.3 41.7 %collective-permute-start.14 = (bf16[1536,512]{1,0:T(8,128)(2,1)}, bf16[1536,512]{1,0:T(8,128)(2,1)}, u32[]{:S(2)}, u32[]{:S(2)}) collective-permute-start(bf16[1536,512]{1,0:T(8,128)(2,1)} %pad_maximum_fusion.10.came0.refs_17_), channel_id=1, source_target_pairs={{0,4},{4,0},{8,12},{12,8},{16,20},{20,16},{24,28},{28,24},{1,5},{5... | collective-permute-start | bytes 4718600 | tf_op jit(solution)/shard_map/ppermute | solution.py:318
  198.1 400.0 %reduce-scatter.3.cloned.1.call-start = ((), (), s32[]{:S(2)}) async-start(), calls=%async_computation.4 | async-start | bytes 3932160 | tf_op jit(solution)/shard_map/reduce_scatter | solution.py:1129
  226.3 48.6 %collective-permute-start.33 = (bf16[512,2048]{1,0:T(8,128)(2,1)S(1)}, bf16[512,2048]{1,0:T(8,128)(2,1)S(1)}, u32[]{:S(2)}, u32[]{:S(2)}) collective-permute-start(bf16[512,2048]{1,0:T(8,128)(2,1)S(1)} %maximum_select_fusion.refs_5_.refs_0_), channel_id=1, source_target_pairs={{0,16},{4,20},{8,24},{12,28},{16,0},{20,4},{24,8},{28,12},{1,17},{... | collective-permute-start | bytes 6291464 | tf_op jit(solution)/shard_map/ppermute | solution.py:318
  227.3 48.6 %collective-permute-start.32 = (bf16[512,2048]{1,0:T(8,128)(2,1)S(1)}, bf16[512,2048]{1,0:T(8,128)(2,1)S(1)}, u32[]{:S(2)}, u32[]{:S(2)}) collective-permute-start(bf16[512,2048]{1,0:T(8,128)(2,1)S(1)} %maximum_select_fusion.refs_5_.refs_0_), channel_id=1, source_target_pairs={{0,8},{4,12},{8,0},{12,4},{16,24},{20,28},{24,16},{28,20},{1,9},{5... | collective-permute-start | bytes 6291464 | tf_op jit(solution)/shard_map/ppermute | solution.py:318
  250.5 67.0 %collective-permute-start.35 = (bf16[512,2048]{1,0:T(8,128)(2,1)}, bf16[512,2048]{1,0:T(8,128)(2,1)S(1)}, u32[]{:S(2)}, u32[]{:S(2)}) collective-permute-start(bf16[512,2048]{1,0:T(8,128)(2,1)} %get-tuple-element.2454.refs_0_), channel_id=1, source_target_pairs={{0,16},{4,20},{8,24},{12,28},{16,0},{20,4},{24,8},{28,12},{1,17},{... | collective-permute-start | bytes 6291464 | tf_op jit(solution)/shard_map/ppermute | solution.py:318
  251.5 66.5 %collective-permute-start.34 = (bf16[512,2048]{1,0:T(8,128)(2,1)}, bf16[512,2048]{1,0:T(8,128)(2,1)S(1)}, u32[]{:S(2)}, u32[]{:S(2)}) collective-permute-start(bf16[512,2048]{1,0:T(8,128)(2,1)} %get-tuple-element.2454.refs_0_), channel_id=1, source_target_pairs={{0,8},{4,12},{8,0},{12,4},{16,24},{20,28},{24,16},{28,20},{1,9},{5... | collective-permute-start | bytes 6291464 | tf_op jit(solution)/shard_map/ppermute | solution.py:318
  321.4 43.6 %collective-permute-start.37 = (bf16[256,2048]{1,0:T(8,128)(2,1)S(1)}, bf16[256,2048]{1,0:T(8,128)(2,1)S(1)}, u32[]{:S(2)}, u32[]{:S(2)}) collective-permute-start(bf16[256,2048]{1,0:T(8,128)(2,1)S(1)} %slice.175), channel_id=1, source_target_pairs={{0,8},{4,12},{8,0},{12,4},{16,24},{20,28},{24,16},{28,20},{1,9},{5... | collective-permute-start | bytes 3145736 | tf_op jit(solution)/shard_map/ppermute | solution.py:318
  322.9 42.6 %collective-permute-start.36 = (bf16[256,2048]{1,0:T(8,128)(2,1)S(1)}, bf16[256,2048]{1,0:T(8,128)(2,1)}, u32[]{:S(2)}, u32[]{:S(2)}) collective-permute-start(bf16[256,2048]{1,0:T(8,128)(2,1)S(1)} %slice.174), channel_id=1, source_target_pairs={{0,16},{4,20},{8,24},{12,28},{16,0},{20,4},{24,8},{28,12},{1,17},{... | collective-permute-start | bytes 3145736 | tf_op jit(solution)/shard_map/ppermute | solution.py:318
  457.5 54.2 %collective-permute-start.42 = (bf16[512,2048]{1,0:T(8,128)(2,1)}, bf16[512,2048]{1,0:T(8,128)(2,1)}, u32[]{:S(2)}, u32[]{:S(2)}) collective-permute-start(bf16[512,2048]{1,0:T(8,128)(2,1)} %get-tuple-element.2285), channel_id=1, source_target_pairs={{0,8},{4,12},{8,0},{12,4},{16,24},{20,28},{24,16},{28,20},{1,9},{5... | collective-permute-start | bytes 6291464 | tf_op jit(solution)/shard_map/ppermute | solution.py:318
  459.0 52.7 %collective-permute-start.43 = (bf16[512,2048]{1,0:T(8,128)(2,1)}, bf16[512,2048]{1,0:T(8,128)(2,1)}, u32[]{:S(2)}, u32[]{:S(2)}) collective-permute-start(bf16[512,2048]{1,0:T(8,128)(2,1)} %get-tuple-element.2286), channel_id=1, source_target_pairs={{0,16},{4,20},{8,24},{12,28},{16,0},{20,4},{24,8},{28,12},{1,17},{... | collective-permute-start | bytes 6291464 | tf_op jit(solution)/shard_map/ppermute | solution.py:318
  511.8 201.4 %reduce-scatter.5.cloned.1.call-start = ((), (), s32[]{:S(2)}) async-start(), calls=%async_computation.5 | async-start | bytes 7864320 | tf_op jit(solution)/shard_map/reduce_scatter | solution.py:1197
  542.8 55.2 %collective-permute-start.47 = (bf16[512,2048]{1,0:T(8,128)(2,1)}, bf16[512,2048]{1,0:T(8,128)(2,1)}, u32[]{:S(2)}, u32[]{:S(2)}) collective-permute-start(bf16[512,2048]{1,0:T(8,128)(2,1)} %get-tuple-element.2469), channel_id=1, source_target_pairs={{0,8},{4,12},{8,0},{12,4},{16,24},{20,28},{24,16},{28,20},{1,9},{5... | collective-permute-start | bytes 6291464 | tf_op jit(solution)/shard_map/ppermute | solution.py:318
  543.8 54.3 %collective-permute-start.48 = (bf16[512,2048]{1,0:T(8,128)(2,1)}, bf16[512,2048]{1,0:T(8,128)(2,1)}, u32[]{:S(2)}, u32[]{:S(2)}) collective-permute-start(bf16[512,2048]{1,0:T(8,128)(2,1)} %get-tuple-element.2470), channel_id=1, source_target_pairs={{0,16},{4,20},{8,24},{12,28},{16,0},{20,4},{24,8},{28,12},{1,17},{... | collective-permute-start | bytes 6291464 | tf_op jit(solution)/shard_map/ppermute | solution.py:318
  598.1 35.9 %collective-permute-start.51 = (bf16[2048,1024]{1,0:T(8,128)(2,1)}, bf16[2048,1024]{1,0:T(8,128)(2,1)S(1)}, u32[]{:S(2)}, u32[]{:S(2)}) collective-permute-start(bf16[2048,1024]{1,0:T(8,128)(2,1)} %row_outer.16), channel_id=1, source_target_pairs={{0,4},{4,0},{8,12},{12,8},{16,20},{20,16},{24,28},{28,24},{1,5},{5... | collective-permute-start | bytes 12582920 | tf_op jit(solution)/shard_map/ppermute | solution.py:318
  636.1 40.5 %collective-permute-start.54 = (bf16[512,768]{1,0:T(8,128)(2,1)}, bf16[512,768]{1,0:T(8,128)(2,1)S(1)}, u32[]{:S(2)}, u32[]{:S(2)}) collective-permute-start(bf16[512,768]{1,0:T(8,128)(2,1)} %reduce-scatter.3.cloned.1.call-done), channel_id=1, source_target_pairs={{0,16},{4,20},{8,24},{12,28},{16,0},{20,4},{24,8},{28,12},{1,17},{... | collective-permute-start | bytes 2359304 | tf_op jit(solution)/shard_map/ppermute | solution.py:318
  637.2 39.4 %collective-permute-start.53 = (bf16[512,768]{1,0:T(8,128)(2,1)}, bf16[512,768]{1,0:T(8,128)(2,1)}, u32[]{:S(2)}, u32[]{:S(2)}) collective-permute-start(bf16[512,768]{1,0:T(8,128)(2,1)} %reduce-scatter.3.cloned.1.call-done), channel_id=1, source_target_pairs={{0,8},{4,12},{8,0},{12,4},{16,24},{20,28},{24,16},{28,20},{1,9},{5... | collective-permute-start | bytes 2359304 | tf_op jit(solution)/shard_map/ppermute | solution.py:318
  638.1 38.4 %collective-permute-start.55 = (bf16[512,512]{1,0:T(8,128)(2,1)}, bf16[512,512]{1,0:T(8,128)(2,1)S(1)}, u32[]{:S(2)}, u32[]{:S(2)}) collective-permute-start(bf16[512,512]{1,0:T(8,128)(2,1)} %get-tuple-element.2603), channel_id=1, source_target_pairs={{4,0},{12,8},{20,16},{28,24},{5,1},{13,9},{21,17},{29,25},{6,2},{1... | collective-permute-start | bytes 1572872 | tf_op jit(solution)/shard_map/ppermute | solution.py:1157
  639.4 37.1 %collective-permute-start.56 = (bf16[512,512]{1,0:T(8,128)(2,1)}, bf16[512,512]{1,0:T(8,128)(2,1)S(1)}, u32[]{:S(2)}, u32[]{:S(2)}) collective-permute-start(bf16[512,512]{1,0:T(8,128)(2,1)} %get-tuple-element.2607), channel_id=1, source_target_pairs={{4,0},{12,8},{20,16},{28,24},{5,1},{13,9},{21,17},{29,25},{6,2},{1... | collective-permute-start | bytes 1572872 | tf_op jit(solution)/shard_map/ppermute | solution.py:1157
  676.6 36.6 %collective-permute-start.59 = (bf16[1024,512]{1,0:T(8,128)(2,1)}, bf16[1024,512]{1,0:T(8,128)(2,1)}, u32[]{:S(2)}, u32[]{:S(2)}) collective-permute-start(bf16[1024,512]{1,0:T(8,128)(2,1)} %get-tuple-element.2698), channel_id=1, source_target_pairs={{0,8},{4,12},{8,0},{12,4},{16,24},{20,28},{24,16},{28,20},{1,9},{5... | collective-permute-start | bytes 3145736 | tf_op jit(solution)/shard_map/ppermute | solution.py:318
  677.8 35.4 %collective-permute-start.60 = (bf16[1024,512]{1,0:T(8,128)(2,1)}, bf16[1024,512]{1,0:T(8,128)(2,1)S(1)}, u32[]{:S(2)}, u32[]{:S(2)}) collective-permute-start(bf16[1024,512]{1,0:T(8,128)(2,1)} %get-tuple-element.2701), channel_id=1, source_target_pairs={{0,16},{4,20},{8,24},{12,28},{16,0},{20,4},{24,8},{28,12},{1,17},{... | collective-permute-start | bytes 3145736 | tf_op jit(solution)/shard_map/ppermute | solution.py:318
  733.3 39.2 %collective-permute-start.65 = (bf16[2048,1024]{1,0:T(8,128)(2,1)}, bf16[2048,1024]{1,0:T(8,128)(2,1)S(1)}, u32[]{:S(2)}, u32[]{:S(2)}) collective-permute-start(bf16[2048,1024]{1,0:T(8,128)(2,1)} %row_outer.20), channel_id=1, source_target_pairs={{0,4},{4,0},{8,12},{12,8},{16,20},{20,16},{24,28},{28,24},{1,5},{5... | collective-permute-start | bytes 12582920 | tf_op jit(solution)/shard_map/ppermute | solution.py:318
  733.3 39.2 %collective-permute-start.67 = (bf16[512,1536]{1,0:T(8,128)(2,1)}, bf16[512,1536]{1,0:T(8,128)(2,1)S(1)}, u32[]{:S(2)}, u32[]{:S(2)}) collective-permute-start(bf16[512,1536]{1,0:T(8,128)(2,1)} %reduce-scatter.5.cloned.1.call-done), channel_id=1, source_target_pairs={{0,16},{4,20},{8,24},{12,28},{16,0},{20,4},{24,8},{28,12},{1,17},{... | collective-permute-start | bytes 4718600 | tf_op jit(solution)/shard_map/ppermute | solution.py:318
  734.4 38.1 %collective-permute-start.66 = (bf16[512,1536]{1,0:T(8,128)(2,1)}, bf16[512,1536]{1,0:T(8,128)(2,1)}, u32[]{:S(2)}, u32[]{:S(2)}) collective-permute-start(bf16[512,1536]{1,0:T(8,128)(2,1)} %reduce-scatter.5.cloned.1.call-done), channel_id=1, source_target_pairs={{0,8},{4,12},{8,0},{12,4},{16,24},{20,28},{24,16},{28,20},{1,9},{5... | collective-permute-start | bytes 4718600 | tf_op jit(solution)/shard_map/ppermute | solution.py:318
  737.9 34.5 %collective-permute-start.69 = (bf16[512,256]{1,0:T(8,128)(2,1)}, bf16[512,256]{1,0:T(8,128)(2,1)}, u32[]{:S(2)}, u32[]{:S(2)}) collective-permute-start(bf16[512,256]{1,0:T(8,128)(2,1)} %get-tuple-element.3101), channel_id=1, source_target_pairs={{0,3},{1,0},{2,1},{3,2},{4,7},{5,4},{6,5},{7,6},{8,11},{9,8},{10,9... | collective-permute-start | bytes 786440 | tf_op jit(solution)/shard_map/ppermute | solution.py:323
  780.0 35.5 %collective-permute-start.75 = (bf16[256,2048]{1,0:T(8,128)(2,1)S(1)}, bf16[256,2048]{1,0:T(8,128)(2,1)S(1)}, u32[]{:S(2)}, u32[]{:S(2)}) collective-permute-start(bf16[256,2048]{1,0:T(8,128)(2,1)S(1)} %get-tuple-element.3036), channel_id=1, source_target_pairs={{0,0},{1,1},{4,2},{5,3},{2,4},{3,5},{6,6},{7,7},{8,8},{9,9},{12,10... | collective-permute-start | bytes 3145736 | tf_op jit(solution)/shard_map/ppermute | solution.py:395
  788.0 37.2 %collective-permute-start.80 = (bf16[256,2048]{1,0:T(8,128)(2,1)S(1)}, bf16[256,2048]{1,0:T(8,128)(2,1)S(1)}, u32[]{:S(2)}, u32[]{:S(2)}) collective-permute-start(bf16[256,2048]{1,0:T(8,128)(2,1)S(1)} %get-tuple-element.3035), channel_id=1, source_target_pairs={{1,0},{0,1},{5,2},{4,3},{3,4},{2,5},{7,6},{6,7},{9,8},{8,9},{13,10... | collective-permute-start | bytes 3145736 | tf_op jit(solution)/shard_map/ppermute | solution.py:395
  816.6 37.8 %collective-permute-start.78 = (bf16[1024,512]{1,0:T(8,128)(2,1)}, bf16[1024,512]{1,0:T(8,128)(2,1)S(1)}, u32[]{:S(2)}, u32[]{:S(2)}) collective-permute-start(bf16[1024,512]{1,0:T(8,128)(2,1)} %get-tuple-element.2890), channel_id=1, source_target_pairs={{0,8},{4,12},{8,0},{12,4},{16,24},{20,28},{24,16},{28,20},{1,9},{5... | collective-permute-start | bytes 3145736 | tf_op jit(solution)/shard_map/ppermute | solution.py:318
  817.6 36.9 %collective-permute-start.79 = (bf16[1024,512]{1,0:T(8,128)(2,1)}, bf16[1024,512]{1,0:T(8,128)(2,1)S(1)}, u32[]{:S(2)}, u32[]{:S(2)}) collective-permute-start(bf16[1024,512]{1,0:T(8,128)(2,1)} %get-tuple-element.2893), channel_id=1, source_target_pairs={{0,16},{4,20},{8,24},{12,28},{16,0},{20,4},{24,8},{28,12},{1,17},{... | collective-permute-start | bytes 3145736 | tf_op jit(solution)/shard_map/ppermute | solution.py:318
  (208 other events, 2737.8 us)
Sparse Core Ops, SparseCore 0:
  89.8 39.9 all-gather.2
  198.2 165.5 all-gather.4
  512.0 58.5 reduce-scatter.2
  598.2 109.2 reduce-scatter.4

commit v11 on v10

--- a/solution.py
+++ b/solution.py
@@ -884,6 +884,9 @@
     s = Stage()
     piece = width // shards
 
+    def three(side, far_shard):
+        return jnp.concatenate([side[:piece], far_shard, side[piece:]], 0)
+
     s.own_blocks = [
         column_block((w_query, key_matrix, value_matrix), me ^ i) for i in range(8)
     ]
@@ -893,7 +896,7 @@
     travelling = jnp.concatenate([s.own_blocks[0], gain_rows], 0)
     s.tokens_cuts = sequence_cuts(tokens)
     s.cotangent_cuts = sequence_cuts(cotangent)
-    s.out_block = column_block((w_out,), me)
+    out_own = lax.all_gather(column_block((w_out,), me), "shard", axis=0, tiled=True)
     s.ffn_block = column_block((w_gate, w_up, w_down), me)
     s.before, s.behind = around(travelling, 1), around(travelling, -1)
     s.other_lengths = across(lengths, CORE)
@@ -905,26 +908,24 @@
     s.x_first = to_sequence(s.tokens_cuts[0], 0)
     s.end()
 
-    out_own = lax.all_gather(s.out_block, "shard", axis=0, tiled=True)
     s.far_piece = s.ahead[:piece]
+    s.came_own = three(s.side, s.far_piece)
+    s.came_own_other = across(s.came_own, CORE)
     s.far_near = near(s.far_piece)
     s.side_last = far(*s.side_near)
     s.x_second = to_sequence(s.tokens_cuts[1], 1)
     s.gains = jnp.concatenate(
         [gain_rows[:2], *(part[piece : piece + 2] for part in (s.before, s.ahead, s.behind))], 1
     )
-    del s.out_block, s.tokens_cuts, s.before, s.behind, s.ahead
-    s.end()
-
-    def three(side, far_shard):
-        return jnp.concatenate([side[:piece], far_shard, side[piece:]], 0)
+    s.out_own = out_own
+    del s.tokens_cuts, s.before, s.behind, s.ahead
+    s.end()
 
     s.far_last = far(*s.far_near)
     s.grad_y_first = to_sequence(s.cotangent_cuts[0], 0)
-    s.came = [
-        three(*pair) for pair in zip((s.side, *s.side_near), (s.far_piece, *s.far_near))
-    ]
-    s.came_other = [across(block, CORE) for block in s.came]
+    came = [three(*pair) for pair in zip(s.side_near, s.far_near)]
+    s.came_other = [s.came_own_other, *(across(block, CORE) for block in came)]
+    s.came = [s.came_own, *came]
     gains = rolled(s.gains.astype(full))
     s.mlp_gains = gains[1:]
     s.attn_gains = gains[:1]
@@ -948,7 +949,7 @@
     cosine, sine = tables(query_pos, head_dim)
     s.cosine, sine = cosine[0, :, 0], sine[0, :, 0]
     s.sine = jnp.concatenate([-sine[:, : head_dim // 2], sine[:, head_dim // 2 :]], 1)
-    s.out_own = out_own
+    del s.came_own, s.came_own_other
     del s.gains, s.x_first, s.x_second, s.other_lengths
     del s.side, s.side_near, s.far_piece, s.far_near
     s.end()
@@ -1011,15 +1012,15 @@
     give_up(0)
     s.out_other = [across(s.out_own, CORE)]
     compute([1], [])
-    s.end()
-
+    s.grad_y_second = grad_y_second
+    s.end()
+
+    ffn_own = lax.all_gather(s.ffn_block, "shard", axis=0, tiled=True)
     give_up(1)
     compute([2], [0])
     s.out_near = out_near
-    s.grad_y_second = grad_y_second
-    s.end()
-
-    ffn_own = lax.all_gather(s.ffn_block, "shard", axis=0, tiled=True)
+    s.end()
+
     s.out_far = far(*s.out_near)
     s.out_other = [*s.out_other, *(across(block, CORE) for block in s.out_near)]
     give_up(2)
@@ -1221,23 +1222,22 @@
     s.end()
 
     s.out_near = send_near((s.out_head[0], s.out_tail[0]))
-    s.down_far = far(*s.down_near)
+    output_sent = from_sequences_send(s.output)
     give_back(0)
     finished1, finished2 = in_order([finish_call(1), finish_call(2)])
     s.finished = s.finished | {1: finished1, 2: finished2}
-    s.gate_up_total = gate_up_total
     s.end()
 
     def odd_half(half):
         return odd_call(s.normed, [s.finished[i][1] for i in range(4)], half)
 
     s.out_far = send_far(s.out_near, (s.out_tail[1], s.out_head[1]), by_columns)
-    s.down_spread = jnp.concatenate([s.down_total, *s.down_near, *s.down_far], 0)
-    s.down_spread_other = across(s.down_spread, CORE)
+    s.down_far = far(*s.down_near)
     (finished,) = in_order([finish_call(0)])
     s.finished = s.finished | {0: finished}
     (s.odd0,) = in_order([odd_half(0)])
-    del s.down_total, s.down_near, s.down_far
+    s.gate_up_total = gate_up_total
+    s.output_first = output_sent[0]
     s.end()
 
     my_group = me.astype(jnp.int32)[None]
@@ -1247,9 +1247,11 @@
 
     s.gate_up_near = near(s.gate_up_total)
     s.came0 = across(s.odd0, CORE)
+    s.down_spread = jnp.concatenate([s.down_total, *s.down_near, *s.down_far], 0)
+    s.down_spread_other = across(s.down_spread, CORE)
     out_sum = total(s.out_near, s.out_far, (s.out_head[2], s.out_tail[2]), by_columns)
     s.out_chunks = jnp.split(out_sum.astype(low), shards, 0)
-    s.out_ring = ring_sum_first(s.out_chunks)
+    s.output_second = output_sent[1]
     weights = [
         pair
         for i in range(4)
@@ -1277,6 +1279,7 @@
     s.grad_tokens = (
         s.grad_resid + norm_back(x_unit, s.inverse_in, grad_in * s.attn_gains)
     ).astype(low)
+    del s.down_total, s.down_near, s.down_far, s.output
     del s.odd0, s.out_near, s.out_far, s.out_head, s.out_tail, s.backs
     del s.own_blocks, s.came, s.came_other, s.grad_resid, s.x_low
     s.end()
@@ -1285,9 +1288,10 @@
         even = [s.finished[i][0] for i in range(4)]
         return [call(s.normed, even, came, half) for call in (head_call, tail_call)]
 
-    output_sent = from_sequences_send(s.output)
+    tokens_sent = from_sequences_send(s.grad_tokens)
     s.came1 = across(s.odd1, CORE)
-    s.out_ring_last = around(rounded_sum(s.out_chunks[3], s.out_ring[0]), 1)
+    s.out_ring = ring_sum_first(s.out_chunks)
+    s.gate_up_far = far(*s.gate_up_near)
     s.head0, s.tail0 = in_order(halves_call(0, s.came0))
     del s.odd1, s.came0
     s.end()
@@ -1297,46 +1301,47 @@
         return jnp.split(own.astype(low), shards, 0)
 
     s.near0 = send_near((s.head0[0], s.tail0[0]))
-    s.gain_came = across(s.gain_parts, CORE)
+    s.gate_up_own = jnp.concatenate([s.gate_up_total, *s.gate_up_near, *s.gate_up_far], 0)
+    s.gate_up_other = across(s.gate_up_own, CORE)
     s.head1, s.tail1, s.whole_down = in_order(
         [*halves_call(1, s.came1), whole_call((units,), s.down_spread, s.down_spread_other)]
     )
-    s.out_total = rounded_sum(s.out_chunks[0], s.out_ring[1], s.out_ring_last)
-    s.output_first = output_sent[0]
-    del s.came1, s.down_spread, s.down_spread_other, s.output, s.finished
-    del s.out_chunks, s.out_ring, s.out_ring_last
+    s.out_ring_last = around(rounded_sum(s.out_chunks[3], s.out_ring[0]), 1)
+    s.tokens_first = tokens_sent[0]
+    del s.came1, s.down_spread, s.down_spread_other, s.finished
+    del s.gate_up_near, s.gate_up_far, s.gate_up_total
     s.end()
 
     s.far0 = send_far(s.near0, (s.tail0[1], s.head0[1]), by_columns)
     s.near1 = send_near((s.head1[0], s.tail1[0]))
-    s.gain_parts = s.gain_parts + s.gain_came
-    s.output_second = output_sent[1]
+    s.out_total = rounded_sum(s.out_chunks[0], s.out_ring[1], s.out_ring_last)
+    (s.whole_gate_up,) = in_order([whole_call((units, units), s.gate_up_own, s.gate_up_other)])
+    s.tokens_second = tokens_sent[1]
+    del s.out_chunks, s.out_ring, s.out_ring_last, s.gate_up_own, s.gate_up_other, s.grad_tokens
     s.end()
 
     s.chunks0 = qkv_chunks(s.near0, s.far0, s.head0, s.tail0)
     s.ring0 = ring_sum_first(s.chunks0)
     s.far1 = send_far(s.near1, (s.tail1[1], s.head1[1]), by_columns)
-    s.gain_came = across(s.gain_parts, ACROSS_X)
+    s.gain_came = across(s.gain_parts, CORE)
     del s.near0, s.far0, s.head0, s.tail0
     s.end()
 
     s.last0 = around(rounded_sum(s.chunks0[3], s.ring0[0]), 1)
     s.chunks1 = qkv_chunks(s.near1, s.far1, s.head1, s.tail1)
     s.ring1 = ring_sum_first(s.chunks1)
-    s.gate_up_far = far(*s.gate_up_near)
     s.gain_parts = s.gain_parts + s.gain_came
+    s.gain_came = across(s.gain_parts, ACROSS_X)
     del s.near1, s.far1, s.head1, s.tail1
     s.end()
 
-    tokens_sent = from_sequences_send(s.grad_tokens)
     query_total = rounded_sum(s.chunks0[0], s.ring0[1], s.last0)
     s.total0 = jnp.concatenate([query_total, s.out_total], 1)
     s.spread0 = near(s.total0)
     s.last1 = around(rounded_sum(s.chunks1[3], s.ring1[0]), 1)
-    s.gate_up_own = jnp.concatenate([s.gate_up_total, *s.gate_up_near, *s.gate_up_far], 0)
-    s.gate_up_other = across(s.gate_up_own, CORE)
+    s.gain_parts = s.gain_parts + s.gain_came
     s.gain_came = across(s.gain_parts, ACROSS_Y)
-    del s.chunks0, s.ring0, s.last0, s.out_total, s.gate_up_near, s.gate_up_far, s.gate_up_total
+    del s.chunks0, s.ring0, s.last0, s.out_total
     s.end()
 
     s.spread_far0 = far(*s.spread0)
@@ -1344,7 +1349,6 @@
     s.spread1 = near(s.total1)
     s.gain_parts = s.gain_parts + s.gain_came
     s.gain_came = lax.ppermute(s.gain_parts, "shard", [(i, i ^ 1) for i in range(shards)])
-    ((s.whole_gate,),) = in_order([whole_call((units,), s.gate_up_own, s.gate_up_other)])
     del s.chunks1, s.ring1, s.last1
     s.end()
 
@@ -1353,9 +1357,7 @@
     s.spread_far1 = far(*s.spread1)
     s.gain_parts = s.gain_parts + s.gain_came
     s.gain_came = lax.ppermute(s.gain_parts, "shard", [(i, i ^ 2) for i in range(shards)])
-    ((s.whole_up,),) = in_order([whole_call((units,), s.gate_up_own, s.gate_up_other, 1)])
-    s.tokens_first = tokens_sent[0]
-    del s.total0, s.spread0, s.spread_far0, s.gate_up_own, s.gate_up_other
+    del s.total0, s.spread0, s.spread_far0
     s.end()
 
     s.own1 = jnp.concatenate([s.total1, *s.spread1, *s.spread_far1], 0)
@@ -1374,7 +1376,7 @@
     )
     return (
         jnp.stack(in_turn([s.output_first, s.output_second])),
-        jnp.stack(in_turn([s.tokens_first, tokens_sent[1]])),
+        jnp.stack(in_turn([s.tokens_first, s.tokens_second])),
         s.wide[0],
         s.whole0[0],
         whole_key,
@@ -1383,8 +1385,7 @@
         s.narrow[head_dim:],
         s.whole0[1],
         s.wide[1],
-        s.whole_gate,
-        s.whole_up,
+        *s.whole_gate_up,
         *s.whole_down,
     )
 

time: 1020 us -> 1020 us (level)
  starting transfers between devices: 145 us -> 157 us
  waiting for transfers between devices: 270 us -> 258 us
    ppermute x12, waiting for transfers between devices: 38.6 us -> 63.4 us  [around(): lax.ppermute(x, 'shard', [(i, (i + by) % count) for i in range(count)])]
    ppermute x78, waiting for transfers between devices: 198 us -> 180 us  [across(): return lax.ppermute(x, 'rep', [(i, i ^ mask) for i in range(count)])]
    ppermute x4, waiting for transfers between devices: 16 us -> 1.29 us  [from_sequences_send(): lax.ppermute(lax.dynamic_index_in_dim(x, turn ^ odd, 0, keepdims=False),...]
    ppermute x78, starting transfers between devices: 91.1 us -> 103 us  [across(): return lax.ppermute(x, 'rep', [(i, i ^ mask) for i in range(count)])]
    pallas_call x5 -> x4, Pallas kernels: 48.4 us -> 44.3 us  [whole_columns(): pl.pallas_call(body, grid_spec=pltpu.PrefetchScalarGridSpec(num_scalar_pr...]
  transfers between devices with their start and end apart: 112 -> 112, of which waited for: 30 -> 38; matrix products, arithmetic and copies ran while one was open for 10% -> 10% of each run, Pallas kernels for 38% -> 38%
where the time goes in v11:
time: 1020 us; the launch traced here: 1010 us
  Pallas kernels  431 us (42%)
  waiting for transfers between devices  258 us (25%)
  starting transfers between devices  157 us (15%)
  local copies, waits for them, and re-layouts  75 us (7%)
  other arithmetic  69.3 us (7%)
  between operations  16.2 us (2%)
    ppermute x78, waiting for transfers between devices, across(): return lax.ppermute(x, 'rep', [(i, i ^ mask) for i in range(count)])  180 us
    pallas_call x13, Pallas kernels, row_outer(): pl.pallas_call(body, grid=(tiles,), out_shape=[jax.ShapeDtypeStruct((tile...  120 us
    pallas_call x16, Pallas kernels, call(): pl.pallas_call(body, grid=(1,), out_shape=outs, in_specs=in_specs, out_sp...  120 us
    ppermute x78, starting transfers between devices, across(): return lax.ppermute(x, 'rep', [(i, i ^ mask) for i in range(count)])  103 us
    ppermute x12, waiting for transfers between devices, around(): lax.ppermute(x, 'shard', [(i, (i + by) % count) for i in range(count)])  63.4 us
    pallas_call x2, Pallas kernels, hidden_units(): pl.pallas_call(body, grid=(3,), out_shape=[jax.ShapeDtypeStruct((rows, un...  59.9 us
    pallas_call x4, Pallas kernels, from_hidden(): pl.pallas_call(body, grid=(4,), out_shape=[jax.ShapeDtypeStruct((2 * rows...  59.2 us
    pallas_call x4, Pallas kernels, whole_columns(): pl.pallas_call(body, grid_spec=pltpu.PrefetchScalarGridSpec(num_scalar_pr...  44.3 us
  transfers between devices with their start and end apart: 112, of which 38 were waited for; matrix products, arithmetic and copies ran while one was open for 10% of the time, Pallas kernels for 38%

profile of v11, /device:TPU:0, one launch (start us, length us, event | category | flops | bytes accessed | tf_op | source)
XLA Modules:
  0.0 1006.2 jit_solution(9652519459018379996)
XLA Ops:
  32.8 10.6 %collective-permute-done = bf16[528,512]{1,0:T(8,128)(2,1)} collective-permute-done((bf16[528,512]{1,0:T(8,128)(2,1)}, bf16[528,512]{1,0:T(8,128)(2,1)}, u32[]{:S(2)}, u32[]{:S(2)}) %collective-permute-start) | collective-permute-done | bytes 540704 | tf_op jit(solution)/shard_map/ppermute | solution.py:323
  48.8 9.4 collective-permute-start.6
  60.6 29.7 %collective-permute-done.3 = bf16[528,512]{1,0:T(8,128)(2,1)} collective-permute-done((bf16[528,512]{1,0:T(8,128)(2,1)}, bf16[528,512]{1,0:T(8,128)(2,1)}, u32[]{:S(2)}, u32[]{:S(2)}) %collective-permute-start.3) | collective-permute-done | bytes 540704 | tf_op jit(solution)/shard_map/ppermute | solution.py:323
  92.2 13.8 %collective-permute-start.7 = (bf16[1536,512]{1,0:T(8,128)(2,1)S(1)}, bf16[1536,512]{1,0:T(8,128)(2,1)}, u32[]{:S(2)}, u32[]{:S(2)}) collective-permute-start(bf16[1536,512]{1,0:T(8,128)(2,1)S(1)} %pad_maximum_fusion.8.came0.refs_9_), channel_id=1, source_target_pairs={{0,4},{4,0},{8,12},{12,8},{16,20},{20,16},{24,28},{28,24},{1,5},{5... | collective-permute-start | bytes 4718600 | tf_op jit(solution)/shard_map/ppermute | solution.py:318
  126.7 9.6 collective-permute-done.10
  161.1 14.0 %collective-permute-start.18 = (bf16[1536,512]{1,0:T(8,128)(2,1)S(1)}, bf16[1536,512]{1,0:T(8,128)(2,1)S(1)}, u32[]{:S(2)}, u32[]{:S(2)}) collective-permute-start(bf16[1536,512]{1,0:T(8,128)(2,1)S(1)} %constant_dynamic-update-slice_fusion.came0.refs_21_), channel_id=1, source_target_pairs={{0,4},{4,0},{8,12},{12,8},{16,20},{20,16},{24,28},{28,24},{1,5},{5... | collective-permute-start | bytes 4718600 | tf_op jit(solution)/shard_map/ppermute | solution.py:318
  267.5 12.1 %close_attention.1 = (f32[512,2048]{1,0:T(8,128)}, bf16[512,2048]{1,0:T(8,128)(2,1)}) custom-call(bf16[512,2048]{1,0:T(8,128)(2,1)} %pad_maximum_fusion.3.x, bf16[512,512]{1,0:T(8,128)(2,1)} %get-tuple-element.2591.refs_0_.refs_1_.refs_4_, bf16[512,512]{1,0:T(8,128)(2,1)} %get-tuple-element.2588.refs_1_.refs_2_.refs_3_, ...), custom_call_target="tpu_custom_call" | custom-call | flops 1 | bytes 1 | tf_op jit(solution)/shard_map/close_attention/pallas_call | solution.py:789
  280.6 21.1 %collective-permute-done.33.refs_7_.refs_2_ = bf16[512,2048]{1,0:T(8,128)(2,1)S(1)} collective-permute-done((bf16[512,2048]{1,0:T(8,128)(2,1)S(1)}, bf16[512,2048]{1,0:T(8,128)(2,1)S(1)}, u32[]{:S(2)}, u32[]{:S(2)}) %collective-permute-start.33) | collective-permute-done | bytes 2097184 | tf_op jit(solution)/shard_map/ppermute | solution.py:318
  303.2 41.7 %collective-permute-done.35.refs_2_ = bf16[512,2048]{1,0:T(8,128)(2,1)S(1)} collective-permute-done((bf16[512,2048]{1,0:T(8,128)(2,1)}, bf16[512,2048]{1,0:T(8,128)(2,1)S(1)}, u32[]{:S(2)}, u32[]{:S(2)}) %collective-permute-start.35) | collective-permute-done | bytes 2097184 | tf_op jit(solution)/shard_map/ppermute | solution.py:318
  351.9 22.0 %collective-permute-done.39.refs_4_ = bf16[256,2048]{1,0:T(8,128)(2,1)S(1)} collective-permute-done((bf16[256,2048]{1,0:T(8,128)(2,1)S(1)}, bf16[256,2048]{1,0:T(8,128)(2,1)S(1)}, u32[]{:S(2)}, u32[]{:S(2)}) %collective-permute-start.39) | collective-permute-done | bytes 1048608 | tf_op jit(solution)/shard_map/ppermute | solution.py:318
  375.4 18.2 %collective-permute-done.37.refs_9_.refs_4_ = bf16[256,2048]{1,0:T(8,128)(2,1)S(1)} collective-permute-done((bf16[256,2048]{1,0:T(8,128)(2,1)S(1)}, bf16[256,2048]{1,0:T(8,128)(2,1)S(1)}, u32[]{:S(2)}, u32[]{:S(2)}) %collective-permute-start.37) | collective-permute-done | bytes 1048608 | tf_op jit(solution)/shard_map/ppermute | solution.py:318
  395.0 29.7 %hidden_units.2 = (bf16[2048,768]{1,0:T(8,128)(2,1)}, bf16[2048,768]{1,0:T(8,128)(2,1)}, bf16[2048,768]{1,0:T(8,128)(2,1)}) custom-call(bf16[512,2048]{1,0:T(8,128)(2,1)} %get-tuple-element.2463.refs_0_, bf16[512,2048]{1,0:T(8,128)(2,1)} %copy-done.15, bf16[512,2048]{1,0:T(8,128)(2,1)} %copy-done.14, bf16[256,2048]{1,0:T(8,128)(2,1)} %copy-done.27, ...), custom_call_target="tpu_custom_call" | custom-call | flops 1 | bytes 1 | tf_op jit(solution)/shard_map/hidden_units/pallas_call | solution.py:656
  424.7 30.2 %hidden_units.3 = (bf16[2048,768]{1,0:T(8,128)(2,1)}, bf16[2048,768]{1,0:T(8,128)(2,1)}, bf16[2048,768]{1,0:T(8,128)(2,1)}) custom-call(bf16[512,2048]{1,0:T(8,128)(2,1)} %get-tuple-element.2463.refs_0_, bf16[512,2048]{1,0:T(8,128)(2,1)} %copy-done.15, bf16[512,2048]{1,0:T(8,128)(2,1)} %copy-done.14, bf16[256,2048]{1,0:T(8,128)(2,1)} %copy-done.27, ...), custom_call_target="tpu_custom_call" | custom-call | flops 1 | bytes 1 | tf_op jit(solution)/shard_map/hidden_units/pallas_call | solution.py:656
  454.9 12.6 %row_outer.13 = bf16[2048,768]{1,0:T(8,128)(2,1)} custom-call(bf16[512,2048]{1,0:T(8,128)(2,1)} %copy-done.7, bf16[512,2048]{1,0:T(8,128)(2,1)} %copy-done.17, bf16[512,2048]{1,0:T(8,128)(2,1)} %copy-done.16, bf16[256,2048]{1,0:T(8,128)(2,1)} %collective-permute-done.36.refs_8_.refs_3_, bf16[256,2048]{1,0:T(8,128)(2,1)} %copy-done.28, ...), custom_call_target="tpu_custom_call" | custom-call | flops 6442450944 | bytes 11534336 | tf_op jit(solution)/shard_map/row_outer/pallas_call | solution.py:739
  467.9 18.9 %from_hidden.4 = (bf16[512,2048]{1,0:T(8,128)(2,1)}, bf16[512,2048]{1,0:T(8,128)(2,1)}) custom-call(bf16[2048,768]{1,0:T(8,128)(2,1)} %get-tuple-element.2474.refs_0_.refs_1_.refs_2_.refs_3_.refs_5_, bf16[2048,768]{1,0:T(8,128)(2,1)} %get-tuple-element.2474.refs_0_.refs_1_.refs_2_.refs_3_.refs_5_, ...), custom_call_target="tpu_custom_call" | custom-call | flops 1 | bytes 1 | tf_op jit(solution)/shard_map/from_hidden/pallas_call | solution.py:695
  488.7 13.2 %row_outer.14 = bf16[2048,768]{1,0:T(8,128)(2,1)} custom-call(bf16[512,2048]{1,0:T(8,128)(2,1)} %copy-done.7, bf16[512,2048]{1,0:T(8,128)(2,1)} %copy-done.17, bf16[512,2048]{1,0:T(8,128)(2,1)} %copy-done.16, bf16[256,2048]{1,0:T(8,128)(2,1)} %collective-permute-done.36.refs_8_.refs_3_, bf16[256,2048]{1,0:T(8,128)(2,1)} %copy-done.28, ...), custom_call_target="tpu_custom_call" | custom-call | flops 6442450944 | bytes 11534336 | tf_op jit(solution)/shard_map/row_outer/pallas_call | solution.py:739
  501.9 18.8 %from_hidden.5 = (bf16[512,2048]{1,0:T(8,128)(2,1)}, bf16[512,2048]{1,0:T(8,128)(2,1)}) custom-call(bf16[2048,768]{1,0:T(8,128)(2,1)} %get-tuple-element.2474.refs_0_.refs_1_.refs_2_.refs_3_.refs_5_, bf16[2048,768]{1,0:T(8,128)(2,1)} %get-tuple-element.2474.refs_0_.refs_1_.refs_2_.refs_3_.refs_5_, ...), custom_call_target="tpu_custom_call" | custom-call | flops 1 | bytes 1 | tf_op jit(solution)/shard_map/from_hidden/pallas_call | solution.py:695
  520.7 19.4 %row_outer.15 = bf16[2048,1536]{1,0:T(8,128)(2,1)} custom-call(bf16[512,2048]{1,0:T(8,128)(2,1)} %get-tuple-element.2463.refs_0_, bf16[512,2048]{1,0:T(8,128)(2,1)} %copy-done.15, bf16[512,2048]{1,0:T(8,128)(2,1)} %copy-done.14, bf16[256,2048]{1,0:T(8,128)(2,1)} %copy-done.27, bf16[256,2048]{1,0:T(8,128)(2,1)} %copy-done.26, ...), custom_call_target="tpu_custom_call" | custom-call | flops 12884901888 | bytes 14680064 | tf_op jit(solution)/shard_map/row_outer/pallas_call | solution.py:739
  547.9 10.7 %from_hidden.6 = (bf16[512,2048]{1,0:T(8,128)(2,1)}, bf16[512,2048]{1,0:T(8,128)(2,1)}) custom-call(bf16[2048,768]{1,0:T(8,128)(2,1)} %get-tuple-element.2383.refs_5_.refs_0_.refs_1_.refs_2_.refs_3_, bf16[2048,768]{1,0:T(8,128)(2,1)} %get-tuple-element.2383.refs_5_.refs_0_.refs_1_.refs_2_.refs_3_, ...), custom_call_target="tpu_custom_call" | custom-call | flops 1 | bytes 1 | tf_op jit(solution)/shard_map/from_hidden/pallas_call | solution.py:695
  558.6 10.8 %from_hidden.7 = (bf16[512,2048]{1,0:T(8,128)(2,1)}, bf16[512,2048]{1,0:T(8,128)(2,1)}) custom-call(bf16[2048,768]{1,0:T(8,128)(2,1)} %get-tuple-element.2383.refs_5_.refs_0_.refs_1_.refs_2_.refs_3_, bf16[2048,768]{1,0:T(8,128)(2,1)} %get-tuple-element.2383.refs_5_.refs_0_.refs_1_.refs_2_.refs_3_, ...), custom_call_target="tpu_custom_call" | custom-call | flops 1 | bytes 1 | tf_op jit(solution)/shard_map/from_hidden/pallas_call | solution.py:695
  583.7 13.3 %attend_back.4 = (bf16[512,512]{1,0:T(8,128)(2,1)}, f32[512,512]{1,0:T(8,128)}, bf16[512,512]{1,0:T(8,128)(2,1)}, f32[1,128]{1,0:T(1,128)}) custom-call(s32[2]{0:T(128)} %pad_add_fusion.info, bf16[512,512]{1,0:T(8,128)(2,1)} %get-tuple-element.2430.query, bf16[512,512]{1,0:T(8,128)(2,1)} %copy-done.43, bf16[512,512]{1,0:T(8,128)(2,1)} %get-tuple-element.2432.own, ...), custom_call_target="tpu_custom_call" | custom-call | flops 1 | bytes 1 | tf_op jit(solution)/shard_map/attend_back/pallas_call | solution.py:616
  607.1 19.7 %row_outer.17 = bf16[2048,1536]{1,0:T(8,128)(2,1)} custom-call(bf16[512,2048]{1,0:T(8,128)(2,1)} %get-tuple-element.2463.refs_0_, bf16[512,2048]{1,0:T(8,128)(2,1)} %copy-done.15, bf16[512,2048]{1,0:T(8,128)(2,1)} %copy-done.14, bf16[256,2048]{1,0:T(8,128)(2,1)} %copy-done.27, bf16[256,2048]{1,0:T(8,128)(2,1)} %copy-done.26, ...), custom_call_target="tpu_custom_call" | custom-call | flops 12884901888 | bytes 14680064 | tf_op jit(solution)/shard_map/row_outer/pallas_call | solution.py:739
  636.2 13.2 %attend_back.5 = (bf16[512,512]{1,0:T(8,128)(2,1)}, f32[512,512]{1,0:T(8,128)}, bf16[512,512]{1,0:T(8,128)(2,1)}, f32[1,128]{1,0:T(1,128)}) custom-call(s32[2]{0:T(128)} %pad_add_fusion.info, bf16[512,512]{1,0:T(8,128)(2,1)} %get-tuple-element.2513.query, bf16[512,512]{1,0:T(8,128)(2,1)} %copy-done.41, bf16[512,512]{1,0:T(8,128)(2,1)} %get-tuple-element.2515.own, ...), custom_call_target="tpu_custom_call" | custom-call | flops 1 | bytes 1 | tf_op jit(solution)/shard_map/attend_back/pallas_call | solution.py:616
  649.4 13.4 %attend_back.6 = (bf16[512,512]{1,0:T(8,128)(2,1)}, f32[512,512]{1,0:T(8,128)}, bf16[512,512]{1,0:T(8,128)(2,1)}, f32[1,128]{1,0:T(1,128)}) custom-call(s32[2]{0:T(128)} %pad_add_fusion.info, bf16[512,512]{1,0:T(8,128)(2,1)} %get-tuple-element.2528.query, bf16[512,512]{1,0:T(8,128)(2,1)} %copy-done.42, bf16[512,512]{1,0:T(8,128)(2,1)} %get-tuple-element.2530.own, ...), custom_call_target="tpu_custom_call" | custom-call | flops 1 | bytes 1 | tf_op jit(solution)/shard_map/attend_back/pallas_call | solution.py:616
  685.4 13.1 %attend_back.7 = (bf16[512,512]{1,0:T(8,128)(2,1)}, f32[512,512]{1,0:T(8,128)}, bf16[512,512]{1,0:T(8,128)(2,1)}, f32[1,128]{1,0:T(1,128)}) custom-call(s32[2]{0:T(128)} %pad_add_fusion.info, bf16[512,512]{1,0:T(8,128)(2,1)} %get-tuple-element.2596.query, bf16[512,512]{1,0:T(8,128)(2,1)} %copy-done.40, bf16[512,512]{1,0:T(8,128)(2,1)} %get-tuple-element.2598.own, ...), custom_call_target="tpu_custom_call" | custom-call | flops 1 | bytes 1 | tf_op jit(solution)/shard_map/attend_back/pallas_call | solution.py:616
  720.7 9.2 collective-permute-done.57
  740.3 8.1 row_outer.20
  777.4 15.8 %back_to_rows.1 = f32[512,2048]{1,0:T(8,128)} custom-call(bf16[512,512]{1,0:T(8,128)(2,1)} %get-tuple-element.2871.refs_0_.refs_4_, bf16[512,512]{1,0:T(8,128)(2,1)} %get-tuple-element.2786.refs_1_, bf16[512,512]{1,0:T(8,128)(2,1)} %get-tuple-element.2868.refs_2_.refs_1_.refs_3_, bf16[512,512]{1,0:T(8,128)(2,1)} %get-tuple-element.2789.refs_2_.refs_3_, ...), custom_call_target="tpu_custom_call" | custom-call | flops 1 | bytes 1 | tf_op jit(solution)/shard_map/back_to_rows/pallas_call | solution.py:842
  852.6 11.1 %whole_columns.4 = f32[512,6144]{1,0:T(8,128)} custom-call(s32[1]{0:T(128)} %bitcast.21.me_ref, bf16[2048,768]{1,0:T(8,128)(2,1)} %constant_dynamic-update-slice_fusion.6.own_ref, bf16[2048,768]{1,0:T(8,128)(2,1)} %collective-permute-done.66.other_ref), custom_call_target="tpu_custom_call" | custom-call | flops 1 | bytes 1 | tf_op jit(solution)/shard_map/whole_columns/pallas_call | solution.py:431
  875.3 17.8 %whole_columns.5 = (f32[512,6144]{1,0:T(8,128)}, f32[512,6144]{1,0:T(8,128)}) custom-call(s32[1]{0:T(128)} %bitcast.21.me_ref, bf16[2048,1536]{1,0:T(8,128)(2,1)} %constant_dynamic-update-slice_fusion.11.own_ref, bf16[2048,1536]{1,0:T(8,128)(2,1)} %collective-permute-done.75.other_ref), custom_call_target="tpu_custom_call" | custom-call | flops 1 | bytes 1 | tf_op jit(solution)/shard_map/whole_columns/pallas_call | solution.py:431
  914.3 10.8 %collective-permute-done.88 = bf16[512,256]{1,0:T(8,128)(2,1)S(1)} collective-permute-done((bf16[512,256]{1,0:T(8,128)(2,1)S(1)}, bf16[512,256]{1,0:T(8,128)(2,1)S(1)}, u32[]{:S(2)}, u32[]{:S(2)}) %collective-permute-start.88) | collective-permute-done | bytes 262176 | tf_op jit(solution)/shard_map/ppermute | solution.py:323
  977.6 9.0 whole_columns.6
  (662 shorter events, 468.8 us)
Async XLA Ops:
  7.2 119.5 %all-gather.3.cloned.1.call-start = ((), (), s32[]{:S(2)}) async-start(), calls=%async_computation.2 | async-start | bytes 1310720 | tf_op jit(solution)/shard_map/all_gather | solution.py:899
  45.7 44.6 %collective-permute-start.5 = (bf16[1024,512]{1,0:T(8,128)(2,1)S(1)}, bf16[1024,512]{1,0:T(8,128)(2,1)}, u32[]{:S(2)}, u32[]{:S(2)}) collective-permute-start(bf16[1024,512]{1,0:T(8,128)(2,1)S(1)} %pad_maximum_fusion.11), channel_id=1, source_target_pairs={{0,16},{4,20},{8,24},{12,28},{16,0},{20,4},{24,8},{28,12},{1,17},{... | collective-permute-start | bytes 3145736 | tf_op jit(solution)/shard_map/ppermute | solution.py:318
  47.3 43.1 %collective-permute-start.4 = (bf16[1024,512]{1,0:T(8,128)(2,1)S(1)}, bf16[1024,512]{1,0:T(8,128)(2,1)}, u32[]{:S(2)}, u32[]{:S(2)}) collective-permute-start(bf16[1024,512]{1,0:T(8,128)(2,1)S(1)} %pad_maximum_fusion.11), channel_id=1, source_target_pairs={{0,8},{4,12},{8,0},{12,4},{16,24},{20,28},{24,16},{28,20},{1,9},{5... | collective-permute-start | bytes 3145736 | tf_op jit(solution)/shard_map/ppermute | solution.py:318
  48.8 41.6 %collective-permute-start.6 = (bf16[256,2048]{1,0:T(8,128)(2,1)}, bf16[256,2048]{1,0:T(8,128)(2,1)}, u32[]{:S(2)}, u32[]{:S(2)}) collective-permute-start(bf16[256,2048]{1,0:T(8,128)(2,1)} %get-tuple-element.1540), channel_id=1, source_target_pairs={{0,0},{1,1},{2,4},{3,5},{4,2},{5,3},{6,6},{7,7},{8,8},{9,9},{10,12... | collective-permute-start | bytes 3145736 | tf_op jit(solution)/shard_map/ppermute | solution.py:388
  58.2 32.1 %collective-permute-start.3 = (bf16[528,512]{1,0:T(8,128)(2,1)}, bf16[528,512]{1,0:T(8,128)(2,1)}, u32[]{:S(2)}, u32[]{:S(2)}) collective-permute-start(bf16[528,512]{1,0:T(8,128)(2,1)} %collective-permute-done), channel_id=1, source_target_pairs={{0,1},{1,2},{2,3},{3,0},{4,5},{5,6},{6,7},{7,4},{8,9},{9,10},{10,1... | collective-permute-start | bytes 1622024 | tf_op jit(solution)/shard_map/ppermute | solution.py:323
  60.6 334.3 %all-gather.5.cloned.1.call-start = ((), (), s32[]{:S(2)}) async-start(), calls=%async_computation.3 | async-start | bytes 11796480 | tf_op jit(solution)/shard_map/all_gather | solution.py:1018
  92.2 44.1 %collective-permute-start.7 = (bf16[1536,512]{1,0:T(8,128)(2,1)S(1)}, bf16[1536,512]{1,0:T(8,128)(2,1)}, u32[]{:S(2)}, u32[]{:S(2)}) collective-permute-start(bf16[1536,512]{1,0:T(8,128)(2,1)S(1)} %pad_maximum_fusion.8.came0.refs_9_), channel_id=1, source_target_pairs={{0,4},{4,0},{8,12},{12,8},{16,20},{20,16},{24,28},{28,24},{1,5},{5... | collective-permute-start | bytes 4718600 | tf_op jit(solution)/shard_map/ppermute | solution.py:318
  199.8 427.0 %reduce-scatter.3.cloned.1.call-start = ((), (), s32[]{:S(2)}) async-start(), calls=%async_computation.4 | async-start | bytes 3932160 | tf_op jit(solution)/shard_map/reduce_scatter | solution.py:1130
  253.0 48.6 %collective-permute-start.33 = (bf16[512,2048]{1,0:T(8,128)(2,1)S(1)}, bf16[512,2048]{1,0:T(8,128)(2,1)S(1)}, u32[]{:S(2)}, u32[]{:S(2)}) collective-permute-start(bf16[512,2048]{1,0:T(8,128)(2,1)S(1)} %maximum_select_fusion.refs_5_.refs_0_), channel_id=1, source_target_pairs={{0,16},{4,20},{8,24},{12,28},{16,0},{20,4},{24,8},{28,12},{1,17},{... | collective-permute-start | bytes 6291464 | tf_op jit(solution)/shard_map/ppermute | solution.py:318
  254.6 48.6 %collective-permute-start.32 = (bf16[512,2048]{1,0:T(8,128)(2,1)S(1)}, bf16[512,2048]{1,0:T(8,128)(2,1)S(1)}, u32[]{:S(2)}, u32[]{:S(2)}) collective-permute-start(bf16[512,2048]{1,0:T(8,128)(2,1)S(1)} %maximum_select_fusion.refs_5_.refs_0_), channel_id=1, source_target_pairs={{0,8},{4,12},{8,0},{12,4},{16,24},{20,28},{24,16},{28,20},{1,9},{5... | collective-permute-start | bytes 6291464 | tf_op jit(solution)/shard_map/ppermute | solution.py:318
  279.5 65.4 %collective-permute-start.35 = (bf16[512,2048]{1,0:T(8,128)(2,1)}, bf16[512,2048]{1,0:T(8,128)(2,1)S(1)}, u32[]{:S(2)}, u32[]{:S(2)}) collective-permute-start(bf16[512,2048]{1,0:T(8,128)(2,1)} %get-tuple-element.2463.refs_0_), channel_id=1, source_target_pairs={{0,16},{4,20},{8,24},{12,28},{16,0},{20,4},{24,8},{28,12},{1,17},{... | collective-permute-start | bytes 6291464 | tf_op jit(solution)/shard_map/ppermute | solution.py:318
  280.1 66.1 %collective-permute-start.34 = (bf16[512,2048]{1,0:T(8,128)(2,1)}, bf16[512,2048]{1,0:T(8,128)(2,1)S(1)}, u32[]{:S(2)}, u32[]{:S(2)}) collective-permute-start(bf16[512,2048]{1,0:T(8,128)(2,1)} %get-tuple-element.2463.refs_0_), channel_id=1, source_target_pairs={{0,8},{4,12},{8,0},{12,4},{16,24},{20,28},{24,16},{28,20},{1,9},{5... | collective-permute-start | bytes 6291464 | tf_op jit(solution)/shard_map/ppermute | solution.py:318
  350.1 43.5 %collective-permute-start.37 = (bf16[256,2048]{1,0:T(8,128)(2,1)S(1)}, bf16[256,2048]{1,0:T(8,128)(2,1)S(1)}, u32[]{:S(2)}, u32[]{:S(2)}) collective-permute-start(bf16[256,2048]{1,0:T(8,128)(2,1)S(1)} %slice.175), channel_id=1, source_target_pairs={{0,8},{4,12},{8,0},{12,4},{16,24},{20,28},{24,16},{28,20},{1,9},{5... | collective-permute-start | bytes 3145736 | tf_op jit(solution)/shard_map/ppermute | solution.py:318
  350.7 44.2 %collective-permute-start.36 = (bf16[256,2048]{1,0:T(8,128)(2,1)S(1)}, bf16[256,2048]{1,0:T(8,128)(2,1)}, u32[]{:S(2)}, u32[]{:S(2)}) collective-permute-start(bf16[256,2048]{1,0:T(8,128)(2,1)S(1)} %slice.174), channel_id=1, source_target_pairs={{0,16},{4,20},{8,24},{12,28},{16,0},{20,4},{24,8},{28,12},{1,17},{... | collective-permute-start | bytes 3145736 | tf_op jit(solution)/shard_map/ppermute | solution.py:318
  486.9 53.3 %collective-permute-start.42 = (bf16[512,2048]{1,0:T(8,128)(2,1)}, bf16[512,2048]{1,0:T(8,128)(2,1)}, u32[]{:S(2)}, u32[]{:S(2)}) collective-permute-start(bf16[512,2048]{1,0:T(8,128)(2,1)} %get-tuple-element.2294), channel_id=1, source_target_pairs={{0,8},{4,12},{8,0},{12,4},{16,24},{20,28},{24,16},{28,20},{1,9},{5... | collective-permute-start | bytes 6291464 | tf_op jit(solution)/shard_map/ppermute | solution.py:318
  487.6 52.6 %collective-permute-start.43 = (bf16[512,2048]{1,0:T(8,128)(2,1)}, bf16[512,2048]{1,0:T(8,128)(2,1)}, u32[]{:S(2)}, u32[]{:S(2)}) collective-permute-start(bf16[512,2048]{1,0:T(8,128)(2,1)} %get-tuple-element.2295), channel_id=1, source_target_pairs={{0,16},{4,20},{8,24},{12,28},{16,0},{20,4},{24,8},{28,12},{1,17},{... | collective-permute-start | bytes 6291464 | tf_op jit(solution)/shard_map/ppermute | solution.py:318
  540.3 216.1 %reduce-scatter.5.cloned.1.call-start = ((), (), s32[]{:S(2)}) async-start(), calls=%async_computation.5 | async-start | bytes 7864320 | tf_op jit(solution)/shard_map/reduce_scatter | solution.py:1198
  571.6 55.2 %collective-permute-start.47 = (bf16[512,2048]{1,0:T(8,128)(2,1)}, bf16[512,2048]{1,0:T(8,128)(2,1)}, u32[]{:S(2)}, u32[]{:S(2)}) collective-permute-start(bf16[512,2048]{1,0:T(8,128)(2,1)} %get-tuple-element.2478), channel_id=1, source_target_pairs={{0,8},{4,12},{8,0},{12,4},{16,24},{20,28},{24,16},{28,20},{1,9},{5... | collective-permute-start | bytes 6291464 | tf_op jit(solution)/shard_map/ppermute | solution.py:318
  572.7 54.1 %collective-permute-start.48 = (bf16[512,2048]{1,0:T(8,128)(2,1)}, bf16[512,2048]{1,0:T(8,128)(2,1)}, u32[]{:S(2)}, u32[]{:S(2)}) collective-permute-start(bf16[512,2048]{1,0:T(8,128)(2,1)} %get-tuple-element.2479), channel_id=1, source_target_pairs={{0,16},{4,20},{8,24},{12,28},{16,0},{20,4},{24,8},{28,12},{1,17},{... | collective-permute-start | bytes 6291464 | tf_op jit(solution)/shard_map/ppermute | solution.py:318
  626.9 36.0 %collective-permute-start.51 = (bf16[2048,1024]{1,0:T(8,128)(2,1)}, bf16[2048,1024]{1,0:T(8,128)(2,1)S(1)}, u32[]{:S(2)}, u32[]{:S(2)}) collective-permute-start(bf16[2048,1024]{1,0:T(8,128)(2,1)} %row_outer.16), channel_id=1, source_target_pairs={{0,4},{4,0},{8,12},{12,8},{16,20},{20,16},{24,28},{28,24},{1,5},{5... | collective-permute-start | bytes 12582920 | tf_op jit(solution)/shard_map/ppermute | solution.py:318
  665.0 40.3 %collective-permute-start.54 = (bf16[512,768]{1,0:T(8,128)(2,1)}, bf16[512,768]{1,0:T(8,128)(2,1)S(1)}, u32[]{:S(2)}, u32[]{:S(2)}) collective-permute-start(bf16[512,768]{1,0:T(8,128)(2,1)} %reduce-scatter.3.cloned.1.call-done), channel_id=1, source_target_pairs={{0,16},{4,20},{8,24},{12,28},{16,0},{20,4},{24,8},{28,12},{1,17},{... | collective-permute-start | bytes 2359304 | tf_op jit(solution)/shard_map/ppermute | solution.py:318
  666.0 39.3 %collective-permute-start.53 = (bf16[512,768]{1,0:T(8,128)(2,1)}, bf16[512,768]{1,0:T(8,128)(2,1)S(1)}, u32[]{:S(2)}, u32[]{:S(2)}) collective-permute-start(bf16[512,768]{1,0:T(8,128)(2,1)} %reduce-scatter.3.cloned.1.call-done), channel_id=1, source_target_pairs={{0,8},{4,12},{8,0},{12,4},{16,24},{20,28},{24,16},{28,20},{1,9},{5... | collective-permute-start | bytes 2359304 | tf_op jit(solution)/shard_map/ppermute | solution.py:318
  667.0 38.3 %collective-permute-start.55 = (bf16[512,512]{1,0:T(8,128)(2,1)}, bf16[512,512]{1,0:T(8,128)(2,1)}, u32[]{:S(2)}, u32[]{:S(2)}) collective-permute-start(bf16[512,512]{1,0:T(8,128)(2,1)} %get-tuple-element.2612), channel_id=1, source_target_pairs={{4,0},{12,8},{20,16},{28,24},{5,1},{13,9},{21,17},{29,25},{6,2},{1... | collective-permute-start | bytes 1572872 | tf_op jit(solution)/shard_map/ppermute | solution.py:1158
  668.2 37.0 %collective-permute-start.56 = (bf16[512,512]{1,0:T(8,128)(2,1)}, bf16[512,512]{1,0:T(8,128)(2,1)}, u32[]{:S(2)}, u32[]{:S(2)}) collective-permute-start(bf16[512,512]{1,0:T(8,128)(2,1)} %get-tuple-element.2616), channel_id=1, source_target_pairs={{4,0},{12,8},{20,16},{28,24},{5,1},{13,9},{21,17},{29,25},{6,2},{1... | collective-permute-start | bytes 1572872 | tf_op jit(solution)/shard_map/ppermute | solution.py:1158
  714.5 34.0 %collective-permute-start.64 = (bf16[256,2048]{1,0:T(8,128)(2,1)S(1)}, bf16[256,2048]{1,0:T(8,128)(2,1)}, u32[]{:S(2)}, u32[]{:S(2)}) collective-permute-start(bf16[256,2048]{1,0:T(8,128)(2,1)S(1)} %get-tuple-element.3056), channel_id=1, source_target_pairs={{0,0},{1,1},{4,2},{5,3},{2,4},{3,5},{6,6},{7,7},{8,8},{9,9},{12,10... | collective-permute-start | bytes 3145736 | tf_op jit(solution)/shard_map/ppermute | solution.py:395
  756.4 48.2 %collective-permute-start.65 = (bf16[2048,1024]{1,0:T(8,128)(2,1)}, bf16[2048,1024]{1,0:T(8,128)(2,1)S(1)}, u32[]{:S(2)}, u32[]{:S(2)}) collective-permute-start(bf16[2048,1024]{1,0:T(8,128)(2,1)} %row_outer.20), channel_id=1, source_target_pairs={{0,4},{4,0},{8,12},{12,8},{16,20},{20,16},{24,28},{28,24},{1,5},{5... | collective-permute-start | bytes 12582920 | tf_op jit(solution)/shard_map/ppermute | solution.py:318
  759.7 44.9 %collective-permute-start.69 = (bf16[256,2048]{1,0:T(8,128)(2,1)}, bf16[256,2048]{1,0:T(8,128)(2,1)}, u32[]{:S(2)}, u32[]{:S(2)}) collective-permute-start(bf16[256,2048]{1,0:T(8,128)(2,1)} %get-tuple-element.3055), channel_id=1, source_target_pairs={{1,0},{0,1},{5,2},{4,3},{3,4},{2,5},{7,6},{6,7},{9,8},{8,9},{13,10... | collective-permute-start | bytes 3145736 | tf_op jit(solution)/shard_map/ppermute | solution.py:395
  759.7 44.9 %collective-permute-start.68 = (bf16[512,1536]{1,0:T(8,128)(2,1)}, bf16[512,1536]{1,0:T(8,128)(2,1)S(1)}, u32[]{:S(2)}, u32[]{:S(2)}) collective-permute-start(bf16[512,1536]{1,0:T(8,128)(2,1)} %reduce-scatter.5.cloned.1.call-done), channel_id=1, source_target_pairs={{0,16},{4,20},{8,24},{12,28},{16,0},{20,4},{24,8},{28,12},{1,17},{... | collective-permute-start | bytes 4718600 | tf_op jit(solution)/shard_map/ppermute | solution.py:318
  761.1 43.4 %collective-permute-start.67 = (bf16[512,1536]{1,0:T(8,128)(2,1)}, bf16[512,1536]{1,0:T(8,128)(2,1)}, u32[]{:S(2)}, u32[]{:S(2)}) collective-permute-start(bf16[512,1536]{1,0:T(8,128)(2,1)} %reduce-scatter.5.cloned.1.call-done), channel_id=1, source_target_pairs={{0,8},{4,12},{8,0},{12,4},{16,24},{20,28},{24,16},{28,20},{1,9},{5... | collective-permute-start | bytes 4718600 | tf_op jit(solution)/shard_map/ppermute | solution.py:318
  768.1 36.5 %collective-permute-start.66 = (bf16[2048,768]{1,0:T(8,128)(2,1)}, bf16[2048,768]{1,0:T(8,128)(2,1)}, u32[]{:S(2)}, u32[]{:S(2)}) collective-permute-start(bf16[2048,768]{1,0:T(8,128)(2,1)} %constant_dynamic-update-slice_fusion.6.own_ref), channel_id=1, source_target_pairs={{0,4},{4,0},{8,12},{12,8},{16,20},{20,16},{24,28},{28,24},{1,5},{5... | collective-permute-start | bytes 9437192 | tf_op jit(solution)/shard_map/ppermute | solution.py:318
  868.4 33.1 %collective-permute-start.82 = (bf16[1024,512]{1,0:T(8,128)(2,1)}, bf16[1024,512]{1,0:T(8,128)(2,1)S(1)}, u32[]{:S(2)}, u32[]{:S(2)}) collective-permute-start(bf16[1024,512]{1,0:T(8,128)(2,1)} %get-tuple-element.2898), channel_id=1, source_target_pairs={{0,8},{4,12},{8,0},{12,4},{16,24},{20,28},{24,16},{28,20},{1,9},{5... | collective-permute-start | bytes 3145736 | tf_op jit(solution)/shard_map/ppermute | solution.py:318
  869.0 32.5 %collective-permute-start.83 = (bf16[1024,512]{1,0:T(8,128)(2,1)}, bf16[1024,512]{1,0:T(8,128)(2,1)S(1)}, u32[]{:S(2)}, u32[]{:S(2)}) collective-permute-start(bf16[1024,512]{1,0:T(8,128)(2,1)} %get-tuple-element.2901), channel_id=1, source_target_pairs={{0,16},{4,20},{8,24},{12,28},{16,0},{20,4},{24,8},{28,12},{1,17},{... | collective-permute-start | bytes 3145736 | tf_op jit(solution)/shard_map/ppermute | solution.py:318
  (208 other events, 2638.4 us)
Sparse Core Ops, SparseCore 0:
  60.7 38.0 all-gather.2
  199.9 167.6 all-gather.4
  540.4 60.0 reduce-scatter.2
  627.0 115.5 reduce-scatter.4

commit v12 on v9

--- a/solution.py
+++ b/solution.py
@@ -379,16 +379,13 @@
     )
 
 
-def to_sequences_send(x):
+def sequence_cuts(x):
     odd = lax.axis_index("shard") & 1
-    return [
-        lax.ppermute(
-            lax.dynamic_index_in_dim(x, turn ^ odd, 0, keepdims=False),
-            ("rep", "shard"),
-            sequence_pairs(turn),
-        )
-        for turn in range(2)
-    ]
+    return [lax.dynamic_index_in_dim(x, turn ^ odd, 0, keepdims=False) for turn in range(2)]
+
+
+def to_sequence(cut, turn):
+    return lax.ppermute(cut, ("rep", "shard"), sequence_pairs(turn))
 
 
 def from_sequences_send(x):
@@ -416,8 +413,8 @@
     )
 
 
-def whole_columns(me, own, other, widths):
-    rows, columns = own.shape[0] // 4, own.shape[1]
+def whole_columns(me, own, other, widths, part=0):
+    rows, columns = own.shape[0] // 4, sum(widths)
 
     def body(me_ref, own_ref, other_ref, *outs):
         def put(block):
@@ -430,7 +427,7 @@
         pl.when(mine)(lambda: put(own_ref))
         pl.when(jnp.logical_not(mine))(lambda: put(other_ref))
 
-    spec = pl.BlockSpec((rows, columns), lambda i, at: ((at[0] ^ i) >> 1, 0))
+    spec = pl.BlockSpec((rows, columns), lambda i, at: ((at[0] ^ i) >> 1, part))
     return pl.pallas_call(
         body,
         grid_spec=pltpu.PrefetchScalarGridSpec(
@@ -885,7 +882,6 @@
     count = lax.axis_size("rep")
 
     s = Stage()
-    s.cotangent = cotangent
     piece = width // shards
 
     s.own_blocks = [
@@ -895,7 +891,7 @@
         [jnp.stack([attn_gain, mlp_gain]), jnp.zeros((14, piece), low)], 0
     )
     travelling = jnp.concatenate([s.own_blocks[0], gain_rows], 0)
-    s.tokens = tokens
+    s.tokens_cuts, s.cotangent_cuts = sequence_cuts(tokens), sequence_cuts(cotangent)
     s.out_block = column_block((w_out,), me)
     s.ffn_block = column_block((w_gate, w_up, w_down), me)
     s.before, s.behind = around(travelling, 1), around(travelling, -1)
@@ -903,9 +899,9 @@
     s.end()
 
     s.ahead = around(s.before, 1)
-    tokens_sent = to_sequences_send(s.tokens)
+    tokens_sent = [to_sequence(cut, turn) for turn, cut in enumerate(s.tokens_cuts)]
     out_own = lax.all_gather(s.out_block, "shard", axis=0, tiled=True)
-    del s.out_block, s.tokens
+    del s.out_block, s.tokens_cuts
     s.end()
 
     parts = (s.before, s.ahead, s.behind)
@@ -917,7 +913,7 @@
     del s.before, s.behind, s.ahead
     s.end()
 
-    grad_y_sent = to_sequences_send(s.cotangent)
+    grad_y_sent = [to_sequence(cut, turn) for turn, cut in enumerate(s.cotangent_cuts)]
     s.came_far = far(*s.came_near)
     s.came_other = [s.came_own, *(across(block, CORE) for block in s.came_near)]
     gains = rolled(s.gains.astype(full))
@@ -944,7 +940,7 @@
     s.cosine, sine = cosine[0, :, 0], sine[0, :, 0]
     s.sine = jnp.concatenate([-sine[:, : head_dim // 2], sine[:, head_dim // 2 :]], 1)
     s.out_own = out_own
-    del s.gains, s.x_came, s.other_lengths, s.cotangent, s.came_own
+    del s.gains, s.x_came, s.other_lengths, s.cotangent_cuts, s.came_own
     s.end()
 
     head_columns = 2 * head_dim
@@ -1026,6 +1022,9 @@
     s.mixed = [a[0] for a in s.attended]
     s.resid, s.mid = close_attention(s.x_low, s.mixed, s.out_blocks, s.mlp_gains)
     s.grad_y_far = far(*s.grad_y_near)
+    s.came = [s.came, *s.came_near, s.came_last[0]]
+    s.came_other = [*s.came_other, s.came_last[1]]
+    del s.came_near, s.came_last
     del s.out_own, s.out_own_other, s.out_near, s.out_near_other, s.out_last
     del s.projected_last, s.earlier_last
     s.end()
@@ -1188,8 +1187,6 @@
 
     s.down_near = near(s.down_total)
     give_back(1, 2)
-    mlp_out = total(s.mlp_came, s.mlp_came_far, by_rows(s.mlp_rest[1]), by_rows)
-    s.output = (s.valid * (s.resid + mlp_out)).astype(low)
     s.out_head, s.out_tail, back, finished = in_order(
         [
             head_call(s.resid_rolled, s.mixed, s.out_came, 0),
@@ -1200,52 +1197,48 @@
     )
     s.backs = s.backs | {0: back}
     s.finished = {3: finished}
-    del s.mlp_came, s.mlp_came_far, s.mlp_rest, s.out_came, s.resid
+    del s.out_came
     s.end()
 
     s.out_near = send_near((s.out_head[0], s.out_tail[0]))
-    s.down_far = far(*s.down_near)
+    mlp_out = total(s.mlp_came, s.mlp_came_far, by_rows(s.mlp_rest[1]), by_rows)
+    s.output = (s.valid * (s.resid + mlp_out)).astype(low)
     give_back(0)
     finished1, finished2 = in_order([finish_call(1), finish_call(2)])
     s.finished = s.finished | {1: finished1, 2: finished2}
-    s.gate_up_total = gate_up_total
-    s.end()
-
-    def odd_half(half):
-        return odd_call(s.normed, [s.finished[i][1] for i in range(4)], half)
-
+    del s.mlp_came, s.mlp_came_far, s.mlp_rest, s.resid
+    s.end()
+
+    output_sent = from_sequences_send(s.output)
     s.out_far = send_far(s.out_near, (s.out_tail[1], s.out_head[1]), by_columns)
-    s.down_spread = jnp.concatenate([s.down_total, *s.down_near, *s.down_far], 0)
-    s.down_spread_other = across(s.down_spread, CORE)
+    s.down_far = far(*s.down_near)
     (finished,) = in_order([finish_call(0)])
     s.finished = s.finished | {0: finished}
-    (s.odd0,) = in_order([odd_half(0)])
-    del s.down_total, s.down_near, s.down_far
+    (s.odd,) = in_order([odd_call(s.normed, [s.finished[i][1] for i in range(4)])])
+    s.gate_up_total = gate_up_total
+    s.output_first = output_sent[0]
+    del s.output
     s.end()
 
     my_group = me.astype(jnp.int32)[None]
 
-    def whole_call(widths, own, other):
-        return lambda first: whole_columns(my_group, first, other, widths), own
+    def whole_call(widths, own, other, part=0):
+        return lambda first: whole_columns(my_group, first, other, widths, part), own
 
     s.gate_up_near = near(s.gate_up_total)
-    s.came0 = across(s.odd0, CORE)
+    s.qkv_came = across(s.odd, CORE)
     out_sum = total(s.out_near, s.out_far, (s.out_head[2], s.out_tail[2]), by_columns)
     s.out_chunks = jnp.split(out_sum.astype(low), shards, 0)
     s.out_ring = ring_sum_first(s.out_chunks)
     weights = [
         pair
-        for i, block in enumerate(zip((s.came, *s.came_near), s.came_other))
-        for pair in ((s.own_blocks[2 * i], block[0]), (s.own_blocks[2 * i + 1], block[1]))
-    ] + [(s.own_blocks[6 + i], s.came_last[i]) for i in range(2)]
+        for i in range(4)
+        for pair in (
+            (s.own_blocks[2 * i], s.came[i]), (s.own_blocks[2 * i + 1], s.came_other[i])
+        )
+    ]
     blocks = [part for i in range(4) for part in s.finished[i][:2]]
-    s.odd1, grad_in = in_order(
-        [
-            odd_half(1),
-            (lambda first: back_to_rows([first, *blocks[1:]], weights), blocks[0]),
-        ]
-    )
-    grad_in = rolled(grad_in)
+    grad_in = rolled(back_to_rows(blocks, weights))
     x_unit = s.x_low.astype(full) * s.inverse_in
     s.gain_parts = jnp.concatenate(
         [
@@ -1258,19 +1251,25 @@
     s.grad_tokens = (
         s.grad_resid + norm_back(x_unit, s.inverse_in, grad_in * s.attn_gains)
     ).astype(low)
-    del s.odd0, s.out_near, s.out_far, s.out_head, s.out_tail, s.backs
-    del s.own_blocks, s.came, s.came_near, s.came_other, s.came_last, s.grad_resid, s.x_low
-    s.end()
-
-    def halves_call(half, came):
-        even = [s.finished[i][0] for i in range(4)]
-        return [call(s.normed, even, came, half) for call in (head_call, tail_call)]
-
-    output_sent = from_sequences_send(s.output)
-    s.came1 = across(s.odd1, CORE)
+    del s.odd, s.out_near, s.out_far, s.out_head, s.out_tail, s.backs
+    del s.own_blocks, s.came, s.came_other, s.grad_resid, s.x_low
+    s.end()
+
+    even = [s.finished[i][0] for i in range(4)]
+    s.head0, s.tail0, s.head1, s.tail1 = in_order(
+        [
+            call(s.normed, even, s.qkv_came, half, range(half, 8, 2))
+            for half in range(2)
+            for call in (head_call, tail_call)
+        ]
+    )
+    tokens_sent = from_sequences_send(s.grad_tokens)
+    s.down_spread = jnp.concatenate([s.down_total, *s.down_near, *s.down_far], 0)
+    s.down_spread_other = across(s.down_spread, CORE)
+    s.output_second = output_sent[1]
     s.out_ring_last = around(rounded_sum(s.out_chunks[3], s.out_ring[0]), 1)
-    s.head0, s.tail0 = in_order(halves_call(0, s.came0))
-    del s.odd1, s.came0
+    s.gate_up_far = far(*s.gate_up_near)
+    del s.qkv_came, s.finished, s.down_total, s.down_near, s.down_far
     s.end()
 
     def qkv_chunks(came, came_far, head, tail):
@@ -1278,35 +1277,34 @@
         return jnp.split(own.astype(low), shards, 0)
 
     s.near0 = send_near((s.head0[0], s.tail0[0]))
-    s.gain_came = across(s.gain_parts, CORE)
-    s.head1, s.tail1, s.whole_down = in_order(
-        [*halves_call(1, s.came1), whole_call((units,), s.down_spread, s.down_spread_other)]
-    )
+    s.gate_up_own = jnp.concatenate([s.gate_up_total, *s.gate_up_near, *s.gate_up_far], 0)
+    s.gate_up_other = across(s.gate_up_own, CORE)
+    (s.whole_down,) = in_order([whole_call((units,), s.down_spread, s.down_spread_other)])
     s.out_total = rounded_sum(s.out_chunks[0], s.out_ring[1], s.out_ring_last)
-    s.output_came = output_sent
-    del s.came1, s.down_spread, s.down_spread_other, s.output, s.finished
-    del s.out_chunks, s.out_ring, s.out_ring_last
-    s.end()
-
-    tokens_sent = from_sequences_send(s.grad_tokens)
+    s.tokens_first = tokens_sent[0]
+    del s.down_spread, s.down_spread_other, s.out_chunks, s.out_ring, s.out_ring_last
+    del s.gate_up_near, s.gate_up_far, s.gate_up_total
+    s.end()
+
     s.far0 = send_far(s.near0, (s.tail0[1], s.head0[1]), by_columns)
     s.near1 = send_near((s.head1[0], s.tail1[0]))
-    s.gain_parts = s.gain_parts + s.gain_came
-    s.tokens_first = tokens_sent[0]
+    (s.whole_gate_up,) = in_order([whole_call((units, units), s.gate_up_own, s.gate_up_other)])
+    s.tokens_second = tokens_sent[1]
+    del s.gate_up_own, s.gate_up_other, s.grad_tokens
     s.end()
 
     s.chunks0 = qkv_chunks(s.near0, s.far0, s.head0, s.tail0)
     s.ring0 = ring_sum_first(s.chunks0)
     s.far1 = send_far(s.near1, (s.tail1[1], s.head1[1]), by_columns)
-    s.gain_came = across(s.gain_parts, ACROSS_X)
+    s.gain_came = across(s.gain_parts, CORE)
     del s.near0, s.far0, s.head0, s.tail0
     s.end()
 
     s.last0 = around(rounded_sum(s.chunks0[3], s.ring0[0]), 1)
     s.chunks1 = qkv_chunks(s.near1, s.far1, s.head1, s.tail1)
     s.ring1 = ring_sum_first(s.chunks1)
-    s.gate_up_far = far(*s.gate_up_near)
     s.gain_parts = s.gain_parts + s.gain_came
+    s.gain_came = across(s.gain_parts, ACROSS_X)
     del s.near1, s.far1, s.head1, s.tail1
     s.end()
 
@@ -1314,10 +1312,9 @@
     s.total0 = jnp.concatenate([query_total, s.out_total], 1)
     s.spread0 = near(s.total0)
     s.last1 = around(rounded_sum(s.chunks1[3], s.ring1[0]), 1)
-    s.gate_up_own = jnp.concatenate([s.gate_up_total, *s.gate_up_near, *s.gate_up_far], 0)
-    s.gate_up_other = across(s.gate_up_own, CORE)
+    s.gain_parts = s.gain_parts + s.gain_came
     s.gain_came = across(s.gain_parts, ACROSS_Y)
-    del s.chunks0, s.ring0, s.last0, s.out_total, s.gate_up_near, s.gate_up_far, s.gate_up_total
+    del s.chunks0, s.ring0, s.last0, s.out_total
     s.end()
 
     s.spread_far0 = far(*s.spread0)
@@ -1325,8 +1322,7 @@
     s.spread1 = near(s.total1)
     s.gain_parts = s.gain_parts + s.gain_came
     s.gain_came = lax.ppermute(s.gain_parts, "shard", [(i, i ^ 1) for i in range(shards)])
-    (s.whole_gate_up,) = in_order([whole_call((units, units), s.gate_up_own, s.gate_up_other)])
-    del s.chunks1, s.ring1, s.last1, s.gate_up_own, s.gate_up_other
+    del s.chunks1, s.ring1, s.last1
     s.end()
 
     s.own0 = jnp.concatenate([s.total0, *s.spread0, *s.spread_far0], 0)
@@ -1352,8 +1348,8 @@
         [whole_call((head_dim, head_dim), s.own1, s.other1)]
     )
     return (
-        jnp.stack(in_turn(s.output_came)),
-        jnp.stack(in_turn([s.tokens_first, tokens_sent[1]])),
+        jnp.stack(in_turn([s.output_first, s.output_second])),
+        jnp.stack(in_turn([s.tokens_first, s.tokens_second])),
         s.wide[0],
         s.whole0[0],
         whole_key,

time: 1000 us -> 989 us (0.989)
  waiting for transfers between devices: 243 us -> 277 us
  starting transfers between devices: 165 us -> 133 us
    ppermute x4, waiting for transfers between devices: 21.4 us -> 51.7 us  [to_sequence(): return lax.ppermute(cut, ('rep', 'shard'), sequence_pairs(turn))]
    ppermute x74 -> x73, starting transfers between devices: 95.3 us -> 68.7 us  [across(): return lax.ppermute(x, 'rep', [(i, i ^ mask) for i in range(count)])]
    ppermute x4, waiting for transfers between devices: 16.1 us -> 0.01 us  [from_sequences_send(): lax.ppermute(lax.dynamic_index_in_dim(x, turn ^ odd, 0, keepdims=False),...]
    ppermute x4, starting transfers between devices: 11.8 us -> 24.2 us  [to_sequence(): return lax.ppermute(cut, ('rep', 'shard'), sequence_pairs(turn))]
    ppermute x12, starting transfers between devices: 37.2 us -> 24.9 us  [around(): lax.ppermute(x, 'shard', [(i, (i + by) % count) for i in range(count)])]
    pallas_call x13 -> x12, Pallas kernels: 120 us -> 114 us  [row_outer(): pl.pallas_call(body, grid=(tiles,), out_shape=[jax.ShapeDtypeStruct((tile...]
    unnamed x252 -> x272, local copies, waits for them, and re-layouts: 28.7 us -> 27.8 us
    ppermute x74 -> x73, waiting for transfers between devices: 159 us -> 160 us  [across(): return lax.ppermute(x, 'rep', [(i, i ^ mask) for i in range(count)])]
  transfers between devices with their start and end apart: 108 -> 107, of which waited for: 31 -> 41; matrix products, arithmetic and copies ran while one was open for 10% -> 9% of each run, Pallas kernels for 38% -> 38%
where the time goes in v12:
time: 989 us; the launch traced here: 980 us
  Pallas kernels  425 us (43%)
  waiting for transfers between devices  277 us (28%)
  starting transfers between devices  133 us (13%)
  local copies, waits for them, and re-layouts  65.3 us (7%)
  other arithmetic  64 us (6%)
  between operations  16.1 us (2%)
    ppermute x73, waiting for transfers between devices, across(): return lax.ppermute(x, 'rep', [(i, i ^ mask) for i in range(count)])  160 us
    pallas_call x16, Pallas kernels, call(): pl.pallas_call(body, grid=(1,), out_shape=outs, in_specs=in_specs, out_sp...  119 us
    pallas_call x12, Pallas kernels, row_outer(): pl.pallas_call(body, grid=(tiles,), out_shape=[jax.ShapeDtypeStruct((tile...  114 us
    ppermute x73, starting transfers between devices, across(): return lax.ppermute(x, 'rep', [(i, i ^ mask) for i in range(count)])  68.7 us
    pallas_call x2, Pallas kernels, hidden_units(): pl.pallas_call(body, grid=(3,), out_shape=[jax.ShapeDtypeStruct((rows, un...  60.1 us
    pallas_call x4, Pallas kernels, from_hidden(): pl.pallas_call(body, grid=(4,), out_shape=[jax.ShapeDtypeStruct((2 * rows...  59.3 us
    ppermute x4, waiting for transfers between devices, to_sequence(): return lax.ppermute(cut, ('rep', 'shard'), sequence_pairs(turn))  51.7 us
    ppermute x12, waiting for transfers between devices, around(): lax.ppermute(x, 'shard', [(i, (i + by) % count) for i in range(count)])  46.9 us
  transfers between devices with their start and end apart: 107, of which 41 were waited for; matrix products, arithmetic and copies ran while one was open for 9% of the time, Pallas kernels for 38%

profile of v12, /device:TPU:0, one launch (start us, length us, event | category | flops | bytes accessed | tf_op | source)
XLA Modules:
  0.0 980.4 jit_solution(9965330100161031134)
XLA Ops:
  33.1 10.3 %collective-permute-done = bf16[528,512]{1,0:T(8,128)(2,1)} collective-permute-done((bf16[528,512]{1,0:T(8,128)(2,1)}, bf16[528,512]{1,0:T(8,128)(2,1)}, u32[]{:S(2)}, u32[]{:S(2)}) %collective-permute-start) | collective-permute-done | bytes 540704 | tf_op jit(solution)/shard_map/ppermute | solution.py:323
  45.1 13.5 %collective-permute-done.3 = bf16[528,512]{1,0:T(8,128)(2,1)S(1)} collective-permute-done((bf16[528,512]{1,0:T(8,128)(2,1)}, bf16[528,512]{1,0:T(8,128)(2,1)S(1)}, u32[]{:S(2)}, u32[]{:S(2)}) %collective-permute-start.3) | collective-permute-done | bytes 540704 | tf_op jit(solution)/shard_map/ppermute | solution.py:323
  64.9 9.5 collective-permute-start.7
  78.8 48.8 %collective-permute-done.8 = bf16[256,2048]{1,0:T(8,128)(2,1)} collective-permute-done((bf16[256,2048]{1,0:T(8,128)(2,1)S(1)}, bf16[256,2048]{1,0:T(8,128)(2,1)}, u32[]{:S(2)}, u32[]{:S(2)}) %collective-permute-start.8) | collective-permute-done | bytes 1048608 | tf_op jit(solution)/shard_map/ppermute | solution.py:388
  134.5 9.6 collective-permute-start.14
  245.3 13.6 %collective-permute-done.28.refs_7_.refs_2_ = bf16[512,2048]{1,0:T(8,128)(2,1)S(1)} collective-permute-done((bf16[512,2048]{1,0:T(8,128)(2,1)S(1)}, bf16[512,2048]{1,0:T(8,128)(2,1)S(1)}, u32[]{:S(2)}, u32[]{:S(2)}) %collective-permute-start.28) | collective-permute-done | bytes 2097184 | tf_op jit(solution)/shard_map/ppermute | solution.py:318
  269.3 11.7 %close_attention.1 = (f32[512,2048]{1,0:T(8,128)}, bf16[512,2048]{1,0:T(8,128)(2,1)}) custom-call(bf16[512,2048]{1,0:T(8,128)(2,1)} %pad_maximum_fusion.3.x, bf16[512,512]{1,0:T(8,128)(2,1)} %get-tuple-element.2435.refs_0_.refs_1_.refs_4_, bf16[512,512]{1,0:T(8,128)(2,1)} %get-tuple-element.2432.refs_1_.refs_2_.refs_3_, ...), custom_call_target="tpu_custom_call" | custom-call | flops 1 | bytes 1 | tf_op jit(solution)/shard_map/close_attention/pallas_call | solution.py:789
  289.4 42.8 %collective-permute-done.33.refs_2_ = bf16[512,2048]{1,0:T(8,128)(2,1)S(1)} collective-permute-done((bf16[512,2048]{1,0:T(8,128)(2,1)}, bf16[512,2048]{1,0:T(8,128)(2,1)S(1)}, u32[]{:S(2)}, u32[]{:S(2)}) %collective-permute-start.33) | collective-permute-done | bytes 2097184 | tf_op jit(solution)/shard_map/ppermute | solution.py:318
  336.5 19.9 %collective-permute-done.35.refs_4_ = bf16[256,2048]{1,0:T(8,128)(2,1)S(1)} collective-permute-done((bf16[256,2048]{1,0:T(8,128)(2,1)S(1)}, bf16[256,2048]{1,0:T(8,128)(2,1)S(1)}, u32[]{:S(2)}, u32[]{:S(2)}) %collective-permute-start.35) | collective-permute-done | bytes 1048608 | tf_op jit(solution)/shard_map/ppermute | solution.py:318
  356.8 9.8 all-gather.5.cloned.1.call-done.refs_10_.refs_11_.refs_12_.refs_4_.refs_9_
  366.6 30.0 %hidden_units.2 = (bf16[2048,768]{1,0:T(8,128)(2,1)}, bf16[2048,768]{1,0:T(8,128)(2,1)}, bf16[2048,768]{1,0:T(8,128)(2,1)}) custom-call(bf16[512,2048]{1,0:T(8,128)(2,1)} %get-tuple-element.2307.refs_0_, bf16[512,2048]{1,0:T(8,128)(2,1)} %copy-done.12, bf16[512,2048]{1,0:T(8,128)(2,1)} %copy-done.11, bf16[256,2048]{1,0:T(8,128)(2,1)} %copy-done.21, ...), custom_call_target="tpu_custom_call" | custom-call | flops 1 | bytes 1 | tf_op jit(solution)/shard_map/hidden_units/pallas_call | solution.py:656
  396.6 30.1 %hidden_units.3 = (bf16[2048,768]{1,0:T(8,128)(2,1)}, bf16[2048,768]{1,0:T(8,128)(2,1)}, bf16[2048,768]{1,0:T(8,128)(2,1)}) custom-call(bf16[512,2048]{1,0:T(8,128)(2,1)} %get-tuple-element.2307.refs_0_, bf16[512,2048]{1,0:T(8,128)(2,1)} %copy-done.12, bf16[512,2048]{1,0:T(8,128)(2,1)} %copy-done.11, bf16[256,2048]{1,0:T(8,128)(2,1)} %copy-done.21, ...), custom_call_target="tpu_custom_call" | custom-call | flops 1 | bytes 1 | tf_op jit(solution)/shard_map/hidden_units/pallas_call | solution.py:656
  426.7 12.6 %row_outer.12 = bf16[2048,768]{1,0:T(8,128)(2,1)} custom-call(bf16[512,2048]{1,0:T(8,128)(2,1)} %copy-done.6, bf16[512,2048]{1,0:T(8,128)(2,1)} %copy-done.14, bf16[512,2048]{1,0:T(8,128)(2,1)} %copy-done.13, bf16[256,2048]{1,0:T(8,128)(2,1)} %copy-done.23, bf16[256,2048]{1,0:T(8,128)(2,1)} %copy-done.22, ...), custom_call_target="tpu_custom_call" | custom-call | flops 6442450944 | bytes 11534336 | tf_op jit(solution)/shard_map/row_outer/pallas_call | solution.py:739
  439.8 18.9 %from_hidden.4 = (bf16[512,2048]{1,0:T(8,128)(2,1)}, bf16[512,2048]{1,0:T(8,128)(2,1)}) custom-call(bf16[2048,768]{1,0:T(8,128)(2,1)} %get-tuple-element.2318.refs_0_.refs_1_.refs_2_.refs_3_.refs_5_, bf16[2048,768]{1,0:T(8,128)(2,1)} %get-tuple-element.2318.refs_0_.refs_1_.refs_2_.refs_3_.refs_5_, ...), custom_call_target="tpu_custom_call" | custom-call | flops 1 | bytes 1 | tf_op jit(solution)/shard_map/from_hidden/pallas_call | solution.py:695
  461.7 13.2 %row_outer.13 = bf16[2048,768]{1,0:T(8,128)(2,1)} custom-call(bf16[512,2048]{1,0:T(8,128)(2,1)} %copy-done.6, bf16[512,2048]{1,0:T(8,128)(2,1)} %copy-done.14, bf16[512,2048]{1,0:T(8,128)(2,1)} %copy-done.13, bf16[256,2048]{1,0:T(8,128)(2,1)} %copy-done.23, bf16[256,2048]{1,0:T(8,128)(2,1)} %copy-done.22, ...), custom_call_target="tpu_custom_call" | custom-call | flops 6442450944 | bytes 11534336 | tf_op jit(solution)/shard_map/row_outer/pallas_call | solution.py:739
  474.9 18.8 %from_hidden.5 = (bf16[512,2048]{1,0:T(8,128)(2,1)}, bf16[512,2048]{1,0:T(8,128)(2,1)}) custom-call(bf16[2048,768]{1,0:T(8,128)(2,1)} %get-tuple-element.2318.refs_0_.refs_1_.refs_2_.refs_3_.refs_5_, bf16[2048,768]{1,0:T(8,128)(2,1)} %get-tuple-element.2318.refs_0_.refs_1_.refs_2_.refs_3_.refs_5_, ...), custom_call_target="tpu_custom_call" | custom-call | flops 1 | bytes 1 | tf_op jit(solution)/shard_map/from_hidden/pallas_call | solution.py:695
  493.7 19.5 %row_outer.14 = bf16[2048,1536]{1,0:T(8,128)(2,1)} custom-call(bf16[512,2048]{1,0:T(8,128)(2,1)} %get-tuple-element.2307.refs_0_, bf16[512,2048]{1,0:T(8,128)(2,1)} %copy-done.12, bf16[512,2048]{1,0:T(8,128)(2,1)} %copy-done.11, bf16[256,2048]{1,0:T(8,128)(2,1)} %copy-done.21, bf16[256,2048]{1,0:T(8,128)(2,1)} %copy-done.20, ...), custom_call_target="tpu_custom_call" | custom-call | flops 12884901888 | bytes 14680064 | tf_op jit(solution)/shard_map/row_outer/pallas_call | solution.py:739
  520.2 10.7 %from_hidden.6 = (bf16[512,2048]{1,0:T(8,128)(2,1)}, bf16[512,2048]{1,0:T(8,128)(2,1)}) custom-call(bf16[2048,768]{1,0:T(8,128)(2,1)} %get-tuple-element.2227.refs_5_.refs_0_.refs_1_.refs_2_.refs_3_, bf16[2048,768]{1,0:T(8,128)(2,1)} %get-tuple-element.2227.refs_5_.refs_0_.refs_1_.refs_2_.refs_3_, ...), custom_call_target="tpu_custom_call" | custom-call | flops 1 | bytes 1 | tf_op jit(solution)/shard_map/from_hidden/pallas_call | solution.py:695
  530.9 10.9 %from_hidden.7 = (bf16[512,2048]{1,0:T(8,128)(2,1)}, bf16[512,2048]{1,0:T(8,128)(2,1)}) custom-call(bf16[2048,768]{1,0:T(8,128)(2,1)} %get-tuple-element.2227.refs_5_.refs_0_.refs_1_.refs_2_.refs_3_, bf16[2048,768]{1,0:T(8,128)(2,1)} %get-tuple-element.2227.refs_5_.refs_0_.refs_1_.refs_2_.refs_3_, ...), custom_call_target="tpu_custom_call" | custom-call | flops 1 | bytes 1 | tf_op jit(solution)/shard_map/from_hidden/pallas_call | solution.py:695
  556.2 13.4 %attend_back.4 = (bf16[512,512]{1,0:T(8,128)(2,1)}, f32[512,512]{1,0:T(8,128)}, bf16[512,512]{1,0:T(8,128)(2,1)}, f32[1,128]{1,0:T(1,128)}) custom-call(s32[2]{0:T(128)} %pad_add_fusion.info, bf16[512,512]{1,0:T(8,128)(2,1)} %get-tuple-element.2274.query, bf16[512,512]{1,0:T(8,128)(2,1)} %copy-done.41, bf16[512,512]{1,0:T(8,128)(2,1)} %get-tuple-element.2276.own, ...), custom_call_target="tpu_custom_call" | custom-call | flops 1 | bytes 1 | tf_op jit(solution)/shard_map/attend_back/pallas_call | solution.py:616
  579.7 19.7 %row_outer.16 = bf16[2048,1536]{1,0:T(8,128)(2,1)} custom-call(bf16[512,2048]{1,0:T(8,128)(2,1)} %get-tuple-element.2307.refs_0_, bf16[512,2048]{1,0:T(8,128)(2,1)} %copy-done.12, bf16[512,2048]{1,0:T(8,128)(2,1)} %copy-done.11, bf16[256,2048]{1,0:T(8,128)(2,1)} %copy-done.21, bf16[256,2048]{1,0:T(8,128)(2,1)} %copy-done.20, ...), custom_call_target="tpu_custom_call" | custom-call | flops 12884901888 | bytes 14680064 | tf_op jit(solution)/shard_map/row_outer/pallas_call | solution.py:739
  608.4 13.2 %attend_back.5 = (bf16[512,512]{1,0:T(8,128)(2,1)}, f32[512,512]{1,0:T(8,128)}, bf16[512,512]{1,0:T(8,128)(2,1)}, f32[1,128]{1,0:T(1,128)}) custom-call(s32[2]{0:T(128)} %pad_add_fusion.info, bf16[512,512]{1,0:T(8,128)(2,1)} %get-tuple-element.2357.query, bf16[512,512]{1,0:T(8,128)(2,1)} %copy-done.40, bf16[512,512]{1,0:T(8,128)(2,1)} %get-tuple-element.2359.own, ...), custom_call_target="tpu_custom_call" | custom-call | flops 1 | bytes 1 | tf_op jit(solution)/shard_map/attend_back/pallas_call | solution.py:616
  621.5 13.6 %attend_back.6 = (bf16[512,512]{1,0:T(8,128)(2,1)}, f32[512,512]{1,0:T(8,128)}, bf16[512,512]{1,0:T(8,128)(2,1)}, f32[1,128]{1,0:T(1,128)}) custom-call(s32[2]{0:T(128)} %pad_add_fusion.info, bf16[512,512]{1,0:T(8,128)(2,1)} %get-tuple-element.2372.query, bf16[512,512]{1,0:T(8,128)(2,1)} %collective-permute-done.21.before, ...), custom_call_target="tpu_custom_call" | custom-call | flops 1 | bytes 1 | tf_op jit(solution)/shard_map/attend_back/pallas_call | solution.py:616
  652.9 13.3 %attend_back.7 = (bf16[512,512]{1,0:T(8,128)(2,1)}, f32[512,512]{1,0:T(8,128)}, bf16[512,512]{1,0:T(8,128)(2,1)}, f32[1,128]{1,0:T(1,128)}) custom-call(s32[2]{0:T(128)} %pad_add_fusion.info, bf16[512,512]{1,0:T(8,128)(2,1)} %get-tuple-element.2440.query, bf16[512,512]{1,0:T(8,128)(2,1)} %copy-done.38, bf16[512,512]{1,0:T(8,128)(2,1)} %get-tuple-element.2442.own, ...), custom_call_target="tpu_custom_call" | custom-call | flops 1 | bytes 1 | tf_op jit(solution)/shard_map/attend_back/pallas_call | solution.py:616
  685.9 14.2 %collective-permute-done.53 = bf16[1024,512]{1,0:T(8,128)(2,1)S(1)} collective-permute-done((bf16[1024,512]{1,0:T(8,128)(2,1)}, bf16[1024,512]{1,0:T(8,128)(2,1)S(1)}, u32[]{:S(2)}, u32[]{:S(2)}) %collective-permute-start.53) | collective-permute-done | bytes 1048608 | tf_op jit(solution)/shard_map/ppermute | solution.py:318
  713.5 10.1 %row_outer.19 = bf16[2048,2048]{1,0:T(8,128)(2,1)} custom-call(bf16[512,2048]{1,0:T(8,128)(2,1)} %pad_maximum_fusion.4.normed.refs_0_, bf16[512,512]{1,0:T(8,128)(2,1)} %get-tuple-element.2636.refs_1_, bf16[512,512]{1,0:T(8,128)(2,1)} %get-tuple-element.2639.refs_2_.refs_3_, bf16[512,512]{1,0:T(8,128)(2,1)} %get-tuple-element.2642.refs_3_.refs_5_, ...), custom_call_target="tpu_custom_call" | custom-call | flops 4294967296 | bytes 4194304 | tf_op jit(solution)/shard_map/row_outer/pallas_call | solution.py:739
  740.3 15.8 %back_to_rows.1 = f32[512,2048]{1,0:T(8,128)} custom-call(bf16[512,512]{1,0:T(8,128)(2,1)} %get-tuple-element.2695.refs_0_.refs_4_, bf16[512,512]{1,0:T(8,128)(2,1)} %get-tuple-element.2636.refs_1_, bf16[512,512]{1,0:T(8,128)(2,1)} %get-tuple-element.2692.refs_2_.refs_1_.refs_3_, bf16[512,512]{1,0:T(8,128)(2,1)} %get-tuple-element.2639.refs_2_.refs_3_, ...), custom_call_target="tpu_custom_call" | custom-call | flops 1 | bytes 1 | tf_op jit(solution)/shard_map/back_to_rows/pallas_call | solution.py:842
  815.0 11.1 %whole_columns.4 = f32[512,6144]{1,0:T(8,128)} custom-call(s32[1]{0:T(128)} %bitcast.21.me_ref, bf16[2048,768]{1,0:T(8,128)(2,1)} %copy-done.19, bf16[2048,768]{1,0:T(8,128)(2,1)} %collective-permute-done.66.other_ref), custom_call_target="tpu_custom_call" | custom-call | flops 1 | bytes 1 | tf_op jit(solution)/shard_map/whole_columns/pallas_call | solution.py:431
  827.3 11.1 %collective-permute-done.72 = bf16[1024,512]{1,0:T(8,128)(2,1)S(1)} collective-permute-done((bf16[1024,512]{1,0:T(8,128)(2,1)}, bf16[1024,512]{1,0:T(8,128)(2,1)S(1)}, u32[]{:S(2)}, u32[]{:S(2)}) %collective-permute-start.72) | collective-permute-done | bytes 1048608 | tf_op jit(solution)/shard_map/ppermute | solution.py:318
  845.9 17.8 %whole_columns.5 = (f32[512,6144]{1,0:T(8,128)}, f32[512,6144]{1,0:T(8,128)}) custom-call(s32[1]{0:T(128)} %bitcast.21.me_ref, bf16[2048,1536]{1,0:T(8,128)(2,1)} %constant_dynamic-update-slice_fusion.9.own_ref, bf16[2048,1536]{1,0:T(8,128)(2,1)} %collective-permute-done.71.other_ref), custom_call_target="tpu_custom_call" | custom-call | flops 1 | bytes 1 | tf_op jit(solution)/shard_map/whole_columns/pallas_call | solution.py:431
  868.3 9.3 collective-permute-start.84
  918.2 11.0 %collective-permute-done.89 = f32[4352]{0:T(1024)S(1)} collective-permute-done((f32[4352]{0:T(1024)S(1)}, f32[4352]{0:T(1024)S(1)}, u32[]{:S(2)}, u32[]{:S(2)}) %collective-permute-start.89) | collective-permute-done | bytes 17440 | tf_op jit(solution)/shard_map/ppermute | solution.py:318
  (640 shorter events, 436.5 us)
Async XLA Ops:
  7.2 144.4 %all-gather.3.cloned.1.call-start = ((), (), s32[]{:S(2)}) async-start(), calls=%async_computation.2 | async-start | bytes 1310720 | tf_op jit(solution)/shard_map/all_gather | solution.py:903
  61.2 66.4 %collective-permute-start.6 = (bf16[1536,512]{1,0:T(8,128)(2,1)S(1)}, bf16[1536,512]{1,0:T(8,128)(2,1)}, u32[]{:S(2)}, u32[]{:S(2)}) collective-permute-start(bf16[1536,512]{1,0:T(8,128)(2,1)S(1)} %pad_maximum_fusion.8.came0.refs_9_), channel_id=1, source_target_pairs={{0,4},{4,0},{8,12},{12,8},{16,20},{20,16},{24,28},{28,24},{1,5},{5... | collective-permute-start | bytes 4718600 | tf_op jit(solution)/shard_map/ppermute | solution.py:318
  61.3 66.4 %collective-permute-start.5 = (bf16[1536,512]{1,0:T(8,128)(2,1)S(1)}, bf16[1536,512]{1,0:T(8,128)(2,1)}, u32[]{:S(2)}, u32[]{:S(2)}) collective-permute-start(bf16[1536,512]{1,0:T(8,128)(2,1)S(1)} %pad_maximum_fusion.8.came0.refs_9_), channel_id=1, source_target_pairs={{0,16},{4,20},{8,24},{12,28},{16,0},{20,4},{24,8},{28,12},{1,17},{... | collective-permute-start | bytes 4718600 | tf_op jit(solution)/shard_map/ppermute | solution.py:318
  62.8 64.8 %collective-permute-start.4 = (bf16[1536,512]{1,0:T(8,128)(2,1)S(1)}, bf16[1536,512]{1,0:T(8,128)(2,1)}, u32[]{:S(2)}, u32[]{:S(2)}) collective-permute-start(bf16[1536,512]{1,0:T(8,128)(2,1)S(1)} %pad_maximum_fusion.8.came0.refs_9_), channel_id=1, source_target_pairs={{0,8},{4,12},{8,0},{12,4},{16,24},{20,28},{24,16},{28,20},{1,9},{5... | collective-permute-start | bytes 4718600 | tf_op jit(solution)/shard_map/ppermute | solution.py:318
  74.4 53.2 %collective-permute-start.8 = (bf16[256,2048]{1,0:T(8,128)(2,1)S(1)}, bf16[256,2048]{1,0:T(8,128)(2,1)}, u32[]{:S(2)}, u32[]{:S(2)}) collective-permute-start(bf16[256,2048]{1,0:T(8,128)(2,1)S(1)} %get-tuple-element.1480), channel_id=1, source_target_pairs={{0,1},{1,0},{2,5},{3,4},{4,3},{5,2},{6,7},{7,6},{8,9},{9,8},{10,13... | collective-permute-start | bytes 3145736 | tf_op jit(solution)/shard_map/ppermute | solution.py:388
  77.4 289.2 %all-gather.5.cloned.1.call-start = ((), (), s32[]{:S(2)}) async-start(), calls=%async_computation.3 | async-start | bytes 11796480 | tf_op jit(solution)/shard_map/all_gather | solution.py:995
  155.7 31.5 %collective-permute-start.13 = (bf16[1536,512]{1,0:T(8,128)(2,1)S(1)}, bf16[1536,512]{1,0:T(8,128)(2,1)S(1)}, u32[]{:S(2)}, u32[]{:S(2)}) collective-permute-start(bf16[1536,512]{1,0:T(8,128)(2,1)S(1)} %constant_dynamic-update-slice_fusion.came0.refs_21_), channel_id=1, source_target_pairs={{0,4},{4,0},{8,12},{12,8},{16,20},{20,16},{24,28},{28,24},{1,5},{5... | collective-permute-start | bytes 4718600 | tf_op jit(solution)/shard_map/ppermute | solution.py:318
  155.7 31.4 %collective-permute-start.15 = (bf16[256,2048]{1,0:T(8,128)(2,1)}, bf16[256,2048]{1,0:T(8,128)(2,1)S(1)}, u32[]{:S(2)}, u32[]{:S(2)}) collective-permute-start(bf16[256,2048]{1,0:T(8,128)(2,1)} %get-tuple-element.1511), channel_id=1, source_target_pairs={{0,1},{1,0},{2,5},{3,4},{4,3},{5,2},{6,7},{7,6},{8,9},{9,8},{10,13... | collective-permute-start | bytes 3145736 | tf_op jit(solution)/shard_map/ppermute | solution.py:388
  189.0 410.4 %reduce-scatter.3.cloned.1.call-start = ((), (), s32[]{:S(2)}) async-start(), calls=%async_computation.4 | async-start | bytes 3932160 | tf_op jit(solution)/shard_map/reduce_scatter | solution.py:1111
  190.2 34.3 %collective-permute-start.24 = (bf16[2048,256]{1,0:T(8,128)(2,1)}, bf16[2048,256]{1,0:T(8,128)(2,1)}, u32[]{:S(2)}, u32[]{:S(2)}) collective-permute-start(bf16[2048,256]{1,0:T(8,128)(2,1)} %collective-permute-done.16.refs_6_.weight0), channel_id=1, source_target_pairs={{0,4},{4,0},{8,12},{12,8},{16,20},{20,16},{24,28},{28,24},{1,5},{5... | collective-permute-start | bytes 3145736 | tf_op jit(solution)/shard_map/ppermute | solution.py:318
  194.8 29.8 %collective-permute-start.25 = (bf16[2048,256]{1,0:T(8,128)(2,1)S(1)}, bf16[2048,256]{1,0:T(8,128)(2,1)}, u32[]{:S(2)}, u32[]{:S(2)}) collective-permute-start(bf16[2048,256]{1,0:T(8,128)(2,1)S(1)} %collective-permute-done.17.refs_8_.weight0), channel_id=1, source_target_pairs={{0,4},{4,0},{8,12},{12,8},{16,20},{20,16},{24,28},{28,24},{1,5},{5... | collective-permute-start | bytes 3145736 | tf_op jit(solution)/shard_map/ppermute | solution.py:318
  211.2 47.7 %collective-permute-start.28 = (bf16[512,2048]{1,0:T(8,128)(2,1)S(1)}, bf16[512,2048]{1,0:T(8,128)(2,1)S(1)}, u32[]{:S(2)}, u32[]{:S(2)}) collective-permute-start(bf16[512,2048]{1,0:T(8,128)(2,1)S(1)} %maximum_select_fusion.refs_5_.refs_0_), channel_id=1, source_target_pairs={{0,16},{4,20},{8,24},{12,28},{16,0},{20,4},{24,8},{28,12},{1,17},{... | collective-permute-start | bytes 6291464 | tf_op jit(solution)/shard_map/ppermute | solution.py:318
  213.8 46.6 %collective-permute-start.27 = (bf16[512,2048]{1,0:T(8,128)(2,1)S(1)}, bf16[512,2048]{1,0:T(8,128)(2,1)S(1)}, u32[]{:S(2)}, u32[]{:S(2)}) collective-permute-start(bf16[512,2048]{1,0:T(8,128)(2,1)S(1)} %maximum_select_fusion.refs_5_.refs_0_), channel_id=1, source_target_pairs={{0,8},{4,12},{8,0},{12,4},{16,24},{20,28},{24,16},{28,20},{1,9},{5... | collective-permute-start | bytes 6291464 | tf_op jit(solution)/shard_map/ppermute | solution.py:318
  286.9 45.2 %collective-permute-start.33 = (bf16[512,2048]{1,0:T(8,128)(2,1)}, bf16[512,2048]{1,0:T(8,128)(2,1)S(1)}, u32[]{:S(2)}, u32[]{:S(2)}) collective-permute-start(bf16[512,2048]{1,0:T(8,128)(2,1)} %get-tuple-element.2307.refs_0_), channel_id=1, source_target_pairs={{0,16},{4,20},{8,24},{12,28},{16,0},{20,4},{24,8},{28,12},{1,17},{... | collective-permute-start | bytes 6291464 | tf_op jit(solution)/shard_map/ppermute | solution.py:318
  288.2 45.2 %collective-permute-start.32 = (bf16[512,2048]{1,0:T(8,128)(2,1)}, bf16[512,2048]{1,0:T(8,128)(2,1)S(1)}, u32[]{:S(2)}, u32[]{:S(2)}) collective-permute-start(bf16[512,2048]{1,0:T(8,128)(2,1)} %get-tuple-element.2307.refs_0_), channel_id=1, source_target_pairs={{0,8},{4,12},{8,0},{12,4},{16,24},{20,28},{24,16},{28,20},{1,9},{5... | collective-permute-start | bytes 6291464 | tf_op jit(solution)/shard_map/ppermute | solution.py:318
  366.6 30.1 %collective-permute-start.36 = (bf16[2048,2304]{1,0:T(8,128)(2,1)}, bf16[2048,2304]{1,0:T(8,128)(2,1)}, u32[]{:S(2)}, u32[]{:S(2)}) collective-permute-start(bf16[2048,2304]{1,0:T(8,128)(2,1)} %all-gather.5.cloned.1.call-done.refs_10_.refs_11_.refs_12_.refs_4_.refs_9_), channel_id=1, source_target_pairs={{0,4},{4,0},{8,12},{12,8},{16,20},{20,16},{24,28},{28,24},{1,5},{5... | collective-permute-start | bytes 28311560 | tf_op jit(solution)/shard_map/ppermute | solution.py:318
  458.7 54.5 %collective-permute-start.38 = (bf16[512,2048]{1,0:T(8,128)(2,1)}, bf16[512,2048]{1,0:T(8,128)(2,1)}, u32[]{:S(2)}, u32[]{:S(2)}) collective-permute-start(bf16[512,2048]{1,0:T(8,128)(2,1)} %get-tuple-element.2138), channel_id=1, source_target_pairs={{0,8},{4,12},{8,0},{12,4},{16,24},{20,28},{24,16},{28,20},{1,9},{5... | collective-permute-start | bytes 6291464 | tf_op jit(solution)/shard_map/ppermute | solution.py:318
  460.2 53.0 %collective-permute-start.39 = (bf16[512,2048]{1,0:T(8,128)(2,1)}, bf16[512,2048]{1,0:T(8,128)(2,1)}, u32[]{:S(2)}, u32[]{:S(2)}) collective-permute-start(bf16[512,2048]{1,0:T(8,128)(2,1)} %get-tuple-element.2139), channel_id=1, source_target_pairs={{0,16},{4,20},{8,24},{12,28},{16,0},{20,4},{24,8},{28,12},{1,17},{... | collective-permute-start | bytes 6291464 | tf_op jit(solution)/shard_map/ppermute | solution.py:318
  513.2 30.6 %collective-permute-start.40 = (bf16[2048,1536]{1,0:T(8,128)(2,1)}, bf16[2048,1536]{1,0:T(8,128)(2,1)}, u32[]{:S(2)}, u32[]{:S(2)}) collective-permute-start(bf16[2048,1536]{1,0:T(8,128)(2,1)} %row_outer.14), channel_id=1, source_target_pairs={{0,4},{4,0},{8,12},{12,8},{16,20},{20,16},{24,28},{28,24},{1,5},{5... | collective-permute-start | bytes 18874376 | tf_op jit(solution)/shard_map/ppermute | solution.py:318
  513.3 215.0 %reduce-scatter.5.cloned.1.call-start = ((), (), s32[]{:S(2)}) async-start(), calls=%async_computation.5 | async-start | bytes 7864320 | tf_op jit(solution)/shard_map/reduce_scatter | solution.py:1179
  543.8 55.6 %collective-permute-start.43 = (bf16[512,2048]{1,0:T(8,128)(2,1)}, bf16[512,2048]{1,0:T(8,128)(2,1)}, u32[]{:S(2)}, u32[]{:S(2)}) collective-permute-start(bf16[512,2048]{1,0:T(8,128)(2,1)} %get-tuple-element.2322), channel_id=1, source_target_pairs={{0,8},{4,12},{8,0},{12,4},{16,24},{20,28},{24,16},{28,20},{1,9},{5... | collective-permute-start | bytes 6291464 | tf_op jit(solution)/shard_map/ppermute | solution.py:318
  545.3 54.1 %collective-permute-start.44 = (bf16[512,2048]{1,0:T(8,128)(2,1)}, bf16[512,2048]{1,0:T(8,128)(2,1)}, u32[]{:S(2)}, u32[]{:S(2)}) collective-permute-start(bf16[512,2048]{1,0:T(8,128)(2,1)} %get-tuple-element.2323), channel_id=1, source_target_pairs={{0,16},{4,20},{8,24},{12,28},{16,0},{20,4},{24,8},{28,12},{1,17},{... | collective-permute-start | bytes 6291464 | tf_op jit(solution)/shard_map/ppermute | solution.py:318
  599.5 35.8 %collective-permute-start.47 = (bf16[2048,1024]{1,0:T(8,128)(2,1)}, bf16[2048,1024]{1,0:T(8,128)(2,1)S(1)}, u32[]{:S(2)}, u32[]{:S(2)}) collective-permute-start(bf16[2048,1024]{1,0:T(8,128)(2,1)} %row_outer.15), channel_id=1, source_target_pairs={{0,4},{4,0},{8,12},{12,8},{16,20},{20,16},{24,28},{28,24},{1,5},{5... | collective-permute-start | bytes 12582920 | tf_op jit(solution)/shard_map/ppermute | solution.py:318
  604.4 30.8 %collective-permute-start.46 = (bf16[256,2048]{1,0:T(8,128)(2,1)}, bf16[256,2048]{1,0:T(8,128)(2,1)S(1)}, u32[]{:S(2)}, u32[]{:S(2)}) collective-permute-start(bf16[256,2048]{1,0:T(8,128)(2,1)} %get-tuple-element.2907), channel_id=1, source_target_pairs={{0,16},{4,20},{8,24},{12,28},{16,0},{20,4},{24,8},{28,12},{1,17},{... | collective-permute-start | bytes 3145736 | tf_op jit(solution)/shard_map/ppermute | solution.py:318
  637.4 32.8 %collective-permute-start.50 = (bf16[512,768]{1,0:T(8,128)(2,1)}, bf16[512,768]{1,0:T(8,128)(2,1)S(1)}, u32[]{:S(2)}, u32[]{:S(2)}) collective-permute-start(bf16[512,768]{1,0:T(8,128)(2,1)} %reduce-scatter.3.cloned.1.call-done), channel_id=1, source_target_pairs={{0,16},{4,20},{8,24},{12,28},{16,0},{20,4},{24,8},{28,12},{1,17},{... | collective-permute-start | bytes 2359304 | tf_op jit(solution)/shard_map/ppermute | solution.py:318
  638.8 31.4 %collective-permute-start.49 = (bf16[512,768]{1,0:T(8,128)(2,1)}, bf16[512,768]{1,0:T(8,128)(2,1)S(1)}, u32[]{:S(2)}, u32[]{:S(2)}) collective-permute-start(bf16[512,768]{1,0:T(8,128)(2,1)} %reduce-scatter.3.cloned.1.call-done), channel_id=1, source_target_pairs={{0,8},{4,12},{8,0},{12,4},{16,24},{20,28},{24,16},{28,20},{1,9},{5... | collective-permute-start | bytes 2359304 | tf_op jit(solution)/shard_map/ppermute | solution.py:318
  639.5 30.7 %collective-permute-start.51 = (bf16[512,512]{1,0:T(8,128)(2,1)}, bf16[512,512]{1,0:T(8,128)(2,1)}, u32[]{:S(2)}, u32[]{:S(2)}) collective-permute-start(bf16[512,512]{1,0:T(8,128)(2,1)} %get-tuple-element.2456), channel_id=1, source_target_pairs={{4,0},{12,8},{20,16},{28,24},{5,1},{13,9},{21,17},{29,25},{6,2},{1... | collective-permute-start | bytes 1572872 | tf_op jit(solution)/shard_map/ppermute | solution.py:1139
  728.3 40.8 %collective-permute-start.65 = (bf16[2048,2048]{1,0:T(8,128)(2,1)}, bf16[2048,2048]{1,0:T(8,128)(2,1)}, u32[]{:S(2)}, u32[]{:S(2)}) collective-permute-start(bf16[2048,2048]{1,0:T(8,128)(2,1)} %row_outer.19), channel_id=1, source_target_pairs={{0,4},{4,0},{8,12},{12,8},{16,20},{20,16},{24,28},{28,24},{1,5},{5... | collective-permute-start | bytes 25165832 | tf_op jit(solution)/shard_map/ppermute | solution.py:318
  731.6 36.6 %collective-permute-start.62 = (bf16[512,1536]{1,0:T(8,128)(2,1)}, bf16[512,1536]{1,0:T(8,128)(2,1)S(1)}, u32[]{:S(2)}, u32[]{:S(2)}) collective-permute-start(bf16[512,1536]{1,0:T(8,128)(2,1)} %reduce-scatter.5.cloned.1.call-done), channel_id=1, source_target_pairs={{0,16},{4,20},{8,24},{12,28},{16,0},{20,4},{24,8},{28,12},{1,17},{... | collective-permute-start | bytes 4718600 | tf_op jit(solution)/shard_map/ppermute | solution.py:318
  732.3 36.7 %collective-permute-start.61 = (bf16[512,1536]{1,0:T(8,128)(2,1)}, bf16[512,1536]{1,0:T(8,128)(2,1)S(1)}, u32[]{:S(2)}, u32[]{:S(2)}) collective-permute-start(bf16[512,1536]{1,0:T(8,128)(2,1)} %reduce-scatter.5.cloned.1.call-done), channel_id=1, source_target_pairs={{0,8},{4,12},{8,0},{12,4},{16,24},{20,28},{24,16},{28,20},{1,9},{5... | collective-permute-start | bytes 4718600 | tf_op jit(solution)/shard_map/ppermute | solution.py:318
  771.4 32.0 %collective-permute-start.66 = (bf16[2048,768]{1,0:T(8,128)(2,1)S(1)}, bf16[2048,768]{1,0:T(8,128)(2,1)}, u32[]{:S(2)}, u32[]{:S(2)}) collective-permute-start(bf16[2048,768]{1,0:T(8,128)(2,1)S(1)} %constant_dynamic-update-slice_fusion.4.own_ref), channel_id=1, source_target_pairs={{0,4},{4,0},{8,12},{12,8},{16,20},{20,16},{24,28},{28,24},{1,5},{5... | collective-permute-start | bytes 9437192 | tf_op jit(solution)/shard_map/ppermute | solution.py:318
  815.0 48.7 %collective-permute-start.79 = (bf16[256,2048]{1,0:T(8,128)(2,1)S(1)}, bf16[256,2048]{1,0:T(8,128)(2,1)S(1)}, u32[]{:S(2)}, u32[]{:S(2)}) collective-permute-start(bf16[256,2048]{1,0:T(8,128)(2,1)S(1)} %get-tuple-element.2901), channel_id=1, source_target_pairs={{1,0},{0,1},{5,2},{4,3},{3,4},{2,5},{7,6},{6,7},{9,8},{8,9},{13,10... | collective-permute-start | bytes 3145736 | tf_op jit(solution)/shard_map/ppermute | solution.py:395
  (203 other events, 2299.8 us)
Sparse Core Ops, SparseCore 0:
  77.5 47.1 all-gather.2
  189.1 177.3 all-gather.4
  513.4 57.2 reduce-scatter.2
  599.6 107.9 reduce-scatter.4

commit v13 on v12

--- a/solution.py
+++ b/solution.py
@@ -1187,37 +1187,37 @@
 
     s.down_near = near(s.down_total)
     give_back(1, 2)
-    s.out_head, s.out_tail, back, finished = in_order(
+    s.out_head, s.out_tail = in_order(
         [
             head_call(s.resid_rolled, s.mixed, s.out_came, 0),
             tail_call(s.resid_rolled, s.mixed, s.out_came, 0),
-            back_call(0),
-            finish_call(3),
         ]
     )
+    del s.out_came
+    s.end()
+
+    s.out_near = send_near((s.out_head[0], s.out_tail[0]))
+    back, finished = in_order([back_call(0), finish_call(3)])
     s.backs = s.backs | {0: back}
     s.finished = {3: finished}
-    del s.out_came
-    s.end()
-
-    s.out_near = send_near((s.out_head[0], s.out_tail[0]))
+    s.end()
+
+    s.out_far = send_far(s.out_near, (s.out_tail[1], s.out_head[1]), by_columns)
+    s.down_far = far(*s.down_near)
     mlp_out = total(s.mlp_came, s.mlp_came_far, by_rows(s.mlp_rest[1]), by_rows)
     s.output = (s.valid * (s.resid + mlp_out)).astype(low)
     give_back(0)
     finished1, finished2 = in_order([finish_call(1), finish_call(2)])
     s.finished = s.finished | {1: finished1, 2: finished2}
+    s.gate_up_total = gate_up_total
     del s.mlp_came, s.mlp_came_far, s.mlp_rest, s.resid
     s.end()
 
     output_sent = from_sequences_send(s.output)
-    s.out_far = send_far(s.out_near, (s.out_tail[1], s.out_head[1]), by_columns)
-    s.down_far = far(*s.down_near)
+    gate_up_near = near(s.gate_up_total)
     (finished,) = in_order([finish_call(0)])
     s.finished = s.finished | {0: finished}
     (s.odd,) = in_order([odd_call(s.normed, [s.finished[i][1] for i in range(4)])])
-    s.gate_up_total = gate_up_total
-    s.output_first = output_sent[0]
-    del s.output
     s.end()
 
     my_group = me.astype(jnp.int32)[None]
@@ -1225,11 +1225,9 @@
     def whole_call(widths, own, other, part=0):
         return lambda first: whole_columns(my_group, first, other, widths, part), own
 
-    s.gate_up_near = near(s.gate_up_total)
     s.qkv_came = across(s.odd, CORE)
     out_sum = total(s.out_near, s.out_far, (s.out_head[2], s.out_tail[2]), by_columns)
     s.out_chunks = jnp.split(out_sum.astype(low), shards, 0)
-    s.out_ring = ring_sum_first(s.out_chunks)
     weights = [
         pair
         for i in range(4)
@@ -1251,8 +1249,13 @@
     s.grad_tokens = (
         s.grad_resid + norm_back(x_unit, s.inverse_in, grad_in * s.attn_gains)
     ).astype(low)
-    del s.odd, s.out_near, s.out_far, s.out_head, s.out_tail, s.backs
+    s.down_spread = jnp.concatenate([s.down_total, *s.down_near, *s.down_far], 0)
+    s.down_spread_other = across(s.down_spread, CORE)
+    s.gate_up_near = gate_up_near
+    s.output_first = output_sent[0]
+    del s.odd, s.out_near, s.out_far, s.out_head, s.out_tail, s.backs, s.output
     del s.own_blocks, s.came, s.came_other, s.grad_resid, s.x_low
+    del s.down_total, s.down_near, s.down_far
     s.end()
 
     even = [s.finished[i][0] for i in range(4)]
@@ -1264,12 +1267,10 @@
         ]
     )
     tokens_sent = from_sequences_send(s.grad_tokens)
-    s.down_spread = jnp.concatenate([s.down_total, *s.down_near, *s.down_far], 0)
-    s.down_spread_other = across(s.down_spread, CORE)
     s.output_second = output_sent[1]
-    s.out_ring_last = around(rounded_sum(s.out_chunks[3], s.out_ring[0]), 1)
+    s.out_ring = ring_sum_first(s.out_chunks)
     s.gate_up_far = far(*s.gate_up_near)
-    del s.qkv_came, s.finished, s.down_total, s.down_near, s.down_far
+    del s.qkv_came, s.finished
     s.end()
 
     def qkv_chunks(came, came_far, head, tail):
@@ -1280,17 +1281,19 @@
     s.gate_up_own = jnp.concatenate([s.gate_up_total, *s.gate_up_near, *s.gate_up_far], 0)
     s.gate_up_other = across(s.gate_up_own, CORE)
     (s.whole_down,) = in_order([whole_call((units,), s.down_spread, s.down_spread_other)])
-    s.out_total = rounded_sum(s.out_chunks[0], s.out_ring[1], s.out_ring_last)
+    s.out_ring_last = around(rounded_sum(s.out_chunks[3], s.out_ring[0]), 1)
     s.tokens_first = tokens_sent[0]
-    del s.down_spread, s.down_spread_other, s.out_chunks, s.out_ring, s.out_ring_last
+    del s.down_spread, s.down_spread_other
     del s.gate_up_near, s.gate_up_far, s.gate_up_total
     s.end()
 
     s.far0 = send_far(s.near0, (s.tail0[1], s.head0[1]), by_columns)
     s.near1 = send_near((s.head1[0], s.tail1[0]))
+    s.out_total = rounded_sum(s.out_chunks[0], s.out_ring[1], s.out_ring_last)
     (s.whole_gate_up,) = in_order([whole_call((units, units), s.gate_up_own, s.gate_up_other)])
     s.tokens_second = tokens_sent[1]
     del s.gate_up_own, s.gate_up_other, s.grad_tokens
+    del s.out_chunks, s.out_ring, s.out_ring_last
     s.end()
 
     s.chunks0 = qkv_chunks(s.near0, s.far0, s.head0, s.tail0)

time: 989 us -> 994 us (level)
  starting transfers between devices: 133 us -> 145 us
    ppermute x73, waiting for transfers between devices: 160 us -> 133 us  [across(): return lax.ppermute(x, 'rep', [(i, i ^ mask) for i in range(count)])]
    ppermute x12, waiting for transfers between devices: 46.9 us -> 62 us  [around(): lax.ppermute(x, 'shard', [(i, (i + by) % count) for i in range(count)])]
    unnamed x272 -> x268, local copies, waits for them, and re-layouts: 27.8 us -> 29.8 us
  transfers between devices with their start and end apart: 107 -> 107, of which waited for: 41 -> 40; matrix products, arithmetic and copies ran while one was open for 9% -> 8% of each run, Pallas kernels for 38% -> 37%
where the time goes in v13:
time: 994 us; the launch traced here: 984 us
  Pallas kernels  425 us (43%)
  waiting for transfers between devices  268 us (27%)
  starting transfers between devices  145 us (15%)
  local copies, waits for them, and re-layouts  68.8 us (7%)
  other arithmetic  60.8 us (6%)
  between operations  16 us (2%)
    ppermute x73, waiting for transfers between devices, across(): return lax.ppermute(x, 'rep', [(i, i ^ mask) for i in range(count)])  133 us
    pallas_call x16, Pallas kernels, call(): pl.pallas_call(body, grid=(1,), out_shape=outs, in_specs=in_specs, out_sp...  119 us
    pallas_call x12, Pallas kernels, row_outer(): pl.pallas_call(body, grid=(tiles,), out_shape=[jax.ShapeDtypeStruct((tile...  114 us
    ppermute x73, starting transfers between devices, across(): return lax.ppermute(x, 'rep', [(i, i ^ mask) for i in range(count)])  69 us
    ppermute x12, waiting for transfers between devices, around(): lax.ppermute(x, 'shard', [(i, (i + by) % count) for i in range(count)])  62 us
    pallas_call x2, Pallas kernels, hidden_units(): pl.pallas_call(body, grid=(3,), out_shape=[jax.ShapeDtypeStruct((rows, un...  59.8 us
    pallas_call x4, Pallas kernels, from_hidden(): pl.pallas_call(body, grid=(4,), out_shape=[jax.ShapeDtypeStruct((2 * rows...  59.3 us
    ppermute x4, waiting for transfers between devices, to_sequence(): return lax.ppermute(cut, ('rep', 'shard'), sequence_pairs(turn))  51.7 us
  transfers between devices with their start and end apart: 107, of which 40 were waited for; matrix products, arithmetic and copies ran while one was open for 8% of the time, Pallas kernels for 37%

profile of v13, /device:TPU:0, one launch (start us, length us, event | category | flops | bytes accessed | tf_op | source)
XLA Modules:
  0.0 984.2 jit_solution(4465470997103218743)
XLA Ops:
  33.1 10.3 %collective-permute-done = bf16[528,512]{1,0:T(8,128)(2,1)} collective-permute-done((bf16[528,512]{1,0:T(8,128)(2,1)}, bf16[528,512]{1,0:T(8,128)(2,1)}, u32[]{:S(2)}, u32[]{:S(2)}) %collective-permute-start) | collective-permute-done | bytes 540704 | tf_op jit(solution)/shard_map/ppermute | solution.py:323
  45.1 13.5 %collective-permute-done.3 = bf16[528,512]{1,0:T(8,128)(2,1)S(1)} collective-permute-done((bf16[528,512]{1,0:T(8,128)(2,1)}, bf16[528,512]{1,0:T(8,128)(2,1)S(1)}, u32[]{:S(2)}, u32[]{:S(2)}) %collective-permute-start.3) | collective-permute-done | bytes 540704 | tf_op jit(solution)/shard_map/ppermute | solution.py:323
  64.9 9.5 collective-permute-start.7
  78.7 48.8 %collective-permute-done.8 = bf16[256,2048]{1,0:T(8,128)(2,1)} collective-permute-done((bf16[256,2048]{1,0:T(8,128)(2,1)S(1)}, bf16[256,2048]{1,0:T(8,128)(2,1)}, u32[]{:S(2)}, u32[]{:S(2)}) %collective-permute-start.8) | collective-permute-done | bytes 1048608 | tf_op jit(solution)/shard_map/ppermute | solution.py:388
  134.4 10.0 %collective-permute-start.14 = (bf16[256,2048]{1,0:T(8,128)(2,1)}, bf16[256,2048]{1,0:T(8,128)(2,1)}, u32[]{:S(2)}, u32[]{:S(2)}) collective-permute-start(bf16[256,2048]{1,0:T(8,128)(2,1)} %get-tuple-element.1588), channel_id=1, source_target_pairs={{0,0},{1,1},{2,4},{3,5},{4,2},{5,3},{6,6},{7,7},{8,8},{9,9},{10,12... | collective-permute-start | bytes 3145736 | tf_op jit(solution)/shard_map/ppermute | solution.py:388
  245.3 13.7 %collective-permute-done.28.refs_7_.refs_2_ = bf16[512,2048]{1,0:T(8,128)(2,1)S(1)} collective-permute-done((bf16[512,2048]{1,0:T(8,128)(2,1)S(1)}, bf16[512,2048]{1,0:T(8,128)(2,1)S(1)}, u32[]{:S(2)}, u32[]{:S(2)}) %collective-permute-start.28) | collective-permute-done | bytes 2097184 | tf_op jit(solution)/shard_map/ppermute | solution.py:318
  269.1 11.7 %close_attention.1 = (f32[512,2048]{1,0:T(8,128)}, bf16[512,2048]{1,0:T(8,128)(2,1)}) custom-call(bf16[512,2048]{1,0:T(8,128)(2,1)} %pad_maximum_fusion.3.x, bf16[512,512]{1,0:T(8,128)(2,1)} %get-tuple-element.2545.refs_0_.refs_1_.refs_4_, bf16[512,512]{1,0:T(8,128)(2,1)} %get-tuple-element.2546.refs_1_.refs_2_.refs_3_, ...), custom_call_target="tpu_custom_call" | custom-call | flops 1 | bytes 1 | tf_op jit(solution)/shard_map/close_attention/pallas_call | solution.py:789
  289.4 42.8 %collective-permute-done.33.refs_2_ = bf16[512,2048]{1,0:T(8,128)(2,1)S(1)} collective-permute-done((bf16[512,2048]{1,0:T(8,128)(2,1)}, bf16[512,2048]{1,0:T(8,128)(2,1)S(1)}, u32[]{:S(2)}, u32[]{:S(2)}) %collective-permute-start.33) | collective-permute-done | bytes 2097184 | tf_op jit(solution)/shard_map/ppermute | solution.py:318
  336.5 19.9 %collective-permute-done.35.refs_4_ = bf16[256,2048]{1,0:T(8,128)(2,1)S(1)} collective-permute-done((bf16[256,2048]{1,0:T(8,128)(2,1)S(1)}, bf16[256,2048]{1,0:T(8,128)(2,1)S(1)}, u32[]{:S(2)}, u32[]{:S(2)}) %collective-permute-start.35) | collective-permute-done | bytes 1048608 | tf_op jit(solution)/shard_map/ppermute | solution.py:318
  356.7 9.7 all-gather.5.cloned.1.call-done.refs_10_.refs_11_.refs_12_.refs_4_.refs_9_
  366.6 29.7 %hidden_units.2 = (bf16[2048,768]{1,0:T(8,128)(2,1)}, bf16[2048,768]{1,0:T(8,128)(2,1)}, bf16[2048,768]{1,0:T(8,128)(2,1)}) custom-call(bf16[512,2048]{1,0:T(8,128)(2,1)} %get-tuple-element.2385.refs_0_, bf16[512,2048]{1,0:T(8,128)(2,1)} %copy-done.12, bf16[512,2048]{1,0:T(8,128)(2,1)} %copy-done.11, bf16[256,2048]{1,0:T(8,128)(2,1)} %copy-done.21, ...), custom_call_target="tpu_custom_call" | custom-call | flops 1 | bytes 1 | tf_op jit(solution)/shard_map/hidden_units/pallas_call | solution.py:656
  396.2 30.1 %hidden_units.3 = (bf16[2048,768]{1,0:T(8,128)(2,1)}, bf16[2048,768]{1,0:T(8,128)(2,1)}, bf16[2048,768]{1,0:T(8,128)(2,1)}) custom-call(bf16[512,2048]{1,0:T(8,128)(2,1)} %get-tuple-element.2385.refs_0_, bf16[512,2048]{1,0:T(8,128)(2,1)} %copy-done.12, bf16[512,2048]{1,0:T(8,128)(2,1)} %copy-done.11, bf16[256,2048]{1,0:T(8,128)(2,1)} %copy-done.21, ...), custom_call_target="tpu_custom_call" | custom-call | flops 1 | bytes 1 | tf_op jit(solution)/shard_map/hidden_units/pallas_call | solution.py:656
  426.4 12.6 %row_outer.12 = bf16[2048,768]{1,0:T(8,128)(2,1)} custom-call(bf16[512,2048]{1,0:T(8,128)(2,1)} %copy-done.6, bf16[512,2048]{1,0:T(8,128)(2,1)} %copy-done.14, bf16[512,2048]{1,0:T(8,128)(2,1)} %copy-done.13, bf16[256,2048]{1,0:T(8,128)(2,1)} %copy-done.23, bf16[256,2048]{1,0:T(8,128)(2,1)} %copy-done.22, ...), custom_call_target="tpu_custom_call" | custom-call | flops 6442450944 | bytes 11534336 | tf_op jit(solution)/shard_map/row_outer/pallas_call | solution.py:739
  439.4 18.9 %from_hidden.4 = (bf16[512,2048]{1,0:T(8,128)(2,1)}, bf16[512,2048]{1,0:T(8,128)(2,1)}) custom-call(bf16[2048,768]{1,0:T(8,128)(2,1)} %get-tuple-element.2396.refs_0_.refs_1_.refs_2_.refs_3_.refs_5_, bf16[2048,768]{1,0:T(8,128)(2,1)} %get-tuple-element.2396.refs_0_.refs_1_.refs_2_.refs_3_.refs_5_, ...), custom_call_target="tpu_custom_call" | custom-call | flops 1 | bytes 1 | tf_op jit(solution)/shard_map/from_hidden/pallas_call | solution.py:695
  461.3 13.2 %row_outer.13 = bf16[2048,768]{1,0:T(8,128)(2,1)} custom-call(bf16[512,2048]{1,0:T(8,128)(2,1)} %copy-done.6, bf16[512,2048]{1,0:T(8,128)(2,1)} %copy-done.14, bf16[512,2048]{1,0:T(8,128)(2,1)} %copy-done.13, bf16[256,2048]{1,0:T(8,128)(2,1)} %copy-done.23, bf16[256,2048]{1,0:T(8,128)(2,1)} %copy-done.22, ...), custom_call_target="tpu_custom_call" | custom-call | flops 6442450944 | bytes 11534336 | tf_op jit(solution)/shard_map/row_outer/pallas_call | solution.py:739
  474.5 18.8 %from_hidden.5 = (bf16[512,2048]{1,0:T(8,128)(2,1)}, bf16[512,2048]{1,0:T(8,128)(2,1)}) custom-call(bf16[2048,768]{1,0:T(8,128)(2,1)} %get-tuple-element.2396.refs_0_.refs_1_.refs_2_.refs_3_.refs_5_, bf16[2048,768]{1,0:T(8,128)(2,1)} %get-tuple-element.2396.refs_0_.refs_1_.refs_2_.refs_3_.refs_5_, ...), custom_call_target="tpu_custom_call" | custom-call | flops 1 | bytes 1 | tf_op jit(solution)/shard_map/from_hidden/pallas_call | solution.py:695
  493.4 19.4 %row_outer.14 = bf16[2048,1536]{1,0:T(8,128)(2,1)} custom-call(bf16[512,2048]{1,0:T(8,128)(2,1)} %get-tuple-element.2385.refs_0_, bf16[512,2048]{1,0:T(8,128)(2,1)} %copy-done.12, bf16[512,2048]{1,0:T(8,128)(2,1)} %copy-done.11, bf16[256,2048]{1,0:T(8,128)(2,1)} %copy-done.21, bf16[256,2048]{1,0:T(8,128)(2,1)} %copy-done.20, ...), custom_call_target="tpu_custom_call" | custom-call | flops 12884901888 | bytes 14680064 | tf_op jit(solution)/shard_map/row_outer/pallas_call | solution.py:739
  519.8 10.7 %from_hidden.6 = (bf16[512,2048]{1,0:T(8,128)(2,1)}, bf16[512,2048]{1,0:T(8,128)(2,1)}) custom-call(bf16[2048,768]{1,0:T(8,128)(2,1)} %get-tuple-element.2305.refs_5_.refs_0_.refs_1_.refs_2_.refs_3_, bf16[2048,768]{1,0:T(8,128)(2,1)} %get-tuple-element.2305.refs_5_.refs_0_.refs_1_.refs_2_.refs_3_, ...), custom_call_target="tpu_custom_call" | custom-call | flops 1 | bytes 1 | tf_op jit(solution)/shard_map/from_hidden/pallas_call | solution.py:695
  530.5 10.9 %from_hidden.7 = (bf16[512,2048]{1,0:T(8,128)(2,1)}, bf16[512,2048]{1,0:T(8,128)(2,1)}) custom-call(bf16[2048,768]{1,0:T(8,128)(2,1)} %get-tuple-element.2305.refs_5_.refs_0_.refs_1_.refs_2_.refs_3_, bf16[2048,768]{1,0:T(8,128)(2,1)} %get-tuple-element.2305.refs_5_.refs_0_.refs_1_.refs_2_.refs_3_, ...), custom_call_target="tpu_custom_call" | custom-call | flops 1 | bytes 1 | tf_op jit(solution)/shard_map/from_hidden/pallas_call | solution.py:695
  555.6 13.4 %attend_back.4 = (bf16[512,512]{1,0:T(8,128)(2,1)}, f32[512,512]{1,0:T(8,128)}, bf16[512,512]{1,0:T(8,128)(2,1)}, f32[1,128]{1,0:T(1,128)}) custom-call(s32[2]{0:T(128)} %pad_add_fusion.info, bf16[512,512]{1,0:T(8,128)(2,1)} %get-tuple-element.2352.query, bf16[512,512]{1,0:T(8,128)(2,1)} %copy-done.36, bf16[512,512]{1,0:T(8,128)(2,1)} %get-tuple-element.2354.own, ...), custom_call_target="tpu_custom_call" | custom-call | flops 1 | bytes 1 | tf_op jit(solution)/shard_map/attend_back/pallas_call | solution.py:616
  579.1 19.7 %row_outer.16 = bf16[2048,1536]{1,0:T(8,128)(2,1)} custom-call(bf16[512,2048]{1,0:T(8,128)(2,1)} %get-tuple-element.2385.refs_0_, bf16[512,2048]{1,0:T(8,128)(2,1)} %copy-done.12, bf16[512,2048]{1,0:T(8,128)(2,1)} %copy-done.11, bf16[256,2048]{1,0:T(8,128)(2,1)} %copy-done.21, bf16[256,2048]{1,0:T(8,128)(2,1)} %copy-done.20, ...), custom_call_target="tpu_custom_call" | custom-call | flops 12884901888 | bytes 14680064 | tf_op jit(solution)/shard_map/row_outer/pallas_call | solution.py:739
  608.1 13.3 %attend_back.5 = (bf16[512,512]{1,0:T(8,128)(2,1)}, f32[512,512]{1,0:T(8,128)}, bf16[512,512]{1,0:T(8,128)(2,1)}, f32[1,128]{1,0:T(1,128)}) custom-call(s32[2]{0:T(128)} %pad_add_fusion.info, bf16[512,512]{1,0:T(8,128)(2,1)} %get-tuple-element.2440.query, bf16[512,512]{1,0:T(8,128)(2,1)} %copy-done.35, bf16[512,512]{1,0:T(8,128)(2,1)} %get-tuple-element.2442.own, ...), custom_call_target="tpu_custom_call" | custom-call | flops 1 | bytes 1 | tf_op jit(solution)/shard_map/attend_back/pallas_call | solution.py:616
  621.3 13.6 %attend_back.6 = (bf16[512,512]{1,0:T(8,128)(2,1)}, f32[512,512]{1,0:T(8,128)}, bf16[512,512]{1,0:T(8,128)(2,1)}, f32[1,128]{1,0:T(1,128)}) custom-call(s32[2]{0:T(128)} %pad_add_fusion.info, bf16[512,512]{1,0:T(8,128)(2,1)} %get-tuple-element.2455.query, bf16[512,512]{1,0:T(8,128)(2,1)} %collective-permute-done.21.before, ...), custom_call_target="tpu_custom_call" | custom-call | flops 1 | bytes 1 | tf_op jit(solution)/shard_map/attend_back/pallas_call | solution.py:616
  661.7 13.2 %attend_back.7 = (bf16[512,512]{1,0:T(8,128)(2,1)}, f32[512,512]{1,0:T(8,128)}, bf16[512,512]{1,0:T(8,128)(2,1)}, f32[1,128]{1,0:T(1,128)}) custom-call(s32[2]{0:T(128)} %pad_add_fusion.info, bf16[512,512]{1,0:T(8,128)(2,1)} %get-tuple-element.2590.query, bf16[512,512]{1,0:T(8,128)(2,1)} %copy-done.33, bf16[512,512]{1,0:T(8,128)(2,1)} %get-tuple-element.2592.own, ...), custom_call_target="tpu_custom_call" | custom-call | flops 1 | bytes 1 | tf_op jit(solution)/shard_map/attend_back/pallas_call | solution.py:616
  715.6 10.1 %row_outer.19 = bf16[2048,2048]{1,0:T(8,128)(2,1)} custom-call(bf16[512,2048]{1,0:T(8,128)(2,1)} %pad_maximum_fusion.4.normed.refs_0_, bf16[512,512]{1,0:T(8,128)(2,1)} %get-tuple-element.2793.refs_1_, bf16[512,512]{1,0:T(8,128)(2,1)} %get-tuple-element.2796.refs_2_.refs_3_, bf16[512,512]{1,0:T(8,128)(2,1)} %get-tuple-element.2799.refs_3_.refs_5_, ...), custom_call_target="tpu_custom_call" | custom-call | flops 4294967296 | bytes 4194304 | tf_op jit(solution)/shard_map/row_outer/pallas_call | solution.py:739
  729.4 9.6 collective-permute-start.63
  740.2 16.9 %back_to_rows.1 = f32[512,2048]{1,0:T(8,128)} custom-call(bf16[512,512]{1,0:T(8,128)(2,1)} %get-tuple-element.2848.refs_0_.refs_4_, bf16[512,512]{1,0:T(8,128)(2,1)} %get-tuple-element.2793.refs_1_, bf16[512,512]{1,0:T(8,128)(2,1)} %get-tuple-element.2845.refs_2_.refs_1_.refs_3_, bf16[512,512]{1,0:T(8,128)(2,1)} %get-tuple-element.2796.refs_2_.refs_3_, ...), custom_call_target="tpu_custom_call" | custom-call | flops 1 | bytes 1 | tf_op jit(solution)/shard_map/back_to_rows/pallas_call | solution.py:842
  816.3 11.1 %whole_columns.4 = f32[512,6144]{1,0:T(8,128)} custom-call(s32[1]{0:T(128)} %bitcast.21.me_ref, bf16[2048,768]{1,0:T(8,128)(2,1)} %copy-done.19, bf16[2048,768]{1,0:T(8,128)(2,1)} %collective-permute-done.60.other_ref), custom_call_target="tpu_custom_call" | custom-call | flops 1 | bytes 1 | tf_op jit(solution)/shard_map/whole_columns/pallas_call | solution.py:431
  847.9 17.8 %whole_columns.5 = (f32[512,6144]{1,0:T(8,128)}, f32[512,6144]{1,0:T(8,128)}) custom-call(s32[1]{0:T(128)} %bitcast.21.me_ref, bf16[2048,1536]{1,0:T(8,128)(2,1)} %constant_dynamic-update-slice_fusion.9.own_ref, bf16[2048,1536]{1,0:T(8,128)(2,1)} %collective-permute-done.70.other_ref), custom_call_target="tpu_custom_call" | custom-call | flops 1 | bytes 1 | tf_op jit(solution)/shard_map/whole_columns/pallas_call | solution.py:431
  871.2 12.8 %collective-permute-start.84 = (bf16[512,256]{1,0:T(8,128)(2,1)S(1)}, bf16[512,256]{1,0:T(8,128)(2,1)S(1)}, u32[]{:S(2)}, u32[]{:S(2)}) collective-permute-start(bf16[512,256]{1,0:T(8,128)(2,1)S(1)} %get-tuple-element.3115), channel_id=1, source_target_pairs={{0,3},{1,0},{2,1},{3,2},{4,7},{5,4},{6,5},{7,6},{8,11},{9,8},{10,9... | collective-permute-start | bytes 786440 | tf_op jit(solution)/shard_map/ppermute | solution.py:323
  892.9 12.0 %collective-permute-done.83 = bf16[512,256]{1,0:T(8,128)(2,1)S(1)} collective-permute-done((bf16[512,256]{1,0:T(8,128)(2,1)S(1)}, bf16[512,256]{1,0:T(8,128)(2,1)S(1)}, u32[]{:S(2)}, u32[]{:S(2)}) %collective-permute-start.83) | collective-permute-done | bytes 262176 | tf_op jit(solution)/shard_map/ppermute | solution.py:323
  955.6 9.0 whole_columns.6
  (636 shorter events, 441.5 us)
Async XLA Ops:
  7.2 144.7 %all-gather.3.cloned.1.call-start = ((), (), s32[]{:S(2)}) async-start(), calls=%async_computation.2 | async-start | bytes 1310720 | tf_op jit(solution)/shard_map/all_gather | solution.py:903
  61.2 66.4 %collective-permute-start.6 = (bf16[1536,512]{1,0:T(8,128)(2,1)S(1)}, bf16[1536,512]{1,0:T(8,128)(2,1)}, u32[]{:S(2)}, u32[]{:S(2)}) collective-permute-start(bf16[1536,512]{1,0:T(8,128)(2,1)S(1)} %pad_maximum_fusion.8.came0.refs_9_), channel_id=1, source_target_pairs={{0,4},{4,0},{8,12},{12,8},{16,20},{20,16},{24,28},{28,24},{1,5},{5... | collective-permute-start | bytes 4718600 | tf_op jit(solution)/shard_map/ppermute | solution.py:318
  61.2 66.3 %collective-permute-start.5 = (bf16[1536,512]{1,0:T(8,128)(2,1)S(1)}, bf16[1536,512]{1,0:T(8,128)(2,1)}, u32[]{:S(2)}, u32[]{:S(2)}) collective-permute-start(bf16[1536,512]{1,0:T(8,128)(2,1)S(1)} %pad_maximum_fusion.8.came0.refs_9_), channel_id=1, source_target_pairs={{0,16},{4,20},{8,24},{12,28},{16,0},{20,4},{24,8},{28,12},{1,17},{... | collective-permute-start | bytes 4718600 | tf_op jit(solution)/shard_map/ppermute | solution.py:318
  62.8 64.7 %collective-permute-start.4 = (bf16[1536,512]{1,0:T(8,128)(2,1)S(1)}, bf16[1536,512]{1,0:T(8,128)(2,1)}, u32[]{:S(2)}, u32[]{:S(2)}) collective-permute-start(bf16[1536,512]{1,0:T(8,128)(2,1)S(1)} %pad_maximum_fusion.8.came0.refs_9_), channel_id=1, source_target_pairs={{0,8},{4,12},{8,0},{12,4},{16,24},{20,28},{24,16},{28,20},{1,9},{5... | collective-permute-start | bytes 4718600 | tf_op jit(solution)/shard_map/ppermute | solution.py:318
  74.3 53.2 %collective-permute-start.8 = (bf16[256,2048]{1,0:T(8,128)(2,1)S(1)}, bf16[256,2048]{1,0:T(8,128)(2,1)}, u32[]{:S(2)}, u32[]{:S(2)}) collective-permute-start(bf16[256,2048]{1,0:T(8,128)(2,1)S(1)} %get-tuple-element.1558), channel_id=1, source_target_pairs={{0,1},{1,0},{2,5},{3,4},{4,3},{5,2},{6,7},{7,6},{8,9},{9,8},{10,13... | collective-permute-start | bytes 3145736 | tf_op jit(solution)/shard_map/ppermute | solution.py:388
  77.3 289.2 %all-gather.5.cloned.1.call-start = ((), (), s32[]{:S(2)}) async-start(), calls=%async_computation.3 | async-start | bytes 11796480 | tf_op jit(solution)/shard_map/all_gather | solution.py:995
  155.6 31.5 %collective-permute-start.13 = (bf16[1536,512]{1,0:T(8,128)(2,1)S(1)}, bf16[1536,512]{1,0:T(8,128)(2,1)S(1)}, u32[]{:S(2)}, u32[]{:S(2)}) collective-permute-start(bf16[1536,512]{1,0:T(8,128)(2,1)S(1)} %constant_dynamic-update-slice_fusion.came0.refs_21_), channel_id=1, source_target_pairs={{0,4},{4,0},{8,12},{12,8},{16,20},{20,16},{24,28},{28,24},{1,5},{5... | collective-permute-start | bytes 4718600 | tf_op jit(solution)/shard_map/ppermute | solution.py:318
  155.7 31.4 %collective-permute-start.15 = (bf16[256,2048]{1,0:T(8,128)(2,1)}, bf16[256,2048]{1,0:T(8,128)(2,1)S(1)}, u32[]{:S(2)}, u32[]{:S(2)}) collective-permute-start(bf16[256,2048]{1,0:T(8,128)(2,1)} %get-tuple-element.1589), channel_id=1, source_target_pairs={{0,1},{1,0},{2,5},{3,4},{4,3},{5,2},{6,7},{7,6},{8,9},{9,8},{10,13... | collective-permute-start | bytes 3145736 | tf_op jit(solution)/shard_map/ppermute | solution.py:388
  188.9 409.9 %reduce-scatter.3.cloned.1.call-start = ((), (), s32[]{:S(2)}) async-start(), calls=%async_computation.4 | async-start | bytes 3932160 | tf_op jit(solution)/shard_map/reduce_scatter | solution.py:1111
  190.1 34.4 %collective-permute-start.24 = (bf16[2048,256]{1,0:T(8,128)(2,1)}, bf16[2048,256]{1,0:T(8,128)(2,1)}, u32[]{:S(2)}, u32[]{:S(2)}) collective-permute-start(bf16[2048,256]{1,0:T(8,128)(2,1)} %collective-permute-done.16.refs_6_.weight0), channel_id=1, source_target_pairs={{0,4},{4,0},{8,12},{12,8},{16,20},{20,16},{24,28},{28,24},{1,5},{5... | collective-permute-start | bytes 3145736 | tf_op jit(solution)/shard_map/ppermute | solution.py:318
  194.8 29.8 %collective-permute-start.25 = (bf16[2048,256]{1,0:T(8,128)(2,1)S(1)}, bf16[2048,256]{1,0:T(8,128)(2,1)}, u32[]{:S(2)}, u32[]{:S(2)}) collective-permute-start(bf16[2048,256]{1,0:T(8,128)(2,1)S(1)} %collective-permute-done.17.refs_8_.weight0), channel_id=1, source_target_pairs={{0,4},{4,0},{8,12},{12,8},{16,20},{20,16},{24,28},{28,24},{1,5},{5... | collective-permute-start | bytes 3145736 | tf_op jit(solution)/shard_map/ppermute | solution.py:318
  211.2 47.7 %collective-permute-start.28 = (bf16[512,2048]{1,0:T(8,128)(2,1)S(1)}, bf16[512,2048]{1,0:T(8,128)(2,1)S(1)}, u32[]{:S(2)}, u32[]{:S(2)}) collective-permute-start(bf16[512,2048]{1,0:T(8,128)(2,1)S(1)} %maximum_select_fusion.refs_5_.refs_0_), channel_id=1, source_target_pairs={{0,16},{4,20},{8,24},{12,28},{16,0},{20,4},{24,8},{28,12},{1,17},{... | collective-permute-start | bytes 6291464 | tf_op jit(solution)/shard_map/ppermute | solution.py:318
  213.8 46.6 %collective-permute-start.27 = (bf16[512,2048]{1,0:T(8,128)(2,1)S(1)}, bf16[512,2048]{1,0:T(8,128)(2,1)S(1)}, u32[]{:S(2)}, u32[]{:S(2)}) collective-permute-start(bf16[512,2048]{1,0:T(8,128)(2,1)S(1)} %maximum_select_fusion.refs_5_.refs_0_), channel_id=1, source_target_pairs={{0,8},{4,12},{8,0},{12,4},{16,24},{20,28},{24,16},{28,20},{1,9},{5... | collective-permute-start | bytes 6291464 | tf_op jit(solution)/shard_map/ppermute | solution.py:318
  286.9 45.2 %collective-permute-start.33 = (bf16[512,2048]{1,0:T(8,128)(2,1)}, bf16[512,2048]{1,0:T(8,128)(2,1)S(1)}, u32[]{:S(2)}, u32[]{:S(2)}) collective-permute-start(bf16[512,2048]{1,0:T(8,128)(2,1)} %get-tuple-element.2385.refs_0_), channel_id=1, source_target_pairs={{0,16},{4,20},{8,24},{12,28},{16,0},{20,4},{24,8},{28,12},{1,17},{... | collective-permute-start | bytes 6291464 | tf_op jit(solution)/shard_map/ppermute | solution.py:318
  288.2 45.2 %collective-permute-start.32 = (bf16[512,2048]{1,0:T(8,128)(2,1)}, bf16[512,2048]{1,0:T(8,128)(2,1)S(1)}, u32[]{:S(2)}, u32[]{:S(2)}) collective-permute-start(bf16[512,2048]{1,0:T(8,128)(2,1)} %get-tuple-element.2385.refs_0_), channel_id=1, source_target_pairs={{0,8},{4,12},{8,0},{12,4},{16,24},{20,28},{24,16},{28,20},{1,9},{5... | collective-permute-start | bytes 6291464 | tf_op jit(solution)/shard_map/ppermute | solution.py:318
  366.5 29.8 %collective-permute-start.36 = (bf16[2048,2304]{1,0:T(8,128)(2,1)}, bf16[2048,2304]{1,0:T(8,128)(2,1)}, u32[]{:S(2)}, u32[]{:S(2)}) collective-permute-start(bf16[2048,2304]{1,0:T(8,128)(2,1)} %all-gather.5.cloned.1.call-done.refs_10_.refs_11_.refs_12_.refs_4_.refs_9_), channel_id=1, source_target_pairs={{0,4},{4,0},{8,12},{12,8},{16,20},{20,16},{24,28},{28,24},{1,5},{5... | collective-permute-start | bytes 28311560 | tf_op jit(solution)/shard_map/ppermute | solution.py:318
  458.3 54.5 %collective-permute-start.38 = (bf16[512,2048]{1,0:T(8,128)(2,1)}, bf16[512,2048]{1,0:T(8,128)(2,1)}, u32[]{:S(2)}, u32[]{:S(2)}) collective-permute-start(bf16[512,2048]{1,0:T(8,128)(2,1)} %get-tuple-element.2216), channel_id=1, source_target_pairs={{0,8},{4,12},{8,0},{12,4},{16,24},{20,28},{24,16},{28,20},{1,9},{5... | collective-permute-start | bytes 6291464 | tf_op jit(solution)/shard_map/ppermute | solution.py:318
  459.9 53.0 %collective-permute-start.39 = (bf16[512,2048]{1,0:T(8,128)(2,1)}, bf16[512,2048]{1,0:T(8,128)(2,1)}, u32[]{:S(2)}, u32[]{:S(2)}) collective-permute-start(bf16[512,2048]{1,0:T(8,128)(2,1)} %get-tuple-element.2217), channel_id=1, source_target_pairs={{0,16},{4,20},{8,24},{12,28},{16,0},{20,4},{24,8},{28,12},{1,17},{... | collective-permute-start | bytes 6291464 | tf_op jit(solution)/shard_map/ppermute | solution.py:318
  512.8 30.6 %collective-permute-start.40 = (bf16[2048,1536]{1,0:T(8,128)(2,1)}, bf16[2048,1536]{1,0:T(8,128)(2,1)}, u32[]{:S(2)}, u32[]{:S(2)}) collective-permute-start(bf16[2048,1536]{1,0:T(8,128)(2,1)} %row_outer.14), channel_id=1, source_target_pairs={{0,4},{4,0},{8,12},{12,8},{16,20},{20,16},{24,28},{28,24},{1,5},{5... | collective-permute-start | bytes 18874376 | tf_op jit(solution)/shard_map/ppermute | solution.py:318
  512.9 198.3 %reduce-scatter.5.cloned.1.call-start = ((), (), s32[]{:S(2)}) async-start(), calls=%async_computation.5 | async-start | bytes 7864320 | tf_op jit(solution)/shard_map/reduce_scatter | solution.py:1179
  543.4 55.4 %collective-permute-start.43 = (bf16[512,2048]{1,0:T(8,128)(2,1)}, bf16[512,2048]{1,0:T(8,128)(2,1)}, u32[]{:S(2)}, u32[]{:S(2)}) collective-permute-start(bf16[512,2048]{1,0:T(8,128)(2,1)} %get-tuple-element.2400), channel_id=1, source_target_pairs={{0,8},{4,12},{8,0},{12,4},{16,24},{20,28},{24,16},{28,20},{1,9},{5... | collective-permute-start | bytes 6291464 | tf_op jit(solution)/shard_map/ppermute | solution.py:318
  544.9 53.9 %collective-permute-start.44 = (bf16[512,2048]{1,0:T(8,128)(2,1)}, bf16[512,2048]{1,0:T(8,128)(2,1)}, u32[]{:S(2)}, u32[]{:S(2)}) collective-permute-start(bf16[512,2048]{1,0:T(8,128)(2,1)} %get-tuple-element.2401), channel_id=1, source_target_pairs={{0,16},{4,20},{8,24},{12,28},{16,0},{20,4},{24,8},{28,12},{1,17},{... | collective-permute-start | bytes 6291464 | tf_op jit(solution)/shard_map/ppermute | solution.py:318
  598.8 36.1 %collective-permute-start.47 = (bf16[2048,1024]{1,0:T(8,128)(2,1)}, bf16[2048,1024]{1,0:T(8,128)(2,1)S(1)}, u32[]{:S(2)}, u32[]{:S(2)}) collective-permute-start(bf16[2048,1024]{1,0:T(8,128)(2,1)} %row_outer.15), channel_id=1, source_target_pairs={{0,4},{4,0},{8,12},{12,8},{16,20},{20,16},{24,28},{28,24},{1,5},{5... | collective-permute-start | bytes 12582920 | tf_op jit(solution)/shard_map/ppermute | solution.py:318
  603.8 31.1 %collective-permute-start.46 = (bf16[256,2048]{1,0:T(8,128)(2,1)}, bf16[256,2048]{1,0:T(8,128)(2,1)S(1)}, u32[]{:S(2)}, u32[]{:S(2)}) collective-permute-start(bf16[256,2048]{1,0:T(8,128)(2,1)} %get-tuple-element.3063), channel_id=1, source_target_pairs={{0,16},{4,20},{8,24},{12,28},{16,0},{20,4},{24,8},{28,12},{1,17},{... | collective-permute-start | bytes 3145736 | tf_op jit(solution)/shard_map/ppermute | solution.py:318
  725.7 40.8 %collective-permute-start.64 = (bf16[2048,2048]{1,0:T(8,128)(2,1)}, bf16[2048,2048]{1,0:T(8,128)(2,1)}, u32[]{:S(2)}, u32[]{:S(2)}) collective-permute-start(bf16[2048,2048]{1,0:T(8,128)(2,1)} %row_outer.19), channel_id=1, source_target_pairs={{0,4},{4,0},{8,12},{12,8},{16,20},{20,16},{24,28},{28,24},{1,5},{5... | collective-permute-start | bytes 25165832 | tf_op jit(solution)/shard_map/ppermute | solution.py:318
  725.7 40.8 %collective-permute-start.62 = (bf16[512,1536]{1,0:T(8,128)(2,1)}, bf16[512,1536]{1,0:T(8,128)(2,1)}, u32[]{:S(2)}, u32[]{:S(2)}) collective-permute-start(bf16[512,1536]{1,0:T(8,128)(2,1)} %reduce-scatter.5.cloned.1.call-done), channel_id=1, source_target_pairs={{0,16},{4,20},{8,24},{12,28},{16,0},{20,4},{24,8},{28,12},{1,17},{... | collective-permute-start | bytes 4718600 | tf_op jit(solution)/shard_map/ppermute | solution.py:318
  726.4 40.1 %collective-permute-start.61 = (bf16[512,1536]{1,0:T(8,128)(2,1)}, bf16[512,1536]{1,0:T(8,128)(2,1)}, u32[]{:S(2)}, u32[]{:S(2)}) collective-permute-start(bf16[512,1536]{1,0:T(8,128)(2,1)} %reduce-scatter.5.cloned.1.call-done), channel_id=1, source_target_pairs={{0,8},{4,12},{8,0},{12,4},{16,24},{20,28},{24,16},{28,20},{1,9},{5... | collective-permute-start | bytes 4718600 | tf_op jit(solution)/shard_map/ppermute | solution.py:318
  729.4 36.2 %collective-permute-start.63 = (bf16[256,2048]{1,0:T(8,128)(2,1)}, bf16[256,2048]{1,0:T(8,128)(2,1)}, u32[]{:S(2)}, u32[]{:S(2)}) collective-permute-start(bf16[256,2048]{1,0:T(8,128)(2,1)} %get-tuple-element.3060), channel_id=1, source_target_pairs={{0,0},{1,1},{4,2},{5,3},{2,4},{3,5},{6,6},{7,7},{8,8},{9,9},{12,10... | collective-permute-start | bytes 3145736 | tf_op jit(solution)/shard_map/ppermute | solution.py:395
  768.9 34.3 %collective-permute-start.66 = (bf16[256,1536]{1,0:T(8,128)(2,1)S(1)}, bf16[256,1536]{1,0:T(8,128)(2,1)S(1)}, u32[]{:S(2)}, u32[]{:S(2)}) collective-permute-start(bf16[256,1536]{1,0:T(8,128)(2,1)S(1)} %slice.155), channel_id=1, source_target_pairs={{0,8},{4,12},{8,0},{12,4},{16,24},{20,28},{24,16},{28,20},{1,9},{5... | collective-permute-start | bytes 2359304 | tf_op jit(solution)/shard_map/ppermute | solution.py:318
  769.5 33.7 %collective-permute-start.65 = (bf16[256,1536]{1,0:T(8,128)(2,1)S(1)}, bf16[256,1536]{1,0:T(8,128)(2,1)S(1)}, u32[]{:S(2)}, u32[]{:S(2)}) collective-permute-start(bf16[256,1536]{1,0:T(8,128)(2,1)S(1)} %slice.154), channel_id=1, source_target_pairs={{0,16},{4,20},{8,24},{12,28},{16,0},{20,4},{24,8},{28,12},{1,17},{... | collective-permute-start | bytes 2359304 | tf_op jit(solution)/shard_map/ppermute | solution.py:318
  770.8 32.3 %collective-permute-start.68 = (bf16[512,256]{1,0:T(8,128)(2,1)S(1)}, bf16[512,256]{1,0:T(8,128)(2,1)S(1)}, u32[]{:S(2)}, u32[]{:S(2)}) collective-permute-start(bf16[512,256]{1,0:T(8,128)(2,1)S(1)} %get-tuple-element.2860), channel_id=1, source_target_pairs={{0,3},{1,0},{2,1},{3,2},{4,7},{5,4},{6,5},{7,6},{8,11},{9,8},{10,9... | collective-permute-start | bytes 786440 | tf_op jit(solution)/shard_map/ppermute | solution.py:323
  836.5 32.9 %collective-permute-start.79 = (bf16[256,2048]{1,0:T(8,128)(2,1)S(1)}, bf16[256,2048]{1,0:T(8,128)(2,1)S(1)}, u32[]{:S(2)}, u32[]{:S(2)}) collective-permute-start(bf16[256,2048]{1,0:T(8,128)(2,1)S(1)} %get-tuple-element.3057), channel_id=1, source_target_pairs={{1,0},{0,1},{5,2},{4,3},{3,4},{2,5},{7,6},{6,7},{9,8},{8,9},{13,10... | collective-permute-start | bytes 3145736 | tf_op jit(solution)/shard_map/ppermute | solution.py:395
  (201 other events, 2290.1 us)
Sparse Core Ops, SparseCore 0:
  77.4 47.1 all-gather.2
  189.1 177.3 all-gather.4
  513.0 57.2 reduce-scatter.2
  599.0 107.9 reduce-scatter.4

commit v14 on v12

--- a/solution.py
+++ b/solution.py
@@ -607,21 +607,54 @@
     gain_part[...] = total
 
 
-def vmem_call(body, outs, scratch=(), scalars=0, name=None):
+class Late:
+    def __init__(self, ref, copy):
+        self.ref, self.copy, self.shape = ref, copy, ref.shape
+
+    def wait(self):
+        if self.copy is not None:
+            self.copy.wait()
+            self.copy = None
+
+    def __getitem__(self, at):
+        self.wait()
+        return self.ref[at]
+
+
+def vmem_call(body, outs, scratch=(), scalars=0, name=None, order=None):
     def call(*args):
-        in_specs = [
-            pl.BlockSpec(memory_space=pltpu.SMEM if i < scalars else pltpu.VMEM)
-            for i in range(len(args))
-        ]
+        count = len(args) - scalars
+
+        def late_body(*refs):
+            held = refs[len(args) + len(outs) : len(args) + len(outs) + count]
+            sems = refs[-1]
+            late = [
+                Late(held[i], pltpu.make_async_copy(refs[scalars + i], held[i], sems.at[i]))
+                for i in range(count)
+            ]
+            for i in order or range(count):
+                late[i].copy.start()
+            body(
+                *refs[:scalars], *late, *refs[len(args) : len(args) + len(outs)],
+                *refs[len(args) + len(outs) + count : -1],
+            )
+            for one in late:
+                one.wait()
+
         return pl.pallas_call(
-            body,
+            late_body,
             grid=(1,),
             out_shape=outs,
-            in_specs=in_specs,
-            out_specs=jax.tree.map(lambda _: pl.BlockSpec(memory_space=pltpu.VMEM), outs),
-            scratch_shapes=scratch,
+            in_specs=[pl.BlockSpec(memory_space=pltpu.SMEM)] * scalars
+            + [pl.BlockSpec(memory_space=pl.ANY)] * count,
+            out_specs=[pl.BlockSpec(memory_space=pltpu.VMEM)] * len(outs),
+            scratch_shapes=[
+                *(pltpu.VMEM(a.shape, a.dtype) for a in args[scalars:]),
+                *scratch,
+                pltpu.SemaphoreType.DMA((count,)),
+            ],
             compiler_params=pltpu.CompilerParams(vmem_limit_bytes=VMEM_BYTES),
-        cost_estimate=FREE,
+            cost_estimate=FREE,
             name=name,
         )(*args)
 
@@ -635,9 +668,27 @@
     rows, cut = sum(heights), units // 3
 
     def body(*refs):
-        gate_w, up_w, w_down, act, grad_gate, grad_up = refs[2 * count :]
+        gate_w, up_w, w_down, act, grad_gate, grad_up = refs[2 * count : 2 * count + 6]
+        held, sems = refs[2 * count + 6 : -1], refs[-1]
+        copies = [
+            pltpu.make_async_copy(refs[i], held[i], sems.at[i]) for i in range(2 * count)
+        ]
+        first = pl.program_id(0) == 0
+
+        @pl.when(first)
+        def _():
+            for i in range(count):
+                copies[i].start()
+                copies[count + i].start()
+
         start = 0
-        for mid, grad_y in zip(refs[:count], refs[count : 2 * count]):
+        for i, (mid, grad_y) in enumerate(zip(held[:count], held[count:])):
+
+            @pl.when(first)
+            def _(i=i):
+                copies[i].wait()
+                copies[count + i].wait()
+
             at = slice(start, start + mid.shape[0])
             start += mid.shape[0]
             gate = jnp.dot(mid[...], gate_w[...], preferred_element_type=jnp.float32)
@@ -650,21 +701,21 @@
             grad_gate[at, :] = slope.astype(jnp.bfloat16)
             grad_up[at, :] = (grad_act * swish).astype(jnp.bfloat16)
 
-    row_specs = [
-        pl.BlockSpec((h, width), lambda j: (0, 0), pipeline_mode=pl.Buffered(1)) for h in heights
-    ]
     return pl.pallas_call(
         body,
         grid=(3,),
         out_shape=[jax.ShapeDtypeStruct((rows, units), jnp.bfloat16)] * 3,
         in_specs=[
-            *row_specs,
-            *row_specs,
+            *(pl.BlockSpec(memory_space=pl.ANY) for _ in range(2 * count)),
             pl.BlockSpec((width, cut), lambda j: (0, j)),
             pl.BlockSpec((width, cut), lambda j: (0, j + 3)),
             pl.BlockSpec((width, cut), lambda j: (0, j + 6)),
         ],
         out_specs=[pl.BlockSpec((rows, cut), lambda j: (0, j))] * 3,
+        scratch_shapes=[
+            *(pltpu.VMEM((h, width), jnp.bfloat16) for h in heights + heights),
+            pltpu.SemaphoreType.DMA((2 * count,)),
+        ],
         compiler_params=pltpu.CompilerParams(vmem_limit_bytes=VMEM_BYTES),
         cost_estimate=FREE,
         name="hidden_units",
@@ -915,7 +966,6 @@
 
     grad_y_sent = [to_sequence(cut, turn) for turn, cut in enumerate(s.cotangent_cuts)]
     s.came_far = far(*s.came_near)
-    s.came_other = [s.came_own, *(across(block, CORE) for block in s.came_near)]
     gains = rolled(s.gains.astype(full))
     s.mlp_gains = gains[1:]
     s.attn_gains = gains[:1]
@@ -940,7 +990,7 @@
     s.cosine, sine = cosine[0, :, 0], sine[0, :, 0]
     s.sine = jnp.concatenate([-sine[:, : head_dim // 2], sine[:, head_dim // 2 :]], 1)
     s.out_own = out_own
-    del s.gains, s.x_came, s.other_lengths, s.cotangent_cuts, s.came_own
+    del s.gains, s.x_came, s.other_lengths, s.cotangent_cuts
     s.end()
 
     head_columns = 2 * head_dim
@@ -961,6 +1011,7 @@
         + [pltpu.VMEM((rows, block_columns), low)],
         scalars=1,
         name="attend_back",
+        order=(4, 5, 0, 1, 2, 3, 7, 8, 9, 10, 6),
     )
     finish = vmem_call(finish_body, [quad_rows, quad_rows, gain_sum], name="finish")
     upward = [(i, i + 1) for i in range(0, count, 2)]
@@ -981,15 +1032,10 @@
     came_last = jnp.concatenate(s.came_far, 0)
     s.came_last = (came_last, across(came_last, CORE))
     s.out_near = near(s.out_own)
-    s.out_own_other = across(s.out_own, CORE)
-    s.projected = in_order(
-        [
-            project_call(i, block, other)
-            for i, (block, other) in enumerate(zip((s.came, *s.came_near), s.came_other))
-        ]
-    )
+    s.came_other = [s.came_own, *(across(block, CORE) for block in s.came_near)]
+    s.projected = in_order([project_call(0, s.came, s.came_own)])
     s.grad_y_came = grad_y_sent
-    del s.came_far
+    del s.came_far, s.came_own
     s.end()
 
     ffn_own = lax.all_gather(s.ffn_block, "shard", axis=0, tiled=True)
@@ -997,39 +1043,44 @@
     s.grad_y = jnp.where(s.valid > 0, grad_y, jnp.zeros_like(grad_y))
     grad_y_near = near(s.grad_y)
     s.out_far = far(*s.out_near)
+    s.out_own_other = across(s.out_own, CORE)
     s.out_near_other = [across(block, CORE) for block in s.out_near]
-    s.earlier = [lax.ppermute(p[2], "rep", upward) for p in s.projected]
-    (s.projected_last,) = in_order([project_call(3, *s.came_last)])
+    s.earlier = [lax.ppermute(s.projected[0][2], "rep", upward)]
+    s.projected = s.projected + in_order(
+        [
+            project_call(1, s.came_near[0], s.came_other[1]),
+            project_call(2, s.came_near[1], s.came_other[2]),
+            project_call(3, *s.came_last),
+        ]
+    )
     del s.ffn_block, s.grad_y_came
     s.end()
 
     out_last = jnp.concatenate(s.out_far, 0)
     s.out_last = (out_last, across(out_last, CORE))
-    s.earlier_last = lax.ppermute(s.projected_last[2], "rep", upward)
-    s.attended = in_order([attend_call(*pair) for pair in zip(s.projected, s.earlier)])
-    s.grad_y_near = grad_y_near
+    s.earlier = s.earlier + [lax.ppermute(p[2], "rep", upward) for p in s.projected[1:]]
+    s.attended = in_order([attend_call(s.projected[0], s.earlier[0])])
     del s.out_far
     s.end()
 
-    s.projected = [*s.projected, s.projected_last]
-    s.earlier = [*s.earlier, s.earlier_last]
     s.out_blocks = [
         s.out_own, s.out_own_other, s.out_near[0], s.out_near_other[0], s.out_near[1],
         s.out_near_other[1], *s.out_last,
     ]
-    (last,) = in_order([attend_call(s.projected_last, s.earlier_last)])
-    s.attended = [*s.attended, last]
+    s.attended = s.attended + in_order(
+        [attend_call(s.projected[i], s.earlier[i]) for i in (1, 2, 3)]
+    )
     s.mixed = [a[0] for a in s.attended]
     s.resid, s.mid = close_attention(s.x_low, s.mixed, s.out_blocks, s.mlp_gains)
-    s.grad_y_far = far(*s.grad_y_near)
+    s.grad_y_near = grad_y_near
     s.came = [s.came, *s.came_near, s.came_last[0]]
     s.came_other = [*s.came_other, s.came_last[1]]
     del s.came_near, s.came_last
     del s.out_own, s.out_own_other, s.out_near, s.out_near_other, s.out_last
-    del s.projected_last, s.earlier_last
     s.end()
 
     s.mid_near = near(s.mid)
+    s.grad_y_far = far(*s.grad_y_near)
     s.end()
 
     s.mid_far = far(*s.mid_near)

time: 989 us -> 1020 us (1.031)
  starting transfers between devices: 133 us -> 157 us
  Pallas kernels: 425 us -> 442 us
    ppermute x73, starting transfers between devices: 68.7 us -> 98.8 us  [across(): return lax.ppermute(x, 'rep', [(i, i ^ mask) for i in range(count)])]
    ppermute x4, starting transfers between devices: 24.2 us -> 11.1 us  [to_sequence(): return lax.ppermute(cut, ('rep', 'shard'), sequence_pairs(turn))]
    pallas_call x2, Pallas kernels: 60.1 us -> 70.6 us  [hidden_units(): pl.pallas_call(body, grid=(3,), out_shape=[jax.ShapeDtypeStruct((rows, un...]
  transfers between devices with their start and end apart: 107 -> 107, of which waited for: 41 -> 35; matrix products, arithmetic and copies ran while one was open for 9% -> 8% of each run, Pallas kernels for 38% -> 38%
where the time goes in v14:
time: 1020 us; the launch traced here: 1010 us
  Pallas kernels  442 us (43%)
  waiting for transfers between devices  269 us (26%)
  starting transfers between devices  157 us (15%)
  local copies, waits for them, and re-layouts  67.9 us (7%)
  other arithmetic  60.7 us (6%)
  between operations  16.3 us (2%)
    ppermute x73, waiting for transfers between devices, across(): return lax.ppermute(x, 'rep', [(i, i ^ mask) for i in range(count)])  168 us
    pallas_call x16, Pallas kernels, call(): pl.pallas_call(late_body, grid=(1,), out_shape=outs, in_specs=[pl.BlockSp...  126 us
    pallas_call x12, Pallas kernels, row_outer(): pl.pallas_call(body, grid=(tiles,), out_shape=[jax.ShapeDtypeStruct((tile...  114 us
    ppermute x73, starting transfers between devices, across(): return lax.ppermute(x, 'rep', [(i, i ^ mask) for i in range(count)])  98.8 us
    pallas_call x2, Pallas kernels, hidden_units(): pl.pallas_call(body, grid=(3,), out_shape=[jax.ShapeDtypeStruct((rows, un...  70.6 us
    pallas_call x4, Pallas kernels, from_hidden(): pl.pallas_call(body, grid=(4,), out_shape=[jax.ShapeDtypeStruct((2 * rows...  59.4 us
    ppermute x4, waiting for transfers between devices, to_sequence(): return lax.ppermute(cut, ('rep', 'shard'), sequence_pairs(turn))  50.8 us
    pallas_call x4, Pallas kernels, whole_columns(): pl.pallas_call(body, grid_spec=pltpu.PrefetchScalarGridSpec(num_scalar_pr...  44.4 us
  transfers between devices with their start and end apart: 107, of which 35 were waited for; matrix products, arithmetic and copies ran while one was open for 8% of the time, Pallas kernels for 38%

profile of v14, /device:TPU:0, one launch (start us, length us, event | category | flops | bytes accessed | tf_op | source)
XLA Modules:
  0.0 1012.3 jit_solution(5626462474958410215)
XLA Ops:
  33.2 10.3 %collective-permute-done = bf16[528,512]{1,0:T(8,128)(2,1)} collective-permute-done((bf16[528,512]{1,0:T(8,128)(2,1)}, bf16[528,512]{1,0:T(8,128)(2,1)}, u32[]{:S(2)}, u32[]{:S(2)}) %collective-permute-start) | collective-permute-done | bytes 540704 | tf_op jit(solution)/shard_map/ppermute | solution.py:323
  45.1 13.5 %collective-permute-done.3 = bf16[528,512]{1,0:T(8,128)(2,1)S(1)} collective-permute-done((bf16[528,512]{1,0:T(8,128)(2,1)}, bf16[528,512]{1,0:T(8,128)(2,1)S(1)}, u32[]{:S(2)}, u32[]{:S(2)}) %collective-permute-start.3) | collective-permute-done | bytes 540704 | tf_op jit(solution)/shard_map/ppermute | solution.py:323
  64.9 9.5 collective-permute-start.7
  78.8 49.0 %collective-permute-done.8 = bf16[256,2048]{1,0:T(8,128)(2,1)} collective-permute-done((bf16[256,2048]{1,0:T(8,128)(2,1)}, bf16[256,2048]{1,0:T(8,128)(2,1)}, u32[]{:S(2)}, u32[]{:S(2)}) %collective-permute-start.8) | collective-permute-done | bytes 1048608 | tf_op jit(solution)/shard_map/ppermute | solution.py:388
  176.8 19.2 %collective-permute-start.21 = (bf16[2048,256]{1,0:T(8,128)(2,1)}, bf16[2048,256]{1,0:T(8,128)(2,1)}, u32[]{:S(2)}, u32[]{:S(2)}) collective-permute-start(bf16[2048,256]{1,0:T(8,128)(2,1)} %collective-permute-done.16.refs_6_), channel_id=1, source_target_pairs={{0,4},{4,0},{8,12},{12,8},{16,20},{20,16},{24,28},{28,24},{1,5},{5... | collective-permute-start | bytes 3145736 | tf_op jit(solution)/shard_map/ppermute | solution.py:318
  202.2 8.3 collective-permute-done.20
  270.4 11.7 %close_attention.1 = (f32[512,2048]{1,0:T(8,128)}, bf16[512,2048]{1,0:T(8,128)(2,1)}) custom-call(bf16[512,2048]{1,0:T(8,128)(2,1)} %pad_maximum_fusion.3.x, bf16[512,512]{1,0:T(8,128)(2,1)} %get-tuple-element.2397.refs_0_.refs_1_.refs_4_, bf16[512,512]{1,0:T(8,128)(2,1)} %get-tuple-element.2394.refs_1_.refs_2_.refs_3_, ...), custom_call_target="tpu_custom_call" | custom-call | flops 1 | bytes 1 | tf_op jit(solution)/shard_map/close_attention/pallas_call | solution.py:840
  286.6 64.6 %collective-permute-done.31.refs_9_.refs_4_ = bf16[256,2048]{1,0:T(8,128)(2,1)S(1)} collective-permute-done((bf16[256,2048]{1,0:T(8,128)(2,1)S(1)}, bf16[256,2048]{1,0:T(8,128)(2,1)S(1)}, u32[]{:S(2)}, u32[]{:S(2)}) %collective-permute-start.31) | collective-permute-done | bytes 1048608 | tf_op jit(solution)/shard_map/ppermute | solution.py:318
  355.9 20.0 %collective-permute-done.35.refs_4_ = bf16[256,2048]{1,0:T(8,128)(2,1)S(1)} collective-permute-done((bf16[256,2048]{1,0:T(8,128)(2,1)S(1)}, bf16[256,2048]{1,0:T(8,128)(2,1)S(1)}, u32[]{:S(2)}, u32[]{:S(2)}) %collective-permute-start.35) | collective-permute-done | bytes 1048608 | tf_op jit(solution)/shard_map/ppermute | solution.py:318
  377.3 35.1 %hidden_units.2 = (bf16[2048,768]{1,0:T(8,128)(2,1)}, bf16[2048,768]{1,0:T(8,128)(2,1)}, bf16[2048,768]{1,0:T(8,128)(2,1)}) custom-call(bf16[512,2048]{1,0:T(8,128)(2,1)} %get-tuple-element.2269.refs_0_, bf16[512,2048]{1,0:T(8,128)(2,1)} %copy-done.12, bf16[512,2048]{1,0:T(8,128)(2,1)} %copy-done.11, bf16[256,2048]{1,0:T(8,128)(2,1)} %copy-done.23, ...), custom_call_target="tpu_custom_call" | custom-call | flops 1 | bytes 1 | tf_op jit(solution)/shard_map/hidden_units/pallas_call | solution.py:704
  412.4 35.5 %hidden_units.3 = (bf16[2048,768]{1,0:T(8,128)(2,1)}, bf16[2048,768]{1,0:T(8,128)(2,1)}, bf16[2048,768]{1,0:T(8,128)(2,1)}) custom-call(bf16[512,2048]{1,0:T(8,128)(2,1)} %get-tuple-element.2269.refs_0_, bf16[512,2048]{1,0:T(8,128)(2,1)} %copy-done.12, bf16[512,2048]{1,0:T(8,128)(2,1)} %copy-done.11, bf16[256,2048]{1,0:T(8,128)(2,1)} %copy-done.23, ...), custom_call_target="tpu_custom_call" | custom-call | flops 1 | bytes 1 | tf_op jit(solution)/shard_map/hidden_units/pallas_call | solution.py:704
  448.0 12.6 %row_outer.12 = bf16[2048,768]{1,0:T(8,128)(2,1)} custom-call(bf16[512,2048]{1,0:T(8,128)(2,1)} %copy-done.6, bf16[512,2048]{1,0:T(8,128)(2,1)} %copy-done.14, bf16[512,2048]{1,0:T(8,128)(2,1)} %copy-done.13, bf16[256,2048]{1,0:T(8,128)(2,1)} %copy-done.25, bf16[256,2048]{1,0:T(8,128)(2,1)} %copy-done.24, ...), custom_call_target="tpu_custom_call" | custom-call | flops 6442450944 | bytes 11534336 | tf_op jit(solution)/shard_map/row_outer/pallas_call | solution.py:790
  460.6 18.9 %from_hidden.4 = (bf16[512,2048]{1,0:T(8,128)(2,1)}, bf16[512,2048]{1,0:T(8,128)(2,1)}) custom-call(bf16[2048,768]{1,0:T(8,128)(2,1)} %get-tuple-element.2280.refs_0_.refs_1_.refs_2_.refs_3_.refs_5_, bf16[2048,768]{1,0:T(8,128)(2,1)} %get-tuple-element.2280.refs_0_.refs_1_.refs_2_.refs_3_.refs_5_, ...), custom_call_target="tpu_custom_call" | custom-call | flops 1 | bytes 1 | tf_op jit(solution)/shard_map/from_hidden/pallas_call | solution.py:746
  481.6 13.2 %row_outer.13 = bf16[2048,768]{1,0:T(8,128)(2,1)} custom-call(bf16[512,2048]{1,0:T(8,128)(2,1)} %copy-done.6, bf16[512,2048]{1,0:T(8,128)(2,1)} %copy-done.14, bf16[512,2048]{1,0:T(8,128)(2,1)} %copy-done.13, bf16[256,2048]{1,0:T(8,128)(2,1)} %copy-done.25, bf16[256,2048]{1,0:T(8,128)(2,1)} %copy-done.24, ...), custom_call_target="tpu_custom_call" | custom-call | flops 6442450944 | bytes 11534336 | tf_op jit(solution)/shard_map/row_outer/pallas_call | solution.py:790
  494.9 19.0 %from_hidden.5 = (bf16[512,2048]{1,0:T(8,128)(2,1)}, bf16[512,2048]{1,0:T(8,128)(2,1)}) custom-call(bf16[2048,768]{1,0:T(8,128)(2,1)} %get-tuple-element.2280.refs_0_.refs_1_.refs_2_.refs_3_.refs_5_, bf16[2048,768]{1,0:T(8,128)(2,1)} %get-tuple-element.2280.refs_0_.refs_1_.refs_2_.refs_3_.refs_5_, ...), custom_call_target="tpu_custom_call" | custom-call | flops 1 | bytes 1 | tf_op jit(solution)/shard_map/from_hidden/pallas_call | solution.py:746
  513.8 19.3 %row_outer.14 = bf16[2048,1536]{1,0:T(8,128)(2,1)} custom-call(bf16[512,2048]{1,0:T(8,128)(2,1)} %get-tuple-element.2269.refs_0_, bf16[512,2048]{1,0:T(8,128)(2,1)} %copy-done.12, bf16[512,2048]{1,0:T(8,128)(2,1)} %copy-done.11, bf16[256,2048]{1,0:T(8,128)(2,1)} %copy-done.23, bf16[256,2048]{1,0:T(8,128)(2,1)} %copy-done.22, ...), custom_call_target="tpu_custom_call" | custom-call | flops 12884901888 | bytes 14680064 | tf_op jit(solution)/shard_map/row_outer/pallas_call | solution.py:790
  540.5 10.7 %from_hidden.6 = (bf16[512,2048]{1,0:T(8,128)(2,1)}, bf16[512,2048]{1,0:T(8,128)(2,1)}) custom-call(bf16[2048,768]{1,0:T(8,128)(2,1)} %get-tuple-element.2189.refs_5_.refs_0_.refs_1_.refs_2_.refs_3_, bf16[2048,768]{1,0:T(8,128)(2,1)} %get-tuple-element.2189.refs_5_.refs_0_.refs_1_.refs_2_.refs_3_, ...), custom_call_target="tpu_custom_call" | custom-call | flops 1 | bytes 1 | tf_op jit(solution)/shard_map/from_hidden/pallas_call | solution.py:746
  551.1 10.8 %from_hidden.7 = (bf16[512,2048]{1,0:T(8,128)(2,1)}, bf16[512,2048]{1,0:T(8,128)(2,1)}) custom-call(bf16[2048,768]{1,0:T(8,128)(2,1)} %get-tuple-element.2189.refs_5_.refs_0_.refs_1_.refs_2_.refs_3_, bf16[2048,768]{1,0:T(8,128)(2,1)} %get-tuple-element.2189.refs_5_.refs_0_.refs_1_.refs_2_.refs_3_, ...), custom_call_target="tpu_custom_call" | custom-call | flops 1 | bytes 1 | tf_op jit(solution)/shard_map/from_hidden/pallas_call | solution.py:746
  577.1 13.9 %attend_back.4 = (bf16[512,512]{1,0:T(8,128)(2,1)}, f32[512,512]{1,0:T(8,128)}, bf16[512,512]{1,0:T(8,128)(2,1)}, f32[1,128]{1,0:T(1,128)}) custom-call(s32[2]{0:T(128)} %pad_add_fusion.refs_0_, bf16[512,512]{1,0:T(8,128)(2,1)} %get-tuple-element.2236.refs_1_, bf16[512,512]{1,0:T(8,128)(2,1)} %collective-permute-done.26.refs_2_, ...), custom_call_target="tpu_custom_call" | custom-call | flops 1 | bytes 1 | tf_op jit(solution)/shard_map/attend_back/pallas_call | solution.py:644
  601.0 19.8 %row_outer.16 = bf16[2048,1536]{1,0:T(8,128)(2,1)} custom-call(bf16[512,2048]{1,0:T(8,128)(2,1)} %get-tuple-element.2269.refs_0_, bf16[512,2048]{1,0:T(8,128)(2,1)} %copy-done.12, bf16[512,2048]{1,0:T(8,128)(2,1)} %copy-done.11, bf16[256,2048]{1,0:T(8,128)(2,1)} %copy-done.23, bf16[256,2048]{1,0:T(8,128)(2,1)} %copy-done.22, ...), custom_call_target="tpu_custom_call" | custom-call | flops 12884901888 | bytes 14680064 | tf_op jit(solution)/shard_map/row_outer/pallas_call | solution.py:790
  630.0 13.5 %attend_back.5 = (bf16[512,512]{1,0:T(8,128)(2,1)}, f32[512,512]{1,0:T(8,128)}, bf16[512,512]{1,0:T(8,128)(2,1)}, f32[1,128]{1,0:T(1,128)}) custom-call(s32[2]{0:T(128)} %pad_add_fusion.refs_0_, bf16[512,512]{1,0:T(8,128)(2,1)} %get-tuple-element.2319.refs_1_, bf16[512,512]{1,0:T(8,128)(2,1)} %copy-done.37, bf16[512,512]{1,0:T(8,128)(2,1)} %get-tuple-element.2321.refs_3_, ...), custom_call_target="tpu_custom_call" | custom-call | flops 1 | bytes 1 | tf_op jit(solution)/shard_map/attend_back/pallas_call | solution.py:644
  643.5 13.8 %attend_back.6 = (bf16[512,512]{1,0:T(8,128)(2,1)}, f32[512,512]{1,0:T(8,128)}, bf16[512,512]{1,0:T(8,128)(2,1)}, f32[1,128]{1,0:T(1,128)}) custom-call(s32[2]{0:T(128)} %pad_add_fusion.refs_0_, bf16[512,512]{1,0:T(8,128)(2,1)} %get-tuple-element.2334.refs_1_, bf16[512,512]{1,0:T(8,128)(2,1)} %collective-permute-done.25.refs_2_, ...), custom_call_target="tpu_custom_call" | custom-call | flops 1 | bytes 1 | tf_op jit(solution)/shard_map/attend_back/pallas_call | solution.py:644
  674.0 13.5 %attend_back.7 = (bf16[512,512]{1,0:T(8,128)(2,1)}, f32[512,512]{1,0:T(8,128)}, bf16[512,512]{1,0:T(8,128)(2,1)}, f32[1,128]{1,0:T(1,128)}) custom-call(s32[2]{0:T(128)} %pad_add_fusion.refs_0_, bf16[512,512]{1,0:T(8,128)(2,1)} %get-tuple-element.2402.refs_1_, bf16[512,512]{1,0:T(8,128)(2,1)} %copy-done.36, bf16[512,512]{1,0:T(8,128)(2,1)} %get-tuple-element.2404.refs_3_, ...), custom_call_target="tpu_custom_call" | custom-call | flops 1 | bytes 1 | tf_op jit(solution)/shard_map/attend_back/pallas_call | solution.py:644
  707.7 15.6 %collective-permute-done.53 = bf16[1024,512]{1,0:T(8,128)(2,1)S(1)} collective-permute-done((bf16[1024,512]{1,0:T(8,128)(2,1)}, bf16[1024,512]{1,0:T(8,128)(2,1)S(1)}, u32[]{:S(2)}, u32[]{:S(2)}) %collective-permute-start.53) | collective-permute-done | bytes 1048608 | tf_op jit(solution)/shard_map/ppermute | solution.py:318
  736.6 10.2 %row_outer.19 = bf16[2048,2048]{1,0:T(8,128)(2,1)} custom-call(bf16[512,2048]{1,0:T(8,128)(2,1)} %pad_maximum_fusion.4.refs_0_, bf16[512,512]{1,0:T(8,128)(2,1)} %get-tuple-element.2598.refs_1_, bf16[512,512]{1,0:T(8,128)(2,1)} %get-tuple-element.2601.refs_2_.refs_3_, bf16[512,512]{1,0:T(8,128)(2,1)} %get-tuple-element.2604.refs_3_.refs_5_, ...), custom_call_target="tpu_custom_call" | custom-call | flops 4294967296 | bytes 4194304 | tf_op jit(solution)/shard_map/row_outer/pallas_call | solution.py:790
  748.7 15.5 %collective-permute-start.65 = (bf16[2048,2048]{1,0:T(8,128)(2,1)}, bf16[2048,2048]{1,0:T(8,128)(2,1)}, u32[]{:S(2)}, u32[]{:S(2)}) collective-permute-start(bf16[2048,2048]{1,0:T(8,128)(2,1)} %row_outer.19), channel_id=1, source_target_pairs={{0,4},{4,0},{8,12},{12,8},{16,20},{20,16},{24,28},{28,24},{1,5},{5... | collective-permute-start | bytes 25165832 | tf_op jit(solution)/shard_map/ppermute | solution.py:318
  772.3 15.8 %back_to_rows.1 = f32[512,2048]{1,0:T(8,128)} custom-call(bf16[512,512]{1,0:T(8,128)(2,1)} %get-tuple-element.2657.refs_0_.refs_4_, bf16[512,512]{1,0:T(8,128)(2,1)} %get-tuple-element.2598.refs_1_, bf16[512,512]{1,0:T(8,128)(2,1)} %get-tuple-element.2654.refs_2_.refs_1_.refs_3_, bf16[512,512]{1,0:T(8,128)(2,1)} %get-tuple-element.2601.refs_2_.refs_3_, ...), custom_call_target="tpu_custom_call" | custom-call | flops 1 | bytes 1 | tf_op jit(solution)/shard_map/back_to_rows/pallas_call | solution.py:893
  848.8 11.1 %whole_columns.4 = f32[512,6144]{1,0:T(8,128)} custom-call(s32[1]{0:T(128)} %bitcast.21.me_ref, bf16[2048,768]{1,0:T(8,128)(2,1)} %copy-done.21, bf16[2048,768]{1,0:T(8,128)(2,1)} %collective-permute-done.66.other_ref), custom_call_target="tpu_custom_call" | custom-call | flops 1 | bytes 1 | tf_op jit(solution)/shard_map/whole_columns/pallas_call | solution.py:431
  860.1 12.1 %collective-permute-done.72 = bf16[1024,512]{1,0:T(8,128)(2,1)S(1)} collective-permute-done((bf16[1024,512]{1,0:T(8,128)(2,1)}, bf16[1024,512]{1,0:T(8,128)(2,1)S(1)}, u32[]{:S(2)}, u32[]{:S(2)}) %collective-permute-start.72) | collective-permute-done | bytes 1048608 | tf_op jit(solution)/shard_map/ppermute | solution.py:318
  879.0 17.8 %whole_columns.5 = (f32[512,6144]{1,0:T(8,128)}, f32[512,6144]{1,0:T(8,128)}) custom-call(s32[1]{0:T(128)} %bitcast.21.me_ref, bf16[2048,1536]{1,0:T(8,128)(2,1)} %constant_dynamic-update-slice_fusion.9.own_ref, bf16[2048,1536]{1,0:T(8,128)(2,1)} %collective-permute-done.71.other_ref), custom_call_target="tpu_custom_call" | custom-call | flops 1 | bytes 1 | tf_op jit(solution)/shard_map/whole_columns/pallas_call | solution.py:431
  950.2 10.0 collective-permute-done.89
  983.6 9.0 whole_columns.6
  (640 shorter events, 423.1 us)
Async XLA Ops:
  7.2 136.9 %all-gather.3.cloned.1.call-start = ((), (), s32[]{:S(2)}) async-start(), calls=%async_computation.2 | async-start | bytes 1310720 | tf_op jit(solution)/shard_map/all_gather | solution.py:954
  61.2 66.6 %collective-permute-start.6 = (bf16[1536,512]{1,0:T(8,128)(2,1)S(1)}, bf16[1536,512]{1,0:T(8,128)(2,1)}, u32[]{:S(2)}, u32[]{:S(2)}) collective-permute-start(bf16[1536,512]{1,0:T(8,128)(2,1)S(1)} %pad_maximum_fusion.8.refs_2_.refs_9_), channel_id=1, source_target_pairs={{0,4},{4,0},{8,12},{12,8},{16,20},{20,16},{24,28},{28,24},{1,5},{5... | collective-permute-start | bytes 4718600 | tf_op jit(solution)/shard_map/ppermute | solution.py:318
  61.3 66.6 %collective-permute-start.5 = (bf16[1536,512]{1,0:T(8,128)(2,1)S(1)}, bf16[1536,512]{1,0:T(8,128)(2,1)}, u32[]{:S(2)}, u32[]{:S(2)}) collective-permute-start(bf16[1536,512]{1,0:T(8,128)(2,1)S(1)} %pad_maximum_fusion.8.refs_2_.refs_9_), channel_id=1, source_target_pairs={{0,16},{4,20},{8,24},{12,28},{16,0},{20,4},{24,8},{28,12},{1,17},{... | collective-permute-start | bytes 4718600 | tf_op jit(solution)/shard_map/ppermute | solution.py:318
  62.8 65.0 %collective-permute-start.4 = (bf16[1536,512]{1,0:T(8,128)(2,1)S(1)}, bf16[1536,512]{1,0:T(8,128)(2,1)}, u32[]{:S(2)}, u32[]{:S(2)}) collective-permute-start(bf16[1536,512]{1,0:T(8,128)(2,1)S(1)} %pad_maximum_fusion.8.refs_2_.refs_9_), channel_id=1, source_target_pairs={{0,8},{4,12},{8,0},{12,4},{16,24},{20,28},{24,16},{28,20},{1,9},{5... | collective-permute-start | bytes 4718600 | tf_op jit(solution)/shard_map/ppermute | solution.py:318
  74.4 53.4 %collective-permute-start.8 = (bf16[256,2048]{1,0:T(8,128)(2,1)}, bf16[256,2048]{1,0:T(8,128)(2,1)}, u32[]{:S(2)}, u32[]{:S(2)}) collective-permute-start(bf16[256,2048]{1,0:T(8,128)(2,1)} %get-tuple-element.1461), channel_id=1, source_target_pairs={{0,1},{1,0},{2,5},{3,4},{4,3},{5,2},{6,7},{7,6},{8,9},{9,8},{10,13... | collective-permute-start | bytes 3145736 | tf_op jit(solution)/shard_map/ppermute | solution.py:388
  77.4 298.9 %all-gather.5.cloned.1.call-start = ((), (), s32[]{:S(2)}) async-start(), calls=%async_computation.3 | async-start | bytes 11796480 | tf_op jit(solution)/shard_map/all_gather | solution.py:1041
  175.7 445.1 %reduce-scatter.3.cloned.1.call-start = ((), (), s32[]{:S(2)}) async-start(), calls=%async_computation.4 | async-start | bytes 3932160 | tf_op jit(solution)/shard_map/reduce_scatter | solution.py:1162
  176.8 60.3 %collective-permute-start.21 = (bf16[2048,256]{1,0:T(8,128)(2,1)}, bf16[2048,256]{1,0:T(8,128)(2,1)}, u32[]{:S(2)}, u32[]{:S(2)}) collective-permute-start(bf16[2048,256]{1,0:T(8,128)(2,1)} %collective-permute-done.16.refs_6_), channel_id=1, source_target_pairs={{0,4},{4,0},{8,12},{12,8},{16,20},{20,16},{24,28},{28,24},{1,5},{5... | collective-permute-start | bytes 3145736 | tf_op jit(solution)/shard_map/ppermute | solution.py:318
  196.1 41.1 %collective-permute-start.22 = (bf16[2048,256]{1,0:T(8,128)(2,1)S(1)}, bf16[2048,256]{1,0:T(8,128)(2,1)}, u32[]{:S(2)}, u32[]{:S(2)}) collective-permute-start(bf16[2048,256]{1,0:T(8,128)(2,1)S(1)} %collective-permute-done.17.refs_8_.refs_6_), channel_id=1, source_target_pairs={{0,4},{4,0},{8,12},{12,8},{16,20},{20,16},{24,28},{28,24},{1,5},{5... | collective-permute-start | bytes 3145736 | tf_op jit(solution)/shard_map/ppermute | solution.py:318
  211.7 70.4 %collective-permute-start.29 = (bf16[512,2048]{1,0:T(8,128)(2,1)S(1)}, bf16[512,2048]{1,0:T(8,128)(2,1)S(1)}, u32[]{:S(2)}, u32[]{:S(2)}) collective-permute-start(bf16[512,2048]{1,0:T(8,128)(2,1)S(1)} %maximum_select_fusion.refs_5_.refs_0_), channel_id=1, source_target_pairs={{0,16},{4,20},{8,24},{12,28},{16,0},{20,4},{24,8},{28,12},{1,17},{... | collective-permute-start | bytes 6291464 | tf_op jit(solution)/shard_map/ppermute | solution.py:318
  212.6 69.6 %collective-permute-start.28 = (bf16[512,2048]{1,0:T(8,128)(2,1)S(1)}, bf16[512,2048]{1,0:T(8,128)(2,1)S(1)}, u32[]{:S(2)}, u32[]{:S(2)}) collective-permute-start(bf16[512,2048]{1,0:T(8,128)(2,1)S(1)} %maximum_select_fusion.refs_5_.refs_0_), channel_id=1, source_target_pairs={{0,8},{4,12},{8,0},{12,4},{16,24},{20,28},{24,16},{28,20},{1,9},{5... | collective-permute-start | bytes 6291464 | tf_op jit(solution)/shard_map/ppermute | solution.py:318
  282.2 69.0 %collective-permute-start.33 = (bf16[512,2048]{1,0:T(8,128)(2,1)}, bf16[512,2048]{1,0:T(8,128)(2,1)S(1)}, u32[]{:S(2)}, u32[]{:S(2)}) collective-permute-start(bf16[512,2048]{1,0:T(8,128)(2,1)} %get-tuple-element.2269.refs_0_), channel_id=1, source_target_pairs={{0,16},{4,20},{8,24},{12,28},{16,0},{20,4},{24,8},{28,12},{1,17},{... | collective-permute-start | bytes 6291464 | tf_op jit(solution)/shard_map/ppermute | solution.py:318
  283.5 68.7 %collective-permute-start.32 = (bf16[512,2048]{1,0:T(8,128)(2,1)}, bf16[512,2048]{1,0:T(8,128)(2,1)S(1)}, u32[]{:S(2)}, u32[]{:S(2)}) collective-permute-start(bf16[512,2048]{1,0:T(8,128)(2,1)} %get-tuple-element.2269.refs_0_), channel_id=1, source_target_pairs={{0,8},{4,12},{8,0},{12,4},{16,24},{20,28},{24,16},{28,20},{1,9},{5... | collective-permute-start | bytes 6291464 | tf_op jit(solution)/shard_map/ppermute | solution.py:318
  284.3 66.9 %collective-permute-start.31 = (bf16[256,2048]{1,0:T(8,128)(2,1)S(1)}, bf16[256,2048]{1,0:T(8,128)(2,1)S(1)}, u32[]{:S(2)}, u32[]{:S(2)}) collective-permute-start(bf16[256,2048]{1,0:T(8,128)(2,1)S(1)} %slice.143), channel_id=1, source_target_pairs={{0,8},{4,12},{8,0},{12,4},{16,24},{20,28},{24,16},{28,20},{1,9},{5... | collective-permute-start | bytes 3145736 | tf_op jit(solution)/shard_map/ppermute | solution.py:318
  285.8 65.4 %collective-permute-start.30 = (bf16[256,2048]{1,0:T(8,128)(2,1)S(1)}, bf16[256,2048]{1,0:T(8,128)(2,1)S(1)}, u32[]{:S(2)}, u32[]{:S(2)}) collective-permute-start(bf16[256,2048]{1,0:T(8,128)(2,1)S(1)} %slice.142), channel_id=1, source_target_pairs={{0,16},{4,20},{8,24},{12,28},{16,0},{20,4},{24,8},{28,12},{1,17},{... | collective-permute-start | bytes 3145736 | tf_op jit(solution)/shard_map/ppermute | solution.py:318
  376.3 36.1 %collective-permute-start.36 = (bf16[2048,2304]{1,0:T(8,128)(2,1)}, bf16[2048,2304]{1,0:T(8,128)(2,1)}, u32[]{:S(2)}, u32[]{:S(2)}) collective-permute-start(bf16[2048,2304]{1,0:T(8,128)(2,1)} %all-gather.5.cloned.1.call-done.refs_10_.refs_11_.refs_12_.refs_4_.refs_9_), channel_id=1, source_target_pairs={{0,4},{4,0},{8,12},{12,8},{16,20},{20,16},{24,28},{28,24},{1,5},{5... | collective-permute-start | bytes 28311560 | tf_op jit(solution)/shard_map/ppermute | solution.py:318
  479.5 53.7 %collective-permute-start.38 = (bf16[512,2048]{1,0:T(8,128)(2,1)}, bf16[512,2048]{1,0:T(8,128)(2,1)}, u32[]{:S(2)}, u32[]{:S(2)}) collective-permute-start(bf16[512,2048]{1,0:T(8,128)(2,1)} %get-tuple-element.2100), channel_id=1, source_target_pairs={{0,8},{4,12},{8,0},{12,4},{16,24},{20,28},{24,16},{28,20},{1,9},{5... | collective-permute-start | bytes 6291464 | tf_op jit(solution)/shard_map/ppermute | solution.py:318
  480.9 52.3 %collective-permute-start.39 = (bf16[512,2048]{1,0:T(8,128)(2,1)}, bf16[512,2048]{1,0:T(8,128)(2,1)}, u32[]{:S(2)}, u32[]{:S(2)}) collective-permute-start(bf16[512,2048]{1,0:T(8,128)(2,1)} %get-tuple-element.2101), channel_id=1, source_target_pairs={{0,16},{4,20},{8,24},{12,28},{16,0},{20,4},{24,8},{28,12},{1,17},{... | collective-permute-start | bytes 6291464 | tf_op jit(solution)/shard_map/ppermute | solution.py:318
  533.1 31.6 %collective-permute-start.40 = (bf16[2048,1536]{1,0:T(8,128)(2,1)}, bf16[2048,1536]{1,0:T(8,128)(2,1)}, u32[]{:S(2)}, u32[]{:S(2)}) collective-permute-start(bf16[2048,1536]{1,0:T(8,128)(2,1)} %row_outer.14), channel_id=1, source_target_pairs={{0,4},{4,0},{8,12},{12,8},{16,20},{20,16},{24,28},{28,24},{1,5},{5... | collective-permute-start | bytes 18874376 | tf_op jit(solution)/shard_map/ppermute | solution.py:318
  533.2 215.5 %reduce-scatter.5.cloned.1.call-start = ((), (), s32[]{:S(2)}) async-start(), calls=%async_computation.5 | async-start | bytes 7864320 | tf_op jit(solution)/shard_map/reduce_scatter | solution.py:1230
  564.7 56.1 %collective-permute-start.43 = (bf16[512,2048]{1,0:T(8,128)(2,1)}, bf16[512,2048]{1,0:T(8,128)(2,1)}, u32[]{:S(2)}, u32[]{:S(2)}) collective-permute-start(bf16[512,2048]{1,0:T(8,128)(2,1)} %get-tuple-element.2284), channel_id=1, source_target_pairs={{0,8},{4,12},{8,0},{12,4},{16,24},{20,28},{24,16},{28,20},{1,9},{5... | collective-permute-start | bytes 6291464 | tf_op jit(solution)/shard_map/ppermute | solution.py:318
  565.7 55.2 %collective-permute-start.44 = (bf16[512,2048]{1,0:T(8,128)(2,1)}, bf16[512,2048]{1,0:T(8,128)(2,1)}, u32[]{:S(2)}, u32[]{:S(2)}) collective-permute-start(bf16[512,2048]{1,0:T(8,128)(2,1)} %get-tuple-element.2285), channel_id=1, source_target_pairs={{0,16},{4,20},{8,24},{12,28},{16,0},{20,4},{24,8},{28,12},{1,17},{... | collective-permute-start | bytes 6291464 | tf_op jit(solution)/shard_map/ppermute | solution.py:318
  620.9 36.5 %collective-permute-start.47 = (bf16[2048,1024]{1,0:T(8,128)(2,1)}, bf16[2048,1024]{1,0:T(8,128)(2,1)S(1)}, u32[]{:S(2)}, u32[]{:S(2)}) collective-permute-start(bf16[2048,1024]{1,0:T(8,128)(2,1)} %row_outer.15), channel_id=1, source_target_pairs={{0,4},{4,0},{8,12},{12,8},{16,20},{20,16},{24,28},{28,24},{1,5},{5... | collective-permute-start | bytes 12582920 | tf_op jit(solution)/shard_map/ppermute | solution.py:318
  625.8 31.5 %collective-permute-start.46 = (bf16[256,2048]{1,0:T(8,128)(2,1)}, bf16[256,2048]{1,0:T(8,128)(2,1)S(1)}, u32[]{:S(2)}, u32[]{:S(2)}) collective-permute-start(bf16[256,2048]{1,0:T(8,128)(2,1)} %get-tuple-element.2869), channel_id=1, source_target_pairs={{0,16},{4,20},{8,24},{12,28},{16,0},{20,4},{24,8},{28,12},{1,17},{... | collective-permute-start | bytes 3145736 | tf_op jit(solution)/shard_map/ppermute | solution.py:318
  658.4 33.3 %collective-permute-start.50 = (bf16[512,768]{1,0:T(8,128)(2,1)}, bf16[512,768]{1,0:T(8,128)(2,1)S(1)}, u32[]{:S(2)}, u32[]{:S(2)}) collective-permute-start(bf16[512,768]{1,0:T(8,128)(2,1)} %reduce-scatter.3.cloned.1.call-done), channel_id=1, source_target_pairs={{0,16},{4,20},{8,24},{12,28},{16,0},{20,4},{24,8},{28,12},{1,17},{... | collective-permute-start | bytes 2359304 | tf_op jit(solution)/shard_map/ppermute | solution.py:318
  659.2 32.5 %collective-permute-start.49 = (bf16[512,768]{1,0:T(8,128)(2,1)}, bf16[512,768]{1,0:T(8,128)(2,1)S(1)}, u32[]{:S(2)}, u32[]{:S(2)}) collective-permute-start(bf16[512,768]{1,0:T(8,128)(2,1)} %reduce-scatter.3.cloned.1.call-done), channel_id=1, source_target_pairs={{0,8},{4,12},{8,0},{12,4},{16,24},{20,28},{24,16},{28,20},{1,9},{5... | collective-permute-start | bytes 2359304 | tf_op jit(solution)/shard_map/ppermute | solution.py:318
  660.5 31.1 %collective-permute-start.51 = (bf16[512,512]{1,0:T(8,128)(2,1)}, bf16[512,512]{1,0:T(8,128)(2,1)}, u32[]{:S(2)}, u32[]{:S(2)}) collective-permute-start(bf16[512,512]{1,0:T(8,128)(2,1)} %get-tuple-element.2418), channel_id=1, source_target_pairs={{4,0},{12,8},{20,16},{28,24},{5,1},{13,9},{21,17},{29,25},{6,2},{1... | collective-permute-start | bytes 1572872 | tf_op jit(solution)/shard_map/ppermute | solution.py:1190
  748.7 52.5 %collective-permute-start.65 = (bf16[2048,2048]{1,0:T(8,128)(2,1)}, bf16[2048,2048]{1,0:T(8,128)(2,1)}, u32[]{:S(2)}, u32[]{:S(2)}) collective-permute-start(bf16[2048,2048]{1,0:T(8,128)(2,1)} %row_outer.19), channel_id=1, source_target_pairs={{0,4},{4,0},{8,12},{12,8},{16,20},{20,16},{24,28},{28,24},{1,5},{5... | collective-permute-start | bytes 25165832 | tf_op jit(solution)/shard_map/ppermute | solution.py:318
  764.2 36.6 %collective-permute-start.62 = (bf16[512,1536]{1,0:T(8,128)(2,1)}, bf16[512,1536]{1,0:T(8,128)(2,1)S(1)}, u32[]{:S(2)}, u32[]{:S(2)}) collective-permute-start(bf16[512,1536]{1,0:T(8,128)(2,1)} %reduce-scatter.5.cloned.1.call-done), channel_id=1, source_target_pairs={{0,16},{4,20},{8,24},{12,28},{16,0},{20,4},{24,8},{28,12},{1,17},{... | collective-permute-start | bytes 4718600 | tf_op jit(solution)/shard_map/ppermute | solution.py:318
  764.9 36.3 %collective-permute-start.61 = (bf16[512,1536]{1,0:T(8,128)(2,1)}, bf16[512,1536]{1,0:T(8,128)(2,1)S(1)}, u32[]{:S(2)}, u32[]{:S(2)}) collective-permute-start(bf16[512,1536]{1,0:T(8,128)(2,1)} %reduce-scatter.5.cloned.1.call-done), channel_id=1, source_target_pairs={{0,8},{4,12},{8,0},{12,4},{16,24},{20,28},{24,16},{28,20},{1,9},{5... | collective-permute-start | bytes 4718600 | tf_op jit(solution)/shard_map/ppermute | solution.py:318
  803.5 32.5 %collective-permute-start.66 = (bf16[2048,768]{1,0:T(8,128)(2,1)S(1)}, bf16[2048,768]{1,0:T(8,128)(2,1)}, u32[]{:S(2)}, u32[]{:S(2)}) collective-permute-start(bf16[2048,768]{1,0:T(8,128)(2,1)S(1)} %constant_dynamic-update-slice_fusion.4.own_ref), channel_id=1, source_target_pairs={{0,4},{4,0},{8,12},{12,8},{16,20},{20,16},{24,28},{28,24},{1,5},{5... | collective-permute-start | bytes 9437192 | tf_op jit(solution)/shard_map/ppermute | solution.py:318
  848.7 48.1 %collective-permute-start.79 = (bf16[256,2048]{1,0:T(8,128)(2,1)S(1)}, bf16[256,2048]{1,0:T(8,128)(2,1)S(1)}, u32[]{:S(2)}, u32[]{:S(2)}) collective-permute-start(bf16[256,2048]{1,0:T(8,128)(2,1)S(1)} %get-tuple-element.2863), channel_id=1, source_target_pairs={{1,0},{0,1},{5,2},{4,3},{3,4},{2,5},{7,6},{6,7},{9,8},{8,9},{13,10... | collective-permute-start | bytes 3145736 | tf_op jit(solution)/shard_map/ppermute | solution.py:395
  (203 other events, 2270.3 us)
Sparse Core Ops, SparseCore 0:
  77.5 47.2 all-gather.2
  175.8 195.8 all-gather.4
  533.4 69.6 reduce-scatter.2
  621.0 119.4 reduce-scatter.4

commit v15 on v12

--- a/solution.py
+++ b/solution.py
@@ -1267,7 +1267,6 @@
     s.down_spread = jnp.concatenate([s.down_total, *s.down_near, *s.down_far], 0)
     s.down_spread_other = across(s.down_spread, CORE)
     s.output_second = output_sent[1]
-    s.out_ring_last = around(rounded_sum(s.out_chunks[3], s.out_ring[0]), 1)
     s.gate_up_far = far(*s.gate_up_near)
     del s.qkv_came, s.finished, s.down_total, s.down_near, s.down_far
     s.end()
@@ -1277,34 +1276,36 @@
         return jnp.split(own.astype(low), shards, 0)
 
     s.near0 = send_near((s.head0[0], s.tail0[0]))
-    s.gate_up_own = jnp.concatenate([s.gate_up_total, *s.gate_up_near, *s.gate_up_far], 0)
-    s.gate_up_other = across(s.gate_up_own, CORE)
-    (s.whole_down,) = in_order([whole_call((units,), s.down_spread, s.down_spread_other)])
-    s.out_total = rounded_sum(s.out_chunks[0], s.out_ring[1], s.out_ring_last)
+    s.out_ring_last = around(rounded_sum(s.out_chunks[3], s.out_ring[0]), 1)
     s.tokens_first = tokens_sent[0]
-    del s.down_spread, s.down_spread_other, s.out_chunks, s.out_ring, s.out_ring_last
-    del s.gate_up_near, s.gate_up_far, s.gate_up_total
+    s.gain_came = across(s.gain_parts, CORE)
     s.end()
 
     s.far0 = send_far(s.near0, (s.tail0[1], s.head0[1]), by_columns)
     s.near1 = send_near((s.head1[0], s.tail1[0]))
-    (s.whole_gate_up,) = in_order([whole_call((units, units), s.gate_up_own, s.gate_up_other)])
+    (s.whole_down,) = in_order([whole_call((units,), s.down_spread, s.down_spread_other)])
+    first = lax.optimization_barrier((s.gate_up_total, s.whole_down[0]))[0]
+    s.gate_up_own = jnp.concatenate([first, *s.gate_up_near, *s.gate_up_far], 0)
+    s.out_total = rounded_sum(s.out_chunks[0], s.out_ring[1], s.out_ring_last)
+    s.gain_parts = s.gain_parts + s.gain_came
     s.tokens_second = tokens_sent[1]
-    del s.gate_up_own, s.gate_up_other, s.grad_tokens
+    del s.down_spread, s.down_spread_other, s.out_chunks, s.out_ring, s.out_ring_last
+    del s.gate_up_near, s.gate_up_far, s.gate_up_total, s.grad_tokens
     s.end()
 
     s.chunks0 = qkv_chunks(s.near0, s.far0, s.head0, s.tail0)
     s.ring0 = ring_sum_first(s.chunks0)
     s.far1 = send_far(s.near1, (s.tail1[1], s.head1[1]), by_columns)
-    s.gain_came = across(s.gain_parts, CORE)
+    s.gate_up_other = across(s.gate_up_own, CORE)
     del s.near0, s.far0, s.head0, s.tail0
     s.end()
 
     s.last0 = around(rounded_sum(s.chunks0[3], s.ring0[0]), 1)
     s.chunks1 = qkv_chunks(s.near1, s.far1, s.head1, s.tail1)
     s.ring1 = ring_sum_first(s.chunks1)
-    s.gain_parts = s.gain_parts + s.gain_came
     s.gain_came = across(s.gain_parts, ACROSS_X)
+    (s.whole_gate_up,) = in_order([whole_call((units, units), s.gate_up_own, s.gate_up_other)])
+    del s.gate_up_own, s.gate_up_other
     del s.near1, s.far1, s.head1, s.tail1
     s.end()
 

time: 989 us -> 983 us (level)
    unnamed x272 -> x282, local copies, waits for them, and re-layouts: 27.8 us -> 21.4 us
  transfers between devices with their start and end apart: 107 -> 107, of which waited for: 41 -> 34; matrix products, arithmetic and copies ran while one was open for 9% -> 10% of each run, Pallas kernels for 38% -> 39%
where the time goes in v15:
time: 983 us; the launch traced here: 974 us
  Pallas kernels  424 us (43%)
  waiting for transfers between devices  270 us (27%)
  starting transfers between devices  134 us (14%)
  other arithmetic  67.9 us (7%)
  local copies, waits for them, and re-layouts  60.8 us (6%)
  between operations  16.3 us (2%)
    ppermute x73, waiting for transfers between devices, across(): return lax.ppermute(x, 'rep', [(i, i ^ mask) for i in range(count)])  159 us
    pallas_call x16, Pallas kernels, call(): pl.pallas_call(body, grid=(1,), out_shape=outs, in_specs=in_specs, out_sp...  119 us
    pallas_call x12, Pallas kernels, row_outer(): pl.pallas_call(body, grid=(tiles,), out_shape=[jax.ShapeDtypeStruct((tile...  114 us
    ppermute x73, starting transfers between devices, across(): return lax.ppermute(x, 'rep', [(i, i ^ mask) for i in range(count)])  67.4 us
    pallas_call x2, Pallas kernels, hidden_units(): pl.pallas_call(body, grid=(3,), out_shape=[jax.ShapeDtypeStruct((rows, un...  59.6 us
    pallas_call x4, Pallas kernels, from_hidden(): pl.pallas_call(body, grid=(4,), out_shape=[jax.ShapeDtypeStruct((2 * rows...  59.4 us
    ppermute x4, waiting for transfers between devices, to_sequence(): return lax.ppermute(cut, ('rep', 'shard'), sequence_pairs(turn))  51.7 us
    pallas_call x4, Pallas kernels, whole_columns(): pl.pallas_call(body, grid_spec=pltpu.PrefetchScalarGridSpec(num_scalar_pr...  44.4 us
  transfers between devices with their start and end apart: 107, of which 34 were waited for; matrix products, arithmetic and copies ran while one was open for 10% of the time, Pallas kernels for 39%

profile of v15, /device:TPU:0, one launch (start us, length us, event | category | flops | bytes accessed | tf_op | source)
XLA Modules:
  0.0 973.5 jit_solution(5500787797437204301)
XLA Ops:
  33.1 10.3 %collective-permute-done = bf16[528,512]{1,0:T(8,128)(2,1)} collective-permute-done((bf16[528,512]{1,0:T(8,128)(2,1)}, bf16[528,512]{1,0:T(8,128)(2,1)}, u32[]{:S(2)}, u32[]{:S(2)}) %collective-permute-start) | collective-permute-done | bytes 540704 | tf_op jit(solution)/shard_map/ppermute | solution.py:323
  45.1 13.5 %collective-permute-done.3 = bf16[528,512]{1,0:T(8,128)(2,1)S(1)} collective-permute-done((bf16[528,512]{1,0:T(8,128)(2,1)}, bf16[528,512]{1,0:T(8,128)(2,1)S(1)}, u32[]{:S(2)}, u32[]{:S(2)}) %collective-permute-start.3) | collective-permute-done | bytes 540704 | tf_op jit(solution)/shard_map/ppermute | solution.py:323
  64.9 9.4 collective-permute-start.7
  78.7 48.8 %collective-permute-done.8 = bf16[256,2048]{1,0:T(8,128)(2,1)} collective-permute-done((bf16[256,2048]{1,0:T(8,128)(2,1)S(1)}, bf16[256,2048]{1,0:T(8,128)(2,1)}, u32[]{:S(2)}, u32[]{:S(2)}) %collective-permute-start.8) | collective-permute-done | bytes 1048608 | tf_op jit(solution)/shard_map/ppermute | solution.py:388
  134.4 9.6 collective-permute-start.14
  245.4 13.6 %collective-permute-done.28.refs_7_.refs_2_ = bf16[512,2048]{1,0:T(8,128)(2,1)S(1)} collective-permute-done((bf16[512,2048]{1,0:T(8,128)(2,1)S(1)}, bf16[512,2048]{1,0:T(8,128)(2,1)S(1)}, u32[]{:S(2)}, u32[]{:S(2)}) %collective-permute-start.28) | collective-permute-done | bytes 2097184 | tf_op jit(solution)/shard_map/ppermute | solution.py:318
  269.4 11.7 %close_attention.1 = (f32[512,2048]{1,0:T(8,128)}, bf16[512,2048]{1,0:T(8,128)(2,1)}) custom-call(bf16[512,2048]{1,0:T(8,128)(2,1)} %pad_maximum_fusion.3.x, bf16[512,512]{1,0:T(8,128)(2,1)} %get-tuple-element.2442.refs_0_.refs_1_.refs_4_, bf16[512,512]{1,0:T(8,128)(2,1)} %get-tuple-element.2439.refs_1_.refs_2_.refs_3_, ...), custom_call_target="tpu_custom_call" | custom-call | flops 1 | bytes 1 | tf_op jit(solution)/shard_map/close_attention/pallas_call | solution.py:789
  289.5 42.8 %collective-permute-done.33.refs_2_ = bf16[512,2048]{1,0:T(8,128)(2,1)S(1)} collective-permute-done((bf16[512,2048]{1,0:T(8,128)(2,1)}, bf16[512,2048]{1,0:T(8,128)(2,1)S(1)}, u32[]{:S(2)}, u32[]{:S(2)}) %collective-permute-start.33) | collective-permute-done | bytes 2097184 | tf_op jit(solution)/shard_map/ppermute | solution.py:318
  336.6 19.9 %collective-permute-done.35.refs_4_ = bf16[256,2048]{1,0:T(8,128)(2,1)S(1)} collective-permute-done((bf16[256,2048]{1,0:T(8,128)(2,1)S(1)}, bf16[256,2048]{1,0:T(8,128)(2,1)S(1)}, u32[]{:S(2)}, u32[]{:S(2)}) %collective-permute-start.35) | collective-permute-done | bytes 1048608 | tf_op jit(solution)/shard_map/ppermute | solution.py:318
  356.9 9.7 all-gather.5.cloned.1.call-done.refs_10_.refs_11_.refs_12_.refs_4_.refs_9_
  366.6 29.7 %hidden_units.2 = (bf16[2048,768]{1,0:T(8,128)(2,1)}, bf16[2048,768]{1,0:T(8,128)(2,1)}, bf16[2048,768]{1,0:T(8,128)(2,1)}) custom-call(bf16[512,2048]{1,0:T(8,128)(2,1)} %get-tuple-element.2314.refs_0_, bf16[512,2048]{1,0:T(8,128)(2,1)} %copy-done.12, bf16[512,2048]{1,0:T(8,128)(2,1)} %copy-done.11, bf16[256,2048]{1,0:T(8,128)(2,1)} %copy-done.23, ...), custom_call_target="tpu_custom_call" | custom-call | flops 1 | bytes 1 | tf_op jit(solution)/shard_map/hidden_units/pallas_call | solution.py:656
  396.3 29.9 %hidden_units.3 = (bf16[2048,768]{1,0:T(8,128)(2,1)}, bf16[2048,768]{1,0:T(8,128)(2,1)}, bf16[2048,768]{1,0:T(8,128)(2,1)}) custom-call(bf16[512,2048]{1,0:T(8,128)(2,1)} %get-tuple-element.2314.refs_0_, bf16[512,2048]{1,0:T(8,128)(2,1)} %copy-done.12, bf16[512,2048]{1,0:T(8,128)(2,1)} %copy-done.11, bf16[256,2048]{1,0:T(8,128)(2,1)} %copy-done.23, ...), custom_call_target="tpu_custom_call" | custom-call | flops 1 | bytes 1 | tf_op jit(solution)/shard_map/hidden_units/pallas_call | solution.py:656
  426.2 12.6 %row_outer.12 = bf16[2048,768]{1,0:T(8,128)(2,1)} custom-call(bf16[512,2048]{1,0:T(8,128)(2,1)} %copy-done.6, bf16[512,2048]{1,0:T(8,128)(2,1)} %copy-done.14, bf16[512,2048]{1,0:T(8,128)(2,1)} %copy-done.13, bf16[256,2048]{1,0:T(8,128)(2,1)} %copy-done.25, bf16[256,2048]{1,0:T(8,128)(2,1)} %copy-done.24, ...), custom_call_target="tpu_custom_call" | custom-call | flops 6442450944 | bytes 11534336 | tf_op jit(solution)/shard_map/row_outer/pallas_call | solution.py:739
  439.2 19.0 %from_hidden.4 = (bf16[512,2048]{1,0:T(8,128)(2,1)}, bf16[512,2048]{1,0:T(8,128)(2,1)}) custom-call(bf16[2048,768]{1,0:T(8,128)(2,1)} %get-tuple-element.2325.refs_0_.refs_1_.refs_2_.refs_3_.refs_5_, bf16[2048,768]{1,0:T(8,128)(2,1)} %get-tuple-element.2325.refs_0_.refs_1_.refs_2_.refs_3_.refs_5_, ...), custom_call_target="tpu_custom_call" | custom-call | flops 1 | bytes 1 | tf_op jit(solution)/shard_map/from_hidden/pallas_call | solution.py:695
  461.2 13.2 %row_outer.13 = bf16[2048,768]{1,0:T(8,128)(2,1)} custom-call(bf16[512,2048]{1,0:T(8,128)(2,1)} %copy-done.6, bf16[512,2048]{1,0:T(8,128)(2,1)} %copy-done.14, bf16[512,2048]{1,0:T(8,128)(2,1)} %copy-done.13, bf16[256,2048]{1,0:T(8,128)(2,1)} %copy-done.25, bf16[256,2048]{1,0:T(8,128)(2,1)} %copy-done.24, ...), custom_call_target="tpu_custom_call" | custom-call | flops 6442450944 | bytes 11534336 | tf_op jit(solution)/shard_map/row_outer/pallas_call | solution.py:739
  474.4 18.8 %from_hidden.5 = (bf16[512,2048]{1,0:T(8,128)(2,1)}, bf16[512,2048]{1,0:T(8,128)(2,1)}) custom-call(bf16[2048,768]{1,0:T(8,128)(2,1)} %get-tuple-element.2325.refs_0_.refs_1_.refs_2_.refs_3_.refs_5_, bf16[2048,768]{1,0:T(8,128)(2,1)} %get-tuple-element.2325.refs_0_.refs_1_.refs_2_.refs_3_.refs_5_, ...), custom_call_target="tpu_custom_call" | custom-call | flops 1 | bytes 1 | tf_op jit(solution)/shard_map/from_hidden/pallas_call | solution.py:695
  493.3 19.5 %row_outer.14 = bf16[2048,1536]{1,0:T(8,128)(2,1)} custom-call(bf16[512,2048]{1,0:T(8,128)(2,1)} %get-tuple-element.2314.refs_0_, bf16[512,2048]{1,0:T(8,128)(2,1)} %copy-done.12, bf16[512,2048]{1,0:T(8,128)(2,1)} %copy-done.11, bf16[256,2048]{1,0:T(8,128)(2,1)} %copy-done.23, bf16[256,2048]{1,0:T(8,128)(2,1)} %copy-done.22, ...), custom_call_target="tpu_custom_call" | custom-call | flops 12884901888 | bytes 14680064 | tf_op jit(solution)/shard_map/row_outer/pallas_call | solution.py:739
  519.7 10.8 %from_hidden.6 = (bf16[512,2048]{1,0:T(8,128)(2,1)}, bf16[512,2048]{1,0:T(8,128)(2,1)}) custom-call(bf16[2048,768]{1,0:T(8,128)(2,1)} %get-tuple-element.2234.refs_5_.refs_0_.refs_1_.refs_2_.refs_3_, bf16[2048,768]{1,0:T(8,128)(2,1)} %get-tuple-element.2234.refs_5_.refs_0_.refs_1_.refs_2_.refs_3_, ...), custom_call_target="tpu_custom_call" | custom-call | flops 1 | bytes 1 | tf_op jit(solution)/shard_map/from_hidden/pallas_call | solution.py:695
  530.5 10.9 %from_hidden.7 = (bf16[512,2048]{1,0:T(8,128)(2,1)}, bf16[512,2048]{1,0:T(8,128)(2,1)}) custom-call(bf16[2048,768]{1,0:T(8,128)(2,1)} %get-tuple-element.2234.refs_5_.refs_0_.refs_1_.refs_2_.refs_3_, bf16[2048,768]{1,0:T(8,128)(2,1)} %get-tuple-element.2234.refs_5_.refs_0_.refs_1_.refs_2_.refs_3_, ...), custom_call_target="tpu_custom_call" | custom-call | flops 1 | bytes 1 | tf_op jit(solution)/shard_map/from_hidden/pallas_call | solution.py:695
  555.8 13.3 %attend_back.4 = (bf16[512,512]{1,0:T(8,128)(2,1)}, f32[512,512]{1,0:T(8,128)}, bf16[512,512]{1,0:T(8,128)(2,1)}, f32[1,128]{1,0:T(1,128)}) custom-call(s32[2]{0:T(128)} %pad_add_fusion.info, bf16[512,512]{1,0:T(8,128)(2,1)} %get-tuple-element.2281.query, bf16[512,512]{1,0:T(8,128)(2,1)} %copy-done.40, bf16[512,512]{1,0:T(8,128)(2,1)} %get-tuple-element.2283.own, ...), custom_call_target="tpu_custom_call" | custom-call | flops 1 | bytes 1 | tf_op jit(solution)/shard_map/attend_back/pallas_call | solution.py:616
  579.2 19.7 %row_outer.16 = bf16[2048,1536]{1,0:T(8,128)(2,1)} custom-call(bf16[512,2048]{1,0:T(8,128)(2,1)} %get-tuple-element.2314.refs_0_, bf16[512,2048]{1,0:T(8,128)(2,1)} %copy-done.12, bf16[512,2048]{1,0:T(8,128)(2,1)} %copy-done.11, bf16[256,2048]{1,0:T(8,128)(2,1)} %copy-done.23, bf16[256,2048]{1,0:T(8,128)(2,1)} %copy-done.22, ...), custom_call_target="tpu_custom_call" | custom-call | flops 12884901888 | bytes 14680064 | tf_op jit(solution)/shard_map/row_outer/pallas_call | solution.py:739
  607.8 13.2 %attend_back.5 = (bf16[512,512]{1,0:T(8,128)(2,1)}, f32[512,512]{1,0:T(8,128)}, bf16[512,512]{1,0:T(8,128)(2,1)}, f32[1,128]{1,0:T(1,128)}) custom-call(s32[2]{0:T(128)} %pad_add_fusion.info, bf16[512,512]{1,0:T(8,128)(2,1)} %get-tuple-element.2364.query, bf16[512,512]{1,0:T(8,128)(2,1)} %copy-done.39, bf16[512,512]{1,0:T(8,128)(2,1)} %get-tuple-element.2366.own, ...), custom_call_target="tpu_custom_call" | custom-call | flops 1 | bytes 1 | tf_op jit(solution)/shard_map/attend_back/pallas_call | solution.py:616
  621.0 13.6 %attend_back.6 = (bf16[512,512]{1,0:T(8,128)(2,1)}, f32[512,512]{1,0:T(8,128)}, bf16[512,512]{1,0:T(8,128)(2,1)}, f32[1,128]{1,0:T(1,128)}) custom-call(s32[2]{0:T(128)} %pad_add_fusion.info, bf16[512,512]{1,0:T(8,128)(2,1)} %get-tuple-element.2379.query, bf16[512,512]{1,0:T(8,128)(2,1)} %collective-permute-done.21.before, ...), custom_call_target="tpu_custom_call" | custom-call | flops 1 | bytes 1 | tf_op jit(solution)/shard_map/attend_back/pallas_call | solution.py:616
  651.1 13.3 %attend_back.7 = (bf16[512,512]{1,0:T(8,128)(2,1)}, f32[512,512]{1,0:T(8,128)}, bf16[512,512]{1,0:T(8,128)(2,1)}, f32[1,128]{1,0:T(1,128)}) custom-call(s32[2]{0:T(128)} %pad_add_fusion.info, bf16[512,512]{1,0:T(8,128)(2,1)} %get-tuple-element.2447.query, bf16[512,512]{1,0:T(8,128)(2,1)} %copy-done.37, bf16[512,512]{1,0:T(8,128)(2,1)} %get-tuple-element.2449.own, ...), custom_call_target="tpu_custom_call" | custom-call | flops 1 | bytes 1 | tf_op jit(solution)/shard_map/attend_back/pallas_call | solution.py:616
  684.1 15.7 %collective-permute-done.53 = bf16[1024,512]{1,0:T(8,128)(2,1)S(1)} collective-permute-done((bf16[1024,512]{1,0:T(8,128)(2,1)}, bf16[1024,512]{1,0:T(8,128)(2,1)S(1)}, u32[]{:S(2)}, u32[]{:S(2)}) %collective-permute-start.53) | collective-permute-done | bytes 1048608 | tf_op jit(solution)/shard_map/ppermute | solution.py:318
  713.5 10.1 %row_outer.19 = bf16[2048,2048]{1,0:T(8,128)(2,1)} custom-call(bf16[512,2048]{1,0:T(8,128)(2,1)} %pad_maximum_fusion.4.normed.refs_0_, bf16[512,512]{1,0:T(8,128)(2,1)} %get-tuple-element.2643.refs_1_, bf16[512,512]{1,0:T(8,128)(2,1)} %get-tuple-element.2646.refs_2_.refs_3_, bf16[512,512]{1,0:T(8,128)(2,1)} %get-tuple-element.2649.refs_3_.refs_5_, ...), custom_call_target="tpu_custom_call" | custom-call | flops 4294967296 | bytes 4194304 | tf_op jit(solution)/shard_map/row_outer/pallas_call | solution.py:739
  738.7 15.8 %back_to_rows.1 = f32[512,2048]{1,0:T(8,128)} custom-call(bf16[512,512]{1,0:T(8,128)(2,1)} %get-tuple-element.2702.refs_0_.refs_4_, bf16[512,512]{1,0:T(8,128)(2,1)} %get-tuple-element.2643.refs_1_, bf16[512,512]{1,0:T(8,128)(2,1)} %get-tuple-element.2699.refs_2_.refs_1_.refs_3_, bf16[512,512]{1,0:T(8,128)(2,1)} %get-tuple-element.2646.refs_2_.refs_3_, ...), custom_call_target="tpu_custom_call" | custom-call | flops 1 | bytes 1 | tf_op jit(solution)/shard_map/back_to_rows/pallas_call | solution.py:842
  776.6 9.6 collective-permute-start.74
  832.0 11.2 %whole_columns.4 = f32[512,6144]{1,0:T(8,128)} custom-call(s32[1]{0:T(128)} %bitcast.21.me_ref, bf16[2048,768]{1,0:T(8,128)(2,1)} %copy-done.21, bf16[2048,768]{1,0:T(8,128)(2,1)} %collective-permute-done.66.other_ref), custom_call_target="tpu_custom_call" | custom-call | flops 1 | bytes 1 | tf_op jit(solution)/shard_map/whole_columns/pallas_call | solution.py:431
  846.3 16.4 %collective-permute-done.77 = bf16[1024,512]{1,0:T(8,128)(2,1)} collective-permute-done((bf16[1024,512]{1,0:T(8,128)(2,1)}, bf16[1024,512]{1,0:T(8,128)(2,1)}, u32[]{:S(2)}, u32[]{:S(2)}) %collective-permute-start.77) | collective-permute-done | bytes 1048608 | tf_op jit(solution)/shard_map/ppermute | solution.py:318
  893.7 17.8 %whole_columns.5 = (f32[512,6144]{1,0:T(8,128)}, f32[512,6144]{1,0:T(8,128)}) custom-call(s32[1]{0:T(128)} %bitcast.21.me_ref, bf16[2048,1536]{1,0:T(8,128)(2,1)} %copy-done.15, bf16[2048,1536]{1,0:T(8,128)(2,1)} %copy-done.19), custom_call_target="tpu_custom_call" | custom-call | flops 1 | bytes 1 | tf_op jit(solution)/shard_map/whole_columns/pallas_call | solution.py:431
  914.5 9.3 collective-permute-done.89
  (650 shorter events, 424.6 us)
Async XLA Ops:
  7.2 144.2 %all-gather.3.cloned.1.call-start = ((), (), s32[]{:S(2)}) async-start(), calls=%async_computation.2 | async-start | bytes 1310720 | tf_op jit(solution)/shard_map/all_gather | solution.py:903
  61.2 66.3 %collective-permute-start.6 = (bf16[1536,512]{1,0:T(8,128)(2,1)S(1)}, bf16[1536,512]{1,0:T(8,128)(2,1)}, u32[]{:S(2)}, u32[]{:S(2)}) collective-permute-start(bf16[1536,512]{1,0:T(8,128)(2,1)S(1)} %pad_maximum_fusion.8.came0.refs_9_), channel_id=1, source_target_pairs={{0,4},{4,0},{8,12},{12,8},{16,20},{20,16},{24,28},{28,24},{1,5},{5... | collective-permute-start | bytes 4718600 | tf_op jit(solution)/shard_map/ppermute | solution.py:318
  61.3 66.2 %collective-permute-start.5 = (bf16[1536,512]{1,0:T(8,128)(2,1)S(1)}, bf16[1536,512]{1,0:T(8,128)(2,1)}, u32[]{:S(2)}, u32[]{:S(2)}) collective-permute-start(bf16[1536,512]{1,0:T(8,128)(2,1)S(1)} %pad_maximum_fusion.8.came0.refs_9_), channel_id=1, source_target_pairs={{0,16},{4,20},{8,24},{12,28},{16,0},{20,4},{24,8},{28,12},{1,17},{... | collective-permute-start | bytes 4718600 | tf_op jit(solution)/shard_map/ppermute | solution.py:318
  62.8 64.7 %collective-permute-start.4 = (bf16[1536,512]{1,0:T(8,128)(2,1)S(1)}, bf16[1536,512]{1,0:T(8,128)(2,1)}, u32[]{:S(2)}, u32[]{:S(2)}) collective-permute-start(bf16[1536,512]{1,0:T(8,128)(2,1)S(1)} %pad_maximum_fusion.8.came0.refs_9_), channel_id=1, source_target_pairs={{0,8},{4,12},{8,0},{12,4},{16,24},{20,28},{24,16},{28,20},{1,9},{5... | collective-permute-start | bytes 4718600 | tf_op jit(solution)/shard_map/ppermute | solution.py:318
  74.3 53.2 %collective-permute-start.8 = (bf16[256,2048]{1,0:T(8,128)(2,1)S(1)}, bf16[256,2048]{1,0:T(8,128)(2,1)}, u32[]{:S(2)}, u32[]{:S(2)}) collective-permute-start(bf16[256,2048]{1,0:T(8,128)(2,1)S(1)} %get-tuple-element.1487), channel_id=1, source_target_pairs={{0,1},{1,0},{2,5},{3,4},{4,3},{5,2},{6,7},{7,6},{8,9},{9,8},{10,13... | collective-permute-start | bytes 3145736 | tf_op jit(solution)/shard_map/ppermute | solution.py:388
  77.2 289.3 %all-gather.5.cloned.1.call-start = ((), (), s32[]{:S(2)}) async-start(), calls=%async_computation.3 | async-start | bytes 11796480 | tf_op jit(solution)/shard_map/all_gather | solution.py:995
  155.6 31.6 %collective-permute-start.13 = (bf16[1536,512]{1,0:T(8,128)(2,1)S(1)}, bf16[1536,512]{1,0:T(8,128)(2,1)S(1)}, u32[]{:S(2)}, u32[]{:S(2)}) collective-permute-start(bf16[1536,512]{1,0:T(8,128)(2,1)S(1)} %constant_dynamic-update-slice_fusion.came0.refs_21_), channel_id=1, source_target_pairs={{0,4},{4,0},{8,12},{12,8},{16,20},{20,16},{24,28},{28,24},{1,5},{5... | collective-permute-start | bytes 4718600 | tf_op jit(solution)/shard_map/ppermute | solution.py:318
  155.6 31.4 %collective-permute-start.15 = (bf16[256,2048]{1,0:T(8,128)(2,1)}, bf16[256,2048]{1,0:T(8,128)(2,1)S(1)}, u32[]{:S(2)}, u32[]{:S(2)}) collective-permute-start(bf16[256,2048]{1,0:T(8,128)(2,1)} %get-tuple-element.1518), channel_id=1, source_target_pairs={{0,1},{1,0},{2,5},{3,4},{4,3},{5,2},{6,7},{7,6},{8,9},{9,8},{10,13... | collective-permute-start | bytes 3145736 | tf_op jit(solution)/shard_map/ppermute | solution.py:388
  188.9 409.9 %reduce-scatter.3.cloned.1.call-start = ((), (), s32[]{:S(2)}) async-start(), calls=%async_computation.4 | async-start | bytes 3932160 | tf_op jit(solution)/shard_map/reduce_scatter | solution.py:1111
  190.1 34.5 %collective-permute-start.24 = (bf16[2048,256]{1,0:T(8,128)(2,1)}, bf16[2048,256]{1,0:T(8,128)(2,1)}, u32[]{:S(2)}, u32[]{:S(2)}) collective-permute-start(bf16[2048,256]{1,0:T(8,128)(2,1)} %collective-permute-done.16.refs_6_.weight0), channel_id=1, source_target_pairs={{0,4},{4,0},{8,12},{12,8},{16,20},{20,16},{24,28},{28,24},{1,5},{5... | collective-permute-start | bytes 3145736 | tf_op jit(solution)/shard_map/ppermute | solution.py:318
  211.4 47.7 %collective-permute-start.28 = (bf16[512,2048]{1,0:T(8,128)(2,1)S(1)}, bf16[512,2048]{1,0:T(8,128)(2,1)S(1)}, u32[]{:S(2)}, u32[]{:S(2)}) collective-permute-start(bf16[512,2048]{1,0:T(8,128)(2,1)S(1)} %maximum_select_fusion.refs_5_.refs_0_), channel_id=1, source_target_pairs={{0,16},{4,20},{8,24},{12,28},{16,0},{20,4},{24,8},{28,12},{1,17},{... | collective-permute-start | bytes 6291464 | tf_op jit(solution)/shard_map/ppermute | solution.py:318
  213.9 46.6 %collective-permute-start.27 = (bf16[512,2048]{1,0:T(8,128)(2,1)S(1)}, bf16[512,2048]{1,0:T(8,128)(2,1)S(1)}, u32[]{:S(2)}, u32[]{:S(2)}) collective-permute-start(bf16[512,2048]{1,0:T(8,128)(2,1)S(1)} %maximum_select_fusion.refs_5_.refs_0_), channel_id=1, source_target_pairs={{0,8},{4,12},{8,0},{12,4},{16,24},{20,28},{24,16},{28,20},{1,9},{5... | collective-permute-start | bytes 6291464 | tf_op jit(solution)/shard_map/ppermute | solution.py:318
  287.0 45.2 %collective-permute-start.33 = (bf16[512,2048]{1,0:T(8,128)(2,1)}, bf16[512,2048]{1,0:T(8,128)(2,1)S(1)}, u32[]{:S(2)}, u32[]{:S(2)}) collective-permute-start(bf16[512,2048]{1,0:T(8,128)(2,1)} %get-tuple-element.2314.refs_0_), channel_id=1, source_target_pairs={{0,16},{4,20},{8,24},{12,28},{16,0},{20,4},{24,8},{28,12},{1,17},{... | collective-permute-start | bytes 6291464 | tf_op jit(solution)/shard_map/ppermute | solution.py:318
  288.3 45.2 %collective-permute-start.32 = (bf16[512,2048]{1,0:T(8,128)(2,1)}, bf16[512,2048]{1,0:T(8,128)(2,1)S(1)}, u32[]{:S(2)}, u32[]{:S(2)}) collective-permute-start(bf16[512,2048]{1,0:T(8,128)(2,1)} %get-tuple-element.2314.refs_0_), channel_id=1, source_target_pairs={{0,8},{4,12},{8,0},{12,4},{16,24},{20,28},{24,16},{28,20},{1,9},{5... | collective-permute-start | bytes 6291464 | tf_op jit(solution)/shard_map/ppermute | solution.py:318
  458.2 54.5 %collective-permute-start.38 = (bf16[512,2048]{1,0:T(8,128)(2,1)}, bf16[512,2048]{1,0:T(8,128)(2,1)}, u32[]{:S(2)}, u32[]{:S(2)}) collective-permute-start(bf16[512,2048]{1,0:T(8,128)(2,1)} %get-tuple-element.2145), channel_id=1, source_target_pairs={{0,8},{4,12},{8,0},{12,4},{16,24},{20,28},{24,16},{28,20},{1,9},{5... | collective-permute-start | bytes 6291464 | tf_op jit(solution)/shard_map/ppermute | solution.py:318
  459.8 53.0 %collective-permute-start.39 = (bf16[512,2048]{1,0:T(8,128)(2,1)}, bf16[512,2048]{1,0:T(8,128)(2,1)}, u32[]{:S(2)}, u32[]{:S(2)}) collective-permute-start(bf16[512,2048]{1,0:T(8,128)(2,1)} %get-tuple-element.2146), channel_id=1, source_target_pairs={{0,16},{4,20},{8,24},{12,28},{16,0},{20,4},{24,8},{28,12},{1,17},{... | collective-permute-start | bytes 6291464 | tf_op jit(solution)/shard_map/ppermute | solution.py:318
  512.9 216.1 %reduce-scatter.5.cloned.1.call-start = ((), (), s32[]{:S(2)}) async-start(), calls=%async_computation.5 | async-start | bytes 7864320 | tf_op jit(solution)/shard_map/reduce_scatter | solution.py:1179
  543.3 55.6 %collective-permute-start.43 = (bf16[512,2048]{1,0:T(8,128)(2,1)}, bf16[512,2048]{1,0:T(8,128)(2,1)}, u32[]{:S(2)}, u32[]{:S(2)}) collective-permute-start(bf16[512,2048]{1,0:T(8,128)(2,1)} %get-tuple-element.2329), channel_id=1, source_target_pairs={{0,8},{4,12},{8,0},{12,4},{16,24},{20,28},{24,16},{28,20},{1,9},{5... | collective-permute-start | bytes 6291464 | tf_op jit(solution)/shard_map/ppermute | solution.py:318
  544.8 54.0 %collective-permute-start.44 = (bf16[512,2048]{1,0:T(8,128)(2,1)}, bf16[512,2048]{1,0:T(8,128)(2,1)}, u32[]{:S(2)}, u32[]{:S(2)}) collective-permute-start(bf16[512,2048]{1,0:T(8,128)(2,1)} %get-tuple-element.2330), channel_id=1, source_target_pairs={{0,16},{4,20},{8,24},{12,28},{16,0},{20,4},{24,8},{28,12},{1,17},{... | collective-permute-start | bytes 6291464 | tf_op jit(solution)/shard_map/ppermute | solution.py:318
  598.9 35.7 %collective-permute-start.47 = (bf16[2048,1024]{1,0:T(8,128)(2,1)}, bf16[2048,1024]{1,0:T(8,128)(2,1)S(1)}, u32[]{:S(2)}, u32[]{:S(2)}) collective-permute-start(bf16[2048,1024]{1,0:T(8,128)(2,1)} %row_outer.15), channel_id=1, source_target_pairs={{0,4},{4,0},{8,12},{12,8},{16,20},{20,16},{24,28},{28,24},{1,5},{5... | collective-permute-start | bytes 12582920 | tf_op jit(solution)/shard_map/ppermute | solution.py:318
  635.6 32.7 %collective-permute-start.50 = (bf16[512,768]{1,0:T(8,128)(2,1)}, bf16[512,768]{1,0:T(8,128)(2,1)S(1)}, u32[]{:S(2)}, u32[]{:S(2)}) collective-permute-start(bf16[512,768]{1,0:T(8,128)(2,1)} %reduce-scatter.3.cloned.1.call-done), channel_id=1, source_target_pairs={{0,16},{4,20},{8,24},{12,28},{16,0},{20,4},{24,8},{28,12},{1,17},{... | collective-permute-start | bytes 2359304 | tf_op jit(solution)/shard_map/ppermute | solution.py:318
  729.0 38.9 %collective-permute-start.65 = (bf16[2048,2048]{1,0:T(8,128)(2,1)}, bf16[2048,2048]{1,0:T(8,128)(2,1)}, u32[]{:S(2)}, u32[]{:S(2)}) collective-permute-start(bf16[2048,2048]{1,0:T(8,128)(2,1)} %row_outer.19), channel_id=1, source_target_pairs={{0,4},{4,0},{8,12},{12,8},{16,20},{20,16},{24,28},{28,24},{1,5},{5... | collective-permute-start | bytes 25165832 | tf_op jit(solution)/shard_map/ppermute | solution.py:318
  730.1 36.6 %collective-permute-start.62 = (bf16[512,1536]{1,0:T(8,128)(2,1)}, bf16[512,1536]{1,0:T(8,128)(2,1)S(1)}, u32[]{:S(2)}, u32[]{:S(2)}) collective-permute-start(bf16[512,1536]{1,0:T(8,128)(2,1)} %reduce-scatter.5.cloned.1.call-done), channel_id=1, source_target_pairs={{0,16},{4,20},{8,24},{12,28},{16,0},{20,4},{24,8},{28,12},{1,17},{... | collective-permute-start | bytes 4718600 | tf_op jit(solution)/shard_map/ppermute | solution.py:318
  731.6 36.3 %collective-permute-start.61 = (bf16[512,1536]{1,0:T(8,128)(2,1)}, bf16[512,1536]{1,0:T(8,128)(2,1)S(1)}, u32[]{:S(2)}, u32[]{:S(2)}) collective-permute-start(bf16[512,1536]{1,0:T(8,128)(2,1)} %reduce-scatter.5.cloned.1.call-done), channel_id=1, source_target_pairs={{0,8},{4,12},{8,0},{12,4},{16,24},{20,28},{24,16},{28,20},{1,9},{5... | collective-permute-start | bytes 4718600 | tf_op jit(solution)/shard_map/ppermute | solution.py:318
  770.2 36.5 %collective-permute-start.66 = (bf16[2048,768]{1,0:T(8,128)(2,1)S(1)}, bf16[2048,768]{1,0:T(8,128)(2,1)}, u32[]{:S(2)}, u32[]{:S(2)}) collective-permute-start(bf16[2048,768]{1,0:T(8,128)(2,1)S(1)} %constant_dynamic-update-slice_fusion.4.own_ref), channel_id=1, source_target_pairs={{0,4},{4,0},{8,12},{12,8},{16,20},{20,16},{24,28},{28,24},{1,5},{5... | collective-permute-start | bytes 9437192 | tf_op jit(solution)/shard_map/ppermute | solution.py:318
  770.3 36.3 %collective-permute-start.69 = (bf16[256,2048]{1,0:T(8,128)(2,1)}, bf16[256,2048]{1,0:T(8,128)(2,1)S(1)}, u32[]{:S(2)}, u32[]{:S(2)}) collective-permute-start(bf16[256,2048]{1,0:T(8,128)(2,1)} %get-tuple-element.2917), channel_id=1, source_target_pairs={{1,0},{0,1},{5,2},{4,3},{3,4},{2,5},{7,6},{6,7},{9,8},{8,9},{13,10... | collective-permute-start | bytes 3145736 | tf_op jit(solution)/shard_map/ppermute | solution.py:395
  773.0 33.6 %collective-permute-start.68 = (bf16[256,1536]{1,0:T(8,128)(2,1)}, bf16[256,1536]{1,0:T(8,128)(2,1)}, u32[]{:S(2)}, u32[]{:S(2)}) collective-permute-start(bf16[256,1536]{1,0:T(8,128)(2,1)} %slice.155), channel_id=1, source_target_pairs={{0,8},{4,12},{8,0},{12,4},{16,24},{20,28},{24,16},{28,20},{1,9},{5... | collective-permute-start | bytes 2359304 | tf_op jit(solution)/shard_map/ppermute | solution.py:318
  774.5 32.2 %collective-permute-start.67 = (bf16[256,1536]{1,0:T(8,128)(2,1)}, bf16[256,1536]{1,0:T(8,128)(2,1)}, u32[]{:S(2)}, u32[]{:S(2)}) collective-permute-start(bf16[256,1536]{1,0:T(8,128)(2,1)} %slice.154), channel_id=1, source_target_pairs={{0,16},{4,20},{8,24},{12,28},{16,0},{20,4},{24,8},{28,12},{1,17},{... | collective-permute-start | bytes 2359304 | tf_op jit(solution)/shard_map/ppermute | solution.py:318
  776.6 34.5 %collective-permute-start.74 = (bf16[256,2048]{1,0:T(8,128)(2,1)}, bf16[256,2048]{1,0:T(8,128)(2,1)}, u32[]{:S(2)}, u32[]{:S(2)}) collective-permute-start(bf16[256,2048]{1,0:T(8,128)(2,1)} %get-tuple-element.2916), channel_id=1, source_target_pairs={{0,0},{1,1},{4,2},{5,3},{2,4},{3,5},{6,6},{7,7},{8,8},{9,9},{12,10... | collective-permute-start | bytes 3145736 | tf_op jit(solution)/shard_map/ppermute | solution.py:395
  811.1 35.2 %collective-permute-start.79 = (bf16[256,2048]{1,0:T(8,128)(2,1)}, bf16[256,2048]{1,0:T(8,128)(2,1)S(1)}, u32[]{:S(2)}, u32[]{:S(2)}) collective-permute-start(bf16[256,2048]{1,0:T(8,128)(2,1)} %get-tuple-element.2915), channel_id=1, source_target_pairs={{1,0},{0,1},{5,2},{4,3},{3,4},{2,5},{7,6},{6,7},{9,8},{8,9},{13,10... | collective-permute-start | bytes 3145736 | tf_op jit(solution)/shard_map/ppermute | solution.py:395
  830.5 32.2 %collective-permute-start.77 = (bf16[1024,512]{1,0:T(8,128)(2,1)}, bf16[1024,512]{1,0:T(8,128)(2,1)}, u32[]{:S(2)}, u32[]{:S(2)}) collective-permute-start(bf16[1024,512]{1,0:T(8,128)(2,1)} %get-tuple-element.2765), channel_id=1, source_target_pairs={{0,8},{4,12},{8,0},{12,4},{16,24},{20,28},{24,16},{28,20},{1,9},{5... | collective-permute-start | bytes 3145736 | tf_op jit(solution)/shard_map/ppermute | solution.py:318
  831.1 31.6 %collective-permute-start.78 = (bf16[1024,512]{1,0:T(8,128)(2,1)}, bf16[1024,512]{1,0:T(8,128)(2,1)}, u32[]{:S(2)}, u32[]{:S(2)}) collective-permute-start(bf16[1024,512]{1,0:T(8,128)(2,1)} %get-tuple-element.2768), channel_id=1, source_target_pairs={{0,16},{4,20},{8,24},{12,28},{16,0},{20,4},{24,8},{28,12},{1,17},{... | collective-permute-start | bytes 3145736 | tf_op jit(solution)/shard_map/ppermute | solution.py:318
  (208 other events, 2405.4 us)
Sparse Core Ops, SparseCore 0:
  77.3 47.1 all-gather.2
  189.1 177.4 all-gather.4
  513.0 57.2 reduce-scatter.2
  599.0 107.9 reduce-scatter.4

commit v16 on v15

--- a/solution.py
+++ b/solution.py
@@ -1263,7 +1263,9 @@
             for call in (head_call, tail_call)
         ]
     )
-    tokens_sent = from_sequences_send(s.grad_tokens)
+    tokens_sent = from_sequences_send(
+        lax.optimization_barrier((s.grad_tokens, s.tail1[0]))[0]
+    )
     s.down_spread = jnp.concatenate([s.down_total, *s.down_near, *s.down_far], 0)
     s.down_spread_other = across(s.down_spread, CORE)
     s.output_second = output_sent[1]
@@ -1304,8 +1306,7 @@
     s.chunks1 = qkv_chunks(s.near1, s.far1, s.head1, s.tail1)
     s.ring1 = ring_sum_first(s.chunks1)
     s.gain_came = across(s.gain_parts, ACROSS_X)
-    (s.whole_gate_up,) = in_order([whole_call((units, units), s.gate_up_own, s.gate_up_other)])
-    del s.gate_up_own, s.gate_up_other
+    ((s.whole_gate,),) = in_order([whole_call((units,), s.gate_up_own, s.gate_up_other)])
     del s.near1, s.far1, s.head1, s.tail1
     s.end()
 
@@ -1315,6 +1316,8 @@
     s.last1 = around(rounded_sum(s.chunks1[3], s.ring1[0]), 1)
     s.gain_parts = s.gain_parts + s.gain_came
     s.gain_came = across(s.gain_parts, ACROSS_Y)
+    ((s.whole_up,),) = in_order([whole_call((units,), s.gate_up_own, s.gate_up_other, 1)])
+    del s.gate_up_own, s.gate_up_other
     del s.chunks0, s.ring0, s.last0, s.out_total
     s.end()
 
@@ -1359,7 +1362,8 @@
         s.narrow[head_dim:],
         s.whole0[1],
         s.wide[1],
-        *s.whole_gate_up,
+        s.whole_gate,
+        s.whole_up,
         *s.whole_down,
     )
 

time: 983 us -> 981 us (level)
    ppermute x12, waiting for transfers between devices: 41.6 us -> 60.6 us  [around(): lax.ppermute(x, 'shard', [(i, (i + by) % count) for i in range(count)])]
    ppermute x73, waiting for transfers between devices: 159 us -> 143 us  [across(): return lax.ppermute(x, 'rep', [(i, i ^ mask) for i in range(count)])]
    pallas_call x4 -> x5, Pallas kernels: 44.4 us -> 48.6 us  [whole_columns(): pl.pallas_call(body, grid_spec=pltpu.PrefetchScalarGridSpec(num_scalar_pr...]
    unnamed x282 -> x284, local copies, waits for them, and re-layouts: 21.4 us -> 23.9 us
  transfers between devices with their start and end apart: 107 -> 107, of which waited for: 34 -> 33; matrix products, arithmetic and copies ran while one was open for 10% -> 9% of each run, Pallas kernels for 39% -> 39%
where the time goes in v16:
time: 981 us; the launch traced here: 972 us
  Pallas kernels  428 us (44%)
  waiting for transfers between devices  273 us (28%)
  starting transfers between devices  129 us (13%)
  other arithmetic  64.8 us (7%)
  local copies, waits for them, and re-layouts  61.4 us (6%)
  between operations  16.2 us (2%)
    ppermute x73, waiting for transfers between devices, across(): return lax.ppermute(x, 'rep', [(i, i ^ mask) for i in range(count)])  143 us
    pallas_call x16, Pallas kernels, call(): pl.pallas_call(body, grid=(1,), out_shape=outs, in_specs=in_specs, out_sp...  119 us
    pallas_call x12, Pallas kernels, row_outer(): pl.pallas_call(body, grid=(tiles,), out_shape=[jax.ShapeDtypeStruct((tile...  114 us
    ppermute x73, starting transfers between devices, across(): return lax.ppermute(x, 'rep', [(i, i ^ mask) for i in range(count)])  69.4 us
    ppermute x12, waiting for transfers between devices, around(): lax.ppermute(x, 'shard', [(i, (i + by) % count) for i in range(count)])  60.6 us
    pallas_call x2, Pallas kernels, hidden_units(): pl.pallas_call(body, grid=(3,), out_shape=[jax.ShapeDtypeStruct((rows, un...  59.8 us
    pallas_call x4, Pallas kernels, from_hidden(): pl.pallas_call(body, grid=(4,), out_shape=[jax.ShapeDtypeStruct((2 * rows...  59.4 us
    ppermute x4, waiting for transfers between devices, to_sequence(): return lax.ppermute(cut, ('rep', 'shard'), sequence_pairs(turn))  51.7 us
  transfers between devices with their start and end apart: 107, of which 33 were waited for; matrix products, arithmetic and copies ran while one was open for 9% of the time, Pallas kernels for 39%

profile of v16, /device:TPU:0, one launch (start us, length us, event | category | flops | bytes accessed | tf_op | source)
XLA Modules:
  0.0 972.3 jit_solution(3723974778841718357)
XLA Ops:
  33.1 10.3 %collective-permute-done = bf16[528,512]{1,0:T(8,128)(2,1)} collective-permute-done((bf16[528,512]{1,0:T(8,128)(2,1)}, bf16[528,512]{1,0:T(8,128)(2,1)}, u32[]{:S(2)}, u32[]{:S(2)}) %collective-permute-start) | collective-permute-done | bytes 540704 | tf_op jit(solution)/shard_map/ppermute | solution.py:323
  45.1 13.5 %collective-permute-done.3 = bf16[528,512]{1,0:T(8,128)(2,1)S(1)} collective-permute-done((bf16[528,512]{1,0:T(8,128)(2,1)}, bf16[528,512]{1,0:T(8,128)(2,1)S(1)}, u32[]{:S(2)}, u32[]{:S(2)}) %collective-permute-start.3) | collective-permute-done | bytes 540704 | tf_op jit(solution)/shard_map/ppermute | solution.py:323
  64.9 9.4 collective-permute-start.7
  78.7 48.8 %collective-permute-done.8 = bf16[256,2048]{1,0:T(8,128)(2,1)} collective-permute-done((bf16[256,2048]{1,0:T(8,128)(2,1)S(1)}, bf16[256,2048]{1,0:T(8,128)(2,1)}, u32[]{:S(2)}, u32[]{:S(2)}) %collective-permute-start.8) | collective-permute-done | bytes 1048608 | tf_op jit(solution)/shard_map/ppermute | solution.py:388
  134.4 9.9 %collective-permute-start.14 = (bf16[256,2048]{1,0:T(8,128)(2,1)}, bf16[256,2048]{1,0:T(8,128)(2,1)}, u32[]{:S(2)}, u32[]{:S(2)}) collective-permute-start(bf16[256,2048]{1,0:T(8,128)(2,1)} %get-tuple-element.1517), channel_id=1, source_target_pairs={{0,0},{1,1},{2,4},{3,5},{4,2},{5,3},{6,6},{7,7},{8,8},{9,9},{10,12... | collective-permute-start | bytes 3145736 | tf_op jit(solution)/shard_map/ppermute | solution.py:388
  245.4 13.7 %collective-permute-done.28.refs_7_.refs_2_ = bf16[512,2048]{1,0:T(8,128)(2,1)S(1)} collective-permute-done((bf16[512,2048]{1,0:T(8,128)(2,1)S(1)}, bf16[512,2048]{1,0:T(8,128)(2,1)S(1)}, u32[]{:S(2)}, u32[]{:S(2)}) %collective-permute-start.28) | collective-permute-done | bytes 2097184 | tf_op jit(solution)/shard_map/ppermute | solution.py:318
  269.2 11.7 %close_attention.1 = (f32[512,2048]{1,0:T(8,128)}, bf16[512,2048]{1,0:T(8,128)(2,1)}) custom-call(bf16[512,2048]{1,0:T(8,128)(2,1)} %pad_maximum_fusion.3.x, bf16[512,512]{1,0:T(8,128)(2,1)} %get-tuple-element.2442.refs_0_.refs_1_.refs_4_, bf16[512,512]{1,0:T(8,128)(2,1)} %get-tuple-element.2439.refs_1_.refs_2_.refs_3_, ...), custom_call_target="tpu_custom_call" | custom-call | flops 1 | bytes 1 | tf_op jit(solution)/shard_map/close_attention/pallas_call | solution.py:789
  289.5 42.8 %collective-permute-done.33.refs_2_ = bf16[512,2048]{1,0:T(8,128)(2,1)S(1)} collective-permute-done((bf16[512,2048]{1,0:T(8,128)(2,1)}, bf16[512,2048]{1,0:T(8,128)(2,1)S(1)}, u32[]{:S(2)}, u32[]{:S(2)}) %collective-permute-start.33) | collective-permute-done | bytes 2097184 | tf_op jit(solution)/shard_map/ppermute | solution.py:318
  336.6 19.9 %collective-permute-done.35.refs_4_ = bf16[256,2048]{1,0:T(8,128)(2,1)S(1)} collective-permute-done((bf16[256,2048]{1,0:T(8,128)(2,1)S(1)}, bf16[256,2048]{1,0:T(8,128)(2,1)S(1)}, u32[]{:S(2)}, u32[]{:S(2)}) %collective-permute-start.35) | collective-permute-done | bytes 1048608 | tf_op jit(solution)/shard_map/ppermute | solution.py:318
  356.9 9.7 all-gather.5.cloned.1.call-done.refs_10_.refs_11_.refs_12_.refs_4_.refs_9_
  366.6 29.7 %hidden_units.2 = (bf16[2048,768]{1,0:T(8,128)(2,1)}, bf16[2048,768]{1,0:T(8,128)(2,1)}, bf16[2048,768]{1,0:T(8,128)(2,1)}) custom-call(bf16[512,2048]{1,0:T(8,128)(2,1)} %get-tuple-element.2314.refs_0_, bf16[512,2048]{1,0:T(8,128)(2,1)} %copy-done.14, bf16[512,2048]{1,0:T(8,128)(2,1)} %copy-done.13, bf16[256,2048]{1,0:T(8,128)(2,1)} %copy-done.23, ...), custom_call_target="tpu_custom_call" | custom-call | flops 1 | bytes 1 | tf_op jit(solution)/shard_map/hidden_units/pallas_call | solution.py:656
  396.3 30.1 %hidden_units.3 = (bf16[2048,768]{1,0:T(8,128)(2,1)}, bf16[2048,768]{1,0:T(8,128)(2,1)}, bf16[2048,768]{1,0:T(8,128)(2,1)}) custom-call(bf16[512,2048]{1,0:T(8,128)(2,1)} %get-tuple-element.2314.refs_0_, bf16[512,2048]{1,0:T(8,128)(2,1)} %copy-done.14, bf16[512,2048]{1,0:T(8,128)(2,1)} %copy-done.13, bf16[256,2048]{1,0:T(8,128)(2,1)} %copy-done.23, ...), custom_call_target="tpu_custom_call" | custom-call | flops 1 | bytes 1 | tf_op jit(solution)/shard_map/hidden_units/pallas_call | solution.py:656
  426.4 12.6 %row_outer.12 = bf16[2048,768]{1,0:T(8,128)(2,1)} custom-call(bf16[512,2048]{1,0:T(8,128)(2,1)} %copy-done.6, bf16[512,2048]{1,0:T(8,128)(2,1)} %copy-done.16, bf16[512,2048]{1,0:T(8,128)(2,1)} %copy-done.15, bf16[256,2048]{1,0:T(8,128)(2,1)} %copy-done.25, bf16[256,2048]{1,0:T(8,128)(2,1)} %copy-done.24, ...), custom_call_target="tpu_custom_call" | custom-call | flops 6442450944 | bytes 11534336 | tf_op jit(solution)/shard_map/row_outer/pallas_call | solution.py:739
  439.5 19.0 %from_hidden.4 = (bf16[512,2048]{1,0:T(8,128)(2,1)}, bf16[512,2048]{1,0:T(8,128)(2,1)}) custom-call(bf16[2048,768]{1,0:T(8,128)(2,1)} %get-tuple-element.2325.refs_0_.refs_1_.refs_2_.refs_3_.refs_5_, bf16[2048,768]{1,0:T(8,128)(2,1)} %get-tuple-element.2325.refs_0_.refs_1_.refs_2_.refs_3_.refs_5_, ...), custom_call_target="tpu_custom_call" | custom-call | flops 1 | bytes 1 | tf_op jit(solution)/shard_map/from_hidden/pallas_call | solution.py:695
  461.5 13.2 %row_outer.13 = bf16[2048,768]{1,0:T(8,128)(2,1)} custom-call(bf16[512,2048]{1,0:T(8,128)(2,1)} %copy-done.6, bf16[512,2048]{1,0:T(8,128)(2,1)} %copy-done.16, bf16[512,2048]{1,0:T(8,128)(2,1)} %copy-done.15, bf16[256,2048]{1,0:T(8,128)(2,1)} %copy-done.25, bf16[256,2048]{1,0:T(8,128)(2,1)} %copy-done.24, ...), custom_call_target="tpu_custom_call" | custom-call | flops 6442450944 | bytes 11534336 | tf_op jit(solution)/shard_map/row_outer/pallas_call | solution.py:739
  474.7 18.8 %from_hidden.5 = (bf16[512,2048]{1,0:T(8,128)(2,1)}, bf16[512,2048]{1,0:T(8,128)(2,1)}) custom-call(bf16[2048,768]{1,0:T(8,128)(2,1)} %get-tuple-element.2325.refs_0_.refs_1_.refs_2_.refs_3_.refs_5_, bf16[2048,768]{1,0:T(8,128)(2,1)} %get-tuple-element.2325.refs_0_.refs_1_.refs_2_.refs_3_.refs_5_, ...), custom_call_target="tpu_custom_call" | custom-call | flops 1 | bytes 1 | tf_op jit(solution)/shard_map/from_hidden/pallas_call | solution.py:695
  493.5 19.4 %row_outer.14 = bf16[2048,1536]{1,0:T(8,128)(2,1)} custom-call(bf16[512,2048]{1,0:T(8,128)(2,1)} %get-tuple-element.2314.refs_0_, bf16[512,2048]{1,0:T(8,128)(2,1)} %copy-done.14, bf16[512,2048]{1,0:T(8,128)(2,1)} %copy-done.13, bf16[256,2048]{1,0:T(8,128)(2,1)} %copy-done.23, bf16[256,2048]{1,0:T(8,128)(2,1)} %copy-done.22, ...), custom_call_target="tpu_custom_call" | custom-call | flops 12884901888 | bytes 14680064 | tf_op jit(solution)/shard_map/row_outer/pallas_call | solution.py:739
  519.9 10.7 %from_hidden.6 = (bf16[512,2048]{1,0:T(8,128)(2,1)}, bf16[512,2048]{1,0:T(8,128)(2,1)}) custom-call(bf16[2048,768]{1,0:T(8,128)(2,1)} %get-tuple-element.2234.refs_5_.refs_0_.refs_1_.refs_2_.refs_3_, bf16[2048,768]{1,0:T(8,128)(2,1)} %get-tuple-element.2234.refs_5_.refs_0_.refs_1_.refs_2_.refs_3_, ...), custom_call_target="tpu_custom_call" | custom-call | flops 1 | bytes 1 | tf_op jit(solution)/shard_map/from_hidden/pallas_call | solution.py:695
  530.7 10.9 %from_hidden.7 = (bf16[512,2048]{1,0:T(8,128)(2,1)}, bf16[512,2048]{1,0:T(8,128)(2,1)}) custom-call(bf16[2048,768]{1,0:T(8,128)(2,1)} %get-tuple-element.2234.refs_5_.refs_0_.refs_1_.refs_2_.refs_3_, bf16[2048,768]{1,0:T(8,128)(2,1)} %get-tuple-element.2234.refs_5_.refs_0_.refs_1_.refs_2_.refs_3_, ...), custom_call_target="tpu_custom_call" | custom-call | flops 1 | bytes 1 | tf_op jit(solution)/shard_map/from_hidden/pallas_call | solution.py:695
  555.8 13.3 %attend_back.4 = (bf16[512,512]{1,0:T(8,128)(2,1)}, f32[512,512]{1,0:T(8,128)}, bf16[512,512]{1,0:T(8,128)(2,1)}, f32[1,128]{1,0:T(1,128)}) custom-call(s32[2]{0:T(128)} %pad_add_fusion.info, bf16[512,512]{1,0:T(8,128)(2,1)} %get-tuple-element.2281.query, bf16[512,512]{1,0:T(8,128)(2,1)} %copy-done.43, bf16[512,512]{1,0:T(8,128)(2,1)} %get-tuple-element.2283.own, ...), custom_call_target="tpu_custom_call" | custom-call | flops 1 | bytes 1 | tf_op jit(solution)/shard_map/attend_back/pallas_call | solution.py:616
  579.2 19.7 %row_outer.16 = bf16[2048,1536]{1,0:T(8,128)(2,1)} custom-call(bf16[512,2048]{1,0:T(8,128)(2,1)} %get-tuple-element.2314.refs_0_, bf16[512,2048]{1,0:T(8,128)(2,1)} %copy-done.14, bf16[512,2048]{1,0:T(8,128)(2,1)} %copy-done.13, bf16[256,2048]{1,0:T(8,128)(2,1)} %copy-done.23, bf16[256,2048]{1,0:T(8,128)(2,1)} %copy-done.22, ...), custom_call_target="tpu_custom_call" | custom-call | flops 12884901888 | bytes 14680064 | tf_op jit(solution)/shard_map/row_outer/pallas_call | solution.py:739
  608.1 13.2 %attend_back.5 = (bf16[512,512]{1,0:T(8,128)(2,1)}, f32[512,512]{1,0:T(8,128)}, bf16[512,512]{1,0:T(8,128)(2,1)}, f32[1,128]{1,0:T(1,128)}) custom-call(s32[2]{0:T(128)} %pad_add_fusion.info, bf16[512,512]{1,0:T(8,128)(2,1)} %get-tuple-element.2364.query, bf16[512,512]{1,0:T(8,128)(2,1)} %copy-done.42, bf16[512,512]{1,0:T(8,128)(2,1)} %get-tuple-element.2366.own, ...), custom_call_target="tpu_custom_call" | custom-call | flops 1 | bytes 1 | tf_op jit(solution)/shard_map/attend_back/pallas_call | solution.py:616
  621.3 13.5 %attend_back.6 = (bf16[512,512]{1,0:T(8,128)(2,1)}, f32[512,512]{1,0:T(8,128)}, bf16[512,512]{1,0:T(8,128)(2,1)}, f32[1,128]{1,0:T(1,128)}) custom-call(s32[2]{0:T(128)} %pad_add_fusion.info, bf16[512,512]{1,0:T(8,128)(2,1)} %get-tuple-element.2379.query, bf16[512,512]{1,0:T(8,128)(2,1)} %collective-permute-done.21.before, ...), custom_call_target="tpu_custom_call" | custom-call | flops 1 | bytes 1 | tf_op jit(solution)/shard_map/attend_back/pallas_call | solution.py:616
  652.5 13.3 %attend_back.7 = (bf16[512,512]{1,0:T(8,128)(2,1)}, f32[512,512]{1,0:T(8,128)}, bf16[512,512]{1,0:T(8,128)(2,1)}, f32[1,128]{1,0:T(1,128)}) custom-call(s32[2]{0:T(128)} %pad_add_fusion.info, bf16[512,512]{1,0:T(8,128)(2,1)} %get-tuple-element.2447.query, bf16[512,512]{1,0:T(8,128)(2,1)} %copy-done.40, bf16[512,512]{1,0:T(8,128)(2,1)} %get-tuple-element.2449.own, ...), custom_call_target="tpu_custom_call" | custom-call | flops 1 | bytes 1 | tf_op jit(solution)/shard_map/attend_back/pallas_call | solution.py:616
  685.0 14.3 %collective-permute-done.53 = bf16[1024,512]{1,0:T(8,128)(2,1)S(1)} collective-permute-done((bf16[1024,512]{1,0:T(8,128)(2,1)}, bf16[1024,512]{1,0:T(8,128)(2,1)S(1)}, u32[]{:S(2)}, u32[]{:S(2)}) %collective-permute-start.53) | collective-permute-done | bytes 1048608 | tf_op jit(solution)/shard_map/ppermute | solution.py:318
  712.6 10.1 %row_outer.19 = bf16[2048,2048]{1,0:T(8,128)(2,1)} custom-call(bf16[512,2048]{1,0:T(8,128)(2,1)} %pad_maximum_fusion.4.normed.refs_0_, bf16[512,512]{1,0:T(8,128)(2,1)} %get-tuple-element.2643.refs_1_, bf16[512,512]{1,0:T(8,128)(2,1)} %get-tuple-element.2646.refs_2_.refs_3_, bf16[512,512]{1,0:T(8,128)(2,1)} %get-tuple-element.2649.refs_3_.refs_5_, ...), custom_call_target="tpu_custom_call" | custom-call | flops 4294967296 | bytes 4194304 | tf_op jit(solution)/shard_map/row_outer/pallas_call | solution.py:739
  739.9 15.8 %back_to_rows.1 = f32[512,2048]{1,0:T(8,128)} custom-call(bf16[512,512]{1,0:T(8,128)(2,1)} %get-tuple-element.2702.refs_0_.refs_4_, bf16[512,512]{1,0:T(8,128)(2,1)} %get-tuple-element.2643.refs_1_, bf16[512,512]{1,0:T(8,128)(2,1)} %get-tuple-element.2699.refs_2_.refs_1_.refs_3_, bf16[512,512]{1,0:T(8,128)(2,1)} %get-tuple-element.2646.refs_2_.refs_3_, ...), custom_call_target="tpu_custom_call" | custom-call | flops 1 | bytes 1 | tf_op jit(solution)/shard_map/back_to_rows/pallas_call | solution.py:842
  806.1 22.8 %collective-permute-done.73 = bf16[512,256]{1,0:T(8,128)(2,1)S(1)} collective-permute-done((bf16[512,256]{1,0:T(8,128)(2,1)S(1)}, bf16[512,256]{1,0:T(8,128)(2,1)S(1)}, u32[]{:S(2)}, u32[]{:S(2)}) %collective-permute-start.73) | collective-permute-done | bytes 262176 | tf_op jit(solution)/shard_map/ppermute | solution.py:323
  835.1 11.2 %whole_columns.5 = f32[512,6144]{1,0:T(8,128)} custom-call(s32[1]{0:T(128)} %bitcast.21.me_ref, bf16[2048,768]{1,0:T(8,128)(2,1)} %copy-done.21, bf16[2048,768]{1,0:T(8,128)(2,1)} %collective-permute-done.66.other_ref), custom_call_target="tpu_custom_call" | custom-call | flops 1 | bytes 1 | tf_op jit(solution)/shard_map/whole_columns/pallas_call | solution.py:431
  850.7 17.3 %collective-permute-done.77 = bf16[1024,512]{1,0:T(8,128)(2,1)S(1)} collective-permute-done((bf16[1024,512]{1,0:T(8,128)(2,1)}, bf16[1024,512]{1,0:T(8,128)(2,1)S(1)}, u32[]{:S(2)}, u32[]{:S(2)}) %collective-permute-start.77) | collective-permute-done | bytes 1048608 | tf_op jit(solution)/shard_map/ppermute | solution.py:318
  892.6 11.0 %whole_columns.6 = f32[512,6144]{1,0:T(8,128)} custom-call(s32[1]{0:T(128)} %bitcast.21.me_ref, bf16[2048,1536]{1,0:T(8,128)(2,1)} %copy-done.9, bf16[2048,1536]{1,0:T(8,128)(2,1)} %copy-done.10), custom_call_target="tpu_custom_call" | custom-call | flops 1 | bytes 1 | tf_op jit(solution)/shard_map/whole_columns/pallas_call | solution.py:431
  910.5 11.0 %whole_columns.7 = f32[512,6144]{1,0:T(8,128)} custom-call(s32[1]{0:T(128)} %bitcast.21.me_ref, bf16[2048,1536]{1,0:T(8,128)(2,1)} %copy-done.9, bf16[2048,1536]{1,0:T(8,128)(2,1)} %copy-done.10), custom_call_target="tpu_custom_call" | custom-call | flops 1 | bytes 1 | tf_op jit(solution)/shard_map/whole_columns/pallas_call | solution.py:431
  (653 shorter events, 415.5 us)
Async XLA Ops:
  7.2 144.5 %all-gather.3.cloned.1.call-start = ((), (), s32[]{:S(2)}) async-start(), calls=%async_computation.2 | async-start | bytes 1310720 | tf_op jit(solution)/shard_map/all_gather | solution.py:903
  61.2 66.3 %collective-permute-start.6 = (bf16[1536,512]{1,0:T(8,128)(2,1)S(1)}, bf16[1536,512]{1,0:T(8,128)(2,1)}, u32[]{:S(2)}, u32[]{:S(2)}) collective-permute-start(bf16[1536,512]{1,0:T(8,128)(2,1)S(1)} %pad_maximum_fusion.8.came0.refs_9_), channel_id=1, source_target_pairs={{0,4},{4,0},{8,12},{12,8},{16,20},{20,16},{24,28},{28,24},{1,5},{5... | collective-permute-start | bytes 4718600 | tf_op jit(solution)/shard_map/ppermute | solution.py:318
  61.3 66.2 %collective-permute-start.5 = (bf16[1536,512]{1,0:T(8,128)(2,1)S(1)}, bf16[1536,512]{1,0:T(8,128)(2,1)}, u32[]{:S(2)}, u32[]{:S(2)}) collective-permute-start(bf16[1536,512]{1,0:T(8,128)(2,1)S(1)} %pad_maximum_fusion.8.came0.refs_9_), channel_id=1, source_target_pairs={{0,16},{4,20},{8,24},{12,28},{16,0},{20,4},{24,8},{28,12},{1,17},{... | collective-permute-start | bytes 4718600 | tf_op jit(solution)/shard_map/ppermute | solution.py:318
  62.8 64.7 %collective-permute-start.4 = (bf16[1536,512]{1,0:T(8,128)(2,1)S(1)}, bf16[1536,512]{1,0:T(8,128)(2,1)}, u32[]{:S(2)}, u32[]{:S(2)}) collective-permute-start(bf16[1536,512]{1,0:T(8,128)(2,1)S(1)} %pad_maximum_fusion.8.came0.refs_9_), channel_id=1, source_target_pairs={{0,8},{4,12},{8,0},{12,4},{16,24},{20,28},{24,16},{28,20},{1,9},{5... | collective-permute-start | bytes 4718600 | tf_op jit(solution)/shard_map/ppermute | solution.py:318
  74.3 53.2 %collective-permute-start.8 = (bf16[256,2048]{1,0:T(8,128)(2,1)S(1)}, bf16[256,2048]{1,0:T(8,128)(2,1)}, u32[]{:S(2)}, u32[]{:S(2)}) collective-permute-start(bf16[256,2048]{1,0:T(8,128)(2,1)S(1)} %get-tuple-element.1487), channel_id=1, source_target_pairs={{0,1},{1,0},{2,5},{3,4},{4,3},{5,2},{6,7},{7,6},{8,9},{9,8},{10,13... | collective-permute-start | bytes 3145736 | tf_op jit(solution)/shard_map/ppermute | solution.py:388
  77.2 289.3 %all-gather.5.cloned.1.call-start = ((), (), s32[]{:S(2)}) async-start(), calls=%async_computation.3 | async-start | bytes 11796480 | tf_op jit(solution)/shard_map/all_gather | solution.py:995
  155.6 31.6 %collective-permute-start.13 = (bf16[1536,512]{1,0:T(8,128)(2,1)S(1)}, bf16[1536,512]{1,0:T(8,128)(2,1)S(1)}, u32[]{:S(2)}, u32[]{:S(2)}) collective-permute-start(bf16[1536,512]{1,0:T(8,128)(2,1)S(1)} %constant_dynamic-update-slice_fusion.came0.refs_21_), channel_id=1, source_target_pairs={{0,4},{4,0},{8,12},{12,8},{16,20},{20,16},{24,28},{28,24},{1,5},{5... | collective-permute-start | bytes 4718600 | tf_op jit(solution)/shard_map/ppermute | solution.py:318
  155.6 31.4 %collective-permute-start.15 = (bf16[256,2048]{1,0:T(8,128)(2,1)}, bf16[256,2048]{1,0:T(8,128)(2,1)S(1)}, u32[]{:S(2)}, u32[]{:S(2)}) collective-permute-start(bf16[256,2048]{1,0:T(8,128)(2,1)} %get-tuple-element.1518), channel_id=1, source_target_pairs={{0,1},{1,0},{2,5},{3,4},{4,3},{5,2},{6,7},{7,6},{8,9},{9,8},{10,13... | collective-permute-start | bytes 3145736 | tf_op jit(solution)/shard_map/ppermute | solution.py:388
  188.9 409.9 %reduce-scatter.3.cloned.1.call-start = ((), (), s32[]{:S(2)}) async-start(), calls=%async_computation.4 | async-start | bytes 3932160 | tf_op jit(solution)/shard_map/reduce_scatter | solution.py:1111
  190.1 34.5 %collective-permute-start.24 = (bf16[2048,256]{1,0:T(8,128)(2,1)}, bf16[2048,256]{1,0:T(8,128)(2,1)}, u32[]{:S(2)}, u32[]{:S(2)}) collective-permute-start(bf16[2048,256]{1,0:T(8,128)(2,1)} %collective-permute-done.16.refs_6_.weight0), channel_id=1, source_target_pairs={{0,4},{4,0},{8,12},{12,8},{16,20},{20,16},{24,28},{28,24},{1,5},{5... | collective-permute-start | bytes 3145736 | tf_op jit(solution)/shard_map/ppermute | solution.py:318
  211.4 47.7 %collective-permute-start.28 = (bf16[512,2048]{1,0:T(8,128)(2,1)S(1)}, bf16[512,2048]{1,0:T(8,128)(2,1)S(1)}, u32[]{:S(2)}, u32[]{:S(2)}) collective-permute-start(bf16[512,2048]{1,0:T(8,128)(2,1)S(1)} %maximum_select_fusion.refs_5_.refs_0_), channel_id=1, source_target_pairs={{0,16},{4,20},{8,24},{12,28},{16,0},{20,4},{24,8},{28,12},{1,17},{... | collective-permute-start | bytes 6291464 | tf_op jit(solution)/shard_map/ppermute | solution.py:318
  213.9 46.6 %collective-permute-start.27 = (bf16[512,2048]{1,0:T(8,128)(2,1)S(1)}, bf16[512,2048]{1,0:T(8,128)(2,1)S(1)}, u32[]{:S(2)}, u32[]{:S(2)}) collective-permute-start(bf16[512,2048]{1,0:T(8,128)(2,1)S(1)} %maximum_select_fusion.refs_5_.refs_0_), channel_id=1, source_target_pairs={{0,8},{4,12},{8,0},{12,4},{16,24},{20,28},{24,16},{28,20},{1,9},{5... | collective-permute-start | bytes 6291464 | tf_op jit(solution)/shard_map/ppermute | solution.py:318
  287.0 45.2 %collective-permute-start.33 = (bf16[512,2048]{1,0:T(8,128)(2,1)}, bf16[512,2048]{1,0:T(8,128)(2,1)S(1)}, u32[]{:S(2)}, u32[]{:S(2)}) collective-permute-start(bf16[512,2048]{1,0:T(8,128)(2,1)} %get-tuple-element.2314.refs_0_), channel_id=1, source_target_pairs={{0,16},{4,20},{8,24},{12,28},{16,0},{20,4},{24,8},{28,12},{1,17},{... | collective-permute-start | bytes 6291464 | tf_op jit(solution)/shard_map/ppermute | solution.py:318
  288.3 45.2 %collective-permute-start.32 = (bf16[512,2048]{1,0:T(8,128)(2,1)}, bf16[512,2048]{1,0:T(8,128)(2,1)S(1)}, u32[]{:S(2)}, u32[]{:S(2)}) collective-permute-start(bf16[512,2048]{1,0:T(8,128)(2,1)} %get-tuple-element.2314.refs_0_), channel_id=1, source_target_pairs={{0,8},{4,12},{8,0},{12,4},{16,24},{20,28},{24,16},{28,20},{1,9},{5... | collective-permute-start | bytes 6291464 | tf_op jit(solution)/shard_map/ppermute | solution.py:318
  458.5 54.5 %collective-permute-start.38 = (bf16[512,2048]{1,0:T(8,128)(2,1)}, bf16[512,2048]{1,0:T(8,128)(2,1)}, u32[]{:S(2)}, u32[]{:S(2)}) collective-permute-start(bf16[512,2048]{1,0:T(8,128)(2,1)} %get-tuple-element.2145), channel_id=1, source_target_pairs={{0,8},{4,12},{8,0},{12,4},{16,24},{20,28},{24,16},{28,20},{1,9},{5... | collective-permute-start | bytes 6291464 | tf_op jit(solution)/shard_map/ppermute | solution.py:318
  460.0 52.9 %collective-permute-start.39 = (bf16[512,2048]{1,0:T(8,128)(2,1)}, bf16[512,2048]{1,0:T(8,128)(2,1)}, u32[]{:S(2)}, u32[]{:S(2)}) collective-permute-start(bf16[512,2048]{1,0:T(8,128)(2,1)} %get-tuple-element.2146), channel_id=1, source_target_pairs={{0,16},{4,20},{8,24},{12,28},{16,0},{20,4},{24,8},{28,12},{1,17},{... | collective-permute-start | bytes 6291464 | tf_op jit(solution)/shard_map/ppermute | solution.py:318
  512.9 30.6 %collective-permute-start.40 = (bf16[2048,1536]{1,0:T(8,128)(2,1)}, bf16[2048,1536]{1,0:T(8,128)(2,1)}, u32[]{:S(2)}, u32[]{:S(2)}) collective-permute-start(bf16[2048,1536]{1,0:T(8,128)(2,1)} %row_outer.14), channel_id=1, source_target_pairs={{0,4},{4,0},{8,12},{12,8},{16,20},{20,16},{24,28},{28,24},{1,5},{5... | collective-permute-start | bytes 18874376 | tf_op jit(solution)/shard_map/ppermute | solution.py:318
  513.1 214.6 %reduce-scatter.5.cloned.1.call-start = ((), (), s32[]{:S(2)}) async-start(), calls=%async_computation.5 | async-start | bytes 7864320 | tf_op jit(solution)/shard_map/reduce_scatter | solution.py:1179
  543.5 55.4 %collective-permute-start.43 = (bf16[512,2048]{1,0:T(8,128)(2,1)}, bf16[512,2048]{1,0:T(8,128)(2,1)}, u32[]{:S(2)}, u32[]{:S(2)}) collective-permute-start(bf16[512,2048]{1,0:T(8,128)(2,1)} %get-tuple-element.2329), channel_id=1, source_target_pairs={{0,8},{4,12},{8,0},{12,4},{16,24},{20,28},{24,16},{28,20},{1,9},{5... | collective-permute-start | bytes 6291464 | tf_op jit(solution)/shard_map/ppermute | solution.py:318
  545.0 53.8 %collective-permute-start.44 = (bf16[512,2048]{1,0:T(8,128)(2,1)}, bf16[512,2048]{1,0:T(8,128)(2,1)}, u32[]{:S(2)}, u32[]{:S(2)}) collective-permute-start(bf16[512,2048]{1,0:T(8,128)(2,1)} %get-tuple-element.2330), channel_id=1, source_target_pairs={{0,16},{4,20},{8,24},{12,28},{16,0},{20,4},{24,8},{28,12},{1,17},{... | collective-permute-start | bytes 6291464 | tf_op jit(solution)/shard_map/ppermute | solution.py:318
  598.9 36.0 %collective-permute-start.47 = (bf16[2048,1024]{1,0:T(8,128)(2,1)}, bf16[2048,1024]{1,0:T(8,128)(2,1)S(1)}, u32[]{:S(2)}, u32[]{:S(2)}) collective-permute-start(bf16[2048,1024]{1,0:T(8,128)(2,1)} %row_outer.15), channel_id=1, source_target_pairs={{0,4},{4,0},{8,12},{12,8},{16,20},{20,16},{24,28},{28,24},{1,5},{5... | collective-permute-start | bytes 12582920 | tf_op jit(solution)/shard_map/ppermute | solution.py:318
  603.9 31.0 %collective-permute-start.46 = (bf16[256,2048]{1,0:T(8,128)(2,1)}, bf16[256,2048]{1,0:T(8,128)(2,1)S(1)}, u32[]{:S(2)}, u32[]{:S(2)}) collective-permute-start(bf16[256,2048]{1,0:T(8,128)(2,1)} %get-tuple-element.2921), channel_id=1, source_target_pairs={{0,16},{4,20},{8,24},{12,28},{16,0},{20,4},{24,8},{28,12},{1,17},{... | collective-permute-start | bytes 3145736 | tf_op jit(solution)/shard_map/ppermute | solution.py:318
  637.0 32.7 %collective-permute-start.50 = (bf16[512,768]{1,0:T(8,128)(2,1)}, bf16[512,768]{1,0:T(8,128)(2,1)S(1)}, u32[]{:S(2)}, u32[]{:S(2)}) collective-permute-start(bf16[512,768]{1,0:T(8,128)(2,1)} %reduce-scatter.3.cloned.1.call-done), channel_id=1, source_target_pairs={{0,16},{4,20},{8,24},{12,28},{16,0},{20,4},{24,8},{28,12},{1,17},{... | collective-permute-start | bytes 2359304 | tf_op jit(solution)/shard_map/ppermute | solution.py:318
  638.5 31.3 %collective-permute-start.49 = (bf16[512,768]{1,0:T(8,128)(2,1)}, bf16[512,768]{1,0:T(8,128)(2,1)S(1)}, u32[]{:S(2)}, u32[]{:S(2)}) collective-permute-start(bf16[512,768]{1,0:T(8,128)(2,1)} %reduce-scatter.3.cloned.1.call-done), channel_id=1, source_target_pairs={{0,8},{4,12},{8,0},{12,4},{16,24},{20,28},{24,16},{28,20},{1,9},{5... | collective-permute-start | bytes 2359304 | tf_op jit(solution)/shard_map/ppermute | solution.py:318
  639.1 30.6 %collective-permute-start.51 = (bf16[512,512]{1,0:T(8,128)(2,1)}, bf16[512,512]{1,0:T(8,128)(2,1)}, u32[]{:S(2)}, u32[]{:S(2)}) collective-permute-start(bf16[512,512]{1,0:T(8,128)(2,1)} %get-tuple-element.2463), channel_id=1, source_target_pairs={{4,0},{12,8},{20,16},{28,24},{5,1},{13,9},{21,17},{29,25},{6,2},{1... | collective-permute-start | bytes 1572872 | tf_op jit(solution)/shard_map/ppermute | solution.py:1139
  727.6 40.6 %collective-permute-start.65 = (bf16[2048,2048]{1,0:T(8,128)(2,1)}, bf16[2048,2048]{1,0:T(8,128)(2,1)}, u32[]{:S(2)}, u32[]{:S(2)}) collective-permute-start(bf16[2048,2048]{1,0:T(8,128)(2,1)} %row_outer.19), channel_id=1, source_target_pairs={{0,4},{4,0},{8,12},{12,8},{16,20},{20,16},{24,28},{28,24},{1,5},{5... | collective-permute-start | bytes 25165832 | tf_op jit(solution)/shard_map/ppermute | solution.py:318
  730.7 36.6 %collective-permute-start.62 = (bf16[512,1536]{1,0:T(8,128)(2,1)}, bf16[512,1536]{1,0:T(8,128)(2,1)S(1)}, u32[]{:S(2)}, u32[]{:S(2)}) collective-permute-start(bf16[512,1536]{1,0:T(8,128)(2,1)} %reduce-scatter.5.cloned.1.call-done), channel_id=1, source_target_pairs={{0,16},{4,20},{8,24},{12,28},{16,0},{20,4},{24,8},{28,12},{1,17},{... | collective-permute-start | bytes 4718600 | tf_op jit(solution)/shard_map/ppermute | solution.py:318
  731.6 36.6 %collective-permute-start.61 = (bf16[512,1536]{1,0:T(8,128)(2,1)}, bf16[512,1536]{1,0:T(8,128)(2,1)S(1)}, u32[]{:S(2)}, u32[]{:S(2)}) collective-permute-start(bf16[512,1536]{1,0:T(8,128)(2,1)} %reduce-scatter.5.cloned.1.call-done), channel_id=1, source_target_pairs={{0,8},{4,12},{8,0},{12,4},{16,24},{20,28},{24,16},{28,20},{1,9},{5... | collective-permute-start | bytes 4718600 | tf_op jit(solution)/shard_map/ppermute | solution.py:318
  798.8 30.2 %collective-permute-start.71 = (bf16[1024,512]{1,0:T(8,128)(2,1)S(1)}, bf16[1024,512]{1,0:T(8,128)(2,1)S(1)}, u32[]{:S(2)}, u32[]{:S(2)}) collective-permute-start(bf16[1024,512]{1,0:T(8,128)(2,1)S(1)} %copy-done.131), channel_id=1, source_target_pairs={{0,8},{4,12},{8,0},{12,4},{16,24},{20,28},{24,16},{28,20},{1,9},{5... | collective-permute-start | bytes 3145736 | tf_op jit(solution)/shard_map/ppermute | solution.py:318
  805.3 45.4 %collective-permute-start.79 = (bf16[256,2048]{1,0:T(8,128)(2,1)}, bf16[256,2048]{1,0:T(8,128)(2,1)S(1)}, u32[]{:S(2)}, u32[]{:S(2)}) collective-permute-start(bf16[256,2048]{1,0:T(8,128)(2,1)} %get-tuple-element.2915), channel_id=1, source_target_pairs={{1,0},{0,1},{5,2},{4,3},{3,4},{2,5},{7,6},{6,7},{9,8},{8,9},{13,10... | collective-permute-start | bytes 3145736 | tf_op jit(solution)/shard_map/ppermute | solution.py:395
  832.1 36.0 %collective-permute-start.77 = (bf16[1024,512]{1,0:T(8,128)(2,1)}, bf16[1024,512]{1,0:T(8,128)(2,1)S(1)}, u32[]{:S(2)}, u32[]{:S(2)}) collective-permute-start(bf16[1024,512]{1,0:T(8,128)(2,1)} %get-tuple-element.2766), channel_id=1, source_target_pairs={{0,8},{4,12},{8,0},{12,4},{16,24},{20,28},{24,16},{28,20},{1,9},{5... | collective-permute-start | bytes 3145736 | tf_op jit(solution)/shard_map/ppermute | solution.py:318
  833.8 34.2 %collective-permute-start.78 = (bf16[1024,512]{1,0:T(8,128)(2,1)}, bf16[1024,512]{1,0:T(8,128)(2,1)S(1)}, u32[]{:S(2)}, u32[]{:S(2)}) collective-permute-start(bf16[1024,512]{1,0:T(8,128)(2,1)} %get-tuple-element.2769), channel_id=1, source_target_pairs={{0,16},{4,20},{8,24},{12,28},{16,0},{20,4},{24,8},{28,12},{1,17},{... | collective-permute-start | bytes 3145736 | tf_op jit(solution)/shard_map/ppermute | solution.py:318
  (209 other events, 2407.0 us)
Sparse Core Ops, SparseCore 0:
  77.3 47.1 all-gather.2
  189.1 177.4 all-gather.4
  513.2 57.2 reduce-scatter.2
  599.0 108.0 reduce-scatter.4

commit v17 on v16

--- a/solution.py
+++ b/solution.py
@@ -882,6 +882,7 @@
     count = lax.axis_size("rep")
 
     s = Stage()
+    s.cotangent = cotangent
     piece = width // shards
 
     s.own_blocks = [
@@ -891,7 +892,7 @@
         [jnp.stack([attn_gain, mlp_gain]), jnp.zeros((14, piece), low)], 0
     )
     travelling = jnp.concatenate([s.own_blocks[0], gain_rows], 0)
-    s.tokens_cuts, s.cotangent_cuts = sequence_cuts(tokens), sequence_cuts(cotangent)
+    s.tokens = tokens
     s.out_block = column_block((w_out,), me)
     s.ffn_block = column_block((w_gate, w_up, w_down), me)
     s.before, s.behind = around(travelling, 1), around(travelling, -1)
@@ -899,9 +900,9 @@
     s.end()
 
     s.ahead = around(s.before, 1)
-    tokens_sent = [to_sequence(cut, turn) for turn, cut in enumerate(s.tokens_cuts)]
+    tokens_sent = [to_sequence(cut, turn) for turn, cut in enumerate(sequence_cuts(s.tokens))]
     out_own = lax.all_gather(s.out_block, "shard", axis=0, tiled=True)
-    del s.out_block, s.tokens_cuts
+    del s.out_block, s.tokens
     s.end()
 
     parts = (s.before, s.ahead, s.behind)
@@ -913,7 +914,9 @@
     del s.before, s.behind, s.ahead
     s.end()
 
-    grad_y_sent = [to_sequence(cut, turn) for turn, cut in enumerate(s.cotangent_cuts)]
+    grad_y_sent = [
+        to_sequence(cut, turn) for turn, cut in enumerate(sequence_cuts(s.cotangent))
+    ]
     s.came_far = far(*s.came_near)
     s.came_other = [s.came_own, *(across(block, CORE) for block in s.came_near)]
     gains = rolled(s.gains.astype(full))
@@ -940,7 +943,7 @@
     s.cosine, sine = cosine[0, :, 0], sine[0, :, 0]
     s.sine = jnp.concatenate([-sine[:, : head_dim // 2], sine[:, head_dim // 2 :]], 1)
     s.out_own = out_own
-    del s.gains, s.x_came, s.other_lengths, s.cotangent_cuts, s.came_own
+    del s.gains, s.x_came, s.other_lengths, s.cotangent, s.came_own
     s.end()
 
     head_columns = 2 * head_dim

time: 981 us -> 975 us (level)
  waiting for transfers between devices: 273 us -> 249 us
  starting transfers between devices: 129 us -> 142 us
    ppermute x4, waiting for transfers between devices: 51.7 us -> 21.5 us  [to_sequence(): return lax.ppermute(cut, ('rep', 'shard'), sequence_pairs(turn))]
    ppermute x73, starting transfers between devices: 69.4 us -> 95.7 us  [across(): return lax.ppermute(x, 'rep', [(i, i ^ mask) for i in range(count)])]
    ppermute x4, starting transfers between devices: 24.4 us -> 11.8 us  [to_sequence(): return lax.ppermute(cut, ('rep', 'shard'), sequence_pairs(turn))]
    ppermute x73, waiting for transfers between devices: 143 us -> 153 us  [across(): return lax.ppermute(x, 'rep', [(i, i ^ mask) for i in range(count)])]
    unnamed x284 -> x278, local copies, waits for them, and re-layouts: 23.9 us -> 23.6 us
  transfers between devices with their start and end apart: 107 -> 107, of which waited for: 33 -> 36; matrix products, arithmetic and copies ran while one was open for 9% -> 10% of each run, Pallas kernels for 39% -> 39%
where the time goes in v17:
time: 975 us; the launch traced here: 965 us
  Pallas kernels  428 us (44%)
  waiting for transfers between devices  249 us (26%)
  starting transfers between devices  142 us (15%)
  local copies, waits for them, and re-layouts  64.8 us (7%)
  other arithmetic  64.7 us (7%)
  between operations  16.2 us (2%)
    ppermute x73, waiting for transfers between devices, across(): return lax.ppermute(x, 'rep', [(i, i ^ mask) for i in range(count)])  153 us
    pallas_call x16, Pallas kernels, call(): pl.pallas_call(body, grid=(1,), out_shape=outs, in_specs=in_specs, out_sp...  119 us
    pallas_call x12, Pallas kernels, row_outer(): pl.pallas_call(body, grid=(tiles,), out_shape=[jax.ShapeDtypeStruct((tile...  114 us
    ppermute x73, starting transfers between devices, across(): return lax.ppermute(x, 'rep', [(i, i ^ mask) for i in range(count)])  95.7 us
    ppermute x12, waiting for transfers between devices, around(): lax.ppermute(x, 'shard', [(i, (i + by) % count) for i in range(count)])  62.4 us
    pallas_call x2, Pallas kernels, hidden_units(): pl.pallas_call(body, grid=(3,), out_shape=[jax.ShapeDtypeStruct((rows, un...  60.3 us
    pallas_call x4, Pallas kernels, from_hidden(): pl.pallas_call(body, grid=(4,), out_shape=[jax.ShapeDtypeStruct((2 * rows...  59.2 us
    pallas_call x5, Pallas kernels, whole_columns(): pl.pallas_call(body, grid_spec=pltpu.PrefetchScalarGridSpec(num_scalar_pr...  48.6 us
  transfers between devices with their start and end apart: 107, of which 36 were waited for; matrix products, arithmetic and copies ran while one was open for 10% of the time, Pallas kernels for 39%

profile of v17, /device:TPU:0, one launch (start us, length us, event | category | flops | bytes accessed | tf_op | source)
XLA Modules:
  0.0 964.7 jit_solution(9894331588204806962)
XLA Ops:
  32.0 11.3 %collective-permute-done = bf16[528,512]{1,0:T(8,128)(2,1)} collective-permute-done((bf16[528,512]{1,0:T(8,128)(2,1)}, bf16[528,512]{1,0:T(8,128)(2,1)}, u32[]{:S(2)}, u32[]{:S(2)}) %collective-permute-start) | collective-permute-done | bytes 540704 | tf_op jit(solution)/shard_map/ppermute | solution.py:323
  45.0 13.5 %collective-permute-done.3 = bf16[528,512]{1,0:T(8,128)(2,1)S(1)} collective-permute-done((bf16[528,512]{1,0:T(8,128)(2,1)}, bf16[528,512]{1,0:T(8,128)(2,1)S(1)}, u32[]{:S(2)}, u32[]{:S(2)}) %collective-permute-start.3) | collective-permute-done | bytes 540704 | tf_op jit(solution)/shard_map/ppermute | solution.py:323
  67.9 9.5 collective-permute-start.7
  81.9 19.1 %collective-permute-done.8 = bf16[256,2048]{1,0:T(8,128)(2,1)S(1)} collective-permute-done((bf16[256,2048]{1,0:T(8,128)(2,1)}, bf16[256,2048]{1,0:T(8,128)(2,1)S(1)}, u32[]{:S(2)}, u32[]{:S(2)}) %collective-permute-start.8) | collective-permute-done | bytes 1048608 | tf_op jit(solution)/shard_map/ppermute | solution.py:388
  103.1 31.1 %collective-permute-start.11 = (bf16[1536,512]{1,0:T(8,128)(2,1)}, bf16[1536,512]{1,0:T(8,128)(2,1)}, u32[]{:S(2)}, u32[]{:S(2)}) collective-permute-start(bf16[1536,512]{1,0:T(8,128)(2,1)} %collective-permute-done.4.came0.refs_13_), channel_id=1, source_target_pairs={{0,4},{4,0},{8,12},{12,8},{16,20},{20,16},{24,28},{28,24},{1,5},{5... | collective-permute-start | bytes 4718600 | tf_op jit(solution)/shard_map/ppermute | solution.py:318
  147.9 10.6 %collective-permute-done.10 = bf16[768,512]{1,0:T(8,128)(2,1)} collective-permute-done((bf16[768,512]{1,0:T(8,128)(2,1)}, bf16[768,512]{1,0:T(8,128)(2,1)}, u32[]{:S(2)}, u32[]{:S(2)}) %collective-permute-start.10) | collective-permute-done | bytes 786464 | tf_op jit(solution)/shard_map/ppermute | solution.py:318
  243.5 13.4 %collective-permute-done.28.refs_7_.refs_2_ = bf16[512,2048]{1,0:T(8,128)(2,1)S(1)} collective-permute-done((bf16[512,2048]{1,0:T(8,128)(2,1)S(1)}, bf16[512,2048]{1,0:T(8,128)(2,1)S(1)}, u32[]{:S(2)}, u32[]{:S(2)}) %collective-permute-start.28) | collective-permute-done | bytes 2097184 | tf_op jit(solution)/shard_map/ppermute | solution.py:318
  267.3 11.7 %close_attention.1 = (f32[512,2048]{1,0:T(8,128)}, bf16[512,2048]{1,0:T(8,128)(2,1)}) custom-call(bf16[512,2048]{1,0:T(8,128)(2,1)} %pad_maximum_fusion.3.x, bf16[512,512]{1,0:T(8,128)(2,1)} %get-tuple-element.2434.refs_0_.refs_1_.refs_4_, bf16[512,512]{1,0:T(8,128)(2,1)} %get-tuple-element.2431.refs_1_.refs_2_.refs_3_, ...), custom_call_target="tpu_custom_call" | custom-call | flops 1 | bytes 1 | tf_op jit(solution)/shard_map/close_attention/pallas_call | solution.py:789
  287.0 42.7 %collective-permute-done.33.refs_2_ = bf16[512,2048]{1,0:T(8,128)(2,1)S(1)} collective-permute-done((bf16[512,2048]{1,0:T(8,128)(2,1)}, bf16[512,2048]{1,0:T(8,128)(2,1)S(1)}, u32[]{:S(2)}, u32[]{:S(2)}) %collective-permute-start.33) | collective-permute-done | bytes 2097184 | tf_op jit(solution)/shard_map/ppermute | solution.py:318
  334.3 19.4 %collective-permute-done.35.refs_4_ = bf16[256,2048]{1,0:T(8,128)(2,1)S(1)} collective-permute-done((bf16[256,2048]{1,0:T(8,128)(2,1)S(1)}, bf16[256,2048]{1,0:T(8,128)(2,1)S(1)}, u32[]{:S(2)}, u32[]{:S(2)}) %collective-permute-start.35) | collective-permute-done | bytes 1048608 | tf_op jit(solution)/shard_map/ppermute | solution.py:318
  358.6 29.9 %hidden_units.2 = (bf16[2048,768]{1,0:T(8,128)(2,1)}, bf16[2048,768]{1,0:T(8,128)(2,1)}, bf16[2048,768]{1,0:T(8,128)(2,1)}) custom-call(bf16[512,2048]{1,0:T(8,128)(2,1)} %get-tuple-element.2306.refs_0_, bf16[512,2048]{1,0:T(8,128)(2,1)} %copy-done.14, bf16[512,2048]{1,0:T(8,128)(2,1)} %copy-done.13, bf16[256,2048]{1,0:T(8,128)(2,1)} %copy-done.23, ...), custom_call_target="tpu_custom_call" | custom-call | flops 1 | bytes 1 | tf_op jit(solution)/shard_map/hidden_units/pallas_call | solution.py:656
  388.5 30.4 %hidden_units.3 = (bf16[2048,768]{1,0:T(8,128)(2,1)}, bf16[2048,768]{1,0:T(8,128)(2,1)}, bf16[2048,768]{1,0:T(8,128)(2,1)}) custom-call(bf16[512,2048]{1,0:T(8,128)(2,1)} %get-tuple-element.2306.refs_0_, bf16[512,2048]{1,0:T(8,128)(2,1)} %copy-done.14, bf16[512,2048]{1,0:T(8,128)(2,1)} %copy-done.13, bf16[256,2048]{1,0:T(8,128)(2,1)} %copy-done.23, ...), custom_call_target="tpu_custom_call" | custom-call | flops 1 | bytes 1 | tf_op jit(solution)/shard_map/hidden_units/pallas_call | solution.py:656
  418.9 12.6 %row_outer.12 = bf16[2048,768]{1,0:T(8,128)(2,1)} custom-call(bf16[512,2048]{1,0:T(8,128)(2,1)} %copy-done.6, bf16[512,2048]{1,0:T(8,128)(2,1)} %copy-done.16, bf16[512,2048]{1,0:T(8,128)(2,1)} %copy-done.15, bf16[256,2048]{1,0:T(8,128)(2,1)} %copy-done.25, bf16[256,2048]{1,0:T(8,128)(2,1)} %copy-done.24, ...), custom_call_target="tpu_custom_call" | custom-call | flops 6442450944 | bytes 11534336 | tf_op jit(solution)/shard_map/row_outer/pallas_call | solution.py:739
  431.9 18.9 %from_hidden.4 = (bf16[512,2048]{1,0:T(8,128)(2,1)}, bf16[512,2048]{1,0:T(8,128)(2,1)}) custom-call(bf16[2048,768]{1,0:T(8,128)(2,1)} %get-tuple-element.2317.refs_0_.refs_1_.refs_2_.refs_3_.refs_5_, bf16[2048,768]{1,0:T(8,128)(2,1)} %get-tuple-element.2317.refs_0_.refs_1_.refs_2_.refs_3_.refs_5_, ...), custom_call_target="tpu_custom_call" | custom-call | flops 1 | bytes 1 | tf_op jit(solution)/shard_map/from_hidden/pallas_call | solution.py:695
  453.9 13.2 %row_outer.13 = bf16[2048,768]{1,0:T(8,128)(2,1)} custom-call(bf16[512,2048]{1,0:T(8,128)(2,1)} %copy-done.6, bf16[512,2048]{1,0:T(8,128)(2,1)} %copy-done.16, bf16[512,2048]{1,0:T(8,128)(2,1)} %copy-done.15, bf16[256,2048]{1,0:T(8,128)(2,1)} %copy-done.25, bf16[256,2048]{1,0:T(8,128)(2,1)} %copy-done.24, ...), custom_call_target="tpu_custom_call" | custom-call | flops 6442450944 | bytes 11534336 | tf_op jit(solution)/shard_map/row_outer/pallas_call | solution.py:739
  467.1 18.8 %from_hidden.5 = (bf16[512,2048]{1,0:T(8,128)(2,1)}, bf16[512,2048]{1,0:T(8,128)(2,1)}) custom-call(bf16[2048,768]{1,0:T(8,128)(2,1)} %get-tuple-element.2317.refs_0_.refs_1_.refs_2_.refs_3_.refs_5_, bf16[2048,768]{1,0:T(8,128)(2,1)} %get-tuple-element.2317.refs_0_.refs_1_.refs_2_.refs_3_.refs_5_, ...), custom_call_target="tpu_custom_call" | custom-call | flops 1 | bytes 1 | tf_op jit(solution)/shard_map/from_hidden/pallas_call | solution.py:695
  485.9 19.4 %row_outer.14 = bf16[2048,1536]{1,0:T(8,128)(2,1)} custom-call(bf16[512,2048]{1,0:T(8,128)(2,1)} %get-tuple-element.2306.refs_0_, bf16[512,2048]{1,0:T(8,128)(2,1)} %copy-done.14, bf16[512,2048]{1,0:T(8,128)(2,1)} %copy-done.13, bf16[256,2048]{1,0:T(8,128)(2,1)} %copy-done.23, bf16[256,2048]{1,0:T(8,128)(2,1)} %copy-done.22, ...), custom_call_target="tpu_custom_call" | custom-call | flops 12884901888 | bytes 14680064 | tf_op jit(solution)/shard_map/row_outer/pallas_call | solution.py:739
  512.3 10.6 %from_hidden.6 = (bf16[512,2048]{1,0:T(8,128)(2,1)}, bf16[512,2048]{1,0:T(8,128)(2,1)}) custom-call(bf16[2048,768]{1,0:T(8,128)(2,1)} %get-tuple-element.2226.refs_5_.refs_0_.refs_1_.refs_2_.refs_3_, bf16[2048,768]{1,0:T(8,128)(2,1)} %get-tuple-element.2226.refs_5_.refs_0_.refs_1_.refs_2_.refs_3_, ...), custom_call_target="tpu_custom_call" | custom-call | flops 1 | bytes 1 | tf_op jit(solution)/shard_map/from_hidden/pallas_call | solution.py:695
  523.0 10.9 %from_hidden.7 = (bf16[512,2048]{1,0:T(8,128)(2,1)}, bf16[512,2048]{1,0:T(8,128)(2,1)}) custom-call(bf16[2048,768]{1,0:T(8,128)(2,1)} %get-tuple-element.2226.refs_5_.refs_0_.refs_1_.refs_2_.refs_3_, bf16[2048,768]{1,0:T(8,128)(2,1)} %get-tuple-element.2226.refs_5_.refs_0_.refs_1_.refs_2_.refs_3_, ...), custom_call_target="tpu_custom_call" | custom-call | flops 1 | bytes 1 | tf_op jit(solution)/shard_map/from_hidden/pallas_call | solution.py:695
  548.2 13.4 %attend_back.4 = (bf16[512,512]{1,0:T(8,128)(2,1)}, f32[512,512]{1,0:T(8,128)}, bf16[512,512]{1,0:T(8,128)(2,1)}, f32[1,128]{1,0:T(1,128)}) custom-call(s32[2]{0:T(128)} %pad_add_fusion.info, bf16[512,512]{1,0:T(8,128)(2,1)} %get-tuple-element.2273.query, bf16[512,512]{1,0:T(8,128)(2,1)} %copy-done.42, bf16[512,512]{1,0:T(8,128)(2,1)} %get-tuple-element.2275.own, ...), custom_call_target="tpu_custom_call" | custom-call | flops 1 | bytes 1 | tf_op jit(solution)/shard_map/attend_back/pallas_call | solution.py:616
  571.6 19.7 %row_outer.16 = bf16[2048,1536]{1,0:T(8,128)(2,1)} custom-call(bf16[512,2048]{1,0:T(8,128)(2,1)} %get-tuple-element.2306.refs_0_, bf16[512,2048]{1,0:T(8,128)(2,1)} %copy-done.14, bf16[512,2048]{1,0:T(8,128)(2,1)} %copy-done.13, bf16[256,2048]{1,0:T(8,128)(2,1)} %copy-done.23, bf16[256,2048]{1,0:T(8,128)(2,1)} %copy-done.22, ...), custom_call_target="tpu_custom_call" | custom-call | flops 12884901888 | bytes 14680064 | tf_op jit(solution)/shard_map/row_outer/pallas_call | solution.py:739
  600.6 13.2 %attend_back.5 = (bf16[512,512]{1,0:T(8,128)(2,1)}, f32[512,512]{1,0:T(8,128)}, bf16[512,512]{1,0:T(8,128)(2,1)}, f32[1,128]{1,0:T(1,128)}) custom-call(s32[2]{0:T(128)} %pad_add_fusion.info, bf16[512,512]{1,0:T(8,128)(2,1)} %get-tuple-element.2356.query, bf16[512,512]{1,0:T(8,128)(2,1)} %copy-done.41, bf16[512,512]{1,0:T(8,128)(2,1)} %get-tuple-element.2358.own, ...), custom_call_target="tpu_custom_call" | custom-call | flops 1 | bytes 1 | tf_op jit(solution)/shard_map/attend_back/pallas_call | solution.py:616
  613.8 13.5 %attend_back.6 = (bf16[512,512]{1,0:T(8,128)(2,1)}, f32[512,512]{1,0:T(8,128)}, bf16[512,512]{1,0:T(8,128)(2,1)}, f32[1,128]{1,0:T(1,128)}) custom-call(s32[2]{0:T(128)} %pad_add_fusion.info, bf16[512,512]{1,0:T(8,128)(2,1)} %get-tuple-element.2371.query, bf16[512,512]{1,0:T(8,128)(2,1)} %collective-permute-done.21.before, ...), custom_call_target="tpu_custom_call" | custom-call | flops 1 | bytes 1 | tf_op jit(solution)/shard_map/attend_back/pallas_call | solution.py:616
  645.0 13.3 %attend_back.7 = (bf16[512,512]{1,0:T(8,128)(2,1)}, f32[512,512]{1,0:T(8,128)}, bf16[512,512]{1,0:T(8,128)(2,1)}, f32[1,128]{1,0:T(1,128)}) custom-call(s32[2]{0:T(128)} %pad_add_fusion.info, bf16[512,512]{1,0:T(8,128)(2,1)} %get-tuple-element.2439.query, bf16[512,512]{1,0:T(8,128)(2,1)} %copy-done.39, bf16[512,512]{1,0:T(8,128)(2,1)} %get-tuple-element.2441.own, ...), custom_call_target="tpu_custom_call" | custom-call | flops 1 | bytes 1 | tf_op jit(solution)/shard_map/attend_back/pallas_call | solution.py:616
  677.5 14.2 %collective-permute-done.53 = bf16[1024,512]{1,0:T(8,128)(2,1)S(1)} collective-permute-done((bf16[1024,512]{1,0:T(8,128)(2,1)}, bf16[1024,512]{1,0:T(8,128)(2,1)S(1)}, u32[]{:S(2)}, u32[]{:S(2)}) %collective-permute-start.53) | collective-permute-done | bytes 1048608 | tf_op jit(solution)/shard_map/ppermute | solution.py:318
  705.0 10.1 %row_outer.19 = bf16[2048,2048]{1,0:T(8,128)(2,1)} custom-call(bf16[512,2048]{1,0:T(8,128)(2,1)} %pad_maximum_fusion.4.normed.refs_0_, bf16[512,512]{1,0:T(8,128)(2,1)} %get-tuple-element.2635.refs_1_, bf16[512,512]{1,0:T(8,128)(2,1)} %get-tuple-element.2638.refs_2_.refs_3_, bf16[512,512]{1,0:T(8,128)(2,1)} %get-tuple-element.2641.refs_3_.refs_5_, ...), custom_call_target="tpu_custom_call" | custom-call | flops 4294967296 | bytes 4194304 | tf_op jit(solution)/shard_map/row_outer/pallas_call | solution.py:739
  732.3 15.8 %back_to_rows.1 = f32[512,2048]{1,0:T(8,128)} custom-call(bf16[512,512]{1,0:T(8,128)(2,1)} %get-tuple-element.2694.refs_0_.refs_4_, bf16[512,512]{1,0:T(8,128)(2,1)} %get-tuple-element.2635.refs_1_, bf16[512,512]{1,0:T(8,128)(2,1)} %get-tuple-element.2691.refs_2_.refs_1_.refs_3_, bf16[512,512]{1,0:T(8,128)(2,1)} %get-tuple-element.2638.refs_2_.refs_3_, ...), custom_call_target="tpu_custom_call" | custom-call | flops 1 | bytes 1 | tf_op jit(solution)/shard_map/back_to_rows/pallas_call | solution.py:842
  798.5 22.8 %collective-permute-done.73 = bf16[512,256]{1,0:T(8,128)(2,1)S(1)} collective-permute-done((bf16[512,256]{1,0:T(8,128)(2,1)S(1)}, bf16[512,256]{1,0:T(8,128)(2,1)S(1)}, u32[]{:S(2)}, u32[]{:S(2)}) %collective-permute-start.73) | collective-permute-done | bytes 262176 | tf_op jit(solution)/shard_map/ppermute | solution.py:323
  827.5 11.2 %whole_columns.5 = f32[512,6144]{1,0:T(8,128)} custom-call(s32[1]{0:T(128)} %bitcast.21.me_ref, bf16[2048,768]{1,0:T(8,128)(2,1)} %copy-done.21, bf16[2048,768]{1,0:T(8,128)(2,1)} %collective-permute-done.66.other_ref), custom_call_target="tpu_custom_call" | custom-call | flops 1 | bytes 1 | tf_op jit(solution)/shard_map/whole_columns/pallas_call | solution.py:431
  843.1 17.3 %collective-permute-done.77 = bf16[1024,512]{1,0:T(8,128)(2,1)S(1)} collective-permute-done((bf16[1024,512]{1,0:T(8,128)(2,1)}, bf16[1024,512]{1,0:T(8,128)(2,1)S(1)}, u32[]{:S(2)}, u32[]{:S(2)}) %collective-permute-start.77) | collective-permute-done | bytes 1048608 | tf_op jit(solution)/shard_map/ppermute | solution.py:318
  885.0 11.0 %whole_columns.6 = f32[512,6144]{1,0:T(8,128)} custom-call(s32[1]{0:T(128)} %bitcast.21.me_ref, bf16[2048,1536]{1,0:T(8,128)(2,1)} %copy-done.9, bf16[2048,1536]{1,0:T(8,128)(2,1)} %copy-done.10), custom_call_target="tpu_custom_call" | custom-call | flops 1 | bytes 1 | tf_op jit(solution)/shard_map/whole_columns/pallas_call | solution.py:431
  902.9 11.0 %whole_columns.7 = f32[512,6144]{1,0:T(8,128)} custom-call(s32[1]{0:T(128)} %bitcast.21.me_ref, bf16[2048,1536]{1,0:T(8,128)(2,1)} %copy-done.9, bf16[2048,1536]{1,0:T(8,128)(2,1)} %copy-done.10), custom_call_target="tpu_custom_call" | custom-call | flops 1 | bytes 1 | tf_op jit(solution)/shard_map/whole_columns/pallas_call | solution.py:431
  (648 shorter events, 414.9 us)
Async XLA Ops:
  7.2 140.7 %all-gather.3.cloned.1.call-start = ((), (), s32[]{:S(2)}) async-start(), calls=%async_computation.2 | async-start | bytes 1310720 | tf_op jit(solution)/shard_map/all_gather | solution.py:904
  61.1 40.0 %collective-permute-start.6 = (bf16[1536,512]{1,0:T(8,128)(2,1)S(1)}, bf16[1536,512]{1,0:T(8,128)(2,1)}, u32[]{:S(2)}, u32[]{:S(2)}) collective-permute-start(bf16[1536,512]{1,0:T(8,128)(2,1)S(1)} %pad_maximum_fusion.8.came0.refs_9_), channel_id=1, source_target_pairs={{0,4},{4,0},{8,12},{12,8},{16,20},{20,16},{24,28},{28,24},{1,5},{5... | collective-permute-start | bytes 4718600 | tf_op jit(solution)/shard_map/ppermute | solution.py:318
  61.2 39.9 %collective-permute-start.5 = (bf16[1536,512]{1,0:T(8,128)(2,1)S(1)}, bf16[1536,512]{1,0:T(8,128)(2,1)}, u32[]{:S(2)}, u32[]{:S(2)}) collective-permute-start(bf16[1536,512]{1,0:T(8,128)(2,1)S(1)} %pad_maximum_fusion.8.came0.refs_9_), channel_id=1, source_target_pairs={{0,16},{4,20},{8,24},{12,28},{16,0},{20,4},{24,8},{28,12},{1,17},{... | collective-permute-start | bytes 4718600 | tf_op jit(solution)/shard_map/ppermute | solution.py:318
  62.7 38.3 %collective-permute-start.4 = (bf16[1536,512]{1,0:T(8,128)(2,1)S(1)}, bf16[1536,512]{1,0:T(8,128)(2,1)}, u32[]{:S(2)}, u32[]{:S(2)}) collective-permute-start(bf16[1536,512]{1,0:T(8,128)(2,1)S(1)} %pad_maximum_fusion.8.came0.refs_9_), channel_id=1, source_target_pairs={{0,8},{4,12},{8,0},{12,4},{16,24},{20,28},{24,16},{28,20},{1,9},{5... | collective-permute-start | bytes 4718600 | tf_op jit(solution)/shard_map/ppermute | solution.py:318
  67.9 33.2 %collective-permute-start.8 = (bf16[256,2048]{1,0:T(8,128)(2,1)}, bf16[256,2048]{1,0:T(8,128)(2,1)S(1)}, u32[]{:S(2)}, u32[]{:S(2)}) collective-permute-start(bf16[256,2048]{1,0:T(8,128)(2,1)} %get-tuple-element.2933), channel_id=1, source_target_pairs={{0,1},{1,0},{2,5},{3,4},{4,3},{5,2},{6,7},{7,6},{8,9},{9,8},{10,13... | collective-permute-start | bytes 3145736 | tf_op jit(solution)/shard_map/ppermute | solution.py:388
  67.9 33.1 %collective-permute-start.7 = (bf16[256,2048]{1,0:T(8,128)(2,1)}, bf16[256,2048]{1,0:T(8,128)(2,1)}, u32[]{:S(2)}, u32[]{:S(2)}) collective-permute-start(bf16[256,2048]{1,0:T(8,128)(2,1)} %get-tuple-element.2934), channel_id=1, source_target_pairs={{0,0},{1,1},{2,4},{3,5},{4,2},{5,3},{6,6},{7,7},{8,8},{9,9},{10,12... | collective-permute-start | bytes 3145736 | tf_op jit(solution)/shard_map/ppermute | solution.py:388
  80.3 278.2 %all-gather.5.cloned.1.call-start = ((), (), s32[]{:S(2)}) async-start(), calls=%async_computation.3 | async-start | bytes 11796480 | tf_op jit(solution)/shard_map/all_gather | solution.py:998
  103.1 55.7 %collective-permute-start.11 = (bf16[1536,512]{1,0:T(8,128)(2,1)}, bf16[1536,512]{1,0:T(8,128)(2,1)}, u32[]{:S(2)}, u32[]{:S(2)}) collective-permute-start(bf16[1536,512]{1,0:T(8,128)(2,1)} %collective-permute-done.4.came0.refs_13_), channel_id=1, source_target_pairs={{0,4},{4,0},{8,12},{12,8},{16,20},{20,16},{24,28},{28,24},{1,5},{5... | collective-permute-start | bytes 4718600 | tf_op jit(solution)/shard_map/ppermute | solution.py:318
  192.4 398.9 %reduce-scatter.3.cloned.1.call-start = ((), (), s32[]{:S(2)}) async-start(), calls=%async_computation.4 | async-start | bytes 3932160 | tf_op jit(solution)/shard_map/reduce_scatter | solution.py:1114
  210.0 46.9 %collective-permute-start.28 = (bf16[512,2048]{1,0:T(8,128)(2,1)S(1)}, bf16[512,2048]{1,0:T(8,128)(2,1)S(1)}, u32[]{:S(2)}, u32[]{:S(2)}) collective-permute-start(bf16[512,2048]{1,0:T(8,128)(2,1)S(1)} %maximum_select_fusion.refs_5_.refs_0_), channel_id=1, source_target_pairs={{0,16},{4,20},{8,24},{12,28},{16,0},{20,4},{24,8},{28,12},{1,17},{... | collective-permute-start | bytes 6291464 | tf_op jit(solution)/shard_map/ppermute | solution.py:318
  211.6 46.6 %collective-permute-start.27 = (bf16[512,2048]{1,0:T(8,128)(2,1)S(1)}, bf16[512,2048]{1,0:T(8,128)(2,1)S(1)}, u32[]{:S(2)}, u32[]{:S(2)}) collective-permute-start(bf16[512,2048]{1,0:T(8,128)(2,1)S(1)} %maximum_select_fusion.refs_5_.refs_0_), channel_id=1, source_target_pairs={{0,8},{4,12},{8,0},{12,4},{16,24},{20,28},{24,16},{28,20},{1,9},{5... | collective-permute-start | bytes 6291464 | tf_op jit(solution)/shard_map/ppermute | solution.py:318
  284.9 44.9 %collective-permute-start.33 = (bf16[512,2048]{1,0:T(8,128)(2,1)}, bf16[512,2048]{1,0:T(8,128)(2,1)S(1)}, u32[]{:S(2)}, u32[]{:S(2)}) collective-permute-start(bf16[512,2048]{1,0:T(8,128)(2,1)} %get-tuple-element.2306.refs_0_), channel_id=1, source_target_pairs={{0,16},{4,20},{8,24},{12,28},{16,0},{20,4},{24,8},{28,12},{1,17},{... | collective-permute-start | bytes 6291464 | tf_op jit(solution)/shard_map/ppermute | solution.py:318
  286.1 44.9 %collective-permute-start.32 = (bf16[512,2048]{1,0:T(8,128)(2,1)}, bf16[512,2048]{1,0:T(8,128)(2,1)S(1)}, u32[]{:S(2)}, u32[]{:S(2)}) collective-permute-start(bf16[512,2048]{1,0:T(8,128)(2,1)} %get-tuple-element.2306.refs_0_), channel_id=1, source_target_pairs={{0,8},{4,12},{8,0},{12,4},{16,24},{20,28},{24,16},{28,20},{1,9},{5... | collective-permute-start | bytes 6291464 | tf_op jit(solution)/shard_map/ppermute | solution.py:318
  358.5 30.0 %collective-permute-start.36 = (bf16[2048,2304]{1,0:T(8,128)(2,1)}, bf16[2048,2304]{1,0:T(8,128)(2,1)}, u32[]{:S(2)}, u32[]{:S(2)}) collective-permute-start(bf16[2048,2304]{1,0:T(8,128)(2,1)} %all-gather.5.cloned.1.call-done.refs_10_.refs_11_.refs_12_.refs_4_.refs_9_), channel_id=1, source_target_pairs={{0,4},{4,0},{8,12},{12,8},{16,20},{20,16},{24,28},{28,24},{1,5},{5... | collective-permute-start | bytes 28311560 | tf_op jit(solution)/shard_map/ppermute | solution.py:318
  450.9 54.5 %collective-permute-start.38 = (bf16[512,2048]{1,0:T(8,128)(2,1)}, bf16[512,2048]{1,0:T(8,128)(2,1)}, u32[]{:S(2)}, u32[]{:S(2)}) collective-permute-start(bf16[512,2048]{1,0:T(8,128)(2,1)} %get-tuple-element.2137), channel_id=1, source_target_pairs={{0,8},{4,12},{8,0},{12,4},{16,24},{20,28},{24,16},{28,20},{1,9},{5... | collective-permute-start | bytes 6291464 | tf_op jit(solution)/shard_map/ppermute | solution.py:318
  452.4 52.9 %collective-permute-start.39 = (bf16[512,2048]{1,0:T(8,128)(2,1)}, bf16[512,2048]{1,0:T(8,128)(2,1)}, u32[]{:S(2)}, u32[]{:S(2)}) collective-permute-start(bf16[512,2048]{1,0:T(8,128)(2,1)} %get-tuple-element.2138), channel_id=1, source_target_pairs={{0,16},{4,20},{8,24},{12,28},{16,0},{20,4},{24,8},{28,12},{1,17},{... | collective-permute-start | bytes 6291464 | tf_op jit(solution)/shard_map/ppermute | solution.py:318
  505.3 30.6 %collective-permute-start.40 = (bf16[2048,1536]{1,0:T(8,128)(2,1)}, bf16[2048,1536]{1,0:T(8,128)(2,1)}, u32[]{:S(2)}, u32[]{:S(2)}) collective-permute-start(bf16[2048,1536]{1,0:T(8,128)(2,1)} %row_outer.14), channel_id=1, source_target_pairs={{0,4},{4,0},{8,12},{12,8},{16,20},{20,16},{24,28},{28,24},{1,5},{5... | collective-permute-start | bytes 18874376 | tf_op jit(solution)/shard_map/ppermute | solution.py:318
  505.4 214.7 %reduce-scatter.5.cloned.1.call-start = ((), (), s32[]{:S(2)}) async-start(), calls=%async_computation.5 | async-start | bytes 7864320 | tf_op jit(solution)/shard_map/reduce_scatter | solution.py:1182
  535.9 55.4 %collective-permute-start.43 = (bf16[512,2048]{1,0:T(8,128)(2,1)}, bf16[512,2048]{1,0:T(8,128)(2,1)}, u32[]{:S(2)}, u32[]{:S(2)}) collective-permute-start(bf16[512,2048]{1,0:T(8,128)(2,1)} %get-tuple-element.2321), channel_id=1, source_target_pairs={{0,8},{4,12},{8,0},{12,4},{16,24},{20,28},{24,16},{28,20},{1,9},{5... | collective-permute-start | bytes 6291464 | tf_op jit(solution)/shard_map/ppermute | solution.py:318
  537.5 53.8 %collective-permute-start.44 = (bf16[512,2048]{1,0:T(8,128)(2,1)}, bf16[512,2048]{1,0:T(8,128)(2,1)}, u32[]{:S(2)}, u32[]{:S(2)}) collective-permute-start(bf16[512,2048]{1,0:T(8,128)(2,1)} %get-tuple-element.2322), channel_id=1, source_target_pairs={{0,16},{4,20},{8,24},{12,28},{16,0},{20,4},{24,8},{28,12},{1,17},{... | collective-permute-start | bytes 6291464 | tf_op jit(solution)/shard_map/ppermute | solution.py:318
  591.3 36.0 %collective-permute-start.47 = (bf16[2048,1024]{1,0:T(8,128)(2,1)}, bf16[2048,1024]{1,0:T(8,128)(2,1)S(1)}, u32[]{:S(2)}, u32[]{:S(2)}) collective-permute-start(bf16[2048,1024]{1,0:T(8,128)(2,1)} %row_outer.15), channel_id=1, source_target_pairs={{0,4},{4,0},{8,12},{12,8},{16,20},{20,16},{24,28},{28,24},{1,5},{5... | collective-permute-start | bytes 12582920 | tf_op jit(solution)/shard_map/ppermute | solution.py:318
  596.3 31.0 %collective-permute-start.46 = (bf16[256,2048]{1,0:T(8,128)(2,1)}, bf16[256,2048]{1,0:T(8,128)(2,1)S(1)}, u32[]{:S(2)}, u32[]{:S(2)}) collective-permute-start(bf16[256,2048]{1,0:T(8,128)(2,1)} %get-tuple-element.2913), channel_id=1, source_target_pairs={{0,16},{4,20},{8,24},{12,28},{16,0},{20,4},{24,8},{28,12},{1,17},{... | collective-permute-start | bytes 3145736 | tf_op jit(solution)/shard_map/ppermute | solution.py:318
  629.5 32.7 %collective-permute-start.50 = (bf16[512,768]{1,0:T(8,128)(2,1)}, bf16[512,768]{1,0:T(8,128)(2,1)S(1)}, u32[]{:S(2)}, u32[]{:S(2)}) collective-permute-start(bf16[512,768]{1,0:T(8,128)(2,1)} %reduce-scatter.3.cloned.1.call-done), channel_id=1, source_target_pairs={{0,16},{4,20},{8,24},{12,28},{16,0},{20,4},{24,8},{28,12},{1,17},{... | collective-permute-start | bytes 2359304 | tf_op jit(solution)/shard_map/ppermute | solution.py:318
  630.9 31.4 %collective-permute-start.49 = (bf16[512,768]{1,0:T(8,128)(2,1)}, bf16[512,768]{1,0:T(8,128)(2,1)S(1)}, u32[]{:S(2)}, u32[]{:S(2)}) collective-permute-start(bf16[512,768]{1,0:T(8,128)(2,1)} %reduce-scatter.3.cloned.1.call-done), channel_id=1, source_target_pairs={{0,8},{4,12},{8,0},{12,4},{16,24},{20,28},{24,16},{28,20},{1,9},{5... | collective-permute-start | bytes 2359304 | tf_op jit(solution)/shard_map/ppermute | solution.py:318
  631.5 30.7 %collective-permute-start.51 = (bf16[512,512]{1,0:T(8,128)(2,1)}, bf16[512,512]{1,0:T(8,128)(2,1)}, u32[]{:S(2)}, u32[]{:S(2)}) collective-permute-start(bf16[512,512]{1,0:T(8,128)(2,1)} %get-tuple-element.2455), channel_id=1, source_target_pairs={{4,0},{12,8},{20,16},{28,24},{5,1},{13,9},{21,17},{29,25},{6,2},{1... | collective-permute-start | bytes 1572872 | tf_op jit(solution)/shard_map/ppermute | solution.py:1142
  720.1 40.5 %collective-permute-start.65 = (bf16[2048,2048]{1,0:T(8,128)(2,1)}, bf16[2048,2048]{1,0:T(8,128)(2,1)}, u32[]{:S(2)}, u32[]{:S(2)}) collective-permute-start(bf16[2048,2048]{1,0:T(8,128)(2,1)} %row_outer.19), channel_id=1, source_target_pairs={{0,4},{4,0},{8,12},{12,8},{16,20},{20,16},{24,28},{28,24},{1,5},{5... | collective-permute-start | bytes 25165832 | tf_op jit(solution)/shard_map/ppermute | solution.py:318
  723.1 36.6 %collective-permute-start.62 = (bf16[512,1536]{1,0:T(8,128)(2,1)}, bf16[512,1536]{1,0:T(8,128)(2,1)S(1)}, u32[]{:S(2)}, u32[]{:S(2)}) collective-permute-start(bf16[512,1536]{1,0:T(8,128)(2,1)} %reduce-scatter.5.cloned.1.call-done), channel_id=1, source_target_pairs={{0,16},{4,20},{8,24},{12,28},{16,0},{20,4},{24,8},{28,12},{1,17},{... | collective-permute-start | bytes 4718600 | tf_op jit(solution)/shard_map/ppermute | solution.py:318
  724.0 36.6 %collective-permute-start.61 = (bf16[512,1536]{1,0:T(8,128)(2,1)}, bf16[512,1536]{1,0:T(8,128)(2,1)S(1)}, u32[]{:S(2)}, u32[]{:S(2)}) collective-permute-start(bf16[512,1536]{1,0:T(8,128)(2,1)} %reduce-scatter.5.cloned.1.call-done), channel_id=1, source_target_pairs={{0,8},{4,12},{8,0},{12,4},{16,24},{20,28},{24,16},{28,20},{1,9},{5... | collective-permute-start | bytes 4718600 | tf_op jit(solution)/shard_map/ppermute | solution.py:318
  791.2 30.2 %collective-permute-start.71 = (bf16[1024,512]{1,0:T(8,128)(2,1)S(1)}, bf16[1024,512]{1,0:T(8,128)(2,1)S(1)}, u32[]{:S(2)}, u32[]{:S(2)}) collective-permute-start(bf16[1024,512]{1,0:T(8,128)(2,1)S(1)} %copy-done.128), channel_id=1, source_target_pairs={{0,8},{4,12},{8,0},{12,4},{16,24},{20,28},{24,16},{28,20},{1,9},{5... | collective-permute-start | bytes 3145736 | tf_op jit(solution)/shard_map/ppermute | solution.py:318
  797.7 45.4 %collective-permute-start.79 = (bf16[256,2048]{1,0:T(8,128)(2,1)}, bf16[256,2048]{1,0:T(8,128)(2,1)S(1)}, u32[]{:S(2)}, u32[]{:S(2)}) collective-permute-start(bf16[256,2048]{1,0:T(8,128)(2,1)} %get-tuple-element.2907), channel_id=1, source_target_pairs={{1,0},{0,1},{5,2},{4,3},{3,4},{2,5},{7,6},{6,7},{9,8},{8,9},{13,10... | collective-permute-start | bytes 3145736 | tf_op jit(solution)/shard_map/ppermute | solution.py:395
  824.4 36.0 %collective-permute-start.77 = (bf16[1024,512]{1,0:T(8,128)(2,1)}, bf16[1024,512]{1,0:T(8,128)(2,1)S(1)}, u32[]{:S(2)}, u32[]{:S(2)}) collective-permute-start(bf16[1024,512]{1,0:T(8,128)(2,1)} %get-tuple-element.2758), channel_id=1, source_target_pairs={{0,8},{4,12},{8,0},{12,4},{16,24},{20,28},{24,16},{28,20},{1,9},{5... | collective-permute-start | bytes 3145736 | tf_op jit(solution)/shard_map/ppermute | solution.py:318
  826.2 34.2 %collective-permute-start.78 = (bf16[1024,512]{1,0:T(8,128)(2,1)}, bf16[1024,512]{1,0:T(8,128)(2,1)S(1)}, u32[]{:S(2)}, u32[]{:S(2)}) collective-permute-start(bf16[1024,512]{1,0:T(8,128)(2,1)} %get-tuple-element.2761), channel_id=1, source_target_pairs={{0,16},{4,20},{8,24},{12,28},{16,0},{20,4},{24,8},{28,12},{1,17},{... | collective-permute-start | bytes 3145736 | tf_op jit(solution)/shard_map/ppermute | solution.py:318
  (206 other events, 2372.2 us)
Sparse Core Ops, SparseCore 0:
  80.4 44.4 all-gather.2
  192.5 166.0 all-gather.4
  505.6 57.2 reduce-scatter.2
  591.5 107.9 reduce-scatter.4

commit v18 on v17

--- a/solution.py
+++ b/solution.py
@@ -417,24 +417,27 @@
     rows, columns = own.shape[0] // 4, sum(widths)
 
     def body(me_ref, own_ref, other_ref, *outs):
-        def put(block):
+        def put(blocks):
             start = 0
             for out, width in zip(outs, widths):
-                out[...] = block[:, start : start + width].astype(jnp.float32)
+                for at, block in enumerate(blocks):
+                    out[:, at * width : (at + 1) * width] = block[
+                        :, start : start + width
+                    ].astype(jnp.float32)
                 start += width
 
-        mine = (me_ref[0] ^ pl.program_id(0)) & 1 == 0
-        pl.when(mine)(lambda: put(own_ref))
-        pl.when(jnp.logical_not(mine))(lambda: put(other_ref))
-
-    spec = pl.BlockSpec((rows, columns), lambda i, at: ((at[0] ^ i) >> 1, part))
+        even = me_ref[0] & 1 == 0
+        pl.when(even)(lambda: put((own_ref, other_ref)))
+        pl.when(jnp.logical_not(even))(lambda: put((other_ref, own_ref)))
+
+    spec = pl.BlockSpec((rows, columns), lambda i, at: ((at[0] >> 1) ^ i, part))
     return pl.pallas_call(
         body,
         grid_spec=pltpu.PrefetchScalarGridSpec(
             num_scalar_prefetch=1,
-            grid=(8,),
+            grid=(4,),
             in_specs=[spec, spec],
-            out_specs=[pl.BlockSpec((rows, w), lambda i, at: (0, i)) for w in widths],
+            out_specs=[pl.BlockSpec((rows, 2 * w), lambda i, at: (0, i)) for w in widths],
         ),
         out_shape=[jax.ShapeDtypeStruct((rows, 8 * w), jnp.float32) for w in widths],
         compiler_params=pltpu.CompilerParams(vmem_limit_bytes=VMEM_BYTES),

time: 975 us -> 968 us (level)
  Pallas kernels: 428 us -> 413 us
    pallas_call x5, Pallas kernels: 48.6 us -> 33.8 us  [whole_columns(): pl.pallas_call(body, grid_spec=pltpu.PrefetchScalarGridSpec(num_scalar_pr...]
  transfers between devices with their start and end apart: 107 -> 107, of which waited for: 36 -> 39; matrix products, arithmetic and copies ran while one was open for 10% -> 10% of each run, Pallas kernels for 39% -> 38%
where the time goes in v18:
time: 968 us; the launch traced here: 959 us
  Pallas kernels  413 us (43%)
  waiting for transfers between devices  258 us (27%)
  starting transfers between devices  142 us (15%)
  local copies, waits for them, and re-layouts  64.8 us (7%)
  other arithmetic  64.7 us (7%)
  between operations  16.2 us (2%)
    ppermute x73, waiting for transfers between devices, across(): return lax.ppermute(x, 'rep', [(i, i ^ mask) for i in range(count)])  158 us
    pallas_call x16, Pallas kernels, call(): pl.pallas_call(body, grid=(1,), out_shape=outs, in_specs=in_specs, out_sp...  119 us
    pallas_call x12, Pallas kernels, row_outer(): pl.pallas_call(body, grid=(tiles,), out_shape=[jax.ShapeDtypeStruct((tile...  114 us
    ppermute x73, starting transfers between devices, across(): return lax.ppermute(x, 'rep', [(i, i ^ mask) for i in range(count)])  96.3 us
    ppermute x12, waiting for transfers between devices, around(): lax.ppermute(x, 'shard', [(i, (i + by) % count) for i in range(count)])  65.7 us
    pallas_call x2, Pallas kernels, hidden_units(): pl.pallas_call(body, grid=(3,), out_shape=[jax.ShapeDtypeStruct((rows, un...  60.3 us
    pallas_call x4, Pallas kernels, from_hidden(): pl.pallas_call(body, grid=(4,), out_shape=[jax.ShapeDtypeStruct((2 * rows...  59.2 us
    pallas_call x5, Pallas kernels, whole_columns(): pl.pallas_call(body, grid_spec=pltpu.PrefetchScalarGridSpec(num_scalar_pr...  33.8 us
  transfers between devices with their start and end apart: 107, of which 39 were waited for; matrix products, arithmetic and copies ran while one was open for 10% of the time, Pallas kernels for 38%

profile of v18, /device:TPU:0, one launch (start us, length us, event | category | flops | bytes accessed | tf_op | source)
XLA Modules:
  0.0 958.9 jit_solution(4840336116333476287)
XLA Ops:
  32.0 11.3 %collective-permute-done = bf16[528,512]{1,0:T(8,128)(2,1)} collective-permute-done((bf16[528,512]{1,0:T(8,128)(2,1)}, bf16[528,512]{1,0:T(8,128)(2,1)}, u32[]{:S(2)}, u32[]{:S(2)}) %collective-permute-start) | collective-permute-done | bytes 540704 | tf_op jit(solution)/shard_map/ppermute | solution.py:323
  45.0 13.5 %collective-permute-done.3 = bf16[528,512]{1,0:T(8,128)(2,1)S(1)} collective-permute-done((bf16[528,512]{1,0:T(8,128)(2,1)}, bf16[528,512]{1,0:T(8,128)(2,1)S(1)}, u32[]{:S(2)}, u32[]{:S(2)}) %collective-permute-start.3) | collective-permute-done | bytes 540704 | tf_op jit(solution)/shard_map/ppermute | solution.py:323
  67.9 9.5 collective-permute-start.7
  81.9 19.1 %collective-permute-done.8 = bf16[256,2048]{1,0:T(8,128)(2,1)S(1)} collective-permute-done((bf16[256,2048]{1,0:T(8,128)(2,1)}, bf16[256,2048]{1,0:T(8,128)(2,1)S(1)}, u32[]{:S(2)}, u32[]{:S(2)}) %collective-permute-start.8) | collective-permute-done | bytes 1048608 | tf_op jit(solution)/shard_map/ppermute | solution.py:388
  103.1 31.1 %collective-permute-start.11 = (bf16[1536,512]{1,0:T(8,128)(2,1)}, bf16[1536,512]{1,0:T(8,128)(2,1)}, u32[]{:S(2)}, u32[]{:S(2)}) collective-permute-start(bf16[1536,512]{1,0:T(8,128)(2,1)} %collective-permute-done.4.came0.refs_13_), channel_id=1, source_target_pairs={{0,4},{4,0},{8,12},{12,8},{16,20},{20,16},{24,28},{28,24},{1,5},{5... | collective-permute-start | bytes 4718600 | tf_op jit(solution)/shard_map/ppermute | solution.py:318
  147.9 10.6 %collective-permute-done.10 = bf16[768,512]{1,0:T(8,128)(2,1)} collective-permute-done((bf16[768,512]{1,0:T(8,128)(2,1)}, bf16[768,512]{1,0:T(8,128)(2,1)}, u32[]{:S(2)}, u32[]{:S(2)}) %collective-permute-start.10) | collective-permute-done | bytes 786464 | tf_op jit(solution)/shard_map/ppermute | solution.py:318
  199.9 8.3 collective-permute-done.23
  243.5 13.4 %collective-permute-done.28.refs_7_.refs_2_ = bf16[512,2048]{1,0:T(8,128)(2,1)S(1)} collective-permute-done((bf16[512,2048]{1,0:T(8,128)(2,1)S(1)}, bf16[512,2048]{1,0:T(8,128)(2,1)S(1)}, u32[]{:S(2)}, u32[]{:S(2)}) %collective-permute-start.28) | collective-permute-done | bytes 2097184 | tf_op jit(solution)/shard_map/ppermute | solution.py:318
  267.3 11.7 %close_attention.1 = (f32[512,2048]{1,0:T(8,128)}, bf16[512,2048]{1,0:T(8,128)(2,1)}) custom-call(bf16[512,2048]{1,0:T(8,128)(2,1)} %pad_maximum_fusion.3.x, bf16[512,512]{1,0:T(8,128)(2,1)} %get-tuple-element.2434.refs_0_.refs_1_.refs_4_, bf16[512,512]{1,0:T(8,128)(2,1)} %get-tuple-element.2431.refs_1_.refs_2_.refs_3_, ...), custom_call_target="tpu_custom_call" | custom-call | flops 1 | bytes 1 | tf_op jit(solution)/shard_map/close_attention/pallas_call | solution.py:792
  287.0 42.7 %collective-permute-done.33.refs_2_ = bf16[512,2048]{1,0:T(8,128)(2,1)S(1)} collective-permute-done((bf16[512,2048]{1,0:T(8,128)(2,1)}, bf16[512,2048]{1,0:T(8,128)(2,1)S(1)}, u32[]{:S(2)}, u32[]{:S(2)}) %collective-permute-start.33) | collective-permute-done | bytes 2097184 | tf_op jit(solution)/shard_map/ppermute | solution.py:318
  334.3 19.4 %collective-permute-done.35.refs_4_ = bf16[256,2048]{1,0:T(8,128)(2,1)S(1)} collective-permute-done((bf16[256,2048]{1,0:T(8,128)(2,1)S(1)}, bf16[256,2048]{1,0:T(8,128)(2,1)S(1)}, u32[]{:S(2)}, u32[]{:S(2)}) %collective-permute-start.35) | collective-permute-done | bytes 1048608 | tf_op jit(solution)/shard_map/ppermute | solution.py:318
  358.6 29.9 %hidden_units.2 = (bf16[2048,768]{1,0:T(8,128)(2,1)}, bf16[2048,768]{1,0:T(8,128)(2,1)}, bf16[2048,768]{1,0:T(8,128)(2,1)}) custom-call(bf16[512,2048]{1,0:T(8,128)(2,1)} %get-tuple-element.2306.refs_0_, bf16[512,2048]{1,0:T(8,128)(2,1)} %copy-done.14, bf16[512,2048]{1,0:T(8,128)(2,1)} %copy-done.13, bf16[256,2048]{1,0:T(8,128)(2,1)} %copy-done.23, ...), custom_call_target="tpu_custom_call" | custom-call | flops 1 | bytes 1 | tf_op jit(solution)/shard_map/hidden_units/pallas_call | solution.py:659
  388.5 30.4 %hidden_units.3 = (bf16[2048,768]{1,0:T(8,128)(2,1)}, bf16[2048,768]{1,0:T(8,128)(2,1)}, bf16[2048,768]{1,0:T(8,128)(2,1)}) custom-call(bf16[512,2048]{1,0:T(8,128)(2,1)} %get-tuple-element.2306.refs_0_, bf16[512,2048]{1,0:T(8,128)(2,1)} %copy-done.14, bf16[512,2048]{1,0:T(8,128)(2,1)} %copy-done.13, bf16[256,2048]{1,0:T(8,128)(2,1)} %copy-done.23, ...), custom_call_target="tpu_custom_call" | custom-call | flops 1 | bytes 1 | tf_op jit(solution)/shard_map/hidden_units/pallas_call | solution.py:659
  418.9 12.6 %row_outer.12 = bf16[2048,768]{1,0:T(8,128)(2,1)} custom-call(bf16[512,2048]{1,0:T(8,128)(2,1)} %copy-done.6, bf16[512,2048]{1,0:T(8,128)(2,1)} %copy-done.16, bf16[512,2048]{1,0:T(8,128)(2,1)} %copy-done.15, bf16[256,2048]{1,0:T(8,128)(2,1)} %copy-done.25, bf16[256,2048]{1,0:T(8,128)(2,1)} %copy-done.24, ...), custom_call_target="tpu_custom_call" | custom-call | flops 6442450944 | bytes 11534336 | tf_op jit(solution)/shard_map/row_outer/pallas_call | solution.py:742
  431.9 18.9 %from_hidden.4 = (bf16[512,2048]{1,0:T(8,128)(2,1)}, bf16[512,2048]{1,0:T(8,128)(2,1)}) custom-call(bf16[2048,768]{1,0:T(8,128)(2,1)} %get-tuple-element.2317.refs_0_.refs_1_.refs_2_.refs_3_.refs_5_, bf16[2048,768]{1,0:T(8,128)(2,1)} %get-tuple-element.2317.refs_0_.refs_1_.refs_2_.refs_3_.refs_5_, ...), custom_call_target="tpu_custom_call" | custom-call | flops 1 | bytes 1 | tf_op jit(solution)/shard_map/from_hidden/pallas_call | solution.py:698
  453.9 13.2 %row_outer.13 = bf16[2048,768]{1,0:T(8,128)(2,1)} custom-call(bf16[512,2048]{1,0:T(8,128)(2,1)} %copy-done.6, bf16[512,2048]{1,0:T(8,128)(2,1)} %copy-done.16, bf16[512,2048]{1,0:T(8,128)(2,1)} %copy-done.15, bf16[256,2048]{1,0:T(8,128)(2,1)} %copy-done.25, bf16[256,2048]{1,0:T(8,128)(2,1)} %copy-done.24, ...), custom_call_target="tpu_custom_call" | custom-call | flops 6442450944 | bytes 11534336 | tf_op jit(solution)/shard_map/row_outer/pallas_call | solution.py:742
  467.1 18.8 %from_hidden.5 = (bf16[512,2048]{1,0:T(8,128)(2,1)}, bf16[512,2048]{1,0:T(8,128)(2,1)}) custom-call(bf16[2048,768]{1,0:T(8,128)(2,1)} %get-tuple-element.2317.refs_0_.refs_1_.refs_2_.refs_3_.refs_5_, bf16[2048,768]{1,0:T(8,128)(2,1)} %get-tuple-element.2317.refs_0_.refs_1_.refs_2_.refs_3_.refs_5_, ...), custom_call_target="tpu_custom_call" | custom-call | flops 1 | bytes 1 | tf_op jit(solution)/shard_map/from_hidden/pallas_call | solution.py:698
  485.9 19.4 %row_outer.14 = bf16[2048,1536]{1,0:T(8,128)(2,1)} custom-call(bf16[512,2048]{1,0:T(8,128)(2,1)} %get-tuple-element.2306.refs_0_, bf16[512,2048]{1,0:T(8,128)(2,1)} %copy-done.14, bf16[512,2048]{1,0:T(8,128)(2,1)} %copy-done.13, bf16[256,2048]{1,0:T(8,128)(2,1)} %copy-done.23, bf16[256,2048]{1,0:T(8,128)(2,1)} %copy-done.22, ...), custom_call_target="tpu_custom_call" | custom-call | flops 12884901888 | bytes 14680064 | tf_op jit(solution)/shard_map/row_outer/pallas_call | solution.py:742
  512.3 10.6 %from_hidden.6 = (bf16[512,2048]{1,0:T(8,128)(2,1)}, bf16[512,2048]{1,0:T(8,128)(2,1)}) custom-call(bf16[2048,768]{1,0:T(8,128)(2,1)} %get-tuple-element.2226.refs_5_.refs_0_.refs_1_.refs_2_.refs_3_, bf16[2048,768]{1,0:T(8,128)(2,1)} %get-tuple-element.2226.refs_5_.refs_0_.refs_1_.refs_2_.refs_3_, ...), custom_call_target="tpu_custom_call" | custom-call | flops 1 | bytes 1 | tf_op jit(solution)/shard_map/from_hidden/pallas_call | solution.py:698
  523.0 10.9 %from_hidden.7 = (bf16[512,2048]{1,0:T(8,128)(2,1)}, bf16[512,2048]{1,0:T(8,128)(2,1)}) custom-call(bf16[2048,768]{1,0:T(8,128)(2,1)} %get-tuple-element.2226.refs_5_.refs_0_.refs_1_.refs_2_.refs_3_, bf16[2048,768]{1,0:T(8,128)(2,1)} %get-tuple-element.2226.refs_5_.refs_0_.refs_1_.refs_2_.refs_3_, ...), custom_call_target="tpu_custom_call" | custom-call | flops 1 | bytes 1 | tf_op jit(solution)/shard_map/from_hidden/pallas_call | solution.py:698
  548.2 13.4 %attend_back.4 = (bf16[512,512]{1,0:T(8,128)(2,1)}, f32[512,512]{1,0:T(8,128)}, bf16[512,512]{1,0:T(8,128)(2,1)}, f32[1,128]{1,0:T(1,128)}) custom-call(s32[2]{0:T(128)} %pad_add_fusion.info, bf16[512,512]{1,0:T(8,128)(2,1)} %get-tuple-element.2273.query, bf16[512,512]{1,0:T(8,128)(2,1)} %copy-done.42, bf16[512,512]{1,0:T(8,128)(2,1)} %get-tuple-element.2275.own, ...), custom_call_target="tpu_custom_call" | custom-call | flops 1 | bytes 1 | tf_op jit(solution)/shard_map/attend_back/pallas_call | solution.py:619
  563.5 8.1 row_outer.15
  571.6 19.7 %row_outer.16 = bf16[2048,1536]{1,0:T(8,128)(2,1)} custom-call(bf16[512,2048]{1,0:T(8,128)(2,1)} %get-tuple-element.2306.refs_0_, bf16[512,2048]{1,0:T(8,128)(2,1)} %copy-done.14, bf16[512,2048]{1,0:T(8,128)(2,1)} %copy-done.13, bf16[256,2048]{1,0:T(8,128)(2,1)} %copy-done.23, bf16[256,2048]{1,0:T(8,128)(2,1)} %copy-done.22, ...), custom_call_target="tpu_custom_call" | custom-call | flops 12884901888 | bytes 14680064 | tf_op jit(solution)/shard_map/row_outer/pallas_call | solution.py:742
  600.6 13.2 %attend_back.5 = (bf16[512,512]{1,0:T(8,128)(2,1)}, f32[512,512]{1,0:T(8,128)}, bf16[512,512]{1,0:T(8,128)(2,1)}, f32[1,128]{1,0:T(1,128)}) custom-call(s32[2]{0:T(128)} %pad_add_fusion.info, bf16[512,512]{1,0:T(8,128)(2,1)} %get-tuple-element.2356.query, bf16[512,512]{1,0:T(8,128)(2,1)} %copy-done.41, bf16[512,512]{1,0:T(8,128)(2,1)} %get-tuple-element.2358.own, ...), custom_call_target="tpu_custom_call" | custom-call | flops 1 | bytes 1 | tf_op jit(solution)/shard_map/attend_back/pallas_call | solution.py:619
  613.8 13.5 %attend_back.6 = (bf16[512,512]{1,0:T(8,128)(2,1)}, f32[512,512]{1,0:T(8,128)}, bf16[512,512]{1,0:T(8,128)(2,1)}, f32[1,128]{1,0:T(1,128)}) custom-call(s32[2]{0:T(128)} %pad_add_fusion.info, bf16[512,512]{1,0:T(8,128)(2,1)} %get-tuple-element.2371.query, bf16[512,512]{1,0:T(8,128)(2,1)} %collective-permute-done.21.before, ...), custom_call_target="tpu_custom_call" | custom-call | flops 1 | bytes 1 | tf_op jit(solution)/shard_map/attend_back/pallas_call | solution.py:619
  645.0 13.3 %attend_back.7 = (bf16[512,512]{1,0:T(8,128)(2,1)}, f32[512,512]{1,0:T(8,128)}, bf16[512,512]{1,0:T(8,128)(2,1)}, f32[1,128]{1,0:T(1,128)}) custom-call(s32[2]{0:T(128)} %pad_add_fusion.info, bf16[512,512]{1,0:T(8,128)(2,1)} %get-tuple-element.2439.query, bf16[512,512]{1,0:T(8,128)(2,1)} %copy-done.39, bf16[512,512]{1,0:T(8,128)(2,1)} %get-tuple-element.2441.own, ...), custom_call_target="tpu_custom_call" | custom-call | flops 1 | bytes 1 | tf_op jit(solution)/shard_map/attend_back/pallas_call | solution.py:619
  677.5 14.2 %collective-permute-done.53 = bf16[1024,512]{1,0:T(8,128)(2,1)S(1)} collective-permute-done((bf16[1024,512]{1,0:T(8,128)(2,1)}, bf16[1024,512]{1,0:T(8,128)(2,1)S(1)}, u32[]{:S(2)}, u32[]{:S(2)}) %collective-permute-start.53) | collective-permute-done | bytes 1048608 | tf_op jit(solution)/shard_map/ppermute | solution.py:318
  705.0 10.1 %row_outer.19 = bf16[2048,2048]{1,0:T(8,128)(2,1)} custom-call(bf16[512,2048]{1,0:T(8,128)(2,1)} %pad_maximum_fusion.4.normed.refs_0_, bf16[512,512]{1,0:T(8,128)(2,1)} %get-tuple-element.2635.refs_1_, bf16[512,512]{1,0:T(8,128)(2,1)} %get-tuple-element.2638.refs_2_.refs_3_, bf16[512,512]{1,0:T(8,128)(2,1)} %get-tuple-element.2641.refs_3_.refs_5_, ...), custom_call_target="tpu_custom_call" | custom-call | flops 4294967296 | bytes 4194304 | tf_op jit(solution)/shard_map/row_outer/pallas_call | solution.py:742
  732.3 15.8 %back_to_rows.1 = f32[512,2048]{1,0:T(8,128)} custom-call(bf16[512,512]{1,0:T(8,128)(2,1)} %get-tuple-element.2694.refs_0_.refs_4_, bf16[512,512]{1,0:T(8,128)(2,1)} %get-tuple-element.2635.refs_1_, bf16[512,512]{1,0:T(8,128)(2,1)} %get-tuple-element.2691.refs_2_.refs_1_.refs_3_, bf16[512,512]{1,0:T(8,128)(2,1)} %get-tuple-element.2638.refs_2_.refs_3_, ...), custom_call_target="tpu_custom_call" | custom-call | flops 1 | bytes 1 | tf_op jit(solution)/shard_map/back_to_rows/pallas_call | solution.py:845
  798.5 22.8 %collective-permute-done.73 = bf16[512,256]{1,0:T(8,128)(2,1)S(1)} collective-permute-done((bf16[512,256]{1,0:T(8,128)(2,1)S(1)}, bf16[512,256]{1,0:T(8,128)(2,1)S(1)}, u32[]{:S(2)}, u32[]{:S(2)}) %collective-permute-start.73) | collective-permute-done | bytes 262176 | tf_op jit(solution)/shard_map/ppermute | solution.py:323
  827.5 7.9 whole_columns.5
  839.8 20.6 %collective-permute-done.77 = bf16[1024,512]{1,0:T(8,128)(2,1)S(1)} collective-permute-done((bf16[1024,512]{1,0:T(8,128)(2,1)}, bf16[1024,512]{1,0:T(8,128)(2,1)S(1)}, u32[]{:S(2)}, u32[]{:S(2)}) %collective-permute-start.77) | collective-permute-done | bytes 1048608 | tf_op jit(solution)/shard_map/ppermute | solution.py:318
  (648 shorter events, 414.8 us)
Async XLA Ops:
  7.2 140.7 %all-gather.3.cloned.1.call-start = ((), (), s32[]{:S(2)}) async-start(), calls=%async_computation.2 | async-start | bytes 1310720 | tf_op jit(solution)/shard_map/all_gather | solution.py:907
  61.1 40.0 %collective-permute-start.6 = (bf16[1536,512]{1,0:T(8,128)(2,1)S(1)}, bf16[1536,512]{1,0:T(8,128)(2,1)}, u32[]{:S(2)}, u32[]{:S(2)}) collective-permute-start(bf16[1536,512]{1,0:T(8,128)(2,1)S(1)} %pad_maximum_fusion.8.came0.refs_9_), channel_id=1, source_target_pairs={{0,4},{4,0},{8,12},{12,8},{16,20},{20,16},{24,28},{28,24},{1,5},{5... | collective-permute-start | bytes 4718600 | tf_op jit(solution)/shard_map/ppermute | solution.py:318
  61.2 39.9 %collective-permute-start.5 = (bf16[1536,512]{1,0:T(8,128)(2,1)S(1)}, bf16[1536,512]{1,0:T(8,128)(2,1)}, u32[]{:S(2)}, u32[]{:S(2)}) collective-permute-start(bf16[1536,512]{1,0:T(8,128)(2,1)S(1)} %pad_maximum_fusion.8.came0.refs_9_), channel_id=1, source_target_pairs={{0,16},{4,20},{8,24},{12,28},{16,0},{20,4},{24,8},{28,12},{1,17},{... | collective-permute-start | bytes 4718600 | tf_op jit(solution)/shard_map/ppermute | solution.py:318
  62.7 38.3 %collective-permute-start.4 = (bf16[1536,512]{1,0:T(8,128)(2,1)S(1)}, bf16[1536,512]{1,0:T(8,128)(2,1)}, u32[]{:S(2)}, u32[]{:S(2)}) collective-permute-start(bf16[1536,512]{1,0:T(8,128)(2,1)S(1)} %pad_maximum_fusion.8.came0.refs_9_), channel_id=1, source_target_pairs={{0,8},{4,12},{8,0},{12,4},{16,24},{20,28},{24,16},{28,20},{1,9},{5... | collective-permute-start | bytes 4718600 | tf_op jit(solution)/shard_map/ppermute | solution.py:318
  67.9 33.2 %collective-permute-start.8 = (bf16[256,2048]{1,0:T(8,128)(2,1)}, bf16[256,2048]{1,0:T(8,128)(2,1)S(1)}, u32[]{:S(2)}, u32[]{:S(2)}) collective-permute-start(bf16[256,2048]{1,0:T(8,128)(2,1)} %get-tuple-element.2933), channel_id=1, source_target_pairs={{0,1},{1,0},{2,5},{3,4},{4,3},{5,2},{6,7},{7,6},{8,9},{9,8},{10,13... | collective-permute-start | bytes 3145736 | tf_op jit(solution)/shard_map/ppermute | solution.py:388
  67.9 33.1 %collective-permute-start.7 = (bf16[256,2048]{1,0:T(8,128)(2,1)}, bf16[256,2048]{1,0:T(8,128)(2,1)}, u32[]{:S(2)}, u32[]{:S(2)}) collective-permute-start(bf16[256,2048]{1,0:T(8,128)(2,1)} %get-tuple-element.2934), channel_id=1, source_target_pairs={{0,0},{1,1},{2,4},{3,5},{4,2},{5,3},{6,6},{7,7},{8,8},{9,9},{10,12... | collective-permute-start | bytes 3145736 | tf_op jit(solution)/shard_map/ppermute | solution.py:388
  80.3 278.2 %all-gather.5.cloned.1.call-start = ((), (), s32[]{:S(2)}) async-start(), calls=%async_computation.3 | async-start | bytes 11796480 | tf_op jit(solution)/shard_map/all_gather | solution.py:1001
  103.1 55.7 %collective-permute-start.11 = (bf16[1536,512]{1,0:T(8,128)(2,1)}, bf16[1536,512]{1,0:T(8,128)(2,1)}, u32[]{:S(2)}, u32[]{:S(2)}) collective-permute-start(bf16[1536,512]{1,0:T(8,128)(2,1)} %collective-permute-done.4.came0.refs_13_), channel_id=1, source_target_pairs={{0,4},{4,0},{8,12},{12,8},{16,20},{20,16},{24,28},{28,24},{1,5},{5... | collective-permute-start | bytes 4718600 | tf_op jit(solution)/shard_map/ppermute | solution.py:318
  192.4 398.9 %reduce-scatter.3.cloned.1.call-start = ((), (), s32[]{:S(2)}) async-start(), calls=%async_computation.4 | async-start | bytes 3932160 | tf_op jit(solution)/shard_map/reduce_scatter | solution.py:1117
  210.0 46.9 %collective-permute-start.28 = (bf16[512,2048]{1,0:T(8,128)(2,1)S(1)}, bf16[512,2048]{1,0:T(8,128)(2,1)S(1)}, u32[]{:S(2)}, u32[]{:S(2)}) collective-permute-start(bf16[512,2048]{1,0:T(8,128)(2,1)S(1)} %maximum_select_fusion.refs_5_.refs_0_), channel_id=1, source_target_pairs={{0,16},{4,20},{8,24},{12,28},{16,0},{20,4},{24,8},{28,12},{1,17},{... | collective-permute-start | bytes 6291464 | tf_op jit(solution)/shard_map/ppermute | solution.py:318
  211.6 46.6 %collective-permute-start.27 = (bf16[512,2048]{1,0:T(8,128)(2,1)S(1)}, bf16[512,2048]{1,0:T(8,128)(2,1)S(1)}, u32[]{:S(2)}, u32[]{:S(2)}) collective-permute-start(bf16[512,2048]{1,0:T(8,128)(2,1)S(1)} %maximum_select_fusion.refs_5_.refs_0_), channel_id=1, source_target_pairs={{0,8},{4,12},{8,0},{12,4},{16,24},{20,28},{24,16},{28,20},{1,9},{5... | collective-permute-start | bytes 6291464 | tf_op jit(solution)/shard_map/ppermute | solution.py:318
  284.9 44.9 %collective-permute-start.33 = (bf16[512,2048]{1,0:T(8,128)(2,1)}, bf16[512,2048]{1,0:T(8,128)(2,1)S(1)}, u32[]{:S(2)}, u32[]{:S(2)}) collective-permute-start(bf16[512,2048]{1,0:T(8,128)(2,1)} %get-tuple-element.2306.refs_0_), channel_id=1, source_target_pairs={{0,16},{4,20},{8,24},{12,28},{16,0},{20,4},{24,8},{28,12},{1,17},{... | collective-permute-start | bytes 6291464 | tf_op jit(solution)/shard_map/ppermute | solution.py:318
  286.1 44.9 %collective-permute-start.32 = (bf16[512,2048]{1,0:T(8,128)(2,1)}, bf16[512,2048]{1,0:T(8,128)(2,1)S(1)}, u32[]{:S(2)}, u32[]{:S(2)}) collective-permute-start(bf16[512,2048]{1,0:T(8,128)(2,1)} %get-tuple-element.2306.refs_0_), channel_id=1, source_target_pairs={{0,8},{4,12},{8,0},{12,4},{16,24},{20,28},{24,16},{28,20},{1,9},{5... | collective-permute-start | bytes 6291464 | tf_op jit(solution)/shard_map/ppermute | solution.py:318
  358.5 30.0 %collective-permute-start.36 = (bf16[2048,2304]{1,0:T(8,128)(2,1)}, bf16[2048,2304]{1,0:T(8,128)(2,1)}, u32[]{:S(2)}, u32[]{:S(2)}) collective-permute-start(bf16[2048,2304]{1,0:T(8,128)(2,1)} %all-gather.5.cloned.1.call-done.refs_10_.refs_11_.refs_12_.refs_4_.refs_9_), channel_id=1, source_target_pairs={{0,4},{4,0},{8,12},{12,8},{16,20},{20,16},{24,28},{28,24},{1,5},{5... | collective-permute-start | bytes 28311560 | tf_op jit(solution)/shard_map/ppermute | solution.py:318
  450.9 54.5 %collective-permute-start.38 = (bf16[512,2048]{1,0:T(8,128)(2,1)}, bf16[512,2048]{1,0:T(8,128)(2,1)}, u32[]{:S(2)}, u32[]{:S(2)}) collective-permute-start(bf16[512,2048]{1,0:T(8,128)(2,1)} %get-tuple-element.2137), channel_id=1, source_target_pairs={{0,8},{4,12},{8,0},{12,4},{16,24},{20,28},{24,16},{28,20},{1,9},{5... | collective-permute-start | bytes 6291464 | tf_op jit(solution)/shard_map/ppermute | solution.py:318
  452.4 52.9 %collective-permute-start.39 = (bf16[512,2048]{1,0:T(8,128)(2,1)}, bf16[512,2048]{1,0:T(8,128)(2,1)}, u32[]{:S(2)}, u32[]{:S(2)}) collective-permute-start(bf16[512,2048]{1,0:T(8,128)(2,1)} %get-tuple-element.2138), channel_id=1, source_target_pairs={{0,16},{4,20},{8,24},{12,28},{16,0},{20,4},{24,8},{28,12},{1,17},{... | collective-permute-start | bytes 6291464 | tf_op jit(solution)/shard_map/ppermute | solution.py:318
  505.3 30.6 %collective-permute-start.40 = (bf16[2048,1536]{1,0:T(8,128)(2,1)}, bf16[2048,1536]{1,0:T(8,128)(2,1)}, u32[]{:S(2)}, u32[]{:S(2)}) collective-permute-start(bf16[2048,1536]{1,0:T(8,128)(2,1)} %row_outer.14), channel_id=1, source_target_pairs={{0,4},{4,0},{8,12},{12,8},{16,20},{20,16},{24,28},{28,24},{1,5},{5... | collective-permute-start | bytes 18874376 | tf_op jit(solution)/shard_map/ppermute | solution.py:318
  505.4 214.7 %reduce-scatter.5.cloned.1.call-start = ((), (), s32[]{:S(2)}) async-start(), calls=%async_computation.5 | async-start | bytes 7864320 | tf_op jit(solution)/shard_map/reduce_scatter | solution.py:1185
  535.9 55.4 %collective-permute-start.43 = (bf16[512,2048]{1,0:T(8,128)(2,1)}, bf16[512,2048]{1,0:T(8,128)(2,1)}, u32[]{:S(2)}, u32[]{:S(2)}) collective-permute-start(bf16[512,2048]{1,0:T(8,128)(2,1)} %get-tuple-element.2321), channel_id=1, source_target_pairs={{0,8},{4,12},{8,0},{12,4},{16,24},{20,28},{24,16},{28,20},{1,9},{5... | collective-permute-start | bytes 6291464 | tf_op jit(solution)/shard_map/ppermute | solution.py:318
  537.5 53.8 %collective-permute-start.44 = (bf16[512,2048]{1,0:T(8,128)(2,1)}, bf16[512,2048]{1,0:T(8,128)(2,1)}, u32[]{:S(2)}, u32[]{:S(2)}) collective-permute-start(bf16[512,2048]{1,0:T(8,128)(2,1)} %get-tuple-element.2322), channel_id=1, source_target_pairs={{0,16},{4,20},{8,24},{12,28},{16,0},{20,4},{24,8},{28,12},{1,17},{... | collective-permute-start | bytes 6291464 | tf_op jit(solution)/shard_map/ppermute | solution.py:318
  591.3 36.0 %collective-permute-start.47 = (bf16[2048,1024]{1,0:T(8,128)(2,1)}, bf16[2048,1024]{1,0:T(8,128)(2,1)S(1)}, u32[]{:S(2)}, u32[]{:S(2)}) collective-permute-start(bf16[2048,1024]{1,0:T(8,128)(2,1)} %row_outer.15), channel_id=1, source_target_pairs={{0,4},{4,0},{8,12},{12,8},{16,20},{20,16},{24,28},{28,24},{1,5},{5... | collective-permute-start | bytes 12582920 | tf_op jit(solution)/shard_map/ppermute | solution.py:318
  596.3 31.0 %collective-permute-start.46 = (bf16[256,2048]{1,0:T(8,128)(2,1)}, bf16[256,2048]{1,0:T(8,128)(2,1)S(1)}, u32[]{:S(2)}, u32[]{:S(2)}) collective-permute-start(bf16[256,2048]{1,0:T(8,128)(2,1)} %get-tuple-element.2913), channel_id=1, source_target_pairs={{0,16},{4,20},{8,24},{12,28},{16,0},{20,4},{24,8},{28,12},{1,17},{... | collective-permute-start | bytes 3145736 | tf_op jit(solution)/shard_map/ppermute | solution.py:318
  629.5 32.7 %collective-permute-start.50 = (bf16[512,768]{1,0:T(8,128)(2,1)}, bf16[512,768]{1,0:T(8,128)(2,1)S(1)}, u32[]{:S(2)}, u32[]{:S(2)}) collective-permute-start(bf16[512,768]{1,0:T(8,128)(2,1)} %reduce-scatter.3.cloned.1.call-done), channel_id=1, source_target_pairs={{0,16},{4,20},{8,24},{12,28},{16,0},{20,4},{24,8},{28,12},{1,17},{... | collective-permute-start | bytes 2359304 | tf_op jit(solution)/shard_map/ppermute | solution.py:318
  630.9 31.4 %collective-permute-start.49 = (bf16[512,768]{1,0:T(8,128)(2,1)}, bf16[512,768]{1,0:T(8,128)(2,1)S(1)}, u32[]{:S(2)}, u32[]{:S(2)}) collective-permute-start(bf16[512,768]{1,0:T(8,128)(2,1)} %reduce-scatter.3.cloned.1.call-done), channel_id=1, source_target_pairs={{0,8},{4,12},{8,0},{12,4},{16,24},{20,28},{24,16},{28,20},{1,9},{5... | collective-permute-start | bytes 2359304 | tf_op jit(solution)/shard_map/ppermute | solution.py:318
  631.5 30.7 %collective-permute-start.51 = (bf16[512,512]{1,0:T(8,128)(2,1)}, bf16[512,512]{1,0:T(8,128)(2,1)}, u32[]{:S(2)}, u32[]{:S(2)}) collective-permute-start(bf16[512,512]{1,0:T(8,128)(2,1)} %get-tuple-element.2455), channel_id=1, source_target_pairs={{4,0},{12,8},{20,16},{28,24},{5,1},{13,9},{21,17},{29,25},{6,2},{1... | collective-permute-start | bytes 1572872 | tf_op jit(solution)/shard_map/ppermute | solution.py:1145
  720.1 40.5 %collective-permute-start.65 = (bf16[2048,2048]{1,0:T(8,128)(2,1)}, bf16[2048,2048]{1,0:T(8,128)(2,1)}, u32[]{:S(2)}, u32[]{:S(2)}) collective-permute-start(bf16[2048,2048]{1,0:T(8,128)(2,1)} %row_outer.19), channel_id=1, source_target_pairs={{0,4},{4,0},{8,12},{12,8},{16,20},{20,16},{24,28},{28,24},{1,5},{5... | collective-permute-start | bytes 25165832 | tf_op jit(solution)/shard_map/ppermute | solution.py:318
  723.1 36.6 %collective-permute-start.62 = (bf16[512,1536]{1,0:T(8,128)(2,1)}, bf16[512,1536]{1,0:T(8,128)(2,1)S(1)}, u32[]{:S(2)}, u32[]{:S(2)}) collective-permute-start(bf16[512,1536]{1,0:T(8,128)(2,1)} %reduce-scatter.5.cloned.1.call-done), channel_id=1, source_target_pairs={{0,16},{4,20},{8,24},{12,28},{16,0},{20,4},{24,8},{28,12},{1,17},{... | collective-permute-start | bytes 4718600 | tf_op jit(solution)/shard_map/ppermute | solution.py:318
  724.0 36.6 %collective-permute-start.61 = (bf16[512,1536]{1,0:T(8,128)(2,1)}, bf16[512,1536]{1,0:T(8,128)(2,1)S(1)}, u32[]{:S(2)}, u32[]{:S(2)}) collective-permute-start(bf16[512,1536]{1,0:T(8,128)(2,1)} %reduce-scatter.5.cloned.1.call-done), channel_id=1, source_target_pairs={{0,8},{4,12},{8,0},{12,4},{16,24},{20,28},{24,16},{28,20},{1,9},{5... | collective-permute-start | bytes 4718600 | tf_op jit(solution)/shard_map/ppermute | solution.py:318
  791.2 30.2 %collective-permute-start.71 = (bf16[1024,512]{1,0:T(8,128)(2,1)S(1)}, bf16[1024,512]{1,0:T(8,128)(2,1)S(1)}, u32[]{:S(2)}, u32[]{:S(2)}) collective-permute-start(bf16[1024,512]{1,0:T(8,128)(2,1)S(1)} %copy-done.128), channel_id=1, source_target_pairs={{0,8},{4,12},{8,0},{12,4},{16,24},{20,28},{24,16},{28,20},{1,9},{5... | collective-permute-start | bytes 3145736 | tf_op jit(solution)/shard_map/ppermute | solution.py:318
  797.7 42.1 %collective-permute-start.79 = (bf16[256,2048]{1,0:T(8,128)(2,1)}, bf16[256,2048]{1,0:T(8,128)(2,1)S(1)}, u32[]{:S(2)}, u32[]{:S(2)}) collective-permute-start(bf16[256,2048]{1,0:T(8,128)(2,1)} %get-tuple-element.2907), channel_id=1, source_target_pairs={{1,0},{0,1},{5,2},{4,3},{3,4},{2,5},{7,6},{6,7},{9,8},{8,9},{13,10... | collective-permute-start | bytes 3145736 | tf_op jit(solution)/shard_map/ppermute | solution.py:395
  824.4 36.0 %collective-permute-start.77 = (bf16[1024,512]{1,0:T(8,128)(2,1)}, bf16[1024,512]{1,0:T(8,128)(2,1)S(1)}, u32[]{:S(2)}, u32[]{:S(2)}) collective-permute-start(bf16[1024,512]{1,0:T(8,128)(2,1)} %get-tuple-element.2758), channel_id=1, source_target_pairs={{0,8},{4,12},{8,0},{12,4},{16,24},{20,28},{24,16},{28,20},{1,9},{5... | collective-permute-start | bytes 3145736 | tf_op jit(solution)/shard_map/ppermute | solution.py:318
  826.2 34.2 %collective-permute-start.78 = (bf16[1024,512]{1,0:T(8,128)(2,1)}, bf16[1024,512]{1,0:T(8,128)(2,1)S(1)}, u32[]{:S(2)}, u32[]{:S(2)}) collective-permute-start(bf16[1024,512]{1,0:T(8,128)(2,1)} %get-tuple-element.2761), channel_id=1, source_target_pairs={{0,16},{4,20},{8,24},{12,28},{16,0},{20,4},{24,8},{28,12},{1,17},{... | collective-permute-start | bytes 3145736 | tf_op jit(solution)/shard_map/ppermute | solution.py:318
  (206 other events, 2360.4 us)
Sparse Core Ops, SparseCore 0:
  80.4 44.4 all-gather.2
  192.5 166.0 all-gather.4
  505.6 57.2 reduce-scatter.2
  591.5 107.9 reduce-scatter.4
